TPU v7x, 32 devices: a whole 2x2x4 slice. The times are simulated.
32 devices in a mesh: rep: 8 (over y, x, core), tp: 4 (over z).
Axes of the slice: x: 2, y: 2, z: 4, core: 2. Of those that a mesh axis runs over, the one named last changes fastest.
Arguments:
- residual: bfloat16 [16384, 8192], P(('rep', 'tp')), may hold values from -6 to 6
- norm_gain: bfloat16 [8192], P(('rep', 'tp')), may hold values from 0.5 to 1.5
- value_weight: bfloat16 [8192, 512], P(('rep', 'tp')), may hold values from -0.0625 to 0.0625
- value_cot: bfloat16 [16384, 512], P(('rep', 'tp')), may hold values from -12 to 12
- trainee_logp: float32 [16384], P(('rep', 'tp')), may hold values from -40 to -8
- ref_shard_max: float32 [4, 16384], P('tp', 'rep'), may hold values from 90 to 120
- ref_shard_sum: float32 [4, 16384], P('tp', 'rep'), may hold values from 1 to 1000
- ref_target_logit: float32 [4, 16384], P('tp', 'rep'), may hold values from 80 to 120
- target_ids: int32 [16384], P('rep'), may hold values from 0 to 128255
- lengths: int32 [8], replicated, may hold values from 1024 to 2048, as said below
Outputs:
- value_proj: bfloat16 [16384, 512], P(('rep', 'tp'))
- resid_grad: bfloat16 [16384, 8192], P(('rep', 'tp'))
- weight_grad: float32 [8192, 512], P(('rep', 'tp'))
- gain_grad: float32 [8192], P(('rep', 'tp'))
Inputs may be any that keep to these rules, and one draw needn't show every extreme that they name: `lengths`: one sequence has all 2048 tokens live and one has 1024.
All inputs are finite; a program needn't handle non-finite values.
Results may differ from a plain program's by a relative error of at most 0.009.
Values may be sent and summed in bfloat16 or wider, within the bound.
No kernel may reach another device: no remote copies, remote signals or barrier semaphores. Data moves between devices by JAX's collectives and lax.ppermute only.
A program may use at most 192 MiB of HBM per device.

v0:
```python
import jax
import jax.numpy as jnp
from jax import lax
from jax.sharding import PartitionSpec as P

VOCAB = 128256


EPS = 1e-05
BETA = 0.5


def merged(value, axis, join):
    pieces = jax.tree.map(lambda part: lax.all_gather(part, axis), value)
    head = jax.tree.map(lambda part: part[0], pieces)
    tail = jax.tree.map(lambda part: part[1:], pieces)
    total, _ = lax.scan(lambda total, share: (join(total, share), None), head, tail)
    return total


def combine(earlier, later):
    first_max, first_sum, first_target = earlier
    second_max, second_sum, second_target = later
    top_max = jnp.maximum(first_max, second_max)
    merged_sum = first_sum * jnp.exp(first_max - top_max) + second_sum * jnp.exp(
        second_max - top_max
    )
    return (top_max, merged_sum, first_target + second_target)


def per_device(
    residual,
    norm_gain,
    value_weight,
    value_cot,
    trainee_logp,
    ref_shard_max,
    ref_shard_sum,
    ref_target_logit,
    target_ids,
    lengths,
):
    rows_here = residual.shape[0]
    tp_count = lax.axis_size("tp")
    rep_count = lax.axis_size("rep")
    tp_place = lax.axis_index("tp")
    rep_place = lax.axis_index("rep")
    shard_width = VOCAB // tp_count
    owned = jnp.where(
        target_ids // shard_width == tp_place,
        ref_target_logit[0],
        jnp.zeros_like(ref_target_logit[0]),
    )
    top_max, sum_exp, picked = merged((ref_shard_max[0], ref_shard_sum[0], owned), "tp", combine)
    whole_logp = picked - top_max - jnp.log(sum_exp)
    ref_logp = lax.dynamic_slice_in_dim(whole_logp, tp_place * rows_here, rows_here)
    seq_length = lax.dynamic_index_in_dim(lengths, rep_place, keepdims=False)
    positions = tp_place * rows_here + jnp.arange(rows_here, dtype=jnp.int32)
    live_rows = (positions < seq_length).astype(jnp.float32)
    local_sum = jnp.sum(live_rows * (trainee_logp - ref_logp))
    seq_total = lax.psum(local_sum, "tp")
    seq_delta = seq_total / seq_length.astype(jnp.float32)
    seq_weight = 2.0 * jax.nn.sigmoid(BETA * seq_delta) / rep_count
    row_scale = live_rows * seq_weight
    resid_wide = residual.astype(jnp.float32)
    inv_rms = lax.rsqrt(jnp.mean(resid_wide * resid_wide, axis=1, keepdims=True) + EPS)
    unit_rows = resid_wide * inv_rms
    weight_piece = lax.all_gather(value_weight, ("rep", "tp"), axis=0, tiled=True)
    gain_piece = lax.all_gather(norm_gain, ("rep", "tp"), axis=0, tiled=True)
    columns = unit_rows
    normed_part = (columns * gain_piece.astype(jnp.float32)[None, :]).astype(jnp.bfloat16)
    value_acc = jnp.dot(normed_part, weight_piece, preferred_element_type=jnp.float32)
    gain_all = gain_piece
    value_proj, normed, gain_all = (value_acc, normed_part, gain_all)
    scaled = (row_scale[:, None] * value_cot.astype(jnp.float32)).astype(jnp.bfloat16)
    normed_grad = lax.dot_general(
        scaled,
        lax.all_gather(value_weight, ("rep", "tp"), axis=0, tiled=True),
        (((1,), (1,)), ((), ())),
        preferred_element_type=jnp.float32,
    )
    unit_grad = normed_grad * gain_all.astype(jnp.float32)[None, :]
    project_mean = jnp.mean(unit_grad * unit_rows, axis=1, keepdims=True)
    resid_grad = (inv_rms * (unit_grad - unit_rows * project_mean)).astype(jnp.bfloat16)
    gain_grad = lax.psum_scatter(
        jnp.sum(normed_grad * unit_rows, axis=0), ("rep", "tp"), scatter_dimension=0, tiled=True
    )
    columns = normed
    weight_grad = lax.psum_scatter(
        lax.dot_general(
            columns, scaled, (((0,), (0,)), ((), ())), preferred_element_type=jnp.float32
        ),
        ("rep", "tp"),
        scatter_dimension=0,
        tiled=True,
    )
    return (value_proj.astype(jnp.bfloat16), resid_grad, weight_grad, gain_grad)


def solution(mesh):
    placed = (
        P(("rep", "tp"), None),
        P(("rep", "tp")),
        P(("rep", "tp"), None),
        P(("rep", "tp"), None),
        P(("rep", "tp")),
        P("tp", "rep"),
        P("tp", "rep"),
        P("tp", "rep"),
        P("rep"),
        P(),
    )
    return jax.shard_map(
        per_device,
        mesh=mesh,
        in_specs=placed,
        out_specs=(
            P(("rep", "tp"), None),
            P(("rep", "tp"), None),
            P(("rep", "tp"), None),
            P(("rep", "tp")),
        ),
        check_vma=False,
    )
```

profile of v0, /device:TPU:0, one launch (start us, length us, event | category | flops | bytes accessed | tf_op | source)
XLA Modules:
  0.0 523.0 jit_solution(8083593313428735068)
XLA Ops:
  7.2 0.0 all-gather.6.cloned.1.call-start
  7.2 0.7 all-gather.6.cloned.1.call-update
  7.9 0.0 reduce-scatter.2.cloned.1.call-start
  7.9 0.7 fusion.20
  8.7 14.8 %all-gather = f32[8192]{0:T(1024)S(1)} all-gather(f32[2048]{0:T(1024)S(1)} %fusion.20), channel_id=2, replica_groups=mesh['rep'=8,'tp'=4] {'tp'}, dimensions={0}, use_global_device_ids=true | all-gather | bytes 40960 | tf_op jit(solution)/shard_map/all_gather | solution.py:14
  23.5 13.3 %all-gather.2 = f32[4,1,2048]{2,1,0:T(1,128)S(1)} all-gather(f32[1,1,2048]{2,1,0:T(1,128)} %bitcast.36), channel_id=1, replica_groups=mesh['rep'=8,'tp'=4] {'tp'}, dimensions={0}, use_global_device_ids=true | all-gather | bytes 40960 | tf_op jit(solution)/shard_map/all_gather | solution.py:14
  36.8 13.4 %all-gather.3 = f32[4,1,2048]{2,1,0:T(1,128)S(1)} all-gather(f32[1,1,2048]{2,1,0:T(1,128)} %bitcast.37), channel_id=1, replica_groups=mesh['rep'=8,'tp'=4] {'tp'}, dimensions={0}, use_global_device_ids=true | all-gather | bytes 40960 | tf_op jit(solution)/shard_map/all_gather | solution.py:14
  50.2 1.2 dynamic_slice.17
  51.5 0.3 while.14
  51.8 2.0 fusion.25
  53.8 12.5 %psum.7 = f32[]{:T(128)} all-reduce(f32[]{:T(128)} %fusion.25), channel_id=1, replica_groups=mesh['rep'=8,'tp'=4] {'tp'}, use_global_device_ids=true, to_apply=%region_4.5 | all-reduce | flops 1 | bytes 8 | tf_op jit(solution)/shard_map/psum | solution.py:61
  66.9 0.7 reshape.31
  67.6 63.8 %all-gather.1 = bf16[32,1,256]{2,1,0:T(2,128)(2,1)S(1)} all-gather(bf16[1,1,256]{2,1,0:T(2,128)(2,1)S(1)} %reshape.31), channel_id=1, replica_groups=mesh['rep'=8,'tp'=4] {'rep','tp'}, dimensions={0}, use_global_device_ids=true | all-gather | bytes 16896 | tf_op jit(solution)/shard_map/all_gather | solution.py:69
  132.2 5.1 fusion.10
  137.3 0.7 add_rsqrt_fusion
  138.0 0.0 copy-start.1
  138.0 14.0 %fusion.11 = f32[8192,512]{1,0:T(8,128)} fusion(bf16[512,8192]{1,0:T(8,128)(2,1)} %param.12, f32[8192]{0:T(1024)S(1)} %bitcast.31, f32[512]{0:T(512)S(1)} %get-tuple-element.67, bf16[512,512]{1,0:T(8,128)(2,1)} %param.15, f32[512]{0:T(512)S(1)} %get-tuple-element.68), kind=kOutput, calls=%fused_computation.17 | convolution fusion | flops 4312530944 | bytes 25726976 | tf_op jit(solution)/shard_map/dot_general | solution.py:90
  152.0 0.0 reduce-scatter.2.cloned.1.call-update
  152.0 0.0 all-gather.6.cloned.1.call-done
  152.0 0.0 copy-done.1
  152.1 13.5 %fusion.9 = (f32[8192]{0:T(1024)S(1)}, f32[512]{0:T(512)S(1)}, f32[512,8192]{1,0:T(8,128)}) fusion(bf16[512,8192]{1,0:T(8,128)(2,1)} %param.12, f32[512]{0:T(512)S(1)} %get-tuple-element.67, f32[8192]{0:T(1024)S(1)} %bitcast.32, bf16[8192,512]{1,0:T(8,128)(2,1)} %all-gather.6.cloned.1.call-done, bf16[512,512]{1,0:T(8,128)(2,1)S(1)} %copy-done.1, ...), kind=kOutput, calls=%fused_computation.15 | convolution fusion | flops 4325105152 | bytes 34150400 | tf_op jit(solution)/shard_map/dot_general | solution.py:76
  165.6 42.4 %all-reduce = f32[8192]{0:T(1024)S(1)} all-reduce(f32[8192]{0:T(1024)S(1)} %get-tuple-element.46), channel_id=4, replica_groups=mesh['rep'=8,'tp'=4] {'rep','tp'}, use_global_device_ids=true, to_apply=%region_8.9.clone | all-reduce | flops 8192 | bytes 65536
  208.0 0.6 dynamic-slice
  208.6 0.0 copy-start
  208.6 11.3 %fusion.15 = bf16[512,512]{1,0:T(8,128)(2,1)} fusion(bf16[8192,512]{1,0:T(8,128)(2,1)} %all-gather.6.cloned.1.call-done, bf16[512,8192]{1,0:T(8,128)(2,1)} %param.12, f32[8192]{0:T(1024)S(1)} %bitcast.33, f32[512]{0:T(512)S(1)} %get-tuple-element.67), kind=kOutput, calls=%fused_computation.19 | convolution fusion | flops 4312006656 | bytes 17336320 | tf_op jit(solution)/shard_map/dot_general | solution.py:72
  219.9 0.0 copy-done
  219.9 9.2 %fusion.8 = bf16[512,8192]{1,0:T(8,128)(2,1)} fusion(bf16[512,8192]{1,0:T(8,128)(2,1)} %param.12, f32[512,8192]{1,0:T(8,128)S(1)} %copy-done, f32[512]{0:T(512)S(1)} %broadcast_multiply_fusion, f32[8192]{0:T(1024)S(1)} %bitcast.34, f32[512]{0:T(512)S(1)} %get-tuple-element.67), kind=kLoop, calls=%fused_computation.14 | loop fusion | flops 29360128 | bytes 33591296 | tf_op jit(solution)/shard_map/convert_element_type | solution.py:84
  229.1 287.1 %reduce-scatter.2.cloned.1.call-done = f32[256,512]{1,0:T(8,128)} async-done(((f32[8192,512]{1,0:T(8,128)}), f32[256,512]{1,0:T(8,128)}) %reduce-scatter.2.cloned.1.call-update) | async-done | bytes 524304 | tf_op jit(solution)/shard_map/reduce_scatter | solution.py:89
  (23 shorter events, 0.2 us)
Async XLA Ops:
  7.2 144.9 %all-gather.6.cloned.1.call-start = ((), (), s32[]{:S(2)}) async-start(), calls=%async_computation.1 | async-start | bytes 8650752 | tf_op jit(solution)/shard_map/all_gather | solution.py:68
  7.9 508.3 %reduce-scatter.2.cloned.1.call-start = ((), (), s32[]{:S(2)}) async-start(), calls=%async_computation.2 | async-start | bytes 17301504 | tf_op jit(solution)/shard_map/reduce_scatter | solution.py:89
  138.0 14.1 %copy-start.1 = (bf16[512,512]{1,0:T(8,128)(2,1)S(1)}, bf16[512,512]{1,0:T(8,128)(2,1)}, u32[]{:S(2)}) copy-start(bf16[512,512]{1,0:T(8,128)(2,1)} %param.15) | copy-start | bytes 1572868
  208.6 11.3 %copy-start = (f32[512,8192]{1,0:T(8,128)S(1)}, f32[512,8192]{1,0:T(8,128)}, u32[]{:S(2)}) copy-start(f32[512,8192]{1,0:T(8,128)} %get-tuple-element.66) | copy-start | bytes 50331652
Sparse Core Ops, SparseCore 0:
  10.9 80.2 all-gather.5
  152.1 364.0 reduce-scatter.1
where the time goes:
time: 524 us; the launch traced here: 523 us
  waiting for transfers between devices  288 us (55%)
  blocking collectives  160 us (31%)
  matrix products  38.8 us (7%)
  other arithmetic  17.8 us (3%)
  between operations  15.5 us (3%)
    reduce_scatter x1, waiting for transfers between devices, per_device(): lax.psum_scatter(lax.dot_general(columns, scaled, (((0,), (0,)), ((), ())...  287 us
    all_gather x1, blocking collectives, per_device(): gain_piece = lax.all_gather(norm_gain, ('rep', 'tp'), axis=0, tiled=True)  63.8 us
    unnamed x1, blocking collectives  42.4 us
    all_gather x3, blocking collectives, merged(): pieces = jax.tree.map(lambda part: lax.all_gather(part, axis), value)  41.5 us
    dot_general x1, matrix products, per_device(): lax.dot_general(columns, scaled, (((0,), (0,)), ((), ())), preferred_elem...  14 us
    dot_general x1, matrix products, per_device(): lax.dot_general(scaled, lax.all_gather(value_weight, ('rep', 'tp'), axis=...  13.5 us
    psum x1, blocking collectives, per_device(): seq_total = lax.psum(local_sum, 'tp')  12.5 us
    dot_general x1, matrix products, per_device(): jnp.dot(normed_part, weight_piece, preferred_element_type=jnp.float32)  11.3 us
  transfers between devices with their start and end apart: 2, of which 1 were waited for; matrix products, arithmetic and copies ran while one was open for 11% of the time, Pallas kernels for 0%

commit v1 on v0

v1 whole, which is shorter than its diff:
```python
import functools

import jax
import jax.numpy as jnp
from jax import lax
from jax.experimental import pallas as pl
from jax.experimental.pallas import tpu as pltpu
from jax.sharding import PartitionSpec as P

VOCAB = 128256
EPS = 1e-05
BETA = 0.5
CORES = 2
OUTER = 2


def shift_pairs(count, stride, size, step):
    pairs = []
    for place in range(count):
        digit = (place // stride) % size
        pairs.append((place, place + ((digit + step) % size - digit) * stride))
    return pairs


def swap(value, axis, stride, size, step):
    return lax.ppermute(value, axis, shift_pairs(lax.axis_size(axis), stride, size, step))


def partial_kernel(blocks_ref, places_ref, resid_ref, cot_ref, out_ref):
    product = lax.dot_general(
        resid_ref[...], cot_ref[...], (((0,), (0,)), ((), ())), preferred_element_type=jnp.float32
    )
    out_ref[0] = product.astype(out_ref.dtype)


def partial_add_kernel(blocks_ref, places_ref, resid_ref, cot_ref, other_ref, out_ref):
    product = lax.dot_general(
        resid_ref[...], cot_ref[...], (((0,), (0,)), ((), ())), preferred_element_type=jnp.float32
    )
    out_ref[0] = (product + other_ref[0].astype(jnp.float32)).astype(out_ref.dtype)


def partial_grad(resid, cot, first_col, width, blocks, places, depth, other):
    rows = resid.shape[0]
    count = blocks.shape[0]
    col = first_col // width
    in_specs = [
        pl.BlockSpec((rows, depth), lambda i, b, p: (0, b[i])),
        pl.BlockSpec((rows, width), lambda i, b, p: (0, col)),
    ]
    operands = [resid, cot]
    if other is not None:
        in_specs.append(pl.BlockSpec((1, depth, width), lambda i, b, p: (p[i], 0, col)))
        operands.append(other)
    return pl.pallas_call(
        partial_kernel if other is None else partial_add_kernel,
        out_shape=jax.ShapeDtypeStruct((count, depth, width), jnp.bfloat16),
        grid_spec=pltpu.PrefetchScalarGridSpec(
            num_scalar_prefetch=2,
            grid=(count,),
            in_specs=in_specs,
            out_specs=pl.BlockSpec((1, depth, width), lambda i, b, p: (i, 0, 0)),
        ),
        cost_estimate=pl.CostEstimate(
            flops=2 * rows * count * depth * width,
            bytes_accessed=2 * count * depth * (rows + 2 * width),
            transcendentals=0,
        ),
        compiler_params=pltpu.CompilerParams(vmem_limit_bytes=40 * 1024 * 1024),
    )(blocks, places, *operands)


def sequence_weight(trainee_logp, shard_max, shard_sum, owned, seq_length, rep_count, tp_count, tp_place):
    rows_here = trainee_logp.shape[0]
    seq = shard_max.shape[0]
    packed = jnp.concatenate([shard_max, shard_sum, owned, trainee_logp]).reshape(-1, 128)
    shares = [packed] + [swap(packed, "tp", 1, tp_count, s) for s in range(1, tp_count)]
    shares = [share.reshape(-1) for share in shares]
    top_max = functools.reduce(jnp.maximum, [share[:seq] for share in shares])
    sum_exp = sum(share[seq : 2 * seq] * jnp.exp(share[:seq] - top_max) for share in shares)
    picked = sum(share[2 * seq : 3 * seq] for share in shares)
    ref_logp = picked - top_max - jnp.log(sum_exp)
    total = jnp.zeros((), jnp.float32)
    for s, share in enumerate(shares):
        first = lax.rem(tp_place - s + tp_count, tp_count) * rows_here
        live = first + jnp.arange(rows_here, dtype=jnp.int32) < seq_length
        diff = share[3 * seq :] - lax.dynamic_slice_in_dim(ref_logp, first, rows_here)
        total = total + jnp.sum(jnp.where(live, diff, 0.0))
    seq_delta = total / seq_length.astype(jnp.float32)
    return 2.0 * jax.nn.sigmoid(BETA * seq_delta) / rep_count


def per_device(
    residual,
    norm_gain,
    value_weight,
    value_cot,
    trainee_logp,
    ref_shard_max,
    ref_shard_sum,
    ref_target_logit,
    target_ids,
    lengths,
):
    rows_here, width = residual.shape
    features = value_cot.shape[1]
    half = features // 2
    tp_count = lax.axis_size("tp")
    rep_count = lax.axis_size("rep")
    tp_place = lax.axis_index("tp")
    rep_place = lax.axis_index("rep")
    outer, inner = OUTER, rep_count // (OUTER * CORES)
    depth = width // rep_count
    own_rows = depth // tp_count
    core = lax.rem(rep_place, CORES)
    at_inner = lax.rem(rep_place // CORES, inner)
    at_outer = rep_place // (CORES * inner)

    gain_wide = norm_gain.astype(jnp.float32)[:, None]
    gained = (value_weight.astype(jnp.float32) * gain_wide).astype(jnp.bfloat16)
    weight = lax.all_gather(gained, ("rep", "tp"), axis=0, tiled=True)

    owned = jnp.where(
        target_ids // (VOCAB // tp_count) == tp_place,
        ref_target_logit[0],
        jnp.zeros_like(ref_target_logit[0]),
    )
    seq_length = lax.dynamic_index_in_dim(lengths, rep_place, keepdims=False)
    seq_weight = sequence_weight(
        trainee_logp, ref_shard_max[0], ref_shard_sum[0], owned, seq_length, rep_count, tp_count, tp_place
    )
    positions = tp_place * rows_here + jnp.arange(rows_here, dtype=jnp.int32)
    row_scale = (positions < seq_length).astype(jnp.float32) * seq_weight
    resid_wide = residual.astype(jnp.float32)
    inv_rms = lax.rsqrt(jnp.mean(resid_wide * resid_wide, axis=1, keepdims=True) + EPS)
    cot = (inv_rms * row_scale[:, None] * value_cot.astype(jnp.float32)).astype(jnp.bfloat16)

    chips = jnp.arange(outer * inner, dtype=jnp.int32)
    theirs = partial_grad(residual, cot, 0, features, chips * CORES + (1 - core), chips, depth, None)
    other = swap(theirs, "rep", 1, CORES, 1)

    def block_at(step_outer, step_inner):
        return lax.rem(at_outer + step_outer, outer) * inner + lax.rem(at_inner + step_inner, inner)

    def own_blocks(first_col, steps):
        places = jnp.stack([block_at(o, i) for o, i in steps]).astype(jnp.int32)
        return partial_grad(residual, cot, first_col, half, places * CORES + core, places, depth, other)

    def widen(parts):
        return sum(part.astype(jnp.float32) for part in parts)

    sent_a = [own_blocks(0, [(o, s) for o in range(outer)]) for s in range(1, inner)]
    got_a = [swap(x, "rep", CORES, inner, s + 1) for s, x in enumerate(sent_a)]
    sent_b = [own_blocks(half, [(s, i) for i in range(inner)]) for s in range(1, outer)]
    got_b = [swap(x, "rep", CORES * inner, outer, s + 1) for s, x in enumerate(sent_b)]
    kept_a = own_blocks(0, [(o, 0) for o in range(outer)])
    kept_b = own_blocks(half, [(0, i) for i in range(inner)])

    sent_a = [widen([kept_a[o]] + [g[o] for g in got_a]).astype(jnp.bfloat16) for o in range(1, outer)]
    next_a = [swap(x, "rep", CORES * inner, outer, s + 1) for s, x in enumerate(sent_a)]
    sent_b = [widen([kept_b[i]] + [g[i] for g in got_b]).astype(jnp.bfloat16) for i in range(1, inner)]
    next_b = [swap(x, "rep", CORES, inner, s + 1) for s, x in enumerate(sent_b)]
    chip_a = widen([kept_a[0]] + [g[0] for g in got_a] + next_a)
    chip_b = widen([kept_b[0]] + [g[0] for g in got_b] + next_b)

    def rows_for(step):
        first = lax.rem(tp_place + step, tp_count) * own_rows
        return jnp.concatenate(
            [lax.dynamic_slice_in_dim(part, first, own_rows) for part in (chip_a, chip_b)], axis=1
        )

    last = [
        swap(rows_for(s).astype(jnp.bfloat16), "tp", 1, tp_count, s) for s in range(1, tp_count)
    ]
    unit_grad_rows = rows_for(0) + widen(last)
    weight_grad = gain_wide * unit_grad_rows
    gain_grad = jnp.sum(value_weight.astype(jnp.float32) * unit_grad_rows, axis=1)

    value_acc = jnp.dot(residual, weight, preferred_element_type=jnp.float32)
    value_proj = (inv_rms * value_acc).astype(jnp.bfloat16)
    share = jnp.sum(cot.astype(jnp.float32) * value_acc, axis=1, keepdims=True)
    coefficient = inv_rms * inv_rms * share * (1.0 / width)
    normed_grad = lax.dot_general(
        cot, weight, (((1,), (1,)), ((), ())), preferred_element_type=jnp.float32
    )
    resid_grad = (normed_grad - residual.astype(jnp.float32) * coefficient).astype(jnp.bfloat16)
    return (value_proj, resid_grad, weight_grad, gain_grad)


def solution(mesh):
    placed = (
        P(("rep", "tp"), None),
        P(("rep", "tp")),
        P(("rep", "tp"), None),
        P(("rep", "tp"), None),
        P(("rep", "tp")),
        P("tp", "rep"),
        P("tp", "rep"),
        P("tp", "rep"),
        P("rep"),
        P(),
    )
    return jax.shard_map(
        per_device,
        mesh=mesh,
        in_specs=placed,
        out_specs=(
            P(("rep", "tp"), None),
            P(("rep", "tp"), None),
            P(("rep", "tp"), None),
            P(("rep", "tp")),
        ),
        check_vma=False,
    )
```

time: 524 us -> 204 us (0.39)
  waiting for transfers between devices: 288 us -> 99.2 us
  blocking collectives: 160 us -> 0 us
  matrix products: 38.8 us -> 22.5 us
  Pallas kernels: 0 us -> 15.8 us
  starting transfers between devices: 0.08 us -> 14.6 us
  local copies, waits for them, and re-layouts: 2.72 us -> 10.9 us
    reduce_scatter x1 -> x0, waiting for transfers between devices: 287 us -> none  [per_device(): lax.psum_scatter(lax.dot_general(columns, scaled, (((0,), (0,)), ((), ())...]
    all_gather x4 -> x0, blocking collectives: 105 us -> none  [the longest x1 63.8 us: per_device(): gain_piece = lax.all_gather(norm_gain, ('rep', 'tp'), axis=0, tiled=True)]
    all_gather x1, waiting for transfers between devices: 0.02 us -> 63.4 us  [per_device(): weight = lax.all_gather(gained, ('rep', 'tp'), axis=0, tiled=True)]
    unnamed x1 -> x0, blocking collectives: 42.4 us -> none
    ppermute x0 -> x11, waiting for transfers between devices: none -> 35.7 us  [swap(): lax.ppermute(value, axis, shift_pairs(lax.axis_size(axis), stride, size,...]
    dot_general x3 -> x2, matrix products: 38.8 us -> 22.5 us  [the longest x1 11.5 us: per_device(): lax.dot_general(cot, weight, (((1,), (1,)), ((), ())), preferred_element_...]
    pallas_call x0 -> x5, Pallas kernels: none -> 15.8 us  [partial_grad(): pl.pallas_call(partial_kernel if other is None else partial_add_kernel, o...]
    ppermute x0 -> x11, starting transfers between devices: none -> 14.6 us  [swap(): lax.ppermute(value, axis, shift_pairs(lax.axis_size(axis), stride, size,...]
  transfers between devices with their start and end apart: 2 -> 12, of which waited for: 1 -> 6; matrix products, arithmetic and copies ran while one was open for 11% -> 13% of each run, Pallas kernels for 0% -> 4%
where the time goes in v1:
time: 204 us; the launch traced here: 202 us
  waiting for transfers between devices  99.2 us (49%)
  matrix products  22.5 us (11%)
  other arithmetic  21 us (10%)
  between operations  17.6 us (9%)
  Pallas kernels  15.8 us (8%)
  starting transfers between devices  14.6 us (7%)
  local copies, waits for them, and re-layouts  10.9 us (5%)
    all_gather x1, waiting for transfers between devices, per_device(): weight = lax.all_gather(gained, ('rep', 'tp'), axis=0, tiled=True)  63.4 us
    ppermute x11, waiting for transfers between devices, swap(): lax.ppermute(value, axis, shift_pairs(lax.axis_size(axis), stride, size,...  35.7 us
    pallas_call x5, Pallas kernels, partial_grad(): pl.pallas_call(partial_kernel if other is None else partial_add_kernel, o...  15.8 us
    ppermute x11, starting transfers between devices, swap(): lax.ppermute(value, axis, shift_pairs(lax.axis_size(axis), stride, size,...  14.6 us
    dot_general x1, matrix products, per_device(): lax.dot_general(cot, weight, (((1,), (1,)), ((), ())), preferred_element_...  11.5 us
    dot_general x1, matrix products, per_device(): value_acc = jnp.dot(residual, weight, preferred_element_type=jnp.float32)  11.1 us
    unnamed x18, local copies, waits for them, and re-layouts  10.2 us
    reduce_sum x1, other arithmetic, per_device(): jnp.mean(resid_wide * resid_wide, axis=1, keepdims=True) + EPS  5.1 us
  transfers between devices with their start and end apart: 12, of which 6 were waited for; matrix products, arithmetic and copies ran while one was open for 13% of the time, Pallas kernels for 4%

profile of v1, /device:TPU:0, one launch (start us, length us, event | category | flops | bytes accessed | tf_op | source)
XLA Modules:
  0.0 201.6 jit_solution(16361900488918997160)
XLA Ops:
  8.0 1.8 fusion.3
  10.5 0.7 maximum_bitcast_fusion
  11.2 5.0 %collective-permute-start.2 = (f32[52,128]{1,0:T(8,128)S(1)}, f32[52,128]{1,0:T(8,128)S(1)}, u32[]{:S(2)}, u32[]{:S(2)}) collective-permute-start(f32[52,128]{1,0:T(8,128)S(1)} %maximum_bitcast_fusion), channel_id=1, source_target_pairs={{0,3},{1,0},{2,1},{3,2},{4,7},{5,4},{6,5},{7,6},{8,11},{9,8},{10,9... | collective-permute-start | bytes 79880 | tf_op jit(solution)/shard_map/ppermute | solution.py:26
  16.3 1.0 collective-permute-start
  17.3 5.1 %fusion = f32[512]{0:T(512)S(1)} fusion(bf16[512,8192]{1,0:T(8,128)(2,1)} %resid_ref.9), kind=kLoop, calls=%fused_computation.2 | loop fusion | flops 12582400 | bytes 8390656 | tf_op jit(solution)/shard_map/reduce_sum | solution.py:135
  23.8 1.4 fusion.24
  28.5 63.4 %all-gather.2.cloned.1.call-done = bf16[8192,512]{1,0:T(8,128)(2,1)} async-done(((bf16[256,512]{1,0:T(8,128)(2,1)}), bf16[8192,512]{1,0:T(8,128)(2,1)}) %all-gather.2.cloned.1.call-update) | async-done | bytes 8388624 | tf_op jit(solution)/shard_map/all_gather | solution.py:121
  91.9 11.1 %multiply_reduce_fusion = (f32[512]{0:T(512)S(1)}, bf16[512,512]{1,0:T(8,128)(2,1)S(1)}, bf16[512,512]{1,0:T(8,128)(2,1)}) fusion(bf16[512,512]{1,0:T(8,128)(2,1)S(1)} %copy-done.7, f32[512]{0:T(512)S(1)} %get-tuple-element.27, f32[512]{0:T(512)S(1)} %get-tuple-element.28, bf16[512,8192]{1,0:T(8,128)(2,1)} %resid_ref.9, ...), kind=kOutput, calls=%fused_computation.10 | convolution fusion | flops 4297063936 | bytes 18356224 | tf_op jit(solution)/shard_map/dot_general | solution.py:179
  103.0 3.4 %copy-done = bf16[512,8192]{1,0:T(8,128)(2,1)S(1)} copy-done((bf16[512,8192]{1,0:T(8,128)(2,1)S(1)}, bf16[512,8192]{1,0:T(8,128)(2,1)}, u32[]{:S(2)}) %copy-start) | copy-done | bytes 8388632
  106.3 5.0 %shard_map.129 = bf16[4,1024,512]{2,1,0:T(8,128)(2,1)} custom-call(s32[4]{0:T(128)S(1)} %multiply_add_fusion.3.blocks_ref, s32[4]{0:T(128)S(1)} %iota.28.places_ref, bf16[512,8192]{1,0:T(8,128)(2,1)S(1)} %copy-done, bf16[512,512]{1,0:T(8,128)(2,1)S(1)} %get-tuple-element.17.cot_ref), custom_call_target="tpu_custom_call" | custom-call | flops 2147483648 | bytes 12582912 | tf_op jit(solution)/shard_map/pallas_call | solution.py:55
  111.6 7.2 %collective-permute-done.3.other_ref = bf16[4,1024,512]{2,1,0:T(8,128)(2,1)} collective-permute-done((bf16[4,1024,512]{2,1,0:T(8,128)(2,1)}, bf16[4,1024,512]{2,1,0:T(8,128)(2,1)}, u32[]{:S(2)}, u32[]{:S(2)}) %collective-permute-start.3) | collective-permute-done | bytes 4194336 | tf_op jit(solution)/shard_map/ppermute | solution.py:26
  118.8 3.4 %copy-done.1 = bf16[512,8192]{1,0:T(8,128)(2,1)S(1)} copy-done((bf16[512,8192]{1,0:T(8,128)(2,1)S(1)}, bf16[512,8192]{1,0:T(8,128)(2,1)}, u32[]{:S(2)}) %copy-start.1) | copy-done | bytes 8388632
  122.2 2.7 %shard_map.131 = bf16[2,1024,256]{2,1,0:T(8,128)(2,1)S(1)} custom-call(s32[2]{0:T(128)S(1)} %get-tuple-element.10.blocks_ref, s32[2]{0:T(128)S(1)} %get-tuple-element.11.places_ref, bf16[512,8192]{1,0:T(8,128)(2,1)S(1)} %copy-done.1, bf16[512,512]{1,0:T(8,128)(2,1)S(1)} %get-tuple-element.17.cot_ref, bf16[4,1024,512]{2,1,0:T(8,128)(2,1)} %collective-permute-done.3.other_ref), custom_call_target="tpu_custom_call" | custom-call | flops 536870912 | bytes 4194304 | tf_op jit(solution)/shard_map/pallas_call | solution.py:55
  124.9 1.5 collective-permute-start.4
  126.5 2.7 %shard_map.133 = bf16[2,1024,256]{2,1,0:T(8,128)(2,1)S(1)} custom-call(s32[2]{0:T(128)S(1)} %get-tuple-element.14.blocks_ref, s32[2]{0:T(128)S(1)} %get-tuple-element.15.places_ref, bf16[512,8192]{1,0:T(8,128)(2,1)S(1)} %copy-done.1, bf16[512,512]{1,0:T(8,128)(2,1)S(1)} %get-tuple-element.17.cot_ref, bf16[4,1024,512]{2,1,0:T(8,128)(2,1)} %collective-permute-done.3.other_ref), custom_call_target="tpu_custom_call" | custom-call | flops 536870912 | bytes 4194304 | tf_op jit(solution)/shard_map/pallas_call | solution.py:55
  129.9 3.4 %copy-done.2 = bf16[512,8192]{1,0:T(8,128)(2,1)S(1)} copy-done((bf16[512,8192]{1,0:T(8,128)(2,1)S(1)}, bf16[512,8192]{1,0:T(8,128)(2,1)}, u32[]{:S(2)}) %copy-start.2) | copy-done | bytes 8388632
  133.2 2.7 %shard_map.130 = bf16[2,1024,256]{2,1,0:T(8,128)(2,1)S(1)} custom-call(s32[2]{0:T(128)S(1)} %get-tuple-element.31.blocks_ref, s32[2]{0:T(128)S(1)} %get-tuple-element.32.places_ref, bf16[512,8192]{1,0:T(8,128)(2,1)S(1)} %copy-done.2, bf16[512,512]{1,0:T(8,128)(2,1)S(1)} %get-tuple-element.17.cot_ref, bf16[4,1024,512]{2,1,0:T(8,128)(2,1)} %collective-permute-done.3.other_ref), custom_call_target="tpu_custom_call" | custom-call | flops 536870912 | bytes 4194304 | tf_op jit(solution)/shard_map/pallas_call | solution.py:55
  136.0 14.4 %collective-permute-done.4 = bf16[2,1024,256]{2,1,0:T(8,128)(2,1)} collective-permute-done((bf16[2,1024,256]{2,1,0:T(8,128)(2,1)S(1)}, bf16[2,1024,256]{2,1,0:T(8,128)(2,1)}, u32[]{:S(2)}, u32[]{:S(2)}) %collective-permute-start.4) | collective-permute-done | bytes 1048608 | tf_op jit(solution)/shard_map/ppermute | solution.py:26
  150.4 1.2 fusion.5
  151.6 1.5 collective-permute-start.5
  153.2 2.7 %shard_map.132 = bf16[2,1024,256]{2,1,0:T(8,128)(2,1)S(1)} custom-call(s32[2]{0:T(128)S(1)} %get-tuple-element.29.blocks_ref, s32[2]{0:T(128)S(1)} %get-tuple-element.30.places_ref, bf16[512,8192]{1,0:T(8,128)(2,1)S(1)} %copy-done.2, bf16[512,512]{1,0:T(8,128)(2,1)S(1)} %get-tuple-element.17.cot_ref, bf16[4,1024,512]{2,1,0:T(8,128)(2,1)} %collective-permute-done.3.other_ref), custom_call_target="tpu_custom_call" | custom-call | flops 536870912 | bytes 4194304 | tf_op jit(solution)/shard_map/pallas_call | solution.py:55
  155.9 1.2 fusion.6
  157.7 7.8 %collective-permute-done.5 = bf16[1024,256]{1,0:T(8,128)(2,1)S(1)} collective-permute-done((bf16[1024,256]{1,0:T(8,128)(2,1)S(1)}, bf16[1024,256]{1,0:T(8,128)(2,1)S(1)}, u32[]{:S(2)}, u32[]{:S(2)}) %collective-permute-start.5) | collective-permute-done | bytes 524320 | tf_op jit(solution)/shard_map/ppermute | solution.py:26
  165.5 1.3 bitcast_add_fusion.1
  166.9 3.3 %collective-permute-done.7 = bf16[1024,256]{1,0:T(8,128)(2,1)S(1)} collective-permute-done((bf16[1024,256]{1,0:T(8,128)(2,1)S(1)}, bf16[1024,256]{1,0:T(8,128)(2,1)S(1)}, u32[]{:S(2)}, u32[]{:S(2)}) %collective-permute-start.7) | collective-permute-done | bytes 524320 | tf_op jit(solution)/shard_map/ppermute | solution.py:26
  170.1 1.3 bitcast_add_fusion
  171.5 0.8 pad_maximum_fusion.1
  172.3 1.9 collective-permute-start.9
  174.9 2.0 collective-permute-start.10
  177.6 11.5 %fusion.2 = bf16[512,8192]{1,0:T(8,128)(2,1)} fusion(bf16[512,8192]{1,0:T(8,128)(2,1)} %resid_ref.9, bf16[512,512]{1,0:T(8,128)(2,1)S(1)} %get-tuple-element.17.cot_ref, bf16[8192,512]{1,0:T(8,128)(2,1)} %all-gather.2.cloned.1.call-done, f32[512]{0:T(512)S(1)} %multiply_multiply_fusion), kind=kOutput, calls=%fused_computation.4 | convolution fusion | flops 4311744512 | bytes 25692160 | tf_op jit(solution)/shard_map/dot_general | solution.py:183
  189.2 3.0 %collective-permute-done.9 = bf16[256,512]{1,0:T(8,128)(2,1)S(1)} collective-permute-done((bf16[256,512]{1,0:T(8,128)(2,1)}, bf16[256,512]{1,0:T(8,128)(2,1)S(1)}, u32[]{:S(2)}, u32[]{:S(2)}) %collective-permute-start.9) | collective-permute-done | bytes 262176 | tf_op jit(solution)/shard_map/ppermute | solution.py:26
  192.2 2.5 %fusion.4 = (f32[256]{0:T(256)}, f32[256,512]{1,0:T(8,128)}) fusion(bf16[256,512]{1,0:T(8,128)(2,1)S(1)} %copy-done.3, bf16[256,512]{1,0:T(8,128)(2,1)S(1)} %collective-permute-done.10, bf16[256,512]{1,0:T(8,128)(2,1)S(1)} %collective-permute-done.9, bf16[256,512]{1,0:T(8,128)(2,1)} %collective-permute-done.8, f32[256,256]{1,0:T(8,128)S(1)} %constant_dynamic-slice_fusion, ...), kind=kLoop, calls=%fused_computation.16 | loop fusion | flops 1441536 | bytes 2099200 | tf_op jit(solution)/shard_map/reduce_sum | solution.py:177
  (44 shorter events, 6.2 us)
Async XLA Ops:
  7.2 16.6 %copy-start.6 = (f32[512]{0:T(512)S(1)}, f32[512]{0:T(512)}, u32[]{:S(2)}) copy-start(f32[512]{0:T(512)} %param.14) | copy-start | bytes 6148
  7.2 16.6 %copy-start.4 = (f32[1,2048]{1,0:T(1,128)S(1)}, f32[1,2048]{1,0:T(1,128)}, u32[]{:S(2)}) copy-start(f32[1,2048]{1,0:T(1,128)} %param.16) | copy-start | bytes 24580
  7.2 16.6 %copy-start.5 = (f32[1,2048]{1,0:T(1,128)S(1)}, f32[1,2048]{1,0:T(1,128)}, u32[]{:S(2)}) copy-start(f32[1,2048]{1,0:T(1,128)} %param.15) | copy-start | bytes 24580
  7.2 15.2 %copy-start.8 = (s32[8]{0:T(128)S(1)}, s32[8]{0:T(128)}, u32[]{:S(2)}) copy-start(s32[8]{0:T(128)} %param.19) | copy-start | bytes 100
  7.2 84.7 %copy-start.7 = (bf16[512,512]{1,0:T(8,128)(2,1)S(1)}, bf16[512,512]{1,0:T(8,128)(2,1)}, u32[]{:S(2)}) copy-start(bf16[512,512]{1,0:T(8,128)(2,1)} %param.13) | copy-start | bytes 1572868
  7.2 84.7 %all-gather.2.cloned.1.call-start = ((), (), s32[]{:S(2)}) async-start(), calls=%async_computation | async-start | bytes 8650752 | tf_op jit(solution)/shard_map/all_gather | solution.py:121
  11.2 12.5 %collective-permute-start.2 = (f32[52,128]{1,0:T(8,128)S(1)}, f32[52,128]{1,0:T(8,128)S(1)}, u32[]{:S(2)}, u32[]{:S(2)}) collective-permute-start(f32[52,128]{1,0:T(8,128)S(1)} %maximum_bitcast_fusion), channel_id=1, source_target_pairs={{0,3},{1,0},{2,1},{3,2},{4,7},{5,4},{6,5},{7,6},{8,11},{9,8},{10,9... | collective-permute-start | bytes 79880 | tf_op jit(solution)/shard_map/ppermute | solution.py:26
  16.3 7.4 %collective-permute-start.1 = (f32[52,128]{1,0:T(8,128)S(1)}, f32[52,128]{1,0:T(8,128)S(1)}, u32[]{:S(2)}, u32[]{:S(2)}) collective-permute-start(f32[52,128]{1,0:T(8,128)S(1)} %maximum_bitcast_fusion), channel_id=1, source_target_pairs={{0,2},{1,3},{2,0},{3,1},{4,6},{5,7},{6,4},{7,5},{8,10},{9,11},{10,... | collective-permute-start | bytes 79880 | tf_op jit(solution)/shard_map/ppermute | solution.py:26
  16.3 7.4 %collective-permute-start = (f32[52,128]{1,0:T(8,128)S(1)}, f32[52,128]{1,0:T(8,128)S(1)}, u32[]{:S(2)}, u32[]{:S(2)}) collective-permute-start(f32[52,128]{1,0:T(8,128)S(1)} %maximum_bitcast_fusion), channel_id=1, source_target_pairs={{0,1},{1,2},{2,3},{3,0},{4,5},{5,6},{6,7},{7,4},{8,9},{9,10},{10,1... | collective-permute-start | bytes 79880 | tf_op jit(solution)/shard_map/ppermute | solution.py:26
  102.9 3.4 %copy-start = (bf16[512,8192]{1,0:T(8,128)(2,1)S(1)}, bf16[512,8192]{1,0:T(8,128)(2,1)}, u32[]{:S(2)}) copy-start(bf16[512,8192]{1,0:T(8,128)(2,1)} %resid_ref.9) | copy-start | bytes 25165828
  111.3 7.5 %collective-permute-start.3 = (bf16[4,1024,512]{2,1,0:T(8,128)(2,1)}, bf16[4,1024,512]{2,1,0:T(8,128)(2,1)}, u32[]{:S(2)}, u32[]{:S(2)}) collective-permute-start(bf16[4,1024,512]{2,1,0:T(8,128)(2,1)} %shard_map.129), channel_id=1, source_target_pairs={{0,4},{4,0},{8,12},{12,8},{16,20},{20,16},{24,28},{28,24},{1,5},{5... | collective-permute-start | bytes 12582920 | tf_op jit(solution)/shard_map/ppermute | solution.py:26
  118.8 3.4 %copy-start.1 = (bf16[512,8192]{1,0:T(8,128)(2,1)S(1)}, bf16[512,8192]{1,0:T(8,128)(2,1)}, u32[]{:S(2)}) copy-start(bf16[512,8192]{1,0:T(8,128)(2,1)} %resid_ref.9) | copy-start | bytes 25165828
  124.9 25.5 %collective-permute-start.4 = (bf16[2,1024,256]{2,1,0:T(8,128)(2,1)S(1)}, bf16[2,1024,256]{2,1,0:T(8,128)(2,1)}, u32[]{:S(2)}, u32[]{:S(2)}) collective-permute-start(bf16[2,1024,256]{2,1,0:T(8,128)(2,1)S(1)} %shard_map.131), channel_id=1, source_target_pairs={{0,8},{4,12},{8,0},{12,4},{16,24},{20,28},{24,16},{28,20},{1,9},{5... | collective-permute-start | bytes 3145736 | tf_op jit(solution)/shard_map/ppermute | solution.py:26
  129.2 26.7 %collective-permute-start.6 = (bf16[2,1024,256]{2,1,0:T(8,128)(2,1)S(1)}, bf16[2,1024,256]{2,1,0:T(8,128)(2,1)}, u32[]{:S(2)}, u32[]{:S(2)}) collective-permute-start(bf16[2,1024,256]{2,1,0:T(8,128)(2,1)S(1)} %shard_map.133), channel_id=1, source_target_pairs={{0,16},{4,20},{8,24},{12,28},{16,0},{20,4},{24,8},{28,12},{1,17},{... | collective-permute-start | bytes 3145736 | tf_op jit(solution)/shard_map/ppermute | solution.py:26
  129.9 3.4 %copy-start.2 = (bf16[512,8192]{1,0:T(8,128)(2,1)S(1)}, bf16[512,8192]{1,0:T(8,128)(2,1)}, u32[]{:S(2)}) copy-start(bf16[512,8192]{1,0:T(8,128)(2,1)} %resid_ref.9) | copy-start | bytes 25165828
  151.6 13.9 %collective-permute-start.5 = (bf16[1024,256]{1,0:T(8,128)(2,1)S(1)}, bf16[1024,256]{1,0:T(8,128)(2,1)S(1)}, u32[]{:S(2)}, u32[]{:S(2)}) collective-permute-start(bf16[1024,256]{1,0:T(8,128)(2,1)S(1)} %fusion.5), channel_id=1, source_target_pairs={{0,16},{4,20},{8,24},{12,28},{16,0},{20,4},{24,8},{28,12},{1,17},{... | collective-permute-start | bytes 1572872 | tf_op jit(solution)/shard_map/ppermute | solution.py:26
  157.1 13.1 %collective-permute-start.7 = (bf16[1024,256]{1,0:T(8,128)(2,1)S(1)}, bf16[1024,256]{1,0:T(8,128)(2,1)S(1)}, u32[]{:S(2)}, u32[]{:S(2)}) collective-permute-start(bf16[1024,256]{1,0:T(8,128)(2,1)S(1)} %fusion.6), channel_id=1, source_target_pairs={{0,8},{4,12},{8,0},{12,4},{16,24},{20,28},{24,16},{28,20},{1,9},{5... | collective-permute-start | bytes 1572872 | tf_op jit(solution)/shard_map/ppermute | solution.py:26
  172.3 19.9 %collective-permute-start.9 = (bf16[256,512]{1,0:T(8,128)(2,1)}, bf16[256,512]{1,0:T(8,128)(2,1)S(1)}, u32[]{:S(2)}, u32[]{:S(2)}) collective-permute-start(bf16[256,512]{1,0:T(8,128)(2,1)} %pad_maximum_fusion.1), channel_id=1, source_target_pairs={{0,2},{1,3},{2,0},{3,1},{4,6},{5,7},{6,4},{7,5},{8,10},{9,11},{10,... | collective-permute-start | bytes 786440 | tf_op jit(solution)/shard_map/ppermute | solution.py:26
  174.9 17.3 %collective-permute-start.10 = (bf16[256,512]{1,0:T(8,128)(2,1)}, bf16[256,512]{1,0:T(8,128)(2,1)S(1)}, u32[]{:S(2)}, u32[]{:S(2)}) collective-permute-start(bf16[256,512]{1,0:T(8,128)(2,1)} %pad_maximum_fusion.2), channel_id=1, source_target_pairs={{0,3},{1,0},{2,1},{3,2},{4,7},{5,4},{6,5},{7,6},{8,11},{9,8},{10,9... | collective-permute-start | bytes 786440 | tf_op jit(solution)/shard_map/ppermute | solution.py:26
  177.6 14.6 %copy-start.3 = (bf16[256,512]{1,0:T(8,128)(2,1)S(1)}, bf16[256,512]{1,0:T(8,128)(2,1)}, u32[]{:S(2)}) copy-start(bf16[256,512]{1,0:T(8,128)(2,1)} %param.12) | copy-start | bytes 786436
  177.6 14.6 %collective-permute-start.8 = (bf16[256,512]{1,0:T(8,128)(2,1)}, bf16[256,512]{1,0:T(8,128)(2,1)}, u32[]{:S(2)}, u32[]{:S(2)}) collective-permute-start(bf16[256,512]{1,0:T(8,128)(2,1)} %pad_maximum_fusion), channel_id=1, source_target_pairs={{0,1},{1,2},{2,3},{3,0},{4,5},{5,6},{6,7},{7,4},{8,9},{9,10},{10,1... | collective-permute-start | bytes 786440 | tf_op jit(solution)/shard_map/ppermute | solution.py:26
Sparse Core Ops, SparseCore 0:
  11.6 80.2 all-gather.1

commit v2 on v1

--- a/solution.py
+++ b/solution.py
@@ -14,16 +14,9 @@
 OUTER = 2
 
 
-def shift_pairs(count, stride, size, step):
-    pairs = []
-    for place in range(count):
-        digit = (place // stride) % size
-        pairs.append((place, place + ((digit + step) % size - digit) * stride))
-    return pairs
-
-
-def swap(value, axis, stride, size, step):
-    return lax.ppermute(value, axis, shift_pairs(lax.axis_size(axis), stride, size, step))
+def swap(value, axis, step):
+    size = lax.axis_size(axis)
+    return lax.ppermute(value, axis, [(place, (place + step) % size) for place in range(size)])
 
 
 def partial_kernel(blocks_ref, places_ref, resid_ref, cot_ref, out_ref):
@@ -70,11 +63,122 @@
     )(blocks, places, *operands)
 
 
+def value_kernel(core_ref, resid_ref, own_ref, other_ref, cot_ref, inv_ref, value_ref, coef_ref, total_ref):
+    step = pl.program_id(0)
+    count = pl.num_programs(0)
+
+    @pl.when(step == 0)
+    def _():
+        total_ref[...] = jnp.zeros_like(total_ref)
+
+    @pl.when(step < count // 2)
+    def _():
+        total_ref[...] += jnp.dot(resid_ref[...], own_ref[0], preferred_element_type=jnp.float32)
+
+    @pl.when(step >= count // 2)
+    def _():
+        total_ref[...] += jnp.dot(resid_ref[...], other_ref[0], preferred_element_type=jnp.float32)
+
+    @pl.when(step == count - 1)
+    def _():
+        total = total_ref[...]
+        inv = inv_ref[...]
+        value_ref[...] = (total * inv).astype(value_ref.dtype)
+        share = jnp.sum(total * cot_ref[...].astype(jnp.float32), axis=1, keepdims=True)
+        width = resid_ref.shape[1] * count
+        coef_ref[...] = share * (inv * inv) * (1.0 / width)
+
+
+def weight_specs(chips, depth, features):
+    return [
+        pl.BlockSpec((1, depth, features), lambda i, c: (jnp.minimum(i, chips - 1), 0, 0)),
+        pl.BlockSpec((1, depth, features), lambda i, c: (jnp.maximum(i - chips, 0), 0, 0)),
+    ]
+
+
+def feature_block(chips):
+    return lambda i, c: (0, lax.rem(i, chips) * CORES + jnp.where(i < chips, c[0], 1 - c[0]))
+
+
+def value_product(core, residual, own, other, cot, inv_rms):
+    rows, width = residual.shape
+    chips, depth, features = own.shape
+    whole = lambda i, c: (0, 0)
+    return pl.pallas_call(
+        value_kernel,
+        out_shape=(
+            jax.ShapeDtypeStruct((rows, features), jnp.bfloat16),
+            jax.ShapeDtypeStruct((rows, 1), jnp.float32),
+        ),
+        grid_spec=pltpu.PrefetchScalarGridSpec(
+            num_scalar_prefetch=1,
+            grid=(CORES * chips,),
+            in_specs=[pl.BlockSpec((rows, depth), feature_block(chips))]
+            + weight_specs(chips, depth, features)
+            + [pl.BlockSpec((rows, features), whole), pl.BlockSpec((rows, 1), whole)],
+            out_specs=(pl.BlockSpec((rows, features), whole), pl.BlockSpec((rows, 1), whole)),
+            scratch_shapes=[pltpu.VMEM((rows, features), jnp.float32)],
+        ),
+        cost_estimate=pl.CostEstimate(
+            flops=2 * rows * width * features,
+            bytes_accessed=2 * width * (rows + features),
+            transcendentals=0,
+        ),
+        compiler_params=pltpu.CompilerParams(vmem_limit_bytes=40 * 1024 * 1024),
+    )(core, residual, own, other, cot, inv_rms)
+
+
+def grad_kernel(core_ref, cot_ref, coef_ref, resid_ref, own_ref, other_ref, out_ref):
+    step = pl.program_id(0)
+    count = pl.num_programs(0)
+
+    def write(weight):
+        grad = lax.dot_general(
+            cot_ref[...], weight, (((1,), (1,)), ((), ())), preferred_element_type=jnp.float32
+        )
+        out_ref[...] = (grad - resid_ref[...].astype(jnp.float32) * coef_ref[...]).astype(out_ref.dtype)
+
+    @pl.when(step < count // 2)
+    def _():
+        write(own_ref[0])
+
+    @pl.when(step >= count // 2)
+    def _():
+        write(other_ref[0])
+
+
+def residual_grad(core, cot, coefficient, residual, own, other):
+    rows, width = residual.shape
+    chips, depth, features = own.shape
+    whole = lambda i, c: (0, 0)
+    return pl.pallas_call(
+        grad_kernel,
+        out_shape=jax.ShapeDtypeStruct((rows, width), jnp.bfloat16),
+        grid_spec=pltpu.PrefetchScalarGridSpec(
+            num_scalar_prefetch=1,
+            grid=(CORES * chips,),
+            in_specs=[
+                pl.BlockSpec((rows, features), whole),
+                pl.BlockSpec((rows, 1), whole),
+                pl.BlockSpec((rows, depth), feature_block(chips)),
+            ]
+            + weight_specs(chips, depth, features),
+            out_specs=pl.BlockSpec((rows, depth), feature_block(chips)),
+        ),
+        cost_estimate=pl.CostEstimate(
+            flops=2 * rows * width * features,
+            bytes_accessed=2 * width * (2 * rows + features),
+            transcendentals=0,
+        ),
+        compiler_params=pltpu.CompilerParams(vmem_limit_bytes=40 * 1024 * 1024),
+    )(core, cot, coefficient, residual, own, other)
+
+
 def sequence_weight(trainee_logp, shard_max, shard_sum, owned, seq_length, rep_count, tp_count, tp_place):
     rows_here = trainee_logp.shape[0]
     seq = shard_max.shape[0]
     packed = jnp.concatenate([shard_max, shard_sum, owned, trainee_logp]).reshape(-1, 128)
-    shares = [packed] + [swap(packed, "tp", 1, tp_count, s) for s in range(1, tp_count)]
+    shares = [packed] + [swap(packed, "tp", s) for s in range(1, tp_count)]
     shares = [share.reshape(-1) for share in shares]
     top_max = functools.reduce(jnp.maximum, [share[:seq] for share in shares])
     sum_exp = sum(share[seq : 2 * seq] * jnp.exp(share[:seq] - top_max) for share in shares)
@@ -106,19 +210,21 @@
     features = value_cot.shape[1]
     half = features // 2
     tp_count = lax.axis_size("tp")
-    rep_count = lax.axis_size("rep")
+    outer, inner = lax.axis_size("outer"), lax.axis_size("inner")
+    rep_count = outer * inner * CORES
     tp_place = lax.axis_index("tp")
-    rep_place = lax.axis_index("rep")
-    outer, inner = OUTER, rep_count // (OUTER * CORES)
+    core = lax.axis_index("core")
+    at_inner = lax.axis_index("inner")
+    at_outer = lax.axis_index("outer")
+    rep_place = (at_outer * inner + at_inner) * CORES + core
     depth = width // rep_count
     own_rows = depth // tp_count
-    core = lax.rem(rep_place, CORES)
-    at_inner = lax.rem(rep_place // CORES, inner)
-    at_outer = rep_place // (CORES * inner)
 
     gain_wide = norm_gain.astype(jnp.float32)[:, None]
     gained = (value_weight.astype(jnp.float32) * gain_wide).astype(jnp.bfloat16)
-    weight = lax.all_gather(gained, ("rep", "tp"), axis=0, tiled=True)
+    residual, gained = lax.optimization_barrier((residual, gained))
+    own_weight = lax.all_gather(gained, ("outer", "inner", "tp"), axis=0, tiled=True)
+    own_weight = own_weight.reshape(outer * inner, depth, features)
 
     owned = jnp.where(
         target_ids // (VOCAB // tp_count) == tp_place,
@@ -137,7 +243,7 @@
 
     chips = jnp.arange(outer * inner, dtype=jnp.int32)
     theirs = partial_grad(residual, cot, 0, features, chips * CORES + (1 - core), chips, depth, None)
-    other = swap(theirs, "rep", 1, CORES, 1)
+    other = swap(theirs, "core", 1)
 
     def block_at(step_outer, step_inner):
         return lax.rem(at_outer + step_outer, outer) * inner + lax.rem(at_inner + step_inner, inner)
@@ -150,16 +256,16 @@
         return sum(part.astype(jnp.float32) for part in parts)
 
     sent_a = [own_blocks(0, [(o, s) for o in range(outer)]) for s in range(1, inner)]
-    got_a = [swap(x, "rep", CORES, inner, s + 1) for s, x in enumerate(sent_a)]
+    got_a = [swap(x, "inner", s + 1) for s, x in enumerate(sent_a)]
     sent_b = [own_blocks(half, [(s, i) for i in range(inner)]) for s in range(1, outer)]
-    got_b = [swap(x, "rep", CORES * inner, outer, s + 1) for s, x in enumerate(sent_b)]
+    got_b = [swap(x, "outer", s + 1) for s, x in enumerate(sent_b)]
     kept_a = own_blocks(0, [(o, 0) for o in range(outer)])
     kept_b = own_blocks(half, [(0, i) for i in range(inner)])
 
     sent_a = [widen([kept_a[o]] + [g[o] for g in got_a]).astype(jnp.bfloat16) for o in range(1, outer)]
-    next_a = [swap(x, "rep", CORES * inner, outer, s + 1) for s, x in enumerate(sent_a)]
+    next_a = [swap(x, "outer", s + 1) for s, x in enumerate(sent_a)]
     sent_b = [widen([kept_b[i]] + [g[i] for g in got_b]).astype(jnp.bfloat16) for i in range(1, inner)]
-    next_b = [swap(x, "rep", CORES, inner, s + 1) for s, x in enumerate(sent_b)]
+    next_b = [swap(x, "inner", s + 1) for s, x in enumerate(sent_b)]
     chip_a = widen([kept_a[0]] + [g[0] for g in got_a] + next_a)
     chip_b = widen([kept_b[0]] + [g[0] for g in got_b] + next_b)
 
@@ -170,45 +276,46 @@
         )
 
     last = [
-        swap(rows_for(s).astype(jnp.bfloat16), "tp", 1, tp_count, s) for s in range(1, tp_count)
+        swap(rows_for(s).astype(jnp.bfloat16), "tp", s) for s in range(1, tp_count)
     ]
     unit_grad_rows = rows_for(0) + widen(last)
-    weight_grad = gain_wide * unit_grad_rows
+    norm_gain, value_weight, unit_grad_rows = lax.optimization_barrier(
+        (norm_gain, value_weight, unit_grad_rows)
+    )
+    weight_grad = norm_gain.astype(jnp.float32)[:, None] * unit_grad_rows
     gain_grad = jnp.sum(value_weight.astype(jnp.float32) * unit_grad_rows, axis=1)
 
-    value_acc = jnp.dot(residual, weight, preferred_element_type=jnp.float32)
-    value_proj = (inv_rms * value_acc).astype(jnp.bfloat16)
-    share = jnp.sum(cot.astype(jnp.float32) * value_acc, axis=1, keepdims=True)
-    coefficient = inv_rms * inv_rms * share * (1.0 / width)
-    normed_grad = lax.dot_general(
-        cot, weight, (((1,), (1,)), ((), ())), preferred_element_type=jnp.float32
-    )
-    resid_grad = (normed_grad - residual.astype(jnp.float32) * coefficient).astype(jnp.bfloat16)
+    own_weight, _ = lax.optimization_barrier((own_weight, (sent_a, sent_b)))
+    other_weight = swap(own_weight, "core", 1)
+    core_arg = core.astype(jnp.int32).reshape(1)
+    value_proj, coefficient = value_product(core_arg, residual, own_weight, other_weight, cot, inv_rms)
+    resid_grad = residual_grad(core_arg, cot, coefficient, residual, own_weight, other_weight)
     return (value_proj, resid_grad, weight_grad, gain_grad)
 
 
 def solution(mesh):
-    placed = (
-        P(("rep", "tp"), None),
-        P(("rep", "tp")),
-        P(("rep", "tp"), None),
-        P(("rep", "tp"), None),
-        P(("rep", "tp")),
-        P("tp", "rep"),
-        P("tp", "rep"),
-        P("tp", "rep"),
-        P("rep"),
-        P(),
-    )
+    rep_count, tp_count = mesh.shape["rep"], mesh.shape["tp"]
+    split = jax.sharding.Mesh(
+        mesh.devices.reshape(OUTER, rep_count // (OUTER * CORES), CORES, tp_count),
+        ("outer", "inner", "core", "tp"),
+    )
+    rep = ("outer", "inner", "core")
+    rows = rep + ("tp",)
     return jax.shard_map(
         per_device,
-        mesh=mesh,
-        in_specs=placed,
-        out_specs=(
-            P(("rep", "tp"), None),
-            P(("rep", "tp"), None),
-            P(("rep", "tp"), None),
-            P(("rep", "tp")),
-        ),
+        mesh=split,
+        in_specs=(
+            P(rows, None),
+            P(rows),
+            P(rows, None),
+            P(rows, None),
+            P(rows),
+            P("tp", rep),
+            P("tp", rep),
+            P("tp", rep),
+            P(rep),
+            P(),
+        ),
+        out_specs=(P(rows, None), P(rows, None), P(rows, None), P(rows)),
         check_vma=False,
     )

time: 204 us -> 182 us (0.89)
  waiting for transfers between devices: 99.2 us -> 75.6 us
  Pallas kernels: 15.8 us -> 38.8 us
  matrix products: 22.5 us -> 0 us
    all_gather x1, waiting for transfers between devices: 63.4 us -> 9.1 us  [per_device(): lax.all_gather(gained, ('outer', 'inner', 'tp'), axis=0, tiled=True)]
    ppermute x11 -> x12, waiting for transfers between devices: 35.7 us -> 66.5 us  [swap(): lax.ppermute(value, axis, [(place, (place + step) % size) for place in ra...]
    pallas_call x0 -> x2, Pallas kernels: none -> 23 us  [the longest x1 12.1 us: residual_grad(): pl.pallas_call(grad_kernel, out_shape=jax.ShapeDtypeStruct((rows, width),...]
    dot_general x2 -> x0, matrix products: 22.5 us -> none  [the longest x1 11.5 us: per_device(): lax.dot_general(cot, weight, (((1,), (1,)), ((), ())), preferred_element_...]
    ppermute x11 -> x12, starting transfers between devices: 14.6 us -> 15.1 us  [swap(): lax.ppermute(value, axis, [(place, (place + step) % size) for place in ra...]
    unnamed x18 -> x26, local copies, waits for them, and re-layouts: 10.2 us -> 9.99 us
  transfers between devices with their start and end apart: 12 -> 13, of which waited for: 6 -> 6; matrix products, arithmetic and copies ran while one was open for 13% -> 11% of each run, Pallas kernels for 4% -> 9%
where the time goes in v2:
time: 182 us; the launch traced here: 179 us
  waiting for transfers between devices  75.6 us (42%)
  Pallas kernels  38.8 us (21%)
  other arithmetic  19.5 us (11%)
  between operations  17.7 us (10%)
  starting transfers between devices  15.1 us (8%)
  local copies, waits for them, and re-layouts  11.8 us (6%)
    ppermute x12, waiting for transfers between devices, swap(): lax.ppermute(value, axis, [(place, (place + step) % size) for place in ra...  66.5 us
    pallas_call x5, Pallas kernels, partial_grad(): pl.pallas_call(partial_kernel if other is None else partial_add_kernel, o...  15.8 us
    ppermute x12, starting transfers between devices, swap(): lax.ppermute(value, axis, [(place, (place + step) % size) for place in ra...  15.1 us
    pallas_call x1, Pallas kernels, residual_grad(): pl.pallas_call(grad_kernel, out_shape=jax.ShapeDtypeStruct((rows, width),...  12.1 us
    pallas_call x1, Pallas kernels, value_product(): pl.pallas_call(value_kernel, out_shape=(jax.ShapeDtypeStruct((rows, featu...  10.9 us
    unnamed x26, local copies, waits for them, and re-layouts  9.99 us
    all_gather x1, waiting for transfers between devices, per_device(): lax.all_gather(gained, ('outer', 'inner', 'tp'), axis=0, tiled=True)  9.1 us
    reduce_sum x1, other arithmetic, per_device(): jnp.mean(resid_wide * resid_wide, axis=1, keepdims=True) + EPS  5.1 us
  transfers between devices with their start and end apart: 13, of which 6 were waited for; matrix products, arithmetic and copies ran while one was open for 11% of the time, Pallas kernels for 9%

profile of v2, /device:TPU:0, one launch (start us, length us, event | category | flops | bytes accessed | tf_op | source)
XLA Modules:
  0.0 178.7 jit_solution(4456143453803597123)
XLA Ops:
  8.0 1.8 multiply_convert_fusion.1
  11.2 5.0 %collective-permute-start.2 = (f32[52,128]{1,0:T(8,128)S(1)}, f32[52,128]{1,0:T(8,128)S(1)}, u32[]{:S(2)}, u32[]{:S(2)}) collective-permute-start(f32[52,128]{1,0:T(8,128)S(1)} %maximum_bitcast_fusion), channel_id=1, source_target_pairs={{0,3},{1,0},{2,1},{3,2},{4,7},{5,4},{6,5},{7,6},{8,11},{9,8},{10,9... | collective-permute-start | bytes 79880 | tf_op jit(solution)/shard_map/ppermute | solution.py:19
  16.3 1.0 collective-permute-start
  17.3 5.1 %multiply_reduce_fusion = f32[512]{0:T(512)S(1)} fusion(bf16[512,8192]{1,0:T(8,128)(2,1)} %resid_ref.6), kind=kLoop, calls=%fused_computation | loop fusion | flops 12582400 | bytes 8390656 | tf_op jit(solution)/shard_map/reduce_sum | solution.py:241
  23.8 1.4 fusion.19
  28.7 3.4 %copy-done = bf16[512,8192]{1,0:T(8,128)(2,1)S(1)} copy-done((bf16[512,8192]{1,0:T(8,128)(2,1)S(1)}, bf16[512,8192]{1,0:T(8,128)(2,1)}, u32[]{:S(2)}) %copy-start) | copy-done | bytes 8388632
  32.1 5.0 %shard_map.129 = bf16[4,1024,512]{2,1,0:T(8,128)(2,1)} custom-call(s32[4]{0:T(128)S(1)} %multiply_add_fusion.3.blocks_ref, s32[4]{0:T(128)S(1)} %iota.28.places_ref, bf16[512,8192]{1,0:T(8,128)(2,1)S(1)} %copy-done, bf16[512,512]{1,0:T(8,128)(2,1)S(1)} %multiply_convert_fusion.cot_ref), custom_call_target="tpu_custom_call" | custom-call | flops 2147483648 | bytes 12582912 | tf_op jit(solution)/shard_map/pallas_call | solution.py:48
  37.2 7.4 %collective-permute-done.3.other_ref = bf16[4,1024,512]{2,1,0:T(8,128)(2,1)} collective-permute-done((bf16[4,1024,512]{2,1,0:T(8,128)(2,1)}, bf16[4,1024,512]{2,1,0:T(8,128)(2,1)}, u32[]{:S(2)}, u32[]{:S(2)}) %collective-permute-start.3) | collective-permute-done | bytes 4194336 | tf_op jit(solution)/shard_map/ppermute | solution.py:19
  44.6 3.4 %copy-done.1 = bf16[512,8192]{1,0:T(8,128)(2,1)S(1)} copy-done((bf16[512,8192]{1,0:T(8,128)(2,1)S(1)}, bf16[512,8192]{1,0:T(8,128)(2,1)}, u32[]{:S(2)}) %copy-start.1) | copy-done | bytes 8388632
  48.0 2.7 %shard_map.131 = bf16[2,1024,256]{2,1,0:T(8,128)(2,1)S(1)} custom-call(s32[2]{0:T(128)S(1)} %get-tuple-element.30.blocks_ref, s32[2]{0:T(128)S(1)} %get-tuple-element.31.places_ref, bf16[512,8192]{1,0:T(8,128)(2,1)S(1)} %copy-done.1, bf16[512,512]{1,0:T(8,128)(2,1)S(1)} %multiply_convert_fusion.cot_ref, bf16[4,1024,512]{2,1,0:T(8,128)(2,1)} %collective-permute-done.3.other_ref), custom_call_target="tpu_custom_call" | custom-call | flops 536870912 | bytes 4194304 | tf_op jit(solution)/shard_map/pallas_call | solution.py:48
  50.7 1.6 collective-permute-start.4
  52.4 2.7 %shard_map.133 = bf16[2,1024,256]{2,1,0:T(8,128)(2,1)S(1)} custom-call(s32[2]{0:T(128)S(1)} %get-tuple-element.26.blocks_ref, s32[2]{0:T(128)S(1)} %get-tuple-element.27.places_ref, bf16[512,8192]{1,0:T(8,128)(2,1)S(1)} %copy-done.1, bf16[512,512]{1,0:T(8,128)(2,1)S(1)} %multiply_convert_fusion.cot_ref, bf16[4,1024,512]{2,1,0:T(8,128)(2,1)} %collective-permute-done.3.other_ref), custom_call_target="tpu_custom_call" | custom-call | flops 536870912 | bytes 4194304 | tf_op jit(solution)/shard_map/pallas_call | solution.py:48
  55.1 1.6 collective-permute-start.5
  56.7 2.7 %shard_map.132 = bf16[2,1024,256]{2,1,0:T(8,128)(2,1)S(1)} custom-call(s32[2]{0:T(128)S(1)} %get-tuple-element.42.blocks_ref, s32[2]{0:T(128)S(1)} %get-tuple-element.43.places_ref, bf16[512,8192]{1,0:T(8,128)(2,1)S(1)} %copy-done.1, bf16[512,512]{1,0:T(8,128)(2,1)S(1)} %multiply_convert_fusion.cot_ref, bf16[4,1024,512]{2,1,0:T(8,128)(2,1)} %collective-permute-done.3.other_ref), custom_call_target="tpu_custom_call" | custom-call | flops 536870912 | bytes 4194304 | tf_op jit(solution)/shard_map/pallas_call | solution.py:48
  59.4 2.7 %shard_map.130 = bf16[2,1024,256]{2,1,0:T(8,128)(2,1)S(1)} custom-call(s32[2]{0:T(128)S(1)} %get-tuple-element.44.blocks_ref, s32[2]{0:T(128)S(1)} %get-tuple-element.45.places_ref, bf16[512,8192]{1,0:T(8,128)(2,1)S(1)} %copy-done.1, bf16[512,512]{1,0:T(8,128)(2,1)S(1)} %multiply_convert_fusion.cot_ref, bf16[4,1024,512]{2,1,0:T(8,128)(2,1)} %collective-permute-done.3.other_ref), custom_call_target="tpu_custom_call" | custom-call | flops 536870912 | bytes 4194304 | tf_op jit(solution)/shard_map/pallas_call | solution.py:48
  62.1 27.0 %collective-permute-done.4 = bf16[2,1024,256]{2,1,0:T(8,128)(2,1)S(1)} collective-permute-done((bf16[2,1024,256]{2,1,0:T(8,128)(2,1)S(1)}, bf16[2,1024,256]{2,1,0:T(8,128)(2,1)S(1)}, u32[]{:S(2)}, u32[]{:S(2)}) %collective-permute-start.4) | collective-permute-done | bytes 1048608 | tf_op jit(solution)/shard_map/ppermute | solution.py:19
  89.1 1.1 fusion
  90.2 4.8 %collective-permute-done.5 = bf16[2,1024,256]{2,1,0:T(8,128)(2,1)S(1)} collective-permute-done((bf16[2,1024,256]{2,1,0:T(8,128)(2,1)S(1)}, bf16[2,1024,256]{2,1,0:T(8,128)(2,1)S(1)}, u32[]{:S(2)}, u32[]{:S(2)}) %collective-permute-start.5) | collective-permute-done | bytes 1048608 | tf_op jit(solution)/shard_map/ppermute | solution.py:19
  95.0 1.0 copy-done.5
  96.1 9.1 %all-gather.2.cloned.1.call-done = bf16[4096,512]{1,0:T(8,128)(2,1)} async-done(((bf16[256,512]{1,0:T(8,128)(2,1)}), bf16[4096,512]{1,0:T(8,128)(2,1)}) %all-gather.2.cloned.1.call-update) | async-done | bytes 4194320 | tf_op jit(solution)/shard_map/all_gather | solution.py:226
  106.0 1.3 collective-permute-start.8
  107.2 12.6 %collective-permute-done.7 = bf16[1024,256]{1,0:T(8,128)(2,1)} collective-permute-done((bf16[1024,256]{1,0:T(8,128)(2,1)}, bf16[1024,256]{1,0:T(8,128)(2,1)}, u32[]{:S(2)}, u32[]{:S(2)}) %collective-permute-start.7) | collective-permute-done | bytes 524320 | tf_op jit(solution)/shard_map/ppermute | solution.py:19
  119.9 1.4 bitcast_add_fusion.1
  121.3 1.7 bitcast_add_fusion
  123.8 1.8 %collective-permute-start.10 = (bf16[256,512]{1,0:T(8,128)(2,1)}, bf16[256,512]{1,0:T(8,128)(2,1)S(1)}, u32[]{:S(2)}, u32[]{:S(2)}) collective-permute-start(bf16[256,512]{1,0:T(8,128)(2,1)} %pad_maximum_fusion.1), channel_id=1, source_target_pairs={{0,2},{1,3},{2,0},{3,1},{4,6},{5,7},{6,4},{7,5},{8,10},{9,11},{10,... | collective-permute-start | bytes 786440 | tf_op jit(solution)/shard_map/ppermute | solution.py:19
  126.3 1.8 %collective-permute-start.11 = (bf16[256,512]{1,0:T(8,128)(2,1)}, bf16[256,512]{1,0:T(8,128)(2,1)S(1)}, u32[]{:S(2)}, u32[]{:S(2)}) collective-permute-start(bf16[256,512]{1,0:T(8,128)(2,1)} %pad_maximum_fusion.2), channel_id=1, source_target_pairs={{0,3},{1,0},{2,1},{3,2},{4,7},{5,4},{6,5},{7,6},{8,11},{9,8},{10,9... | collective-permute-start | bytes 786440 | tf_op jit(solution)/shard_map/ppermute | solution.py:19
  129.2 1.0 constant_dynamic-slice_fusion.1
  130.2 14.7 %collective-permute-done.10 = bf16[256,512]{1,0:T(8,128)(2,1)S(1)} collective-permute-done((bf16[256,512]{1,0:T(8,128)(2,1)}, bf16[256,512]{1,0:T(8,128)(2,1)S(1)}, u32[]{:S(2)}, u32[]{:S(2)}) %collective-permute-start.10) | collective-permute-done | bytes 262176 | tf_op jit(solution)/shard_map/ppermute | solution.py:19
  145.1 1.5 multiply_reduce_fusion.1
  146.7 2.2 %copy-done.2 = bf16[4096,512]{1,0:T(8,128)(2,1)S(1)} copy-done((bf16[4096,512]{1,0:T(8,128)(2,1)S(1)}, bf16[4096,512]{1,0:T(8,128)(2,1)}, u32[]{:S(2)}) %copy-start.2) | copy-done | bytes 4194328
  148.8 10.9 %shard_map.134 = (bf16[512,512]{1,0:T(8,128)(2,1)}, f32[512,1]{1,0:T(8,128)S(1)}) custom-call(s32[1]{0:T(128)} %bitcast.core_ref, bf16[512,8192]{1,0:T(8,128)(2,1)} %resid_ref.6, bf16[4,1024,512]{2,1,0:T(8,128)(2,1)S(1)} %bitcast.104, bf16[4,1024,512]{2,1,0:T(8,128)(2,1)} %collective-permute-done.6.other_ref, ...), custom_call_target="tpu_custom_call" | custom-call | flops 4294967296 | bytes 16777216 | tf_op jit(solution)/shard_map/pallas_call | solution.py:107
  159.7 12.1 %shard_map.135 = bf16[512,8192]{1,0:T(8,128)(2,1)} custom-call(s32[1]{0:T(128)} %bitcast.core_ref, bf16[512,512]{1,0:T(8,128)(2,1)S(1)} %multiply_convert_fusion.cot_ref, f32[512,1]{1,0:T(8,128)S(1)} %get-tuple-element.16.coef_ref, bf16[512,8192]{1,0:T(8,128)(2,1)} %resid_ref.6, bf16[4,1024,512]{2,1,0:T(8,128)(2,1)S(1)} %bitcast.105, ...), custom_call_target="tpu_custom_call" | custom-call | flops 4294967296 | bytes 25165824 | tf_op jit(solution)/shard_map/pallas_call | solution.py:154
  (57 shorter events, 7.6 us)
Async XLA Ops:
  7.2 16.6 %copy-start.10 = (f32[512]{0:T(512)S(1)}, f32[512]{0:T(512)}, u32[]{:S(2)}) copy-start(f32[512]{0:T(512)} %param.14) | copy-start | bytes 6148
  7.2 16.6 %copy-start.8 = (f32[1,2048]{1,0:T(1,128)S(1)}, f32[1,2048]{1,0:T(1,128)}, u32[]{:S(2)}) copy-start(f32[1,2048]{1,0:T(1,128)} %param.16) | copy-start | bytes 24580
  7.2 16.6 %copy-start.9 = (f32[1,2048]{1,0:T(1,128)S(1)}, f32[1,2048]{1,0:T(1,128)}, u32[]{:S(2)}) copy-start(f32[1,2048]{1,0:T(1,128)} %param.15) | copy-start | bytes 24580
  7.2 15.2 %copy-start.11 = (s32[8]{0:T(128)S(1)}, s32[8]{0:T(128)}, u32[]{:S(2)}) copy-start(s32[8]{0:T(128)} %param.19) | copy-start | bytes 100
  7.2 21.3 %copy-start.7 = (bf16[512,512]{1,0:T(8,128)(2,1)S(1)}, bf16[512,512]{1,0:T(8,128)(2,1)}, u32[]{:S(2)}) copy-start(bf16[512,512]{1,0:T(8,128)(2,1)} %param.13) | copy-start | bytes 1572868
  7.2 98.0 %all-gather.2.cloned.1.call-start = ((), (), s32[]{:S(2)}) async-start(), calls=%async_computation | async-start | bytes 4456448 | tf_op jit(solution)/shard_map/all_gather | solution.py:226
  11.2 12.5 %collective-permute-start.2 = (f32[52,128]{1,0:T(8,128)S(1)}, f32[52,128]{1,0:T(8,128)S(1)}, u32[]{:S(2)}, u32[]{:S(2)}) collective-permute-start(f32[52,128]{1,0:T(8,128)S(1)} %maximum_bitcast_fusion), channel_id=1, source_target_pairs={{0,3},{1,0},{2,1},{3,2},{4,7},{5,4},{6,5},{7,6},{8,11},{9,8},{10,9... | collective-permute-start | bytes 79880 | tf_op jit(solution)/shard_map/ppermute | solution.py:19
  16.3 7.4 %collective-permute-start.1 = (f32[52,128]{1,0:T(8,128)S(1)}, f32[52,128]{1,0:T(8,128)S(1)}, u32[]{:S(2)}, u32[]{:S(2)}) collective-permute-start(f32[52,128]{1,0:T(8,128)S(1)} %maximum_bitcast_fusion), channel_id=1, source_target_pairs={{0,2},{1,3},{2,0},{3,1},{4,6},{5,7},{6,4},{7,5},{8,10},{9,11},{10,... | collective-permute-start | bytes 79880 | tf_op jit(solution)/shard_map/ppermute | solution.py:19
  16.3 7.5 %collective-permute-start = (f32[52,128]{1,0:T(8,128)S(1)}, f32[52,128]{1,0:T(8,128)S(1)}, u32[]{:S(2)}, u32[]{:S(2)}) collective-permute-start(f32[52,128]{1,0:T(8,128)S(1)} %maximum_bitcast_fusion), channel_id=1, source_target_pairs={{0,1},{1,2},{2,3},{3,0},{4,5},{5,6},{6,7},{7,4},{8,9},{9,10},{10,1... | collective-permute-start | bytes 79880 | tf_op jit(solution)/shard_map/ppermute | solution.py:19
  28.7 3.4 %copy-start = (bf16[512,8192]{1,0:T(8,128)(2,1)S(1)}, bf16[512,8192]{1,0:T(8,128)(2,1)}, u32[]{:S(2)}) copy-start(bf16[512,8192]{1,0:T(8,128)(2,1)} %resid_ref.6) | copy-start | bytes 25165828
  37.1 7.5 %collective-permute-start.3 = (bf16[4,1024,512]{2,1,0:T(8,128)(2,1)}, bf16[4,1024,512]{2,1,0:T(8,128)(2,1)}, u32[]{:S(2)}, u32[]{:S(2)}) collective-permute-start(bf16[4,1024,512]{2,1,0:T(8,128)(2,1)} %shard_map.129), channel_id=1, source_target_pairs={{0,4},{4,0},{1,5},{5,1},{2,6},{6,2},{3,7},{7,3},{8,12},{12,8},{9,1... | collective-permute-start | bytes 12582920 | tf_op jit(solution)/shard_map/ppermute | solution.py:19
  44.6 3.4 %copy-start.1 = (bf16[512,8192]{1,0:T(8,128)(2,1)S(1)}, bf16[512,8192]{1,0:T(8,128)(2,1)}, u32[]{:S(2)}) copy-start(bf16[512,8192]{1,0:T(8,128)(2,1)} %resid_ref.6) | copy-start | bytes 25165828
  50.7 38.3 %collective-permute-start.4 = (bf16[2,1024,256]{2,1,0:T(8,128)(2,1)S(1)}, bf16[2,1024,256]{2,1,0:T(8,128)(2,1)S(1)}, u32[]{:S(2)}, u32[]{:S(2)}) collective-permute-start(bf16[2,1024,256]{2,1,0:T(8,128)(2,1)S(1)} %shard_map.131), channel_id=1, source_target_pairs={{0,8},{8,0},{1,9},{9,1},{2,10},{10,2},{3,11},{11,3},{4,12},{12,4},... | collective-permute-start | bytes 3145736 | tf_op jit(solution)/shard_map/ppermute | solution.py:19
  55.1 39.9 %collective-permute-start.5 = (bf16[2,1024,256]{2,1,0:T(8,128)(2,1)S(1)}, bf16[2,1024,256]{2,1,0:T(8,128)(2,1)S(1)}, u32[]{:S(2)}, u32[]{:S(2)}) collective-permute-start(bf16[2,1024,256]{2,1,0:T(8,128)(2,1)S(1)} %shard_map.133), channel_id=1, source_target_pairs={{0,16},{16,0},{1,17},{17,1},{2,18},{18,2},{3,19},{19,3},{4,20},{20... | collective-permute-start | bytes 3145736 | tf_op jit(solution)/shard_map/ppermute | solution.py:19
  62.1 83.0 %copy-start.12 = (bf16[256]{0:T(256)(128)(2,1)S(1)}, bf16[256]{0:T(256)(128)(2,1)}, u32[]{:S(2)}) copy-start(bf16[256]{0:T(256)(128)(2,1)} %param.11) | copy-start | bytes 1540
  62.1 83.0 %copy-start.6 = (bf16[256,512]{1,0:T(8,128)(2,1)S(1)}, bf16[256,512]{1,0:T(8,128)(2,1)}, u32[]{:S(2)}) copy-start(bf16[256,512]{1,0:T(8,128)(2,1)} %param.12) | copy-start | bytes 786436
  89.1 5.9 %copy-start.4 = (bf16[2,1024,256]{2,1,0:T(8,128)(2,1)}, bf16[2,1024,256]{2,1,0:T(8,128)(2,1)S(1)}, u32[]{:S(2)}) copy-start(bf16[2,1024,256]{2,1,0:T(8,128)(2,1)S(1)} %collective-permute-done.4) | copy-start | bytes 3145732
  95.0 1.0 copy-start.5
  105.2 41.5 %collective-permute-start.6 = (bf16[4,1024,512]{2,1,0:T(8,128)(2,1)}, bf16[4,1024,512]{2,1,0:T(8,128)(2,1)}, u32[]{:S(2)}, u32[]{:S(2)}) collective-permute-start(bf16[4,1024,512]{2,1,0:T(8,128)(2,1)} %bitcast.103), channel_id=1, source_target_pairs={{0,4},{4,0},{1,5},{5,1},{2,6},{6,2},{3,7},{7,3},{8,12},{12,8},{9,1... | collective-permute-start | bytes 12582920 | tf_op jit(solution)/shard_map/ppermute | solution.py:19
  105.2 14.7 %collective-permute-start.7 = (bf16[1024,256]{1,0:T(8,128)(2,1)}, bf16[1024,256]{1,0:T(8,128)(2,1)}, u32[]{:S(2)}, u32[]{:S(2)}) collective-permute-start(bf16[1024,256]{1,0:T(8,128)(2,1)} %fusion), channel_id=1, source_target_pairs={{0,16},{16,0},{1,17},{17,1},{2,18},{18,2},{3,19},{19,3},{4,20},{20... | collective-permute-start | bytes 1572872 | tf_op jit(solution)/shard_map/ppermute | solution.py:19
  106.0 15.3 %collective-permute-start.8 = (bf16[1024,256]{1,0:T(8,128)(2,1)S(1)}, bf16[1024,256]{1,0:T(8,128)(2,1)}, u32[]{:S(2)}, u32[]{:S(2)}) collective-permute-start(bf16[1024,256]{1,0:T(8,128)(2,1)S(1)} %fusion.1), channel_id=1, source_target_pairs={{0,8},{8,0},{1,9},{9,1},{2,10},{10,2},{3,11},{11,3},{4,12},{12,4},... | collective-permute-start | bytes 1572872 | tf_op jit(solution)/shard_map/ppermute | solution.py:19
  121.2 1.8 copy-start.3
  123.8 21.2 %collective-permute-start.10 = (bf16[256,512]{1,0:T(8,128)(2,1)}, bf16[256,512]{1,0:T(8,128)(2,1)S(1)}, u32[]{:S(2)}, u32[]{:S(2)}) collective-permute-start(bf16[256,512]{1,0:T(8,128)(2,1)} %pad_maximum_fusion.1), channel_id=1, source_target_pairs={{0,2},{1,3},{2,0},{3,1},{4,6},{5,7},{6,4},{7,5},{8,10},{9,11},{10,... | collective-permute-start | bytes 786440 | tf_op jit(solution)/shard_map/ppermute | solution.py:19
  126.3 18.6 %collective-permute-start.11 = (bf16[256,512]{1,0:T(8,128)(2,1)}, bf16[256,512]{1,0:T(8,128)(2,1)S(1)}, u32[]{:S(2)}, u32[]{:S(2)}) collective-permute-start(bf16[256,512]{1,0:T(8,128)(2,1)} %pad_maximum_fusion.2), channel_id=1, source_target_pairs={{0,3},{1,0},{2,1},{3,2},{4,7},{5,4},{6,5},{7,6},{8,11},{9,8},{10,9... | collective-permute-start | bytes 786440 | tf_op jit(solution)/shard_map/ppermute | solution.py:19
  128.9 16.1 %collective-permute-start.9 = (bf16[256,512]{1,0:T(8,128)(2,1)}, bf16[256,512]{1,0:T(8,128)(2,1)S(1)}, u32[]{:S(2)}, u32[]{:S(2)}) collective-permute-start(bf16[256,512]{1,0:T(8,128)(2,1)} %pad_maximum_fusion), channel_id=1, source_target_pairs={{0,1},{1,2},{2,3},{3,0},{4,5},{5,6},{6,7},{7,4},{8,9},{9,10},{10,1... | collective-permute-start | bytes 786440 | tf_op jit(solution)/shard_map/ppermute | solution.py:19
  146.7 2.2 %copy-start.2 = (bf16[4096,512]{1,0:T(8,128)(2,1)S(1)}, bf16[4096,512]{1,0:T(8,128)(2,1)}, u32[]{:S(2)}) copy-start(bf16[4096,512]{1,0:T(8,128)(2,1)} %all-gather.2.cloned.1.call-done) | copy-start | bytes 12582916
Sparse Core Ops, SparseCore 0:
  11.4 93.7 all-gather.1

commit v3 on v2

v3 whole, which is shorter than its diff:
```python
import functools

import jax
import jax.numpy as jnp
from jax import lax
from jax.experimental import pallas as pl
from jax.experimental.pallas import tpu as pltpu
from jax.sharding import PartitionSpec as P

VOCAB = 128256
EPS = 1e-05
BETA = 0.5
CORES = 2
OUTER = 2
VMEM_BYTES = 48 * 1024 * 1024
BF16 = jnp.bfloat16
F32 = jnp.float32


def swap(value, axis, step):
    size = lax.axis_size(axis)
    return lax.ppermute(value, axis, [(place, (place + step) % size) for place in range(size)])


def after(value, *earlier):
    return lax.optimization_barrier((value, earlier))[0]


def widen(parts):
    return functools.reduce(jnp.add, [part.astype(F32) for part in parts])


def chunk_order(tp_count):
    order = [0]
    for step in range(1, tp_count // 2 + 1):
        order += [step] if 2 * step == tp_count else [step, tp_count - step]
    return order


def inner_first(order, chunk):
    return order.index(chunk) % 2 == 0


def theirs_kernel(places_ref, cot_ref, first_ref, second_ref, out_ref):
    for slot, resid_ref in enumerate((first_ref, second_ref)):
        product = lax.dot_general(
            resid_ref[...], cot_ref[...], (((0,), (0,)), ((), ())), preferred_element_type=F32
        )
        out_ref[slot, 0] = product.astype(BF16)


def ours_kernel(places_ref, cot_ref, first_ref, second_ref, other_ref, *outs):
    step = pl.program_id(0)
    at_outer, at_inner = step // 2, lax.rem(step, 2)
    for slot, resid_ref in enumerate((first_ref, second_ref)):
        send_ref, keep_ref = outs[2 * slot : 2 * slot + 2]
        product = lax.dot_general(
            resid_ref[...], cot_ref[...], (((0,), (0,)), ((), ())), preferred_element_type=F32
        )
        total = (product + other_ref[slot, 0].astype(F32)).astype(BF16)
        way, place = (at_inner, at_outer) if slot == 0 else (at_outer, at_inner)

        @pl.when(way == 1)
        def _():
            send_ref[place] = total

        @pl.when(way == 0)
        def _():
            keep_ref[place] = total


def pair_product(residual, cot, places, rows, other):
    tokens, features = cot.shape
    steps = places.shape[0] // 2
    whole = lambda i, p: (0, 0)
    in_specs = [
        pl.BlockSpec((tokens, features), whole),
        pl.BlockSpec((tokens, rows), lambda i, p: (0, p[i])),
        pl.BlockSpec((tokens, rows), lambda i, p: (0, p[steps + i])),
    ]
    operands = [cot, residual, residual]
    block = pl.BlockSpec((2, 1, rows, features), lambda i, p: (0, i, 0, 0))
    if other is None:
        kernel, out_specs = theirs_kernel, block
        out_shape = jax.ShapeDtypeStruct((2, steps, rows, features), BF16)
    else:
        kernel = ours_kernel
        in_specs.append(block)
        operands.append(other)
        out_specs = [pl.BlockSpec((2, rows, features), lambda i, p: (0, 0, 0))] * 4
        out_shape = [jax.ShapeDtypeStruct((2, rows, features), BF16)] * 4
    return pl.pallas_call(
        kernel,
        out_shape=out_shape,
        grid_spec=pltpu.PrefetchScalarGridSpec(
            num_scalar_prefetch=1, grid=(steps,), in_specs=in_specs, out_specs=out_specs
        ),
        cost_estimate=pl.CostEstimate(
            flops=4 * tokens * steps * rows * features,
            bytes_accessed=4 * steps * rows * (tokens + 2 * features),
            transcendentals=0,
        ),
        compiler_params=pltpu.CompilerParams(vmem_limit_bytes=VMEM_BYTES),
    )(places, *operands)


def place_weight(step, inner_flags, offsets_ref, pieces, weight_ref):
    at_outer, at_inner = lax.rem(step // 2, 2), lax.rem(step, 2)
    rows = pieces[0].shape[1]
    chunks = len(inner_flags)
    for core in range(CORES):
        for chunk, flag in enumerate(inner_flags):
            way = at_outer if flag else at_inner
            where = pl.ds(pl.multiple_of(offsets_ref[chunk], rows), rows)
            for late in range(2):
                piece = pieces[(core * chunks + chunk) * 2 + late]

                @pl.when(jnp.logical_and(step // 4 == core, way == late))
                def _():
                    weight_ref[where, :] = piece[0]


def piece_specs(inner_flags, rows, features):
    specs = []
    for core in range(CORES):
        for flag in inner_flags:
            for late in range(2):
                if flag:
                    index = lambda i, *_, first=4 * core + 2 * late: (jnp.clip(i - first, 0, 1), 0, 0)
                else:
                    index = lambda i, *_, first=4 * core: (jnp.clip(i - first, 0, 3) // 2, 0, 0)
                specs.append(pl.BlockSpec((1, rows, features), index))
    return specs


def value_kernel(inner_flags, places_ref, offsets_ref, resid_ref, cot_ref, inv_ref, *rest):
    pieces, (value_ref, coef_ref, weight_ref, total_ref) = rest[:-4], rest[-4:]
    step = pl.program_id(0)
    count = pl.num_programs(0)
    place_weight(step, inner_flags, offsets_ref, pieces, weight_ref)

    @pl.when(step == 0)
    def _():
        total_ref[...] = jnp.zeros_like(total_ref)

    total_ref[...] += jnp.dot(resid_ref[...], weight_ref[...], preferred_element_type=F32)

    @pl.when(step == count - 1)
    def _():
        total = total_ref[...]
        inv = inv_ref[...]
        value_ref[...] = (total * inv).astype(BF16)
        share = jnp.sum(total * cot_ref[...].astype(F32), axis=1, keepdims=True)
        width = resid_ref.shape[1] * count
        coef_ref[...] = share * (inv * inv) * (1.0 / width)


def grad_kernel(inner_flags, places_ref, offsets_ref, resid_ref, cot_ref, coef_ref, *rest):
    pieces, (out_ref, weight_ref) = rest[:-2], rest[-2:]
    place_weight(pl.program_id(0), inner_flags, offsets_ref, pieces, weight_ref)
    grad = lax.dot_general(
        cot_ref[...], weight_ref[...], (((1,), (1,)), ((), ())), preferred_element_type=F32
    )
    out_ref[...] = (grad - resid_ref[...].astype(F32) * coef_ref[...]).astype(BF16)


def weight_call(kernel, inner_flags, places, offsets, residual, cot, column, pieces, whole_out):
    tokens, width = residual.shape
    rows, features = pieces[0].shape[1:]
    steps = places.shape[0]
    depth = width // steps
    whole = lambda i, *_: (0, 0)
    block = pl.BlockSpec((tokens, depth), lambda i, p, o: (0, p[i]))
    scratch = [pltpu.VMEM((depth, features), BF16)]
    if whole_out:
        out_shape = [
            jax.ShapeDtypeStruct((tokens, features), BF16),
            jax.ShapeDtypeStruct((tokens, 1), F32),
        ]
        out_specs = [pl.BlockSpec((tokens, features), whole), pl.BlockSpec((tokens, 1), whole)]
        scratch.append(pltpu.VMEM((tokens, features), F32))
    else:
        out_shape, out_specs = jax.ShapeDtypeStruct((tokens, width), BF16), block
    return pl.pallas_call(
        functools.partial(kernel, inner_flags),
        out_shape=out_shape,
        grid_spec=pltpu.PrefetchScalarGridSpec(
            num_scalar_prefetch=2,
            grid=(steps,),
            in_specs=[block, pl.BlockSpec((tokens, features), whole), pl.BlockSpec((tokens, 1), whole)]
            + piece_specs(inner_flags, rows, features),
            out_specs=out_specs,
            scratch_shapes=scratch,
        ),
        cost_estimate=pl.CostEstimate(
            flops=2 * tokens * width * features,
            bytes_accessed=2 * width * (2 * tokens + features),
            transcendentals=0,
        ),
        compiler_params=pltpu.CompilerParams(vmem_limit_bytes=VMEM_BYTES),
    )(places, offsets, residual, cot, column, *pieces)


def sequence_weight(trainee_logp, shard_max, shard_sum, owned, seq_length, rep_count, tp_count, tp_place):
    rows_here = trainee_logp.shape[0]
    seq = shard_max.shape[0]
    packed = jnp.concatenate([shard_max, shard_sum, owned, trainee_logp]).reshape(-1, 128)
    shares = [packed] + [swap(packed, "tp", s) for s in range(1, tp_count)]
    shares = [share.reshape(-1) for share in shares]
    top_max = functools.reduce(jnp.maximum, [share[:seq] for share in shares])
    sum_exp = sum(share[seq : 2 * seq] * jnp.exp(share[:seq] - top_max) for share in shares)
    picked = sum(share[2 * seq : 3 * seq] for share in shares)
    ref_logp = picked - top_max - jnp.log(sum_exp)
    total = jnp.zeros((), F32)
    for s, share in enumerate(shares):
        first = lax.rem(tp_place - s + tp_count, tp_count) * rows_here
        live = first + jnp.arange(rows_here, dtype=jnp.int32) < seq_length
        diff = share[3 * seq :] - lax.dynamic_slice_in_dim(ref_logp, first, rows_here)
        total = total + jnp.sum(jnp.where(live, diff, 0.0))
    seq_delta = total / seq_length.astype(F32)
    return 2.0 * jax.nn.sigmoid(BETA * seq_delta) / rep_count


def per_device(
    residual,
    norm_gain,
    value_weight,
    value_cot,
    trainee_logp,
    ref_shard_max,
    ref_shard_sum,
    ref_target_logit,
    target_ids,
    lengths,
):
    rows_here, width = residual.shape
    features = value_cot.shape[1]
    tp_count = lax.axis_size("tp")
    outer, inner = lax.axis_size("outer"), lax.axis_size("inner")
    rep_count = outer * inner * CORES
    tp_place = lax.axis_index("tp")
    core = lax.axis_index("core")
    at_inner = lax.axis_index("inner")
    at_outer = lax.axis_index("outer")
    rep_place = (at_outer * inner + at_inner) * CORES + core
    depth = width // rep_count
    rows = depth // tp_count
    order = chunk_order(tp_count)
    in_place = rows % 128 == 0 and outer == 2 and inner == 2

    gained = (value_weight.astype(F32) * norm_gain.astype(F32)[:, None]).astype(BF16)
    residual, gained = lax.optimization_barrier((residual, gained))
    arrived = [gained]
    for k in order[1:]:
        arrived.append(swap(gained if k == order[1] else after(gained, arrived[-1]), "tp", k))
    own_pieces, nears = [], []
    for k, block in zip(order, arrived):
        first, second = ("inner", "outer") if inner_first(order, k) else ("outer", "inner")
        nears.append([swap(block, first, s) for s in range(1, lax.axis_size(first))])
        near = jnp.stack([block] + nears[-1])
        far = [swap(near, second, s) for s in range(1, lax.axis_size(second))]
        own_pieces.append([near] + far)
    other_pieces = [[swap(piece, "core", 1) for piece in pieces] for pieces in own_pieces]

    owned = jnp.where(
        target_ids // (VOCAB // tp_count) == tp_place,
        ref_target_logit[0],
        jnp.zeros_like(ref_target_logit[0]),
    )
    seq_length = lax.dynamic_index_in_dim(lengths, rep_place, keepdims=False)
    seq_weight = sequence_weight(
        trainee_logp, ref_shard_max[0], ref_shard_sum[0], owned, seq_length, rep_count, tp_count, tp_place
    )
    positions = tp_place * rows_here + jnp.arange(rows_here, dtype=jnp.int32)
    row_scale = (positions < seq_length).astype(F32) * seq_weight
    resid_wide = residual.astype(F32)
    inv_rms = lax.rsqrt(jnp.mean(resid_wide * resid_wide, axis=1, keepdims=True) + EPS)
    cot = (inv_rms * row_scale[:, None] * value_cot.astype(F32)).astype(BF16)
    cot = after(cot, arrived[1], nears[0])

    def place_of(o, i, c, k):
        chip = lax.rem(at_outer + o, outer) * inner + lax.rem(at_inner + i, inner)
        return (chip * CORES + c) * tp_count + lax.rem(tp_place + k, tp_count)

    chips = [(o, i) for o in range(outer) for i in range(inner)]
    if not in_place:
        product = lax.dot_general(residual, cot, (((0,), (0,)), ((), ())), preferred_element_type=F32)
        product = product.astype(BF16).reshape(-1, rows, features)

    def places_of(pair, c):
        return jnp.stack([place_of(o, i, c, k) for k in pair for o, i in chips]).astype(jnp.int32)

    def for_other(pair, cot):
        places = places_of(pair, 1 - core)
        if in_place:
            return pair_product(residual, cot, places, rows, None)
        return product[places].reshape(2, len(chips), rows, features)

    def for_us(pair, other):
        places = places_of(pair, core)
        if in_place:
            send_a, keep_a, send_b, keep_b = pair_product(residual, cot, places, rows, other)
            return ([send_a], keep_a), ([send_b], keep_b)
        total = widen([product[places], other.reshape(-1, rows, features)]).astype(BF16)
        total = total.reshape(2, outer, inner, rows, features)
        first = ([total[0, :, s] for s in range(1, inner)], total[0, :, 0])
        second = ([total[1, s] for s in range(1, outer)], total[1, 0])
        return first, second

    backward = order[::-1]
    pairs = [backward[i : i + 2] for i in range(0, tp_count, 2)]
    theirs = []
    for n, pair in enumerate(pairs):
        theirs.append(for_other(pair, after(cot, theirs, arrived[2], nears[1]) if n else cot))
    others = [swap(part, "core", 1) for part in theirs]
    others[0] = after(others[0], theirs, nears[2])
    chunk_sums = {}
    sent = []
    for pair, other in zip(pairs, others):
        if sent:
            other = after(other, sent, arrived[3])
        for k, axes, (sends, keep) in zip(
            pair, (("inner", "outer"), ("outer", "inner")), for_us(pair, other)
        ):
            sent += sends
            got = [swap(send, axes[0], s + 1) for s, send in enumerate(sends)]
            later = [
                swap(widen([part[s] for part in [keep] + got]).astype(BF16), axes[1], s)
                for s in range(1, lax.axis_size(axes[1]))
            ]
            chunk_sums[k] = widen([part[0] for part in [keep] + got] + later)
    last = [swap(chunk_sums[k].astype(BF16), "tp", k) for k in backward[:-1]]
    grad_rows = widen([chunk_sums[0]] + last)
    late_gain, late_weight, grad_rows = lax.optimization_barrier((norm_gain, value_weight, grad_rows))
    weight_grad = late_gain.astype(F32)[:, None] * grad_rows
    gain_grad = jnp.sum(late_weight.astype(F32) * grad_rows, axis=1)

    if in_place:
        pieces = [piece for side in (own_pieces, other_pieces) for both in side for piece in both]
        flags = tuple(inner_first(order, k) for k in order)
        places = jnp.stack([place_of(o, i, c, 0) // tp_count for c in (core, 1 - core) for o, i in chips])
        offsets = jnp.stack([lax.rem(tp_place - k + tp_count, tp_count) * rows for k in order])
        places, offsets = places.astype(jnp.int32), offsets.astype(jnp.int32)
        value_proj, coefficient = weight_call(
            value_kernel, flags, places, offsets, residual, cot, after(inv_rms, sent), pieces, True
        )
        resid_grad = weight_call(
            grad_kernel, flags, places, offsets, residual, cot, coefficient, pieces, False
        )
    else:
        weight = []
        for side in (own_pieces, other_pieces):
            for k, pieces in zip(order, side):
                both = jnp.stack(pieces)
                weight.append(both if inner_first(order, k) else jnp.swapaxes(both, 0, 1))
        weight = jnp.stack(weight).reshape(CORES, tp_count, outer, inner, rows, features)
        by_place = [order.index(k) for k in range(tp_count)]
        weight = weight[:, jnp.array(by_place)]
        weight = weight[jnp.array([core, 1 - core])]
        weight = weight[:, (tp_place - jnp.arange(tp_count)) % tp_count]
        weight = weight[:, :, (at_outer - jnp.arange(outer)) % outer]
        weight = weight[:, :, :, (at_inner - jnp.arange(inner)) % inner]
        weight = weight.transpose(2, 3, 0, 1, 4, 5).reshape(width, features)
        value_acc = jnp.dot(residual, weight, preferred_element_type=F32)
        value_proj = (inv_rms * value_acc).astype(BF16)
        share = jnp.sum(cot.astype(F32) * value_acc, axis=1, keepdims=True)
        coefficient = inv_rms * inv_rms * share * (1.0 / width)
        normed_grad = lax.dot_general(
            cot, weight, (((1,), (1,)), ((), ())), preferred_element_type=F32
        )
        resid_grad = (normed_grad - residual.astype(F32) * coefficient).astype(BF16)
    return (value_proj, resid_grad, weight_grad, gain_grad)


def solution(mesh):
    rep_count, tp_count = mesh.shape["rep"], mesh.shape["tp"]
    split = jax.sharding.Mesh(
        mesh.devices.reshape(OUTER, rep_count // (OUTER * CORES), CORES, tp_count),
        ("outer", "inner", "core", "tp"),
    )
    rep = ("outer", "inner", "core")
    rows = rep + ("tp",)
    return jax.shard_map(
        per_device,
        mesh=split,
        in_specs=(
            P(rows, None),
            P(rows),
            P(rows, None),
            P(rows, None),
            P(rows),
            P("tp", rep),
            P("tp", rep),
            P("tp", rep),
            P(rep),
            P(),
        ),
        out_specs=(P(rows, None), P(rows, None), P(rows, None), P(rows)),
        check_vma=False,
    )
```

time: 182 us -> 167 us (0.918); the launches traced: 179 us -> 166 us
  waiting for transfers between devices: 75.6 us -> 55.2 us
  starting transfers between devices: 15.1 us -> 34.9 us
  between operations: 17.7 us -> 4.42 us
  Pallas kernels: 38.8 us -> 47.5 us
  other arithmetic: 19.5 us -> 15.1 us
  local copies, waits for them, and re-layouts: 11.8 us -> 8.97 us
    ppermute x12 -> x35, starting transfers between devices: 15.1 us -> 34.9 us  [swap(): lax.ppermute(value, axis, [(place, (place + step) % size) for place in ra...]
    ppermute x12 -> x35, waiting for transfers between devices: 66.5 us -> 55.2 us  [swap(): lax.ppermute(value, axis, [(place, (place + step) % size) for place in ra...]
    all_gather x1 -> x0, waiting for transfers between devices: 9.1 us -> none  [per_device(): lax.all_gather(gained, ('outer', 'inner', 'tp'), axis=0, tiled=True)]
    pallas_call x7 -> x6, Pallas kernels: 38.8 us -> 47.5 us  [the longest x2 25.8 us: weight_call(): pl.pallas_call(functools.partial(kernel, inner_flags), out_shape=out_shap...]
    add x6 -> x1, other arithmetic: 3.33 us -> 0.2 us  [widen(): return functools.reduce(jnp.add, [part.astype(F32) for part in parts])]
    unnamed x26 -> x42, local copies, waits for them, and re-layouts: 9.99 us -> 7.81 us
    concatenate x3 -> x0, other arithmetic: 2.16 us -> none  [rows_for(): jnp.concatenate([lax.dynamic_slice_in_dim(part, first, own_rows) for part...]
    convert_element_type x6 -> x11, other arithmetic: 3.91 us -> 4.48 us  [the longest x4 1.35 us: per_device(): widen([part[s] for part in [keep] + got]).astype(BF16)]
  transfers between devices with their start and end apart: 13 -> 35, of which waited for: 6 -> 10; matrix products, arithmetic and copies ran while one was open for 11% -> 8% of each run, Pallas kernels for 9% -> 25%
where the time goes in v3:
time: 167 us; the launch traced here: 166 us
  waiting for transfers between devices  55.2 us (33%)
  Pallas kernels  47.5 us (28%)
  starting transfers between devices  34.9 us (21%)
  other arithmetic  15.1 us (9%)
  local copies, waits for them, and re-layouts  8.97 us (5%)
  between operations  4.42 us (3%)
    ppermute x35, waiting for transfers between devices, swap(): lax.ppermute(value, axis, [(place, (place + step) % size) for place in ra...  55.2 us
    ppermute x35, starting transfers between devices, swap(): lax.ppermute(value, axis, [(place, (place + step) % size) for place in ra...  34.9 us
    pallas_call x2, Pallas kernels, weight_call(): pl.pallas_call(functools.partial(kernel, inner_flags), out_shape=out_shap...  25.8 us
    pallas_call x4, Pallas kernels, pair_product(): pl.pallas_call(kernel, out_shape=out_shape, grid_spec=pltpu.PrefetchScala...  21.7 us
    unnamed x42, local copies, waits for them, and re-layouts  7.81 us
    reduce_sum x1, other arithmetic, per_device(): jnp.mean(resid_wide * resid_wide, axis=1, keepdims=True) + EPS  5.1 us
  transfers between devices with their start and end apart: 35, of which 10 were waited for; matrix products, arithmetic and copies ran while one was open for 8% of the time, Pallas kernels for 25%

profile of v3, /device:TPU:0, one launch (start us, length us, event | category | flops | bytes accessed | tf_op | source)
XLA Modules:
  0.0 166.1 jit_solution(8218727040604586143)
XLA Ops:
  2.2 3.0 %collective-permute-start = (f32[52,128]{1,0:T(8,128)S(1)}, f32[52,128]{1,0:T(8,128)S(1)}, u32[]{:S(2)}, u32[]{:S(2)}) collective-permute-start(f32[52,128]{1,0:T(8,128)S(1)} %maximum_bitcast_fusion), channel_id=1, source_target_pairs={{0,1},{1,2},{2,3},{3,0},{4,5},{5,6},{6,7},{7,4},{8,9},{9,10},{10,1... | collective-permute-start | bytes 79880 | tf_op jit(solution)/shard_map/ppermute | solution.py:22
  5.2 2.6 %collective-permute-start.1 = (f32[52,128]{1,0:T(8,128)S(1)}, f32[52,128]{1,0:T(8,128)S(1)}, u32[]{:S(2)}, u32[]{:S(2)}) collective-permute-start(f32[52,128]{1,0:T(8,128)S(1)} %maximum_bitcast_fusion), channel_id=1, source_target_pairs={{0,2},{1,3},{2,0},{3,1},{4,6},{5,7},{6,4},{7,5},{8,10},{9,11},{10,... | collective-permute-start | bytes 79880 | tf_op jit(solution)/shard_map/ppermute | solution.py:22
  11.6 1.5 collective-permute-start.4
  13.1 5.1 %multiply_reduce_fusion = f32[512]{0:T(512)S(1)} fusion(bf16[512,8192]{1,0:T(8,128)(2,1)} %resid_ref.1), kind=kLoop, calls=%fused_computation | loop fusion | flops 12582400 | bytes 8390656 | tf_op jit(solution)/shard_map/reduce_sum | solution.py:277
  24.6 5.2 %shard_map.129 = bf16[2,4,256,512]{3,2,1,0:T(8,128)(2,1)} custom-call(s32[8]{0:T(128)S(1)} %stack.217.places_ref, bf16[512,512]{1,0:T(8,128)(2,1)S(1)} %multiply_convert_fusion.cot_ref, bf16[512,8192]{1,0:T(8,128)(2,1)} %resid_ref.1, bf16[512,8192]{1,0:T(8,128)(2,1)} %resid_ref.1), custom_call_target="tpu_custom_call" | custom-call | flops 1073741824 | bytes 6291456 | tf_op jit(solution)/shard_map/pallas_call | solution.py:92
  29.9 3.1 %collective-permute-start.6 = (bf16[256,512]{1,0:T(8,128)(2,1)S(1)}, bf16[256,512]{1,0:T(8,128)(2,1)S(1)}, u32[]{:S(2)}, u32[]{:S(2)}) collective-permute-start(bf16[256,512]{1,0:T(8,128)(2,1)S(1)} %multiply_convert_fusion.1), channel_id=1, source_target_pairs={{0,3},{1,0},{2,1},{3,2},{4,7},{5,4},{6,5},{7,6},{8,11},{9,8},{10,9... | collective-permute-start | bytes 786440 | tf_op jit(solution)/shard_map/ppermute | solution.py:22
  33.0 1.5 collective-permute-start.7
  34.6 4.6 %collective-permute-done.6 = bf16[256,512]{1,0:T(8,128)(2,1)S(1)} collective-permute-done((bf16[256,512]{1,0:T(8,128)(2,1)S(1)}, bf16[256,512]{1,0:T(8,128)(2,1)S(1)}, u32[]{:S(2)}, u32[]{:S(2)}) %collective-permute-start.6) | collective-permute-done | bytes 262176 | tf_op jit(solution)/shard_map/ppermute | solution.py:22
  39.2 2.2 %collective-permute-done.7 = bf16[256,512]{1,0:T(8,128)(2,1)S(1)} collective-permute-done((bf16[256,512]{1,0:T(8,128)(2,1)S(1)}, bf16[256,512]{1,0:T(8,128)(2,1)S(1)}, u32[]{:S(2)}, u32[]{:S(2)}) %collective-permute-start.7) | collective-permute-done | bytes 262176 | tf_op jit(solution)/shard_map/ppermute | solution.py:22
  41.4 5.2 %shard_map.130 = bf16[2,4,256,512]{3,2,1,0:T(8,128)(2,1)} custom-call(s32[8]{0:T(128)S(1)} %stack.226.places_ref, bf16[512,512]{1,0:T(8,128)(2,1)S(1)} %multiply_convert_fusion.cot_ref, bf16[512,8192]{1,0:T(8,128)(2,1)} %resid_ref.1, bf16[512,8192]{1,0:T(8,128)(2,1)} %resid_ref.1), custom_call_target="tpu_custom_call" | custom-call | flops 1073741824 | bytes 6291456 | tf_op jit(solution)/shard_map/pallas_call | solution.py:92
  47.2 1.6 collective-permute-start.11
  48.8 6.5 %collective-permute-done.8 = bf16[256,512]{1,0:T(8,128)(2,1)S(1)} collective-permute-done((bf16[256,512]{1,0:T(8,128)(2,1)S(1)}, bf16[256,512]{1,0:T(8,128)(2,1)S(1)}, u32[]{:S(2)}, u32[]{:S(2)}) %collective-permute-start.8) | collective-permute-done | bytes 262176 | tf_op jit(solution)/shard_map/ppermute | solution.py:22
  55.4 13.8 %collective-permute-done.10 = bf16[256,512]{1,0:T(8,128)(2,1)S(1)} collective-permute-done((bf16[256,512]{1,0:T(8,128)(2,1)S(1)}, bf16[256,512]{1,0:T(8,128)(2,1)S(1)}, u32[]{:S(2)}, u32[]{:S(2)}) %collective-permute-start.10) | collective-permute-done | bytes 262176 | tf_op jit(solution)/shard_map/ppermute | solution.py:22
  70.6 1.5 collective-permute-start.14
  72.2 7.1 %collective-permute-done.14 = bf16[256,512]{1,0:T(8,128)(2,1)S(1)} collective-permute-done((bf16[256,512]{1,0:T(8,128)(2,1)S(1)}, bf16[256,512]{1,0:T(8,128)(2,1)S(1)}, u32[]{:S(2)}, u32[]{:S(2)}) %collective-permute-start.14) | collective-permute-done | bytes 262176 | tf_op jit(solution)/shard_map/ppermute | solution.py:22
  79.3 1.5 collective-permute-start.13
  80.9 2.3 %collective-permute-done.12.rest_3_ = bf16[2,256,512]{2,1,0:T(8,128)(2,1)} collective-permute-done((bf16[2,256,512]{2,1,0:T(8,128)(2,1)S(1)}, bf16[2,256,512]{2,1,0:T(8,128)(2,1)}, u32[]{:S(2)}, u32[]{:S(2)}) %collective-permute-start.12) | collective-permute-done | bytes 524320 | tf_op jit(solution)/shard_map/ppermute | solution.py:22
  84.7 6.0 %shard_map.131 = (bf16[2,256,512]{2,1,0:T(8,128)(2,1)}, bf16[2,256,512]{2,1,0:T(8,128)(2,1)S(1)}, bf16[2,256,512]{2,1,0:T(8,128)(2,1)S(1)}, bf16[2,256,512]{2,1,0:T(8,128)(2,1)S(1)}) custom-call(s32[8]{0:T(128)S(1)} %stack.208.places_ref, bf16[512,512]{1,0:T(8,128)(2,1)S(1)} %multiply_convert_fusion.cot_ref, bf16[512,8192]{1,0:T(8,128)(2,1)} %resid_ref.1, ...), custom_call_target="tpu_custom_call" | custom-call | flops 1073741824 | bytes 6291456 | tf_op jit(solution)/shard_map/pallas_call | solution.py:92
  93.1 1.5 collective-permute-start.26
  95.1 3.8 %collective-permute-done.15.rest_7_ = bf16[2,256,512]{2,1,0:T(8,128)(2,1)} collective-permute-done((bf16[2,256,512]{2,1,0:T(8,128)(2,1)S(1)}, bf16[2,256,512]{2,1,0:T(8,128)(2,1)}, u32[]{:S(2)}, u32[]{:S(2)}) %collective-permute-start.15) | collective-permute-done | bytes 524320 | tf_op jit(solution)/shard_map/ppermute | solution.py:22
  99.6 5.2 %shard_map.132 = (bf16[2,256,512]{2,1,0:T(8,128)(2,1)S(1)}, bf16[2,256,512]{2,1,0:T(8,128)(2,1)S(1)}, bf16[2,256,512]{2,1,0:T(8,128)(2,1)S(1)}, bf16[2,256,512]{2,1,0:T(8,128)(2,1)S(1)}) custom-call(s32[8]{0:T(128)S(1)} %stack.235.places_ref, bf16[512,512]{1,0:T(8,128)(2,1)S(1)} %multiply_convert_fusion.cot_ref, bf16[512,8192]{1,0:T(8,128)(2,1)} %resid_ref.1, ...), custom_call_target="tpu_custom_call" | custom-call | flops 1073741824 | bytes 6291456 | tf_op jit(solution)/shard_map/pallas_call | solution.py:92
  109.7 1.5 collective-permute-start.29
  113.5 1.5 collective-permute-start.27
  116.1 12.4 %shard_map.133 = (bf16[512,512]{1,0:T(8,128)(2,1)}, f32[512,1]{1,0:T(8,128)S(1)}) custom-call(s32[8]{0:T(128)S(1)} %stack.194.places_ref, s32[4]{0:T(128)S(1)} %pad_add_fusion.offsets_ref, bf16[512,8192]{1,0:T(8,128)(2,1)} %resid_ref.1, bf16[512,512]{1,0:T(8,128)(2,1)S(1)} %multiply_convert_fusion.cot_ref, f32[512,1]{1,0:T(8,128)S(1)} %copy.14.inv_ref, ...), custom_call_target="tpu_custom_call" | custom-call | flops 4294967296 | bytes 25165824 | tf_op jit(solution)/shard_map/pallas_call | solution.py:184
  128.5 1.6 collective-permute-start.30
  130.1 10.2 %collective-permute-done.27 = bf16[256,512]{1,0:T(8,128)(2,1)S(1)} collective-permute-done((bf16[256,512]{1,0:T(8,128)(2,1)S(1)}, bf16[256,512]{1,0:T(8,128)(2,1)S(1)}, u32[]{:S(2)}, u32[]{:S(2)}) %collective-permute-start.27) | collective-permute-done | bytes 262176 | tf_op jit(solution)/shard_map/ppermute | solution.py:22
  141.6 1.6 collective-permute-start.33
  143.2 1.8 %collective-permute-start.31 = (bf16[256,512]{1,0:T(8,128)(2,1)S(1)}, bf16[256,512]{1,0:T(8,128)(2,1)S(1)}, u32[]{:S(2)}, u32[]{:S(2)}) collective-permute-start(bf16[256,512]{1,0:T(8,128)(2,1)S(1)} %fusion.1), channel_id=1, source_target_pairs={{0,3},{1,0},{2,1},{3,2},{4,7},{5,4},{6,5},{7,6},{8,11},{9,8},{10,9... | collective-permute-start | bytes 786440 | tf_op jit(solution)/shard_map/ppermute | solution.py:22
  145.7 3.0 %collective-permute-done.33 = bf16[256,512]{1,0:T(8,128)(2,1)S(1)} collective-permute-done((bf16[256,512]{1,0:T(8,128)(2,1)S(1)}, bf16[256,512]{1,0:T(8,128)(2,1)S(1)}, u32[]{:S(2)}, u32[]{:S(2)}) %collective-permute-start.33) | collective-permute-done | bytes 262176 | tf_op jit(solution)/shard_map/ppermute | solution.py:22
  148.8 2.0 %collective-permute-start.34 = (bf16[256,512]{1,0:T(8,128)(2,1)S(1)}, bf16[256,512]{1,0:T(8,128)(2,1)S(1)}, u32[]{:S(2)}, u32[]{:S(2)}) collective-permute-start(bf16[256,512]{1,0:T(8,128)(2,1)S(1)} %fusion), channel_id=1, source_target_pairs={{0,1},{1,2},{2,3},{3,0},{4,5},{5,6},{6,7},{7,4},{8,9},{9,10},{10,1... | collective-permute-start | bytes 786440 | tf_op jit(solution)/shard_map/ppermute | solution.py:22
  150.8 13.5 %shard_map.134 = bf16[512,8192]{1,0:T(8,128)(2,1)} custom-call(s32[8]{0:T(128)S(1)} %stack.194.places_ref, s32[4]{0:T(128)S(1)} %pad_add_fusion.offsets_ref, bf16[512,8192]{1,0:T(8,128)(2,1)} %resid_ref.1, bf16[512,512]{1,0:T(8,128)(2,1)S(1)} %multiply_convert_fusion.cot_ref, f32[512,1]{1,0:T(8,128)S(1)} %get-tuple-element.40.coef_ref, ...), custom_call_target="tpu_custom_call" | custom-call | flops 4294967296 | bytes 25165824 | tf_op jit(solution)/shard_map/pallas_call | solution.py:184
  164.6 1.5 multiply_reduce_fusion.1
  (117 shorter events, 26.0 us)
Async XLA Ops:
  2.2 17.4 %collective-permute-start = (f32[52,128]{1,0:T(8,128)S(1)}, f32[52,128]{1,0:T(8,128)S(1)}, u32[]{:S(2)}, u32[]{:S(2)}) collective-permute-start(f32[52,128]{1,0:T(8,128)S(1)} %maximum_bitcast_fusion), channel_id=1, source_target_pairs={{0,1},{1,2},{2,3},{3,0},{4,5},{5,6},{6,7},{7,4},{8,9},{9,10},{10,1... | collective-permute-start | bytes 79880 | tf_op jit(solution)/shard_map/ppermute | solution.py:22
  5.2 14.4 %collective-permute-start.1 = (f32[52,128]{1,0:T(8,128)S(1)}, f32[52,128]{1,0:T(8,128)S(1)}, u32[]{:S(2)}, u32[]{:S(2)}) collective-permute-start(f32[52,128]{1,0:T(8,128)S(1)} %maximum_bitcast_fusion), channel_id=1, source_target_pairs={{0,2},{1,3},{2,0},{3,1},{4,6},{5,7},{6,4},{7,5},{8,10},{9,11},{10,... | collective-permute-start | bytes 79880 | tf_op jit(solution)/shard_map/ppermute | solution.py:22
  7.8 11.8 %collective-permute-start.2 = (f32[52,128]{1,0:T(8,128)S(1)}, f32[52,128]{1,0:T(8,128)S(1)}, u32[]{:S(2)}, u32[]{:S(2)}) collective-permute-start(f32[52,128]{1,0:T(8,128)S(1)} %maximum_bitcast_fusion), channel_id=1, source_target_pairs={{0,3},{1,0},{2,1},{3,2},{4,7},{5,4},{6,5},{7,6},{8,11},{9,8},{10,9... | collective-permute-start | bytes 79880 | tf_op jit(solution)/shard_map/ppermute | solution.py:22
  10.9 13.7 %collective-permute-start.3 = (bf16[256,512]{1,0:T(8,128)(2,1)S(1)}, bf16[256,512]{1,0:T(8,128)(2,1)S(1)}, u32[]{:S(2)}, u32[]{:S(2)}) collective-permute-start(bf16[256,512]{1,0:T(8,128)(2,1)S(1)} %multiply_convert_fusion.1), channel_id=1, source_target_pairs={{0,1},{1,2},{2,3},{3,0},{4,5},{5,6},{6,7},{7,4},{8,9},{9,10},{10,1... | collective-permute-start | bytes 786440 | tf_op jit(solution)/shard_map/ppermute | solution.py:22
  11.6 13.0 %collective-permute-start.4 = (bf16[256,512]{1,0:T(8,128)(2,1)S(1)}, bf16[256,512]{1,0:T(8,128)(2,1)S(1)}, u32[]{:S(2)}, u32[]{:S(2)}) collective-permute-start(bf16[256,512]{1,0:T(8,128)(2,1)S(1)} %multiply_convert_fusion.1), channel_id=1, source_target_pairs={{0,8},{8,0},{1,9},{9,1},{2,10},{10,2},{3,11},{11,3},{4,12},{12,4},... | collective-permute-start | bytes 786440 | tf_op jit(solution)/shard_map/ppermute | solution.py:22
  29.9 54.2 %collective-permute-start.5 = (bf16[2,4,256,512]{3,2,1,0:T(8,128)(2,1)}, bf16[2,4,256,512]{3,2,1,0:T(8,128)(2,1)}, u32[]{:S(2)}, u32[]{:S(2)}) collective-permute-start(bf16[2,4,256,512]{3,2,1,0:T(8,128)(2,1)} %shard_map.129), channel_id=1, source_target_pairs={{0,4},{4,0},{1,5},{5,1},{2,6},{6,2},{3,7},{7,3},{8,12},{12,8},{9,1... | collective-permute-start | bytes 6291464 | tf_op jit(solution)/shard_map/ppermute | solution.py:22
  29.9 9.4 %collective-permute-start.6 = (bf16[256,512]{1,0:T(8,128)(2,1)S(1)}, bf16[256,512]{1,0:T(8,128)(2,1)S(1)}, u32[]{:S(2)}, u32[]{:S(2)}) collective-permute-start(bf16[256,512]{1,0:T(8,128)(2,1)S(1)} %multiply_convert_fusion.1), channel_id=1, source_target_pairs={{0,3},{1,0},{2,1},{3,2},{4,7},{5,4},{6,5},{7,6},{8,11},{9,8},{10,9... | collective-permute-start | bytes 786440 | tf_op jit(solution)/shard_map/ppermute | solution.py:22
  46.6 52.2 %collective-permute-start.9 = (bf16[2,4,256,512]{3,2,1,0:T(8,128)(2,1)}, bf16[2,4,256,512]{3,2,1,0:T(8,128)(2,1)}, u32[]{:S(2)}, u32[]{:S(2)}) collective-permute-start(bf16[2,4,256,512]{3,2,1,0:T(8,128)(2,1)} %shard_map.130), channel_id=1, source_target_pairs={{0,4},{4,0},{1,5},{5,1},{2,6},{6,2},{3,7},{7,3},{8,12},{12,8},{9,1... | collective-permute-start | bytes 6291464 | tf_op jit(solution)/shard_map/ppermute | solution.py:22
  46.6 8.7 %collective-permute-start.8 = (bf16[256,512]{1,0:T(8,128)(2,1)S(1)}, bf16[256,512]{1,0:T(8,128)(2,1)S(1)}, u32[]{:S(2)}, u32[]{:S(2)}) collective-permute-start(bf16[256,512]{1,0:T(8,128)(2,1)S(1)} %collective-permute-done.6), channel_id=1, source_target_pairs={{0,8},{8,0},{1,9},{9,1},{2,10},{10,2},{3,11},{11,3},{4,12},{12,4},... | collective-permute-start | bytes 786440 | tf_op jit(solution)/shard_map/ppermute | solution.py:22
  47.2 22.6 %collective-permute-start.11 = (bf16[2,256,512]{2,1,0:T(8,128)(2,1)S(1)}, bf16[2,256,512]{2,1,0:T(8,128)(2,1)S(1)}, u32[]{:S(2)}, u32[]{:S(2)}) collective-permute-start(bf16[2,256,512]{2,1,0:T(8,128)(2,1)S(1)} %pad_maximum_fusion.rest_0_), channel_id=1, source_target_pairs={{0,16},{16,0},{1,17},{17,1},{2,18},{18,2},{3,19},{19,3},{4,20},{20... | collective-permute-start | bytes 1572872 | tf_op jit(solution)/shard_map/ppermute | solution.py:22
  48.8 21.0 %collective-permute-start.16 = (bf16[2,256,512]{2,1,0:T(8,128)(2,1)S(1)}, bf16[2,256,512]{2,1,0:T(8,128)(2,1)S(1)}, u32[]{:S(2)}, u32[]{:S(2)}) collective-permute-start(bf16[2,256,512]{2,1,0:T(8,128)(2,1)S(1)} %pad_maximum_fusion.rest_0_), channel_id=1, source_target_pairs={{0,4},{4,0},{1,5},{5,1},{2,6},{6,2},{3,7},{7,3},{8,12},{12,8},{9,1... | collective-permute-start | bytes 1572872 | tf_op jit(solution)/shard_map/ppermute | solution.py:22
  55.4 13.9 %collective-permute-start.10 = (bf16[256,512]{1,0:T(8,128)(2,1)S(1)}, bf16[256,512]{1,0:T(8,128)(2,1)S(1)}, u32[]{:S(2)}, u32[]{:S(2)}) collective-permute-start(bf16[256,512]{1,0:T(8,128)(2,1)S(1)} %multiply_convert_fusion.1), channel_id=1, source_target_pairs={{0,2},{1,3},{2,0},{3,1},{4,6},{5,7},{6,4},{7,5},{8,10},{9,11},{10,... | collective-permute-start | bytes 786440 | tf_op jit(solution)/shard_map/ppermute | solution.py:22
  69.2 14.0 %collective-permute-start.12 = (bf16[2,256,512]{2,1,0:T(8,128)(2,1)S(1)}, bf16[2,256,512]{2,1,0:T(8,128)(2,1)}, u32[]{:S(2)}, u32[]{:S(2)}) collective-permute-start(bf16[2,256,512]{2,1,0:T(8,128)(2,1)S(1)} %pad_maximum_fusion.1.rest_2_), channel_id=1, source_target_pairs={{0,8},{8,0},{1,9},{9,1},{2,10},{10,2},{3,11},{11,3},{4,12},{12,4},... | collective-permute-start | bytes 1572872 | tf_op jit(solution)/shard_map/ppermute | solution.py:22
  69.8 13.4 %collective-permute-start.18 = (bf16[2,256,512]{2,1,0:T(8,128)(2,1)S(1)}, bf16[2,256,512]{2,1,0:T(8,128)(2,1)S(1)}, u32[]{:S(2)}, u32[]{:S(2)}) collective-permute-start(bf16[2,256,512]{2,1,0:T(8,128)(2,1)S(1)} %pad_maximum_fusion.1.rest_2_), channel_id=1, source_target_pairs={{0,4},{4,0},{1,5},{5,1},{2,6},{6,2},{3,7},{7,3},{8,12},{12,8},{9,1... | collective-permute-start | bytes 1572872 | tf_op jit(solution)/shard_map/ppermute | solution.py:22
  79.3 13.8 %collective-permute-start.13 = (bf16[2,256,512]{2,1,0:T(8,128)(2,1)S(1)}, bf16[2,256,512]{2,1,0:T(8,128)(2,1)}, u32[]{:S(2)}, u32[]{:S(2)}) collective-permute-start(bf16[2,256,512]{2,1,0:T(8,128)(2,1)S(1)} %pad_maximum_fusion.2.rest_4_), channel_id=1, source_target_pairs={{0,16},{16,0},{1,17},{17,1},{2,18},{18,2},{3,19},{19,3},{4,20},{20... | collective-permute-start | bytes 1572872 | tf_op jit(solution)/shard_map/ppermute | solution.py:22
  83.2 11.4 %collective-permute-start.20 = (bf16[2,256,512]{2,1,0:T(8,128)(2,1)S(1)}, bf16[2,256,512]{2,1,0:T(8,128)(2,1)}, u32[]{:S(2)}, u32[]{:S(2)}) collective-permute-start(bf16[2,256,512]{2,1,0:T(8,128)(2,1)S(1)} %pad_maximum_fusion.2.rest_4_), channel_id=1, source_target_pairs={{0,4},{4,0},{1,5},{5,1},{2,6},{6,2},{3,7},{7,3},{8,12},{12,8},{9,1... | collective-permute-start | bytes 1572872 | tf_op jit(solution)/shard_map/ppermute | solution.py:22
  83.2 11.4 %collective-permute-start.17 = (bf16[2,256,512]{2,1,0:T(8,128)(2,1)S(1)}, bf16[2,256,512]{2,1,0:T(8,128)(2,1)}, u32[]{:S(2)}, u32[]{:S(2)}) collective-permute-start(bf16[2,256,512]{2,1,0:T(8,128)(2,1)S(1)} %collective-permute-done.11.rest_1_), channel_id=1, source_target_pairs={{0,4},{4,0},{1,5},{5,1},{2,6},{6,2},{3,7},{7,3},{8,12},{12,8},{9,1... | collective-permute-start | bytes 1572872 | tf_op jit(solution)/shard_map/ppermute | solution.py:22
  84.0 14.8 %collective-permute-start.15 = (bf16[2,256,512]{2,1,0:T(8,128)(2,1)S(1)}, bf16[2,256,512]{2,1,0:T(8,128)(2,1)}, u32[]{:S(2)}, u32[]{:S(2)}) collective-permute-start(bf16[2,256,512]{2,1,0:T(8,128)(2,1)S(1)} %pad_maximum_fusion.3.rest_6_), channel_id=1, source_target_pairs={{0,8},{8,0},{1,9},{9,1},{2,10},{10,2},{3,11},{11,3},{4,12},{12,4},... | collective-permute-start | bytes 1572872 | tf_op jit(solution)/shard_map/ppermute | solution.py:22
  93.1 16.6 %collective-permute-start.26 = (bf16[2,256,512]{2,1,0:T(8,128)(2,1)}, bf16[2,256,512]{2,1,0:T(8,128)(2,1)}, u32[]{:S(2)}, u32[]{:S(2)}) collective-permute-start(bf16[2,256,512]{2,1,0:T(8,128)(2,1)} %get-tuple-element.32), channel_id=1, source_target_pairs={{0,8},{8,0},{1,9},{9,1},{2,10},{10,2},{3,11},{11,3},{4,12},{12,4},... | collective-permute-start | bytes 1572872 | tf_op jit(solution)/shard_map/ppermute | solution.py:22
  94.6 17.8 %collective-permute-start.22 = (bf16[2,256,512]{2,1,0:T(8,128)(2,1)S(1)}, bf16[2,256,512]{2,1,0:T(8,128)(2,1)}, u32[]{:S(2)}, u32[]{:S(2)}) collective-permute-start(bf16[2,256,512]{2,1,0:T(8,128)(2,1)S(1)} %pad_maximum_fusion.3.rest_6_), channel_id=1, source_target_pairs={{0,4},{4,0},{1,5},{5,1},{2,6},{6,2},{3,7},{7,3},{8,12},{12,8},{9,1... | collective-permute-start | bytes 1572872 | tf_op jit(solution)/shard_map/ppermute | solution.py:22
  94.6 18.4 %collective-permute-start.19 = (bf16[2,256,512]{2,1,0:T(8,128)(2,1)}, bf16[2,256,512]{2,1,0:T(8,128)(2,1)}, u32[]{:S(2)}, u32[]{:S(2)}) collective-permute-start(bf16[2,256,512]{2,1,0:T(8,128)(2,1)} %collective-permute-done.12.rest_3_), channel_id=1, source_target_pairs={{0,4},{4,0},{1,5},{5,1},{2,6},{6,2},{3,7},{7,3},{8,12},{12,8},{9,1... | collective-permute-start | bytes 1572872 | tf_op jit(solution)/shard_map/ppermute | solution.py:22
  98.9 14.7 %collective-permute-start.21 = (bf16[2,256,512]{2,1,0:T(8,128)(2,1)}, bf16[2,256,512]{2,1,0:T(8,128)(2,1)}, u32[]{:S(2)}, u32[]{:S(2)}) collective-permute-start(bf16[2,256,512]{2,1,0:T(8,128)(2,1)} %collective-permute-done.13.rest_5_), channel_id=1, source_target_pairs={{0,4},{4,0},{1,5},{5,1},{2,6},{6,2},{3,7},{7,3},{8,12},{12,8},{9,1... | collective-permute-start | bytes 1572872 | tf_op jit(solution)/shard_map/ppermute | solution.py:22
  98.9 16.2 %collective-permute-start.23 = (bf16[2,256,512]{2,1,0:T(8,128)(2,1)}, bf16[2,256,512]{2,1,0:T(8,128)(2,1)}, u32[]{:S(2)}, u32[]{:S(2)}) collective-permute-start(bf16[2,256,512]{2,1,0:T(8,128)(2,1)} %collective-permute-done.15.rest_7_), channel_id=1, source_target_pairs={{0,4},{4,0},{1,5},{5,1},{2,6},{6,2},{3,7},{7,3},{8,12},{12,8},{9,1... | collective-permute-start | bytes 1572872 | tf_op jit(solution)/shard_map/ppermute | solution.py:22
  109.7 18.7 %collective-permute-start.29 = (bf16[2,256,512]{2,1,0:T(8,128)(2,1)}, bf16[2,256,512]{2,1,0:T(8,128)(2,1)S(1)}, u32[]{:S(2)}, u32[]{:S(2)}) collective-permute-start(bf16[2,256,512]{2,1,0:T(8,128)(2,1)} %copy-done.10), channel_id=1, source_target_pairs={{0,16},{16,0},{1,17},{17,1},{2,18},{18,2},{3,19},{19,3},{4,20},{20... | collective-permute-start | bytes 1572872 | tf_op jit(solution)/shard_map/ppermute | solution.py:22
  112.4 29.1 %collective-permute-start.32 = (bf16[2,256,512]{2,1,0:T(8,128)(2,1)}, bf16[2,256,512]{2,1,0:T(8,128)(2,1)S(1)}, u32[]{:S(2)}, u32[]{:S(2)}) collective-permute-start(bf16[2,256,512]{2,1,0:T(8,128)(2,1)} %copy-done.12), channel_id=1, source_target_pairs={{0,8},{8,0},{1,9},{9,1},{2,10},{10,2},{3,11},{11,3},{4,12},{12,4},... | collective-permute-start | bytes 1572872 | tf_op jit(solution)/shard_map/ppermute | solution.py:22
  113.0 32.0 %collective-permute-start.24 = (bf16[2,256,512]{2,1,0:T(8,128)(2,1)}, bf16[2,256,512]{2,1,0:T(8,128)(2,1)S(1)}, u32[]{:S(2)}, u32[]{:S(2)}) collective-permute-start(bf16[2,256,512]{2,1,0:T(8,128)(2,1)} %copy-done.11), channel_id=1, source_target_pairs={{0,16},{16,0},{1,17},{17,1},{2,18},{18,2},{3,19},{19,3},{4,20},{20... | collective-permute-start | bytes 1572872 | tf_op jit(solution)/shard_map/ppermute | solution.py:22
  113.5 26.8 %collective-permute-start.27 = (bf16[256,512]{1,0:T(8,128)(2,1)S(1)}, bf16[256,512]{1,0:T(8,128)(2,1)S(1)}, u32[]{:S(2)}, u32[]{:S(2)}) collective-permute-start(bf16[256,512]{1,0:T(8,128)(2,1)S(1)} %fusion.7), channel_id=1, source_target_pairs={{0,16},{16,0},{1,17},{17,1},{2,18},{18,2},{3,19},{19,3},{4,20},{20... | collective-permute-start | bytes 786440 | tf_op jit(solution)/shard_map/ppermute | solution.py:22
  128.5 14.6 %collective-permute-start.30 = (bf16[256,512]{1,0:T(8,128)(2,1)S(1)}, bf16[256,512]{1,0:T(8,128)(2,1)S(1)}, u32[]{:S(2)}, u32[]{:S(2)}) collective-permute-start(bf16[256,512]{1,0:T(8,128)(2,1)S(1)} %fusion.8), channel_id=1, source_target_pairs={{0,8},{8,0},{1,9},{9,1},{2,10},{10,2},{3,11},{11,3},{4,12},{12,4},... | collective-permute-start | bytes 786440 | tf_op jit(solution)/shard_map/ppermute | solution.py:22
  141.4 22.9 %collective-permute-start.28 = (bf16[256,512]{1,0:T(8,128)(2,1)S(1)}, bf16[256,512]{1,0:T(8,128)(2,1)S(1)}, u32[]{:S(2)}, u32[]{:S(2)}) collective-permute-start(bf16[256,512]{1,0:T(8,128)(2,1)S(1)} %fusion.2), channel_id=1, source_target_pairs={{0,2},{1,3},{2,0},{3,1},{4,6},{5,7},{6,4},{7,5},{8,10},{9,11},{10,... | collective-permute-start | bytes 786440 | tf_op jit(solution)/shard_map/ppermute | solution.py:22
  143.2 21.0 %collective-permute-start.31 = (bf16[256,512]{1,0:T(8,128)(2,1)S(1)}, bf16[256,512]{1,0:T(8,128)(2,1)S(1)}, u32[]{:S(2)}, u32[]{:S(2)}) collective-permute-start(bf16[256,512]{1,0:T(8,128)(2,1)S(1)} %fusion.1), channel_id=1, source_target_pairs={{0,3},{1,0},{2,1},{3,2},{4,7},{5,4},{6,5},{7,6},{8,11},{9,8},{10,9... | collective-permute-start | bytes 786440 | tf_op jit(solution)/shard_map/ppermute | solution.py:22
  145.1 19.2 %collective-permute-start.25 = (bf16[256,512]{1,0:T(8,128)(2,1)S(1)}, bf16[256,512]{1,0:T(8,128)(2,1)S(1)}, u32[]{:S(2)}, u32[]{:S(2)}) collective-permute-start(bf16[256,512]{1,0:T(8,128)(2,1)S(1)} %fusion.6), channel_id=1, source_target_pairs={{0,8},{8,0},{1,9},{9,1},{2,10},{10,2},{3,11},{11,3},{4,12},{12,4},... | collective-permute-start | bytes 786440 | tf_op jit(solution)/shard_map/ppermute | solution.py:22
  148.8 15.5 %collective-permute-start.34 = (bf16[256,512]{1,0:T(8,128)(2,1)S(1)}, bf16[256,512]{1,0:T(8,128)(2,1)S(1)}, u32[]{:S(2)}, u32[]{:S(2)}) collective-permute-start(bf16[256,512]{1,0:T(8,128)(2,1)S(1)} %fusion), channel_id=1, source_target_pairs={{0,1},{1,2},{2,3},{3,0},{4,5},{5,6},{6,7},{7,4},{8,9},{9,10},{10,1... | collective-permute-start | bytes 786440 | tf_op jit(solution)/shard_map/ppermute | solution.py:22
  (24 other events, 254.3 us)

commit v4 on v3

v4 whole, which is shorter than its diff:
```python
import functools

import jax
import jax.numpy as jnp
from jax import lax
from jax.experimental import pallas as pl
from jax.experimental.pallas import tpu as pltpu
from jax.sharding import PartitionSpec as P

VOCAB = 128256
EPS = 1e-05
BETA = 0.5
CORES = 2
OUTER = 2
PAIR_VMEM = 14 * 1024 * 1024
WEIGHT_VMEM = 22 * 1024 * 1024
NOMINAL = pl.CostEstimate(flops=1024, bytes_accessed=1024, transcendentals=0)
BF16 = jnp.bfloat16
F32 = jnp.float32


def swap(value, axis, step):
    size = lax.axis_size(axis)
    return lax.ppermute(value, axis, [(place, (place + step) % size) for place in range(size)])


def after(value, *earlier):
    return lax.optimization_barrier((value, earlier))[0]


def widen(parts):
    return functools.reduce(jnp.add, [part.astype(F32) for part in parts])


def chunk_order(tp_count):
    order = [0]
    for step in range(1, tp_count // 2 + 1):
        order += [step] if 2 * step == tp_count else [step, tp_count - step]
    return order


def inner_first(order, chunk):
    return order.index(chunk) % 2 == 0


def theirs_kernel(places_ref, cot_ref, first_ref, second_ref, out_ref):
    for slot, resid_ref in enumerate((first_ref, second_ref)):
        product = jnp.dot(cot_ref[...], resid_ref[...], preferred_element_type=F32)
        out_ref[slot, 0] = product.astype(BF16)


def ours_kernel(places_ref, cot_ref, first_ref, second_ref, other_ref, *outs):
    step = pl.program_id(0)
    at_outer, at_inner = step // 2, lax.rem(step, 2)
    for slot, resid_ref in enumerate((first_ref, second_ref)):
        send_ref, keep_ref = outs[2 * slot : 2 * slot + 2]
        product = jnp.dot(cot_ref[...], resid_ref[...], preferred_element_type=F32)
        total = (product + other_ref[slot, 0].astype(F32)).astype(BF16)
        way, place = (at_inner, at_outer) if slot == 0 else (at_outer, at_inner)

        @pl.when(way == 1)
        def _():
            send_ref[place] = total

        @pl.when(way == 0)
        def _():
            keep_ref[place] = total


def pair_product(residual, cot_t, places, rows, other):
    features, tokens = cot_t.shape
    steps = places.shape[0] // 2
    in_specs = [
        pl.BlockSpec((features, tokens), lambda i, p: (0, 0)),
        pl.BlockSpec((tokens, rows), lambda i, p: (0, p[i])),
        pl.BlockSpec((tokens, rows), lambda i, p: (0, p[steps + i])),
    ]
    operands = [cot_t, residual, residual]
    block = pl.BlockSpec((2, 1, features, rows), lambda i, p: (0, i, 0, 0))
    if other is None:
        kernel, out_specs = theirs_kernel, block
        out_shape = jax.ShapeDtypeStruct((2, steps, features, rows), BF16)
    else:
        kernel = ours_kernel
        in_specs.append(block)
        operands.append(other)
        out_specs = [pl.BlockSpec((2, features, rows), lambda i, p: (0, 0, 0))] * 4
        out_shape = [jax.ShapeDtypeStruct((2, features, rows), BF16)] * 4
    return pl.pallas_call(
        kernel,
        out_shape=out_shape,
        grid_spec=pltpu.PrefetchScalarGridSpec(
            num_scalar_prefetch=1, grid=(steps,), in_specs=in_specs, out_specs=out_specs
        ),
        cost_estimate=NOMINAL,
        compiler_params=pltpu.CompilerParams(vmem_limit_bytes=PAIR_VMEM),
    )(places, *operands)


def place_weight(inner_flags, offsets_ref, pieces, weight_ref):
    step = pl.program_id(0)
    at_outer, at_inner = step // 2, lax.rem(step, 2)
    rows = pieces[0].shape[1]
    for chunk, flag in enumerate(inner_flags):
        way = at_outer if flag else at_inner
        where = pl.ds(pl.multiple_of(offsets_ref[chunk], rows), rows)
        for late in range(2):
            piece = pieces[chunk * 2 + late]

            @pl.when(way == late)
            def _():
                weight_ref[where, :] = piece[0]


def piece_specs(inner_flags, rows, features):
    specs = []
    for flag in inner_flags:
        for late in range(2):
            if flag:
                index = lambda i, *_, first=2 * late: (jnp.clip(i - first, 0, 1), 0, 0)
            else:
                index = lambda i, *_: (i // 2, 0, 0)
            specs.append(pl.BlockSpec((1, rows, features), index))
    return specs


def value_kernel(inner_flags, places_ref, offsets_ref, resid_ref, *rest):
    pieces, (total_ref, weight_ref) = rest[:-2], rest[-2:]
    place_weight(inner_flags, offsets_ref, pieces, weight_ref)
    product = jnp.dot(resid_ref[...], weight_ref[...], preferred_element_type=F32)

    @pl.when(pl.program_id(0) == 0)
    def _():
        total_ref[...] = product

    @pl.when(pl.program_id(0) > 0)
    def _():
        total_ref[...] += product


def value_end_kernel(
    width, inner_flags, places_ref, offsets_ref, resid_ref, first_ref, cot_ref, inv_ref, *rest
):
    pieces, (value_ref, coef_ref, weight_ref, total_ref) = rest[:-4], rest[-4:]
    step = pl.program_id(0)
    place_weight(inner_flags, offsets_ref, pieces, weight_ref)
    product = jnp.dot(resid_ref[...], weight_ref[...], preferred_element_type=F32)

    @pl.when(step == 0)
    def _():
        total_ref[...] = first_ref[...] + product

    @pl.when(step > 0)
    def _():
        total_ref[...] += product

    @pl.when(step == pl.num_programs(0) - 1)
    def _():
        total = total_ref[...]
        inv = inv_ref[...]
        value_ref[...] = (total * inv).astype(BF16)
        share = jnp.sum(total * cot_ref[...].astype(F32), axis=1, keepdims=True)
        coef_ref[...] = share * (inv * inv) * (1.0 / width)


def grad_kernel(inner_flags, places_ref, offsets_ref, resid_ref, cot_ref, coef_ref, *rest):
    pieces, (out_ref, weight_ref) = rest[: 2 * len(inner_flags)], rest[-2:]
    place_weight(inner_flags, offsets_ref, pieces, weight_ref)
    grad = lax.dot_general(
        cot_ref[...], weight_ref[...], (((1,), (1,)), ((), ())), preferred_element_type=F32
    )
    out_ref[...] = (grad - resid_ref[...].astype(F32) * coef_ref[...]).astype(BF16)


def weight_call(kernel, inner_flags, places, offsets, residual, wholes, pieces, out_shape, out_blocks, earlier=None):
    tokens, width = residual.shape
    rows, features = pieces[0].shape[1:]
    steps = places.shape[0]
    depth = width // (CORES * steps)
    block = pl.BlockSpec((tokens, depth), lambda i, p, o: (0, p[i]))

    def whole(array):
        return pl.BlockSpec(array.shape, lambda i, *_: (0, 0))

    scratch = [pltpu.VMEM((depth, features), BF16)]
    if out_blocks:
        out_specs = block
    else:
        out_specs = jax.tree.map(whole, out_shape)
        if isinstance(out_shape, list):
            scratch.append(pltpu.VMEM((tokens, features), F32))
    in_specs = [block] + [whole(array) for array in wholes] + piece_specs(inner_flags, rows, features)
    operands = [places, offsets, residual, *wholes, *pieces]
    aliases = {}
    if earlier is not None:
        aliases = {len(operands): 0}
        in_specs.append(pl.BlockSpec(memory_space=pl.ANY))
        operands.append(earlier)
    return pl.pallas_call(
        functools.partial(kernel, inner_flags),
        out_shape=out_shape,
        grid_spec=pltpu.PrefetchScalarGridSpec(
            num_scalar_prefetch=2,
            grid=(steps,),
            in_specs=in_specs,
            out_specs=out_specs,
            scratch_shapes=scratch,
        ),
        input_output_aliases=aliases,
        cost_estimate=NOMINAL,
        compiler_params=pltpu.CompilerParams(vmem_limit_bytes=WEIGHT_VMEM),
    )(*operands)


def sequence_weight(trainee_logp, shard_max, shard_sum, owned, seq_length, rep_count, tp_count, tp_place):
    rows_here = trainee_logp.shape[0]
    seq = shard_max.shape[0]
    packed = jnp.concatenate([shard_max, shard_sum, owned, trainee_logp]).reshape(-1, 128)
    shares = [packed] + [swap(packed, "tp", s) for s in range(1, tp_count)]
    shares = [share.reshape(-1) for share in shares]
    top_max = functools.reduce(jnp.maximum, [share[:seq] for share in shares])
    sum_exp = sum(share[seq : 2 * seq] * jnp.exp(share[:seq] - top_max) for share in shares)
    picked = sum(share[2 * seq : 3 * seq] for share in shares)
    ref_logp = picked - top_max - jnp.log(sum_exp)
    total = jnp.zeros((), F32)
    for s, share in enumerate(shares):
        first = lax.rem(tp_place - s + tp_count, tp_count) * rows_here
        live = first + jnp.arange(rows_here, dtype=jnp.int32) < seq_length
        diff = share[3 * seq :] - lax.dynamic_slice_in_dim(ref_logp, first, rows_here)
        total = total + jnp.sum(jnp.where(live, diff, 0.0))
    seq_delta = total / seq_length.astype(F32)
    return 2.0 * jax.nn.sigmoid(BETA * seq_delta) / rep_count


def per_device(
    residual,
    norm_gain,
    value_weight,
    value_cot,
    trainee_logp,
    ref_shard_max,
    ref_shard_sum,
    ref_target_logit,
    target_ids,
    lengths,
):
    rows_here, width = residual.shape
    features = value_cot.shape[1]
    tp_count = lax.axis_size("tp")
    outer, inner = lax.axis_size("outer"), lax.axis_size("inner")
    rep_count = outer * inner * CORES
    tp_place = lax.axis_index("tp")
    core = lax.axis_index("core")
    at_inner = lax.axis_index("inner")
    at_outer = lax.axis_index("outer")
    rep_place = (at_outer * inner + at_inner) * CORES + core
    depth = width // rep_count
    rows = depth // tp_count
    order = chunk_order(tp_count)
    in_place = rows % 128 == 0 and outer == 2 and inner == 2

    gained = (value_weight.astype(F32) * norm_gain.astype(F32)[:, None]).astype(BF16)
    residual, gained = lax.optimization_barrier((residual, gained))
    resid_wide = residual.astype(F32)
    squares = jnp.sum(resid_wide * resid_wide, axis=1, keepdims=True)

    owned = jnp.where(
        target_ids // (VOCAB // tp_count) == tp_place,
        ref_target_logit[0],
        jnp.zeros_like(ref_target_logit[0]),
    )
    owned = after(owned, squares)
    seq_length = lax.dynamic_index_in_dim(lengths, rep_place, keepdims=False)
    seq_weight = sequence_weight(
        trainee_logp, ref_shard_max[0], ref_shard_sum[0], owned, seq_length, rep_count, tp_count, tp_place
    )
    positions = tp_place * rows_here + jnp.arange(rows_here, dtype=jnp.int32)
    row_scale = (positions < seq_length).astype(F32) * seq_weight
    inv_rms = lax.rsqrt(squares * (1.0 / width) + EPS)
    cot = (inv_rms * row_scale[:, None] * value_cot.astype(F32)).astype(BF16)
    cot_t = cot.T

    def near_of(k, block):
        first = "inner" if inner_first(order, k) else "outer"
        return [swap(block, first, s) for s in range(1, lax.axis_size(first))]

    def far_of(k, block, nears):
        second = "outer" if inner_first(order, k) else "inner"
        near = jnp.stack([block] + nears)
        return [near] + [swap(near, second, s) for s in range(1, lax.axis_size(second))]

    def place_of(o, i, c, k):
        chip = lax.rem(at_outer + o, outer) * inner + lax.rem(at_inner + i, inner)
        return (chip * CORES + c) * tp_count + lax.rem(tp_place + k, tp_count)

    chips = [(o, i) for o in range(outer) for i in range(inner)]
    if not in_place:
        product = jnp.dot(cot_t, residual, preferred_element_type=F32).astype(BF16)
        product = product.reshape(features, -1, rows).transpose(1, 0, 2)

    def places_of(pair, c):
        return jnp.stack([place_of(o, i, c, k) for k in pair for o, i in chips]).astype(jnp.int32)

    def for_other(pair, cot_t):
        places = places_of(pair, 1 - core)
        if in_place:
            return pair_product(residual, cot_t, places, rows, None)
        return after(product, cot_t)[places].reshape(2, len(chips), features, rows)

    def for_us(pair, other):
        places = places_of(pair, core)
        if in_place:
            send_a, keep_a, send_b, keep_b = pair_product(residual, cot_t, places, rows, other)
            return ([send_a], keep_a), ([send_b], keep_b)
        total = widen([product[places], other.reshape(-1, features, rows)]).astype(BF16)
        total = total.reshape(2, outer, inner, features, rows)
        first = ([total[0, :, s] for s in range(1, inner)], total[0, :, 0])
        second = ([total[1, s] for s in range(1, outer)], total[1, 0])
        return first, second

    def first_round(sides):
        return [
            [swap(send, axis, s + 1) for s, send in enumerate(sends)]
            for axis, (sends, _) in zip(("inner", "outer"), sides)
        ]

    def second_round(sides, got):
        later = []
        for axis, (_, keep), parts in zip(("outer", "inner"), sides, got):
            later.append(
                [
                    swap(widen([part[s] for part in [keep] + parts]).astype(BF16), axis, s)
                    for s in range(1, lax.axis_size(axis))
                ]
            )
        return later

    def summed(sides, got, later):
        return [
            widen([part[0] for part in [keep] + parts] + last)
            for (_, keep), parts, last in zip(sides, got, later)
        ]

    backward = order[::-1]
    pairs = [backward[i : i + 2] for i in range(0, tp_count, 2)]
    own_pieces = {}
    arrived = {0: gained, order[1]: swap(gained, "tp", order[1])}
    near = {0: near_of(0, gained)}
    (arrived[order[1]], near[0], squares_done) = lax.optimization_barrier(
        (arrived[order[1]], near[0], squares)
    )
    near[order[1]] = near_of(order[1], arrived[order[1]])
    own_pieces[0] = far_of(0, gained, near[0])
    arrived[order[2]] = swap(after(gained, squares_done), "tp", order[2])
    near[order[1]], arrived[order[2]], cot_t = lax.optimization_barrier(
        (near[order[1]], arrived[order[2]], cot_t)
    )
    own_pieces[order[1]] = far_of(order[1], arrived[order[1]], near[order[1]])
    near[order[2]] = near_of(order[2], arrived[order[2]])
    for k in order[3:]:
        arrived[k] = swap(after(gained, arrived[order[2]]), "tp", k)
    theirs = [for_other(pairs[0], cot_t)]
    theirs.append(for_other(pairs[1], after(cot_t, theirs[0])))
    near[order[2]], arrived[order[3]], theirs, own_pieces[0] = lax.optimization_barrier(
        (near[order[2]], arrived[order[3]], theirs, own_pieces[0])
    )
    own_pieces[order[2]] = far_of(order[2], arrived[order[2]], near[order[2]])
    near[order[3]] = near_of(order[3], arrived[order[3]])
    others = [swap(part, "core", 1) for part in theirs]
    sides = [for_us(pairs[0], others[0])]
    got = [first_round(sides[0])]
    near[order[3]], side_done, own_pieces[order[1]] = lax.optimization_barrier(
        (near[order[3]], sides[0], own_pieces[order[1]])
    )
    own_pieces[order[3]] = far_of(order[3], arrived[order[3]], near[order[3]])
    sides.append(for_us(pairs[1], after(others[1], side_done)))
    for n in range(2, len(pairs)):
        for k in order[2 * n : 2 * n + 2]:
            own_pieces[k] = far_of(k, arrived[k], near_of(k, arrived[k]))
        others.append(swap(for_other(pairs[n], after(cot_t, sides[-1])), "core", 1))
        sides.append(for_us(pairs[n], others[-1]))
    got[0], side_done = lax.optimization_barrier((got[0], sides[1:]))
    later = [second_round(sides[0], got[0])]
    sides[1:] = after(sides[1:], got[0])
    got += [first_round(side) for side in sides[1:]]
    other_pieces = {
        k: [swap(piece, "core", 1) for piece in pieces] for k, pieces in own_pieces.items()
    }
    value_inv, own_pieces = lax.optimization_barrier((inv_rms, own_pieces))

    if in_place:
        pieces = [
            [piece for k in order for piece in side[k]] for side in (own_pieces, other_pieces)
        ]
        flags = tuple(inner_first(order, k) for k in order)
        places = [
            jnp.stack([place_of(o, i, c, 0) // tp_count for o, i in chips]).astype(jnp.int32)
            for c in (core, 1 - core)
        ]
        offsets = jnp.stack([lax.rem(tp_place - k + tp_count, tp_count) * rows for k in order])
        offsets = offsets.astype(jnp.int32)
        wide = jax.ShapeDtypeStruct((rows_here, features), F32)
        first_total = weight_call(
            value_kernel, flags, places[0], offsets, after(residual, value_inv), [], pieces[0], wide, False
        )
        value_proj, coefficient = weight_call(
            functools.partial(value_end_kernel, width),
            flags,
            places[1],
            offsets,
            residual,
            [first_total, cot, inv_rms],
            pieces[1],
            [
                jax.ShapeDtypeStruct((rows_here, features), BF16),
                jax.ShapeDtypeStruct((rows_here, 1), F32),
            ],
            False,
        )
        later[0], got[1], coefficient = lax.optimization_barrier((later[0], got[1], coefficient))
        later += [second_round(side, parts) for side, parts in zip(sides[1:], got[1:])]
        sums = dict(zip(pairs[0], summed(sides[0], got[0], later[0])))
        last = [swap(sums[k].astype(BF16), "tp", k) for k in pairs[0]]
        grad_shape = jax.ShapeDtypeStruct((rows_here, width), BF16)
        resid_grad = weight_call(
            grad_kernel, flags, places[0], offsets, residual, [cot, coefficient], pieces[0], grad_shape, True
        )
        later[1], coefficient, resid_grad = lax.optimization_barrier((later[1], coefficient, resid_grad))
        sums.update(zip(pairs[1], summed(sides[1], got[1], later[1])))
        last.append(swap(sums[pairs[1][0]].astype(BF16), "tp", pairs[1][0]))
        resid_grad = weight_call(
            grad_kernel,
            flags,
            places[1],
            offsets,
            residual,
            [cot, coefficient],
            pieces[1],
            grad_shape,
            True,
            resid_grad,
        )
    else:
        weight = []
        for side in (own_pieces, other_pieces):
            for k in order:
                both = jnp.stack(side[k])
                weight.append(both if inner_first(order, k) else jnp.swapaxes(both, 0, 1))
        weight = jnp.stack(weight).reshape(CORES, tp_count, outer, inner, rows, features)
        by_place = [order.index(k) for k in range(tp_count)]
        weight = weight[:, jnp.array(by_place)]
        weight = weight[jnp.array([core, 1 - core])]
        weight = weight[:, (tp_place - jnp.arange(tp_count)) % tp_count]
        weight = weight[:, :, (at_outer - jnp.arange(outer)) % outer]
        weight = weight[:, :, :, (at_inner - jnp.arange(inner)) % inner]
        weight = weight.transpose(2, 3, 0, 1, 4, 5).reshape(width, features)
        value_acc = jnp.dot(residual, weight, preferred_element_type=F32)
        value_proj = (inv_rms * value_acc).astype(BF16)
        share = jnp.sum(cot.astype(F32) * value_acc, axis=1, keepdims=True)
        coefficient = inv_rms * inv_rms * share * (1.0 / width)
        normed_grad = lax.dot_general(
            cot, weight, (((1,), (1,)), ((), ())), preferred_element_type=F32
        )
        resid_grad = (normed_grad - residual.astype(F32) * coefficient).astype(BF16)
        later += [second_round(side, parts) for side, parts in zip(sides[1:], got[1:])]
        sums = {}
        for pair, *rounds in zip(pairs, sides, got, later):
            sums.update(zip(pair, summed(*rounds)))
        last = [swap(sums[k].astype(BF16), "tp", k) for k in backward[:-1]]
    grad_rows = widen([sums[0]] + last)
    late_gain, late_weight, grad_rows = lax.optimization_barrier((norm_gain, value_weight, grad_rows))
    weight_grad = (late_gain.astype(F32)[None, :] * grad_rows).T
    gain_grad = jnp.sum(late_weight.astype(F32).T * grad_rows, axis=0)
    return (value_proj, resid_grad, weight_grad, gain_grad)


def solution(mesh):
    rep_count, tp_count = mesh.shape["rep"], mesh.shape["tp"]
    split = jax.sharding.Mesh(
        mesh.devices.reshape(OUTER, rep_count // (OUTER * CORES), CORES, tp_count),
        ("outer", "inner", "core", "tp"),
    )
    rep = ("outer", "inner", "core")
    rows = rep + ("tp",)
    return jax.shard_map(
        per_device,
        mesh=split,
        in_specs=(
            P(rows, None),
            P(rows),
            P(rows, None),
            P(rows, None),
            P(rows),
            P("tp", rep),
            P("tp", rep),
            P("tp", rep),
            P(rep),
            P(),
        ),
        out_specs=(P(rows, None), P(rows, None), P(rows, None), P(rows)),
        check_vma=False,
    )
```

time: 167 us -> 159 us (0.952)
  waiting for transfers between devices: 55.2 us -> 29.8 us
  local copies, waits for them, and re-layouts: 8.97 us -> 27 us
  Pallas kernels: 47.5 us -> 44.5 us
  other arithmetic: 15.1 us -> 17.9 us
    ppermute x35, waiting for transfers between devices: 55.2 us -> 29.8 us  [swap(): lax.ppermute(value, axis, [(place, (place + step) % size) for place in ra...]
    unnamed x42 -> x63, local copies, waits for them, and re-layouts: 7.81 us -> 24.7 us
    pallas_call x4, Pallas kernels: 21.7 us -> 17.9 us  [pair_product(): pl.pallas_call(kernel, out_shape=out_shape, grid_spec=pltpu.PrefetchScala...]
    another operation x4 -> x5, other arithmetic: 0.2 us -> 2.25 us  [the longest x4 2.18 us: far_of(): near = jnp.stack([block] + nears)]
    convert_element_type x8, other arithmetic: 2.61 us -> 4.41 us  [the longest x4 2.18 us: second_round(): widen([part[s] for part in [keep] + parts]).astype(BF16)]
    pallas_call x2 -> x4, Pallas kernels: 25.8 us -> 26.6 us  [weight_call(): pl.pallas_call(functools.partial(kernel, inner_flags), out_shape=out_shap...]
  transfers between devices with their start and end apart: 35 -> 35, of which waited for: 10 -> 7; matrix products, arithmetic and copies ran while one was open for 8% -> 8% of each run, Pallas kernels for 25% -> 28%
where the time goes in v4:
time: 159 us; the launch traced here: 158 us
  Pallas kernels  44.5 us (28%)
  starting transfers between devices  33.7 us (21%)
  waiting for transfers between devices  29.8 us (19%)
  local copies, waits for them, and re-layouts  27 us (17%)
  other arithmetic  17.9 us (11%)
  between operations  4.6 us (3%)
    ppermute x35, starting transfers between devices, swap(): lax.ppermute(value, axis, [(place, (place + step) % size) for place in ra...  33.7 us
    ppermute x35, waiting for transfers between devices, swap(): lax.ppermute(value, axis, [(place, (place + step) % size) for place in ra...  29.8 us
    pallas_call x4, Pallas kernels, weight_call(): pl.pallas_call(functools.partial(kernel, inner_flags), out_shape=out_shap...  26.6 us
    unnamed x63, local copies, waits for them, and re-layouts  24.7 us
    pallas_call x4, Pallas kernels, pair_product(): pl.pallas_call(kernel, out_shape=out_shape, grid_spec=pltpu.PrefetchScala...  17.9 us
    reduce_sum x1, other arithmetic, per_device(): squares = jnp.sum(resid_wide * resid_wide, axis=1, keepdims=True)  5.1 us
  transfers between devices with their start and end apart: 35, of which 7 were waited for; matrix products, arithmetic and copies ran while one was open for 8% of the time, Pallas kernels for 28%

profile of v4, /device:TPU:0, one launch (start us, length us, event | category | flops | bytes accessed | tf_op | source)
XLA Modules:
  0.0 157.5 jit_solution(5472033269045674138)
XLA Ops:
  2.5 5.1 %multiply_reduce_fusion = f32[512]{0:T(512)S(1)} fusion(bf16[512,8192]{1,0:T(8,128)(2,1)} %resid_ref.3), kind=kLoop, calls=%fused_computation | loop fusion | flops 12582400 | bytes 8390656 | tf_op jit(solution)/shard_map/reduce_sum | solution.py:265
  7.7 3.1 %collective-permute-start.4 = (f32[52,128]{1,0:T(8,128)S(1)}, f32[52,128]{1,0:T(8,128)S(1)}, u32[]{:S(2)}, u32[]{:S(2)}) collective-permute-start(f32[52,128]{1,0:T(8,128)S(1)} %maximum_bitcast_fusion), channel_id=1, source_target_pairs={{0,1},{1,2},{2,3},{3,0},{4,5},{5,6},{6,7},{7,4},{8,9},{9,10},{10,1... | collective-permute-start | bytes 79880 | tf_op jit(solution)/shard_map/ppermute | solution.py:24
  10.7 2.6 %collective-permute-start.5 = (f32[52,128]{1,0:T(8,128)S(1)}, f32[52,128]{1,0:T(8,128)S(1)}, u32[]{:S(2)}, u32[]{:S(2)}) collective-permute-start(f32[52,128]{1,0:T(8,128)S(1)} %maximum_bitcast_fusion), channel_id=1, source_target_pairs={{0,2},{1,3},{2,0},{3,1},{4,6},{5,7},{6,4},{7,5},{8,10},{9,11},{10,... | collective-permute-start | bytes 79880 | tf_op jit(solution)/shard_map/ppermute | solution.py:24
  15.4 1.5 collective-permute-start.1
  18.1 3.2 %collective-permute-start.3 = (bf16[256,512]{1,0:T(8,128)(2,1)S(1)}, bf16[256,512]{1,0:T(8,128)(2,1)}, u32[]{:S(2)}, u32[]{:S(2)}) collective-permute-start(bf16[256,512]{1,0:T(8,128)(2,1)S(1)} %multiply_convert_fusion.1), channel_id=1, source_target_pairs={{0,3},{1,0},{2,1},{3,2},{4,7},{5,4},{6,5},{7,6},{8,11},{9,8},{10,9... | collective-permute-start | bytes 786440 | tf_op jit(solution)/shard_map/ppermute | solution.py:24
  25.8 1.5 collective-permute-start.2
  29.4 5.6 %collective-permute-done.2 = bf16[256,512]{1,0:T(8,128)(2,1)S(1)} collective-permute-done((bf16[256,512]{1,0:T(8,128)(2,1)S(1)}, bf16[256,512]{1,0:T(8,128)(2,1)S(1)}, u32[]{:S(2)}, u32[]{:S(2)}) %collective-permute-start.2) | collective-permute-done | bytes 262176 | tf_op jit(solution)/shard_map/ppermute | solution.py:24
  35.0 1.5 collective-permute-start.7
  36.9 3.4 %copy-done = bf16[512,8192]{1,0:T(8,128)(2,1)S(1)} copy-done((bf16[512,8192]{1,0:T(8,128)(2,1)S(1)}, bf16[512,8192]{1,0:T(8,128)(2,1)}, u32[]{:S(2)}) %copy-start) | copy-done | bytes 8388632
  40.3 2.8 %shard_map.129 = bf16[2,4,512,256]{3,2,1,0:T(8,128)(2,1)S(1)} custom-call(s32[8]{0:T(128)S(1)} %stack.212.places_ref, bf16[512,512]{1,0:T(8,128)(2,1)S(1)} %copy.22.cot_ref, bf16[512,8192]{1,0:T(8,128)(2,1)S(1)} %copy-done, bf16[512,8192]{1,0:T(8,128)(2,1)S(1)} %copy-done), custom_call_target="tpu_custom_call" | custom-call | flops 1024 | bytes 1024 | tf_op jit(solution)/shard_map/pallas_call | solution.py:89
  44.7 3.4 %copy-done.1 = bf16[512,8192]{1,0:T(8,128)(2,1)S(1)} copy-done((bf16[512,8192]{1,0:T(8,128)(2,1)S(1)}, bf16[512,8192]{1,0:T(8,128)(2,1)}, u32[]{:S(2)}) %copy-start.1) | copy-done | bytes 8388632
  48.1 3.7 %shard_map.130 = bf16[2,4,512,256]{3,2,1,0:T(8,128)(2,1)} custom-call(s32[8]{0:T(128)S(1)} %stack.221.places_ref, bf16[512,512]{1,0:T(8,128)(2,1)S(1)} %copy.23.cot_ref, bf16[512,8192]{1,0:T(8,128)(2,1)S(1)} %copy-done.1, bf16[512,8192]{1,0:T(8,128)(2,1)S(1)} %copy-done.1), custom_call_target="tpu_custom_call" | custom-call | flops 1024 | bytes 1024 | tf_op jit(solution)/shard_map/pallas_call | solution.py:89
  52.4 1.5 collective-permute-start.10
  56.2 5.3 %collective-permute-done.10 = bf16[256,512]{1,0:T(8,128)(2,1)S(1)} collective-permute-done((bf16[256,512]{1,0:T(8,128)(2,1)S(1)}, bf16[256,512]{1,0:T(8,128)(2,1)S(1)}, u32[]{:S(2)}, u32[]{:S(2)}) %collective-permute-start.10) | collective-permute-done | bytes 262176 | tf_op jit(solution)/shard_map/ppermute | solution.py:24
  61.6 6.1 %collective-permute-done.12.rest_3_ = bf16[2,256,512]{2,1,0:T(8,128)(2,1)S(1)} collective-permute-done((bf16[2,256,512]{2,1,0:T(8,128)(2,1)S(1)}, bf16[2,256,512]{2,1,0:T(8,128)(2,1)S(1)}, u32[]{:S(2)}, u32[]{:S(2)}) %collective-permute-start.12) | collective-permute-done | bytes 524320 | tf_op jit(solution)/shard_map/ppermute | solution.py:24
  70.4 3.4 %copy-done.2 = bf16[512,8192]{1,0:T(8,128)(2,1)S(1)} copy-done((bf16[512,8192]{1,0:T(8,128)(2,1)S(1)}, bf16[512,8192]{1,0:T(8,128)(2,1)}, u32[]{:S(2)}) %copy-start.2) | copy-done | bytes 8388632
  73.8 1.6 %copy-done.10 = bf16[2,4,512,256]{3,2,1,0:T(8,128)(2,1)S(1)} copy-done((bf16[2,4,512,256]{3,2,1,0:T(8,128)(2,1)S(1)}, bf16[2,4,512,256]{3,2,1,0:T(8,128)(2,1)}, u32[]{:S(2)}) %copy-start.10) | copy-done | bytes 2097176
  75.4 5.6 %shard_map.131 = (bf16[2,512,256]{2,1,0:T(8,128)(2,1)}, bf16[2,512,256]{2,1,0:T(8,128)(2,1)S(1)}, bf16[2,512,256]{2,1,0:T(8,128)(2,1)}, bf16[2,512,256]{2,1,0:T(8,128)(2,1)S(1)}) custom-call(s32[8]{0:T(128)S(1)} %stack.233.places_ref, bf16[512,512]{1,0:T(8,128)(2,1)S(1)} %copy.22.cot_ref, bf16[512,8192]{1,0:T(8,128)(2,1)S(1)} %copy-done.2, ...), custom_call_target="tpu_custom_call" | custom-call | flops 1024 | bytes 1024 | tf_op jit(solution)/shard_map/pallas_call | solution.py:89
  85.7 1.6 collective-permute-start.13
  88.4 9.4 %collective-permute-done.24 = bf16[2,512,256]{2,1,0:T(8,128)(2,1)} collective-permute-done((bf16[2,512,256]{2,1,0:T(8,128)(2,1)}, bf16[2,512,256]{2,1,0:T(8,128)(2,1)}, u32[]{:S(2)}, u32[]{:S(2)}) %collective-permute-start.24) | collective-permute-done | bytes 524320 | tf_op jit(solution)/shard_map/ppermute | solution.py:24
  98.5 3.4 %copy-done.3 = bf16[512,8192]{1,0:T(8,128)(2,1)S(1)} copy-done((bf16[512,8192]{1,0:T(8,128)(2,1)S(1)}, bf16[512,8192]{1,0:T(8,128)(2,1)}, u32[]{:S(2)}) %copy-start.3) | copy-done | bytes 8388632
  101.9 5.7 %shard_map.134 = (bf16[2,512,256]{2,1,0:T(8,128)(2,1)S(1)}, bf16[2,512,256]{2,1,0:T(8,128)(2,1)S(1)}, bf16[2,512,256]{2,1,0:T(8,128)(2,1)S(1)}, bf16[2,512,256]{2,1,0:T(8,128)(2,1)S(1)}) custom-call(s32[8]{0:T(128)S(1)} %stack.251.places_ref, bf16[512,512]{1,0:T(8,128)(2,1)S(1)} %copy.22.cot_ref, bf16[512,8192]{1,0:T(8,128)(2,1)S(1)} %copy-done.3, ...), custom_call_target="tpu_custom_call" | custom-call | flops 1024 | bytes 1024 | tf_op jit(solution)/shard_map/pallas_call | solution.py:89
  110.8 1.6 collective-permute-start.27
  112.4 1.5 collective-permute-start.26
  114.2 3.4 %copy-done.4 = bf16[512,8192]{1,0:T(8,128)(2,1)S(1)} copy-done((bf16[512,8192]{1,0:T(8,128)(2,1)S(1)}, bf16[512,8192]{1,0:T(8,128)(2,1)}, u32[]{:S(2)}) %copy-start.4) | copy-done | bytes 8388632
  117.6 5.6 %shard_map.132.first_ref = f32[512,512]{1,0:T(8,128)S(1)} custom-call(s32[4]{0:T(128)S(1)} %get-tuple-element.129.places_ref, s32[4]{0:T(128)S(1)} %get-tuple-element.128.offsets_ref, bf16[512,8192]{1,0:T(8,128)(2,1)S(1)} %copy-done.4, bf16[2,256,512]{2,1,0:T(8,128)(2,1)S(1)} %pad_maximum_fusion.rest_0_, ...), custom_call_target="tpu_custom_call" | custom-call | flops 1024 | bytes 1024 | tf_op jit(solution)/shard_map/pallas_call | solution.py:199
  123.2 7.2 %shard_map.133 = (bf16[512,512]{1,0:T(8,128)(2,1)}, f32[512,1]{1,0:T(8,128)S(1)}) custom-call(s32[4]{0:T(128)S(1)} %pad_add_fusion.places_ref, s32[4]{0:T(128)S(1)} %get-tuple-element.128.offsets_ref, bf16[512,8192]{1,0:T(8,128)(2,1)S(1)} %copy-done.4, f32[512,512]{1,0:T(8,128)S(1)} %shard_map.132.first_ref, ...), custom_call_target="tpu_custom_call" | custom-call | flops 1024 | bytes 1024 | tf_op jit(solution)/shard_map/pallas_call | solution.py:199
  132.8 3.0 %collective-permute-start.32 = (bf16[512,256]{1,0:T(8,128)(2,1)S(1)}, bf16[512,256]{1,0:T(8,128)(2,1)S(1)}, u32[]{:S(2)}, u32[]{:S(2)}) collective-permute-start(bf16[512,256]{1,0:T(8,128)(2,1)S(1)} %fusion.3), channel_id=1, source_target_pairs={{0,2},{1,3},{2,0},{3,1},{4,6},{5,7},{6,4},{7,5},{8,10},{9,11},{10,... | collective-permute-start | bytes 786440 | tf_op jit(solution)/shard_map/ppermute | solution.py:24
  137.0 6.7 %shard_map.135.rest_8_ = bf16[512,8192]{1,0:T(8,128)(2,1)} custom-call(s32[4]{0:T(128)S(1)} %get-tuple-element.129.places_ref, s32[4]{0:T(128)S(1)} %get-tuple-element.128.offsets_ref, bf16[512,8192]{1,0:T(8,128)(2,1)S(1)} %copy-done.4, bf16[512,512]{1,0:T(8,128)(2,1)S(1)} %multiply_convert_fusion.cot_ref, f32[512,1]{1,0:T(8,128)S(1)} %get-tuple-element.105.coef_ref, ...), custom_call_target="tpu_custom_call" | custom-call | flops 1024 | bytes 1024 | tf_op jit(solution)/shard_map/pallas_call | solution.py:199
  143.8 2.1 %collective-permute-start.34 = (bf16[512,256]{1,0:T(8,128)(2,1)S(1)}, bf16[512,256]{1,0:T(8,128)(2,1)S(1)}, u32[]{:S(2)}, u32[]{:S(2)}) collective-permute-start(bf16[512,256]{1,0:T(8,128)(2,1)S(1)} %fusion.1), channel_id=1, source_target_pairs={{0,1},{1,2},{2,3},{3,0},{4,5},{5,6},{6,7},{7,4},{8,9},{9,10},{10,1... | collective-permute-start | bytes 786440 | tf_op jit(solution)/shard_map/ppermute | solution.py:24
  145.9 7.2 %shard_map.136 = bf16[512,8192]{1,0:T(8,128)(2,1)} custom-call(s32[4]{0:T(128)S(1)} %pad_add_fusion.places_ref, s32[4]{0:T(128)S(1)} %get-tuple-element.128.offsets_ref, bf16[512,8192]{1,0:T(8,128)(2,1)S(1)} %copy-done.4, bf16[512,512]{1,0:T(8,128)(2,1)S(1)} %multiply_convert_fusion.cot_ref, ...), custom_call_target="tpu_custom_call", output_to_operand_aliasing={{}: (13, {})} | custom-call | flops 1024 | bytes 1024 | tf_op jit(solution)/shard_map/pallas_call | solution.py:199
  153.1 2.4 %collective-permute-done.33 = bf16[512,256]{1,0:T(8,128)(2,1)S(1)} collective-permute-done((bf16[512,256]{1,0:T(8,128)(2,1)S(1)}, bf16[512,256]{1,0:T(8,128)(2,1)S(1)}, u32[]{:S(2)}, u32[]{:S(2)}) %collective-permute-start.33) | collective-permute-done | bytes 262176 | tf_op jit(solution)/shard_map/ppermute | solution.py:24
  (145 shorter events, 31.5 us)
Async XLA Ops:
  7.7 10.4 %collective-permute-start.4 = (f32[52,128]{1,0:T(8,128)S(1)}, f32[52,128]{1,0:T(8,128)S(1)}, u32[]{:S(2)}, u32[]{:S(2)}) collective-permute-start(f32[52,128]{1,0:T(8,128)S(1)} %maximum_bitcast_fusion), channel_id=1, source_target_pairs={{0,1},{1,2},{2,3},{3,0},{4,5},{5,6},{6,7},{7,4},{8,9},{9,10},{10,1... | collective-permute-start | bytes 79880 | tf_op jit(solution)/shard_map/ppermute | solution.py:24
  10.7 10.6 %collective-permute-start.5 = (f32[52,128]{1,0:T(8,128)S(1)}, f32[52,128]{1,0:T(8,128)S(1)}, u32[]{:S(2)}, u32[]{:S(2)}) collective-permute-start(f32[52,128]{1,0:T(8,128)S(1)} %maximum_bitcast_fusion), channel_id=1, source_target_pairs={{0,2},{1,3},{2,0},{3,1},{4,6},{5,7},{6,4},{7,5},{8,10},{9,11},{10,... | collective-permute-start | bytes 79880 | tf_op jit(solution)/shard_map/ppermute | solution.py:24
  14.7 11.1 %collective-permute-start = (bf16[256,512]{1,0:T(8,128)(2,1)S(1)}, bf16[256,512]{1,0:T(8,128)(2,1)S(1)}, u32[]{:S(2)}, u32[]{:S(2)}) collective-permute-start(bf16[256,512]{1,0:T(8,128)(2,1)S(1)} %multiply_convert_fusion.1), channel_id=1, source_target_pairs={{0,1},{1,2},{2,3},{3,0},{4,5},{5,6},{6,7},{7,4},{8,9},{9,10},{10,1... | collective-permute-start | bytes 786440 | tf_op jit(solution)/shard_map/ppermute | solution.py:24
  15.4 10.4 %collective-permute-start.1 = (bf16[256,512]{1,0:T(8,128)(2,1)S(1)}, bf16[256,512]{1,0:T(8,128)(2,1)S(1)}, u32[]{:S(2)}, u32[]{:S(2)}) collective-permute-start(bf16[256,512]{1,0:T(8,128)(2,1)S(1)} %multiply_convert_fusion.1), channel_id=1, source_target_pairs={{0,8},{8,0},{1,9},{9,1},{2,10},{10,2},{3,11},{11,3},{4,12},{12,4},... | collective-permute-start | bytes 786440 | tf_op jit(solution)/shard_map/ppermute | solution.py:24
  18.1 11.3 %collective-permute-start.3 = (bf16[256,512]{1,0:T(8,128)(2,1)S(1)}, bf16[256,512]{1,0:T(8,128)(2,1)}, u32[]{:S(2)}, u32[]{:S(2)}) collective-permute-start(bf16[256,512]{1,0:T(8,128)(2,1)S(1)} %multiply_convert_fusion.1), channel_id=1, source_target_pairs={{0,3},{1,0},{2,1},{3,2},{4,7},{5,4},{6,5},{7,6},{8,11},{9,8},{10,9... | collective-permute-start | bytes 786440 | tf_op jit(solution)/shard_map/ppermute | solution.py:24
  27.4 24.5 %collective-permute-start.9 = (bf16[2,256,512]{2,1,0:T(8,128)(2,1)S(1)}, bf16[2,256,512]{2,1,0:T(8,128)(2,1)}, u32[]{:S(2)}, u32[]{:S(2)}) collective-permute-start(bf16[2,256,512]{2,1,0:T(8,128)(2,1)S(1)} %pad_maximum_fusion.rest_0_), channel_id=1, source_target_pairs={{0,16},{16,0},{1,17},{17,1},{2,18},{18,2},{3,19},{19,3},{4,20},{20... | collective-permute-start | bytes 1572872 | tf_op jit(solution)/shard_map/ppermute | solution.py:24
  35.0 16.8 %collective-permute-start.8 = (bf16[256,512]{1,0:T(8,128)(2,1)S(1)}, bf16[256,512]{1,0:T(8,128)(2,1)S(1)}, u32[]{:S(2)}, u32[]{:S(2)}) collective-permute-start(bf16[256,512]{1,0:T(8,128)(2,1)S(1)} %multiply_convert_fusion.1), channel_id=1, source_target_pairs={{0,2},{1,3},{2,0},{3,1},{4,6},{5,7},{6,4},{7,5},{8,10},{9,11},{10,... | collective-permute-start | bytes 786440 | tf_op jit(solution)/shard_map/ppermute | solution.py:24
  35.0 16.8 %collective-permute-start.7 = (bf16[256,512]{1,0:T(8,128)(2,1)}, bf16[256,512]{1,0:T(8,128)(2,1)S(1)}, u32[]{:S(2)}, u32[]{:S(2)}) collective-permute-start(bf16[256,512]{1,0:T(8,128)(2,1)} %collective-permute-done.3), channel_id=1, source_target_pairs={{0,8},{8,0},{1,9},{9,1},{2,10},{10,2},{3,11},{11,3},{4,12},{12,4},... | collective-permute-start | bytes 786440 | tf_op jit(solution)/shard_map/ppermute | solution.py:24
  51.8 16.6 %collective-permute-start.11 = (bf16[2,4,512,256]{3,2,1,0:T(8,128)(2,1)S(1)}, bf16[2,4,512,256]{3,2,1,0:T(8,128)(2,1)S(1)}, u32[]{:S(2)}, u32[]{:S(2)}) collective-permute-start(bf16[2,4,512,256]{3,2,1,0:T(8,128)(2,1)S(1)} %copy-done.12), channel_id=1, source_target_pairs={{0,4},{4,0},{1,5},{5,1},{2,6},{6,2},{3,7},{7,3},{8,12},{12,8},{9,1... | collective-permute-start | bytes 6291464 | tf_op jit(solution)/shard_map/ppermute | solution.py:24
  51.9 35.4 %collective-permute-start.23 = (bf16[2,4,512,256]{3,2,1,0:T(8,128)(2,1)}, bf16[2,4,512,256]{3,2,1,0:T(8,128)(2,1)}, u32[]{:S(2)}, u32[]{:S(2)}) collective-permute-start(bf16[2,4,512,256]{3,2,1,0:T(8,128)(2,1)} %shard_map.130), channel_id=1, source_target_pairs={{0,4},{4,0},{1,5},{5,1},{2,6},{6,2},{3,7},{7,3},{8,12},{12,8},{9,1... | collective-permute-start | bytes 6291464 | tf_op jit(solution)/shard_map/ppermute | solution.py:24
  54.0 13.7 %collective-permute-start.12 = (bf16[2,256,512]{2,1,0:T(8,128)(2,1)S(1)}, bf16[2,256,512]{2,1,0:T(8,128)(2,1)S(1)}, u32[]{:S(2)}, u32[]{:S(2)}) collective-permute-start(bf16[2,256,512]{2,1,0:T(8,128)(2,1)S(1)} %pad_maximum_fusion.1.rest_2_), channel_id=1, source_target_pairs={{0,8},{8,0},{1,9},{9,1},{2,10},{10,2},{3,11},{11,3},{4,12},{12,4},... | collective-permute-start | bytes 1572872 | tf_op jit(solution)/shard_map/ppermute | solution.py:24
  55.7 27.0 %collective-permute-start.14 = (bf16[2,256,512]{2,1,0:T(8,128)(2,1)S(1)}, bf16[2,256,512]{2,1,0:T(8,128)(2,1)S(1)}, u32[]{:S(2)}, u32[]{:S(2)}) collective-permute-start(bf16[2,256,512]{2,1,0:T(8,128)(2,1)S(1)} %pad_maximum_fusion.3.rest_4_), channel_id=1, source_target_pairs={{0,16},{16,0},{1,17},{17,1},{2,18},{18,2},{3,19},{19,3},{4,20},{20... | collective-permute-start | bytes 1572872 | tf_op jit(solution)/shard_map/ppermute | solution.py:24
  61.6 21.6 %collective-permute-start.19 = (bf16[2,256,512]{2,1,0:T(8,128)(2,1)S(1)}, bf16[2,256,512]{2,1,0:T(8,128)(2,1)S(1)}, u32[]{:S(2)}, u32[]{:S(2)}) collective-permute-start(bf16[2,256,512]{2,1,0:T(8,128)(2,1)S(1)} %pad_maximum_fusion.3.rest_4_), channel_id=1, source_target_pairs={{0,4},{4,0},{1,5},{5,1},{2,6},{6,2},{3,7},{7,3},{8,12},{12,8},{9,1... | collective-permute-start | bytes 1572872 | tf_op jit(solution)/shard_map/ppermute | solution.py:24
  68.5 17.1 %collective-permute-start.15 = (bf16[2,256,512]{2,1,0:T(8,128)(2,1)S(1)}, bf16[2,256,512]{2,1,0:T(8,128)(2,1)}, u32[]{:S(2)}, u32[]{:S(2)}) collective-permute-start(bf16[2,256,512]{2,1,0:T(8,128)(2,1)S(1)} %pad_maximum_fusion.rest_0_), channel_id=1, source_target_pairs={{0,4},{4,0},{1,5},{5,1},{2,6},{6,2},{3,7},{7,3},{8,12},{12,8},{9,1... | collective-permute-start | bytes 1572872 | tf_op jit(solution)/shard_map/ppermute | solution.py:24
  69.9 15.8 %collective-permute-start.16 = (bf16[2,256,512]{2,1,0:T(8,128)(2,1)}, bf16[2,256,512]{2,1,0:T(8,128)(2,1)}, u32[]{:S(2)}, u32[]{:S(2)}) collective-permute-start(bf16[2,256,512]{2,1,0:T(8,128)(2,1)} %collective-permute-done.9.rest_1_), channel_id=1, source_target_pairs={{0,4},{4,0},{1,5},{5,1},{2,6},{6,2},{3,7},{7,3},{8,12},{12,8},{9,1... | collective-permute-start | bytes 1572872 | tf_op jit(solution)/shard_map/ppermute | solution.py:24
  82.7 15.1 %collective-permute-start.24 = (bf16[2,512,256]{2,1,0:T(8,128)(2,1)}, bf16[2,512,256]{2,1,0:T(8,128)(2,1)}, u32[]{:S(2)}, u32[]{:S(2)}) collective-permute-start(bf16[2,512,256]{2,1,0:T(8,128)(2,1)} %get-tuple-element.72), channel_id=1, source_target_pairs={{0,8},{8,0},{1,9},{9,1},{2,10},{10,2},{3,11},{11,3},{4,12},{12,4},... | collective-permute-start | bytes 1572872 | tf_op jit(solution)/shard_map/ppermute | solution.py:24
  83.2 14.6 %collective-permute-start.25 = (bf16[2,512,256]{2,1,0:T(8,128)(2,1)}, bf16[2,512,256]{2,1,0:T(8,128)(2,1)}, u32[]{:S(2)}, u32[]{:S(2)}) collective-permute-start(bf16[2,512,256]{2,1,0:T(8,128)(2,1)} %get-tuple-element.74), channel_id=1, source_target_pairs={{0,16},{16,0},{1,17},{17,1},{2,18},{18,2},{3,19},{19,3},{4,20},{20... | collective-permute-start | bytes 1572872 | tf_op jit(solution)/shard_map/ppermute | solution.py:24
  85.6 23.1 %collective-permute-start.20 = (bf16[2,256,512]{2,1,0:T(8,128)(2,1)}, bf16[2,256,512]{2,1,0:T(8,128)(2,1)}, u32[]{:S(2)}, u32[]{:S(2)}) collective-permute-start(bf16[2,256,512]{2,1,0:T(8,128)(2,1)} %copy-done.7), channel_id=1, source_target_pairs={{0,4},{4,0},{1,5},{5,1},{2,6},{6,2},{3,7},{7,3},{8,12},{12,8},{9,1... | collective-permute-start | bytes 1572872 | tf_op jit(solution)/shard_map/ppermute | solution.py:24
  85.7 23.6 %collective-permute-start.13 = (bf16[2,256,512]{2,1,0:T(8,128)(2,1)S(1)}, bf16[2,256,512]{2,1,0:T(8,128)(2,1)}, u32[]{:S(2)}, u32[]{:S(2)}) collective-permute-start(bf16[2,256,512]{2,1,0:T(8,128)(2,1)S(1)} %pad_maximum_fusion.2.rest_6_), channel_id=1, source_target_pairs={{0,8},{8,0},{1,9},{9,1},{2,10},{10,2},{3,11},{11,3},{4,12},{12,4},... | collective-permute-start | bytes 1572872 | tf_op jit(solution)/shard_map/ppermute | solution.py:24
  87.3 22.5 %collective-permute-start.21 = (bf16[2,256,512]{2,1,0:T(8,128)(2,1)S(1)}, bf16[2,256,512]{2,1,0:T(8,128)(2,1)}, u32[]{:S(2)}, u32[]{:S(2)}) collective-permute-start(bf16[2,256,512]{2,1,0:T(8,128)(2,1)S(1)} %pad_maximum_fusion.2.rest_6_), channel_id=1, source_target_pairs={{0,4},{4,0},{1,5},{5,1},{2,6},{6,2},{3,7},{7,3},{8,12},{12,8},{9,1... | collective-permute-start | bytes 1572872 | tf_op jit(solution)/shard_map/ppermute | solution.py:24
  97.8 13.0 %collective-permute-start.17 = (bf16[2,256,512]{2,1,0:T(8,128)(2,1)S(1)}, bf16[2,256,512]{2,1,0:T(8,128)(2,1)}, u32[]{:S(2)}, u32[]{:S(2)}) collective-permute-start(bf16[2,256,512]{2,1,0:T(8,128)(2,1)S(1)} %pad_maximum_fusion.1.rest_2_), channel_id=1, source_target_pairs={{0,4},{4,0},{1,5},{5,1},{2,6},{6,2},{3,7},{7,3},{8,12},{12,8},{9,1... | collective-permute-start | bytes 1572872 | tf_op jit(solution)/shard_map/ppermute | solution.py:24
  97.8 14.6 %collective-permute-start.18 = (bf16[2,256,512]{2,1,0:T(8,128)(2,1)}, bf16[2,256,512]{2,1,0:T(8,128)(2,1)}, u32[]{:S(2)}, u32[]{:S(2)}) collective-permute-start(bf16[2,256,512]{2,1,0:T(8,128)(2,1)} %copy-done.5), channel_id=1, source_target_pairs={{0,4},{4,0},{1,5},{5,1},{2,6},{6,2},{3,7},{7,3},{8,12},{12,8},{9,1... | collective-permute-start | bytes 1572872 | tf_op jit(solution)/shard_map/ppermute | solution.py:24
  108.7 21.7 %collective-permute-start.28 = (bf16[2,512,256]{2,1,0:T(8,128)(2,1)S(1)}, bf16[2,512,256]{2,1,0:T(8,128)(2,1)S(1)}, u32[]{:S(2)}, u32[]{:S(2)}) collective-permute-start(bf16[2,512,256]{2,1,0:T(8,128)(2,1)S(1)} %get-tuple-element.98), channel_id=1, source_target_pairs={{0,8},{8,0},{1,9},{9,1},{2,10},{10,2},{3,11},{11,3},{4,12},{12,4},... | collective-permute-start | bytes 1572872 | tf_op jit(solution)/shard_map/ppermute | solution.py:24
  109.3 21.1 %collective-permute-start.29 = (bf16[2,512,256]{2,1,0:T(8,128)(2,1)S(1)}, bf16[2,512,256]{2,1,0:T(8,128)(2,1)S(1)}, u32[]{:S(2)}, u32[]{:S(2)}) collective-permute-start(bf16[2,512,256]{2,1,0:T(8,128)(2,1)S(1)} %get-tuple-element.99), channel_id=1, source_target_pairs={{0,16},{16,0},{1,17},{17,1},{2,18},{18,2},{3,19},{19,3},{4,20},{20... | collective-permute-start | bytes 1572872 | tf_op jit(solution)/shard_map/ppermute | solution.py:24
  109.8 13.4 %collective-permute-start.22 = (bf16[2,256,512]{2,1,0:T(8,128)(2,1)}, bf16[2,256,512]{2,1,0:T(8,128)(2,1)S(1)}, u32[]{:S(2)}, u32[]{:S(2)}) collective-permute-start(bf16[2,256,512]{2,1,0:T(8,128)(2,1)} %collective-permute-done.13.rest_7_), channel_id=1, source_target_pairs={{0,4},{4,0},{1,5},{5,1},{2,6},{6,2},{3,7},{7,3},{8,12},{12,8},{9,1... | collective-permute-start | bytes 1572872 | tf_op jit(solution)/shard_map/ppermute | solution.py:24
  110.8 19.5 %collective-permute-start.27 = (bf16[512,256]{1,0:T(8,128)(2,1)S(1)}, bf16[512,256]{1,0:T(8,128)(2,1)S(1)}, u32[]{:S(2)}, u32[]{:S(2)}) collective-permute-start(bf16[512,256]{1,0:T(8,128)(2,1)S(1)} %fusion.8), channel_id=1, source_target_pairs={{0,8},{8,0},{1,9},{9,1},{2,10},{10,2},{3,11},{11,3},{4,12},{12,4},... | collective-permute-start | bytes 786440 | tf_op jit(solution)/shard_map/ppermute | solution.py:24
  112.4 18.0 %collective-permute-start.26 = (bf16[512,256]{1,0:T(8,128)(2,1)S(1)}, bf16[512,256]{1,0:T(8,128)(2,1)S(1)}, u32[]{:S(2)}, u32[]{:S(2)}) collective-permute-start(bf16[512,256]{1,0:T(8,128)(2,1)S(1)} %fusion.7), channel_id=1, source_target_pairs={{0,16},{16,0},{1,17},{17,1},{2,18},{18,2},{3,19},{19,3},{4,20},{20... | collective-permute-start | bytes 786440 | tf_op jit(solution)/shard_map/ppermute | solution.py:24
  130.4 13.3 %collective-permute-start.31 = (bf16[512,256]{1,0:T(8,128)(2,1)S(1)}, bf16[512,256]{1,0:T(8,128)(2,1)S(1)}, u32[]{:S(2)}, u32[]{:S(2)}) collective-permute-start(bf16[512,256]{1,0:T(8,128)(2,1)S(1)} %fusion.10), channel_id=1, source_target_pairs={{0,8},{8,0},{1,9},{9,1},{2,10},{10,2},{3,11},{11,3},{4,12},{12,4},... | collective-permute-start | bytes 786440 | tf_op jit(solution)/shard_map/ppermute | solution.py:24
  131.1 12.6 %collective-permute-start.30 = (bf16[512,256]{1,0:T(8,128)(2,1)S(1)}, bf16[512,256]{1,0:T(8,128)(2,1)S(1)}, u32[]{:S(2)}, u32[]{:S(2)}) collective-permute-start(bf16[512,256]{1,0:T(8,128)(2,1)S(1)} %fusion.9), channel_id=1, source_target_pairs={{0,16},{16,0},{1,17},{17,1},{2,18},{18,2},{3,19},{19,3},{4,20},{20... | collective-permute-start | bytes 786440 | tf_op jit(solution)/shard_map/ppermute | solution.py:24
  132.8 20.3 %collective-permute-start.32 = (bf16[512,256]{1,0:T(8,128)(2,1)S(1)}, bf16[512,256]{1,0:T(8,128)(2,1)S(1)}, u32[]{:S(2)}, u32[]{:S(2)}) collective-permute-start(bf16[512,256]{1,0:T(8,128)(2,1)S(1)} %fusion.3), channel_id=1, source_target_pairs={{0,2},{1,3},{2,0},{3,1},{4,6},{5,7},{6,4},{7,5},{8,10},{9,11},{10,... | collective-permute-start | bytes 786440 | tf_op jit(solution)/shard_map/ppermute | solution.py:24
  136.8 18.7 %collective-permute-start.33 = (bf16[512,256]{1,0:T(8,128)(2,1)S(1)}, bf16[512,256]{1,0:T(8,128)(2,1)S(1)}, u32[]{:S(2)}, u32[]{:S(2)}) collective-permute-start(bf16[512,256]{1,0:T(8,128)(2,1)S(1)} %fusion.2), channel_id=1, source_target_pairs={{0,3},{1,0},{2,1},{3,2},{4,7},{5,4},{6,5},{7,6},{8,11},{9,8},{10,9... | collective-permute-start | bytes 786440 | tf_op jit(solution)/shard_map/ppermute | solution.py:24
  143.8 11.6 %collective-permute-start.34 = (bf16[512,256]{1,0:T(8,128)(2,1)S(1)}, bf16[512,256]{1,0:T(8,128)(2,1)S(1)}, u32[]{:S(2)}, u32[]{:S(2)}) collective-permute-start(bf16[512,256]{1,0:T(8,128)(2,1)S(1)} %fusion.1), channel_id=1, source_target_pairs={{0,1},{1,2},{2,3},{3,0},{4,5},{5,6},{6,7},{7,4},{8,9},{9,10},{10,1... | collective-permute-start | bytes 786440 | tf_op jit(solution)/shard_map/ppermute | solution.py:24
  (34 other events, 225.6 us)

commit v5 on v4

v5 whole, which is shorter than its diff:
```python
import functools

import jax
import jax.numpy as jnp
from jax import lax
from jax.experimental import pallas as pl
from jax.experimental.pallas import tpu as pltpu
from jax.sharding import PartitionSpec as P

VOCAB = 128256
EPS = 1e-05
BETA = 0.5
CORES = 2
OUTER = 2
PAIR_VMEM = 14 * 1024 * 1024
WEIGHT_VMEM = 22 * 1024 * 1024
NOMINAL = pl.CostEstimate(flops=1024, bytes_accessed=1024, transcendentals=0)
BF16 = jnp.bfloat16
F32 = jnp.float32


def swap(value, axis, step):
    size = lax.axis_size(axis)
    return lax.ppermute(value, axis, [(place, (place + step) % size) for place in range(size)])


def trade(value, axis, mask):
    size = lax.axis_size(axis)
    return lax.ppermute(value, axis, [(place, place ^ mask) for place in range(size)])


def after(value, *earlier):
    return lax.optimization_barrier((value, earlier))[0]


def widen(parts):
    return functools.reduce(jnp.add, [part.astype(F32) for part in parts])


def inner_first(chunk):
    return chunk % 2 == 0


def fetch(resid_hbm, places_ref, blocks_ref, sems, count):
    width = blocks_ref.shape[2]

    def copy(n):
        where = pl.ds(pl.multiple_of(places_ref[n] * width, width), width)
        return pltpu.make_async_copy(resid_hbm.at[:, where], blocks_ref.at[n], sems.at[n])

    @pl.when(pl.program_id(0) == 0)
    def _():
        for n in range(count):
            copy(n).start()

    return copy


def theirs_kernel(places_ref, cot_ref, resid_hbm, out_ref, blocks_ref, sems):
    step = pl.program_id(0)
    steps = blocks_ref.shape[0] // 2
    copy = fetch(resid_hbm, places_ref, blocks_ref, sems, 2 * steps)
    for slot in range(2):
        copy(2 * step + slot).wait()
        product = jnp.dot(cot_ref[...], blocks_ref[2 * step + slot], preferred_element_type=F32)
        out_ref[slot, 0] = product.astype(BF16)


def ours_kernel(places_ref, cot_ref, resid_hbm, other_ref, *rest):
    outs, (blocks_ref, sems) = rest[:4], rest[4:]
    step = pl.program_id(0)
    at_outer, at_inner = step // 2, lax.rem(step, 2)
    steps = blocks_ref.shape[0] // 2
    copy = fetch(resid_hbm, places_ref, blocks_ref, sems, 2 * steps)
    for slot in range(2):
        copy(2 * step + slot).wait()
        send_ref, keep_ref = outs[2 * slot : 2 * slot + 2]
        product = jnp.dot(cot_ref[...], blocks_ref[2 * step + slot], preferred_element_type=F32)
        total = (product + other_ref[slot, 0].astype(F32)).astype(BF16)
        way, place = (at_inner, at_outer) if slot == 0 else (at_outer, at_inner)

        @pl.when(way == 1)
        def _():
            send_ref[place] = total

        @pl.when(way == 0)
        def _():
            keep_ref[place] = total


def pair_product(residual, cot_t, places, rows, other):
    features, tokens = cot_t.shape
    steps = places.shape[0] // 2
    in_specs = [
        pl.BlockSpec((features, tokens), lambda i, p: (0, 0)),
        pl.BlockSpec(memory_space=pltpu.HBM),
    ]
    operands = [cot_t, residual]
    block = pl.BlockSpec((2, 1, features, rows), lambda i, p: (0, i, 0, 0))
    if other is None:
        kernel, out_specs = theirs_kernel, block
        out_shape = jax.ShapeDtypeStruct((2, steps, features, rows), BF16)
    else:
        kernel = ours_kernel
        in_specs.append(block)
        operands.append(other)
        out_specs = [pl.BlockSpec((2, features, rows), lambda i, p: (0, 0, 0))] * 4
        out_shape = [jax.ShapeDtypeStruct((2, features, rows), BF16)] * 4
    return pl.pallas_call(
        kernel,
        out_shape=out_shape,
        grid_spec=pltpu.PrefetchScalarGridSpec(
            num_scalar_prefetch=1,
            grid=(steps,),
            in_specs=in_specs,
            out_specs=out_specs,
            scratch_shapes=[
                pltpu.VMEM((2 * steps, tokens, rows), BF16),
                pltpu.SemaphoreType.DMA((2 * steps,)),
            ],
        ),
        cost_estimate=NOMINAL,
        compiler_params=pltpu.CompilerParams(vmem_limit_bytes=PAIR_VMEM),
    )(places, *operands)


def place_weight(inner_flags, offsets_ref, pieces, weight_ref):
    step = pl.program_id(0)
    at_outer, at_inner = step // 2, lax.rem(step, 2)
    rows = pieces[0].shape[1]
    for chunk, flag in enumerate(inner_flags):
        way = at_outer if flag else at_inner
        where = pl.ds(pl.multiple_of(offsets_ref[chunk], rows), rows)
        for late in range(2):
            piece = pieces[chunk * 2 + late]

            @pl.when(way == late)
            def _():
                weight_ref[0, where, :] = piece[0]


def piece_specs(inner_flags, rows, features):
    specs = []
    for flag in inner_flags:
        for late in range(2):
            if flag:
                index = lambda i, *_, first=2 * late: (jnp.clip(i - first, 0, 1), 0, 0)
            else:
                index = lambda i, *_: (i // 2, 0, 0)
            specs.append(pl.BlockSpec((1, rows, features), index))
    return specs


def value_kernel(inner_flags, places_ref, offsets_ref, resid_hbm, *rest):
    pieces, (total_ref, weight_ref, blocks_ref, sems) = rest[:-4], rest[-4:]
    step = pl.program_id(0)
    copy = fetch(resid_hbm, places_ref, blocks_ref, sems, blocks_ref.shape[0])
    place_weight(inner_flags, offsets_ref, pieces, weight_ref)
    copy(step).wait()
    product = jnp.dot(blocks_ref[step], weight_ref[0], preferred_element_type=F32)

    @pl.when(step == 0)
    def _():
        total_ref[...] = product

    @pl.when(step > 0)
    def _():
        total_ref[...] += product


def value_end_kernel(
    width, places_ref, resid_hbm, weight_ref, first_ref, cot_ref, inv_ref,
    value_ref, coef_ref, blocks_ref, sems, total_ref,
):
    step = pl.program_id(0)
    copy = fetch(resid_hbm, places_ref, blocks_ref, sems, blocks_ref.shape[0])
    copy(step).wait()
    product = jnp.dot(blocks_ref[step], weight_ref[0], preferred_element_type=F32)

    @pl.when(step == 0)
    def _():
        total_ref[...] = first_ref[...] + product

    @pl.when(step > 0)
    def _():
        total_ref[...] += product

    @pl.when(step == pl.num_programs(0) - 1)
    def _():
        total = total_ref[...]
        inv = inv_ref[...]
        value_ref[...] = (total * inv).astype(BF16)
        share = jnp.sum(total * cot_ref[...].astype(F32), axis=1, keepdims=True)
        coef_ref[...] = share * (inv * inv) * (1.0 / width)


def grad_kernel(places_ref, resid_hbm, weight_ref, cot_ref, coef_ref, *rest):
    out_ref, blocks_ref, sems = rest[-3:]
    step = pl.program_id(0)
    copy = fetch(resid_hbm, places_ref, blocks_ref, sems, blocks_ref.shape[0])
    grad = lax.dot_general(
        cot_ref[...], weight_ref[0], (((1,), (1,)), ((), ())), preferred_element_type=F32
    )
    copy(step).wait()
    out_ref[...] = (grad - blocks_ref[step].astype(F32) * coef_ref[...]).astype(BF16)


def whole_block(array):
    return pl.BlockSpec(array.shape, lambda i, *_: (0, 0))


def weight_scratch(tokens, depth, steps):
    return [pltpu.VMEM((steps, tokens, depth), BF16), pltpu.SemaphoreType.DMA((steps,))]


def first_value(inner_flags, places, offsets, residual, pieces):
    tokens, width = residual.shape
    rows, features = pieces[0].shape[1:]
    steps = places.shape[0]
    depth = width // (CORES * steps)
    total = jax.ShapeDtypeStruct((tokens, features), F32)
    return pl.pallas_call(
        functools.partial(value_kernel, inner_flags),
        out_shape=[total, jax.ShapeDtypeStruct((steps, depth, features), BF16)],
        grid_spec=pltpu.PrefetchScalarGridSpec(
            num_scalar_prefetch=2,
            grid=(steps,),
            in_specs=[pl.BlockSpec(memory_space=pltpu.HBM)] + piece_specs(inner_flags, rows, features),
            out_specs=[
                whole_block(total),
                pl.BlockSpec((1, depth, features), lambda i, p, o: (p[i] // CORES, 0, 0)),
            ],
            scratch_shapes=weight_scratch(tokens, depth, steps),
        ),
        cost_estimate=NOMINAL,
        compiler_params=pltpu.CompilerParams(vmem_limit_bytes=WEIGHT_VMEM),
    )(places, offsets, residual, *pieces)


def weight_call(kernel, places, residual, weight, wholes, out_shape, earlier=None):
    tokens, width = residual.shape
    steps, depth, features = weight.shape
    scratch = weight_scratch(tokens, depth, steps)
    if isinstance(out_shape, list):
        out_specs = [whole_block(array) for array in out_shape]
        scratch.append(pltpu.VMEM((tokens, features), F32))
    else:
        out_specs = pl.BlockSpec((tokens, depth), lambda i, p: (0, p[i]))
    in_specs = [
        pl.BlockSpec(memory_space=pltpu.HBM),
        pl.BlockSpec((1, depth, features), lambda i, p: (p[i] // CORES, 0, 0)),
    ] + [whole_block(array) for array in wholes]
    operands = [places, residual, weight, *wholes]
    aliases = {}
    if earlier is not None:
        aliases = {len(operands): 0}
        in_specs.append(pl.BlockSpec(memory_space=pltpu.HBM))
        operands.append(earlier)
    return pl.pallas_call(
        kernel,
        out_shape=out_shape,
        grid_spec=pltpu.PrefetchScalarGridSpec(
            num_scalar_prefetch=1,
            grid=(steps,),
            in_specs=in_specs,
            out_specs=out_specs,
            scratch_shapes=scratch,
        ),
        input_output_aliases=aliases,
        cost_estimate=NOMINAL,
        compiler_params=pltpu.CompilerParams(vmem_limit_bytes=WEIGHT_VMEM),
    )(*operands)


def sequence_weight(shares, rows_here, seq_length, rep_count, tp_place):
    seq = (shares[0].shape[0] - rows_here) // 3
    top_max = functools.reduce(jnp.maximum, [share[:seq] for share in shares])
    sum_exp = sum(share[seq : 2 * seq] * jnp.exp(share[:seq] - top_max) for share in shares)
    picked = sum(share[2 * seq : 3 * seq] for share in shares)
    ref_logp = picked - top_max - jnp.log(sum_exp)
    total = jnp.zeros((), F32)
    for mask, share in enumerate(shares):
        first = jnp.bitwise_xor(tp_place, mask) * rows_here
        live = first + jnp.arange(rows_here, dtype=jnp.int32) < seq_length
        diff = share[3 * seq :] - lax.dynamic_slice_in_dim(ref_logp, first, rows_here)
        total = total + jnp.sum(jnp.where(live, diff, 0.0))
    seq_delta = total / seq_length.astype(F32)
    return 2.0 * jax.nn.sigmoid(BETA * seq_delta) / rep_count


def per_device(
    residual,
    norm_gain,
    value_weight,
    value_cot,
    trainee_logp,
    ref_shard_max,
    ref_shard_sum,
    ref_target_logit,
    target_ids,
    lengths,
):
    rows_here, width = residual.shape
    features = value_cot.shape[1]
    tp_count = lax.axis_size("tp")
    outer, inner = lax.axis_size("outer"), lax.axis_size("inner")
    rep_count = outer * inner * CORES
    tp_place = lax.axis_index("tp")
    core = lax.axis_index("core")
    at_inner = lax.axis_index("inner")
    at_outer = lax.axis_index("outer")
    rep_place = (at_outer * inner + at_inner) * CORES + core
    depth = width // rep_count
    rows = depth // tp_count
    order = list(range(tp_count))
    in_place = rows % 128 == 0 and outer == 2 and inner == 2

    gained = (value_weight.astype(F32) * norm_gain.astype(F32)[:, None]).astype(BF16)
    residual, gained = lax.optimization_barrier((residual, gained))
    resid_wide = residual.astype(F32)
    squares = jnp.sum(resid_wide * resid_wide, axis=1, keepdims=True)

    def near_of(k, block):
        first = "inner" if inner_first(k) else "outer"
        return [swap(block, first, s) for s in range(1, lax.axis_size(first))]

    def far_of(k, block, nears):
        second = "outer" if inner_first(k) else "inner"
        near = jnp.stack([block] + nears)
        return [near] + [swap(near, second, s) for s in range(1, lax.axis_size(second))]

    own_pieces, arrived, near = {}, {0: gained}, {}
    arrived[1] = trade(gained, "tp", 1)
    near[0] = near_of(0, gained)
    arrived[1], near[0], squares, late_gained = lax.optimization_barrier(
        (arrived[1], near[0], squares, gained)
    )

    owned = jnp.where(
        target_ids // (VOCAB // tp_count) == tp_place,
        ref_target_logit[0],
        jnp.zeros_like(ref_target_logit[0]),
    )
    packed = jnp.concatenate([ref_shard_max[0], ref_shard_sum[0], owned, trainee_logp])
    packed = after(packed.reshape(1, -1, 128), squares)
    near[1] = near_of(1, arrived[1])
    arrived[2] = trade(late_gained, "tp", 2)
    packed = jnp.concatenate([packed, trade(packed, "tp", 1)])
    near[1], packed, near[0] = lax.optimization_barrier((near[1], packed, near[0]))
    own_pieces[0] = far_of(0, gained, near[0])
    own_pieces[1] = far_of(1, arrived[1], near[1])
    mask = 2
    while mask < tp_count:
        packed = jnp.concatenate([packed, trade(packed, "tp", mask)])
        mask *= 2
    seq_length = lax.dynamic_index_in_dim(lengths, rep_place, keepdims=False)
    seq_weight = sequence_weight(
        list(packed.reshape(tp_count, -1)), rows_here, seq_length, rep_count, tp_place
    )
    positions = tp_place * rows_here + jnp.arange(rows_here, dtype=jnp.int32)
    row_scale = (positions < seq_length).astype(F32) * seq_weight
    inv_rms = lax.rsqrt(squares * (1.0 / width) + EPS)
    cot = (inv_rms * row_scale[:, None] * value_cot.astype(F32)).astype(BF16)
    cot_t = cot.T

    def place_of(o, i, c, k):
        chip = lax.rem(at_outer + o, outer) * inner + lax.rem(at_inner + i, inner)
        return (chip * CORES + c) * tp_count + jnp.bitwise_xor(tp_place, k)

    chips = [(o, i) for o in range(outer) for i in range(inner)]
    if not in_place:
        product = jnp.dot(cot_t, residual, preferred_element_type=F32).astype(BF16)
        product = product.reshape(features, -1, rows).transpose(1, 0, 2)

    def places_of(pair, c):
        return jnp.stack([place_of(o, i, c, k) for o, i in chips for k in pair]).astype(jnp.int32)

    def for_other(pair, cot_t):
        places = places_of(pair, 1 - core)
        if in_place:
            return pair_product(residual, cot_t, places, rows, None)
        both = after(product, cot_t)[places].reshape(len(chips), 2, features, rows)
        return both.swapaxes(0, 1)

    def for_us(pair, other):
        places = places_of(pair, core)
        if in_place:
            send_a, keep_a, send_b, keep_b = pair_product(residual, cot_t, places, rows, other)
            return ([send_a], keep_a), ([send_b], keep_b)
        both = product[places].reshape(len(chips), 2, features, rows).swapaxes(0, 1)
        total = widen([both, other]).astype(BF16).reshape(2, outer, inner, features, rows)
        first = ([total[0, :, s] for s in range(1, inner)], total[0, :, 0])
        second = ([total[1, s] for s in range(1, outer)], total[1, 0])
        return first, second

    def first_round(sides):
        return [
            [swap(send, axis, s + 1) for s, send in enumerate(sends)]
            for axis, (sends, _) in zip(("inner", "outer"), sides)
        ]

    def second_round(sides, got):
        later = []
        for axis, (_, keep), parts in zip(("outer", "inner"), sides, got):
            later.append(
                [
                    swap(widen([part[s] for part in [keep] + parts]).astype(BF16), axis, s)
                    for s in range(1, lax.axis_size(axis))
                ]
            )
        return later

    def summed(sides, got, later):
        return [
            widen([part[0] for part in [keep] + parts] + last)
            for (_, keep), parts, last in zip(sides, got, later)
        ]

    backward = order[::-1]
    pairs = [backward[i : i + 2] for i in range(0, tp_count, 2)]
    arrived[2], cot_t = lax.optimization_barrier((arrived[2], cot_t))
    for k in order[3:]:
        arrived[k] = trade(after(gained, arrived[2]), "tp", k)
    near[2] = near_of(2, arrived[2])
    theirs = [for_other(pairs[0], cot_t)]
    theirs[0], own_pieces[0], own_pieces[1] = lax.optimization_barrier(
        (theirs[0], own_pieces[0], own_pieces[1])
    )
    others = [swap(theirs[0], "core", 1)]
    theirs.append(for_other(pairs[1], after(cot_t, theirs[0])))
    near[2], arrived[3], theirs[1] = lax.optimization_barrier((near[2], arrived[3], theirs[1]))
    others.append(swap(theirs[1], "core", 1))
    near[3] = near_of(3, arrived[3])
    own_pieces[2] = far_of(2, arrived[2], near[2])
    sides = [for_us(pairs[0], after(others[0], theirs[1]))]
    near[3], sides[0] = lax.optimization_barrier((near[3], sides[0]))
    own_pieces[3] = far_of(3, arrived[3], near[3])
    got = [first_round(sides[0])]
    sides.append(for_us(pairs[1], after(others[1], sides[0])))
    for n in range(2, len(pairs)):
        for k in order[2 * n : 2 * n + 2]:
            own_pieces[k] = far_of(k, arrived[k], near_of(k, arrived[k]))
        others.append(swap(for_other(pairs[n], after(cot_t, sides[-1])), "core", 1))
        sides.append(for_us(pairs[n], others[-1]))
    sides[1:], own_pieces = lax.optimization_barrier((sides[1:], own_pieces))

    if in_place:
        pieces = [piece for k in order for piece in own_pieces[k]]
        flags = tuple(inner_first(k) for k in order)
        places = [
            jnp.stack([place_of(o, i, c, 0) // tp_count for o, i in chips]).astype(jnp.int32)
            for c in (core, 1 - core)
        ]
        offsets = jnp.stack([jnp.bitwise_xor(tp_place, k) * rows for k in order]).astype(jnp.int32)
        total, own_weight = first_value(flags, places[0], offsets, residual, pieces)
    else:
        weight = []
        for k in order:
            both = jnp.stack(own_pieces[k])
            weight.append(both if inner_first(k) else jnp.swapaxes(both, 0, 1))
        weight = jnp.stack(weight)[jnp.bitwise_xor(tp_place, jnp.arange(tp_count))]
        weight = weight[:, (at_outer - jnp.arange(outer)) % outer]
        weight = weight[:, :, (at_inner - jnp.arange(inner)) % inner]
        own_weight = weight.transpose(1, 2, 0, 3, 4).reshape(outer * inner, depth, features)
        total = jnp.zeros((), F32)
    got[0], sides[1:], total, own_weight = lax.optimization_barrier(
        (got[0], sides[1:], total, own_weight)
    )
    other_weight = swap(own_weight, "core", 1)
    later = [second_round(sides[0], got[0])]
    got += [first_round(side) for side in sides[1:]]
    if in_place:
        value_proj, coefficient = weight_call(
            functools.partial(value_end_kernel, width),
            places[1],
            residual,
            other_weight,
            [total, cot, inv_rms],
            [
                jax.ShapeDtypeStruct((rows_here, features), BF16),
                jax.ShapeDtypeStruct((rows_here, 1), F32),
            ],
        )
    else:
        both = jnp.stack([own_weight, other_weight], axis=1)
        weight = jnp.where(core == 0, both, both[:, ::-1]).reshape(width, features)
        value_acc = jnp.dot(residual, weight, preferred_element_type=F32)
        value_proj = (inv_rms * value_acc).astype(BF16)
        share = jnp.sum(cot.astype(F32) * value_acc, axis=1, keepdims=True)
        coefficient = inv_rms * inv_rms * share * (1.0 / width)
    later[0], coefficient = lax.optimization_barrier((later[0], coefficient))
    sums = dict(zip(pairs[0], summed(sides[0], got[0], later[0])))
    last = [trade(sums[k].astype(BF16), "tp", k) for k in pairs[0]]
    got[1:], coefficient, sums = lax.optimization_barrier((got[1:], coefficient, sums))
    later += [second_round(side, parts) for side, parts in zip(sides[1:], got[1:])]
    if in_place:
        grad_shape = jax.ShapeDtypeStruct((rows_here, width), BF16)
        resid_grad = weight_call(
            grad_kernel, places[0], residual, own_weight, [cot, coefficient], grad_shape
        )
        later[1], coefficient, resid_grad = lax.optimization_barrier((later[1], coefficient, resid_grad))
    else:
        normed_grad = lax.dot_general(
            cot, weight, (((1,), (1,)), ((), ())), preferred_element_type=F32
        )
        resid_grad = (normed_grad - residual.astype(F32) * coefficient).astype(BF16)
    for pair, *rounds in zip(pairs[1:], sides[1:], got[1:], later[1:]):
        sums.update(zip(pair, summed(*rounds)))
    last += [trade(sums[k].astype(BF16), "tp", k) for k in backward[2:-1]]
    if in_place:
        resid_grad = weight_call(
            grad_kernel, places[1], residual, other_weight, [cot, coefficient], grad_shape, resid_grad
        )
    grad_rows = widen([sums[0]] + last)
    late_gain, late_weight, grad_rows = lax.optimization_barrier((norm_gain, value_weight, grad_rows))
    weight_grad = (late_gain.astype(F32)[None, :] * grad_rows).T
    gain_grad = jnp.sum(late_weight.astype(F32).T * grad_rows, axis=0)
    return (value_proj, resid_grad, weight_grad, gain_grad)


def solution(mesh):
    rep_count, tp_count = mesh.shape["rep"], mesh.shape["tp"]
    split = jax.sharding.Mesh(
        mesh.devices.reshape(OUTER, rep_count // (OUTER * CORES), CORES, tp_count),
        ("outer", "inner", "core", "tp"),
    )
    rep = ("outer", "inner", "core")
    rows = rep + ("tp",)
    return jax.shard_map(
        per_device,
        mesh=split,
        in_specs=(
            P(rows, None),
            P(rows),
            P(rows, None),
            P(rows, None),
            P(rows),
            P("tp", rep),
            P("tp", rep),
            P("tp", rep),
            P(rep),
            P(),
        ),
        out_specs=(P(rows, None), P(rows, None), P(rows, None), P(rows)),
        check_vma=False,
    )
```

time: 159 us -> 159 us (level)
  waiting for transfers between devices: 29.8 us -> 12.2 us
  Pallas kernels: 44.5 us -> 54.5 us
  local copies, waits for them, and re-layouts: 27 us -> 31.5 us
  other arithmetic: 17.9 us -> 20.1 us
    ppermute x35 -> x19, waiting for transfers between devices: 29.8 us -> 4.03 us  [swap(): lax.ppermute(value, axis, [(place, (place + step) % size) for place in ra...]
    ppermute x0 -> x8, starting transfers between devices: none -> 16.7 us  [trade(): lax.ppermute(value, axis, [(place, place ^ mask) for place in range(size)])]
    ppermute x35 -> x19, starting transfers between devices: 33.7 us -> 17.9 us  [swap(): lax.ppermute(value, axis, [(place, (place + step) % size) for place in ra...]
    ppermute x0 -> x8, waiting for transfers between devices: none -> 8.16 us  [trade(): lax.ppermute(value, axis, [(place, place ^ mask) for place in range(size)])]
    unnamed x63 -> x61, local copies, waits for them, and re-layouts: 24.7 us -> 29.9 us
    pallas_call x4, Pallas kernels: 17.9 us -> 23 us  [pair_product(): pl.pallas_call(kernel, out_shape=out_shape, grid_spec=pltpu.PrefetchScala...]
    pallas_call x4, Pallas kernels: 26.6 us -> 31.5 us  [the longest x3 24.4 us: weight_call(): pl.pallas_call(kernel, out_shape=out_shape, grid_spec=pltpu.PrefetchScala...]
    convert_element_type x3 -> x1, other arithmetic: 2.23 us -> 0.11 us  [per_device(): last += [trade(sums[k].astype(BF16), 'tp', k) for k in backward[2:-1]]]
  transfers between devices with their start and end apart: 35 -> 27, of which waited for: 7 -> 4; matrix products, arithmetic and copies ran while one was open for 8% -> 12% of each run, Pallas kernels for 28% -> 35%
where the time goes in v5:
time: 159 us; the launch traced here: 158 us
  Pallas kernels  54.5 us (34%)
  starting transfers between devices  34.6 us (22%)
  local copies, waits for them, and re-layouts  31.5 us (20%)
  other arithmetic  20.1 us (13%)
  waiting for transfers between devices  12.2 us (8%)
  between operations  4.69 us (3%)
    unnamed x61, local copies, waits for them, and re-layouts  29.9 us
    pallas_call x3, Pallas kernels, weight_call(): pl.pallas_call(kernel, out_shape=out_shape, grid_spec=pltpu.PrefetchScala...  24.4 us
    pallas_call x4, Pallas kernels, pair_product(): pl.pallas_call(kernel, out_shape=out_shape, grid_spec=pltpu.PrefetchScala...  23 us
    ppermute x19, starting transfers between devices, swap(): lax.ppermute(value, axis, [(place, (place + step) % size) for place in ra...  17.9 us
    ppermute x8, starting transfers between devices, trade(): lax.ppermute(value, axis, [(place, place ^ mask) for place in range(size)])  16.7 us
    ppermute x8, waiting for transfers between devices, trade(): lax.ppermute(value, axis, [(place, place ^ mask) for place in range(size)])  8.16 us
    pallas_call x1, Pallas kernels, first_value(): pl.pallas_call(functools.partial(value_kernel, inner_flags), out_shape=[t...  7.14 us
    reduce_sum x1, other arithmetic, per_device(): squares = jnp.sum(resid_wide * resid_wide, axis=1, keepdims=True)  5.1 us
  transfers between devices with their start and end apart: 27, of which 4 were waited for; matrix products, arithmetic and copies ran while one was open for 12% of the time, Pallas kernels for 35%

profile of v5, /device:TPU:0, one launch (start us, length us, event | category | flops | bytes accessed | tf_op | source)
XLA Modules:
  0.0 157.6 jit_solution(13351501943522999537)
XLA Ops:
  1.4 1.8 %multiply_convert_fusion.1 = bf16[256,512]{1,0:T(8,128)(2,1)} fusion(bf16[256,512]{1,0:T(8,128)(2,1)} %param.12, f32[256]{0:T(256)S(1)} %convert_element_type.145), kind=kLoop, calls=%fused_computation.21 | loop fusion | flops 393216 | bytes 525312 | tf_op jit(solution)/shard_map/convert_element_type | solution.py:318
  3.2 3.0 %collective-permute-start = (bf16[256,512]{1,0:T(8,128)(2,1)}, bf16[256,512]{1,0:T(8,128)(2,1)S(1)}, u32[]{:S(2)}, u32[]{:S(2)}) collective-permute-start(bf16[256,512]{1,0:T(8,128)(2,1)} %multiply_convert_fusion.1), channel_id=1, source_target_pairs={{0,1},{1,0},{2,3},{3,2},{4,5},{5,4},{6,7},{7,6},{8,9},{9,8},{10,11... | collective-permute-start | bytes 786440 | tf_op jit(solution)/shard_map/ppermute | solution.py:29
  6.2 1.5 collective-permute-start.1
  7.7 5.1 %multiply_reduce_fusion = f32[512]{0:T(512)S(1)} fusion(bf16[512,8192]{1,0:T(8,128)(2,1)} %resid_hbm.7), kind=kLoop, calls=%fused_computation | loop fusion | flops 12582400 | bytes 8390656 | tf_op jit(solution)/shard_map/reduce_sum | solution.py:321
  14.8 1.5 collective-permute-start.3
  16.4 2.7 %collective-permute-start.2 = (bf16[256,512]{1,0:T(8,128)(2,1)}, bf16[256,512]{1,0:T(8,128)(2,1)}, u32[]{:S(2)}, u32[]{:S(2)}) collective-permute-start(bf16[256,512]{1,0:T(8,128)(2,1)} %multiply_convert_fusion.1), channel_id=1, source_target_pairs={{0,2},{1,3},{2,0},{3,1},{4,6},{5,7},{6,4},{7,5},{8,10},{9,11},{10,... | collective-permute-start | bytes 786440 | tf_op jit(solution)/shard_map/ppermute | solution.py:29
  19.1 2.9 %collective-permute-done.3 = bf16[256,512]{1,0:T(8,128)(2,1)S(1)} collective-permute-done((bf16[256,512]{1,0:T(8,128)(2,1)S(1)}, bf16[256,512]{1,0:T(8,128)(2,1)S(1)}, u32[]{:S(2)}, u32[]{:S(2)}) %collective-permute-start.3) | collective-permute-done | bytes 262176 | tf_op jit(solution)/shard_map/ppermute | solution.py:24
  22.0 2.6 %collective-permute-start.5 = (f32[2,52,128]{2,1,0:T(8,128)S(1)}, f32[2,52,128]{2,1,0:T(8,128)S(1)}, u32[]{:S(2)}, u32[]{:S(2)}) collective-permute-start(f32[2,52,128]{2,1,0:T(8,128)S(1)} %pad_maximum_fusion.4), channel_id=1, source_target_pairs={{0,2},{1,3},{2,0},{3,1},{4,6},{5,7},{6,4},{7,5},{8,10},{9,11},{10,... | collective-permute-start | bytes 159752 | tf_op jit(solution)/shard_map/ppermute | solution.py:29
  26.6 1.6 %collective-permute-start.8 = (bf16[2,256,512]{2,1,0:T(8,128)(2,1)S(1)}, bf16[2,256,512]{2,1,0:T(8,128)(2,1)S(1)}, u32[]{:S(2)}, u32[]{:S(2)}) collective-permute-start(bf16[2,256,512]{2,1,0:T(8,128)(2,1)S(1)} %pad_maximum_fusion.rest_0_), channel_id=1, source_target_pairs={{0,16},{16,0},{1,17},{17,1},{2,18},{18,2},{3,19},{19,3},{4,20},{20... | collective-permute-start | bytes 1572872 | tf_op jit(solution)/shard_map/ppermute | solution.py:24
  28.2 4.5 %collective-permute-done.5 = f32[2,52,128]{2,1,0:T(8,128)S(1)} collective-permute-done((f32[2,52,128]{2,1,0:T(8,128)S(1)}, f32[2,52,128]{2,1,0:T(8,128)S(1)}, u32[]{:S(2)}, u32[]{:S(2)}) %collective-permute-start.5) | collective-permute-done | bytes 53280 | tf_op jit(solution)/shard_map/ppermute | solution.py:29
  32.7 1.4 fusion.29
  38.0 3.4 %copy-done = bf16[512,8192]{1,0:T(8,128)(2,1)S(1)} copy-done((bf16[512,8192]{1,0:T(8,128)(2,1)S(1)}, bf16[512,8192]{1,0:T(8,128)(2,1)}, u32[]{:S(2)}) %copy-start) | copy-done | bytes 8388632
  41.4 5.4 %shard_map.129 = bf16[2,4,512,256]{3,2,1,0:T(8,128)(2,1)} custom-call(s32[8]{0:T(128)S(1)} %stack.211.places_ref, bf16[512,512]{1,0:T(8,128)(2,1)S(1)} %copy.31.cot_ref, bf16[512,8192]{1,0:T(8,128)(2,1)S(1)} %copy-done), custom_call_target="tpu_custom_call" | custom-call | flops 1024 | bytes 1024 | tf_op jit(solution)/shard_map/pallas_call | solution.py:109
  47.6 3.5 %collective-permute-start.7 = (bf16[256,512]{1,0:T(8,128)(2,1)}, bf16[256,512]{1,0:T(8,128)(2,1)}, u32[]{:S(2)}, u32[]{:S(2)}) collective-permute-start(bf16[256,512]{1,0:T(8,128)(2,1)} %multiply_convert_fusion.1), channel_id=1, source_target_pairs={{0,3},{1,2},{2,1},{3,0},{4,7},{5,6},{6,5},{7,4},{8,11},{9,10},{10,... | collective-permute-start | bytes 786440 | tf_op jit(solution)/shard_map/ppermute | solution.py:29
  52.2 3.4 %copy-done.1 = bf16[512,8192]{1,0:T(8,128)(2,1)S(1)} copy-done((bf16[512,8192]{1,0:T(8,128)(2,1)S(1)}, bf16[512,8192]{1,0:T(8,128)(2,1)}, u32[]{:S(2)}) %copy-start.1) | copy-done | bytes 8388632
  55.6 5.2 %shard_map.130 = bf16[2,4,512,256]{3,2,1,0:T(8,128)(2,1)} custom-call(s32[8]{0:T(128)S(1)} %stack.202.places_ref, bf16[512,512]{1,0:T(8,128)(2,1)S(1)} %copy.32.cot_ref, bf16[512,8192]{1,0:T(8,128)(2,1)S(1)} %copy-done.1), custom_call_target="tpu_custom_call" | custom-call | flops 1024 | bytes 1024 | tf_op jit(solution)/shard_map/pallas_call | solution.py:109
  62.6 1.6 %collective-permute-start.15 = (bf16[2,256,512]{2,1,0:T(8,128)(2,1)S(1)}, bf16[2,256,512]{2,1,0:T(8,128)(2,1)}, u32[]{:S(2)}, u32[]{:S(2)}) collective-permute-start(bf16[2,256,512]{2,1,0:T(8,128)(2,1)S(1)} %pad_maximum_fusion.2.rest_4_), channel_id=1, source_target_pairs={{0,16},{16,0},{1,17},{17,1},{2,18},{18,2},{3,19},{19,3},{4,20},{20... | collective-permute-start | bytes 1572872 | tf_op jit(solution)/shard_map/ppermute | solution.py:24
  64.2 3.4 %copy-done.2 = bf16[512,8192]{1,0:T(8,128)(2,1)S(1)} copy-done((bf16[512,8192]{1,0:T(8,128)(2,1)S(1)}, bf16[512,8192]{1,0:T(8,128)(2,1)}, u32[]{:S(2)}) %copy-start.2) | copy-done | bytes 8388632
  67.6 6.7 %shard_map.131 = (bf16[2,512,256]{2,1,0:T(8,128)(2,1)}, bf16[2,512,256]{2,1,0:T(8,128)(2,1)S(1)}, bf16[2,512,256]{2,1,0:T(8,128)(2,1)}, bf16[2,512,256]{2,1,0:T(8,128)(2,1)S(1)}) custom-call(s32[8]{0:T(128)S(1)} %stack.226.places_ref, bf16[512,512]{1,0:T(8,128)(2,1)S(1)} %copy.31.cot_ref, bf16[512,8192]{1,0:T(8,128)(2,1)S(1)} %copy-done.2, ...), custom_call_target="tpu_custom_call" | custom-call | flops 1024 | bytes 1024 | tf_op jit(solution)/shard_map/pallas_call | solution.py:109
  80.5 3.4 %copy-done.3 = bf16[512,8192]{1,0:T(8,128)(2,1)S(1)} copy-done((bf16[512,8192]{1,0:T(8,128)(2,1)S(1)}, bf16[512,8192]{1,0:T(8,128)(2,1)}, u32[]{:S(2)}) %copy-start.3) | copy-done | bytes 8388632
  83.9 5.8 %shard_map.132 = (bf16[2,512,256]{2,1,0:T(8,128)(2,1)S(1)}, bf16[2,512,256]{2,1,0:T(8,128)(2,1)S(1)}, bf16[2,512,256]{2,1,0:T(8,128)(2,1)S(1)}, bf16[2,512,256]{2,1,0:T(8,128)(2,1)S(1)}) custom-call(s32[8]{0:T(128)S(1)} %stack.235.places_ref, bf16[512,512]{1,0:T(8,128)(2,1)S(1)} %copy.31.cot_ref, bf16[512,8192]{1,0:T(8,128)(2,1)S(1)} %copy-done.3, ...), custom_call_target="tpu_custom_call" | custom-call | flops 1024 | bytes 1024 | tf_op jit(solution)/shard_map/pallas_call | solution.py:109
  92.9 3.4 %copy-done.4 = bf16[512,8192]{1,0:T(8,128)(2,1)S(1)} copy-done((bf16[512,8192]{1,0:T(8,128)(2,1)S(1)}, bf16[512,8192]{1,0:T(8,128)(2,1)}, u32[]{:S(2)}) %copy-start.4) | copy-done | bytes 8388632
  96.3 7.1 %shard_map.133 = (f32[512,512]{1,0:T(8,128)S(1)}, bf16[4,1024,512]{2,1,0:T(8,128)(2,1)}) custom-call(s32[4]{0:T(128)S(1)} %get-tuple-element.174.places_ref, s32[4]{0:T(128)S(1)} %get-tuple-element.175.offsets_ref, bf16[512,8192]{1,0:T(8,128)(2,1)S(1)} %copy-done.4, bf16[2,256,512]{2,1,0:T(8,128)(2,1)S(1)} %pad_maximum_fusion.rest_0_, ...), custom_call_target="tpu_custom_call" | custom-call | flops 1024 | bytes 1024 | tf_op jit(solution)/shard_map/pallas_call | solution.py:222
  105.7 1.3 collective-permute-start.21
  108.1 1.6 %collective-permute-start.20 = (bf16[512,256]{1,0:T(8,128)(2,1)S(1)}, bf16[512,256]{1,0:T(8,128)(2,1)S(1)}, u32[]{:S(2)}, u32[]{:S(2)}) collective-permute-start(bf16[512,256]{1,0:T(8,128)(2,1)S(1)} %fusion.5), channel_id=1, source_target_pairs={{0,16},{16,0},{1,17},{17,1},{2,18},{18,2},{3,19},{19,3},{4,20},{20... | collective-permute-start | bytes 786440 | tf_op jit(solution)/shard_map/ppermute | solution.py:24
  112.4 3.4 %copy-done.5 = bf16[512,8192]{1,0:T(8,128)(2,1)S(1)} copy-done((bf16[512,8192]{1,0:T(8,128)(2,1)S(1)}, bf16[512,8192]{1,0:T(8,128)(2,1)}, u32[]{:S(2)}) %copy-start.5) | copy-done | bytes 8388632
  117.0 7.5 %shard_map.134 = (bf16[512,512]{1,0:T(8,128)(2,1)}, f32[512,1]{1,0:T(8,128)S(1)}) custom-call(s32[4]{0:T(128)S(1)} %pad_add_fusion.places_ref, bf16[512,8192]{1,0:T(8,128)(2,1)S(1)} %copy-done.5, bf16[4,1024,512]{2,1,0:T(8,128)(2,1)} %collective-permute-done.17.weight_ref, f32[512,512]{1,0:T(8,128)S(1)} %copy-done.7, ...), custom_call_target="tpu_custom_call" | custom-call | flops 1024 | bytes 1024 | tf_op jit(solution)/shard_map/pallas_call | solution.py:259
  128.8 1.6 %collective-permute-start.22 = (bf16[512,256]{1,0:T(8,128)(2,1)S(1)}, bf16[512,256]{1,0:T(8,128)(2,1)S(1)}, u32[]{:S(2)}, u32[]{:S(2)}) collective-permute-start(bf16[512,256]{1,0:T(8,128)(2,1)S(1)} %fusion.7), channel_id=1, source_target_pairs={{0,16},{16,0},{1,17},{17,1},{2,18},{18,2},{3,19},{19,3},{4,20},{20... | collective-permute-start | bytes 786440 | tf_op jit(solution)/shard_map/ppermute | solution.py:24
  131.4 2.4 %collective-permute-start.25 = (bf16[512,256]{1,0:T(8,128)(2,1)S(1)}, bf16[512,256]{1,0:T(8,128)(2,1)S(1)}, u32[]{:S(2)}, u32[]{:S(2)}) collective-permute-start(bf16[512,256]{1,0:T(8,128)(2,1)S(1)} %bitcast_add_fusion.3), channel_id=1, source_target_pairs={{0,2},{1,3},{2,0},{3,1},{4,6},{5,7},{6,4},{7,5},{8,10},{9,11},{10,... | collective-permute-start | bytes 786440 | tf_op jit(solution)/shard_map/ppermute | solution.py:29
  133.8 8.5 %shard_map.135.rest_0_ = bf16[512,8192]{1,0:T(8,128)(2,1)} custom-call(s32[4]{0:T(128)S(1)} %get-tuple-element.174.places_ref, bf16[512,8192]{1,0:T(8,128)(2,1)S(1)} %copy-done.5, bf16[4,1024,512]{2,1,0:T(8,128)(2,1)} %get-tuple-element.129.weight_ref, bf16[512,512]{1,0:T(8,128)(2,1)S(1)} %multiply_convert_fusion.cot_ref, ...), custom_call_target="tpu_custom_call" | custom-call | flops 1024 | bytes 1024 | tf_op jit(solution)/shard_map/pallas_call | solution.py:259
  143.4 8.5 %shard_map.136 = bf16[512,8192]{1,0:T(8,128)(2,1)} custom-call(s32[4]{0:T(128)S(1)} %pad_add_fusion.places_ref, bf16[512,8192]{1,0:T(8,128)(2,1)S(1)} %copy-done.5, bf16[4,1024,512]{2,1,0:T(8,128)(2,1)} %collective-permute-done.17.weight_ref, bf16[512,512]{1,0:T(8,128)(2,1)S(1)} %multiply_convert_fusion.cot_ref, ...), custom_call_target="tpu_custom_call", output_to_operand_aliasing={{}: (5, {})} | custom-call | flops 1024 | bytes 1024 | tf_op jit(solution)/shard_map/pallas_call | solution.py:259
  151.9 3.7 %collective-permute-done.25 = bf16[512,256]{1,0:T(8,128)(2,1)S(1)} collective-permute-done((bf16[512,256]{1,0:T(8,128)(2,1)S(1)}, bf16[512,256]{1,0:T(8,128)(2,1)S(1)}, u32[]{:S(2)}, u32[]{:S(2)}) %collective-permute-start.25) | collective-permute-done | bytes 262176 | tf_op jit(solution)/shard_map/ppermute | solution.py:29
  (128 shorter events, 34.1 us)
Async XLA Ops:
  0.7 36.9 %copy-start.20 = (bf16[512,512]{1,0:T(8,128)(2,1)S(1)}, bf16[512,512]{1,0:T(8,128)(2,1)}, u32[]{:S(2)}) copy-start(bf16[512,512]{1,0:T(8,128)(2,1)} %param.13) | copy-start | bytes 1572868
  3.2 11.0 %collective-permute-start = (bf16[256,512]{1,0:T(8,128)(2,1)}, bf16[256,512]{1,0:T(8,128)(2,1)S(1)}, u32[]{:S(2)}, u32[]{:S(2)}) collective-permute-start(bf16[256,512]{1,0:T(8,128)(2,1)} %multiply_convert_fusion.1), channel_id=1, source_target_pairs={{0,1},{1,0},{2,3},{3,2},{4,5},{5,4},{6,7},{7,6},{8,9},{9,8},{10,11... | collective-permute-start | bytes 786440 | tf_op jit(solution)/shard_map/ppermute | solution.py:29
  6.2 8.0 %collective-permute-start.1 = (bf16[256,512]{1,0:T(8,128)(2,1)}, bf16[256,512]{1,0:T(8,128)(2,1)S(1)}, u32[]{:S(2)}, u32[]{:S(2)}) collective-permute-start(bf16[256,512]{1,0:T(8,128)(2,1)} %multiply_convert_fusion.1), channel_id=1, source_target_pairs={{0,8},{8,0},{1,9},{9,1},{2,10},{10,2},{3,11},{11,3},{4,12},{12,4},... | collective-permute-start | bytes 786440 | tf_op jit(solution)/shard_map/ppermute | solution.py:24
  14.3 4.9 %collective-permute-start.4 = (f32[1,52,128]{2,1,0:T(8,128)S(1)}, f32[1,52,128]{2,1,0:T(8,128)S(1)}, u32[]{:S(2)}, u32[]{:S(2)}) collective-permute-start(f32[1,52,128]{2,1,0:T(8,128)S(1)} %maximum_bitcast_fusion), channel_id=1, source_target_pairs={{0,1},{1,0},{2,3},{3,2},{4,5},{5,4},{6,7},{7,6},{8,9},{9,8},{10,11... | collective-permute-start | bytes 79880 | tf_op jit(solution)/shard_map/ppermute | solution.py:29
  14.8 7.2 %collective-permute-start.3 = (bf16[256,512]{1,0:T(8,128)(2,1)S(1)}, bf16[256,512]{1,0:T(8,128)(2,1)S(1)}, u32[]{:S(2)}, u32[]{:S(2)}) collective-permute-start(bf16[256,512]{1,0:T(8,128)(2,1)S(1)} %collective-permute-done), channel_id=1, source_target_pairs={{0,16},{16,0},{1,17},{17,1},{2,18},{18,2},{3,19},{19,3},{4,20},{20... | collective-permute-start | bytes 786440 | tf_op jit(solution)/shard_map/ppermute | solution.py:24
  16.4 21.3 %collective-permute-start.2 = (bf16[256,512]{1,0:T(8,128)(2,1)}, bf16[256,512]{1,0:T(8,128)(2,1)}, u32[]{:S(2)}, u32[]{:S(2)}) collective-permute-start(bf16[256,512]{1,0:T(8,128)(2,1)} %multiply_convert_fusion.1), channel_id=1, source_target_pairs={{0,2},{1,3},{2,0},{3,1},{4,6},{5,7},{6,4},{7,5},{8,10},{9,11},{10,... | collective-permute-start | bytes 786440 | tf_op jit(solution)/shard_map/ppermute | solution.py:29
  22.0 10.6 %collective-permute-start.5 = (f32[2,52,128]{2,1,0:T(8,128)S(1)}, f32[2,52,128]{2,1,0:T(8,128)S(1)}, u32[]{:S(2)}, u32[]{:S(2)}) collective-permute-start(f32[2,52,128]{2,1,0:T(8,128)S(1)} %pad_maximum_fusion.4), channel_id=1, source_target_pairs={{0,2},{1,3},{2,0},{3,1},{4,6},{5,7},{6,4},{7,5},{8,10},{9,11},{10,... | collective-permute-start | bytes 159752 | tf_op jit(solution)/shard_map/ppermute | solution.py:29
  24.6 22.1 %collective-permute-start.9 = (bf16[2,256,512]{2,1,0:T(8,128)(2,1)S(1)}, bf16[2,256,512]{2,1,0:T(8,128)(2,1)S(1)}, u32[]{:S(2)}, u32[]{:S(2)}) collective-permute-start(bf16[2,256,512]{2,1,0:T(8,128)(2,1)S(1)} %pad_maximum_fusion.1.rest_2_), channel_id=1, source_target_pairs={{0,8},{8,0},{1,9},{9,1},{2,10},{10,2},{3,11},{11,3},{4,12},{12,4},... | collective-permute-start | bytes 1572872 | tf_op jit(solution)/shard_map/ppermute | solution.py:24
  26.6 20.2 %collective-permute-start.8 = (bf16[2,256,512]{2,1,0:T(8,128)(2,1)S(1)}, bf16[2,256,512]{2,1,0:T(8,128)(2,1)S(1)}, u32[]{:S(2)}, u32[]{:S(2)}) collective-permute-start(bf16[2,256,512]{2,1,0:T(8,128)(2,1)S(1)} %pad_maximum_fusion.rest_0_), channel_id=1, source_target_pairs={{0,16},{16,0},{1,17},{17,1},{2,18},{18,2},{3,19},{19,3},{4,20},{20... | collective-permute-start | bytes 1572872 | tf_op jit(solution)/shard_map/ppermute | solution.py:24
  47.6 16.6 %collective-permute-start.11 = (bf16[2,4,512,256]{3,2,1,0:T(8,128)(2,1)}, bf16[2,4,512,256]{3,2,1,0:T(8,128)(2,1)}, u32[]{:S(2)}, u32[]{:S(2)}) collective-permute-start(bf16[2,4,512,256]{3,2,1,0:T(8,128)(2,1)} %shard_map.129), channel_id=1, source_target_pairs={{0,4},{4,0},{1,5},{5,1},{2,6},{6,2},{3,7},{7,3},{8,12},{12,8},{9,1... | collective-permute-start | bytes 6291464 | tf_op jit(solution)/shard_map/ppermute | solution.py:24
  47.6 13.2 %collective-permute-start.7 = (bf16[256,512]{1,0:T(8,128)(2,1)}, bf16[256,512]{1,0:T(8,128)(2,1)}, u32[]{:S(2)}, u32[]{:S(2)}) collective-permute-start(bf16[256,512]{1,0:T(8,128)(2,1)} %multiply_convert_fusion.1), channel_id=1, source_target_pairs={{0,3},{1,2},{2,1},{3,0},{4,7},{5,6},{6,5},{7,4},{8,11},{9,10},{10,... | collective-permute-start | bytes 786440 | tf_op jit(solution)/shard_map/ppermute | solution.py:29
  51.1 9.7 %collective-permute-start.6 = (bf16[256,512]{1,0:T(8,128)(2,1)}, bf16[256,512]{1,0:T(8,128)(2,1)}, u32[]{:S(2)}, u32[]{:S(2)}) collective-permute-start(bf16[256,512]{1,0:T(8,128)(2,1)} %collective-permute-done.2), channel_id=1, source_target_pairs={{0,8},{8,0},{1,9},{9,1},{2,10},{10,2},{3,11},{11,3},{4,12},{12,4},... | collective-permute-start | bytes 786440 | tf_op jit(solution)/shard_map/ppermute | solution.py:24
  60.8 19.7 %collective-permute-start.14 = (bf16[2,4,512,256]{3,2,1,0:T(8,128)(2,1)}, bf16[2,4,512,256]{3,2,1,0:T(8,128)(2,1)}, u32[]{:S(2)}, u32[]{:S(2)}) collective-permute-start(bf16[2,4,512,256]{3,2,1,0:T(8,128)(2,1)} %shard_map.130), channel_id=1, source_target_pairs={{0,4},{4,0},{1,5},{5,1},{2,6},{6,2},{3,7},{7,3},{8,12},{12,8},{9,1... | collective-permute-start | bytes 6291464 | tf_op jit(solution)/shard_map/ppermute | solution.py:24
  60.9 15.1 %collective-permute-start.10 = (bf16[256,512]{1,0:T(8,128)(2,1)}, bf16[256,512]{1,0:T(8,128)(2,1)S(1)}, u32[]{:S(2)}, u32[]{:S(2)}) collective-permute-start(bf16[256,512]{1,0:T(8,128)(2,1)} %collective-permute-done.7), channel_id=1, source_target_pairs={{0,16},{16,0},{1,17},{17,1},{2,18},{18,2},{3,19},{19,3},{4,20},{20... | collective-permute-start | bytes 786440 | tf_op jit(solution)/shard_map/ppermute | solution.py:24
  62.6 30.3 %collective-permute-start.15 = (bf16[2,256,512]{2,1,0:T(8,128)(2,1)S(1)}, bf16[2,256,512]{2,1,0:T(8,128)(2,1)}, u32[]{:S(2)}, u32[]{:S(2)}) collective-permute-start(bf16[2,256,512]{2,1,0:T(8,128)(2,1)S(1)} %pad_maximum_fusion.2.rest_4_), channel_id=1, source_target_pairs={{0,16},{16,0},{1,17},{17,1},{2,18},{18,2},{3,19},{19,3},{4,20},{20... | collective-permute-start | bytes 1572872 | tf_op jit(solution)/shard_map/ppermute | solution.py:24
  77.8 15.1 %collective-permute-start.16 = (bf16[2,256,512]{2,1,0:T(8,128)(2,1)S(1)}, bf16[2,256,512]{2,1,0:T(8,128)(2,1)}, u32[]{:S(2)}, u32[]{:S(2)}) collective-permute-start(bf16[2,256,512]{2,1,0:T(8,128)(2,1)S(1)} %pad_maximum_fusion.3.rest_6_), channel_id=1, source_target_pairs={{0,8},{8,0},{1,9},{9,1},{2,10},{10,2},{3,11},{11,3},{4,12},{12,4},... | collective-permute-start | bytes 1572872 | tf_op jit(solution)/shard_map/ppermute | solution.py:24
  79.0 25.4 %collective-permute-start.12 = (bf16[2,512,256]{2,1,0:T(8,128)(2,1)}, bf16[2,512,256]{2,1,0:T(8,128)(2,1)}, u32[]{:S(2)}, u32[]{:S(2)}) collective-permute-start(bf16[2,512,256]{2,1,0:T(8,128)(2,1)} %get-tuple-element.100), channel_id=1, source_target_pairs={{0,8},{8,0},{1,9},{9,1},{2,10},{10,2},{3,11},{11,3},{4,12},{12,4},... | collective-permute-start | bytes 1572872 | tf_op jit(solution)/shard_map/ppermute | solution.py:24
  79.9 24.6 %collective-permute-start.13 = (bf16[2,512,256]{2,1,0:T(8,128)(2,1)}, bf16[2,512,256]{2,1,0:T(8,128)(2,1)}, u32[]{:S(2)}, u32[]{:S(2)}) collective-permute-start(bf16[2,512,256]{2,1,0:T(8,128)(2,1)} %get-tuple-element.101), channel_id=1, source_target_pairs={{0,16},{16,0},{1,17},{17,1},{2,18},{18,2},{3,19},{19,3},{4,20},{20... | collective-permute-start | bytes 1572872 | tf_op jit(solution)/shard_map/ppermute | solution.py:24
  104.4 7.9 %collective-permute-start.17 = (bf16[4,1024,512]{2,1,0:T(8,128)(2,1)}, bf16[4,1024,512]{2,1,0:T(8,128)(2,1)}, u32[]{:S(2)}, u32[]{:S(2)}) collective-permute-start(bf16[4,1024,512]{2,1,0:T(8,128)(2,1)} %get-tuple-element.129.weight_ref), channel_id=1, source_target_pairs={{0,4},{4,0},{1,5},{5,1},{2,6},{6,2},{3,7},{7,3},{8,12},{12,8},{9,1... | collective-permute-start | bytes 12582920 | tf_op jit(solution)/shard_map/ppermute | solution.py:24
  104.5 19.9 %copy-start.13 = (bf16[2,512,256]{2,1,0:T(8,128)(2,1)S(1)}, bf16[2,512,256]{2,1,0:T(8,128)(2,1)}, u32[]{:S(2)}) copy-start(bf16[2,512,256]{2,1,0:T(8,128)(2,1)} %copy-done.12) | copy-start | bytes 1572868
  105.7 18.7 %collective-permute-start.21 = (bf16[512,256]{1,0:T(8,128)(2,1)S(1)}, bf16[512,256]{1,0:T(8,128)(2,1)S(1)}, u32[]{:S(2)}, u32[]{:S(2)}) collective-permute-start(bf16[512,256]{1,0:T(8,128)(2,1)S(1)} %fusion.6), channel_id=1, source_target_pairs={{0,8},{8,0},{1,9},{9,1},{2,10},{10,2},{3,11},{11,3},{4,12},{12,4},... | collective-permute-start | bytes 786440 | tf_op jit(solution)/shard_map/ppermute | solution.py:24
  108.1 17.5 %copy-start.11 = (bf16[2,512,256]{2,1,0:T(8,128)(2,1)S(1)}, bf16[2,512,256]{2,1,0:T(8,128)(2,1)}, u32[]{:S(2)}) copy-start(bf16[2,512,256]{2,1,0:T(8,128)(2,1)} %copy-done.10) | copy-start | bytes 1572868
  108.1 16.4 %collective-permute-start.20 = (bf16[512,256]{1,0:T(8,128)(2,1)S(1)}, bf16[512,256]{1,0:T(8,128)(2,1)S(1)}, u32[]{:S(2)}, u32[]{:S(2)}) collective-permute-start(bf16[512,256]{1,0:T(8,128)(2,1)S(1)} %fusion.5), channel_id=1, source_target_pairs={{0,16},{16,0},{1,17},{17,1},{2,18},{18,2},{3,19},{19,3},{4,20},{20... | collective-permute-start | bytes 786440 | tf_op jit(solution)/shard_map/ppermute | solution.py:24
  109.7 16.9 %collective-permute-start.18 = (bf16[2,512,256]{2,1,0:T(8,128)(2,1)}, bf16[2,512,256]{2,1,0:T(8,128)(2,1)S(1)}, u32[]{:S(2)}, u32[]{:S(2)}) collective-permute-start(bf16[2,512,256]{2,1,0:T(8,128)(2,1)} %copy-done.19), channel_id=1, source_target_pairs={{0,8},{8,0},{1,9},{9,1},{2,10},{10,2},{3,11},{11,3},{4,12},{12,4},... | collective-permute-start | bytes 1572872 | tf_op jit(solution)/shard_map/ppermute | solution.py:24
  110.6 17.2 %collective-permute-start.19 = (bf16[2,512,256]{2,1,0:T(8,128)(2,1)}, bf16[2,512,256]{2,1,0:T(8,128)(2,1)S(1)}, u32[]{:S(2)}, u32[]{:S(2)}) collective-permute-start(bf16[2,512,256]{2,1,0:T(8,128)(2,1)} %copy-done.18), channel_id=1, source_target_pairs={{0,16},{16,0},{1,17},{17,1},{2,18},{18,2},{3,19},{19,3},{4,20},{20... | collective-permute-start | bytes 1572872 | tf_op jit(solution)/shard_map/ppermute | solution.py:24
  111.1 16.7 %copy-start.17 = (bf16[2,512,256]{2,1,0:T(8,128)(2,1)S(1)}, bf16[2,512,256]{2,1,0:T(8,128)(2,1)}, u32[]{:S(2)}) copy-start(bf16[2,512,256]{2,1,0:T(8,128)(2,1)} %copy-done.16) | copy-start | bytes 1572868
  127.8 14.4 %collective-permute-start.23 = (bf16[512,256]{1,0:T(8,128)(2,1)S(1)}, bf16[512,256]{1,0:T(8,128)(2,1)S(1)}, u32[]{:S(2)}, u32[]{:S(2)}) collective-permute-start(bf16[512,256]{1,0:T(8,128)(2,1)S(1)} %fusion.8), channel_id=1, source_target_pairs={{0,8},{8,0},{1,9},{9,1},{2,10},{10,2},{3,11},{11,3},{4,12},{12,4},... | collective-permute-start | bytes 786440 | tf_op jit(solution)/shard_map/ppermute | solution.py:24
  128.8 13.5 %collective-permute-start.22 = (bf16[512,256]{1,0:T(8,128)(2,1)S(1)}, bf16[512,256]{1,0:T(8,128)(2,1)S(1)}, u32[]{:S(2)}, u32[]{:S(2)}) collective-permute-start(bf16[512,256]{1,0:T(8,128)(2,1)S(1)} %fusion.7), channel_id=1, source_target_pairs={{0,16},{16,0},{1,17},{17,1},{2,18},{18,2},{3,19},{19,3},{4,20},{20... | collective-permute-start | bytes 786440 | tf_op jit(solution)/shard_map/ppermute | solution.py:24
  130.4 21.5 %collective-permute-start.24 = (bf16[512,256]{1,0:T(8,128)(2,1)S(1)}, bf16[512,256]{1,0:T(8,128)(2,1)S(1)}, u32[]{:S(2)}, u32[]{:S(2)}) collective-permute-start(bf16[512,256]{1,0:T(8,128)(2,1)S(1)} %bitcast_add_fusion.2), channel_id=1, source_target_pairs={{0,3},{1,2},{2,1},{3,0},{4,7},{5,6},{6,5},{7,4},{8,11},{9,10},{10,... | collective-permute-start | bytes 786440 | tf_op jit(solution)/shard_map/ppermute | solution.py:29
  131.4 24.2 %collective-permute-start.25 = (bf16[512,256]{1,0:T(8,128)(2,1)S(1)}, bf16[512,256]{1,0:T(8,128)(2,1)S(1)}, u32[]{:S(2)}, u32[]{:S(2)}) collective-permute-start(bf16[512,256]{1,0:T(8,128)(2,1)S(1)} %bitcast_add_fusion.3), channel_id=1, source_target_pairs={{0,2},{1,3},{2,0},{3,1},{4,6},{5,7},{6,4},{7,5},{8,10},{9,11},{10,... | collective-permute-start | bytes 786440 | tf_op jit(solution)/shard_map/ppermute | solution.py:29
  142.4 13.5 %copy-start.29 = (bf16[256]{0:T(256)(128)(2,1)S(1)}, bf16[256]{0:T(256)(128)(2,1)}, u32[]{:S(2)}) copy-start(bf16[256]{0:T(256)(128)(2,1)} %param.11) | copy-start | bytes 1540
  142.4 13.2 %collective-permute-start.26 = (bf16[512,256]{1,0:T(8,128)(2,1)S(1)}, bf16[512,256]{1,0:T(8,128)(2,1)S(1)}, u32[]{:S(2)}, u32[]{:S(2)}) collective-permute-start(bf16[512,256]{1,0:T(8,128)(2,1)S(1)} %fusion.1), channel_id=1, source_target_pairs={{0,1},{1,0},{2,3},{3,2},{4,5},{5,4},{6,7},{7,6},{8,9},{9,8},{10,11... | collective-permute-start | bytes 786440 | tf_op jit(solution)/shard_map/ppermute | solution.py:29
  (25 other events, 142.8 us)

commit v6 on v5

--- a/solution.py
+++ b/solution.py
@@ -29,6 +29,10 @@
     return lax.ppermute(value, axis, [(place, place ^ mask) for place in range(size)])
 
 
+def in_hbm(array):
+    return pltpu.with_memory_space_constraint(array, pltpu.HBM)
+
+
 def after(value, *earlier):
     return lax.optimization_barrier((value, earlier))[0]
 
@@ -41,41 +45,43 @@
     return chunk % 2 == 0
 
 
-def fetch(resid_hbm, places_ref, blocks_ref, sems, count):
-    width = blocks_ref.shape[2]
-
-    def copy(n):
-        where = pl.ds(pl.multiple_of(places_ref[n] * width, width), width)
-        return pltpu.make_async_copy(resid_hbm.at[:, where], blocks_ref.at[n], sems.at[n])
-
-    @pl.when(pl.program_id(0) == 0)
-    def _():
-        for n in range(count):
-            copy(n).start()
-
-    return copy
-
-
-def theirs_kernel(places_ref, cot_ref, resid_hbm, out_ref, blocks_ref, sems):
-    step = pl.program_id(0)
-    steps = blocks_ref.shape[0] // 2
-    copy = fetch(resid_hbm, places_ref, blocks_ref, sems, 2 * steps)
-    for slot in range(2):
-        copy(2 * step + slot).wait()
-        product = jnp.dot(cot_ref[...], blocks_ref[2 * step + slot], preferred_element_type=F32)
-        out_ref[slot, 0] = product.astype(BF16)
-
-
-def ours_kernel(places_ref, cot_ref, resid_hbm, other_ref, *rest):
-    outs, (blocks_ref, sems) = rest[:4], rest[4:]
+def theirs_kernel(places_ref, cot_ref, *rest):
+    count = len(rest) * 2 // 3
+    blocks, outs = rest[:count], rest[count:]
+    for slot, resid_ref in enumerate(blocks):
+        product = jnp.dot(cot_ref[...], resid_ref[...], preferred_element_type=F32)
+        outs[slot // 2][slot % 2, 0] = product.astype(BF16)
+
+
+def theirs_product(residual, cot_t, places, rows):
+    features, tokens = cot_t.shape
+    steps = 4
+    slots = places.shape[0] // steps
+    block = pl.BlockSpec((2, 1, features, rows), lambda i, p: (0, i, 0, 0))
+    return pl.pallas_call(
+        theirs_kernel,
+        out_shape=[pltpu.HBM((2, steps, features, rows), BF16)] * (slots // 2),
+        grid_spec=pltpu.PrefetchScalarGridSpec(
+            num_scalar_prefetch=1,
+            grid=(steps,),
+            in_specs=[pl.BlockSpec((features, tokens), lambda i, p: (0, 0))]
+            + [
+                pl.BlockSpec((tokens, rows), lambda i, p, slot=slot: (0, p[slots * i + slot]))
+                for slot in range(slots)
+            ],
+            out_specs=[block] * (slots // 2),
+        ),
+        cost_estimate=NOMINAL,
+        compiler_params=pltpu.CompilerParams(vmem_limit_bytes=PAIR_VMEM),
+    )(places, cot_t, *[in_hbm(residual)] * slots)
+
+
+def ours_kernel(places_ref, cot_ref, first_ref, second_ref, other_ref, *outs):
     step = pl.program_id(0)
     at_outer, at_inner = step // 2, lax.rem(step, 2)
-    steps = blocks_ref.shape[0] // 2
-    copy = fetch(resid_hbm, places_ref, blocks_ref, sems, 2 * steps)
-    for slot in range(2):
-        copy(2 * step + slot).wait()
+    for slot, resid_ref in enumerate((first_ref, second_ref)):
         send_ref, keep_ref = outs[2 * slot : 2 * slot + 2]
-        product = jnp.dot(cot_ref[...], blocks_ref[2 * step + slot], preferred_element_type=F32)
+        product = jnp.dot(cot_ref[...], resid_ref[...], preferred_element_type=F32)
         total = (product + other_ref[slot, 0].astype(F32)).astype(BF16)
         way, place = (at_inner, at_outer) if slot == 0 else (at_outer, at_inner)
 
@@ -88,40 +94,26 @@
             keep_ref[place] = total
 
 
-def pair_product(residual, cot_t, places, rows, other):
+def ours_product(residual, cot_t, places, rows, other):
     features, tokens = cot_t.shape
     steps = places.shape[0] // 2
-    in_specs = [
-        pl.BlockSpec((features, tokens), lambda i, p: (0, 0)),
-        pl.BlockSpec(memory_space=pltpu.HBM),
-    ]
-    operands = [cot_t, residual]
-    block = pl.BlockSpec((2, 1, features, rows), lambda i, p: (0, i, 0, 0))
-    if other is None:
-        kernel, out_specs = theirs_kernel, block
-        out_shape = jax.ShapeDtypeStruct((2, steps, features, rows), BF16)
-    else:
-        kernel = ours_kernel
-        in_specs.append(block)
-        operands.append(other)
-        out_specs = [pl.BlockSpec((2, features, rows), lambda i, p: (0, 0, 0))] * 4
-        out_shape = [jax.ShapeDtypeStruct((2, features, rows), BF16)] * 4
     return pl.pallas_call(
-        kernel,
-        out_shape=out_shape,
+        ours_kernel,
+        out_shape=[jax.ShapeDtypeStruct((2, features, rows), BF16)] * 4,
         grid_spec=pltpu.PrefetchScalarGridSpec(
             num_scalar_prefetch=1,
             grid=(steps,),
-            in_specs=in_specs,
-            out_specs=out_specs,
-            scratch_shapes=[
-                pltpu.VMEM((2 * steps, tokens, rows), BF16),
-                pltpu.SemaphoreType.DMA((2 * steps,)),
+            in_specs=[
+                pl.BlockSpec((features, tokens), lambda i, p: (0, 0)),
+                pl.BlockSpec((tokens, rows), lambda i, p: (0, p[2 * i])),
+                pl.BlockSpec((tokens, rows), lambda i, p: (0, p[2 * i + 1])),
+                pl.BlockSpec((2, 1, features, rows), lambda i, p: (0, i, 0, 0)),
             ],
+            out_specs=[pl.BlockSpec((2, features, rows), lambda i, p: (0, 0, 0))] * 4,
         ),
         cost_estimate=NOMINAL,
         compiler_params=pltpu.CompilerParams(vmem_limit_bytes=PAIR_VMEM),
-    )(places, *operands)
+    )(places, cot_t, in_hbm(residual), in_hbm(residual), other)
 
 
 def place_weight(inner_flags, offsets_ref, pieces, weight_ref):
@@ -151,13 +143,11 @@
     return specs
 
 
-def value_kernel(inner_flags, places_ref, offsets_ref, resid_hbm, *rest):
-    pieces, (total_ref, weight_ref, blocks_ref, sems) = rest[:-4], rest[-4:]
+def value_kernel(inner_flags, places_ref, offsets_ref, resid_ref, *rest):
+    pieces, (total_ref, weight_ref) = rest[:-2], rest[-2:]
     step = pl.program_id(0)
-    copy = fetch(resid_hbm, places_ref, blocks_ref, sems, blocks_ref.shape[0])
     place_weight(inner_flags, offsets_ref, pieces, weight_ref)
-    copy(step).wait()
-    product = jnp.dot(blocks_ref[step], weight_ref[0], preferred_element_type=F32)
+    product = jnp.dot(resid_ref[...], weight_ref[0], preferred_element_type=F32)
 
     @pl.when(step == 0)
     def _():
@@ -169,13 +159,10 @@
 
 
 def value_end_kernel(
-    width, places_ref, resid_hbm, weight_ref, first_ref, cot_ref, inv_ref,
-    value_ref, coef_ref, blocks_ref, sems, total_ref,
+    width, places_ref, resid_ref, weight_ref, first_ref, cot_ref, inv_ref, value_ref, coef_ref, total_ref
 ):
     step = pl.program_id(0)
-    copy = fetch(resid_hbm, places_ref, blocks_ref, sems, blocks_ref.shape[0])
-    copy(step).wait()
-    product = jnp.dot(blocks_ref[step], weight_ref[0], preferred_element_type=F32)
+    product = jnp.dot(resid_ref[...], weight_ref[0], preferred_element_type=F32)
 
     @pl.when(step == 0)
     def _():
@@ -194,23 +181,16 @@
         coef_ref[...] = share * (inv * inv) * (1.0 / width)
 
 
-def grad_kernel(places_ref, resid_hbm, weight_ref, cot_ref, coef_ref, *rest):
-    out_ref, blocks_ref, sems = rest[-3:]
-    step = pl.program_id(0)
-    copy = fetch(resid_hbm, places_ref, blocks_ref, sems, blocks_ref.shape[0])
+def grad_kernel(places_ref, resid_ref, weight_ref, cot_ref, coef_ref, *rest):
+    out_ref = rest[-1]
     grad = lax.dot_general(
         cot_ref[...], weight_ref[0], (((1,), (1,)), ((), ())), preferred_element_type=F32
     )
-    copy(step).wait()
-    out_ref[...] = (grad - blocks_ref[step].astype(F32) * coef_ref[...]).astype(BF16)
+    out_ref[...] = (grad - resid_ref[...].astype(F32) * coef_ref[...]).astype(BF16)
 
 
 def whole_block(array):
     return pl.BlockSpec(array.shape, lambda i, *_: (0, 0))
-
-
-def weight_scratch(tokens, depth, steps):
-    return [pltpu.VMEM((steps, tokens, depth), BF16), pltpu.SemaphoreType.DMA((steps,))]
 
 
 def first_value(inner_flags, places, offsets, residual, pieces):
@@ -221,36 +201,36 @@
     total = jax.ShapeDtypeStruct((tokens, features), F32)
     return pl.pallas_call(
         functools.partial(value_kernel, inner_flags),
-        out_shape=[total, jax.ShapeDtypeStruct((steps, depth, features), BF16)],
+        out_shape=[total, pltpu.HBM((steps, depth, features), BF16)],
         grid_spec=pltpu.PrefetchScalarGridSpec(
             num_scalar_prefetch=2,
             grid=(steps,),
-            in_specs=[pl.BlockSpec(memory_space=pltpu.HBM)] + piece_specs(inner_flags, rows, features),
+            in_specs=[pl.BlockSpec((tokens, depth), lambda i, p, o: (0, p[i]))]
+            + piece_specs(inner_flags, rows, features),
             out_specs=[
                 whole_block(total),
                 pl.BlockSpec((1, depth, features), lambda i, p, o: (p[i] // CORES, 0, 0)),
             ],
-            scratch_shapes=weight_scratch(tokens, depth, steps),
         ),
         cost_estimate=NOMINAL,
         compiler_params=pltpu.CompilerParams(vmem_limit_bytes=WEIGHT_VMEM),
-    )(places, offsets, residual, *pieces)
+    )(places, offsets, in_hbm(residual), *pieces)
 
 
 def weight_call(kernel, places, residual, weight, wholes, out_shape, earlier=None):
     tokens, width = residual.shape
     steps, depth, features = weight.shape
-    scratch = weight_scratch(tokens, depth, steps)
+    scratch = []
     if isinstance(out_shape, list):
         out_specs = [whole_block(array) for array in out_shape]
         scratch.append(pltpu.VMEM((tokens, features), F32))
     else:
         out_specs = pl.BlockSpec((tokens, depth), lambda i, p: (0, p[i]))
     in_specs = [
-        pl.BlockSpec(memory_space=pltpu.HBM),
+        pl.BlockSpec((tokens, depth), lambda i, p: (0, p[i])),
         pl.BlockSpec((1, depth, features), lambda i, p: (p[i] // CORES, 0, 0)),
     ] + [whole_block(array) for array in wholes]
-    operands = [places, residual, weight, *wholes]
+    operands = [places, in_hbm(residual), weight, *wholes]
     aliases = {}
     if earlier is not None:
         aliases = {len(operands): 0}
@@ -377,15 +357,13 @@
 
     def for_other(pair, cot_t):
         places = places_of(pair, 1 - core)
-        if in_place:
-            return pair_product(residual, cot_t, places, rows, None)
         both = after(product, cot_t)[places].reshape(len(chips), 2, features, rows)
         return both.swapaxes(0, 1)
 
     def for_us(pair, other):
         places = places_of(pair, core)
         if in_place:
-            send_a, keep_a, send_b, keep_b = pair_product(residual, cot_t, places, rows, other)
+            send_a, keep_a, send_b, keep_b = ours_product(residual, cot_t, places, rows, other)
             return ([send_a], keep_a), ([send_b], keep_b)
         both = product[places].reshape(len(chips), 2, features, rows).swapaxes(0, 1)
         total = widen([both, other]).astype(BF16).reshape(2, outer, inner, features, rows)
@@ -422,17 +400,17 @@
     for k in order[3:]:
         arrived[k] = trade(after(gained, arrived[2]), "tp", k)
     near[2] = near_of(2, arrived[2])
-    theirs = [for_other(pairs[0], cot_t)]
-    theirs[0], own_pieces[0], own_pieces[1] = lax.optimization_barrier(
-        (theirs[0], own_pieces[0], own_pieces[1])
-    )
-    others = [swap(theirs[0], "core", 1)]
-    theirs.append(for_other(pairs[1], after(cot_t, theirs[0])))
-    near[2], arrived[3], theirs[1] = lax.optimization_barrier((near[2], arrived[3], theirs[1]))
-    others.append(swap(theirs[1], "core", 1))
+    if in_place:
+        theirs = theirs_product(residual, cot_t, places_of(backward, 1 - core), rows)
+    else:
+        theirs = [for_other(pair, cot_t) for pair in pairs]
+    near[2], arrived[3], theirs, own_pieces[0], own_pieces[1] = lax.optimization_barrier(
+        (near[2], arrived[3], theirs, own_pieces[0], own_pieces[1])
+    )
+    others = [swap(part, "core", 1) for part in theirs]
     near[3] = near_of(3, arrived[3])
     own_pieces[2] = far_of(2, arrived[2], near[2])
-    sides = [for_us(pairs[0], after(others[0], theirs[1]))]
+    sides = [for_us(pairs[0], others[0])]
     near[3], sides[0] = lax.optimization_barrier((near[3], sides[0]))
     own_pieces[3] = far_of(3, arrived[3], near[3])
     got = [first_round(sides[0])]
@@ -440,8 +418,7 @@
     for n in range(2, len(pairs)):
         for k in order[2 * n : 2 * n + 2]:
             own_pieces[k] = far_of(k, arrived[k], near_of(k, arrived[k]))
-        others.append(swap(for_other(pairs[n], after(cot_t, sides[-1])), "core", 1))
-        sides.append(for_us(pairs[n], others[-1]))
+        sides.append(for_us(pairs[n], others[n]))
     sides[1:], own_pieces = lax.optimization_barrier((sides[1:], own_pieces))
 
     if in_place:
@@ -496,7 +473,7 @@
     if in_place:
         grad_shape = jax.ShapeDtypeStruct((rows_here, width), BF16)
         resid_grad = weight_call(
-            grad_kernel, places[0], residual, own_weight, [cot, coefficient], grad_shape
+            grad_kernel, places[0], residual, in_hbm(own_weight), [cot, coefficient], grad_shape
         )
         later[1], coefficient, resid_grad = lax.optimization_barrier((later[1], coefficient, resid_grad))
     else:

time: 159 us -> 144 us (0.906)
  local copies, waits for them, and re-layouts: 31.5 us -> 10.9 us
  waiting for transfers between devices: 12.2 us -> 23.4 us
  Pallas kernels: 54.5 us -> 49.5 us
    unnamed x61 -> x49, local copies, waits for them, and re-layouts: 29.9 us -> 9.57 us
    ppermute x19, waiting for transfers between devices: 4.03 us -> 13.5 us  [swap(): lax.ppermute(value, axis, [(place, (place + step) % size) for place in ra...]
    pallas_call x4 -> x3, Pallas kernels: 23 us -> 19.2 us  [the longest x2 12.6 us: ours_product(): pl.pallas_call(ours_kernel, out_shape=[jax.ShapeDtypeStruct((2, features,...]
    ppermute x8, waiting for transfers between devices: 8.16 us -> 9.9 us  [trade(): lax.ppermute(value, axis, [(place, place ^ mask) for place in range(size)])]
  transfers between devices with their start and end apart: 27 -> 27, of which waited for: 4 -> 9; matrix products, arithmetic and copies ran while one was open for 12% -> 12% of each run, Pallas kernels for 35% -> 35%
where the time goes in v6:
time: 144 us; the launch traced here: 143 us
  Pallas kernels  49.5 us (34%)
  starting transfers between devices  34.7 us (24%)
  waiting for transfers between devices  23.4 us (16%)
  other arithmetic  20 us (14%)
  local copies, waits for them, and re-layouts  10.9 us (8%)
  between operations  4.36 us (3%)
    pallas_call x3, Pallas kernels, weight_call(): pl.pallas_call(kernel, out_shape=out_shape, grid_spec=pltpu.PrefetchScala...  22.8 us
    ppermute x19, starting transfers between devices, swap(): lax.ppermute(value, axis, [(place, (place + step) % size) for place in ra...  17.7 us
    ppermute x8, starting transfers between devices, trade(): lax.ppermute(value, axis, [(place, place ^ mask) for place in range(size)])  16.9 us
    ppermute x19, waiting for transfers between devices, swap(): lax.ppermute(value, axis, [(place, (place + step) % size) for place in ra...  13.5 us
    pallas_call x2, Pallas kernels, ours_product(): pl.pallas_call(ours_kernel, out_shape=[jax.ShapeDtypeStruct((2, features,...  12.6 us
    ppermute x8, waiting for transfers between devices, trade(): lax.ppermute(value, axis, [(place, place ^ mask) for place in range(size)])  9.9 us
    unnamed x49, local copies, waits for them, and re-layouts  9.57 us
    pallas_call x1, Pallas kernels, first_value(): pl.pallas_call(functools.partial(value_kernel, inner_flags), out_shape=[t...  7.49 us
  transfers between devices with their start and end apart: 27, of which 9 were waited for; matrix products, arithmetic and copies ran while one was open for 12% of the time, Pallas kernels for 35%

profile of v6, /device:TPU:0, one launch (start us, length us, event | category | flops | bytes accessed | tf_op | source)
XLA Modules:
  0.0 142.8 jit_solution(6071136113200075911)
XLA Ops:
  1.4 1.8 %multiply_convert_fusion.1 = bf16[256,512]{1,0:T(8,128)(2,1)} fusion(bf16[256,512]{1,0:T(8,128)(2,1)} %param.12, f32[256]{0:T(256)S(1)} %convert_element_type.145), kind=kLoop, calls=%fused_computation.21 | loop fusion | flops 393216 | bytes 525312 | tf_op jit(solution)/shard_map/convert_element_type | solution.py:298
  3.2 3.0 %collective-permute-start = (bf16[256,512]{1,0:T(8,128)(2,1)}, bf16[256,512]{1,0:T(8,128)(2,1)S(1)}, u32[]{:S(2)}, u32[]{:S(2)}) collective-permute-start(bf16[256,512]{1,0:T(8,128)(2,1)} %multiply_convert_fusion.1), channel_id=1, source_target_pairs={{0,1},{1,0},{2,3},{3,2},{4,5},{5,4},{6,7},{7,6},{8,9},{9,8},{10,11... | collective-permute-start | bytes 786440 | tf_op jit(solution)/shard_map/ppermute | solution.py:29
  6.2 1.5 %collective-permute-start.1 = (bf16[256,512]{1,0:T(8,128)(2,1)}, bf16[256,512]{1,0:T(8,128)(2,1)S(1)}, u32[]{:S(2)}, u32[]{:S(2)}) collective-permute-start(bf16[256,512]{1,0:T(8,128)(2,1)} %multiply_convert_fusion.1), channel_id=1, source_target_pairs={{0,8},{8,0},{1,9},{9,1},{2,10},{10,2},{3,11},{11,3},{4,12},{12,4},... | collective-permute-start | bytes 786440 | tf_op jit(solution)/shard_map/ppermute | solution.py:24
  7.7 5.1 %multiply_reduce_fusion = f32[512]{0:T(512)S(1)} fusion(bf16[512,8192]{1,0:T(8,128)(2,1)} %resid_ref.3), kind=kLoop, calls=%fused_computation | loop fusion | flops 12582400 | bytes 8390656 | tf_op jit(solution)/shard_map/reduce_sum | solution.py:301
  14.7 1.5 %collective-permute-start.3 = (bf16[256,512]{1,0:T(8,128)(2,1)S(1)}, bf16[256,512]{1,0:T(8,128)(2,1)S(1)}, u32[]{:S(2)}, u32[]{:S(2)}) collective-permute-start(bf16[256,512]{1,0:T(8,128)(2,1)S(1)} %collective-permute-done), channel_id=1, source_target_pairs={{0,16},{16,0},{1,17},{17,1},{2,18},{18,2},{3,19},{19,3},{4,20},{20... | collective-permute-start | bytes 786440 | tf_op jit(solution)/shard_map/ppermute | solution.py:24
  16.4 2.7 %collective-permute-start.2 = (bf16[256,512]{1,0:T(8,128)(2,1)}, bf16[256,512]{1,0:T(8,128)(2,1)}, u32[]{:S(2)}, u32[]{:S(2)}) collective-permute-start(bf16[256,512]{1,0:T(8,128)(2,1)} %multiply_convert_fusion.1), channel_id=1, source_target_pairs={{0,2},{1,3},{2,0},{3,1},{4,6},{5,7},{6,4},{7,5},{8,10},{9,11},{10,... | collective-permute-start | bytes 786440 | tf_op jit(solution)/shard_map/ppermute | solution.py:29
  19.0 2.9 %collective-permute-done.3 = bf16[256,512]{1,0:T(8,128)(2,1)S(1)} collective-permute-done((bf16[256,512]{1,0:T(8,128)(2,1)S(1)}, bf16[256,512]{1,0:T(8,128)(2,1)S(1)}, u32[]{:S(2)}, u32[]{:S(2)}) %collective-permute-start.3) | collective-permute-done | bytes 262176 | tf_op jit(solution)/shard_map/ppermute | solution.py:24
  21.9 2.6 %collective-permute-start.5 = (f32[2,52,128]{2,1,0:T(8,128)S(1)}, f32[2,52,128]{2,1,0:T(8,128)S(1)}, u32[]{:S(2)}, u32[]{:S(2)}) collective-permute-start(f32[2,52,128]{2,1,0:T(8,128)S(1)} %pad_maximum_fusion.4), channel_id=1, source_target_pairs={{0,2},{1,3},{2,0},{3,1},{4,6},{5,7},{6,4},{7,5},{8,10},{9,11},{10,... | collective-permute-start | bytes 159752 | tf_op jit(solution)/shard_map/ppermute | solution.py:29
  26.6 1.6 %collective-permute-start.8 = (bf16[2,256,512]{2,1,0:T(8,128)(2,1)S(1)}, bf16[2,256,512]{2,1,0:T(8,128)(2,1)S(1)}, u32[]{:S(2)}, u32[]{:S(2)}) collective-permute-start(bf16[2,256,512]{2,1,0:T(8,128)(2,1)S(1)} %pad_maximum_fusion.rest_0_), channel_id=1, source_target_pairs={{0,16},{16,0},{1,17},{17,1},{2,18},{18,2},{3,19},{19,3},{4,20},{20... | collective-permute-start | bytes 1572872 | tf_op jit(solution)/shard_map/ppermute | solution.py:24
  28.2 4.4 %collective-permute-done.5 = f32[2,52,128]{2,1,0:T(8,128)S(1)} collective-permute-done((f32[2,52,128]{2,1,0:T(8,128)S(1)}, f32[2,52,128]{2,1,0:T(8,128)S(1)}, u32[]{:S(2)}, u32[]{:S(2)}) %collective-permute-start.5) | collective-permute-done | bytes 53280 | tf_op jit(solution)/shard_map/ppermute | solution.py:29
  32.6 1.4 fusion.29
  37.6 3.6 %collective-permute-start.7 = (bf16[256,512]{1,0:T(8,128)(2,1)}, bf16[256,512]{1,0:T(8,128)(2,1)}, u32[]{:S(2)}, u32[]{:S(2)}) collective-permute-start(bf16[256,512]{1,0:T(8,128)(2,1)} %multiply_convert_fusion.1), channel_id=1, source_target_pairs={{0,3},{1,2},{2,1},{3,0},{4,7},{5,6},{6,5},{7,4},{8,11},{9,10},{10,... | collective-permute-start | bytes 786440 | tf_op jit(solution)/shard_map/ppermute | solution.py:29
  42.4 6.6 %shard_map.129 = (bf16[2,4,512,256]{3,2,1,0:T(8,128)(2,1)}, bf16[2,4,512,256]{3,2,1,0:T(8,128)(2,1)}) custom-call(s32[16]{0:T(128)S(1)} %stack.207.places_ref, bf16[512,512]{1,0:T(8,128)(2,1)S(1)} %copy.29.cot_ref, bf16[512,8192]{1,0:T(8,128)(2,1)} %resid_ref.3, bf16[512,8192]{1,0:T(8,128)(2,1)} %resid_ref.3, bf16[512,8192]{1,0:T(8,128)(2,1)} %resid_ref.3, ...), custom_call_target="tpu_custom_call" | custom-call | flops 1024 | bytes 1024 | tf_op jit(solution)/shard_map/pallas_call | solution.py:61
  52.4 1.6 %collective-permute-start.15 = (bf16[2,256,512]{2,1,0:T(8,128)(2,1)S(1)}, bf16[2,256,512]{2,1,0:T(8,128)(2,1)}, u32[]{:S(2)}, u32[]{:S(2)}) collective-permute-start(bf16[2,256,512]{2,1,0:T(8,128)(2,1)S(1)} %pad_maximum_fusion.2.rest_4_), channel_id=1, source_target_pairs={{0,16},{16,0},{1,17},{17,1},{2,18},{18,2},{3,19},{19,3},{4,20},{20... | collective-permute-start | bytes 1572872 | tf_op jit(solution)/shard_map/ppermute | solution.py:24
  54.8 6.8 %shard_map.130 = (bf16[2,512,256]{2,1,0:T(8,128)(2,1)}, bf16[2,512,256]{2,1,0:T(8,128)(2,1)S(1)}, bf16[2,512,256]{2,1,0:T(8,128)(2,1)}, bf16[2,512,256]{2,1,0:T(8,128)(2,1)S(1)}) custom-call(s32[8]{0:T(128)S(1)} %stack.222.places_ref, bf16[512,512]{1,0:T(8,128)(2,1)S(1)} %copy.29.cot_ref, bf16[512,8192]{1,0:T(8,128)(2,1)} %resid_ref.3, ...), custom_call_target="tpu_custom_call" | custom-call | flops 1024 | bytes 1024 | tf_op jit(solution)/shard_map/pallas_call | solution.py:100
  65.9 1.2 collective-permute-start.12
  67.7 5.8 %shard_map.131 = (bf16[2,512,256]{2,1,0:T(8,128)(2,1)S(1)}, bf16[2,512,256]{2,1,0:T(8,128)(2,1)S(1)}, bf16[2,512,256]{2,1,0:T(8,128)(2,1)S(1)}, bf16[2,512,256]{2,1,0:T(8,128)(2,1)S(1)}) custom-call(s32[8]{0:T(128)S(1)} %stack.231.places_ref, bf16[512,512]{1,0:T(8,128)(2,1)S(1)} %copy.29.cot_ref, bf16[512,8192]{1,0:T(8,128)(2,1)} %resid_ref.3, ...), custom_call_target="tpu_custom_call" | custom-call | flops 1024 | bytes 1024 | tf_op jit(solution)/shard_map/pallas_call | solution.py:100
  76.7 3.1 %collective-permute-done.16.rest_7_ = bf16[2,256,512]{2,1,0:T(8,128)(2,1)} collective-permute-done((bf16[2,256,512]{2,1,0:T(8,128)(2,1)S(1)}, bf16[2,256,512]{2,1,0:T(8,128)(2,1)}, u32[]{:S(2)}, u32[]{:S(2)}) %collective-permute-start.16) | collective-permute-done | bytes 524320 | tf_op jit(solution)/shard_map/ppermute | solution.py:24
  79.9 7.5 %shard_map.132 = (f32[512,512]{1,0:T(8,128)S(1)}, bf16[4,1024,512]{2,1,0:T(8,128)(2,1)}) custom-call(s32[4]{0:T(128)S(1)} %get-tuple-element.174.places_ref, s32[4]{0:T(128)S(1)} %get-tuple-element.175.offsets_ref, bf16[512,8192]{1,0:T(8,128)(2,1)} %resid_ref.3, bf16[2,256,512]{2,1,0:T(8,128)(2,1)S(1)} %pad_maximum_fusion.rest_0_, ...), custom_call_target="tpu_custom_call" | custom-call | flops 1024 | bytes 1024 | tf_op jit(solution)/shard_map/pallas_call | solution.py:202
  88.3 2.0 %collective-permute-done.12 = bf16[2,512,256]{2,1,0:T(8,128)(2,1)} collective-permute-done((bf16[2,512,256]{2,1,0:T(8,128)(2,1)}, bf16[2,512,256]{2,1,0:T(8,128)(2,1)}, u32[]{:S(2)}, u32[]{:S(2)}) %collective-permute-start.12) | collective-permute-done | bytes 524320 | tf_op jit(solution)/shard_map/ppermute | solution.py:24
  95.2 1.5 %collective-permute-start.19 = (bf16[2,512,256]{2,1,0:T(8,128)(2,1)}, bf16[2,512,256]{2,1,0:T(8,128)(2,1)S(1)}, u32[]{:S(2)}, u32[]{:S(2)}) collective-permute-start(bf16[2,512,256]{2,1,0:T(8,128)(2,1)} %copy-done.12), channel_id=1, source_target_pairs={{0,16},{16,0},{1,17},{17,1},{2,18},{18,2},{3,19},{19,3},{4,20},{20... | collective-permute-start | bytes 1572872 | tf_op jit(solution)/shard_map/ppermute | solution.py:24
  96.7 1.3 multiply_convert_fusion.cot_ref
  98.0 1.2 copy-done.1
  99.3 7.4 %shard_map.133 = (bf16[512,512]{1,0:T(8,128)(2,1)}, f32[512,1]{1,0:T(8,128)S(1)}) custom-call(s32[4]{0:T(128)S(1)} %pad_add_fusion.places_ref, bf16[512,8192]{1,0:T(8,128)(2,1)} %resid_ref.3, bf16[4,1024,512]{2,1,0:T(8,128)(2,1)} %collective-permute-done.17.weight_ref, f32[512,512]{1,0:T(8,128)S(1)} %copy-done.1, ...), custom_call_target="tpu_custom_call" | custom-call | flops 1024 | bytes 1024 | tf_op jit(solution)/shard_map/pallas_call | solution.py:239
  108.8 2.6 %collective-permute-done.18 = bf16[2,512,256]{2,1,0:T(8,128)(2,1)S(1)} collective-permute-done((bf16[2,512,256]{2,1,0:T(8,128)(2,1)}, bf16[2,512,256]{2,1,0:T(8,128)(2,1)S(1)}, u32[]{:S(2)}, u32[]{:S(2)}) %collective-permute-start.18) | collective-permute-done | bytes 524320 | tf_op jit(solution)/shard_map/ppermute | solution.py:24
  111.4 1.8 %collective-permute-done.19 = bf16[2,512,256]{2,1,0:T(8,128)(2,1)S(1)} collective-permute-done((bf16[2,512,256]{2,1,0:T(8,128)(2,1)}, bf16[2,512,256]{2,1,0:T(8,128)(2,1)S(1)}, u32[]{:S(2)}, u32[]{:S(2)}) %collective-permute-start.19) | collective-permute-done | bytes 524320 | tf_op jit(solution)/shard_map/ppermute | solution.py:24
  113.2 1.2 collective-permute-start.23
  115.1 2.2 %collective-permute-start.24 = (bf16[512,256]{1,0:T(8,128)(2,1)S(1)}, bf16[512,256]{1,0:T(8,128)(2,1)S(1)}, u32[]{:S(2)}, u32[]{:S(2)}) collective-permute-start(bf16[512,256]{1,0:T(8,128)(2,1)S(1)} %bitcast_add_fusion.2), channel_id=1, source_target_pairs={{0,3},{1,2},{2,1},{3,0},{4,7},{5,6},{6,5},{7,4},{8,11},{9,10},{10,... | collective-permute-start | bytes 786440 | tf_op jit(solution)/shard_map/ppermute | solution.py:29
  117.3 2.4 %collective-permute-start.25 = (bf16[512,256]{1,0:T(8,128)(2,1)S(1)}, bf16[512,256]{1,0:T(8,128)(2,1)S(1)}, u32[]{:S(2)}, u32[]{:S(2)}) collective-permute-start(bf16[512,256]{1,0:T(8,128)(2,1)S(1)} %bitcast_add_fusion.3), channel_id=1, source_target_pairs={{0,2},{1,3},{2,0},{3,1},{4,6},{5,7},{6,4},{7,5},{8,10},{9,11},{10,... | collective-permute-start | bytes 786440 | tf_op jit(solution)/shard_map/ppermute | solution.py:29
  119.6 7.7 %shard_map.134.rest_0_ = bf16[512,8192]{1,0:T(8,128)(2,1)} custom-call(s32[4]{0:T(128)S(1)} %get-tuple-element.174.places_ref, bf16[512,8192]{1,0:T(8,128)(2,1)} %resid_ref.3, bf16[4,1024,512]{2,1,0:T(8,128)(2,1)} %get-tuple-element.129.weight_ref, bf16[512,512]{1,0:T(8,128)(2,1)S(1)} %multiply_convert_fusion.cot_ref, f32[512,1]{1,0:T(8,128)S(1)} %get-tuple-element.145.coef_ref), custom_call_target="tpu_custom_call" | custom-call | flops 1024 | bytes 1024 | tf_op jit(solution)/shard_map/pallas_call | solution.py:239
  127.6 7.7 %shard_map.135 = bf16[512,8192]{1,0:T(8,128)(2,1)} custom-call(s32[4]{0:T(128)S(1)} %pad_add_fusion.places_ref, bf16[512,8192]{1,0:T(8,128)(2,1)} %resid_ref.3, bf16[4,1024,512]{2,1,0:T(8,128)(2,1)} %collective-permute-done.17.weight_ref, bf16[512,512]{1,0:T(8,128)(2,1)S(1)} %multiply_convert_fusion.cot_ref, ...), custom_call_target="tpu_custom_call", output_to_operand_aliasing={{}: (5, {})} | custom-call | flops 1024 | bytes 1024 | tf_op jit(solution)/shard_map/pallas_call | solution.py:239
  135.3 5.5 %collective-permute-done.25 = bf16[512,256]{1,0:T(8,128)(2,1)S(1)} collective-permute-done((bf16[512,256]{1,0:T(8,128)(2,1)S(1)}, bf16[512,256]{1,0:T(8,128)(2,1)S(1)}, u32[]{:S(2)}, u32[]{:S(2)}) %collective-permute-start.25) | collective-permute-done | bytes 262176 | tf_op jit(solution)/shard_map/ppermute | solution.py:29
  (113 shorter events, 29.6 us)
Async XLA Ops:
  0.7 36.7 %copy-start.14 = (bf16[512,512]{1,0:T(8,128)(2,1)S(1)}, bf16[512,512]{1,0:T(8,128)(2,1)}, u32[]{:S(2)}) copy-start(bf16[512,512]{1,0:T(8,128)(2,1)} %param.13) | copy-start | bytes 1572868
  3.2 11.0 %collective-permute-start = (bf16[256,512]{1,0:T(8,128)(2,1)}, bf16[256,512]{1,0:T(8,128)(2,1)S(1)}, u32[]{:S(2)}, u32[]{:S(2)}) collective-permute-start(bf16[256,512]{1,0:T(8,128)(2,1)} %multiply_convert_fusion.1), channel_id=1, source_target_pairs={{0,1},{1,0},{2,3},{3,2},{4,5},{5,4},{6,7},{7,6},{8,9},{9,8},{10,11... | collective-permute-start | bytes 786440 | tf_op jit(solution)/shard_map/ppermute | solution.py:29
  6.2 8.0 %collective-permute-start.1 = (bf16[256,512]{1,0:T(8,128)(2,1)}, bf16[256,512]{1,0:T(8,128)(2,1)S(1)}, u32[]{:S(2)}, u32[]{:S(2)}) collective-permute-start(bf16[256,512]{1,0:T(8,128)(2,1)} %multiply_convert_fusion.1), channel_id=1, source_target_pairs={{0,8},{8,0},{1,9},{9,1},{2,10},{10,2},{3,11},{11,3},{4,12},{12,4},... | collective-permute-start | bytes 786440 | tf_op jit(solution)/shard_map/ppermute | solution.py:24
  14.2 4.8 %collective-permute-start.4 = (f32[1,52,128]{2,1,0:T(8,128)S(1)}, f32[1,52,128]{2,1,0:T(8,128)S(1)}, u32[]{:S(2)}, u32[]{:S(2)}) collective-permute-start(f32[1,52,128]{2,1,0:T(8,128)S(1)} %maximum_bitcast_fusion), channel_id=1, source_target_pairs={{0,1},{1,0},{2,3},{3,2},{4,5},{5,4},{6,7},{7,6},{8,9},{9,8},{10,11... | collective-permute-start | bytes 79880 | tf_op jit(solution)/shard_map/ppermute | solution.py:29
  14.7 7.2 %collective-permute-start.3 = (bf16[256,512]{1,0:T(8,128)(2,1)S(1)}, bf16[256,512]{1,0:T(8,128)(2,1)S(1)}, u32[]{:S(2)}, u32[]{:S(2)}) collective-permute-start(bf16[256,512]{1,0:T(8,128)(2,1)S(1)} %collective-permute-done), channel_id=1, source_target_pairs={{0,16},{16,0},{1,17},{17,1},{2,18},{18,2},{3,19},{19,3},{4,20},{20... | collective-permute-start | bytes 786440 | tf_op jit(solution)/shard_map/ppermute | solution.py:24
  16.4 21.3 %collective-permute-start.2 = (bf16[256,512]{1,0:T(8,128)(2,1)}, bf16[256,512]{1,0:T(8,128)(2,1)}, u32[]{:S(2)}, u32[]{:S(2)}) collective-permute-start(bf16[256,512]{1,0:T(8,128)(2,1)} %multiply_convert_fusion.1), channel_id=1, source_target_pairs={{0,2},{1,3},{2,0},{3,1},{4,6},{5,7},{6,4},{7,5},{8,10},{9,11},{10,... | collective-permute-start | bytes 786440 | tf_op jit(solution)/shard_map/ppermute | solution.py:29
  21.9 10.6 %collective-permute-start.5 = (f32[2,52,128]{2,1,0:T(8,128)S(1)}, f32[2,52,128]{2,1,0:T(8,128)S(1)}, u32[]{:S(2)}, u32[]{:S(2)}) collective-permute-start(f32[2,52,128]{2,1,0:T(8,128)S(1)} %pad_maximum_fusion.4), channel_id=1, source_target_pairs={{0,2},{1,3},{2,0},{3,1},{4,6},{5,7},{6,4},{7,5},{8,10},{9,11},{10,... | collective-permute-start | bytes 159752 | tf_op jit(solution)/shard_map/ppermute | solution.py:29
  24.5 24.9 %collective-permute-start.9 = (bf16[2,256,512]{2,1,0:T(8,128)(2,1)S(1)}, bf16[2,256,512]{2,1,0:T(8,128)(2,1)S(1)}, u32[]{:S(2)}, u32[]{:S(2)}) collective-permute-start(bf16[2,256,512]{2,1,0:T(8,128)(2,1)S(1)} %pad_maximum_fusion.1.rest_2_), channel_id=1, source_target_pairs={{0,8},{8,0},{1,9},{9,1},{2,10},{10,2},{3,11},{11,3},{4,12},{12,4},... | collective-permute-start | bytes 1572872 | tf_op jit(solution)/shard_map/ppermute | solution.py:24
  26.6 22.9 %collective-permute-start.8 = (bf16[2,256,512]{2,1,0:T(8,128)(2,1)S(1)}, bf16[2,256,512]{2,1,0:T(8,128)(2,1)S(1)}, u32[]{:S(2)}, u32[]{:S(2)}) collective-permute-start(bf16[2,256,512]{2,1,0:T(8,128)(2,1)S(1)} %pad_maximum_fusion.rest_0_), channel_id=1, source_target_pairs={{0,16},{16,0},{1,17},{17,1},{2,18},{18,2},{3,19},{19,3},{4,20},{20... | collective-permute-start | bytes 1572872 | tf_op jit(solution)/shard_map/ppermute | solution.py:24
  37.6 11.4 %collective-permute-start.7 = (bf16[256,512]{1,0:T(8,128)(2,1)}, bf16[256,512]{1,0:T(8,128)(2,1)}, u32[]{:S(2)}, u32[]{:S(2)}) collective-permute-start(bf16[256,512]{1,0:T(8,128)(2,1)} %multiply_convert_fusion.1), channel_id=1, source_target_pairs={{0,3},{1,2},{2,1},{3,0},{4,7},{5,6},{6,5},{7,4},{8,11},{9,10},{10,... | collective-permute-start | bytes 786440 | tf_op jit(solution)/shard_map/ppermute | solution.py:29
  41.2 8.3 %collective-permute-start.6 = (bf16[256,512]{1,0:T(8,128)(2,1)}, bf16[256,512]{1,0:T(8,128)(2,1)}, u32[]{:S(2)}, u32[]{:S(2)}) collective-permute-start(bf16[256,512]{1,0:T(8,128)(2,1)} %collective-permute-done.2), channel_id=1, source_target_pairs={{0,8},{8,0},{1,9},{9,1},{2,10},{10,2},{3,11},{11,3},{4,12},{12,4},... | collective-permute-start | bytes 786440 | tf_op jit(solution)/shard_map/ppermute | solution.py:24
  50.3 4.5 %collective-permute-start.11 = (bf16[2,4,512,256]{3,2,1,0:T(8,128)(2,1)}, bf16[2,4,512,256]{3,2,1,0:T(8,128)(2,1)}, u32[]{:S(2)}, u32[]{:S(2)}) collective-permute-start(bf16[2,4,512,256]{3,2,1,0:T(8,128)(2,1)} %get-tuple-element.94), channel_id=1, source_target_pairs={{0,4},{4,0},{1,5},{5,1},{2,6},{6,2},{3,7},{7,3},{8,12},{12,8},{9,1... | collective-permute-start | bytes 6291464 | tf_op jit(solution)/shard_map/ppermute | solution.py:24
  50.3 17.4 %collective-permute-start.14 = (bf16[2,4,512,256]{3,2,1,0:T(8,128)(2,1)}, bf16[2,4,512,256]{3,2,1,0:T(8,128)(2,1)}, u32[]{:S(2)}, u32[]{:S(2)}) collective-permute-start(bf16[2,4,512,256]{3,2,1,0:T(8,128)(2,1)} %get-tuple-element.101), channel_id=1, source_target_pairs={{0,4},{4,0},{1,5},{5,1},{2,6},{6,2},{3,7},{7,3},{8,12},{12,8},{9,1... | collective-permute-start | bytes 6291464 | tf_op jit(solution)/shard_map/ppermute | solution.py:24
  50.8 12.4 %collective-permute-start.10 = (bf16[256,512]{1,0:T(8,128)(2,1)}, bf16[256,512]{1,0:T(8,128)(2,1)S(1)}, u32[]{:S(2)}, u32[]{:S(2)}) collective-permute-start(bf16[256,512]{1,0:T(8,128)(2,1)} %collective-permute-done.7), channel_id=1, source_target_pairs={{0,16},{16,0},{1,17},{17,1},{2,18},{18,2},{3,19},{19,3},{4,20},{20... | collective-permute-start | bytes 786440 | tf_op jit(solution)/shard_map/ppermute | solution.py:24
  52.4 24.3 %collective-permute-start.15 = (bf16[2,256,512]{2,1,0:T(8,128)(2,1)S(1)}, bf16[2,256,512]{2,1,0:T(8,128)(2,1)}, u32[]{:S(2)}, u32[]{:S(2)}) collective-permute-start(bf16[2,256,512]{2,1,0:T(8,128)(2,1)S(1)} %pad_maximum_fusion.2.rest_4_), channel_id=1, source_target_pairs={{0,16},{16,0},{1,17},{17,1},{2,18},{18,2},{3,19},{19,3},{4,20},{20... | collective-permute-start | bytes 1572872 | tf_op jit(solution)/shard_map/ppermute | solution.py:24
  64.9 14.9 %collective-permute-start.16 = (bf16[2,256,512]{2,1,0:T(8,128)(2,1)S(1)}, bf16[2,256,512]{2,1,0:T(8,128)(2,1)}, u32[]{:S(2)}, u32[]{:S(2)}) collective-permute-start(bf16[2,256,512]{2,1,0:T(8,128)(2,1)S(1)} %pad_maximum_fusion.3.rest_6_), channel_id=1, source_target_pairs={{0,8},{8,0},{1,9},{9,1},{2,10},{10,2},{3,11},{11,3},{4,12},{12,4},... | collective-permute-start | bytes 1572872 | tf_op jit(solution)/shard_map/ppermute | solution.py:24
  65.9 24.4 %collective-permute-start.12 = (bf16[2,512,256]{2,1,0:T(8,128)(2,1)}, bf16[2,512,256]{2,1,0:T(8,128)(2,1)}, u32[]{:S(2)}, u32[]{:S(2)}) collective-permute-start(bf16[2,512,256]{2,1,0:T(8,128)(2,1)} %get-tuple-element.99), channel_id=1, source_target_pairs={{0,8},{8,0},{1,9},{9,1},{2,10},{10,2},{3,11},{11,3},{4,12},{12,4},... | collective-permute-start | bytes 1572872 | tf_op jit(solution)/shard_map/ppermute | solution.py:24
  67.0 23.3 %collective-permute-start.13 = (bf16[2,512,256]{2,1,0:T(8,128)(2,1)}, bf16[2,512,256]{2,1,0:T(8,128)(2,1)}, u32[]{:S(2)}, u32[]{:S(2)}) collective-permute-start(bf16[2,512,256]{2,1,0:T(8,128)(2,1)} %get-tuple-element.100), channel_id=1, source_target_pairs={{0,16},{16,0},{1,17},{17,1},{2,18},{18,2},{3,19},{19,3},{4,20},{20... | collective-permute-start | bytes 1572872 | tf_op jit(solution)/shard_map/ppermute | solution.py:24
  90.3 7.7 %collective-permute-start.17 = (bf16[4,1024,512]{2,1,0:T(8,128)(2,1)}, bf16[4,1024,512]{2,1,0:T(8,128)(2,1)}, u32[]{:S(2)}, u32[]{:S(2)}) collective-permute-start(bf16[4,1024,512]{2,1,0:T(8,128)(2,1)} %get-tuple-element.129.weight_ref), channel_id=1, source_target_pairs={{0,4},{4,0},{1,5},{5,1},{2,6},{6,2},{3,7},{7,3},{8,12},{12,8},{9,1... | collective-permute-start | bytes 12582920 | tf_op jit(solution)/shard_map/ppermute | solution.py:24
  90.3 16.3 %copy-start.7 = (bf16[2,512,256]{2,1,0:T(8,128)(2,1)S(1)}, bf16[2,512,256]{2,1,0:T(8,128)(2,1)}, u32[]{:S(2)}) copy-start(bf16[2,512,256]{2,1,0:T(8,128)(2,1)} %copy-done.6) | copy-start | bytes 1572868
  91.4 15.2 %collective-permute-start.21 = (bf16[512,256]{1,0:T(8,128)(2,1)S(1)}, bf16[512,256]{1,0:T(8,128)(2,1)S(1)}, u32[]{:S(2)}, u32[]{:S(2)}) collective-permute-start(bf16[512,256]{1,0:T(8,128)(2,1)S(1)} %fusion.6), channel_id=1, source_target_pairs={{0,8},{8,0},{1,9},{9,1},{2,10},{10,2},{3,11},{11,3},{4,12},{12,4},... | collective-permute-start | bytes 786440 | tf_op jit(solution)/shard_map/ppermute | solution.py:24
  93.4 13.2 %collective-permute-start.20 = (bf16[512,256]{1,0:T(8,128)(2,1)S(1)}, bf16[512,256]{1,0:T(8,128)(2,1)S(1)}, u32[]{:S(2)}, u32[]{:S(2)}) collective-permute-start(bf16[512,256]{1,0:T(8,128)(2,1)S(1)} %fusion.5), channel_id=1, source_target_pairs={{0,16},{16,0},{1,17},{17,1},{2,18},{18,2},{3,19},{19,3},{4,20},{20... | collective-permute-start | bytes 786440 | tf_op jit(solution)/shard_map/ppermute | solution.py:24
  94.1 17.3 %collective-permute-start.18 = (bf16[2,512,256]{2,1,0:T(8,128)(2,1)}, bf16[2,512,256]{2,1,0:T(8,128)(2,1)S(1)}, u32[]{:S(2)}, u32[]{:S(2)}) collective-permute-start(bf16[2,512,256]{2,1,0:T(8,128)(2,1)} %copy-done.13), channel_id=1, source_target_pairs={{0,8},{8,0},{1,9},{9,1},{2,10},{10,2},{3,11},{11,3},{4,12},{12,4},... | collective-permute-start | bytes 1572872 | tf_op jit(solution)/shard_map/ppermute | solution.py:24
  95.2 17.9 %collective-permute-start.19 = (bf16[2,512,256]{2,1,0:T(8,128)(2,1)}, bf16[2,512,256]{2,1,0:T(8,128)(2,1)S(1)}, u32[]{:S(2)}, u32[]{:S(2)}) collective-permute-start(bf16[2,512,256]{2,1,0:T(8,128)(2,1)} %copy-done.12), channel_id=1, source_target_pairs={{0,16},{16,0},{1,17},{17,1},{2,18},{18,2},{3,19},{19,3},{4,20},{20... | collective-permute-start | bytes 1572872 | tf_op jit(solution)/shard_map/ppermute | solution.py:24
  96.7 16.4 %copy-start.11 = (bf16[2,512,256]{2,1,0:T(8,128)(2,1)S(1)}, bf16[2,512,256]{2,1,0:T(8,128)(2,1)}, u32[]{:S(2)}) copy-start(bf16[2,512,256]{2,1,0:T(8,128)(2,1)} %copy-done.10) | copy-start | bytes 1572868
  99.3 15.2 %copy-start.9 = (bf16[2,512,256]{2,1,0:T(8,128)(2,1)S(1)}, bf16[2,512,256]{2,1,0:T(8,128)(2,1)}, u32[]{:S(2)}) copy-start(bf16[2,512,256]{2,1,0:T(8,128)(2,1)} %copy-done.8) | copy-start | bytes 1572868
  113.2 14.1 %collective-permute-start.23 = (bf16[512,256]{1,0:T(8,128)(2,1)S(1)}, bf16[512,256]{1,0:T(8,128)(2,1)S(1)}, u32[]{:S(2)}, u32[]{:S(2)}) collective-permute-start(bf16[512,256]{1,0:T(8,128)(2,1)S(1)} %fusion.8), channel_id=1, source_target_pairs={{0,8},{8,0},{1,9},{9,1},{2,10},{10,2},{3,11},{11,3},{4,12},{12,4},... | collective-permute-start | bytes 786440 | tf_op jit(solution)/shard_map/ppermute | solution.py:24
  114.5 12.8 %collective-permute-start.22 = (bf16[512,256]{1,0:T(8,128)(2,1)S(1)}, bf16[512,256]{1,0:T(8,128)(2,1)S(1)}, u32[]{:S(2)}, u32[]{:S(2)}) collective-permute-start(bf16[512,256]{1,0:T(8,128)(2,1)S(1)} %fusion.7), channel_id=1, source_target_pairs={{0,16},{16,0},{1,17},{17,1},{2,18},{18,2},{3,19},{19,3},{4,20},{20... | collective-permute-start | bytes 786440 | tf_op jit(solution)/shard_map/ppermute | solution.py:24
  115.1 20.2 %collective-permute-start.24 = (bf16[512,256]{1,0:T(8,128)(2,1)S(1)}, bf16[512,256]{1,0:T(8,128)(2,1)S(1)}, u32[]{:S(2)}, u32[]{:S(2)}) collective-permute-start(bf16[512,256]{1,0:T(8,128)(2,1)S(1)} %bitcast_add_fusion.2), channel_id=1, source_target_pairs={{0,3},{1,2},{2,1},{3,0},{4,7},{5,6},{6,5},{7,4},{8,11},{9,10},{10,... | collective-permute-start | bytes 786440 | tf_op jit(solution)/shard_map/ppermute | solution.py:29
  117.3 23.5 %collective-permute-start.25 = (bf16[512,256]{1,0:T(8,128)(2,1)S(1)}, bf16[512,256]{1,0:T(8,128)(2,1)S(1)}, u32[]{:S(2)}, u32[]{:S(2)}) collective-permute-start(bf16[512,256]{1,0:T(8,128)(2,1)S(1)} %bitcast_add_fusion.3), channel_id=1, source_target_pairs={{0,2},{1,3},{2,0},{3,1},{4,6},{5,7},{6,4},{7,5},{8,10},{9,11},{10,... | collective-permute-start | bytes 786440 | tf_op jit(solution)/shard_map/ppermute | solution.py:29
  127.5 13.7 %copy-start.23 = (bf16[256]{0:T(256)(128)(2,1)S(1)}, bf16[256]{0:T(256)(128)(2,1)}, u32[]{:S(2)}) copy-start(bf16[256]{0:T(256)(128)(2,1)} %param.11) | copy-start | bytes 1540
  127.5 13.3 %collective-permute-start.26 = (bf16[512,256]{1,0:T(8,128)(2,1)S(1)}, bf16[512,256]{1,0:T(8,128)(2,1)S(1)}, u32[]{:S(2)}, u32[]{:S(2)}) collective-permute-start(bf16[512,256]{1,0:T(8,128)(2,1)S(1)} %fusion.1), channel_id=1, source_target_pairs={{0,1},{1,0},{2,3},{3,2},{4,5},{5,4},{6,7},{7,6},{8,9},{9,8},{10,11... | collective-permute-start | bytes 786440 | tf_op jit(solution)/shard_map/ppermute | solution.py:29
  (19 other events, 127.2 us)

commit v7 on v6

--- a/solution.py
+++ b/solution.py
@@ -79,27 +79,32 @@
 def ours_kernel(places_ref, cot_ref, first_ref, second_ref, other_ref, *outs):
     step = pl.program_id(0)
     at_outer, at_inner = step // 2, lax.rem(step, 2)
-    for slot, resid_ref in enumerate((first_ref, second_ref)):
+    totals = [
+        (
+            jnp.dot(cot_ref[...], resid_ref[...], preferred_element_type=F32)
+            + other_ref[slot, 0].astype(F32)
+        ).astype(BF16)
+        for slot, resid_ref in enumerate((first_ref, second_ref))
+    ]
+    for slot, way in enumerate((at_inner, at_outer)):
         send_ref, keep_ref = outs[2 * slot : 2 * slot + 2]
-        product = jnp.dot(cot_ref[...], resid_ref[...], preferred_element_type=F32)
-        total = (product + other_ref[slot, 0].astype(F32)).astype(BF16)
-        way, place = (at_inner, at_outer) if slot == 0 else (at_outer, at_inner)
 
         @pl.when(way == 1)
         def _():
-            send_ref[place] = total
+            send_ref[0] = totals[slot]
 
         @pl.when(way == 0)
         def _():
-            keep_ref[place] = total
+            keep_ref[0] = totals[slot]
 
 
 def ours_product(residual, cot_t, places, rows, other):
     features, tokens = cot_t.shape
     steps = places.shape[0] // 2
+    indices = [lambda i: i // 2, lambda i: i // 2, lambda i: jnp.maximum(i - 2, 0), lambda i: jnp.minimum(i, 1)]
     return pl.pallas_call(
         ours_kernel,
-        out_shape=[jax.ShapeDtypeStruct((2, features, rows), BF16)] * 4,
+        out_shape=[pltpu.HBM((2, features, rows), BF16)] * 4,
         grid_spec=pltpu.PrefetchScalarGridSpec(
             num_scalar_prefetch=1,
             grid=(steps,),
@@ -109,7 +114,10 @@
                 pl.BlockSpec((tokens, rows), lambda i, p: (0, p[2 * i + 1])),
                 pl.BlockSpec((2, 1, features, rows), lambda i, p: (0, i, 0, 0)),
             ],
-            out_specs=[pl.BlockSpec((2, features, rows), lambda i, p: (0, 0, 0))] * 4,
+            out_specs=[
+                pl.BlockSpec((1, features, rows), lambda i, p, index=index: (index(i), 0, 0))
+                for index in indices
+            ],
         ),
         cost_estimate=NOMINAL,
         compiler_params=pltpu.CompilerParams(vmem_limit_bytes=PAIR_VMEM),
@@ -198,7 +206,7 @@
     rows, features = pieces[0].shape[1:]
     steps = places.shape[0]
     depth = width // (CORES * steps)
-    total = jax.ShapeDtypeStruct((tokens, features), F32)
+    total = pltpu.HBM((tokens, features), F32)
     return pl.pallas_call(
         functools.partial(value_kernel, inner_flags),
         out_shape=[total, pltpu.HBM((steps, depth, features), BF16)],
@@ -252,20 +260,83 @@
     )(*operands)
 
 
-def sequence_weight(shares, rows_here, seq_length, rep_count, tp_place):
-    seq = (shares[0].shape[0] - rows_here) // 3
-    top_max = functools.reduce(jnp.maximum, [share[:seq] for share in shares])
-    sum_exp = sum(share[seq : 2 * seq] * jnp.exp(share[:seq] - top_max) for share in shares)
-    picked = sum(share[2 * seq : 3 * seq] for share in shares)
+def squares_kernel(resid_ref, out_ref):
+    wide = resid_ref[...].astype(F32)
+    out_ref[...] = jnp.sum(wide * wide, axis=1, keepdims=True)
+
+
+def row_squares(residual):
+    tokens, width = residual.shape
+    rows = 64
+    return pl.pallas_call(
+        squares_kernel,
+        out_shape=jax.ShapeDtypeStruct((tokens, 1), F32),
+        grid=(tokens // rows,),
+        in_specs=[pl.BlockSpec((rows, width), lambda i: (i, 0))],
+        out_specs=pl.BlockSpec((rows, 1), lambda i: (i, 0)),
+        cost_estimate=NOMINAL,
+        compiler_params=pltpu.CompilerParams(vmem_limit_bytes=PAIR_VMEM),
+    )(in_hbm(residual))
+
+
+def cot_kernel(width, rep_count, info_ref, shares_ref, squares_ref, value_cot_ref, cot_ref, cot_t_ref, inv_ref):
+    place, length = info_ref[0], info_ref[1]
+    rows = value_cot_ref.shape[0]
+    own = rows // 128
+    seq = (shares_ref.shape[1] - own) // 3
+    shares = range(shares_ref.shape[0])
+
+    def below(first, shape):
+        at = lax.broadcasted_iota(jnp.int32, shape, 0) * 128 + lax.broadcasted_iota(jnp.int32, shape, 1)
+        return first + at < length
+
+    def summed(mask, value):
+        return jnp.sum(jnp.where(mask, value, 0.0), axis=(0, 1), keepdims=True)
+
+    maxes = [shares_ref[m, 0:seq] for m in shares]
+    top_max = functools.reduce(jnp.maximum, maxes)
+    sum_exp = functools.reduce(
+        jnp.add, [shares_ref[m, seq : 2 * seq] * jnp.exp(maxes[m] - top_max) for m in shares]
+    )
+    picked = functools.reduce(jnp.add, [shares_ref[m, 2 * seq : 3 * seq] for m in shares])
     ref_logp = picked - top_max - jnp.log(sum_exp)
-    total = jnp.zeros((), F32)
-    for mask, share in enumerate(shares):
-        first = jnp.bitwise_xor(tp_place, mask) * rows_here
-        live = first + jnp.arange(rows_here, dtype=jnp.int32) < seq_length
-        diff = share[3 * seq :] - lax.dynamic_slice_in_dim(ref_logp, first, rows_here)
-        total = total + jnp.sum(jnp.where(live, diff, 0.0))
-    seq_delta = total / seq_length.astype(F32)
-    return 2.0 * jax.nn.sigmoid(BETA * seq_delta) / rep_count
+    total = -summed(below(0, (seq, 128)), ref_logp)
+    for m in shares:
+        first = jnp.bitwise_xor(place, m) * rows
+        total += summed(below(first, (own, 128)), shares_ref[m, 3 * seq :])
+    seq_delta = total / jnp.full((1, 1), length, jnp.int32).astype(F32)
+    weight = (2.0 / rep_count) * jax.nn.sigmoid(BETA * seq_delta)
+    inv = lax.rsqrt(squares_ref[...] * (1.0 / width) + EPS)
+    live = place * rows + lax.broadcasted_iota(jnp.int32, (rows, 1), 0) < length
+    scaled = jnp.where(live, inv * weight, 0.0) * value_cot_ref[...].astype(F32)
+    cot_ref[...] = scaled.astype(BF16)
+    cot_t_ref[...] = scaled.T.astype(BF16)
+    inv_ref[...] = inv
+
+
+def scaled_cot(width, rep_count, info, shares, squares, value_cot):
+    rows, features = value_cot.shape
+
+    def whole(array):
+        return pl.BlockSpec(array.shape, lambda i, p: (0,) * array.ndim)
+
+    out_shape = [
+        jax.ShapeDtypeStruct((rows, features), BF16),
+        jax.ShapeDtypeStruct((features, rows), BF16),
+        jax.ShapeDtypeStruct((rows, 1), F32),
+    ]
+    return pl.pallas_call(
+        functools.partial(cot_kernel, width, rep_count),
+        out_shape=out_shape,
+        grid_spec=pltpu.PrefetchScalarGridSpec(
+            num_scalar_prefetch=1,
+            grid=(1,),
+            in_specs=[whole(shares), whole(squares), whole(value_cot)],
+            out_specs=[pl.BlockSpec(array.shape, lambda i, p: (0, 0)) for array in out_shape],
+        ),
+        cost_estimate=NOMINAL,
+        compiler_params=pltpu.CompilerParams(vmem_limit_bytes=PAIR_VMEM),
+    )(info, shares, squares, value_cot)
 
 
 def per_device(
@@ -297,8 +368,7 @@
 
     gained = (value_weight.astype(F32) * norm_gain.astype(F32)[:, None]).astype(BF16)
     residual, gained = lax.optimization_barrier((residual, gained))
-    resid_wide = residual.astype(F32)
-    squares = jnp.sum(resid_wide * resid_wide, axis=1, keepdims=True)
+    squares = row_squares(residual)
 
     def near_of(k, block):
         first = "inner" if inner_first(k) else "outer"
@@ -309,43 +379,38 @@
         near = jnp.stack([block] + nears)
         return [near] + [swap(near, second, s) for s in range(1, lax.axis_size(second))]
 
-    own_pieces, arrived, near = {}, {0: gained}, {}
-    arrived[1] = trade(gained, "tp", 1)
-    near[0] = near_of(0, gained)
-    arrived[1], near[0], squares, late_gained = lax.optimization_barrier(
-        (arrived[1], near[0], squares, gained)
-    )
-
     owned = jnp.where(
         target_ids // (VOCAB // tp_count) == tp_place,
         ref_target_logit[0],
         jnp.zeros_like(ref_target_logit[0]),
     )
     packed = jnp.concatenate([ref_shard_max[0], ref_shard_sum[0], owned, trainee_logp])
-    packed = after(packed.reshape(1, -1, 128), squares)
+    packed = packed.reshape(1, -1, 128)
+    own_pieces, near = {}, {}
+    arrived = {0: gained, 1: trade(gained, "tp", 1), 2: trade(gained, "tp", 2)}
+    near[0] = near_of(0, gained)
+    packed = jnp.concatenate([packed, trade(packed, "tp", 1)])
+    arrived[1], near[0], packed, squares, late_gained = lax.optimization_barrier(
+        (arrived[1], near[0], packed, squares, gained)
+    )
     near[1] = near_of(1, arrived[1])
-    arrived[2] = trade(late_gained, "tp", 2)
-    packed = jnp.concatenate([packed, trade(packed, "tp", 1)])
-    near[1], packed, near[0] = lax.optimization_barrier((near[1], packed, near[0]))
-    own_pieces[0] = far_of(0, gained, near[0])
-    own_pieces[1] = far_of(1, arrived[1], near[1])
+    for k in order[3:]:
+        arrived[k] = trade(late_gained, "tp", k)
     mask = 2
     while mask < tp_count:
         packed = jnp.concatenate([packed, trade(packed, "tp", mask)])
         mask *= 2
+    near[1], arrived[2], packed = lax.optimization_barrier((near[1], arrived[2], packed))
+    own_pieces[1] = far_of(1, arrived[1], near[1])
+    near[2] = near_of(2, arrived[2])
+    own_pieces[0] = far_of(0, gained, near[0])
     seq_length = lax.dynamic_index_in_dim(lengths, rep_place, keepdims=False)
-    seq_weight = sequence_weight(
-        list(packed.reshape(tp_count, -1)), rows_here, seq_length, rep_count, tp_place
-    )
-    positions = tp_place * rows_here + jnp.arange(rows_here, dtype=jnp.int32)
-    row_scale = (positions < seq_length).astype(F32) * seq_weight
-    inv_rms = lax.rsqrt(squares * (1.0 / width) + EPS)
-    cot = (inv_rms * row_scale[:, None] * value_cot.astype(F32)).astype(BF16)
-    cot_t = cot.T
+    info = jnp.stack([tp_place, seq_length]).astype(jnp.int32)
+    cot, cot_t, inv_rms = scaled_cot(width, rep_count, info, packed, squares, value_cot)
 
     def place_of(o, i, c, k):
         chip = lax.rem(at_outer + o, outer) * inner + lax.rem(at_inner + i, inner)
-        return (chip * CORES + c) * tp_count + jnp.bitwise_xor(tp_place, k)
+        return (chip * CORES + c) * tp_count + lax.rem(tp_place + k, tp_count)
 
     chips = [(o, i) for o in range(outer) for i in range(inner)]
     if not in_place:
@@ -396,19 +461,20 @@
 
     backward = order[::-1]
     pairs = [backward[i : i + 2] for i in range(0, tp_count, 2)]
-    arrived[2], cot_t = lax.optimization_barrier((arrived[2], cot_t))
-    for k in order[3:]:
-        arrived[k] = trade(after(gained, arrived[2]), "tp", k)
-    near[2] = near_of(2, arrived[2])
-    if in_place:
-        theirs = theirs_product(residual, cot_t, places_of(backward, 1 - core), rows)
-    else:
-        theirs = [for_other(pair, cot_t) for pair in pairs]
-    near[2], arrived[3], theirs, own_pieces[0], own_pieces[1] = lax.optimization_barrier(
-        (near[2], arrived[3], theirs, own_pieces[0], own_pieces[1])
+    def for_others(part, cot_t):
+        if in_place:
+            return theirs_product(residual, cot_t, places_of(part, 1 - core), rows)
+        return [for_other(part, cot_t)]
+
+    theirs = for_others(pairs[0], cot_t)
+    theirs, arrived[3] = lax.optimization_barrier((theirs, arrived[3]))
+    near[3] = near_of(3, arrived[3])
+    for pair in pairs[1:]:
+        theirs += for_others(pair, after(cot_t, theirs))
+    near[2], near[3], theirs, own_pieces[0], own_pieces[1] = lax.optimization_barrier(
+        (near[2], near[3], theirs, own_pieces[0], own_pieces[1])
     )
     others = [swap(part, "core", 1) for part in theirs]
-    near[3] = near_of(3, arrived[3])
     own_pieces[2] = far_of(2, arrived[2], near[2])
     sides = [for_us(pairs[0], others[0])]
     near[3], sides[0] = lax.optimization_barrier((near[3], sides[0]))
@@ -467,7 +533,7 @@
         coefficient = inv_rms * inv_rms * share * (1.0 / width)
     later[0], coefficient = lax.optimization_barrier((later[0], coefficient))
     sums = dict(zip(pairs[0], summed(sides[0], got[0], later[0])))
-    last = [trade(sums[k].astype(BF16), "tp", k) for k in pairs[0]]
+    last = [swap(sums[k].astype(BF16), "tp", k) for k in pairs[0]]
     got[1:], coefficient, sums = lax.optimization_barrier((got[1:], coefficient, sums))
     later += [second_round(side, parts) for side, parts in zip(sides[1:], got[1:])]
     if in_place:
@@ -483,7 +549,7 @@
         resid_grad = (normed_grad - residual.astype(F32) * coefficient).astype(BF16)
     for pair, *rounds in zip(pairs[1:], sides[1:], got[1:], later[1:]):
         sums.update(zip(pair, summed(*rounds)))
-    last += [trade(sums[k].astype(BF16), "tp", k) for k in backward[2:-1]]
+    last += [swap(sums[k].astype(BF16), "tp", k) for k in backward[2:-1]]
     if in_place:
         resid_grad = weight_call(
             grad_kernel, places[1], residual, other_weight, [cot, coefficient], grad_shape, resid_grad

time: 144 us -> 142 us (0.986)
  Pallas kernels: 49.5 us -> 60.5 us
  other arithmetic: 20 us -> 14.1 us
  waiting for transfers between devices: 23.4 us -> 29.2 us
  local copies, waits for them, and re-layouts: 10.9 us -> 5.16 us
  starting transfers between devices: 34.7 us -> 30.8 us
  between operations: 4.36 us -> 0.89 us
    ppermute x19 -> x22, waiting for transfers between devices: 13.5 us -> 22.5 us  [swap(): lax.ppermute(value, axis, [(place, (place + step) % size) for place in ra...]
    pallas_call x2 -> x4, Pallas kernels: 12.6 us -> 19.6 us  [the longest x2 11.9 us: ours_product(): pl.pallas_call(ours_kernel, out_shape=[pltpu.HBM((2, features, rows), BF1...]
    ppermute x8 -> x5, starting transfers between devices: 16.9 us -> 10 us  [trade(): lax.ppermute(value, axis, [(place, place ^ mask) for place in range(size)])]
    reduce_sum x2 -> x0, other arithmetic: 6.5 us -> none  [the longest x1 5.1 us: per_device(): squares = jnp.sum(resid_wide * resid_wide, axis=1, keepdims=True)]
    unnamed x49 -> x35, local copies, waits for them, and re-layouts: 9.57 us -> 4.11 us
    pallas_call x1 -> x2, Pallas kernels: 6.65 us -> 10.3 us  [theirs_product(): pl.pallas_call(theirs_kernel, out_shape=[pltpu.HBM((2, steps, features, r...]
    ppermute x8 -> x5, waiting for transfers between devices: 9.9 us -> 6.72 us  [trade(): lax.ppermute(value, axis, [(place, place ^ mask) for place in range(size)])]
    ppermute x19 -> x22, starting transfers between devices: 17.7 us -> 20.8 us  [swap(): lax.ppermute(value, axis, [(place, (place + step) % size) for place in ra...]
  transfers between devices with their start and end apart: 27 -> 27, of which waited for: 9 -> 8; matrix products, arithmetic and copies ran while one was open for 12% -> 8% of each run, Pallas kernels for 35% -> 43%
where the time goes in v7:
time: 142 us; the launch traced here: 141 us
  Pallas kernels  60.5 us (43%)
  starting transfers between devices  30.8 us (22%)
  waiting for transfers between devices  29.2 us (21%)
  other arithmetic  14.1 us (10%)
  local copies, waits for them, and re-layouts  5.16 us (4%)
    pallas_call x3, Pallas kernels, weight_call(): pl.pallas_call(kernel, out_shape=out_shape, grid_spec=pltpu.PrefetchScala...  22.8 us
    ppermute x22, waiting for transfers between devices, swap(): lax.ppermute(value, axis, [(place, (place + step) % size) for place in ra...  22.5 us
    ppermute x22, starting transfers between devices, swap(): lax.ppermute(value, axis, [(place, (place + step) % size) for place in ra...  20.8 us
    pallas_call x2, Pallas kernels, ours_product(): pl.pallas_call(ours_kernel, out_shape=[pltpu.HBM((2, features, rows), BF1...  11.9 us
    pallas_call x2, Pallas kernels, theirs_product(): pl.pallas_call(theirs_kernel, out_shape=[pltpu.HBM((2, steps, features, r...  10.3 us
    ppermute x5, starting transfers between devices, trade(): lax.ppermute(value, axis, [(place, place ^ mask) for place in range(size)])  10 us
    pallas_call x1, Pallas kernels, first_value(): pl.pallas_call(functools.partial(value_kernel, inner_flags), out_shape=[t...  7.82 us
    ppermute x5, waiting for transfers between devices, trade(): lax.ppermute(value, axis, [(place, place ^ mask) for place in range(size)])  6.72 us
  transfers between devices with their start and end apart: 27, of which 8 were waited for; matrix products, arithmetic and copies ran while one was open for 8% of the time, Pallas kernels for 43%

profile of v7, /device:TPU:0, one launch (start us, length us, event | category | flops | bytes accessed | tf_op | source)
XLA Modules:
  0.0 140.7 jit_solution(12064780495534583922)
XLA Ops:
  1.3 1.8 %multiply_convert_fusion = bf16[256,512]{1,0:T(8,128)(2,1)} fusion(bf16[256,512]{1,0:T(8,128)(2,1)} %param.12, f32[256]{0:T(256)S(1)} %convert_element_type.132), kind=kLoop, calls=%fused_computation.19 | loop fusion | flops 393216 | bytes 525312 | tf_op jit(solution)/shard_map/convert_element_type | solution.py:369
  3.1 3.0 %collective-permute-start = (bf16[256,512]{1,0:T(8,128)(2,1)}, bf16[256,512]{1,0:T(8,128)(2,1)S(1)}, u32[]{:S(2)}, u32[]{:S(2)}) collective-permute-start(bf16[256,512]{1,0:T(8,128)(2,1)} %multiply_convert_fusion), channel_id=1, source_target_pairs={{0,1},{1,0},{2,3},{3,2},{4,5},{5,4},{6,7},{7,6},{8,9},{9,8},{10,11... | collective-permute-start | bytes 786440 | tf_op jit(solution)/shard_map/ppermute | solution.py:29
  6.1 1.5 %collective-permute-start.1 = (bf16[256,512]{1,0:T(8,128)(2,1)}, bf16[256,512]{1,0:T(8,128)(2,1)S(1)}, u32[]{:S(2)}, u32[]{:S(2)}) collective-permute-start(bf16[256,512]{1,0:T(8,128)(2,1)} %multiply_convert_fusion), channel_id=1, source_target_pairs={{0,8},{8,0},{1,9},{9,1},{2,10},{10,2},{3,11},{11,3},{4,12},{12,4},... | collective-permute-start | bytes 786440 | tf_op jit(solution)/shard_map/ppermute | solution.py:24
  9.5 2.6 %collective-permute-start.4 = (bf16[256,512]{1,0:T(8,128)(2,1)}, bf16[256,512]{1,0:T(8,128)(2,1)}, u32[]{:S(2)}, u32[]{:S(2)}) collective-permute-start(bf16[256,512]{1,0:T(8,128)(2,1)} %multiply_convert_fusion), channel_id=1, source_target_pairs={{0,2},{1,3},{2,0},{3,1},{4,6},{5,7},{6,4},{7,5},{8,10},{9,11},{10,... | collective-permute-start | bytes 786440 | tf_op jit(solution)/shard_map/ppermute | solution.py:29
  12.1 6.7 %shard_map.129.squares_ref = f32[512,1]{1,0:T(8,128)S(1)} custom-call(bf16[512,8192]{1,0:T(8,128)(2,1)} %resid_ref.4), custom_call_target="tpu_custom_call" | custom-call | flops 1024 | bytes 1024 | tf_op jit(solution)/shard_map/pallas_call | solution.py:271
  18.8 1.6 %collective-permute-start.3 = (bf16[256,512]{1,0:T(8,128)(2,1)S(1)}, bf16[256,512]{1,0:T(8,128)(2,1)S(1)}, u32[]{:S(2)}, u32[]{:S(2)}) collective-permute-start(bf16[256,512]{1,0:T(8,128)(2,1)S(1)} %collective-permute-done), channel_id=1, source_target_pairs={{0,16},{16,0},{1,17},{17,1},{2,18},{18,2},{3,19},{19,3},{4,20},{20... | collective-permute-start | bytes 786440 | tf_op jit(solution)/shard_map/ppermute | solution.py:24
  20.7 3.6 %collective-permute-start.7 = (bf16[256,512]{1,0:T(8,128)(2,1)}, bf16[256,512]{1,0:T(8,128)(2,1)}, u32[]{:S(2)}, u32[]{:S(2)}) collective-permute-start(bf16[256,512]{1,0:T(8,128)(2,1)} %multiply_convert_fusion), channel_id=1, source_target_pairs={{0,3},{1,2},{2,1},{3,0},{4,7},{5,6},{6,5},{7,4},{8,11},{9,10},{10,... | collective-permute-start | bytes 786440 | tf_op jit(solution)/shard_map/ppermute | solution.py:29
  25.9 6.7 %collective-permute-done.5 = f32[2,52,128]{2,1,0:T(8,128)S(1)} collective-permute-done((f32[2,52,128]{2,1,0:T(8,128)S(1)}, f32[2,52,128]{2,1,0:T(8,128)S(1)}, u32[]{:S(2)}, u32[]{:S(2)}) %collective-permute-start.5) | collective-permute-done | bytes 53280 | tf_op jit(solution)/shard_map/ppermute | solution.py:29
  36.7 5.2 %shard_map.131 = bf16[2,4,512,256]{3,2,1,0:T(8,128)(2,1)} custom-call(s32[8]{0:T(128)S(1)} %stack.209.places_ref, bf16[512,512]{1,0:T(8,128)(2,1)S(1)} %get-tuple-element.90.cot_ref, bf16[512,8192]{1,0:T(8,128)(2,1)} %resid_ref.4, bf16[512,8192]{1,0:T(8,128)(2,1)} %resid_ref.4), custom_call_target="tpu_custom_call" | custom-call | flops 1024 | bytes 1024 | tf_op jit(solution)/shard_map/pallas_call | solution.py:61
  41.9 2.1 %collective-permute-start.8 = (bf16[256,512]{1,0:T(8,128)(2,1)}, bf16[256,512]{1,0:T(8,128)(2,1)}, u32[]{:S(2)}, u32[]{:S(2)}) collective-permute-start(bf16[256,512]{1,0:T(8,128)(2,1)} %collective-permute-done.7), channel_id=1, source_target_pairs={{0,16},{16,0},{1,17},{17,1},{2,18},{18,2},{3,19},{19,3},{4,20},{20... | collective-permute-start | bytes 786440 | tf_op jit(solution)/shard_map/ppermute | solution.py:24
  44.0 2.0 %collective-permute-start.6 = (bf16[256,512]{1,0:T(8,128)(2,1)}, bf16[256,512]{1,0:T(8,128)(2,1)}, u32[]{:S(2)}, u32[]{:S(2)}) collective-permute-start(bf16[256,512]{1,0:T(8,128)(2,1)} %collective-permute-done.4), channel_id=1, source_target_pairs={{0,8},{8,0},{1,9},{9,1},{2,10},{10,2},{3,11},{11,3},{4,12},{12,4},... | collective-permute-start | bytes 786440 | tf_op jit(solution)/shard_map/ppermute | solution.py:24
  46.0 5.1 %shard_map.132 = bf16[2,4,512,256]{3,2,1,0:T(8,128)(2,1)} custom-call(s32[8]{0:T(128)S(1)} %stack.220.places_ref, bf16[512,512]{1,0:T(8,128)(2,1)S(1)} %get-tuple-element.90.cot_ref, bf16[512,8192]{1,0:T(8,128)(2,1)} %resid_ref.4, bf16[512,8192]{1,0:T(8,128)(2,1)} %resid_ref.4), custom_call_target="tpu_custom_call" | custom-call | flops 1024 | bytes 1024 | tf_op jit(solution)/shard_map/pallas_call | solution.py:61
  53.8 2.7 %collective-permute-done.11.other_ref = bf16[2,4,512,256]{3,2,1,0:T(8,128)(2,1)} collective-permute-done((bf16[2,4,512,256]{3,2,1,0:T(8,128)(2,1)}, bf16[2,4,512,256]{3,2,1,0:T(8,128)(2,1)}, u32[]{:S(2)}, u32[]{:S(2)}) %collective-permute-start.11) | collective-permute-done | bytes 2097184 | tf_op jit(solution)/shard_map/ppermute | solution.py:24
  56.5 6.0 %shard_map.133 = (bf16[2,512,256]{2,1,0:T(8,128)(2,1)}, bf16[2,512,256]{2,1,0:T(8,128)(2,1)}, bf16[2,512,256]{2,1,0:T(8,128)(2,1)}, bf16[2,512,256]{2,1,0:T(8,128)(2,1)}) custom-call(s32[8]{0:T(128)S(1)} %stack.235.places_ref, bf16[512,512]{1,0:T(8,128)(2,1)S(1)} %get-tuple-element.90.cot_ref, bf16[512,8192]{1,0:T(8,128)(2,1)} %resid_ref.4, ...), custom_call_target="tpu_custom_call" | custom-call | flops 1024 | bytes 1024 | tf_op jit(solution)/shard_map/pallas_call | solution.py:105
  63.5 1.5 %collective-permute-start.16 = (bf16[2,256,512]{2,1,0:T(8,128)(2,1)S(1)}, bf16[2,256,512]{2,1,0:T(8,128)(2,1)}, u32[]{:S(2)}, u32[]{:S(2)}) collective-permute-start(bf16[2,256,512]{2,1,0:T(8,128)(2,1)S(1)} %pad_maximum_fusion.3.rest_6_), channel_id=1, source_target_pairs={{0,8},{8,0},{1,9},{9,1},{2,10},{10,2},{3,11},{11,3},{4,12},{12,4},... | collective-permute-start | bytes 1572872 | tf_op jit(solution)/shard_map/ppermute | solution.py:24
  65.9 6.0 %shard_map.134 = (bf16[2,512,256]{2,1,0:T(8,128)(2,1)}, bf16[2,512,256]{2,1,0:T(8,128)(2,1)}, bf16[2,512,256]{2,1,0:T(8,128)(2,1)}, bf16[2,512,256]{2,1,0:T(8,128)(2,1)}) custom-call(s32[8]{0:T(128)S(1)} %stack.244.places_ref, bf16[512,512]{1,0:T(8,128)(2,1)S(1)} %get-tuple-element.90.cot_ref, bf16[512,8192]{1,0:T(8,128)(2,1)} %resid_ref.4, ...), custom_call_target="tpu_custom_call" | custom-call | flops 1024 | bytes 1024 | tf_op jit(solution)/shard_map/pallas_call | solution.py:105
  71.8 6.6 %collective-permute-done.16.rest_7_ = bf16[2,256,512]{2,1,0:T(8,128)(2,1)} collective-permute-done((bf16[2,256,512]{2,1,0:T(8,128)(2,1)S(1)}, bf16[2,256,512]{2,1,0:T(8,128)(2,1)}, u32[]{:S(2)}, u32[]{:S(2)}) %collective-permute-start.16) | collective-permute-done | bytes 524320 | tf_op jit(solution)/shard_map/ppermute | solution.py:24
  78.5 7.8 %shard_map.135 = (f32[512,512]{1,0:T(8,128)}, bf16[4,1024,512]{2,1,0:T(8,128)(2,1)}) custom-call(s32[4]{0:T(128)S(1)} %get-tuple-element.160.places_ref, s32[4]{0:T(128)S(1)} %get-tuple-element.161.offsets_ref, bf16[512,8192]{1,0:T(8,128)(2,1)} %resid_ref.4, bf16[2,256,512]{2,1,0:T(8,128)(2,1)S(1)} %pad_maximum_fusion.rest_0_, ...), custom_call_target="tpu_custom_call" | custom-call | flops 1024 | bytes 1024 | tf_op jit(solution)/shard_map/pallas_call | solution.py:210
  86.3 2.6 %collective-permute-done.12 = bf16[2,512,256]{2,1,0:T(8,128)(2,1)} collective-permute-done((bf16[2,512,256]{2,1,0:T(8,128)(2,1)}, bf16[2,512,256]{2,1,0:T(8,128)(2,1)}, u32[]{:S(2)}, u32[]{:S(2)}) %collective-permute-start.12) | collective-permute-done | bytes 524320 | tf_op jit(solution)/shard_map/ppermute | solution.py:24
  89.9 1.5 %collective-permute-start.21 = (bf16[512,256]{1,0:T(8,128)(2,1)S(1)}, bf16[512,256]{1,0:T(8,128)(2,1)}, u32[]{:S(2)}, u32[]{:S(2)}) collective-permute-start(bf16[512,256]{1,0:T(8,128)(2,1)S(1)} %fusion.6), channel_id=1, source_target_pairs={{0,8},{8,0},{1,9},{9,1},{2,10},{10,2},{3,11},{11,3},{4,12},{12,4},... | collective-permute-start | bytes 786440 | tf_op jit(solution)/shard_map/ppermute | solution.py:24
  91.5 1.7 %fusion.5 = bf16[512,256]{1,0:T(8,128)(2,1)} fusion(bf16[2,512,256]{2,1,0:T(8,128)(2,1)} %collective-permute-done.12, bf16[2,512,256]{2,1,0:T(8,128)(2,1)S(1)} %copy-done.11), kind=kLoop, calls=%fused_computation.20 | loop fusion | flops 524288 | bytes 786432 | tf_op jit(solution)/shard_map/convert_element_type | solution.py:450
  93.8 1.9 %collective-permute-start.19 = (bf16[2,512,256]{2,1,0:T(8,128)(2,1)}, bf16[2,512,256]{2,1,0:T(8,128)(2,1)S(1)}, u32[]{:S(2)}, u32[]{:S(2)}) collective-permute-start(bf16[2,512,256]{2,1,0:T(8,128)(2,1)} %get-tuple-element.136), channel_id=1, source_target_pairs={{0,16},{16,0},{1,17},{17,1},{2,18},{18,2},{3,19},{19,3},{4,20},{20... | collective-permute-start | bytes 1572872 | tf_op jit(solution)/shard_map/ppermute | solution.py:24
  96.4 1.2 copy-done
  97.6 7.4 %shard_map.136 = (bf16[512,512]{1,0:T(8,128)(2,1)}, f32[512,1]{1,0:T(8,128)S(1)}) custom-call(s32[4]{0:T(128)S(1)} %pad_add_fusion.places_ref, bf16[512,8192]{1,0:T(8,128)(2,1)} %resid_ref.4, bf16[4,1024,512]{2,1,0:T(8,128)(2,1)} %collective-permute-done.17.weight_ref, f32[512,512]{1,0:T(8,128)S(1)} %copy-done, ...), custom_call_target="tpu_custom_call" | custom-call | flops 1024 | bytes 1024 | tf_op jit(solution)/shard_map/pallas_call | solution.py:247
  105.1 1.1 bitcast_add_fusion.2
  106.2 1.1 bitcast_add_fusion.3
  107.3 2.6 %collective-permute-done.18 = bf16[2,512,256]{2,1,0:T(8,128)(2,1)S(1)} collective-permute-done((bf16[2,512,256]{2,1,0:T(8,128)(2,1)}, bf16[2,512,256]{2,1,0:T(8,128)(2,1)S(1)}, u32[]{:S(2)}, u32[]{:S(2)}) %collective-permute-start.18) | collective-permute-done | bytes 524320 | tf_op jit(solution)/shard_map/ppermute | solution.py:24
  110.0 3.1 %collective-permute-done.19 = bf16[2,512,256]{2,1,0:T(8,128)(2,1)S(1)} collective-permute-done((bf16[2,512,256]{2,1,0:T(8,128)(2,1)}, bf16[2,512,256]{2,1,0:T(8,128)(2,1)S(1)}, u32[]{:S(2)}, u32[]{:S(2)}) %collective-permute-start.19) | collective-permute-done | bytes 524320 | tf_op jit(solution)/shard_map/ppermute | solution.py:24
  114.2 4.0 %collective-permute-start.24 = (bf16[512,256]{1,0:T(8,128)(2,1)S(1)}, bf16[512,256]{1,0:T(8,128)(2,1)S(1)}, u32[]{:S(2)}, u32[]{:S(2)}) collective-permute-start(bf16[512,256]{1,0:T(8,128)(2,1)S(1)} %bitcast_add_fusion.2), channel_id=1, source_target_pairs={{0,3},{1,0},{2,1},{3,2},{4,7},{5,4},{6,5},{7,6},{8,11},{9,8},{10,9... | collective-permute-start | bytes 786440 | tf_op jit(solution)/shard_map/ppermute | solution.py:24
  118.2 7.7 %shard_map.137.rest_0_ = bf16[512,8192]{1,0:T(8,128)(2,1)} custom-call(s32[4]{0:T(128)S(1)} %get-tuple-element.160.places_ref, bf16[512,8192]{1,0:T(8,128)(2,1)} %resid_ref.4, bf16[4,1024,512]{2,1,0:T(8,128)(2,1)} %get-tuple-element.129.weight_ref, bf16[512,512]{1,0:T(8,128)(2,1)S(1)} %get-tuple-element.131.cot_ref, f32[512,1]{1,0:T(8,128)S(1)} %get-tuple-element.147.coef_ref), custom_call_target="tpu_custom_call" | custom-call | flops 1024 | bytes 1024 | tf_op jit(solution)/shard_map/pallas_call | solution.py:247
  126.6 7.7 %shard_map.138 = bf16[512,8192]{1,0:T(8,128)(2,1)} custom-call(s32[4]{0:T(128)S(1)} %pad_add_fusion.places_ref, bf16[512,8192]{1,0:T(8,128)(2,1)} %resid_ref.4, bf16[4,1024,512]{2,1,0:T(8,128)(2,1)} %collective-permute-done.17.weight_ref, bf16[512,512]{1,0:T(8,128)(2,1)S(1)} %get-tuple-element.131.cot_ref, ...), custom_call_target="tpu_custom_call", output_to_operand_aliasing={{}: (5, {})} | custom-call | flops 1024 | bytes 1024 | tf_op jit(solution)/shard_map/pallas_call | solution.py:247
  134.3 4.3 %collective-permute-done.25 = bf16[512,256]{1,0:T(8,128)(2,1)S(1)} collective-permute-done((bf16[512,256]{1,0:T(8,128)(2,1)S(1)}, bf16[512,256]{1,0:T(8,128)(2,1)S(1)}, u32[]{:S(2)}, u32[]{:S(2)}) %collective-permute-start.25) | collective-permute-done | bytes 262176 | tf_op jit(solution)/shard_map/ppermute | solution.py:24
  (96 shorter events, 19.4 us)
Async XLA Ops:
  3.1 15.7 %collective-permute-start = (bf16[256,512]{1,0:T(8,128)(2,1)}, bf16[256,512]{1,0:T(8,128)(2,1)S(1)}, u32[]{:S(2)}, u32[]{:S(2)}) collective-permute-start(bf16[256,512]{1,0:T(8,128)(2,1)} %multiply_convert_fusion), channel_id=1, source_target_pairs={{0,1},{1,0},{2,3},{3,2},{4,5},{5,4},{6,7},{7,6},{8,9},{9,8},{10,11... | collective-permute-start | bytes 786440 | tf_op jit(solution)/shard_map/ppermute | solution.py:29
  6.1 12.7 %collective-permute-start.1 = (bf16[256,512]{1,0:T(8,128)(2,1)}, bf16[256,512]{1,0:T(8,128)(2,1)S(1)}, u32[]{:S(2)}, u32[]{:S(2)}) collective-permute-start(bf16[256,512]{1,0:T(8,128)(2,1)} %multiply_convert_fusion), channel_id=1, source_target_pairs={{0,8},{8,0},{1,9},{9,1},{2,10},{10,2},{3,11},{11,3},{4,12},{12,4},... | collective-permute-start | bytes 786440 | tf_op jit(solution)/shard_map/ppermute | solution.py:24
  9.0 24.2 %copy-start.15 = (s32[8]{0:T(128)S(1)}, s32[8]{0:T(128)}, u32[]{:S(2)}) copy-start(s32[8]{0:T(128)} %param.19) | copy-start | bytes 100
  9.0 9.7 %collective-permute-start.2 = (f32[1,52,128]{2,1,0:T(8,128)S(1)}, f32[1,52,128]{2,1,0:T(8,128)S(1)}, u32[]{:S(2)}, u32[]{:S(2)}) collective-permute-start(f32[1,52,128]{2,1,0:T(8,128)S(1)} %maximum_bitcast_fusion), channel_id=1, source_target_pairs={{0,1},{1,0},{2,3},{3,2},{4,5},{5,4},{6,7},{7,6},{8,9},{9,8},{10,11... | collective-permute-start | bytes 79880 | tf_op jit(solution)/shard_map/ppermute | solution.py:29
  9.5 23.2 %collective-permute-start.4 = (bf16[256,512]{1,0:T(8,128)(2,1)}, bf16[256,512]{1,0:T(8,128)(2,1)}, u32[]{:S(2)}, u32[]{:S(2)}) collective-permute-start(bf16[256,512]{1,0:T(8,128)(2,1)} %multiply_convert_fusion), channel_id=1, source_target_pairs={{0,2},{1,3},{2,0},{3,1},{4,6},{5,7},{6,4},{7,5},{8,10},{9,11},{10,... | collective-permute-start | bytes 786440 | tf_op jit(solution)/shard_map/ppermute | solution.py:29
  18.8 13.9 %collective-permute-start.3 = (bf16[256,512]{1,0:T(8,128)(2,1)S(1)}, bf16[256,512]{1,0:T(8,128)(2,1)S(1)}, u32[]{:S(2)}, u32[]{:S(2)}) collective-permute-start(bf16[256,512]{1,0:T(8,128)(2,1)S(1)} %collective-permute-done), channel_id=1, source_target_pairs={{0,16},{16,0},{1,17},{17,1},{2,18},{18,2},{3,19},{19,3},{4,20},{20... | collective-permute-start | bytes 786440 | tf_op jit(solution)/shard_map/ppermute | solution.py:24
  20.4 12.3 %collective-permute-start.5 = (f32[2,52,128]{2,1,0:T(8,128)S(1)}, f32[2,52,128]{2,1,0:T(8,128)S(1)}, u32[]{:S(2)}, u32[]{:S(2)}) collective-permute-start(f32[2,52,128]{2,1,0:T(8,128)S(1)} %pad_maximum_fusion.5), channel_id=1, source_target_pairs={{0,2},{1,3},{2,0},{3,1},{4,6},{5,7},{6,4},{7,5},{8,10},{9,11},{10,... | collective-permute-start | bytes 159752 | tf_op jit(solution)/shard_map/ppermute | solution.py:29
  20.7 21.2 %collective-permute-start.7 = (bf16[256,512]{1,0:T(8,128)(2,1)}, bf16[256,512]{1,0:T(8,128)(2,1)}, u32[]{:S(2)}, u32[]{:S(2)}) collective-permute-start(bf16[256,512]{1,0:T(8,128)(2,1)} %multiply_convert_fusion), channel_id=1, source_target_pairs={{0,3},{1,2},{2,1},{3,0},{4,7},{5,6},{6,5},{7,4},{8,11},{9,10},{10,... | collective-permute-start | bytes 786440 | tf_op jit(solution)/shard_map/ppermute | solution.py:29
  25.3 25.8 %collective-permute-start.9 = (bf16[2,256,512]{2,1,0:T(8,128)(2,1)S(1)}, bf16[2,256,512]{2,1,0:T(8,128)(2,1)S(1)}, u32[]{:S(2)}, u32[]{:S(2)}) collective-permute-start(bf16[2,256,512]{2,1,0:T(8,128)(2,1)S(1)} %pad_maximum_fusion.rest_0_), channel_id=1, source_target_pairs={{0,16},{16,0},{1,17},{17,1},{2,18},{18,2},{3,19},{19,3},{4,20},{20... | collective-permute-start | bytes 1572872 | tf_op jit(solution)/shard_map/ppermute | solution.py:24
  32.7 19.3 %collective-permute-start.10 = (bf16[2,256,512]{2,1,0:T(8,128)(2,1)S(1)}, bf16[2,256,512]{2,1,0:T(8,128)(2,1)S(1)}, u32[]{:S(2)}, u32[]{:S(2)}) collective-permute-start(bf16[2,256,512]{2,1,0:T(8,128)(2,1)S(1)} %pad_maximum_fusion.1.rest_2_), channel_id=1, source_target_pairs={{0,8},{8,0},{1,9},{9,1},{2,10},{10,2},{3,11},{11,3},{4,12},{12,4},... | collective-permute-start | bytes 1572872 | tf_op jit(solution)/shard_map/ppermute | solution.py:24
  41.9 9.3 %collective-permute-start.8 = (bf16[256,512]{1,0:T(8,128)(2,1)}, bf16[256,512]{1,0:T(8,128)(2,1)}, u32[]{:S(2)}, u32[]{:S(2)}) collective-permute-start(bf16[256,512]{1,0:T(8,128)(2,1)} %collective-permute-done.7), channel_id=1, source_target_pairs={{0,16},{16,0},{1,17},{17,1},{2,18},{18,2},{3,19},{19,3},{4,20},{20... | collective-permute-start | bytes 786440 | tf_op jit(solution)/shard_map/ppermute | solution.py:24
  44.0 7.2 %collective-permute-start.6 = (bf16[256,512]{1,0:T(8,128)(2,1)}, bf16[256,512]{1,0:T(8,128)(2,1)}, u32[]{:S(2)}, u32[]{:S(2)}) collective-permute-start(bf16[256,512]{1,0:T(8,128)(2,1)} %collective-permute-done.4), channel_id=1, source_target_pairs={{0,8},{8,0},{1,9},{9,1},{2,10},{10,2},{3,11},{11,3},{4,12},{12,4},... | collective-permute-start | bytes 786440 | tf_op jit(solution)/shard_map/ppermute | solution.py:24
  52.0 4.5 %collective-permute-start.11 = (bf16[2,4,512,256]{3,2,1,0:T(8,128)(2,1)}, bf16[2,4,512,256]{3,2,1,0:T(8,128)(2,1)}, u32[]{:S(2)}, u32[]{:S(2)}) collective-permute-start(bf16[2,4,512,256]{3,2,1,0:T(8,128)(2,1)} %shard_map.131), channel_id=1, source_target_pairs={{0,4},{4,0},{1,5},{5,1},{2,6},{6,2},{3,7},{7,3},{8,12},{12,8},{9,1... | collective-permute-start | bytes 6291464 | tf_op jit(solution)/shard_map/ppermute | solution.py:24
  52.0 13.9 %collective-permute-start.14 = (bf16[2,4,512,256]{3,2,1,0:T(8,128)(2,1)}, bf16[2,4,512,256]{3,2,1,0:T(8,128)(2,1)}, u32[]{:S(2)}, u32[]{:S(2)}) collective-permute-start(bf16[2,4,512,256]{3,2,1,0:T(8,128)(2,1)} %shard_map.132), channel_id=1, source_target_pairs={{0,4},{4,0},{1,5},{5,1},{2,6},{6,2},{3,7},{7,3},{8,12},{12,8},{9,1... | collective-permute-start | bytes 6291464 | tf_op jit(solution)/shard_map/ppermute | solution.py:24
  53.7 18.2 %collective-permute-start.15 = (bf16[2,256,512]{2,1,0:T(8,128)(2,1)S(1)}, bf16[2,256,512]{2,1,0:T(8,128)(2,1)}, u32[]{:S(2)}, u32[]{:S(2)}) collective-permute-start(bf16[2,256,512]{2,1,0:T(8,128)(2,1)S(1)} %pad_maximum_fusion.2.rest_4_), channel_id=1, source_target_pairs={{0,16},{16,0},{1,17},{17,1},{2,18},{18,2},{3,19},{19,3},{4,20},{20... | collective-permute-start | bytes 1572872 | tf_op jit(solution)/shard_map/ppermute | solution.py:24
  63.5 14.9 %collective-permute-start.16 = (bf16[2,256,512]{2,1,0:T(8,128)(2,1)S(1)}, bf16[2,256,512]{2,1,0:T(8,128)(2,1)}, u32[]{:S(2)}, u32[]{:S(2)}) collective-permute-start(bf16[2,256,512]{2,1,0:T(8,128)(2,1)S(1)} %pad_maximum_fusion.3.rest_6_), channel_id=1, source_target_pairs={{0,8},{8,0},{1,9},{9,1},{2,10},{10,2},{3,11},{11,3},{4,12},{12,4},... | collective-permute-start | bytes 1572872 | tf_op jit(solution)/shard_map/ppermute | solution.py:24
  65.0 23.9 %collective-permute-start.12 = (bf16[2,512,256]{2,1,0:T(8,128)(2,1)}, bf16[2,512,256]{2,1,0:T(8,128)(2,1)}, u32[]{:S(2)}, u32[]{:S(2)}) collective-permute-start(bf16[2,512,256]{2,1,0:T(8,128)(2,1)} %get-tuple-element.99), channel_id=1, source_target_pairs={{0,8},{8,0},{1,9},{9,1},{2,10},{10,2},{3,11},{11,3},{4,12},{12,4},... | collective-permute-start | bytes 1572872 | tf_op jit(solution)/shard_map/ppermute | solution.py:24
  65.6 23.3 %collective-permute-start.13 = (bf16[2,512,256]{2,1,0:T(8,128)(2,1)}, bf16[2,512,256]{2,1,0:T(8,128)(2,1)}, u32[]{:S(2)}, u32[]{:S(2)}) collective-permute-start(bf16[2,512,256]{2,1,0:T(8,128)(2,1)} %get-tuple-element.100), channel_id=1, source_target_pairs={{0,16},{16,0},{1,17},{17,1},{2,18},{18,2},{3,19},{19,3},{4,20},{20... | collective-permute-start | bytes 1572872 | tf_op jit(solution)/shard_map/ppermute | solution.py:24
  78.5 13.0 %copy-start.11 = (bf16[2,512,256]{2,1,0:T(8,128)(2,1)S(1)}, bf16[2,512,256]{2,1,0:T(8,128)(2,1)}, u32[]{:S(2)}) copy-start(bf16[2,512,256]{2,1,0:T(8,128)(2,1)} %get-tuple-element.102) | copy-start | bytes 1572868
  78.5 17.9 %copy-start.7 = (f32[512,1]{1,0:T(8,128)S(1)}, f32[512,1]{1,0:T(8,128)}, u32[]{:S(2)}) copy-start(f32[512,1]{1,0:T(8,128)} %copy-done.6) | copy-start | bytes 6148
  88.9 7.5 %collective-permute-start.17 = (bf16[4,1024,512]{2,1,0:T(8,128)(2,1)}, bf16[4,1024,512]{2,1,0:T(8,128)(2,1)}, u32[]{:S(2)}, u32[]{:S(2)}) collective-permute-start(bf16[4,1024,512]{2,1,0:T(8,128)(2,1)} %get-tuple-element.129.weight_ref), channel_id=1, source_target_pairs={{0,4},{4,0},{1,5},{5,1},{2,6},{6,2},{3,7},{7,3},{8,12},{12,8},{9,1... | collective-permute-start | bytes 12582920 | tf_op jit(solution)/shard_map/ppermute | solution.py:24
  89.9 15.1 %collective-permute-start.21 = (bf16[512,256]{1,0:T(8,128)(2,1)S(1)}, bf16[512,256]{1,0:T(8,128)(2,1)}, u32[]{:S(2)}, u32[]{:S(2)}) collective-permute-start(bf16[512,256]{1,0:T(8,128)(2,1)S(1)} %fusion.6), channel_id=1, source_target_pairs={{0,8},{8,0},{1,9},{9,1},{2,10},{10,2},{3,11},{11,3},{4,12},{12,4},... | collective-permute-start | bytes 786440 | tf_op jit(solution)/shard_map/ppermute | solution.py:24
  93.2 11.9 %collective-permute-start.20 = (bf16[512,256]{1,0:T(8,128)(2,1)}, bf16[512,256]{1,0:T(8,128)(2,1)}, u32[]{:S(2)}, u32[]{:S(2)}) collective-permute-start(bf16[512,256]{1,0:T(8,128)(2,1)} %fusion.5), channel_id=1, source_target_pairs={{0,16},{16,0},{1,17},{17,1},{2,18},{18,2},{3,19},{19,3},{4,20},{20... | collective-permute-start | bytes 786440 | tf_op jit(solution)/shard_map/ppermute | solution.py:24
  93.3 16.7 %collective-permute-start.18 = (bf16[2,512,256]{2,1,0:T(8,128)(2,1)}, bf16[2,512,256]{2,1,0:T(8,128)(2,1)S(1)}, u32[]{:S(2)}, u32[]{:S(2)}) collective-permute-start(bf16[2,512,256]{2,1,0:T(8,128)(2,1)} %get-tuple-element.135), channel_id=1, source_target_pairs={{0,8},{8,0},{1,9},{9,1},{2,10},{10,2},{3,11},{11,3},{4,12},{12,4},... | collective-permute-start | bytes 1572872 | tf_op jit(solution)/shard_map/ppermute | solution.py:24
  93.8 19.2 %collective-permute-start.19 = (bf16[2,512,256]{2,1,0:T(8,128)(2,1)}, bf16[2,512,256]{2,1,0:T(8,128)(2,1)S(1)}, u32[]{:S(2)}, u32[]{:S(2)}) collective-permute-start(bf16[2,512,256]{2,1,0:T(8,128)(2,1)} %get-tuple-element.136), channel_id=1, source_target_pairs={{0,16},{16,0},{1,17},{17,1},{2,18},{18,2},{3,19},{19,3},{4,20},{20... | collective-permute-start | bytes 1572872 | tf_op jit(solution)/shard_map/ppermute | solution.py:24
  97.6 15.4 %copy-start.14 = (bf16[2,512,256]{2,1,0:T(8,128)(2,1)S(1)}, bf16[2,512,256]{2,1,0:T(8,128)(2,1)}, u32[]{:S(2)}) copy-start(bf16[2,512,256]{2,1,0:T(8,128)(2,1)} %get-tuple-element.144) | copy-start | bytes 1572868
  97.6 16.1 %copy-start.13 = (bf16[2,512,256]{2,1,0:T(8,128)(2,1)S(1)}, bf16[2,512,256]{2,1,0:T(8,128)(2,1)}, u32[]{:S(2)}) copy-start(bf16[2,512,256]{2,1,0:T(8,128)(2,1)} %get-tuple-element.134) | copy-start | bytes 1572868
  113.1 12.8 %collective-permute-start.23 = (bf16[512,256]{1,0:T(8,128)(2,1)S(1)}, bf16[512,256]{1,0:T(8,128)(2,1)S(1)}, u32[]{:S(2)}, u32[]{:S(2)}) collective-permute-start(bf16[512,256]{1,0:T(8,128)(2,1)S(1)} %fusion.8), channel_id=1, source_target_pairs={{0,8},{8,0},{1,9},{9,1},{2,10},{10,2},{3,11},{11,3},{4,12},{12,4},... | collective-permute-start | bytes 786440 | tf_op jit(solution)/shard_map/ppermute | solution.py:24
  113.8 12.0 %collective-permute-start.22 = (bf16[512,256]{1,0:T(8,128)(2,1)S(1)}, bf16[512,256]{1,0:T(8,128)(2,1)S(1)}, u32[]{:S(2)}, u32[]{:S(2)}) collective-permute-start(bf16[512,256]{1,0:T(8,128)(2,1)S(1)} %fusion.7), channel_id=1, source_target_pairs={{0,16},{16,0},{1,17},{17,1},{2,18},{18,2},{3,19},{19,3},{4,20},{20... | collective-permute-start | bytes 786440 | tf_op jit(solution)/shard_map/ppermute | solution.py:24
  114.2 20.1 %collective-permute-start.24 = (bf16[512,256]{1,0:T(8,128)(2,1)S(1)}, bf16[512,256]{1,0:T(8,128)(2,1)S(1)}, u32[]{:S(2)}, u32[]{:S(2)}) collective-permute-start(bf16[512,256]{1,0:T(8,128)(2,1)S(1)} %bitcast_add_fusion.2), channel_id=1, source_target_pairs={{0,3},{1,0},{2,1},{3,2},{4,7},{5,4},{6,5},{7,6},{8,11},{9,8},{10,9... | collective-permute-start | bytes 786440 | tf_op jit(solution)/shard_map/ppermute | solution.py:24
  118.2 20.4 %collective-permute-start.25 = (bf16[512,256]{1,0:T(8,128)(2,1)S(1)}, bf16[512,256]{1,0:T(8,128)(2,1)S(1)}, u32[]{:S(2)}, u32[]{:S(2)}) collective-permute-start(bf16[512,256]{1,0:T(8,128)(2,1)S(1)} %bitcast_add_fusion.3), channel_id=1, source_target_pairs={{0,2},{1,3},{2,0},{3,1},{4,6},{5,7},{6,4},{7,5},{8,10},{9,11},{10,... | collective-permute-start | bytes 786440 | tf_op jit(solution)/shard_map/ppermute | solution.py:24
  126.0 12.6 %collective-permute-start.26 = (bf16[512,256]{1,0:T(8,128)(2,1)S(1)}, bf16[512,256]{1,0:T(8,128)(2,1)S(1)}, u32[]{:S(2)}, u32[]{:S(2)}) collective-permute-start(bf16[512,256]{1,0:T(8,128)(2,1)S(1)} %fusion.1), channel_id=1, source_target_pairs={{0,1},{1,2},{2,3},{3,0},{4,5},{5,6},{6,7},{7,4},{8,9},{9,10},{10,1... | collective-permute-start | bytes 786440 | tf_op jit(solution)/shard_map/ppermute | solution.py:24
  (12 other events, 96.1 us)

commit v8 on v7

--- a/solution.py
+++ b/solution.py
@@ -33,12 +33,23 @@
     return pltpu.with_memory_space_constraint(array, pltpu.HBM)
 
 
+def in_vmem(array):
+    return pltpu.with_memory_space_constraint(array, pltpu.VMEM)
+
+
 def after(value, *earlier):
     return lax.optimization_barrier((value, earlier))[0]
 
 
 def widen(parts):
     return functools.reduce(jnp.add, [part.astype(F32) for part in parts])
+
+
+def chunk_shifts(tp_count):
+    shifts = [0]
+    for step in range(1, tp_count // 2 + 1):
+        shifts += [step] if 2 * step == tp_count else [step, tp_count - step]
+    return shifts
 
 
 def inner_first(chunk):
@@ -73,7 +84,7 @@
         ),
         cost_estimate=NOMINAL,
         compiler_params=pltpu.CompilerParams(vmem_limit_bytes=PAIR_VMEM),
-    )(places, cot_t, *[in_hbm(residual)] * slots)
+    )(places, cot_t, *[in_vmem(residual)] * slots)
 
 
 def ours_kernel(places_ref, cot_ref, first_ref, second_ref, other_ref, *outs):
@@ -121,7 +132,7 @@
         ),
         cost_estimate=NOMINAL,
         compiler_params=pltpu.CompilerParams(vmem_limit_bytes=PAIR_VMEM),
-    )(places, cot_t, in_hbm(residual), in_hbm(residual), other)
+    )(places, cot_t, in_vmem(residual), in_vmem(residual), other)
 
 
 def place_weight(inner_flags, offsets_ref, pieces, weight_ref):
@@ -206,10 +217,10 @@
     rows, features = pieces[0].shape[1:]
     steps = places.shape[0]
     depth = width // (CORES * steps)
-    total = pltpu.HBM((tokens, features), F32)
+    total = jax.ShapeDtypeStruct((tokens, features), F32)
     return pl.pallas_call(
         functools.partial(value_kernel, inner_flags),
-        out_shape=[total, pltpu.HBM((steps, depth, features), BF16)],
+        out_shape=[total, pltpu.VMEM((steps, depth, features), BF16)],
         grid_spec=pltpu.PrefetchScalarGridSpec(
             num_scalar_prefetch=2,
             grid=(steps,),
@@ -222,7 +233,7 @@
         ),
         cost_estimate=NOMINAL,
         compiler_params=pltpu.CompilerParams(vmem_limit_bytes=WEIGHT_VMEM),
-    )(places, offsets, in_hbm(residual), *pieces)
+    )(places, offsets, in_vmem(residual), *pieces)
 
 
 def weight_call(kernel, places, residual, weight, wholes, out_shape, earlier=None):
@@ -238,7 +249,7 @@
         pl.BlockSpec((tokens, depth), lambda i, p: (0, p[i])),
         pl.BlockSpec((1, depth, features), lambda i, p: (p[i] // CORES, 0, 0)),
     ] + [whole_block(array) for array in wholes]
-    operands = [places, in_hbm(residual), weight, *wholes]
+    operands = [places, in_vmem(residual), in_vmem(weight), *wholes]
     aliases = {}
     if earlier is not None:
         aliases = {len(operands): 0}
@@ -260,20 +271,23 @@
     )(*operands)
 
 
-def squares_kernel(resid_ref, out_ref):
-    wide = resid_ref[...].astype(F32)
+def squares_kernel(resid_ref, out_ref, kept_ref):
+    block = resid_ref[...]
+    kept_ref[...] = block
+    wide = block.astype(F32)
     out_ref[...] = jnp.sum(wide * wide, axis=1, keepdims=True)
 
 
 def row_squares(residual):
     tokens, width = residual.shape
     rows = 64
+    block = pl.BlockSpec((rows, width), lambda i: (i, 0))
     return pl.pallas_call(
         squares_kernel,
-        out_shape=jax.ShapeDtypeStruct((tokens, 1), F32),
+        out_shape=[jax.ShapeDtypeStruct((tokens, 1), F32), pltpu.VMEM((tokens, width), BF16)],
         grid=(tokens // rows,),
-        in_specs=[pl.BlockSpec((rows, width), lambda i: (i, 0))],
-        out_specs=pl.BlockSpec((rows, 1), lambda i: (i, 0)),
+        in_specs=[block],
+        out_specs=[pl.BlockSpec((rows, 1), lambda i: (i, 0)), block],
         cost_estimate=NOMINAL,
         compiler_params=pltpu.CompilerParams(vmem_limit_bytes=PAIR_VMEM),
     )(in_hbm(residual))
@@ -364,11 +378,21 @@
     depth = width // rep_count
     rows = depth // tp_count
     order = list(range(tp_count))
+    shifts = chunk_shifts(tp_count)
     in_place = rows % 128 == 0 and outer == 2 and inner == 2
 
+    owned = jnp.where(
+        target_ids // (VOCAB // tp_count) == tp_place,
+        ref_target_logit[0],
+        jnp.zeros_like(ref_target_logit[0]),
+    )
+    packed = jnp.concatenate([ref_shard_max[0], ref_shard_sum[0], owned, trainee_logp])
+    packed = packed.reshape(1, -1, 128)
+    packed = jnp.concatenate([packed, trade(packed, "tp", 1)])
+
     gained = (value_weight.astype(F32) * norm_gain.astype(F32)[:, None]).astype(BF16)
-    residual, gained = lax.optimization_barrier((residual, gained))
-    squares = row_squares(residual)
+    residual, gained, packed = lax.optimization_barrier((residual, gained, packed))
+    squares, residual = row_squares(residual)
 
     def near_of(k, block):
         first = "inner" if inner_first(k) else "outer"
@@ -379,31 +403,23 @@
         near = jnp.stack([block] + nears)
         return [near] + [swap(near, second, s) for s in range(1, lax.axis_size(second))]
 
-    owned = jnp.where(
-        target_ids // (VOCAB // tp_count) == tp_place,
-        ref_target_logit[0],
-        jnp.zeros_like(ref_target_logit[0]),
-    )
-    packed = jnp.concatenate([ref_shard_max[0], ref_shard_sum[0], owned, trainee_logp])
-    packed = packed.reshape(1, -1, 128)
-    own_pieces, near = {}, {}
-    arrived = {0: gained, 1: trade(gained, "tp", 1), 2: trade(gained, "tp", 2)}
-    near[0] = near_of(0, gained)
-    packed = jnp.concatenate([packed, trade(packed, "tp", 1)])
-    arrived[1], near[0], packed, squares, late_gained = lax.optimization_barrier(
-        (arrived[1], near[0], packed, squares, gained)
-    )
-    near[1] = near_of(1, arrived[1])
-    for k in order[3:]:
-        arrived[k] = trade(late_gained, "tp", k)
     mask = 2
     while mask < tp_count:
         packed = jnp.concatenate([packed, trade(packed, "tp", mask)])
         mask *= 2
-    near[1], arrived[2], packed = lax.optimization_barrier((near[1], arrived[2], packed))
+    own_pieces, near = {}, {}
+    arrived = {0: gained, 1: swap(gained, "tp", shifts[1])}
+    near[0] = near_of(0, gained)
+    arrived[1], near[0], packed, squares, late_gained = lax.optimization_barrier(
+        (arrived[1], near[0], packed, squares, gained)
+    )
+    near[1] = near_of(1, arrived[1])
+    arrived[2] = swap(late_gained, "tp", shifts[2])
+    own_pieces[0] = far_of(0, gained, near[0])
+    near[1], packed, late_gained = lax.optimization_barrier((near[1], packed, late_gained))
+    for k in order[3:]:
+        arrived[k] = swap(late_gained, "tp", shifts[k])
     own_pieces[1] = far_of(1, arrived[1], near[1])
-    near[2] = near_of(2, arrived[2])
-    own_pieces[0] = far_of(0, gained, near[0])
     seq_length = lax.dynamic_index_in_dim(lengths, rep_place, keepdims=False)
     info = jnp.stack([tp_place, seq_length]).astype(jnp.int32)
     cot, cot_t, inv_rms = scaled_cot(width, rep_count, info, packed, squares, value_cot)
@@ -467,18 +483,19 @@
         return [for_other(part, cot_t)]
 
     theirs = for_others(pairs[0], cot_t)
+    theirs, arrived[2] = lax.optimization_barrier((theirs, arrived[2]))
+    near[2] = near_of(2, arrived[2])
+    for pair in pairs[1:]:
+        theirs += for_others(pair, after(cot_t, theirs))
     theirs, arrived[3] = lax.optimization_barrier((theirs, arrived[3]))
     near[3] = near_of(3, arrived[3])
-    for pair in pairs[1:]:
-        theirs += for_others(pair, after(cot_t, theirs))
     near[2], near[3], theirs, own_pieces[0], own_pieces[1] = lax.optimization_barrier(
         (near[2], near[3], theirs, own_pieces[0], own_pieces[1])
     )
     others = [swap(part, "core", 1) for part in theirs]
     own_pieces[2] = far_of(2, arrived[2], near[2])
+    own_pieces[3] = far_of(3, arrived[3], near[3])
     sides = [for_us(pairs[0], others[0])]
-    near[3], sides[0] = lax.optimization_barrier((near[3], sides[0]))
-    own_pieces[3] = far_of(3, arrived[3], near[3])
     got = [first_round(sides[0])]
     sides.append(for_us(pairs[1], after(others[1], sides[0])))
     for n in range(2, len(pairs)):
@@ -494,14 +511,16 @@
             jnp.stack([place_of(o, i, c, 0) // tp_count for o, i in chips]).astype(jnp.int32)
             for c in (core, 1 - core)
         ]
-        offsets = jnp.stack([jnp.bitwise_xor(tp_place, k) * rows for k in order]).astype(jnp.int32)
+        offsets = jnp.stack([lax.rem(tp_place - shift + tp_count, tp_count) * rows for shift in shifts])
+        offsets = offsets.astype(jnp.int32)
         total, own_weight = first_value(flags, places[0], offsets, residual, pieces)
     else:
         weight = []
         for k in order:
             both = jnp.stack(own_pieces[k])
             weight.append(both if inner_first(k) else jnp.swapaxes(both, 0, 1))
-        weight = jnp.stack(weight)[jnp.bitwise_xor(tp_place, jnp.arange(tp_count))]
+        by_shift = jnp.array([shifts.index(shift) for shift in range(tp_count)])
+        weight = jnp.stack(weight)[by_shift[(tp_place - jnp.arange(tp_count)) % tp_count]]
         weight = weight[:, (at_outer - jnp.arange(outer)) % outer]
         weight = weight[:, :, (at_inner - jnp.arange(inner)) % inner]
         own_weight = weight.transpose(1, 2, 0, 3, 4).reshape(outer * inner, depth, features)
@@ -539,7 +558,7 @@
     if in_place:
         grad_shape = jax.ShapeDtypeStruct((rows_here, width), BF16)
         resid_grad = weight_call(
-            grad_kernel, places[0], residual, in_hbm(own_weight), [cot, coefficient], grad_shape
+            grad_kernel, places[0], residual, own_weight, [cot, coefficient], grad_shape
         )
         later[1], coefficient, resid_grad = lax.optimization_barrier((later[1], coefficient, resid_grad))
     else:

time: 142 us -> 147 us (1.035)
  local copies, waits for them, and re-layouts: 5.16 us -> 25.4 us
  waiting for transfers between devices: 29.2 us -> 16.8 us
  Pallas kernels: 60.5 us -> 54.9 us
  starting transfers between devices: 30.8 us -> 33.2 us
    unnamed x35 -> x51, local copies, waits for them, and re-layouts: 4.11 us -> 24.3 us
    ppermute x22 -> x25, starting transfers between devices: 20.8 us -> 27.6 us  [swap(): lax.ppermute(value, axis, [(place, (place + step) % size) for place in ra...]
    ppermute x5 -> x2, waiting for transfers between devices: 6.72 us -> 0.01 us  [trade(): lax.ppermute(value, axis, [(place, place ^ mask) for place in range(size)])]
    ppermute x22 -> x25, waiting for transfers between devices: 22.5 us -> 16.7 us  [swap(): lax.ppermute(value, axis, [(place, (place + step) % size) for place in ra...]
    ppermute x5 -> x2, starting transfers between devices: 10 us -> 5.61 us  [trade(): lax.ppermute(value, axis, [(place, place ^ mask) for place in range(size)])]
    pallas_call x2, Pallas kernels: 10.3 us -> 7.56 us  [theirs_product(): pl.pallas_call(theirs_kernel, out_shape=[pltpu.HBM((2, steps, features, r...]
    pallas_call x3, Pallas kernels: 22.8 us -> 20.6 us  [weight_call(): pl.pallas_call(kernel, out_shape=out_shape, grid_spec=pltpu.PrefetchScala...]
  transfers between devices with their start and end apart: 27 -> 27, of which waited for: 8 -> 5; matrix products, arithmetic and copies ran while one was open for 8% -> 9% of each run, Pallas kernels for 43% -> 38%
where the time goes in v8:
time: 147 us; the launch traced here: 146 us
  Pallas kernels  54.9 us (37%)
  starting transfers between devices  33.2 us (23%)
  local copies, waits for them, and re-layouts  25.4 us (17%)
  waiting for transfers between devices  16.8 us (11%)
  other arithmetic  14.7 us (10%)
    ppermute x25, starting transfers between devices, swap(): lax.ppermute(value, axis, [(place, (place + step) % size) for place in ra...  27.6 us
    unnamed x51, local copies, waits for them, and re-layouts  24.3 us
    pallas_call x3, Pallas kernels, weight_call(): pl.pallas_call(kernel, out_shape=out_shape, grid_spec=pltpu.PrefetchScala...  20.6 us
    ppermute x25, waiting for transfers between devices, swap(): lax.ppermute(value, axis, [(place, (place + step) % size) for place in ra...  16.7 us
    pallas_call x2, Pallas kernels, ours_product(): pl.pallas_call(ours_kernel, out_shape=[pltpu.HBM((2, features, rows), BF1...  12 us
    pallas_call x2, Pallas kernels, theirs_product(): pl.pallas_call(theirs_kernel, out_shape=[pltpu.HBM((2, steps, features, r...  7.56 us
    pallas_call x1, Pallas kernels, row_squares(): pl.pallas_call(squares_kernel, out_shape=[jax.ShapeDtypeStruct((tokens, 1...  6.93 us
    pallas_call x1, Pallas kernels, first_value(): pl.pallas_call(functools.partial(value_kernel, inner_flags), out_shape=[t...  6.78 us
  transfers between devices with their start and end apart: 27, of which 5 were waited for; matrix products, arithmetic and copies ran while one was open for 9% of the time, Pallas kernels for 38%

profile of v8, /device:TPU:0, one launch (start us, length us, event | category | flops | bytes accessed | tf_op | source)
XLA Modules:
  0.0 146.0 jit_solution(7409390397259055246)
XLA Ops:
  2.1 3.0 %collective-permute-start = (f32[1,52,128]{2,1,0:T(8,128)S(1)}, f32[1,52,128]{2,1,0:T(8,128)S(1)}, u32[]{:S(2)}, u32[]{:S(2)}) collective-permute-start(f32[1,52,128]{2,1,0:T(8,128)S(1)} %maximum_bitcast_fusion), channel_id=1, source_target_pairs={{0,1},{1,0},{2,3},{3,2},{4,5},{5,4},{6,7},{7,6},{8,9},{9,8},{10,11... | collective-permute-start | bytes 79880 | tf_op jit(solution)/shard_map/ppermute | solution.py:29
  5.8 1.8 %multiply_convert_fusion = bf16[256,512]{1,0:T(8,128)(2,1)} fusion(bf16[256,512]{1,0:T(8,128)(2,1)} %param.12, f32[256]{0:T(256)S(1)} %convert_element_type.132), kind=kLoop, calls=%fused_computation.19 | loop fusion | flops 393216 | bytes 525312 | tf_op jit(solution)/shard_map/convert_element_type | solution.py:393
  7.6 1.5 %collective-permute-start.1 = (bf16[256,512]{1,0:T(8,128)(2,1)}, bf16[256,512]{1,0:T(8,128)(2,1)S(1)}, u32[]{:S(2)}, u32[]{:S(2)}) collective-permute-start(bf16[256,512]{1,0:T(8,128)(2,1)} %multiply_convert_fusion), channel_id=1, source_target_pairs={{0,1},{1,2},{2,3},{3,0},{4,5},{5,6},{6,7},{7,4},{8,9},{9,10},{10,1... | collective-permute-start | bytes 786440 | tf_op jit(solution)/shard_map/ppermute | solution.py:24
  10.6 2.6 %collective-permute-start.3 = (f32[2,52,128]{2,1,0:T(8,128)S(1)}, f32[2,52,128]{2,1,0:T(8,128)S(1)}, u32[]{:S(2)}, u32[]{:S(2)}) collective-permute-start(f32[2,52,128]{2,1,0:T(8,128)S(1)} %pad_maximum_fusion.5), channel_id=1, source_target_pairs={{0,2},{1,3},{2,0},{3,1},{4,6},{5,7},{6,4},{7,5},{8,10},{9,11},{10,... | collective-permute-start | bytes 159752 | tf_op jit(solution)/shard_map/ppermute | solution.py:29
  13.1 6.9 %shard_map.129 = (f32[512,1]{1,0:T(8,128)S(1)}, bf16[512,8192]{1,0:T(8,128)(2,1)S(1)}) custom-call(bf16[512,8192]{1,0:T(8,128)(2,1)} %resid_ref), custom_call_target="tpu_custom_call" | custom-call | flops 1024 | bytes 1024 | tf_op jit(solution)/shard_map/pallas_call | solution.py:285
  20.1 3.4 %copy-done = bf16[512,8192]{1,0:T(8,128)(2,1)} copy-done((bf16[512,8192]{1,0:T(8,128)(2,1)}, bf16[512,8192]{1,0:T(8,128)(2,1)S(1)}, u32[]{:S(2)}) %copy-start) | copy-done | bytes 8388632
  23.5 1.6 %collective-permute-start.4 = (bf16[256,512]{1,0:T(8,128)(2,1)S(1)}, bf16[256,512]{1,0:T(8,128)(2,1)S(1)}, u32[]{:S(2)}, u32[]{:S(2)}) collective-permute-start(bf16[256,512]{1,0:T(8,128)(2,1)S(1)} %collective-permute-done.1), channel_id=1, source_target_pairs={{0,16},{16,0},{1,17},{17,1},{2,18},{18,2},{3,19},{19,3},{4,20},{20... | collective-permute-start | bytes 786440 | tf_op jit(solution)/shard_map/ppermute | solution.py:24
  28.2 3.3 %collective-permute-done.4 = bf16[256,512]{1,0:T(8,128)(2,1)S(1)} collective-permute-done((bf16[256,512]{1,0:T(8,128)(2,1)S(1)}, bf16[256,512]{1,0:T(8,128)(2,1)S(1)}, u32[]{:S(2)}, u32[]{:S(2)}) %collective-permute-start.4) | collective-permute-done | bytes 262176 | tf_op jit(solution)/shard_map/ppermute | solution.py:24
  37.0 3.4 %copy-done.1 = bf16[512,8192]{1,0:T(8,128)(2,1)S(1)} copy-done((bf16[512,8192]{1,0:T(8,128)(2,1)S(1)}, bf16[512,8192]{1,0:T(8,128)(2,1)}, u32[]{:S(2)}) %copy-start.1) | copy-done | bytes 8388632
  40.4 3.8 %shard_map.131 = bf16[2,4,512,256]{3,2,1,0:T(8,128)(2,1)} custom-call(s32[8]{0:T(128)S(1)} %stack.220.places_ref, bf16[512,512]{1,0:T(8,128)(2,1)S(1)} %get-tuple-element.93.cot_ref, bf16[512,8192]{1,0:T(8,128)(2,1)S(1)} %copy-done.1, bf16[512,8192]{1,0:T(8,128)(2,1)S(1)} %copy-done.1), custom_call_target="tpu_custom_call" | custom-call | flops 1024 | bytes 1024 | tf_op jit(solution)/shard_map/pallas_call | solution.py:72
  44.2 1.5 %collective-permute-start.6 = (bf16[256,512]{1,0:T(8,128)(2,1)}, bf16[256,512]{1,0:T(8,128)(2,1)S(1)}, u32[]{:S(2)}, u32[]{:S(2)}) collective-permute-start(bf16[256,512]{1,0:T(8,128)(2,1)} %collective-permute-done.5), channel_id=1, source_target_pairs={{0,8},{8,0},{1,9},{9,1},{2,10},{10,2},{3,11},{11,3},{4,12},{12,4},... | collective-permute-start | bytes 786440 | tf_op jit(solution)/shard_map/ppermute | solution.py:24
  45.7 3.8 %shard_map.132 = bf16[2,4,512,256]{3,2,1,0:T(8,128)(2,1)} custom-call(s32[8]{0:T(128)S(1)} %stack.229.places_ref, bf16[512,512]{1,0:T(8,128)(2,1)S(1)} %get-tuple-element.93.cot_ref, bf16[512,8192]{1,0:T(8,128)(2,1)S(1)} %copy-done.1, bf16[512,8192]{1,0:T(8,128)(2,1)S(1)} %copy-done.1), custom_call_target="tpu_custom_call" | custom-call | flops 1024 | bytes 1024 | tf_op jit(solution)/shard_map/pallas_call | solution.py:72
  49.5 2.5 %collective-permute-start.8 = (bf16[256,512]{1,0:T(8,128)(2,1)}, bf16[256,512]{1,0:T(8,128)(2,1)S(1)}, u32[]{:S(2)}, u32[]{:S(2)}) collective-permute-start(bf16[256,512]{1,0:T(8,128)(2,1)} %collective-permute-done.7), channel_id=1, source_target_pairs={{0,16},{16,0},{1,17},{17,1},{2,18},{18,2},{3,19},{19,3},{4,20},{20... | collective-permute-start | bytes 786440 | tf_op jit(solution)/shard_map/ppermute | solution.py:24
  53.5 3.1 %collective-permute-done.8 = bf16[256,512]{1,0:T(8,128)(2,1)S(1)} collective-permute-done((bf16[256,512]{1,0:T(8,128)(2,1)}, bf16[256,512]{1,0:T(8,128)(2,1)S(1)}, u32[]{:S(2)}, u32[]{:S(2)}) %collective-permute-start.8) | collective-permute-done | bytes 262176 | tf_op jit(solution)/shard_map/ppermute | solution.py:24
  60.5 2.1 %collective-permute-start.15 = (bf16[2,256,512]{2,1,0:T(8,128)(2,1)S(1)}, bf16[2,256,512]{2,1,0:T(8,128)(2,1)}, u32[]{:S(2)}, u32[]{:S(2)}) collective-permute-start(bf16[2,256,512]{2,1,0:T(8,128)(2,1)S(1)} %pad_maximum_fusion.2.rest_4_), channel_id=1, source_target_pairs={{0,16},{16,0},{1,17},{17,1},{2,18},{18,2},{3,19},{19,3},{4,20},{20... | collective-permute-start | bytes 1572872 | tf_op jit(solution)/shard_map/ppermute | solution.py:24
  62.7 3.4 %copy-done.2 = bf16[512,8192]{1,0:T(8,128)(2,1)S(1)} copy-done((bf16[512,8192]{1,0:T(8,128)(2,1)S(1)}, bf16[512,8192]{1,0:T(8,128)(2,1)}, u32[]{:S(2)}) %copy-start.2) | copy-done | bytes 8388632
  66.0 5.7 %shard_map.133 = (bf16[2,512,256]{2,1,0:T(8,128)(2,1)}, bf16[2,512,256]{2,1,0:T(8,128)(2,1)}, bf16[2,512,256]{2,1,0:T(8,128)(2,1)}, bf16[2,512,256]{2,1,0:T(8,128)(2,1)}) custom-call(s32[8]{0:T(128)S(1)} %stack.209.places_ref, bf16[512,512]{1,0:T(8,128)(2,1)S(1)} %get-tuple-element.93.cot_ref, bf16[512,8192]{1,0:T(8,128)(2,1)S(1)} %copy-done.2, ...), custom_call_target="tpu_custom_call" | custom-call | flops 1024 | bytes 1024 | tf_op jit(solution)/shard_map/pallas_call | solution.py:116
  71.7 1.5 %collective-permute-start.12 = (bf16[2,512,256]{2,1,0:T(8,128)(2,1)}, bf16[2,512,256]{2,1,0:T(8,128)(2,1)}, u32[]{:S(2)}, u32[]{:S(2)}) collective-permute-start(bf16[2,512,256]{2,1,0:T(8,128)(2,1)} %get-tuple-element.101), channel_id=1, source_target_pairs={{0,8},{8,0},{1,9},{9,1},{2,10},{10,2},{3,11},{11,3},{4,12},{12,4},... | collective-permute-start | bytes 1572872 | tf_op jit(solution)/shard_map/ppermute | solution.py:24
  73.5 3.4 %copy-done.3 = bf16[512,8192]{1,0:T(8,128)(2,1)S(1)} copy-done((bf16[512,8192]{1,0:T(8,128)(2,1)S(1)}, bf16[512,8192]{1,0:T(8,128)(2,1)}, u32[]{:S(2)}) %copy-start.3) | copy-done | bytes 8388632
  76.9 6.4 %shard_map.134 = (bf16[2,512,256]{2,1,0:T(8,128)(2,1)}, bf16[2,512,256]{2,1,0:T(8,128)(2,1)}, bf16[2,512,256]{2,1,0:T(8,128)(2,1)}, bf16[2,512,256]{2,1,0:T(8,128)(2,1)}) custom-call(s32[8]{0:T(128)S(1)} %stack.244.places_ref, bf16[512,512]{1,0:T(8,128)(2,1)S(1)} %get-tuple-element.93.cot_ref, bf16[512,8192]{1,0:T(8,128)(2,1)S(1)} %copy-done.3, ...), custom_call_target="tpu_custom_call" | custom-call | flops 1024 | bytes 1024 | tf_op jit(solution)/shard_map/pallas_call | solution.py:116
  83.3 6.8 %shard_map.135 = (f32[512,512]{1,0:T(8,128)S(1)}, bf16[4,1024,512]{2,1,0:T(8,128)(2,1)}) custom-call(s32[4]{0:T(128)S(1)} %get-tuple-element.162.places_ref, s32[4]{0:T(128)S(1)} %get-tuple-element.163.offsets_ref, bf16[512,8192]{1,0:T(8,128)(2,1)S(1)} %copy-done.4, bf16[2,256,512]{2,1,0:T(8,128)(2,1)S(1)} %pad_maximum_fusion.rest_0_, ...), custom_call_target="tpu_custom_call" | custom-call | flops 1024 | bytes 1024 | tf_op jit(solution)/shard_map/pallas_call | solution.py:221
  91.0 1.7 %fusion.6 = bf16[512,256]{1,0:T(8,128)(2,1)} fusion(bf16[2,512,256]{2,1,0:T(8,128)(2,1)} %collective-permute-done.13, bf16[2,512,256]{2,1,0:T(8,128)(2,1)S(1)} %copy-done.16), kind=kLoop, calls=%fused_computation.21 | loop fusion | flops 524288 | bytes 786432 | tf_op jit(solution)/shard_map/convert_element_type | solution.py:466
  92.8 1.5 %collective-permute-start.21 = (bf16[512,256]{1,0:T(8,128)(2,1)}, bf16[512,256]{1,0:T(8,128)(2,1)}, u32[]{:S(2)}, u32[]{:S(2)}) collective-permute-start(bf16[512,256]{1,0:T(8,128)(2,1)} %fusion.6), channel_id=1, source_target_pairs={{0,8},{8,0},{1,9},{9,1},{2,10},{10,2},{3,11},{11,3},{4,12},{12,4},... | collective-permute-start | bytes 786440 | tf_op jit(solution)/shard_map/ppermute | solution.py:24
  94.3 1.7 %fusion.5 = bf16[512,256]{1,0:T(8,128)(2,1)} fusion(bf16[2,512,256]{2,1,0:T(8,128)(2,1)} %collective-permute-done.12, bf16[2,512,256]{2,1,0:T(8,128)(2,1)S(1)} %copy-done.17), kind=kLoop, calls=%fused_computation.20 | loop fusion | flops 524288 | bytes 786432 | tf_op jit(solution)/shard_map/convert_element_type | solution.py:466
  98.6 3.4 %copy-done.5 = bf16[512,8192]{1,0:T(8,128)(2,1)S(1)} copy-done((bf16[512,8192]{1,0:T(8,128)(2,1)S(1)}, bf16[512,8192]{1,0:T(8,128)(2,1)}, u32[]{:S(2)}) %copy-start.5) | copy-done | bytes 8388632
  103.2 6.9 %shard_map.136 = (bf16[512,512]{1,0:T(8,128)(2,1)}, f32[512,1]{1,0:T(8,128)S(1)}) custom-call(s32[4]{0:T(128)S(1)} %pad_add_fusion.places_ref, bf16[512,8192]{1,0:T(8,128)(2,1)S(1)} %copy-done.5, bf16[4,1024,512]{2,1,0:T(8,128)(2,1)} %collective-permute-done.17.weight_ref, f32[512,512]{1,0:T(8,128)S(1)} %copy-done.7, ...), custom_call_target="tpu_custom_call" | custom-call | flops 1024 | bytes 1024 | tf_op jit(solution)/shard_map/pallas_call | solution.py:258
  112.9 2.9 %collective-permute-done.19 = bf16[2,512,256]{2,1,0:T(8,128)(2,1)S(1)} collective-permute-done((bf16[2,512,256]{2,1,0:T(8,128)(2,1)}, bf16[2,512,256]{2,1,0:T(8,128)(2,1)S(1)}, u32[]{:S(2)}, u32[]{:S(2)}) %collective-permute-start.19) | collective-permute-done | bytes 524320 | tf_op jit(solution)/shard_map/ppermute | solution.py:24
  116.8 1.8 %collective-permute-start.22 = (bf16[512,256]{1,0:T(8,128)(2,1)S(1)}, bf16[512,256]{1,0:T(8,128)(2,1)S(1)}, u32[]{:S(2)}, u32[]{:S(2)}) collective-permute-start(bf16[512,256]{1,0:T(8,128)(2,1)S(1)} %fusion.7), channel_id=1, source_target_pairs={{0,16},{16,0},{1,17},{17,1},{2,18},{18,2},{3,19},{19,3},{4,20},{20... | collective-permute-start | bytes 786440 | tf_op jit(solution)/shard_map/ppermute | solution.py:24
  118.6 2.7 %collective-permute-start.24 = (bf16[512,256]{1,0:T(8,128)(2,1)S(1)}, bf16[512,256]{1,0:T(8,128)(2,1)S(1)}, u32[]{:S(2)}, u32[]{:S(2)}) collective-permute-start(bf16[512,256]{1,0:T(8,128)(2,1)S(1)} %bitcast_add_fusion.2), channel_id=1, source_target_pairs={{0,3},{1,0},{2,1},{3,2},{4,7},{5,4},{6,5},{7,6},{8,11},{9,8},{10,9... | collective-permute-start | bytes 786440 | tf_op jit(solution)/shard_map/ppermute | solution.py:24
  122.1 6.9 %shard_map.137.rest_0_ = bf16[512,8192]{1,0:T(8,128)(2,1)} custom-call(s32[4]{0:T(128)S(1)} %get-tuple-element.162.places_ref, bf16[512,8192]{1,0:T(8,128)(2,1)S(1)} %copy-done.5, bf16[4,1024,512]{2,1,0:T(8,128)(2,1)} %get-tuple-element.131.weight_ref, bf16[512,512]{1,0:T(8,128)(2,1)S(1)} %get-tuple-element.133.cot_ref, f32[512,1]{1,0:T(8,128)S(1)} %get-tuple-element.149.coef_ref), custom_call_target="tpu_custom_call" | custom-call | flops 1024 | bytes 1024 | tf_op jit(solution)/shard_map/pallas_call | solution.py:258
  130.2 6.9 %shard_map.138 = bf16[512,8192]{1,0:T(8,128)(2,1)} custom-call(s32[4]{0:T(128)S(1)} %pad_add_fusion.places_ref, bf16[512,8192]{1,0:T(8,128)(2,1)S(1)} %copy-done.5, bf16[4,1024,512]{2,1,0:T(8,128)(2,1)} %collective-permute-done.17.weight_ref, bf16[512,512]{1,0:T(8,128)(2,1)S(1)} %get-tuple-element.133.cot_ref, ...), custom_call_target="tpu_custom_call", output_to_operand_aliasing={{}: (5, {})} | custom-call | flops 1024 | bytes 1024 | tf_op jit(solution)/shard_map/pallas_call | solution.py:258
  137.1 6.8 %collective-permute-done.25 = bf16[512,256]{1,0:T(8,128)(2,1)S(1)} collective-permute-done((bf16[512,256]{1,0:T(8,128)(2,1)S(1)}, bf16[512,256]{1,0:T(8,128)(2,1)S(1)}, u32[]{:S(2)}, u32[]{:S(2)}) %collective-permute-start.25) | collective-permute-done | bytes 262176 | tf_op jit(solution)/shard_map/ppermute | solution.py:24
  (112 shorter events, 30.7 us)
Async XLA Ops:
  2.1 5.4 %collective-permute-start = (f32[1,52,128]{2,1,0:T(8,128)S(1)}, f32[1,52,128]{2,1,0:T(8,128)S(1)}, u32[]{:S(2)}, u32[]{:S(2)}) collective-permute-start(f32[1,52,128]{2,1,0:T(8,128)S(1)} %maximum_bitcast_fusion), channel_id=1, source_target_pairs={{0,1},{1,0},{2,3},{3,2},{4,5},{5,4},{6,7},{7,6},{8,9},{9,8},{10,11... | collective-permute-start | bytes 79880 | tf_op jit(solution)/shard_map/ppermute | solution.py:29
  7.6 25.0 %copy-start.23 = (s32[8]{0:T(128)S(1)}, s32[8]{0:T(128)}, u32[]{:S(2)}) copy-start(s32[8]{0:T(128)} %param.19) | copy-start | bytes 100
  7.6 15.9 %collective-permute-start.1 = (bf16[256,512]{1,0:T(8,128)(2,1)}, bf16[256,512]{1,0:T(8,128)(2,1)S(1)}, u32[]{:S(2)}, u32[]{:S(2)}) collective-permute-start(bf16[256,512]{1,0:T(8,128)(2,1)} %multiply_convert_fusion), channel_id=1, source_target_pairs={{0,1},{1,2},{2,3},{3,0},{4,5},{5,6},{6,7},{7,4},{8,9},{9,10},{10,1... | collective-permute-start | bytes 786440 | tf_op jit(solution)/shard_map/ppermute | solution.py:24
  9.1 14.4 %collective-permute-start.2 = (bf16[256,512]{1,0:T(8,128)(2,1)}, bf16[256,512]{1,0:T(8,128)(2,1)S(1)}, u32[]{:S(2)}, u32[]{:S(2)}) collective-permute-start(bf16[256,512]{1,0:T(8,128)(2,1)} %multiply_convert_fusion), channel_id=1, source_target_pairs={{0,8},{8,0},{1,9},{9,1},{2,10},{10,2},{3,11},{11,3},{4,12},{12,4},... | collective-permute-start | bytes 786440 | tf_op jit(solution)/shard_map/ppermute | solution.py:24
  10.6 12.9 %collective-permute-start.3 = (f32[2,52,128]{2,1,0:T(8,128)S(1)}, f32[2,52,128]{2,1,0:T(8,128)S(1)}, u32[]{:S(2)}, u32[]{:S(2)}) collective-permute-start(f32[2,52,128]{2,1,0:T(8,128)S(1)} %pad_maximum_fusion.5), channel_id=1, source_target_pairs={{0,2},{1,3},{2,0},{3,1},{4,6},{5,7},{6,4},{7,5},{8,10},{9,11},{10,... | collective-permute-start | bytes 159752 | tf_op jit(solution)/shard_map/ppermute | solution.py:29
  23.5 8.0 %collective-permute-start.4 = (bf16[256,512]{1,0:T(8,128)(2,1)S(1)}, bf16[256,512]{1,0:T(8,128)(2,1)S(1)}, u32[]{:S(2)}, u32[]{:S(2)}) collective-permute-start(bf16[256,512]{1,0:T(8,128)(2,1)S(1)} %collective-permute-done.1), channel_id=1, source_target_pairs={{0,16},{16,0},{1,17},{17,1},{2,18},{18,2},{3,19},{19,3},{4,20},{20... | collective-permute-start | bytes 786440 | tf_op jit(solution)/shard_map/ppermute | solution.py:24
  25.1 19.1 %collective-permute-start.5 = (bf16[256,512]{1,0:T(8,128)(2,1)}, bf16[256,512]{1,0:T(8,128)(2,1)}, u32[]{:S(2)}, u32[]{:S(2)}) collective-permute-start(bf16[256,512]{1,0:T(8,128)(2,1)} %multiply_convert_fusion), channel_id=1, source_target_pairs={{0,3},{1,0},{2,1},{3,2},{4,7},{5,4},{6,5},{7,6},{8,11},{9,8},{10,9... | collective-permute-start | bytes 786440 | tf_op jit(solution)/shard_map/ppermute | solution.py:24
  27.6 24.3 %collective-permute-start.9 = (bf16[2,256,512]{2,1,0:T(8,128)(2,1)S(1)}, bf16[2,256,512]{2,1,0:T(8,128)(2,1)S(1)}, u32[]{:S(2)}, u32[]{:S(2)}) collective-permute-start(bf16[2,256,512]{2,1,0:T(8,128)(2,1)S(1)} %pad_maximum_fusion.rest_0_), channel_id=1, source_target_pairs={{0,16},{16,0},{1,17},{17,1},{2,18},{18,2},{3,19},{19,3},{4,20},{20... | collective-permute-start | bytes 1572872 | tf_op jit(solution)/shard_map/ppermute | solution.py:24
  31.5 17.9 %collective-permute-start.7 = (bf16[256,512]{1,0:T(8,128)(2,1)}, bf16[256,512]{1,0:T(8,128)(2,1)}, u32[]{:S(2)}, u32[]{:S(2)}) collective-permute-start(bf16[256,512]{1,0:T(8,128)(2,1)} %multiply_convert_fusion), channel_id=1, source_target_pairs={{0,2},{1,3},{2,0},{3,1},{4,6},{5,7},{6,4},{7,5},{8,10},{9,11},{10,... | collective-permute-start | bytes 786440 | tf_op jit(solution)/shard_map/ppermute | solution.py:24
  31.9 20.8 %collective-permute-start.10 = (bf16[2,256,512]{2,1,0:T(8,128)(2,1)S(1)}, bf16[2,256,512]{2,1,0:T(8,128)(2,1)S(1)}, u32[]{:S(2)}, u32[]{:S(2)}) collective-permute-start(bf16[2,256,512]{2,1,0:T(8,128)(2,1)S(1)} %pad_maximum_fusion.1.rest_2_), channel_id=1, source_target_pairs={{0,8},{8,0},{1,9},{9,1},{2,10},{10,2},{3,11},{11,3},{4,12},{12,4},... | collective-permute-start | bytes 1572872 | tf_op jit(solution)/shard_map/ppermute | solution.py:24
  44.2 8.5 %collective-permute-start.6 = (bf16[256,512]{1,0:T(8,128)(2,1)}, bf16[256,512]{1,0:T(8,128)(2,1)S(1)}, u32[]{:S(2)}, u32[]{:S(2)}) collective-permute-start(bf16[256,512]{1,0:T(8,128)(2,1)} %collective-permute-done.5), channel_id=1, source_target_pairs={{0,8},{8,0},{1,9},{9,1},{2,10},{10,2},{3,11},{11,3},{4,12},{12,4},... | collective-permute-start | bytes 786440 | tf_op jit(solution)/shard_map/ppermute | solution.py:24
  49.5 7.0 %collective-permute-start.8 = (bf16[256,512]{1,0:T(8,128)(2,1)}, bf16[256,512]{1,0:T(8,128)(2,1)S(1)}, u32[]{:S(2)}, u32[]{:S(2)}) collective-permute-start(bf16[256,512]{1,0:T(8,128)(2,1)} %collective-permute-done.7), channel_id=1, source_target_pairs={{0,16},{16,0},{1,17},{17,1},{2,18},{18,2},{3,19},{19,3},{4,20},{20... | collective-permute-start | bytes 786440 | tf_op jit(solution)/shard_map/ppermute | solution.py:24
  57.2 5.5 %collective-permute-start.11 = (bf16[2,4,512,256]{3,2,1,0:T(8,128)(2,1)}, bf16[2,4,512,256]{3,2,1,0:T(8,128)(2,1)}, u32[]{:S(2)}, u32[]{:S(2)}) collective-permute-start(bf16[2,4,512,256]{3,2,1,0:T(8,128)(2,1)} %shard_map.131), channel_id=1, source_target_pairs={{0,4},{4,0},{1,5},{5,1},{2,6},{6,2},{3,7},{7,3},{8,12},{12,8},{9,1... | collective-permute-start | bytes 6291464 | tf_op jit(solution)/shard_map/ppermute | solution.py:24
  57.2 16.3 %collective-permute-start.14 = (bf16[2,4,512,256]{3,2,1,0:T(8,128)(2,1)}, bf16[2,4,512,256]{3,2,1,0:T(8,128)(2,1)}, u32[]{:S(2)}, u32[]{:S(2)}) collective-permute-start(bf16[2,4,512,256]{3,2,1,0:T(8,128)(2,1)} %shard_map.132), channel_id=1, source_target_pairs={{0,4},{4,0},{1,5},{5,1},{2,6},{6,2},{3,7},{7,3},{8,12},{12,8},{9,1... | collective-permute-start | bytes 6291464 | tf_op jit(solution)/shard_map/ppermute | solution.py:24
  58.8 24.4 %collective-permute-start.16 = (bf16[2,256,512]{2,1,0:T(8,128)(2,1)S(1)}, bf16[2,256,512]{2,1,0:T(8,128)(2,1)}, u32[]{:S(2)}, u32[]{:S(2)}) collective-permute-start(bf16[2,256,512]{2,1,0:T(8,128)(2,1)S(1)} %pad_maximum_fusion.3.rest_6_), channel_id=1, source_target_pairs={{0,8},{8,0},{1,9},{9,1},{2,10},{10,2},{3,11},{11,3},{4,12},{12,4},... | collective-permute-start | bytes 1572872 | tf_op jit(solution)/shard_map/ppermute | solution.py:24
  60.5 22.7 %collective-permute-start.15 = (bf16[2,256,512]{2,1,0:T(8,128)(2,1)S(1)}, bf16[2,256,512]{2,1,0:T(8,128)(2,1)}, u32[]{:S(2)}, u32[]{:S(2)}) collective-permute-start(bf16[2,256,512]{2,1,0:T(8,128)(2,1)S(1)} %pad_maximum_fusion.2.rest_4_), channel_id=1, source_target_pairs={{0,16},{16,0},{1,17},{17,1},{2,18},{18,2},{3,19},{19,3},{4,20},{20... | collective-permute-start | bytes 1572872 | tf_op jit(solution)/shard_map/ppermute | solution.py:24
  71.7 19.3 %collective-permute-start.12 = (bf16[2,512,256]{2,1,0:T(8,128)(2,1)}, bf16[2,512,256]{2,1,0:T(8,128)(2,1)}, u32[]{:S(2)}, u32[]{:S(2)}) collective-permute-start(bf16[2,512,256]{2,1,0:T(8,128)(2,1)} %get-tuple-element.101), channel_id=1, source_target_pairs={{0,8},{8,0},{1,9},{9,1},{2,10},{10,2},{3,11},{11,3},{4,12},{12,4},... | collective-permute-start | bytes 1572872 | tf_op jit(solution)/shard_map/ppermute | solution.py:24
  73.2 17.8 %collective-permute-start.13 = (bf16[2,512,256]{2,1,0:T(8,128)(2,1)}, bf16[2,512,256]{2,1,0:T(8,128)(2,1)}, u32[]{:S(2)}, u32[]{:S(2)}) collective-permute-start(bf16[2,512,256]{2,1,0:T(8,128)(2,1)} %get-tuple-element.102), channel_id=1, source_target_pairs={{0,16},{16,0},{1,17},{17,1},{2,18},{18,2},{3,19},{19,3},{4,20},{20... | collective-permute-start | bytes 1572872 | tf_op jit(solution)/shard_map/ppermute | solution.py:24
  91.0 7.6 %collective-permute-start.17 = (bf16[4,1024,512]{2,1,0:T(8,128)(2,1)}, bf16[4,1024,512]{2,1,0:T(8,128)(2,1)}, u32[]{:S(2)}, u32[]{:S(2)}) collective-permute-start(bf16[4,1024,512]{2,1,0:T(8,128)(2,1)} %get-tuple-element.131.weight_ref), channel_id=1, source_target_pairs={{0,4},{4,0},{1,5},{5,1},{2,6},{6,2},{3,7},{7,3},{8,12},{12,8},{9,1... | collective-permute-start | bytes 12582920 | tf_op jit(solution)/shard_map/ppermute | solution.py:24
  92.8 17.3 %collective-permute-start.21 = (bf16[512,256]{1,0:T(8,128)(2,1)}, bf16[512,256]{1,0:T(8,128)(2,1)}, u32[]{:S(2)}, u32[]{:S(2)}) collective-permute-start(bf16[512,256]{1,0:T(8,128)(2,1)} %fusion.6), channel_id=1, source_target_pairs={{0,8},{8,0},{1,9},{9,1},{2,10},{10,2},{3,11},{11,3},{4,12},{12,4},... | collective-permute-start | bytes 786440 | tf_op jit(solution)/shard_map/ppermute | solution.py:24
  96.0 14.1 %collective-permute-start.20 = (bf16[512,256]{1,0:T(8,128)(2,1)}, bf16[512,256]{1,0:T(8,128)(2,1)}, u32[]{:S(2)}, u32[]{:S(2)}) collective-permute-start(bf16[512,256]{1,0:T(8,128)(2,1)} %fusion.5), channel_id=1, source_target_pairs={{0,16},{16,0},{1,17},{17,1},{2,18},{18,2},{3,19},{19,3},{4,20},{20... | collective-permute-start | bytes 786440 | tf_op jit(solution)/shard_map/ppermute | solution.py:24
  97.0 15.9 %collective-permute-start.18 = (bf16[2,512,256]{2,1,0:T(8,128)(2,1)}, bf16[2,512,256]{2,1,0:T(8,128)(2,1)S(1)}, u32[]{:S(2)}, u32[]{:S(2)}) collective-permute-start(bf16[2,512,256]{2,1,0:T(8,128)(2,1)} %get-tuple-element.137), channel_id=1, source_target_pairs={{0,8},{8,0},{1,9},{9,1},{2,10},{10,2},{3,11},{11,3},{4,12},{12,4},... | collective-permute-start | bytes 1572872 | tf_op jit(solution)/shard_map/ppermute | solution.py:24
  98.4 17.4 %collective-permute-start.19 = (bf16[2,512,256]{2,1,0:T(8,128)(2,1)}, bf16[2,512,256]{2,1,0:T(8,128)(2,1)S(1)}, u32[]{:S(2)}, u32[]{:S(2)}) collective-permute-start(bf16[2,512,256]{2,1,0:T(8,128)(2,1)} %get-tuple-element.138), channel_id=1, source_target_pairs={{0,16},{16,0},{1,17},{17,1},{2,18},{18,2},{3,19},{19,3},{4,20},{20... | collective-permute-start | bytes 1572872 | tf_op jit(solution)/shard_map/ppermute | solution.py:24
  103.2 12.6 %copy-start.20 = (bf16[2,512,256]{2,1,0:T(8,128)(2,1)S(1)}, bf16[2,512,256]{2,1,0:T(8,128)(2,1)}, u32[]{:S(2)}) copy-start(bf16[2,512,256]{2,1,0:T(8,128)(2,1)} %get-tuple-element.146) | copy-start | bytes 1572868
  103.2 13.5 %copy-start.19 = (bf16[2,512,256]{2,1,0:T(8,128)(2,1)S(1)}, bf16[2,512,256]{2,1,0:T(8,128)(2,1)}, u32[]{:S(2)}) copy-start(bf16[2,512,256]{2,1,0:T(8,128)(2,1)} %get-tuple-element.136) | copy-start | bytes 1572868
  115.9 13.1 %collective-permute-start.23 = (bf16[512,256]{1,0:T(8,128)(2,1)S(1)}, bf16[512,256]{1,0:T(8,128)(2,1)S(1)}, u32[]{:S(2)}, u32[]{:S(2)}) collective-permute-start(bf16[512,256]{1,0:T(8,128)(2,1)S(1)} %fusion.8), channel_id=1, source_target_pairs={{0,8},{8,0},{1,9},{9,1},{2,10},{10,2},{3,11},{11,3},{4,12},{12,4},... | collective-permute-start | bytes 786440 | tf_op jit(solution)/shard_map/ppermute | solution.py:24
  116.8 12.2 %collective-permute-start.22 = (bf16[512,256]{1,0:T(8,128)(2,1)S(1)}, bf16[512,256]{1,0:T(8,128)(2,1)S(1)}, u32[]{:S(2)}, u32[]{:S(2)}) collective-permute-start(bf16[512,256]{1,0:T(8,128)(2,1)S(1)} %fusion.7), channel_id=1, source_target_pairs={{0,16},{16,0},{1,17},{17,1},{2,18},{18,2},{3,19},{19,3},{4,20},{20... | collective-permute-start | bytes 786440 | tf_op jit(solution)/shard_map/ppermute | solution.py:24
  118.6 18.6 %collective-permute-start.24 = (bf16[512,256]{1,0:T(8,128)(2,1)S(1)}, bf16[512,256]{1,0:T(8,128)(2,1)S(1)}, u32[]{:S(2)}, u32[]{:S(2)}) collective-permute-start(bf16[512,256]{1,0:T(8,128)(2,1)S(1)} %bitcast_add_fusion.2), channel_id=1, source_target_pairs={{0,3},{1,0},{2,1},{3,2},{4,7},{5,4},{6,5},{7,6},{8,11},{9,8},{10,9... | collective-permute-start | bytes 786440 | tf_op jit(solution)/shard_map/ppermute | solution.py:24
  121.3 22.7 %collective-permute-start.25 = (bf16[512,256]{1,0:T(8,128)(2,1)S(1)}, bf16[512,256]{1,0:T(8,128)(2,1)S(1)}, u32[]{:S(2)}, u32[]{:S(2)}) collective-permute-start(bf16[512,256]{1,0:T(8,128)(2,1)S(1)} %bitcast_add_fusion.3), channel_id=1, source_target_pairs={{0,2},{1,3},{2,0},{3,1},{4,6},{5,7},{6,4},{7,5},{8,10},{9,11},{10,... | collective-permute-start | bytes 786440 | tf_op jit(solution)/shard_map/ppermute | solution.py:24
  129.1 15.1 %copy-start.15 = (bf16[256,512]{1,0:T(8,128)(2,1)S(1)}, bf16[256,512]{1,0:T(8,128)(2,1)}, u32[]{:S(2)}) copy-start(bf16[256,512]{1,0:T(8,128)(2,1)} %param.12) | copy-start | bytes 786436
  129.1 15.2 %copy-start.24 = (bf16[256]{0:T(256)(128)(2,1)S(1)}, bf16[256]{0:T(256)(128)(2,1)}, u32[]{:S(2)}) copy-start(bf16[256]{0:T(256)(128)(2,1)} %param.11) | copy-start | bytes 1540
  129.1 14.9 %collective-permute-start.26 = (bf16[512,256]{1,0:T(8,128)(2,1)S(1)}, bf16[512,256]{1,0:T(8,128)(2,1)S(1)}, u32[]{:S(2)}, u32[]{:S(2)}) collective-permute-start(bf16[512,256]{1,0:T(8,128)(2,1)S(1)} %fusion.1), channel_id=1, source_target_pairs={{0,1},{1,2},{2,3},{3,0},{4,5},{5,6},{6,7},{7,4},{8,9},{9,10},{10,1... | collective-permute-start | bytes 786440 | tf_op jit(solution)/shard_map/ppermute | solution.py:24
  (20 other events, 82.4 us)

commit v9 on v8

--- a/solution.py
+++ b/solution.py
@@ -12,7 +12,7 @@
 BETA = 0.5
 CORES = 2
 OUTER = 2
-PAIR_VMEM = 14 * 1024 * 1024
+PAIR_VMEM = 18 * 1024 * 1024
 WEIGHT_VMEM = 22 * 1024 * 1024
 NOMINAL = pl.CostEstimate(flops=1024, bytes_accessed=1024, transcendentals=0)
 BF16 = jnp.bfloat16
@@ -31,10 +31,6 @@
 
 def in_hbm(array):
     return pltpu.with_memory_space_constraint(array, pltpu.HBM)
-
-
-def in_vmem(array):
-    return pltpu.with_memory_space_constraint(array, pltpu.VMEM)
 
 
 def after(value, *earlier):
@@ -57,82 +53,74 @@
 
 
 def theirs_kernel(places_ref, cot_ref, *rest):
-    count = len(rest) * 2 // 3
-    blocks, outs = rest[:count], rest[count:]
+    blocks, out_ref = rest[:-1], rest[-1]
     for slot, resid_ref in enumerate(blocks):
         product = jnp.dot(cot_ref[...], resid_ref[...], preferred_element_type=F32)
-        outs[slot // 2][slot % 2, 0] = product.astype(BF16)
-
-
-def theirs_product(residual, cot_t, places, rows):
-    features, tokens = cot_t.shape
-    steps = 4
-    slots = places.shape[0] // steps
-    block = pl.BlockSpec((2, 1, features, rows), lambda i, p: (0, i, 0, 0))
-    return pl.pallas_call(
-        theirs_kernel,
-        out_shape=[pltpu.HBM((2, steps, features, rows), BF16)] * (slots // 2),
-        grid_spec=pltpu.PrefetchScalarGridSpec(
-            num_scalar_prefetch=1,
-            grid=(steps,),
-            in_specs=[pl.BlockSpec((features, tokens), lambda i, p: (0, 0))]
-            + [
-                pl.BlockSpec((tokens, rows), lambda i, p, slot=slot: (0, p[slots * i + slot]))
-                for slot in range(slots)
-            ],
-            out_specs=[block] * (slots // 2),
-        ),
-        cost_estimate=NOMINAL,
-        compiler_params=pltpu.CompilerParams(vmem_limit_bytes=PAIR_VMEM),
-    )(places, cot_t, *[in_vmem(residual)] * slots)
-
-
-def ours_kernel(places_ref, cot_ref, first_ref, second_ref, other_ref, *outs):
+        out_ref[slot, 0] = product.astype(BF16)
+
+
+def ours_kernel(places_ref, cot_ref, *rest):
+    slots = len(rest) // 3
+    blocks, other_ref, outs = rest[:slots], rest[slots], rest[slots + 1 :]
     step = pl.program_id(0)
-    at_outer, at_inner = step // 2, lax.rem(step, 2)
+    ways = (lax.rem(step, 2), step // 2)
     totals = [
         (
             jnp.dot(cot_ref[...], resid_ref[...], preferred_element_type=F32)
             + other_ref[slot, 0].astype(F32)
         ).astype(BF16)
-        for slot, resid_ref in enumerate((first_ref, second_ref))
+        for slot, resid_ref in enumerate(blocks)
     ]
-    for slot, way in enumerate((at_inner, at_outer)):
-        send_ref, keep_ref = outs[2 * slot : 2 * slot + 2]
+    for which, way in enumerate(ways):
 
         @pl.when(way == 1)
         def _():
-            send_ref[0] = totals[slot]
+            for slot in range(which, slots, 2):
+                outs[2 * slot][0] = totals[slot]
 
         @pl.when(way == 0)
         def _():
-            keep_ref[0] = totals[slot]
-
-
-def ours_product(residual, cot_t, places, rows, other):
+            for slot in range(which, slots, 2):
+                outs[2 * slot + 1][0] = totals[slot]
+
+
+def grad_product(residual, cot_t, places, rows, other):
     features, tokens = cot_t.shape
-    steps = places.shape[0] // 2
-    indices = [lambda i: i // 2, lambda i: i // 2, lambda i: jnp.maximum(i - 2, 0), lambda i: jnp.minimum(i, 1)]
+    steps = 4
+    slots = places.shape[0] // steps
+    in_specs = [pl.BlockSpec((features, tokens), lambda i, p: (0, 0))] + [
+        pl.BlockSpec((tokens, rows), lambda i, p, slot=slot: (0, p[slots * i + slot]))
+        for slot in range(slots)
+    ]
+    operands = [places, cot_t] + [in_hbm(residual)] * slots
+    block = pl.BlockSpec((slots, 1, features, rows), lambda i, p: (0, i, 0, 0))
+    if other is None:
+        kernel, out_specs = theirs_kernel, block
+        out_shape = pltpu.HBM((slots, steps, features, rows), BF16)
+    else:
+        kernel = ours_kernel
+        in_specs.append(block)
+        operands.append(other)
+        indices = [
+            lambda i: i // 2,
+            lambda i: i // 2,
+            lambda i: jnp.maximum(i - 2, 0),
+            lambda i: jnp.minimum(i, 1),
+        ]
+        out_specs = [
+            pl.BlockSpec((1, features, rows), lambda i, p, index=index: (index(i), 0, 0))
+            for index in indices
+        ] * (slots // 2)
+        out_shape = [pltpu.HBM((2, features, rows), BF16)] * (2 * slots)
     return pl.pallas_call(
-        ours_kernel,
-        out_shape=[pltpu.HBM((2, features, rows), BF16)] * 4,
+        kernel,
+        out_shape=out_shape,
         grid_spec=pltpu.PrefetchScalarGridSpec(
-            num_scalar_prefetch=1,
-            grid=(steps,),
-            in_specs=[
-                pl.BlockSpec((features, tokens), lambda i, p: (0, 0)),
-                pl.BlockSpec((tokens, rows), lambda i, p: (0, p[2 * i])),
-                pl.BlockSpec((tokens, rows), lambda i, p: (0, p[2 * i + 1])),
-                pl.BlockSpec((2, 1, features, rows), lambda i, p: (0, i, 0, 0)),
-            ],
-            out_specs=[
-                pl.BlockSpec((1, features, rows), lambda i, p, index=index: (index(i), 0, 0))
-                for index in indices
-            ],
+            num_scalar_prefetch=1, grid=(steps,), in_specs=in_specs, out_specs=out_specs
         ),
         cost_estimate=NOMINAL,
         compiler_params=pltpu.CompilerParams(vmem_limit_bytes=PAIR_VMEM),
-    )(places, cot_t, in_vmem(residual), in_vmem(residual), other)
+    )(*operands)
 
 
 def place_weight(inner_flags, offsets_ref, pieces, weight_ref):
@@ -217,10 +205,10 @@
     rows, features = pieces[0].shape[1:]
     steps = places.shape[0]
     depth = width // (CORES * steps)
-    total = jax.ShapeDtypeStruct((tokens, features), F32)
+    total = pltpu.HBM((tokens, features), F32)
     return pl.pallas_call(
         functools.partial(value_kernel, inner_flags),
-        out_shape=[total, pltpu.VMEM((steps, depth, features), BF16)],
+        out_shape=[total, pltpu.HBM((steps, depth, features), BF16)],
         grid_spec=pltpu.PrefetchScalarGridSpec(
             num_scalar_prefetch=2,
             grid=(steps,),
@@ -233,7 +221,7 @@
         ),
         cost_estimate=NOMINAL,
         compiler_params=pltpu.CompilerParams(vmem_limit_bytes=WEIGHT_VMEM),
-    )(places, offsets, in_vmem(residual), *pieces)
+    )(places, offsets, in_hbm(residual), *pieces)
 
 
 def weight_call(kernel, places, residual, weight, wholes, out_shape, earlier=None):
@@ -249,7 +237,7 @@
         pl.BlockSpec((tokens, depth), lambda i, p: (0, p[i])),
         pl.BlockSpec((1, depth, features), lambda i, p: (p[i] // CORES, 0, 0)),
     ] + [whole_block(array) for array in wholes]
-    operands = [places, in_vmem(residual), in_vmem(weight), *wholes]
+    operands = [places, in_hbm(residual), weight, *wholes]
     aliases = {}
     if earlier is not None:
         aliases = {len(operands): 0}
@@ -271,28 +259,6 @@
     )(*operands)
 
 
-def squares_kernel(resid_ref, out_ref, kept_ref):
-    block = resid_ref[...]
-    kept_ref[...] = block
-    wide = block.astype(F32)
-    out_ref[...] = jnp.sum(wide * wide, axis=1, keepdims=True)
-
-
-def row_squares(residual):
-    tokens, width = residual.shape
-    rows = 64
-    block = pl.BlockSpec((rows, width), lambda i: (i, 0))
-    return pl.pallas_call(
-        squares_kernel,
-        out_shape=[jax.ShapeDtypeStruct((tokens, 1), F32), pltpu.VMEM((tokens, width), BF16)],
-        grid=(tokens // rows,),
-        in_specs=[block],
-        out_specs=[pl.BlockSpec((rows, 1), lambda i: (i, 0)), block],
-        cost_estimate=NOMINAL,
-        compiler_params=pltpu.CompilerParams(vmem_limit_bytes=PAIR_VMEM),
-    )(in_hbm(residual))
-
-
 def cot_kernel(width, rep_count, info_ref, shares_ref, squares_ref, value_cot_ref, cot_ref, cot_t_ref, inv_ref):
     place, length = info_ref[0], info_ref[1]
     rows = value_cot_ref.shape[0]
@@ -350,7 +316,7 @@
         ),
         cost_estimate=NOMINAL,
         compiler_params=pltpu.CompilerParams(vmem_limit_bytes=PAIR_VMEM),
-    )(info, shares, squares, value_cot)
+    )(info, shares, squares, in_hbm(value_cot))
 
 
 def per_device(
@@ -392,7 +358,8 @@
 
     gained = (value_weight.astype(F32) * norm_gain.astype(F32)[:, None]).astype(BF16)
     residual, gained, packed = lax.optimization_barrier((residual, gained, packed))
-    squares, residual = row_squares(residual)
+    resid_wide = residual.astype(F32)
+    squares = jnp.sum(resid_wide * resid_wide, axis=1, keepdims=True)
 
     def near_of(k, block):
         first = "inner" if inner_first(k) else "outer"
@@ -416,18 +383,23 @@
     near[1] = near_of(1, arrived[1])
     arrived[2] = swap(late_gained, "tp", shifts[2])
     own_pieces[0] = far_of(0, gained, near[0])
-    near[1], packed, late_gained = lax.optimization_barrier((near[1], packed, late_gained))
+    seq_length = lax.dynamic_index_in_dim(lengths, rep_place, keepdims=False)
+    info = jnp.stack([tp_place, seq_length]).astype(jnp.int32)
+    near[1], arrived[2], packed, late_gained, info = lax.optimization_barrier(
+        (near[1], arrived[2], packed, late_gained, info)
+    )
+    near[2] = near_of(2, arrived[2])
     for k in order[3:]:
         arrived[k] = swap(late_gained, "tp", shifts[k])
     own_pieces[1] = far_of(1, arrived[1], near[1])
-    seq_length = lax.dynamic_index_in_dim(lengths, rep_place, keepdims=False)
-    info = jnp.stack([tp_place, seq_length]).astype(jnp.int32)
     cot, cot_t, inv_rms = scaled_cot(width, rep_count, info, packed, squares, value_cot)
 
     def place_of(o, i, c, k):
         chip = lax.rem(at_outer + o, outer) * inner + lax.rem(at_inner + i, inner)
         return (chip * CORES + c) * tp_count + lax.rem(tp_place + k, tp_count)
 
+    backward = order[::-1]
+    pairs = [backward[i : i + 2] for i in range(0, tp_count, 2)]
     chips = [(o, i) for o in range(outer) for i in range(inner)]
     if not in_place:
         product = jnp.dot(cot_t, residual, preferred_element_type=F32).astype(BF16)
@@ -436,21 +408,27 @@
     def places_of(pair, c):
         return jnp.stack([place_of(o, i, c, k) for o, i in chips for k in pair]).astype(jnp.int32)
 
-    def for_other(pair, cot_t):
-        places = places_of(pair, 1 - core)
-        both = after(product, cot_t)[places].reshape(len(chips), 2, features, rows)
+    def for_others(cot_t):
+        places = places_of(backward, 1 - core)
+        if in_place:
+            return grad_product(residual, cot_t, places, rows, None)
+        both = after(product, cot_t)[places].reshape(len(chips), tp_count, features, rows)
         return both.swapaxes(0, 1)
 
-    def for_us(pair, other):
-        places = places_of(pair, core)
+    def for_us(other):
+        places = places_of(backward, core)
         if in_place:
-            send_a, keep_a, send_b, keep_b = ours_product(residual, cot_t, places, rows, other)
-            return ([send_a], keep_a), ([send_b], keep_b)
-        both = product[places].reshape(len(chips), 2, features, rows).swapaxes(0, 1)
-        total = widen([both, other]).astype(BF16).reshape(2, outer, inner, features, rows)
-        first = ([total[0, :, s] for s in range(1, inner)], total[0, :, 0])
-        second = ([total[1, s] for s in range(1, outer)], total[1, 0])
-        return first, second
+            outs = grad_product(residual, cot_t, places, rows, other)
+            sides = [([outs[2 * n]], outs[2 * n + 1]) for n in range(tp_count)]
+        else:
+            both = product[places].reshape(len(chips), tp_count, features, rows).swapaxes(0, 1)
+            total = widen([both, other]).astype(BF16)
+            total = total.reshape(tp_count, outer, inner, features, rows)
+            sides = []
+            for n in range(0, tp_count, 2):
+                sides.append(([total[n, :, s] for s in range(1, inner)], total[n, :, 0]))
+                sides.append(([total[n + 1, s] for s in range(1, outer)], total[n + 1, 0]))
+        return [sides[n : n + 2] for n in range(0, tp_count, 2)]
 
     def first_round(sides):
         return [
@@ -475,33 +453,18 @@
             for (_, keep), parts, last in zip(sides, got, later)
         ]
 
-    backward = order[::-1]
-    pairs = [backward[i : i + 2] for i in range(0, tp_count, 2)]
-    def for_others(part, cot_t):
-        if in_place:
-            return theirs_product(residual, cot_t, places_of(part, 1 - core), rows)
-        return [for_other(part, cot_t)]
-
-    theirs = for_others(pairs[0], cot_t)
-    theirs, arrived[2] = lax.optimization_barrier((theirs, arrived[2]))
-    near[2] = near_of(2, arrived[2])
-    for pair in pairs[1:]:
-        theirs += for_others(pair, after(cot_t, theirs))
-    theirs, arrived[3] = lax.optimization_barrier((theirs, arrived[3]))
-    near[3] = near_of(3, arrived[3])
-    near[2], near[3], theirs, own_pieces[0], own_pieces[1] = lax.optimization_barrier(
-        (near[2], near[3], theirs, own_pieces[0], own_pieces[1])
-    )
-    others = [swap(part, "core", 1) for part in theirs]
-    own_pieces[2] = far_of(2, arrived[2], near[2])
-    own_pieces[3] = far_of(3, arrived[3], near[3])
-    sides = [for_us(pairs[0], others[0])]
+    theirs = for_others(cot_t)
+    theirs, arrived, own_pieces, near = lax.optimization_barrier(
+        (theirs, arrived, own_pieces, near)
+    )
+    other = swap(theirs, "core", 1)
+    for k in order[3:]:
+        near[k] = near_of(k, arrived[k])
+    near, other, own_pieces = lax.optimization_barrier((near, other, own_pieces))
+    for k in order[2:]:
+        own_pieces[k] = far_of(k, arrived[k], near[k])
+    sides = for_us(other)
     got = [first_round(sides[0])]
-    sides.append(for_us(pairs[1], after(others[1], sides[0])))
-    for n in range(2, len(pairs)):
-        for k in order[2 * n : 2 * n + 2]:
-            own_pieces[k] = far_of(k, arrived[k], near_of(k, arrived[k]))
-        sides.append(for_us(pairs[n], others[n]))
     sides[1:], own_pieces = lax.optimization_barrier((sides[1:], own_pieces))
 
     if in_place:
@@ -537,7 +500,7 @@
             places[1],
             residual,
             other_weight,
-            [total, cot, inv_rms],
+            [in_hbm(total), cot, inv_rms],
             [
                 jax.ShapeDtypeStruct((rows_here, features), BF16),
                 jax.ShapeDtypeStruct((rows_here, 1), F32),
@@ -558,7 +521,7 @@
     if in_place:
         grad_shape = jax.ShapeDtypeStruct((rows_here, width), BF16)
         resid_grad = weight_call(
-            grad_kernel, places[0], residual, own_weight, [cot, coefficient], grad_shape
+            grad_kernel, places[0], residual, in_hbm(own_weight), [cot, coefficient], grad_shape
         )
         later[1], coefficient, resid_grad = lax.optimization_barrier((later[1], coefficient, resid_grad))
     else:

time: 147 us -> 136 us (0.925)
  local copies, waits for them, and re-layouts: 25.4 us -> 4.96 us
  waiting for transfers between devices: 16.8 us -> 35.9 us
  Pallas kernels: 54.9 us -> 47.9 us
  starting transfers between devices: 33.2 us -> 26.5 us
  other arithmetic: 14.7 us -> 19.1 us
    unnamed x51 -> x31, local copies, waits for them, and re-layouts: 24.3 us -> 3.92 us
    ppermute x25 -> x24, waiting for transfers between devices: 16.7 us -> 34.2 us  [swap(): lax.ppermute(value, axis, [(place, (place + step) % size) for place in ra...]
    pallas_call x5 -> x2, Pallas kernels: 26.5 us -> 14.9 us  [grad_product(): pl.pallas_call(kernel, out_shape=out_shape, grid_spec=pltpu.PrefetchScala...]
    ppermute x25 -> x24, starting transfers between devices: 27.6 us -> 20.9 us  [swap(): lax.ppermute(value, axis, [(place, (place + step) % size) for place in ra...]
    reduce_sum x0 -> x1, other arithmetic: none -> 5.1 us  [per_device(): squares = jnp.sum(resid_wide * resid_wide, axis=1, keepdims=True)]
    pallas_call x3, Pallas kernels: 20.6 us -> 23 us  [weight_call(): pl.pallas_call(kernel, out_shape=out_shape, grid_spec=pltpu.PrefetchScala...]
    ppermute x2, waiting for transfers between devices: 0.01 us -> 1.66 us  [trade(): lax.ppermute(value, axis, [(place, place ^ mask) for place in range(size)])]
  transfers between devices with their start and end apart: 27 -> 26, of which waited for: 5 -> 13; matrix products, arithmetic and copies ran while one was open for 9% -> 12% of each run, Pallas kernels for 38% -> 35%
where the time goes in v9:
time: 136 us; the launch traced here: 135 us
  Pallas kernels  47.9 us (35%)
  waiting for transfers between devices  35.9 us (26%)
  starting transfers between devices  26.5 us (19%)
  other arithmetic  19.1 us (14%)
  local copies, waits for them, and re-layouts  4.96 us (4%)
    ppermute x24, waiting for transfers between devices, swap(): lax.ppermute(value, axis, [(place, (place + step) % size) for place in ra...  34.2 us
    pallas_call x3, Pallas kernels, weight_call(): pl.pallas_call(kernel, out_shape=out_shape, grid_spec=pltpu.PrefetchScala...  23 us
    ppermute x24, starting transfers between devices, swap(): lax.ppermute(value, axis, [(place, (place + step) % size) for place in ra...  20.9 us
    pallas_call x2, Pallas kernels, grad_product(): pl.pallas_call(kernel, out_shape=out_shape, grid_spec=pltpu.PrefetchScala...  14.9 us
    pallas_call x1, Pallas kernels, first_value(): pl.pallas_call(functools.partial(value_kernel, inner_flags), out_shape=[t...  7.83 us
    ppermute x2, starting transfers between devices, trade(): lax.ppermute(value, axis, [(place, place ^ mask) for place in range(size)])  5.61 us
    reduce_sum x1, other arithmetic, per_device(): squares = jnp.sum(resid_wide * resid_wide, axis=1, keepdims=True)  5.1 us
    unnamed x31, local copies, waits for them, and re-layouts  3.92 us
  transfers between devices with their start and end apart: 26, of which 13 were waited for; matrix products, arithmetic and copies ran while one was open for 12% of the time, Pallas kernels for 35%

profile of v9, /device:TPU:0, one launch (start us, length us, event | category | flops | bytes accessed | tf_op | source)
XLA Modules:
  0.0 135.2 jit_solution(8393155827962662490)
XLA Ops:
  2.1 3.0 %collective-permute-start = (f32[1,52,128]{2,1,0:T(8,128)S(1)}, f32[1,52,128]{2,1,0:T(8,128)S(1)}, u32[]{:S(2)}, u32[]{:S(2)}) collective-permute-start(f32[1,52,128]{2,1,0:T(8,128)S(1)} %maximum_bitcast_fusion), channel_id=1, source_target_pairs={{0,1},{1,0},{2,3},{3,2},{4,5},{5,4},{6,7},{7,6},{8,9},{9,8},{10,11... | collective-permute-start | bytes 79880 | tf_op jit(solution)/shard_map/ppermute | solution.py:29
  5.8 1.8 %multiply_convert_fusion = bf16[256,512]{1,0:T(8,128)(2,1)} fusion(bf16[256,512]{1,0:T(8,128)(2,1)} %param.12, f32[256]{0:T(256)S(1)} %convert_element_type.135), kind=kLoop, calls=%fused_computation.20 | loop fusion | flops 393216 | bytes 525312 | tf_op jit(solution)/shard_map/convert_element_type | solution.py:359
  7.6 1.4 %collective-permute-start.1 = (bf16[256,512]{1,0:T(8,128)(2,1)}, bf16[256,512]{1,0:T(8,128)(2,1)S(1)}, u32[]{:S(2)}, u32[]{:S(2)}) collective-permute-start(bf16[256,512]{1,0:T(8,128)(2,1)} %multiply_convert_fusion), channel_id=1, source_target_pairs={{0,1},{1,2},{2,3},{3,0},{4,5},{5,6},{6,7},{7,4},{8,9},{9,10},{10,1... | collective-permute-start | bytes 786440 | tf_op jit(solution)/shard_map/ppermute | solution.py:24
  9.0 1.5 %collective-permute-start.2 = (bf16[256,512]{1,0:T(8,128)(2,1)}, bf16[256,512]{1,0:T(8,128)(2,1)S(1)}, u32[]{:S(2)}, u32[]{:S(2)}) collective-permute-start(bf16[256,512]{1,0:T(8,128)(2,1)} %multiply_convert_fusion), channel_id=1, source_target_pairs={{0,8},{8,0},{1,9},{9,1},{2,10},{10,2},{3,11},{11,3},{4,12},{12,4},... | collective-permute-start | bytes 786440 | tf_op jit(solution)/shard_map/ppermute | solution.py:24
  10.5 2.6 %collective-permute-start.3 = (f32[2,52,128]{2,1,0:T(8,128)S(1)}, f32[2,52,128]{2,1,0:T(8,128)S(1)}, u32[]{:S(2)}, u32[]{:S(2)}) collective-permute-start(f32[2,52,128]{2,1,0:T(8,128)S(1)} %pad_maximum_fusion.5), channel_id=1, source_target_pairs={{0,2},{1,3},{2,0},{3,1},{4,6},{5,7},{6,4},{7,5},{8,10},{9,11},{10,... | collective-permute-start | bytes 159752 | tf_op jit(solution)/shard_map/ppermute | solution.py:29
  13.1 5.1 %multiply_reduce_fusion = f32[512]{0:T(512)S(1)} fusion(bf16[512,8192]{1,0:T(8,128)(2,1)} %resid_ref.3), kind=kLoop, calls=%fused_computation | loop fusion | flops 12582400 | bytes 8390656 | tf_op jit(solution)/shard_map/reduce_sum | solution.py:362
  18.2 1.7 %collective-permute-done.3 = f32[2,52,128]{2,1,0:T(8,128)S(1)} collective-permute-done((f32[2,52,128]{2,1,0:T(8,128)S(1)}, f32[2,52,128]{2,1,0:T(8,128)S(1)}, u32[]{:S(2)}, u32[]{:S(2)}) %collective-permute-start.3) | collective-permute-done | bytes 53280 | tf_op jit(solution)/shard_map/ppermute | solution.py:29
  19.9 1.6 %collective-permute-start.4 = (bf16[256,512]{1,0:T(8,128)(2,1)S(1)}, bf16[256,512]{1,0:T(8,128)(2,1)S(1)}, u32[]{:S(2)}, u32[]{:S(2)}) collective-permute-start(bf16[256,512]{1,0:T(8,128)(2,1)S(1)} %collective-permute-done.1), channel_id=1, source_target_pairs={{0,16},{16,0},{1,17},{17,1},{2,18},{18,2},{3,19},{19,3},{4,20},{20... | collective-permute-start | bytes 786440 | tf_op jit(solution)/shard_map/ppermute | solution.py:24
  21.5 1.7 %collective-permute-start.5 = (bf16[256,512]{1,0:T(8,128)(2,1)}, bf16[256,512]{1,0:T(8,128)(2,1)}, u32[]{:S(2)}, u32[]{:S(2)}) collective-permute-start(bf16[256,512]{1,0:T(8,128)(2,1)} %multiply_convert_fusion), channel_id=1, source_target_pairs={{0,3},{1,0},{2,1},{3,2},{4,7},{5,4},{6,5},{7,6},{8,11},{9,8},{10,9... | collective-permute-start | bytes 786440 | tf_op jit(solution)/shard_map/ppermute | solution.py:24
  26.0 3.1 %collective-permute-done.4 = bf16[256,512]{1,0:T(8,128)(2,1)S(1)} collective-permute-done((bf16[256,512]{1,0:T(8,128)(2,1)S(1)}, bf16[256,512]{1,0:T(8,128)(2,1)S(1)}, u32[]{:S(2)}, u32[]{:S(2)}) %collective-permute-start.4) | collective-permute-done | bytes 262176 | tf_op jit(solution)/shard_map/ppermute | solution.py:24
  30.2 1.7 %collective-permute-start.9 = (bf16[256,512]{1,0:T(8,128)(2,1)}, bf16[256,512]{1,0:T(8,128)(2,1)}, u32[]{:S(2)}, u32[]{:S(2)}) collective-permute-start(bf16[256,512]{1,0:T(8,128)(2,1)} %collective-permute-done.5), channel_id=1, source_target_pairs={{0,8},{8,0},{1,9},{9,1},{2,10},{10,2},{3,11},{11,3},{4,12},{12,4},... | collective-permute-start | bytes 786440 | tf_op jit(solution)/shard_map/ppermute | solution.py:24
  32.1 2.1 %shard_map.129 = (bf16[512,512]{1,0:T(8,128)(2,1)S(1)}, bf16[512,512]{1,0:T(8,128)(2,1)S(1)}, f32[512,1]{1,0:T(8,128)S(1)}) custom-call(s32[2]{0:T(128)S(1)} %pad_add_fusion.1.info_ref, f32[4,52,128]{2,1,0:T(8,128)S(1)} %pad_maximum_fusion.4.shares_ref, f32[512,1]{1,0:T(8,128)S(1)} %copy.17.squares_ref, bf16[512,512]{1,0:T(8,128)(2,1)} %value_cot_ref.1), custom_call_target="tpu_custom_call" | custom-call | flops 1024 | bytes 1024 | tf_op jit(solution)/shard_map/pallas_call | solution.py:308
  34.2 6.6 %shard_map.130 = bf16[4,4,512,256]{3,2,1,0:T(8,128)(2,1)} custom-call(s32[16]{0:T(128)S(1)} %stack.230.places_ref, bf16[512,512]{1,0:T(8,128)(2,1)S(1)} %get-tuple-element.89.cot_ref, bf16[512,8192]{1,0:T(8,128)(2,1)} %resid_ref.3, bf16[512,8192]{1,0:T(8,128)(2,1)} %resid_ref.3, bf16[512,8192]{1,0:T(8,128)(2,1)} %resid_ref.3, bf16[512,8192]{1,0:T(8,128)(2,1)} %resid_ref.3), custom_call_target="tpu_custom_call" | custom-call | flops 1024 | bytes 1024 | tf_op jit(solution)/shard_map/pallas_call | solution.py:115
  41.7 1.1 collective-permute-done.6
  42.8 5.4 %collective-permute-done.9 = bf16[256,512]{1,0:T(8,128)(2,1)} collective-permute-done((bf16[256,512]{1,0:T(8,128)(2,1)}, bf16[256,512]{1,0:T(8,128)(2,1)}, u32[]{:S(2)}, u32[]{:S(2)}) %collective-permute-start.9) | collective-permute-done | bytes 262176 | tf_op jit(solution)/shard_map/ppermute | solution.py:24
  48.8 8.4 %collective-permute-done.10 = bf16[256,512]{1,0:T(8,128)(2,1)S(1)} collective-permute-done((bf16[256,512]{1,0:T(8,128)(2,1)}, bf16[256,512]{1,0:T(8,128)(2,1)S(1)}, u32[]{:S(2)}, u32[]{:S(2)}) %collective-permute-start.10) | collective-permute-done | bytes 262176 | tf_op jit(solution)/shard_map/ppermute | solution.py:24
  58.6 1.1 pad_maximum_fusion.2.rest_4_
  60.3 8.3 %shard_map.131 = (bf16[2,512,256]{2,1,0:T(8,128)(2,1)}, bf16[2,512,256]{2,1,0:T(8,128)(2,1)}, bf16[2,512,256]{2,1,0:T(8,128)(2,1)}, bf16[2,512,256]{2,1,0:T(8,12...) custom-call(s32[16]{0:T(128)S(1)} %stack.211.places_ref, ...), custom_call_target="tpu_custom_call" | custom-call | flops 1024 | bytes 1024 | tf_op jit(solution)/shard_map/pallas_call | solution.py:115
  68.6 1.8 %collective-permute-start.12 = (bf16[2,512,256]{2,1,0:T(8,128)(2,1)}, bf16[2,512,256]{2,1,0:T(8,128)(2,1)}, u32[]{:S(2)}, u32[]{:S(2)}) collective-permute-start(bf16[2,512,256]{2,1,0:T(8,128)(2,1)} %get-tuple-element.102), channel_id=1, source_target_pairs={{0,8},{8,0},{1,9},{9,1},{2,10},{10,2},{3,11},{11,3},{4,12},{12,4},... | collective-permute-start | bytes 1572872 | tf_op jit(solution)/shard_map/ppermute | solution.py:24
  70.4 1.5 %collective-permute-start.13 = (bf16[2,512,256]{2,1,0:T(8,128)(2,1)}, bf16[2,512,256]{2,1,0:T(8,128)(2,1)}, u32[]{:S(2)}, u32[]{:S(2)}) collective-permute-start(bf16[2,512,256]{2,1,0:T(8,128)(2,1)} %get-tuple-element.103), channel_id=1, source_target_pairs={{0,16},{16,0},{1,17},{17,1},{2,18},{18,2},{3,19},{19,3},{4,20},{20... | collective-permute-start | bytes 1572872 | tf_op jit(solution)/shard_map/ppermute | solution.py:24
  75.9 7.8 %shard_map.132 = (f32[512,512]{1,0:T(8,128)}, bf16[4,1024,512]{2,1,0:T(8,128)(2,1)}) custom-call(s32[4]{0:T(128)S(1)} %get-tuple-element.166.places_ref, s32[4]{0:T(128)S(1)} %get-tuple-element.167.offsets_ref, bf16[512,8192]{1,0:T(8,128)(2,1)} %resid_ref.3, bf16[2,256,512]{2,1,0:T(8,128)(2,1)S(1)} %pad_maximum_fusion.rest_0_, ...), custom_call_target="tpu_custom_call" | custom-call | flops 1024 | bytes 1024 | tf_op jit(solution)/shard_map/pallas_call | solution.py:209
  85.3 2.3 %collective-permute-start.20 = (bf16[512,256]{1,0:T(8,128)(2,1)S(1)}, bf16[512,256]{1,0:T(8,128)(2,1)}, u32[]{:S(2)}, u32[]{:S(2)}) collective-permute-start(bf16[512,256]{1,0:T(8,128)(2,1)S(1)} %fusion.6), channel_id=1, source_target_pairs={{0,8},{8,0},{1,9},{9,1},{2,10},{10,2},{3,11},{11,3},{4,12},{12,4},... | collective-permute-start | bytes 786440 | tf_op jit(solution)/shard_map/ppermute | solution.py:24
  87.6 1.7 %fusion.5 = bf16[512,256]{1,0:T(8,128)(2,1)} fusion(bf16[2,512,256]{2,1,0:T(8,128)(2,1)} %collective-permute-done.12, bf16[2,512,256]{2,1,0:T(8,128)(2,1)S(1)} %copy-done.10), kind=kLoop, calls=%fused_computation.21 | loop fusion | flops 524288 | bytes 786432 | tf_op jit(solution)/shard_map/convert_element_type | solution.py:444
  89.8 1.6 %collective-permute-start.18 = (bf16[2,512,256]{2,1,0:T(8,128)(2,1)}, bf16[2,512,256]{2,1,0:T(8,128)(2,1)S(1)}, u32[]{:S(2)}, u32[]{:S(2)}) collective-permute-start(bf16[2,512,256]{2,1,0:T(8,128)(2,1)} %get-tuple-element.136), channel_id=1, source_target_pairs={{0,16},{16,0},{1,17},{17,1},{2,18},{18,2},{3,19},{19,3},{4,20},{20... | collective-permute-start | bytes 1572872 | tf_op jit(solution)/shard_map/ppermute | solution.py:24
  91.8 7.7 %shard_map.133 = (bf16[512,512]{1,0:T(8,128)(2,1)}, f32[512,1]{1,0:T(8,128)S(1)}) custom-call(s32[4]{0:T(128)S(1)} %pad_add_fusion.places_ref, bf16[512,8192]{1,0:T(8,128)(2,1)} %resid_ref.3, bf16[4,1024,512]{2,1,0:T(8,128)(2,1)} %collective-permute-done.16.weight_ref, f32[512,512]{1,0:T(8,128)} %get-tuple-element.130.first_ref, ...), custom_call_target="tpu_custom_call" | custom-call | flops 1024 | bytes 1024 | tf_op jit(solution)/shard_map/pallas_call | solution.py:246
  99.5 1.1 bitcast_add_fusion.2
  100.6 1.1 bitcast_add_fusion.3
  101.7 4.0 %collective-permute-done.17 = bf16[2,512,256]{2,1,0:T(8,128)(2,1)S(1)} collective-permute-done((bf16[2,512,256]{2,1,0:T(8,128)(2,1)}, bf16[2,512,256]{2,1,0:T(8,128)(2,1)S(1)}, u32[]{:S(2)}, u32[]{:S(2)}) %collective-permute-start.17) | collective-permute-done | bytes 524320 | tf_op jit(solution)/shard_map/ppermute | solution.py:24
  105.7 3.4 %collective-permute-done.18 = bf16[2,512,256]{2,1,0:T(8,128)(2,1)S(1)} collective-permute-done((bf16[2,512,256]{2,1,0:T(8,128)(2,1)}, bf16[2,512,256]{2,1,0:T(8,128)(2,1)S(1)}, u32[]{:S(2)}, u32[]{:S(2)}) %collective-permute-start.18) | collective-permute-done | bytes 524320 | tf_op jit(solution)/shard_map/ppermute | solution.py:24
  111.0 7.7 %shard_map.134.rest_0_ = bf16[512,8192]{1,0:T(8,128)(2,1)} custom-call(s32[4]{0:T(128)S(1)} %get-tuple-element.166.places_ref, bf16[512,8192]{1,0:T(8,128)(2,1)} %resid_ref.3, bf16[4,1024,512]{2,1,0:T(8,128)(2,1)} %get-tuple-element.129.weight_ref, bf16[512,512]{1,0:T(8,128)(2,1)S(1)} %get-tuple-element.131.cot_ref, f32[512,1]{1,0:T(8,128)S(1)} %get-tuple-element.149.coef_ref), custom_call_target="tpu_custom_call" | custom-call | flops 1024 | bytes 1024 | tf_op jit(solution)/shard_map/pallas_call | solution.py:246
  119.9 7.7 %shard_map.135 = bf16[512,8192]{1,0:T(8,128)(2,1)} custom-call(s32[4]{0:T(128)S(1)} %pad_add_fusion.places_ref, bf16[512,8192]{1,0:T(8,128)(2,1)} %resid_ref.3, bf16[4,1024,512]{2,1,0:T(8,128)(2,1)} %collective-permute-done.16.weight_ref, bf16[512,512]{1,0:T(8,128)(2,1)S(1)} %get-tuple-element.131.cot_ref, ...), custom_call_target="tpu_custom_call", output_to_operand_aliasing={{}: (5, {})} | custom-call | flops 1024 | bytes 1024 | tf_op jit(solution)/shard_map/pallas_call | solution.py:246
  127.6 5.6 %collective-permute-done.24 = bf16[512,256]{1,0:T(8,128)(2,1)S(1)} collective-permute-done((bf16[512,256]{1,0:T(8,128)(2,1)S(1)}, bf16[512,256]{1,0:T(8,128)(2,1)S(1)}, u32[]{:S(2)}, u32[]{:S(2)}) %collective-permute-start.24) | collective-permute-done | bytes 262176 | tf_op jit(solution)/shard_map/ppermute | solution.py:24
  (87 shorter events, 21.2 us)
Async XLA Ops:
  0.6 22.5 %copy-start.13 = (s32[8]{0:T(128)S(1)}, s32[8]{0:T(128)}, u32[]{:S(2)}) copy-start(s32[8]{0:T(128)} %param.19) | copy-start | bytes 100
  2.1 5.4 %collective-permute-start = (f32[1,52,128]{2,1,0:T(8,128)S(1)}, f32[1,52,128]{2,1,0:T(8,128)S(1)}, u32[]{:S(2)}, u32[]{:S(2)}) collective-permute-start(f32[1,52,128]{2,1,0:T(8,128)S(1)} %maximum_bitcast_fusion), channel_id=1, source_target_pairs={{0,1},{1,0},{2,3},{3,2},{4,5},{5,4},{6,7},{7,6},{8,9},{9,8},{10,11... | collective-permute-start | bytes 79880 | tf_op jit(solution)/shard_map/ppermute | solution.py:29
  7.6 12.3 %collective-permute-start.1 = (bf16[256,512]{1,0:T(8,128)(2,1)}, bf16[256,512]{1,0:T(8,128)(2,1)S(1)}, u32[]{:S(2)}, u32[]{:S(2)}) collective-permute-start(bf16[256,512]{1,0:T(8,128)(2,1)} %multiply_convert_fusion), channel_id=1, source_target_pairs={{0,1},{1,2},{2,3},{3,0},{4,5},{5,6},{6,7},{7,4},{8,9},{9,10},{10,1... | collective-permute-start | bytes 786440 | tf_op jit(solution)/shard_map/ppermute | solution.py:24
  9.0 10.9 %collective-permute-start.2 = (bf16[256,512]{1,0:T(8,128)(2,1)}, bf16[256,512]{1,0:T(8,128)(2,1)S(1)}, u32[]{:S(2)}, u32[]{:S(2)}) collective-permute-start(bf16[256,512]{1,0:T(8,128)(2,1)} %multiply_convert_fusion), channel_id=1, source_target_pairs={{0,8},{8,0},{1,9},{9,1},{2,10},{10,2},{3,11},{11,3},{4,12},{12,4},... | collective-permute-start | bytes 786440 | tf_op jit(solution)/shard_map/ppermute | solution.py:24
  10.5 9.3 %collective-permute-start.3 = (f32[2,52,128]{2,1,0:T(8,128)S(1)}, f32[2,52,128]{2,1,0:T(8,128)S(1)}, u32[]{:S(2)}, u32[]{:S(2)}) collective-permute-start(f32[2,52,128]{2,1,0:T(8,128)S(1)} %pad_maximum_fusion.5), channel_id=1, source_target_pairs={{0,2},{1,3},{2,0},{3,1},{4,6},{5,7},{6,4},{7,5},{8,10},{9,11},{10,... | collective-permute-start | bytes 159752 | tf_op jit(solution)/shard_map/ppermute | solution.py:29
  19.9 9.2 %collective-permute-start.4 = (bf16[256,512]{1,0:T(8,128)(2,1)S(1)}, bf16[256,512]{1,0:T(8,128)(2,1)S(1)}, u32[]{:S(2)}, u32[]{:S(2)}) collective-permute-start(bf16[256,512]{1,0:T(8,128)(2,1)S(1)} %collective-permute-done.1), channel_id=1, source_target_pairs={{0,16},{16,0},{1,17},{17,1},{2,18},{18,2},{3,19},{19,3},{4,20},{20... | collective-permute-start | bytes 786440 | tf_op jit(solution)/shard_map/ppermute | solution.py:24
  21.5 8.3 %collective-permute-start.5 = (bf16[256,512]{1,0:T(8,128)(2,1)}, bf16[256,512]{1,0:T(8,128)(2,1)}, u32[]{:S(2)}, u32[]{:S(2)}) collective-permute-start(bf16[256,512]{1,0:T(8,128)(2,1)} %multiply_convert_fusion), channel_id=1, source_target_pairs={{0,3},{1,0},{2,1},{3,2},{4,7},{5,4},{6,5},{7,6},{8,11},{9,8},{10,9... | collective-permute-start | bytes 786440 | tf_op jit(solution)/shard_map/ppermute | solution.py:24
  25.5 15.4 %collective-permute-start.7 = (bf16[2,256,512]{2,1,0:T(8,128)(2,1)S(1)}, bf16[2,256,512]{2,1,0:T(8,128)(2,1)S(1)}, u32[]{:S(2)}, u32[]{:S(2)}) collective-permute-start(bf16[2,256,512]{2,1,0:T(8,128)(2,1)S(1)} %pad_maximum_fusion.rest_0_), channel_id=1, source_target_pairs={{0,16},{16,0},{1,17},{17,1},{2,18},{18,2},{3,19},{19,3},{4,20},{20... | collective-permute-start | bytes 1572872 | tf_op jit(solution)/shard_map/ppermute | solution.py:24
  29.8 18.5 %collective-permute-start.8 = (bf16[2,256,512]{2,1,0:T(8,128)(2,1)S(1)}, bf16[2,256,512]{2,1,0:T(8,128)(2,1)S(1)}, u32[]{:S(2)}, u32[]{:S(2)}) collective-permute-start(bf16[2,256,512]{2,1,0:T(8,128)(2,1)S(1)} %pad_maximum_fusion.1.rest_2_), channel_id=1, source_target_pairs={{0,8},{8,0},{1,9},{9,1},{2,10},{10,2},{3,11},{11,3},{4,12},{12,4},... | collective-permute-start | bytes 1572872 | tf_op jit(solution)/shard_map/ppermute | solution.py:24
  29.9 12.9 %collective-permute-start.6 = (bf16[256,512]{1,0:T(8,128)(2,1)}, bf16[256,512]{1,0:T(8,128)(2,1)}, u32[]{:S(2)}, u32[]{:S(2)}) collective-permute-start(bf16[256,512]{1,0:T(8,128)(2,1)} %multiply_convert_fusion), channel_id=1, source_target_pairs={{0,2},{1,3},{2,0},{3,1},{4,6},{5,7},{6,4},{7,5},{8,10},{9,11},{10,... | collective-permute-start | bytes 786440 | tf_op jit(solution)/shard_map/ppermute | solution.py:24
  30.2 18.1 %collective-permute-start.9 = (bf16[256,512]{1,0:T(8,128)(2,1)}, bf16[256,512]{1,0:T(8,128)(2,1)}, u32[]{:S(2)}, u32[]{:S(2)}) collective-permute-start(bf16[256,512]{1,0:T(8,128)(2,1)} %collective-permute-done.5), channel_id=1, source_target_pairs={{0,8},{8,0},{1,9},{9,1},{2,10},{10,2},{3,11},{11,3},{4,12},{12,4},... | collective-permute-start | bytes 786440 | tf_op jit(solution)/shard_map/ppermute | solution.py:24
  48.3 8.9 %collective-permute-start.11 = (bf16[4,4,512,256]{3,2,1,0:T(8,128)(2,1)}, bf16[4,4,512,256]{3,2,1,0:T(8,128)(2,1)}, u32[]{:S(2)}, u32[]{:S(2)}) collective-permute-start(bf16[4,4,512,256]{3,2,1,0:T(8,128)(2,1)} %shard_map.130), channel_id=1, source_target_pairs={{0,4},{4,0},{1,5},{5,1},{2,6},{6,2},{3,7},{7,3},{8,12},{12,8},{9,1... | collective-permute-start | bytes 12582920 | tf_op jit(solution)/shard_map/ppermute | solution.py:24
  48.3 8.9 %collective-permute-start.10 = (bf16[256,512]{1,0:T(8,128)(2,1)}, bf16[256,512]{1,0:T(8,128)(2,1)S(1)}, u32[]{:S(2)}, u32[]{:S(2)}) collective-permute-start(bf16[256,512]{1,0:T(8,128)(2,1)} %collective-permute-done.6), channel_id=1, source_target_pairs={{0,16},{16,0},{1,17},{17,1},{2,18},{18,2},{3,19},{19,3},{4,20},{20... | collective-permute-start | bytes 786440 | tf_op jit(solution)/shard_map/ppermute | solution.py:24
  58.2 14.7 %collective-permute-start.15 = (bf16[2,256,512]{2,1,0:T(8,128)(2,1)S(1)}, bf16[2,256,512]{2,1,0:T(8,128)(2,1)}, u32[]{:S(2)}, u32[]{:S(2)}) collective-permute-start(bf16[2,256,512]{2,1,0:T(8,128)(2,1)S(1)} %pad_maximum_fusion.3.rest_6_), channel_id=1, source_target_pairs={{0,8},{8,0},{1,9},{9,1},{2,10},{10,2},{3,11},{11,3},{4,12},{12,4},... | collective-permute-start | bytes 1572872 | tf_op jit(solution)/shard_map/ppermute | solution.py:24
  59.6 14.2 %collective-permute-start.14 = (bf16[2,256,512]{2,1,0:T(8,128)(2,1)S(1)}, bf16[2,256,512]{2,1,0:T(8,128)(2,1)}, u32[]{:S(2)}, u32[]{:S(2)}) collective-permute-start(bf16[2,256,512]{2,1,0:T(8,128)(2,1)S(1)} %pad_maximum_fusion.2.rest_4_), channel_id=1, source_target_pairs={{0,16},{16,0},{1,17},{17,1},{2,18},{18,2},{3,19},{19,3},{4,20},{20... | collective-permute-start | bytes 1572872 | tf_op jit(solution)/shard_map/ppermute | solution.py:24
  60.3 31.5 %copy-start.5 = (f32[512,1]{1,0:T(8,128)S(1)}, f32[512,1]{1,0:T(8,128)}, u32[]{:S(2)}) copy-start(f32[512,1]{1,0:T(8,128)} %copy-done.4) | copy-start | bytes 6148
  68.6 15.1 %collective-permute-start.12 = (bf16[2,512,256]{2,1,0:T(8,128)(2,1)}, bf16[2,512,256]{2,1,0:T(8,128)(2,1)}, u32[]{:S(2)}, u32[]{:S(2)}) collective-permute-start(bf16[2,512,256]{2,1,0:T(8,128)(2,1)} %get-tuple-element.102), channel_id=1, source_target_pairs={{0,8},{8,0},{1,9},{9,1},{2,10},{10,2},{3,11},{11,3},{4,12},{12,4},... | collective-permute-start | bytes 1572872 | tf_op jit(solution)/shard_map/ppermute | solution.py:24
  70.4 13.8 %collective-permute-start.13 = (bf16[2,512,256]{2,1,0:T(8,128)(2,1)}, bf16[2,512,256]{2,1,0:T(8,128)(2,1)}, u32[]{:S(2)}, u32[]{:S(2)}) collective-permute-start(bf16[2,512,256]{2,1,0:T(8,128)(2,1)} %get-tuple-element.103), channel_id=1, source_target_pairs={{0,16},{16,0},{1,17},{17,1},{2,18},{18,2},{3,19},{19,3},{4,20},{20... | collective-permute-start | bytes 1572872 | tf_op jit(solution)/shard_map/ppermute | solution.py:24
  83.7 15.7 %copy-start.11 = (bf16[2,512,256]{2,1,0:T(8,128)(2,1)S(1)}, bf16[2,512,256]{2,1,0:T(8,128)(2,1)}, u32[]{:S(2)}) copy-start(bf16[2,512,256]{2,1,0:T(8,128)(2,1)} %get-tuple-element.137) | copy-start | bytes 1572868
  84.3 7.5 %collective-permute-start.16 = (bf16[4,1024,512]{2,1,0:T(8,128)(2,1)}, bf16[4,1024,512]{2,1,0:T(8,128)(2,1)}, u32[]{:S(2)}, u32[]{:S(2)}) collective-permute-start(bf16[4,1024,512]{2,1,0:T(8,128)(2,1)} %get-tuple-element.129.weight_ref), channel_id=1, source_target_pairs={{0,4},{4,0},{1,5},{5,1},{2,6},{6,2},{3,7},{7,3},{8,12},{12,8},{9,1... | collective-permute-start | bytes 12582920 | tf_op jit(solution)/shard_map/ppermute | solution.py:24
  85.3 15.3 %copy-start.9 = (bf16[2,512,256]{2,1,0:T(8,128)(2,1)S(1)}, bf16[2,512,256]{2,1,0:T(8,128)(2,1)}, u32[]{:S(2)}) copy-start(bf16[2,512,256]{2,1,0:T(8,128)(2,1)} %get-tuple-element.139) | copy-start | bytes 1572868
  85.3 14.2 %collective-permute-start.20 = (bf16[512,256]{1,0:T(8,128)(2,1)S(1)}, bf16[512,256]{1,0:T(8,128)(2,1)}, u32[]{:S(2)}, u32[]{:S(2)}) collective-permute-start(bf16[512,256]{1,0:T(8,128)(2,1)S(1)} %fusion.6), channel_id=1, source_target_pairs={{0,8},{8,0},{1,9},{9,1},{2,10},{10,2},{3,11},{11,3},{4,12},{12,4},... | collective-permute-start | bytes 786440 | tf_op jit(solution)/shard_map/ppermute | solution.py:24
  89.3 19.8 %copy-start.12 = (bf16[2,512,256]{2,1,0:T(8,128)(2,1)S(1)}, bf16[2,512,256]{2,1,0:T(8,128)(2,1)}, u32[]{:S(2)}) copy-start(bf16[2,512,256]{2,1,0:T(8,128)(2,1)} %get-tuple-element.146) | copy-start | bytes 1572868
  89.3 10.2 %collective-permute-start.19 = (bf16[512,256]{1,0:T(8,128)(2,1)}, bf16[512,256]{1,0:T(8,128)(2,1)}, u32[]{:S(2)}, u32[]{:S(2)}) collective-permute-start(bf16[512,256]{1,0:T(8,128)(2,1)} %fusion.5), channel_id=1, source_target_pairs={{0,16},{16,0},{1,17},{17,1},{2,18},{18,2},{3,19},{19,3},{4,20},{20... | collective-permute-start | bytes 786440 | tf_op jit(solution)/shard_map/ppermute | solution.py:24
  89.3 16.4 %collective-permute-start.17 = (bf16[2,512,256]{2,1,0:T(8,128)(2,1)}, bf16[2,512,256]{2,1,0:T(8,128)(2,1)S(1)}, u32[]{:S(2)}, u32[]{:S(2)}) collective-permute-start(bf16[2,512,256]{2,1,0:T(8,128)(2,1)} %get-tuple-element.135), channel_id=1, source_target_pairs={{0,8},{8,0},{1,9},{9,1},{2,10},{10,2},{3,11},{11,3},{4,12},{12,4},... | collective-permute-start | bytes 1572872 | tf_op jit(solution)/shard_map/ppermute | solution.py:24
  89.8 19.3 %collective-permute-start.18 = (bf16[2,512,256]{2,1,0:T(8,128)(2,1)}, bf16[2,512,256]{2,1,0:T(8,128)(2,1)S(1)}, u32[]{:S(2)}, u32[]{:S(2)}) collective-permute-start(bf16[2,512,256]{2,1,0:T(8,128)(2,1)} %get-tuple-element.136), channel_id=1, source_target_pairs={{0,16},{16,0},{1,17},{17,1},{2,18},{18,2},{3,19},{19,3},{4,20},{20... | collective-permute-start | bytes 1572872 | tf_op jit(solution)/shard_map/ppermute | solution.py:24
  91.8 17.8 %copy-start.7 = (bf16[2,512,256]{2,1,0:T(8,128)(2,1)S(1)}, bf16[2,512,256]{2,1,0:T(8,128)(2,1)}, u32[]{:S(2)}) copy-start(bf16[2,512,256]{2,1,0:T(8,128)(2,1)} %get-tuple-element.134) | copy-start | bytes 1572868
  109.2 9.5 %collective-permute-start.22 = (bf16[512,256]{1,0:T(8,128)(2,1)S(1)}, bf16[512,256]{1,0:T(8,128)(2,1)S(1)}, u32[]{:S(2)}, u32[]{:S(2)}) collective-permute-start(bf16[512,256]{1,0:T(8,128)(2,1)S(1)} %fusion.8), channel_id=1, source_target_pairs={{0,8},{8,0},{1,9},{9,1},{2,10},{10,2},{3,11},{11,3},{4,12},{12,4},... | collective-permute-start | bytes 786440 | tf_op jit(solution)/shard_map/ppermute | solution.py:24
  109.7 9.1 %collective-permute-start.21 = (bf16[512,256]{1,0:T(8,128)(2,1)S(1)}, bf16[512,256]{1,0:T(8,128)(2,1)S(1)}, u32[]{:S(2)}, u32[]{:S(2)}) collective-permute-start(bf16[512,256]{1,0:T(8,128)(2,1)S(1)} %fusion.7), channel_id=1, source_target_pairs={{0,16},{16,0},{1,17},{17,1},{2,18},{18,2},{3,19},{19,3},{4,20},{20... | collective-permute-start | bytes 786440 | tf_op jit(solution)/shard_map/ppermute | solution.py:24
  110.0 17.6 %collective-permute-start.23 = (bf16[512,256]{1,0:T(8,128)(2,1)S(1)}, bf16[512,256]{1,0:T(8,128)(2,1)S(1)}, u32[]{:S(2)}, u32[]{:S(2)}) collective-permute-start(bf16[512,256]{1,0:T(8,128)(2,1)S(1)} %bitcast_add_fusion.2), channel_id=1, source_target_pairs={{0,3},{1,0},{2,1},{3,2},{4,7},{5,4},{6,5},{7,6},{8,11},{9,8},{10,9... | collective-permute-start | bytes 786440 | tf_op jit(solution)/shard_map/ppermute | solution.py:24
  110.9 22.3 %collective-permute-start.24 = (bf16[512,256]{1,0:T(8,128)(2,1)S(1)}, bf16[512,256]{1,0:T(8,128)(2,1)S(1)}, u32[]{:S(2)}, u32[]{:S(2)}) collective-permute-start(bf16[512,256]{1,0:T(8,128)(2,1)S(1)} %bitcast_add_fusion.3), channel_id=1, source_target_pairs={{0,2},{1,3},{2,0},{3,1},{4,6},{5,7},{6,4},{7,5},{8,10},{9,11},{10,... | collective-permute-start | bytes 786440 | tf_op jit(solution)/shard_map/ppermute | solution.py:24
  118.8 14.4 %collective-permute-start.25 = (bf16[512,256]{1,0:T(8,128)(2,1)S(1)}, bf16[512,256]{1,0:T(8,128)(2,1)S(1)}, u32[]{:S(2)}, u32[]{:S(2)}) collective-permute-start(bf16[512,256]{1,0:T(8,128)(2,1)S(1)} %fusion.1), channel_id=1, source_target_pairs={{0,1},{1,2},{2,3},{3,0},{4,5},{5,6},{6,7},{7,4},{8,9},{9,10},{10,1... | collective-permute-start | bytes 786440 | tf_op jit(solution)/shard_map/ppermute | solution.py:24
  (9 other events, 69.1 us)

commit v10 on v9

--- a/solution.py
+++ b/solution.py
@@ -49,7 +49,7 @@
 
 
 def inner_first(chunk):
-    return chunk % 2 == 0
+    return chunk % 4 in (0, 3)
 
 
 def theirs_kernel(places_ref, cot_ref, *rest):
@@ -226,7 +226,8 @@
 
 def weight_call(kernel, places, residual, weight, wholes, out_shape, earlier=None):
     tokens, width = residual.shape
-    steps, depth, features = weight.shape
+    _, depth, features = weight.shape
+    steps = places.shape[0]
     scratch = []
     if isinstance(out_shape, list):
         out_specs = [whole_block(array) for array in out_shape]
@@ -516,25 +517,29 @@
     later[0], coefficient = lax.optimization_barrier((later[0], coefficient))
     sums = dict(zip(pairs[0], summed(sides[0], got[0], later[0])))
     last = [swap(sums[k].astype(BF16), "tp", k) for k in pairs[0]]
-    got[1:], coefficient, sums = lax.optimization_barrier((got[1:], coefficient, sums))
-    later += [second_round(side, parts) for side, parts in zip(sides[1:], got[1:])]
     if in_place:
         grad_shape = jax.ShapeDtypeStruct((rows_here, width), BF16)
         resid_grad = weight_call(
             grad_kernel, places[0], residual, in_hbm(own_weight), [cot, coefficient], grad_shape
         )
-        later[1], coefficient, resid_grad = lax.optimization_barrier((later[1], coefficient, resid_grad))
+        got[1:], resid_grad = lax.optimization_barrier((got[1:], resid_grad))
     else:
         normed_grad = lax.dot_general(
             cot, weight, (((1,), (1,)), ((), ())), preferred_element_type=F32
         )
         resid_grad = (normed_grad - residual.astype(F32) * coefficient).astype(BF16)
+    later += [second_round(side, parts) for side, parts in zip(sides[1:], got[1:])]
+    if in_place:
+        resid_grad = weight_call(
+            grad_kernel, places[1][:2], residual, other_weight, [cot, coefficient], grad_shape, resid_grad
+        )
+        later[1], last, resid_grad = lax.optimization_barrier((later[1], last, resid_grad))
     for pair, *rounds in zip(pairs[1:], sides[1:], got[1:], later[1:]):
         sums.update(zip(pair, summed(*rounds)))
     last += [swap(sums[k].astype(BF16), "tp", k) for k in backward[2:-1]]
     if in_place:
         resid_grad = weight_call(
-            grad_kernel, places[1], residual, other_weight, [cot, coefficient], grad_shape, resid_grad
+            grad_kernel, places[1][2:], residual, other_weight, [cot, coefficient], grad_shape, resid_grad
         )
     grad_rows = widen([sums[0]] + last)
     late_gain, late_weight, grad_rows = lax.optimization_barrier((norm_gain, value_weight, grad_rows))

time: 136 us -> 131 us (0.963)
  waiting for transfers between devices: 35.9 us -> 26 us
  starting transfers between devices: 26.5 us -> 29.7 us
  Pallas kernels: 47.9 us -> 49.5 us
    ppermute x24, waiting for transfers between devices: 34.2 us -> 23.6 us  [swap(): lax.ppermute(value, axis, [(place, (place + step) % size) for place in ra...]
    ppermute x24, starting transfers between devices: 20.9 us -> 24.1 us  [swap(): lax.ppermute(value, axis, [(place, (place + step) % size) for place in ra...]
    convert_element_type x0 -> x2, other arithmetic: none -> 2.27 us  [per_device(): last = [swap(sums[k].astype(BF16), 'tp', k) for k in pairs[0]]]
    add x3 -> x1, other arithmetic: 2.47 us -> 0.22 us  [widen(): return functools.reduce(jnp.add, [part.astype(F32) for part in parts])]
    pallas_call x3 -> x4, Pallas kernels: 23 us -> 24.6 us  [weight_call(): pl.pallas_call(kernel, out_shape=out_shape, grid_spec=pltpu.PrefetchScala...]
  transfers between devices with their start and end apart: 26 -> 26, of which waited for: 13 -> 10; matrix products, arithmetic and copies ran while one was open for 12% -> 13% of each run, Pallas kernels for 35% -> 38%
where the time goes in v10:
time: 131 us; the launch traced here: 130 us
  Pallas kernels  49.5 us (38%)
  starting transfers between devices  29.7 us (23%)
  waiting for transfers between devices  26 us (20%)
  other arithmetic  19.4 us (15%)
  local copies, waits for them, and re-layouts  4.95 us (4%)
    pallas_call x4, Pallas kernels, weight_call(): pl.pallas_call(kernel, out_shape=out_shape, grid_spec=pltpu.PrefetchScala...  24.6 us
    ppermute x24, starting transfers between devices, swap(): lax.ppermute(value, axis, [(place, (place + step) % size) for place in ra...  24.1 us
    ppermute x24, waiting for transfers between devices, swap(): lax.ppermute(value, axis, [(place, (place + step) % size) for place in ra...  23.6 us
    pallas_call x2, Pallas kernels, grad_product(): pl.pallas_call(kernel, out_shape=out_shape, grid_spec=pltpu.PrefetchScala...  14.9 us
    pallas_call x1, Pallas kernels, first_value(): pl.pallas_call(functools.partial(value_kernel, inner_flags), out_shape=[t...  7.87 us
    ppermute x2, starting transfers between devices, trade(): lax.ppermute(value, axis, [(place, place ^ mask) for place in range(size)])  5.61 us
    reduce_sum x1, other arithmetic, per_device(): squares = jnp.sum(resid_wide * resid_wide, axis=1, keepdims=True)  5.1 us
    unnamed x31, local copies, waits for them, and re-layouts  3.91 us
  transfers between devices with their start and end apart: 26, of which 10 were waited for; matrix products, arithmetic and copies ran while one was open for 13% of the time, Pallas kernels for 38%

profile of v10, /device:TPU:0, one launch (start us, length us, event | category | flops | bytes accessed | tf_op | source)
XLA Modules:
  0.0 130.4 jit_solution(3231422169456816112)
XLA Ops:
  2.1 3.0 %collective-permute-start = (f32[1,52,128]{2,1,0:T(8,128)S(1)}, f32[1,52,128]{2,1,0:T(8,128)S(1)}, u32[]{:S(2)}, u32[]{:S(2)}) collective-permute-start(f32[1,52,128]{2,1,0:T(8,128)S(1)} %maximum_bitcast_fusion), channel_id=1, source_target_pairs={{0,1},{1,0},{2,3},{3,2},{4,5},{5,4},{6,7},{7,6},{8,9},{9,8},{10,11... | collective-permute-start | bytes 79880 | tf_op jit(solution)/shard_map/ppermute | solution.py:29
  5.8 1.8 %multiply_convert_fusion = bf16[256,512]{1,0:T(8,128)(2,1)} fusion(bf16[256,512]{1,0:T(8,128)(2,1)} %param.12, f32[256]{0:T(256)S(1)} %convert_element_type.135), kind=kLoop, calls=%fused_computation.22 | loop fusion | flops 393216 | bytes 525312 | tf_op jit(solution)/shard_map/convert_element_type | solution.py:360
  7.6 1.6 %collective-permute-start.2 = (bf16[256,512]{1,0:T(8,128)(2,1)}, bf16[256,512]{1,0:T(8,128)(2,1)S(1)}, u32[]{:S(2)}, u32[]{:S(2)}) collective-permute-start(bf16[256,512]{1,0:T(8,128)(2,1)} %multiply_convert_fusion), channel_id=1, source_target_pairs={{0,8},{8,0},{1,9},{9,1},{2,10},{10,2},{3,11},{11,3},{4,12},{12,4},... | collective-permute-start | bytes 786440 | tf_op jit(solution)/shard_map/ppermute | solution.py:24
  9.1 1.4 %collective-permute-start.1 = (bf16[256,512]{1,0:T(8,128)(2,1)}, bf16[256,512]{1,0:T(8,128)(2,1)S(1)}, u32[]{:S(2)}, u32[]{:S(2)}) collective-permute-start(bf16[256,512]{1,0:T(8,128)(2,1)} %multiply_convert_fusion), channel_id=1, source_target_pairs={{0,1},{1,2},{2,3},{3,0},{4,5},{5,6},{6,7},{7,4},{8,9},{9,10},{10,1... | collective-permute-start | bytes 786440 | tf_op jit(solution)/shard_map/ppermute | solution.py:24
  10.5 2.6 %collective-permute-start.3 = (f32[2,52,128]{2,1,0:T(8,128)S(1)}, f32[2,52,128]{2,1,0:T(8,128)S(1)}, u32[]{:S(2)}, u32[]{:S(2)}) collective-permute-start(f32[2,52,128]{2,1,0:T(8,128)S(1)} %pad_maximum_fusion.5), channel_id=1, source_target_pairs={{0,2},{1,3},{2,0},{3,1},{4,6},{5,7},{6,4},{7,5},{8,10},{9,11},{10,... | collective-permute-start | bytes 159752 | tf_op jit(solution)/shard_map/ppermute | solution.py:29
  13.1 5.1 %multiply_reduce_fusion = f32[512]{0:T(512)S(1)} fusion(bf16[512,8192]{1,0:T(8,128)(2,1)} %resid_ref.4), kind=kLoop, calls=%fused_computation | loop fusion | flops 12582400 | bytes 8390656 | tf_op jit(solution)/shard_map/reduce_sum | solution.py:363
  18.2 2.4 %collective-permute-done.3 = f32[2,52,128]{2,1,0:T(8,128)S(1)} collective-permute-done((f32[2,52,128]{2,1,0:T(8,128)S(1)}, f32[2,52,128]{2,1,0:T(8,128)S(1)}, u32[]{:S(2)}, u32[]{:S(2)}) %collective-permute-start.3) | collective-permute-done | bytes 53280 | tf_op jit(solution)/shard_map/ppermute | solution.py:29
  20.6 2.3 %collective-permute-start.5 = (bf16[256,512]{1,0:T(8,128)(2,1)}, bf16[256,512]{1,0:T(8,128)(2,1)}, u32[]{:S(2)}, u32[]{:S(2)}) collective-permute-start(bf16[256,512]{1,0:T(8,128)(2,1)} %multiply_convert_fusion), channel_id=1, source_target_pairs={{0,3},{1,0},{2,1},{3,2},{4,7},{5,4},{6,5},{7,6},{8,11},{9,8},{10,9... | collective-permute-start | bytes 786440 | tf_op jit(solution)/shard_map/ppermute | solution.py:24
  22.9 1.5 %collective-permute-start.4 = (bf16[256,512]{1,0:T(8,128)(2,1)S(1)}, bf16[256,512]{1,0:T(8,128)(2,1)S(1)}, u32[]{:S(2)}, u32[]{:S(2)}) collective-permute-start(bf16[256,512]{1,0:T(8,128)(2,1)S(1)} %collective-permute-done.1), channel_id=1, source_target_pairs={{0,16},{16,0},{1,17},{17,1},{2,18},{18,2},{3,19},{19,3},{4,20},{20... | collective-permute-start | bytes 786440 | tf_op jit(solution)/shard_map/ppermute | solution.py:24
  27.3 4.4 %collective-permute-done.4 = bf16[256,512]{1,0:T(8,128)(2,1)S(1)} collective-permute-done((bf16[256,512]{1,0:T(8,128)(2,1)S(1)}, bf16[256,512]{1,0:T(8,128)(2,1)S(1)}, u32[]{:S(2)}, u32[]{:S(2)}) %collective-permute-start.4) | collective-permute-done | bytes 262176 | tf_op jit(solution)/shard_map/ppermute | solution.py:24
  32.4 1.9 %collective-permute-start.9 = (bf16[256,512]{1,0:T(8,128)(2,1)}, bf16[256,512]{1,0:T(8,128)(2,1)}, u32[]{:S(2)}, u32[]{:S(2)}) collective-permute-start(bf16[256,512]{1,0:T(8,128)(2,1)} %collective-permute-done.5), channel_id=1, source_target_pairs={{0,16},{16,0},{1,17},{17,1},{2,18},{18,2},{3,19},{19,3},{4,20},{20... | collective-permute-start | bytes 786440 | tf_op jit(solution)/shard_map/ppermute | solution.py:24
  34.5 2.1 %shard_map.129 = (bf16[512,512]{1,0:T(8,128)(2,1)S(1)}, bf16[512,512]{1,0:T(8,128)(2,1)S(1)}, f32[512,1]{1,0:T(8,128)S(1)}) custom-call(s32[2]{0:T(128)S(1)} %pad_add_fusion.1.info_ref, f32[4,52,128]{2,1,0:T(8,128)S(1)} %pad_maximum_fusion.4.shares_ref, f32[512,1]{1,0:T(8,128)S(1)} %copy.18.squares_ref, bf16[512,512]{1,0:T(8,128)(2,1)} %value_cot_ref.1), custom_call_target="tpu_custom_call" | custom-call | flops 1024 | bytes 1024 | tf_op jit(solution)/shard_map/pallas_call | solution.py:309
  36.6 6.6 %shard_map.130 = bf16[4,4,512,256]{3,2,1,0:T(8,128)(2,1)} custom-call(s32[16]{0:T(128)S(1)} %stack.234.places_ref, bf16[512,512]{1,0:T(8,128)(2,1)S(1)} %get-tuple-element.90.cot_ref, bf16[512,8192]{1,0:T(8,128)(2,1)} %resid_ref.4, bf16[512,8192]{1,0:T(8,128)(2,1)} %resid_ref.4, bf16[512,8192]{1,0:T(8,128)(2,1)} %resid_ref.4, bf16[512,8192]{1,0:T(8,128)(2,1)} %resid_ref.4), custom_call_target="tpu_custom_call" | custom-call | flops 1024 | bytes 1024 | tf_op jit(solution)/shard_map/pallas_call | solution.py:115
  44.1 2.1 %collective-permute-done.9 = bf16[256,512]{1,0:T(8,128)(2,1)} collective-permute-done((bf16[256,512]{1,0:T(8,128)(2,1)}, bf16[256,512]{1,0:T(8,128)(2,1)}, u32[]{:S(2)}, u32[]{:S(2)}) %collective-permute-start.9) | collective-permute-done | bytes 262176 | tf_op jit(solution)/shard_map/ppermute | solution.py:24
  46.8 8.3 %collective-permute-done.10 = bf16[256,512]{1,0:T(8,128)(2,1)S(1)} collective-permute-done((bf16[256,512]{1,0:T(8,128)(2,1)}, bf16[256,512]{1,0:T(8,128)(2,1)S(1)}, u32[]{:S(2)}, u32[]{:S(2)}) %collective-permute-start.10) | collective-permute-done | bytes 262176 | tf_op jit(solution)/shard_map/ppermute | solution.py:24
  56.1 1.2 collective-permute-start.15
  59.1 8.3 %shard_map.131 = (bf16[2,512,256]{2,1,0:T(8,128)(2,1)}, bf16[2,512,256]{2,1,0:T(8,128)(2,1)}, bf16[2,512,256]{2,1,0:T(8,128)(2,1)}, bf16[2,512,256]{2,1,0:T(8,12...) custom-call(s32[16]{0:T(128)S(1)} %stack.215.places_ref, ...), custom_call_target="tpu_custom_call" | custom-call | flops 1024 | bytes 1024 | tf_op jit(solution)/shard_map/pallas_call | solution.py:115
  67.4 1.6 %collective-permute-start.12 = (bf16[2,512,256]{2,1,0:T(8,128)(2,1)}, bf16[2,512,256]{2,1,0:T(8,128)(2,1)}, u32[]{:S(2)}, u32[]{:S(2)}) collective-permute-start(bf16[2,512,256]{2,1,0:T(8,128)(2,1)} %get-tuple-element.103), channel_id=1, source_target_pairs={{0,8},{8,0},{1,9},{9,1},{2,10},{10,2},{3,11},{11,3},{4,12},{12,4},... | collective-permute-start | bytes 1572872 | tf_op jit(solution)/shard_map/ppermute | solution.py:24
  69.9 3.5 %collective-permute-done.14.rest_5_ = bf16[2,256,512]{2,1,0:T(8,128)(2,1)} collective-permute-done((bf16[2,256,512]{2,1,0:T(8,128)(2,1)S(1)}, bf16[2,256,512]{2,1,0:T(8,128)(2,1)}, u32[]{:S(2)}, u32[]{:S(2)}) %collective-permute-start.14) | collective-permute-done | bytes 524320 | tf_op jit(solution)/shard_map/ppermute | solution.py:24
  75.5 7.9 %shard_map.132 = (f32[512,512]{1,0:T(8,128)}, bf16[4,1024,512]{2,1,0:T(8,128)(2,1)}) custom-call(s32[4]{0:T(128)S(1)} %get-tuple-element.168.places_ref, s32[4]{0:T(128)S(1)} %get-tuple-element.169.offsets_ref, bf16[512,8192]{1,0:T(8,128)(2,1)} %resid_ref.4, bf16[2,256,512]{2,1,0:T(8,128)(2,1)S(1)} %pad_maximum_fusion.rest_0_, ...), custom_call_target="tpu_custom_call" | custom-call | flops 1024 | bytes 1024 | tf_op jit(solution)/shard_map/pallas_call | solution.py:209
  84.7 1.7 %fusion.7 = bf16[512,256]{1,0:T(8,128)(2,1)} fusion(bf16[2,512,256]{2,1,0:T(8,128)(2,1)} %collective-permute-done.12, bf16[2,512,256]{2,1,0:T(8,128)(2,1)S(1)} %copy-done.10), kind=kLoop, calls=%fused_computation.23 | loop fusion | flops 524288 | bytes 786432 | tf_op jit(solution)/shard_map/convert_element_type | solution.py:445
  87.4 1.8 %collective-permute-start.19 = (bf16[2,512,256]{2,1,0:T(8,128)(2,1)}, bf16[2,512,256]{2,1,0:T(8,128)(2,1)S(1)}, u32[]{:S(2)}, u32[]{:S(2)}) collective-permute-start(bf16[2,512,256]{2,1,0:T(8,128)(2,1)} %get-tuple-element.142), channel_id=1, source_target_pairs={{0,8},{8,0},{1,9},{9,1},{2,10},{10,2},{3,11},{11,3},{4,12},{12,4},... | collective-permute-start | bytes 1572872 | tf_op jit(solution)/shard_map/ppermute | solution.py:24
  89.2 1.2 collective-permute-start.20
  91.0 7.7 %shard_map.133 = (bf16[512,512]{1,0:T(8,128)(2,1)}, f32[512,1]{1,0:T(8,128)S(1)}) custom-call(s32[4]{0:T(128)S(1)} %pad_add_fusion.places_ref, bf16[512,8192]{1,0:T(8,128)(2,1)} %resid_ref.4, bf16[4,1024,512]{2,1,0:T(8,128)(2,1)} %collective-permute-done.16.weight_ref, f32[512,512]{1,0:T(8,128)} %get-tuple-element.131.first_ref, ...), custom_call_target="tpu_custom_call" | custom-call | flops 1024 | bytes 1024 | tf_op jit(solution)/shard_map/pallas_call | solution.py:247
  98.7 1.1 fusion.6
  100.2 1.1 fusion.5
  101.5 7.7 %shard_map.134.rest_0_ = bf16[512,8192]{1,0:T(8,128)(2,1)} custom-call(s32[4]{0:T(128)S(1)} %get-tuple-element.168.places_ref, bf16[512,8192]{1,0:T(8,128)(2,1)} %resid_ref.4, bf16[4,1024,512]{2,1,0:T(8,128)(2,1)} %get-tuple-element.130.weight_ref, bf16[512,512]{1,0:T(8,128)(2,1)S(1)} %get-tuple-element.132.cot_ref, f32[512,1]{1,0:T(8,128)S(1)} %get-tuple-element.140.coef_ref), custom_call_target="tpu_custom_call" | custom-call | flops 1024 | bytes 1024 | tf_op jit(solution)/shard_map/pallas_call | solution.py:247
  110.3 2.1 %collective-permute-start.21 = (bf16[512,256]{1,0:T(8,128)(2,1)S(1)}, bf16[512,256]{1,0:T(8,128)(2,1)S(1)}, u32[]{:S(2)}, u32[]{:S(2)}) collective-permute-start(bf16[512,256]{1,0:T(8,128)(2,1)S(1)} %fusion.9), channel_id=1, source_target_pairs={{0,16},{16,0},{1,17},{17,1},{2,18},{18,2},{3,19},{19,3},{4,20},{20... | collective-permute-start | bytes 786440 | tf_op jit(solution)/shard_map/ppermute | solution.py:24
  112.4 4.6 %shard_map.135.rest_0_ = bf16[512,8192]{1,0:T(8,128)(2,1)} custom-call(s32[2]{0:T(128)S(1)} %pad_add_fusion.5.places_ref, bf16[512,8192]{1,0:T(8,128)(2,1)} %resid_ref.4, bf16[4,1024,512]{2,1,0:T(8,128)(2,1)} %collective-permute-done.16.weight_ref, bf16[512,512]{1,0:T(8,128)(2,1)S(1)} %get-tuple-element.132.cot_ref, ...), custom_call_target="tpu_custom_call", output_to_operand_aliasing={{}: (5, {})} | custom-call | flops 1024 | bytes 1024 | tf_op jit(solution)/shard_map/pallas_call | solution.py:247
  118.5 1.8 %collective-permute-start.25 = (bf16[512,256]{1,0:T(8,128)(2,1)S(1)}, bf16[512,256]{1,0:T(8,128)(2,1)S(1)}, u32[]{:S(2)}, u32[]{:S(2)}) collective-permute-start(bf16[512,256]{1,0:T(8,128)(2,1)S(1)} %fusion.1), channel_id=1, source_target_pairs={{0,1},{1,2},{2,3},{3,0},{4,5},{5,6},{6,7},{7,4},{8,9},{9,10},{10,1... | collective-permute-start | bytes 786440 | tf_op jit(solution)/shard_map/ppermute | solution.py:24
  120.4 4.6 %shard_map.136 = bf16[512,8192]{1,0:T(8,128)(2,1)} custom-call(s32[2]{0:T(128)S(1)} %pad_add_fusion.4.places_ref, bf16[512,8192]{1,0:T(8,128)(2,1)} %resid_ref.4, bf16[4,1024,512]{2,1,0:T(8,128)(2,1)} %collective-permute-done.16.weight_ref, bf16[512,512]{1,0:T(8,128)(2,1)S(1)} %get-tuple-element.132.cot_ref, ...), custom_call_target="tpu_custom_call", output_to_operand_aliasing={{}: (5, {})} | custom-call | flops 1024 | bytes 1024 | tf_op jit(solution)/shard_map/pallas_call | solution.py:247
  125.0 3.3 %collective-permute-done.25 = bf16[512,256]{1,0:T(8,128)(2,1)S(1)} collective-permute-done((bf16[512,256]{1,0:T(8,128)(2,1)S(1)}, bf16[512,256]{1,0:T(8,128)(2,1)S(1)}, u32[]{:S(2)}, u32[]{:S(2)}) %collective-permute-start.25) | collective-permute-done | bytes 262176 | tf_op jit(solution)/shard_map/ppermute | solution.py:24
  (90 shorter events, 21.2 us)
Async XLA Ops:
  0.6 23.8 %copy-start.13 = (s32[8]{0:T(128)S(1)}, s32[8]{0:T(128)}, u32[]{:S(2)}) copy-start(s32[8]{0:T(128)} %param.19) | copy-start | bytes 100
  2.1 5.4 %collective-permute-start = (f32[1,52,128]{2,1,0:T(8,128)S(1)}, f32[1,52,128]{2,1,0:T(8,128)S(1)}, u32[]{:S(2)}, u32[]{:S(2)}) collective-permute-start(f32[1,52,128]{2,1,0:T(8,128)S(1)} %maximum_bitcast_fusion), channel_id=1, source_target_pairs={{0,1},{1,0},{2,3},{3,2},{4,5},{5,4},{6,7},{7,6},{8,9},{9,8},{10,11... | collective-permute-start | bytes 79880 | tf_op jit(solution)/shard_map/ppermute | solution.py:29
  7.6 13.0 %collective-permute-start.2 = (bf16[256,512]{1,0:T(8,128)(2,1)}, bf16[256,512]{1,0:T(8,128)(2,1)S(1)}, u32[]{:S(2)}, u32[]{:S(2)}) collective-permute-start(bf16[256,512]{1,0:T(8,128)(2,1)} %multiply_convert_fusion), channel_id=1, source_target_pairs={{0,8},{8,0},{1,9},{9,1},{2,10},{10,2},{3,11},{11,3},{4,12},{12,4},... | collective-permute-start | bytes 786440 | tf_op jit(solution)/shard_map/ppermute | solution.py:24
  9.1 11.5 %collective-permute-start.1 = (bf16[256,512]{1,0:T(8,128)(2,1)}, bf16[256,512]{1,0:T(8,128)(2,1)S(1)}, u32[]{:S(2)}, u32[]{:S(2)}) collective-permute-start(bf16[256,512]{1,0:T(8,128)(2,1)} %multiply_convert_fusion), channel_id=1, source_target_pairs={{0,1},{1,2},{2,3},{3,0},{4,5},{5,6},{6,7},{7,4},{8,9},{9,10},{10,1... | collective-permute-start | bytes 786440 | tf_op jit(solution)/shard_map/ppermute | solution.py:24
  10.5 10.1 %collective-permute-start.3 = (f32[2,52,128]{2,1,0:T(8,128)S(1)}, f32[2,52,128]{2,1,0:T(8,128)S(1)}, u32[]{:S(2)}, u32[]{:S(2)}) collective-permute-start(f32[2,52,128]{2,1,0:T(8,128)S(1)} %pad_maximum_fusion.5), channel_id=1, source_target_pairs={{0,2},{1,3},{2,0},{3,1},{4,6},{5,7},{6,4},{7,5},{8,10},{9,11},{10,... | collective-permute-start | bytes 159752 | tf_op jit(solution)/shard_map/ppermute | solution.py:29
  20.6 6.7 %collective-permute-start.5 = (bf16[256,512]{1,0:T(8,128)(2,1)}, bf16[256,512]{1,0:T(8,128)(2,1)}, u32[]{:S(2)}, u32[]{:S(2)}) collective-permute-start(bf16[256,512]{1,0:T(8,128)(2,1)} %multiply_convert_fusion), channel_id=1, source_target_pairs={{0,3},{1,0},{2,1},{3,2},{4,7},{5,4},{6,5},{7,6},{8,11},{9,8},{10,9... | collective-permute-start | bytes 786440 | tf_op jit(solution)/shard_map/ppermute | solution.py:24
  22.9 8.8 %collective-permute-start.4 = (bf16[256,512]{1,0:T(8,128)(2,1)S(1)}, bf16[256,512]{1,0:T(8,128)(2,1)S(1)}, u32[]{:S(2)}, u32[]{:S(2)}) collective-permute-start(bf16[256,512]{1,0:T(8,128)(2,1)S(1)} %collective-permute-done.1), channel_id=1, source_target_pairs={{0,16},{16,0},{1,17},{17,1},{2,18},{18,2},{3,19},{19,3},{4,20},{20... | collective-permute-start | bytes 786440 | tf_op jit(solution)/shard_map/ppermute | solution.py:24
  26.7 16.6 %collective-permute-start.7 = (bf16[2,256,512]{2,1,0:T(8,128)(2,1)S(1)}, bf16[2,256,512]{2,1,0:T(8,128)(2,1)S(1)}, u32[]{:S(2)}, u32[]{:S(2)}) collective-permute-start(bf16[2,256,512]{2,1,0:T(8,128)(2,1)S(1)} %pad_maximum_fusion.rest_0_), channel_id=1, source_target_pairs={{0,16},{16,0},{1,17},{17,1},{2,18},{18,2},{3,19},{19,3},{4,20},{20... | collective-permute-start | bytes 1572872 | tf_op jit(solution)/shard_map/ppermute | solution.py:24
  31.8 14.4 %collective-permute-start.8 = (bf16[2,256,512]{2,1,0:T(8,128)(2,1)S(1)}, bf16[2,256,512]{2,1,0:T(8,128)(2,1)S(1)}, u32[]{:S(2)}, u32[]{:S(2)}) collective-permute-start(bf16[2,256,512]{2,1,0:T(8,128)(2,1)S(1)} %pad_maximum_fusion.1.rest_2_), channel_id=1, source_target_pairs={{0,8},{8,0},{1,9},{9,1},{2,10},{10,2},{3,11},{11,3},{4,12},{12,4},... | collective-permute-start | bytes 1572872 | tf_op jit(solution)/shard_map/ppermute | solution.py:24
  32.4 11.7 %collective-permute-start.6 = (bf16[256,512]{1,0:T(8,128)(2,1)}, bf16[256,512]{1,0:T(8,128)(2,1)}, u32[]{:S(2)}, u32[]{:S(2)}) collective-permute-start(bf16[256,512]{1,0:T(8,128)(2,1)} %multiply_convert_fusion), channel_id=1, source_target_pairs={{0,2},{1,3},{2,0},{3,1},{4,6},{5,7},{6,4},{7,5},{8,10},{9,11},{10,... | collective-permute-start | bytes 786440 | tf_op jit(solution)/shard_map/ppermute | solution.py:24
  32.4 13.8 %collective-permute-start.9 = (bf16[256,512]{1,0:T(8,128)(2,1)}, bf16[256,512]{1,0:T(8,128)(2,1)}, u32[]{:S(2)}, u32[]{:S(2)}) collective-permute-start(bf16[256,512]{1,0:T(8,128)(2,1)} %collective-permute-done.5), channel_id=1, source_target_pairs={{0,16},{16,0},{1,17},{17,1},{2,18},{18,2},{3,19},{19,3},{4,20},{20... | collective-permute-start | bytes 786440 | tf_op jit(solution)/shard_map/ppermute | solution.py:24
  46.2 11.1 %copy-start.2 = (bf16[2,256,512]{2,1,0:T(8,128)(2,1)}, bf16[2,256,512]{2,1,0:T(8,128)(2,1)S(1)}, u32[]{:S(2)}) copy-start(bf16[2,256,512]{2,1,0:T(8,128)(2,1)S(1)} %collective-permute-done.8.rest_3_) | copy-start | bytes 1572868
  46.2 8.9 %collective-permute-start.11 = (bf16[4,4,512,256]{3,2,1,0:T(8,128)(2,1)}, bf16[4,4,512,256]{3,2,1,0:T(8,128)(2,1)}, u32[]{:S(2)}, u32[]{:S(2)}) collective-permute-start(bf16[4,4,512,256]{3,2,1,0:T(8,128)(2,1)} %shard_map.130), channel_id=1, source_target_pairs={{0,4},{4,0},{1,5},{5,1},{2,6},{6,2},{3,7},{7,3},{8,12},{12,8},{9,1... | collective-permute-start | bytes 12582920 | tf_op jit(solution)/shard_map/ppermute | solution.py:24
  46.2 8.9 %collective-permute-start.10 = (bf16[256,512]{1,0:T(8,128)(2,1)}, bf16[256,512]{1,0:T(8,128)(2,1)S(1)}, u32[]{:S(2)}, u32[]{:S(2)}) collective-permute-start(bf16[256,512]{1,0:T(8,128)(2,1)} %collective-permute-done.6), channel_id=1, source_target_pairs={{0,8},{8,0},{1,9},{9,1},{2,10},{10,2},{3,11},{11,3},{4,12},{12,4},... | collective-permute-start | bytes 786440 | tf_op jit(solution)/shard_map/ppermute | solution.py:24
  56.1 13.8 %collective-permute-start.15 = (bf16[2,256,512]{2,1,0:T(8,128)(2,1)S(1)}, bf16[2,256,512]{2,1,0:T(8,128)(2,1)}, u32[]{:S(2)}, u32[]{:S(2)}) collective-permute-start(bf16[2,256,512]{2,1,0:T(8,128)(2,1)S(1)} %pad_maximum_fusion.3.rest_6_), channel_id=1, source_target_pairs={{0,16},{16,0},{1,17},{17,1},{2,18},{18,2},{3,19},{19,3},{4,20},{20... | collective-permute-start | bytes 1572872 | tf_op jit(solution)/shard_map/ppermute | solution.py:24
  58.4 15.0 %collective-permute-start.14 = (bf16[2,256,512]{2,1,0:T(8,128)(2,1)S(1)}, bf16[2,256,512]{2,1,0:T(8,128)(2,1)}, u32[]{:S(2)}, u32[]{:S(2)}) collective-permute-start(bf16[2,256,512]{2,1,0:T(8,128)(2,1)S(1)} %pad_maximum_fusion.2.rest_4_), channel_id=1, source_target_pairs={{0,8},{8,0},{1,9},{9,1},{2,10},{10,2},{3,11},{11,3},{4,12},{12,4},... | collective-permute-start | bytes 1572872 | tf_op jit(solution)/shard_map/ppermute | solution.py:24
  59.1 31.9 %copy-start.5 = (f32[512,1]{1,0:T(8,128)S(1)}, f32[512,1]{1,0:T(8,128)}, u32[]{:S(2)}) copy-start(f32[512,1]{1,0:T(8,128)} %copy-done.4) | copy-start | bytes 6148
  67.4 16.0 %collective-permute-start.12 = (bf16[2,512,256]{2,1,0:T(8,128)(2,1)}, bf16[2,512,256]{2,1,0:T(8,128)(2,1)}, u32[]{:S(2)}, u32[]{:S(2)}) collective-permute-start(bf16[2,512,256]{2,1,0:T(8,128)(2,1)} %get-tuple-element.103), channel_id=1, source_target_pairs={{0,8},{8,0},{1,9},{9,1},{2,10},{10,2},{3,11},{11,3},{4,12},{12,4},... | collective-permute-start | bytes 1572872 | tf_op jit(solution)/shard_map/ppermute | solution.py:24
  68.9 14.5 %collective-permute-start.13 = (bf16[2,512,256]{2,1,0:T(8,128)(2,1)}, bf16[2,512,256]{2,1,0:T(8,128)(2,1)}, u32[]{:S(2)}, u32[]{:S(2)}) collective-permute-start(bf16[2,512,256]{2,1,0:T(8,128)(2,1)} %get-tuple-element.104), channel_id=1, source_target_pairs={{0,16},{16,0},{1,17},{17,1},{2,18},{18,2},{3,19},{19,3},{4,20},{20... | collective-permute-start | bytes 1572872 | tf_op jit(solution)/shard_map/ppermute | solution.py:24
  75.5 9.2 %copy-start.10 = (bf16[2,512,256]{2,1,0:T(8,128)(2,1)S(1)}, bf16[2,512,256]{2,1,0:T(8,128)(2,1)}, u32[]{:S(2)}) copy-start(bf16[2,512,256]{2,1,0:T(8,128)(2,1)} %get-tuple-element.135) | copy-start | bytes 1572868
  83.4 15.3 %copy-start.11 = (bf16[2,512,256]{2,1,0:T(8,128)(2,1)S(1)}, bf16[2,512,256]{2,1,0:T(8,128)(2,1)}, u32[]{:S(2)}) copy-start(bf16[2,512,256]{2,1,0:T(8,128)(2,1)} %get-tuple-element.135) | copy-start | bytes 1572868
  83.4 7.6 %collective-permute-start.16 = (bf16[4,1024,512]{2,1,0:T(8,128)(2,1)}, bf16[4,1024,512]{2,1,0:T(8,128)(2,1)}, u32[]{:S(2)}, u32[]{:S(2)}) collective-permute-start(bf16[4,1024,512]{2,1,0:T(8,128)(2,1)} %get-tuple-element.130.weight_ref), channel_id=1, source_target_pairs={{0,4},{4,0},{1,5},{5,1},{2,6},{6,2},{3,7},{7,3},{8,12},{12,8},{9,1... | collective-permute-start | bytes 12582920 | tf_op jit(solution)/shard_map/ppermute | solution.py:24
  84.6 15.7 %copy-start.9 = (bf16[2,512,256]{2,1,0:T(8,128)(2,1)S(1)}, bf16[2,512,256]{2,1,0:T(8,128)(2,1)}, u32[]{:S(2)}) copy-start(bf16[2,512,256]{2,1,0:T(8,128)(2,1)} %get-tuple-element.137) | copy-start | bytes 1572868
  84.6 14.1 %collective-permute-start.18 = (bf16[512,256]{1,0:T(8,128)(2,1)S(1)}, bf16[512,256]{1,0:T(8,128)(2,1)}, u32[]{:S(2)}, u32[]{:S(2)}) collective-permute-start(bf16[512,256]{1,0:T(8,128)(2,1)S(1)} %fusion.8), channel_id=1, source_target_pairs={{0,8},{8,0},{1,9},{9,1},{2,10},{10,2},{3,11},{11,3},{4,12},{12,4},... | collective-permute-start | bytes 786440 | tf_op jit(solution)/shard_map/ppermute | solution.py:24
  86.5 12.2 %collective-permute-start.17 = (bf16[512,256]{1,0:T(8,128)(2,1)}, bf16[512,256]{1,0:T(8,128)(2,1)}, u32[]{:S(2)}, u32[]{:S(2)}) collective-permute-start(bf16[512,256]{1,0:T(8,128)(2,1)} %fusion.7), channel_id=1, source_target_pairs={{0,16},{16,0},{1,17},{17,1},{2,18},{18,2},{3,19},{19,3},{4,20},{20... | collective-permute-start | bytes 786440 | tf_op jit(solution)/shard_map/ppermute | solution.py:24
  87.4 21.8 %collective-permute-start.19 = (bf16[2,512,256]{2,1,0:T(8,128)(2,1)}, bf16[2,512,256]{2,1,0:T(8,128)(2,1)S(1)}, u32[]{:S(2)}, u32[]{:S(2)}) collective-permute-start(bf16[2,512,256]{2,1,0:T(8,128)(2,1)} %get-tuple-element.142), channel_id=1, source_target_pairs={{0,8},{8,0},{1,9},{9,1},{2,10},{10,2},{3,11},{11,3},{4,12},{12,4},... | collective-permute-start | bytes 1572872 | tf_op jit(solution)/shard_map/ppermute | solution.py:24
  89.2 20.0 %collective-permute-start.20 = (bf16[2,512,256]{2,1,0:T(8,128)(2,1)}, bf16[2,512,256]{2,1,0:T(8,128)(2,1)S(1)}, u32[]{:S(2)}, u32[]{:S(2)}) collective-permute-start(bf16[2,512,256]{2,1,0:T(8,128)(2,1)} %get-tuple-element.143), channel_id=1, source_target_pairs={{0,16},{16,0},{1,17},{17,1},{2,18},{18,2},{3,19},{19,3},{4,20},{20... | collective-permute-start | bytes 1572872 | tf_op jit(solution)/shard_map/ppermute | solution.py:24
  99.8 17.2 %collective-permute-start.23 = (bf16[512,256]{1,0:T(8,128)(2,1)S(1)}, bf16[512,256]{1,0:T(8,128)(2,1)S(1)}, u32[]{:S(2)}, u32[]{:S(2)}) collective-permute-start(bf16[512,256]{1,0:T(8,128)(2,1)S(1)} %fusion.6), channel_id=1, source_target_pairs={{0,3},{1,0},{2,1},{3,2},{4,7},{5,4},{6,5},{7,6},{8,11},{9,8},{10,9... | collective-permute-start | bytes 786440 | tf_op jit(solution)/shard_map/ppermute | solution.py:24
  101.4 16.0 %collective-permute-start.24 = (bf16[512,256]{1,0:T(8,128)(2,1)S(1)}, bf16[512,256]{1,0:T(8,128)(2,1)S(1)}, u32[]{:S(2)}, u32[]{:S(2)}) collective-permute-start(bf16[512,256]{1,0:T(8,128)(2,1)S(1)} %fusion.5), channel_id=1, source_target_pairs={{0,2},{1,3},{2,0},{3,1},{4,6},{5,7},{6,4},{7,5},{8,10},{9,11},{10,... | collective-permute-start | bytes 786440 | tf_op jit(solution)/shard_map/ppermute | solution.py:24
  109.3 8.2 %collective-permute-start.22 = (bf16[512,256]{1,0:T(8,128)(2,1)S(1)}, bf16[512,256]{1,0:T(8,128)(2,1)S(1)}, u32[]{:S(2)}, u32[]{:S(2)}) collective-permute-start(bf16[512,256]{1,0:T(8,128)(2,1)S(1)} %fusion.10), channel_id=1, source_target_pairs={{0,8},{8,0},{1,9},{9,1},{2,10},{10,2},{3,11},{11,3},{4,12},{12,4},... | collective-permute-start | bytes 786440 | tf_op jit(solution)/shard_map/ppermute | solution.py:24
  110.3 8.1 %collective-permute-start.21 = (bf16[512,256]{1,0:T(8,128)(2,1)S(1)}, bf16[512,256]{1,0:T(8,128)(2,1)S(1)}, u32[]{:S(2)}, u32[]{:S(2)}) collective-permute-start(bf16[512,256]{1,0:T(8,128)(2,1)S(1)} %fusion.9), channel_id=1, source_target_pairs={{0,16},{16,0},{1,17},{17,1},{2,18},{18,2},{3,19},{19,3},{4,20},{20... | collective-permute-start | bytes 786440 | tf_op jit(solution)/shard_map/ppermute | solution.py:24
  118.5 9.8 %collective-permute-start.25 = (bf16[512,256]{1,0:T(8,128)(2,1)S(1)}, bf16[512,256]{1,0:T(8,128)(2,1)S(1)}, u32[]{:S(2)}, u32[]{:S(2)}) collective-permute-start(bf16[512,256]{1,0:T(8,128)(2,1)S(1)} %fusion.1), channel_id=1, source_target_pairs={{0,1},{1,2},{2,3},{3,0},{4,5},{5,6},{6,7},{7,4},{8,9},{9,10},{10,1... | collective-permute-start | bytes 786440 | tf_op jit(solution)/shard_map/ppermute | solution.py:24
  (9 other events, 50.5 us)

commit v11 on v10

--- a/solution.py
+++ b/solution.py
@@ -123,6 +123,34 @@
     )(*operands)
 
 
+def sum_kernel(counts, *refs):
+    ins, outs = refs[: sum(counts)], refs[sum(counts) :]
+    for n, out_ref in enumerate(outs):
+        first = sum(counts[:n])
+        parts = [ref[...].astype(F32).reshape(out_ref.shape) for ref in ins[first : first + counts[n]]]
+        out_ref[...] = functools.reduce(jnp.add, parts).astype(BF16)
+
+
+def sums_of(groups, slot):
+    shape = groups[0][0].shape[-2:]
+    in_specs = [
+        pl.BlockSpec((1,) + shape, lambda i: (slot, 0, 0))
+        if part.ndim == 3
+        else pl.BlockSpec(shape, lambda i: (0, 0))
+        for parts in groups
+        for part in parts
+    ]
+    return pl.pallas_call(
+        functools.partial(sum_kernel, [len(parts) for parts in groups]),
+        out_shape=[jax.ShapeDtypeStruct(shape, BF16)] * len(groups),
+        grid=(1,),
+        in_specs=in_specs,
+        out_specs=[pl.BlockSpec(shape, lambda i: (0, 0))] * len(groups),
+        cost_estimate=NOMINAL,
+        compiler_params=pltpu.CompilerParams(vmem_limit_bytes=PAIR_VMEM),
+    )(*[part for parts in groups for part in parts])
+
+
 def place_weight(inner_flags, offsets_ref, pieces, weight_ref):
     step = pl.program_id(0)
     at_outer, at_inner = step // 2, lax.rem(step, 2)
@@ -378,8 +406,8 @@
     own_pieces, near = {}, {}
     arrived = {0: gained, 1: swap(gained, "tp", shifts[1])}
     near[0] = near_of(0, gained)
-    arrived[1], near[0], packed, squares, late_gained = lax.optimization_barrier(
-        (arrived[1], near[0], packed, squares, gained)
+    arrived[1], near[0], squares, late_gained = lax.optimization_barrier(
+        (arrived[1], near[0], squares, gained)
     )
     near[1] = near_of(1, arrived[1])
     arrived[2] = swap(late_gained, "tp", shifts[2])
@@ -437,16 +465,19 @@
             for axis, (sends, _) in zip(("inner", "outer"), sides)
         ]
 
-    def second_round(sides, got):
-        later = []
-        for axis, (_, keep), parts in zip(("outer", "inner"), sides, got):
-            later.append(
-                [
-                    swap(widen([part[s] for part in [keep] + parts]).astype(BF16), axis, s)
-                    for s in range(1, lax.axis_size(axis))
-                ]
-            )
-        return later
+    def second_round(sides, got, following=()):
+        axes = ("outer", "inner")
+        groups = [[keep] + parts for (_, keep), parts in zip(sides, got)]
+        if in_place:
+            sent, following = lax.optimization_barrier((sums_of(groups, 1), following))
+            return [[swap(x, axis, 1)] for x, axis in zip(sent, axes)], following
+        return [
+            [
+                swap(widen([part[s] for part in parts]).astype(BF16), axis, s)
+                for s in range(1, lax.axis_size(axis))
+            ]
+            for parts, axis in zip(groups, axes)
+        ], following
 
     def summed(sides, got, later):
         return [
@@ -455,13 +486,11 @@
         ]
 
     theirs = for_others(cot_t)
-    theirs, arrived, own_pieces, near = lax.optimization_barrier(
-        (theirs, arrived, own_pieces, near)
-    )
+    theirs, arrived = lax.optimization_barrier((theirs, arrived))
+    near.update({k: near_of(k, arrived[k]) for k in order[3:]})
+    theirs, own_pieces, near = lax.optimization_barrier((theirs, own_pieces, near))
     other = swap(theirs, "core", 1)
-    for k in order[3:]:
-        near[k] = near_of(k, arrived[k])
-    near, other, own_pieces = lax.optimization_barrier((near, other, own_pieces))
+    near, own_pieces = lax.optimization_barrier((near, own_pieces))
     for k in order[2:]:
         own_pieces[k] = far_of(k, arrived[k], near[k])
     sides = for_us(other)
@@ -493,7 +522,8 @@
         (got[0], sides[1:], total, own_weight)
     )
     other_weight = swap(own_weight, "core", 1)
-    later = [second_round(sides[0], got[0])]
+    first_later, sides[1:] = second_round(sides[0], got[0], sides[1:])
+    later = [first_later]
     got += [first_round(side) for side in sides[1:]]
     if in_place:
         value_proj, coefficient = weight_call(
@@ -515,7 +545,11 @@
         share = jnp.sum(cot.astype(F32) * value_acc, axis=1, keepdims=True)
         coefficient = inv_rms * inv_rms * share * (1.0 / width)
     later[0], coefficient = lax.optimization_barrier((later[0], coefficient))
-    sums = dict(zip(pairs[0], summed(sides[0], got[0], later[0])))
+    if in_place:
+        groups = [[keep] + parts + then for (_, keep), parts, then in zip(sides[0], got[0], later[0])]
+        sums = dict(zip(pairs[0], sums_of(groups, 0)))
+    else:
+        sums = dict(zip(pairs[0], summed(sides[0], got[0], later[0])))
     last = [swap(sums[k].astype(BF16), "tp", k) for k in pairs[0]]
     if in_place:
         grad_shape = jax.ShapeDtypeStruct((rows_here, width), BF16)
@@ -528,7 +562,7 @@
             cot, weight, (((1,), (1,)), ((), ())), preferred_element_type=F32
         )
         resid_grad = (normed_grad - residual.astype(F32) * coefficient).astype(BF16)
-    later += [second_round(side, parts) for side, parts in zip(sides[1:], got[1:])]
+    later += [second_round(side, parts)[0] for side, parts in zip(sides[1:], got[1:])]
     if in_place:
         resid_grad = weight_call(
             grad_kernel, places[1][:2], residual, other_weight, [cot, coefficient], grad_shape, resid_grad

time: 131 us -> 137 us (1.046)
  waiting for transfers between devices: 26 us -> 32.2 us
  other arithmetic: 19.4 us -> 14.2 us
  Pallas kernels: 49.5 us -> 52.7 us
    ppermute x24, waiting for transfers between devices: 23.6 us -> 32.2 us  [swap(): lax.ppermute(value, axis, [(place, (place + step) % size) for place in ra...]
    convert_element_type x6 -> x0, other arithmetic: 5.23 us -> none  [the longest x4 2.96 us: second_round(): widen([part[s] for part in [keep] + parts]).astype(BF16)]
    pallas_call x0 -> x3, Pallas kernels: none -> 3.25 us  [sums_of(): pl.pallas_call(functools.partial(sum_kernel, [len(parts) for parts in gro...]
    ppermute x2, waiting for transfers between devices: 2.37 us -> 0.01 us  [trade(): lax.ppermute(value, axis, [(place, place ^ mask) for place in range(size)])]
    unnamed x31 -> x27, local copies, waits for them, and re-layouts: 3.91 us -> 3.95 us
  transfers between devices with their start and end apart: 26 -> 26, of which waited for: 10 -> 12; matrix products, arithmetic and copies ran while one was open for 13% -> 10% of each run, Pallas kernels for 38% -> 39%
where the time goes in v11:
time: 137 us; the launch traced here: 136 us
  Pallas kernels  52.7 us (38%)
  waiting for transfers between devices  32.2 us (24%)
  starting transfers between devices  30.2 us (22%)
  other arithmetic  14.2 us (10%)
  local copies, waits for them, and re-layouts  5.65 us (4%)
    ppermute x24, waiting for transfers between devices, swap(): lax.ppermute(value, axis, [(place, (place + step) % size) for place in ra...  32.2 us
    pallas_call x4, Pallas kernels, weight_call(): pl.pallas_call(kernel, out_shape=out_shape, grid_spec=pltpu.PrefetchScala...  24.6 us
    ppermute x24, starting transfers between devices, swap(): lax.ppermute(value, axis, [(place, (place + step) % size) for place in ra...  24.5 us
    pallas_call x2, Pallas kernels, grad_product(): pl.pallas_call(kernel, out_shape=out_shape, grid_spec=pltpu.PrefetchScala...  14.9 us
    pallas_call x1, Pallas kernels, first_value(): pl.pallas_call(functools.partial(value_kernel, inner_flags), out_shape=[t...  7.87 us
    ppermute x2, starting transfers between devices, trade(): lax.ppermute(value, axis, [(place, place ^ mask) for place in range(size)])  5.67 us
    reduce_sum x1, other arithmetic, per_device(): squares = jnp.sum(resid_wide * resid_wide, axis=1, keepdims=True)  5.1 us
    unnamed x27, local copies, waits for them, and re-layouts  3.95 us
  transfers between devices with their start and end apart: 26, of which 12 were waited for; matrix products, arithmetic and copies ran while one was open for 10% of the time, Pallas kernels for 39%

profile of v11, /device:TPU:0, one launch (start us, length us, event | category | flops | bytes accessed | tf_op | source)
XLA Modules:
  0.0 135.8 jit_solution(12943224742485993041)
XLA Ops:
  2.1 3.0 %collective-permute-start = (f32[1,52,128]{2,1,0:T(8,128)S(1)}, f32[1,52,128]{2,1,0:T(8,128)S(1)}, u32[]{:S(2)}, u32[]{:S(2)}) collective-permute-start(f32[1,52,128]{2,1,0:T(8,128)S(1)} %maximum_bitcast_fusion), channel_id=1, source_target_pairs={{0,1},{1,0},{2,3},{3,2},{4,5},{5,4},{6,7},{7,6},{8,9},{9,8},{10,11... | collective-permute-start | bytes 79880 | tf_op jit(solution)/shard_map/ppermute | solution.py:29
  5.8 1.8 %multiply_convert_fusion = bf16[256,512]{1,0:T(8,128)(2,1)} fusion(bf16[256,512]{1,0:T(8,128)(2,1)} %param.12, f32[256]{0:T(256)S(1)} %convert_element_type.51), kind=kLoop, calls=%fused_computation.14 | loop fusion | flops 393216 | bytes 525312 | tf_op jit(solution)/shard_map/convert_element_type | solution.py:388
  8.8 1.6 %collective-permute-start.2 = (bf16[256,512]{1,0:T(8,128)(2,1)}, bf16[256,512]{1,0:T(8,128)(2,1)S(1)}, u32[]{:S(2)}, u32[]{:S(2)}) collective-permute-start(bf16[256,512]{1,0:T(8,128)(2,1)} %multiply_convert_fusion), channel_id=1, source_target_pairs={{0,8},{8,0},{1,9},{9,1},{2,10},{10,2},{3,11},{11,3},{4,12},{12,4},... | collective-permute-start | bytes 786440 | tf_op jit(solution)/shard_map/ppermute | solution.py:24
  10.8 5.1 %multiply_reduce_fusion = f32[512]{0:T(512)S(1)} fusion(bf16[512,8192]{1,0:T(8,128)(2,1)} %resid_ref.4), kind=kLoop, calls=%fused_computation | loop fusion | flops 12582400 | bytes 8390656 | tf_op jit(solution)/shard_map/reduce_sum | solution.py:391
  15.9 2.6 %collective-permute-start.5 = (f32[2,52,128]{2,1,0:T(8,128)S(1)}, f32[2,52,128]{2,1,0:T(8,128)S(1)}, u32[]{:S(2)}, u32[]{:S(2)}) collective-permute-start(f32[2,52,128]{2,1,0:T(8,128)S(1)} %pad_maximum_fusion.5), channel_id=1, source_target_pairs={{0,2},{1,3},{2,0},{3,1},{4,6},{5,7},{6,4},{7,5},{8,10},{9,11},{10,... | collective-permute-start | bytes 159752 | tf_op jit(solution)/shard_map/ppermute | solution.py:29
  21.0 1.5 %collective-permute-start.3 = (bf16[256,512]{1,0:T(8,128)(2,1)S(1)}, bf16[256,512]{1,0:T(8,128)(2,1)S(1)}, u32[]{:S(2)}, u32[]{:S(2)}) collective-permute-start(bf16[256,512]{1,0:T(8,128)(2,1)S(1)} %collective-permute-done.1), channel_id=1, source_target_pairs={{0,16},{16,0},{1,17},{17,1},{2,18},{18,2},{3,19},{19,3},{4,20},{20... | collective-permute-start | bytes 786440 | tf_op jit(solution)/shard_map/ppermute | solution.py:24
  24.9 2.2 %collective-permute-done.4 = bf16[256,512]{1,0:T(8,128)(2,1)} collective-permute-done((bf16[256,512]{1,0:T(8,128)(2,1)}, bf16[256,512]{1,0:T(8,128)(2,1)}, u32[]{:S(2)}, u32[]{:S(2)}) %collective-permute-start.4) | collective-permute-done | bytes 262176 | tf_op jit(solution)/shard_map/ppermute | solution.py:24
  27.1 3.1 %collective-permute-done.3 = bf16[256,512]{1,0:T(8,128)(2,1)S(1)} collective-permute-done((bf16[256,512]{1,0:T(8,128)(2,1)S(1)}, bf16[256,512]{1,0:T(8,128)(2,1)S(1)}, u32[]{:S(2)}, u32[]{:S(2)}) %collective-permute-start.3) | collective-permute-done | bytes 262176 | tf_op jit(solution)/shard_map/ppermute | solution.py:24
  31.5 1.6 %collective-permute-start.9 = (bf16[256,512]{1,0:T(8,128)(2,1)}, bf16[256,512]{1,0:T(8,128)(2,1)}, u32[]{:S(2)}, u32[]{:S(2)}) collective-permute-start(bf16[256,512]{1,0:T(8,128)(2,1)} %collective-permute-done.4), channel_id=1, source_target_pairs={{0,16},{16,0},{1,17},{17,1},{2,18},{18,2},{3,19},{19,3},{4,20},{20... | collective-permute-start | bytes 786440 | tf_op jit(solution)/shard_map/ppermute | solution.py:24
  33.1 2.1 %shard_map.129 = (bf16[512,512]{1,0:T(8,128)(2,1)S(1)}, bf16[512,512]{1,0:T(8,128)(2,1)S(1)}, f32[512,1]{1,0:T(8,128)S(1)}) custom-call(s32[2]{0:T(128)S(1)} %pad_add_fusion.1.info_ref, f32[4,52,128]{2,1,0:T(8,128)S(1)} %pad_maximum_fusion.4.shares_ref, f32[512,1]{1,0:T(8,128)S(1)} %copy.18.squares_ref, bf16[512,512]{1,0:T(8,128)(2,1)} %value_cot_ref.1), custom_call_target="tpu_custom_call" | custom-call | flops 1024 | bytes 1024 | tf_op jit(solution)/shard_map/pallas_call | solution.py:337
  35.2 6.6 %shard_map.130 = bf16[4,4,512,256]{3,2,1,0:T(8,128)(2,1)} custom-call(s32[16]{0:T(128)S(1)} %stack.234.places_ref, bf16[512,512]{1,0:T(8,128)(2,1)S(1)} %get-tuple-element.101.cot_ref, bf16[512,8192]{1,0:T(8,128)(2,1)} %resid_ref.4, bf16[512,8192]{1,0:T(8,128)(2,1)} %resid_ref.4, bf16[512,8192]{1,0:T(8,128)(2,1)} %resid_ref.4, bf16[512,8192]{1,0:T(8,128)(2,1)} %resid_ref.4), custom_call_target="tpu_custom_call" | custom-call | flops 1024 | bytes 1024 | tf_op jit(solution)/shard_map/pallas_call | solution.py:115
  41.8 1.6 %collective-permute-start.10 = (bf16[256,512]{1,0:T(8,128)(2,1)}, bf16[256,512]{1,0:T(8,128)(2,1)}, u32[]{:S(2)}, u32[]{:S(2)}) collective-permute-start(bf16[256,512]{1,0:T(8,128)(2,1)} %collective-permute-done.6), channel_id=1, source_target_pairs={{0,8},{8,0},{1,9},{9,1},{2,10},{10,2},{3,11},{11,3},{4,12},{12,4},... | collective-permute-start | bytes 786440 | tf_op jit(solution)/shard_map/ppermute | solution.py:24
  44.6 3.9 %collective-permute-done.10 = bf16[256,512]{1,0:T(8,128)(2,1)} collective-permute-done((bf16[256,512]{1,0:T(8,128)(2,1)}, bf16[256,512]{1,0:T(8,128)(2,1)}, u32[]{:S(2)}, u32[]{:S(2)}) %collective-permute-start.10) | collective-permute-done | bytes 262176 | tf_op jit(solution)/shard_map/ppermute | solution.py:24
  51.3 1.6 %collective-permute-start.14 = (bf16[2,256,512]{2,1,0:T(8,128)(2,1)S(1)}, bf16[2,256,512]{2,1,0:T(8,128)(2,1)}, u32[]{:S(2)}, u32[]{:S(2)}) collective-permute-start(bf16[2,256,512]{2,1,0:T(8,128)(2,1)S(1)} %pad_maximum_fusion.2.rest_4_), channel_id=1, source_target_pairs={{0,8},{8,0},{1,9},{9,1},{2,10},{10,2},{3,11},{11,3},{4,12},{12,4},... | collective-permute-start | bytes 1572872 | tf_op jit(solution)/shard_map/ppermute | solution.py:24
  52.9 3.1 %collective-permute-done.11.rest_4_ = bf16[4,4,512,256]{3,2,1,0:T(8,128)(2,1)} collective-permute-done((bf16[4,4,512,256]{3,2,1,0:T(8,128)(2,1)}, bf16[4,4,512,256]{3,2,1,0:T(8,128)(2,1)}, u32[]{:S(2)}, u32[]{:S(2)}) %collective-permute-start.11) | collective-permute-done | bytes 4194336 | tf_op jit(solution)/shard_map/ppermute | solution.py:24
  56.1 8.3 %shard_map.131 = (bf16[2,512,256]{2,1,0:T(8,128)(2,1)}, bf16[2,512,256]{2,1,0:T(8,128)(2,1)}, bf16[2,512,256]{2,1,0:T(8,128)(2,1)}, bf16[2,512,256]{2,1,0:T(8,12...) custom-call(s32[16]{0:T(128)S(1)} %stack.215.places_ref, ...), custom_call_target="tpu_custom_call" | custom-call | flops 1024 | bytes 1024 | tf_op jit(solution)/shard_map/pallas_call | solution.py:115
  64.4 1.6 %collective-permute-start.12 = (bf16[2,512,256]{2,1,0:T(8,128)(2,1)}, bf16[2,512,256]{2,1,0:T(8,128)(2,1)}, u32[]{:S(2)}, u32[]{:S(2)}) collective-permute-start(bf16[2,512,256]{2,1,0:T(8,128)(2,1)} %get-tuple-element.109), channel_id=1, source_target_pairs={{0,8},{8,0},{1,9},{9,1},{2,10},{10,2},{3,11},{11,3},{4,12},{12,4},... | collective-permute-start | bytes 1572872 | tf_op jit(solution)/shard_map/ppermute | solution.py:24
  68.6 7.9 %shard_map.132 = (f32[512,512]{1,0:T(8,128)}, bf16[4,1024,512]{2,1,0:T(8,128)(2,1)}) custom-call(s32[4]{0:T(128)S(1)} %get-tuple-element.192.places_ref, s32[4]{0:T(128)S(1)} %get-tuple-element.193.offsets_ref, bf16[512,8192]{1,0:T(8,128)(2,1)} %resid_ref.4, bf16[2,256,512]{2,1,0:T(8,128)(2,1)S(1)} %pad_maximum_fusion.rest_0_, ...), custom_call_target="tpu_custom_call" | custom-call | flops 1024 | bytes 1024 | tf_op jit(solution)/shard_map/pallas_call | solution.py:237
  76.5 2.2 %collective-permute-done.12.refs_1_ = bf16[2,512,256]{2,1,0:T(8,128)(2,1)} collective-permute-done((bf16[2,512,256]{2,1,0:T(8,128)(2,1)}, bf16[2,512,256]{2,1,0:T(8,128)(2,1)}, u32[]{:S(2)}, u32[]{:S(2)}) %collective-permute-start.12) | collective-permute-done | bytes 524320 | tf_op jit(solution)/shard_map/ppermute | solution.py:24
  79.9 1.9 %shard_map.134 = (bf16[512,256]{1,0:T(8,128)(2,1)}, bf16[512,256]{1,0:T(8,128)(2,1)}) custom-call(bf16[2,512,256]{2,1,0:T(8,128)(2,1)S(1)} %copy-done, bf16[2,512,256]{2,1,0:T(8,128)(2,1)} %collective-permute-done.12.refs_1_, bf16[2,512,256]{2,1,0:T(8,128)(2,1)S(1)} %copy-done.1, bf16[2,512,256]{2,1,0:T(8,128)(2,1)} %collective-permute-done.13.refs_3_.refs_4_), custom_call_target="tpu_custom_call" | custom-call | flops 1024 | bytes 1024 | tf_op jit(solution)/shard_map/pallas_call | solution.py:143
  82.8 1.6 %collective-permute-start.17 = (bf16[512,256]{1,0:T(8,128)(2,1)}, bf16[512,256]{1,0:T(8,128)(2,1)S(1)}, u32[]{:S(2)}, u32[]{:S(2)}) collective-permute-start(bf16[512,256]{1,0:T(8,128)(2,1)} %get-tuple-element.157), channel_id=1, source_target_pairs={{0,16},{16,0},{1,17},{17,1},{2,18},{18,2},{3,19},{19,3},{4,20},{20... | collective-permute-start | bytes 786440 | tf_op jit(solution)/shard_map/ppermute | solution.py:24
  84.4 1.5 %collective-permute-start.18 = (bf16[512,256]{1,0:T(8,128)(2,1)}, bf16[512,256]{1,0:T(8,128)(2,1)S(1)}, u32[]{:S(2)}, u32[]{:S(2)}) collective-permute-start(bf16[512,256]{1,0:T(8,128)(2,1)} %get-tuple-element.158), channel_id=1, source_target_pairs={{0,8},{8,0},{1,9},{9,1},{2,10},{10,2},{3,11},{11,3},{4,12},{12,4},... | collective-permute-start | bytes 786440 | tf_op jit(solution)/shard_map/ppermute | solution.py:24
  86.0 1.5 %collective-permute-done.16.weight_ref = bf16[4,1024,512]{2,1,0:T(8,128)(2,1)} collective-permute-done((bf16[4,1024,512]{2,1,0:T(8,128)(2,1)}, bf16[4,1024,512]{2,1,0:T(8,128)(2,1)}, u32[]{:S(2)}, u32[]{:S(2)}) %collective-permute-start.16) | collective-permute-done | bytes 4194336 | tf_op jit(solution)/shard_map/ppermute | solution.py:24
  87.4 7.7 %shard_map.133 = (bf16[512,512]{1,0:T(8,128)(2,1)}, f32[512,1]{1,0:T(8,128)S(1)}) custom-call(s32[4]{0:T(128)S(1)} %pad_add_fusion.places_ref, bf16[512,8192]{1,0:T(8,128)(2,1)} %resid_ref.4, bf16[4,1024,512]{2,1,0:T(8,128)(2,1)} %collective-permute-done.16.weight_ref, f32[512,512]{1,0:T(8,128)} %get-tuple-element.143.first_ref, ...), custom_call_target="tpu_custom_call" | custom-call | flops 1024 | bytes 1024 | tf_op jit(solution)/shard_map/pallas_call | solution.py:275
  95.1 7.2 %collective-permute-done.17.refs_2_ = bf16[512,256]{1,0:T(8,128)(2,1)S(1)} collective-permute-done((bf16[512,256]{1,0:T(8,128)(2,1)}, bf16[512,256]{1,0:T(8,128)(2,1)S(1)}, u32[]{:S(2)}, u32[]{:S(2)}) %collective-permute-start.17) | collective-permute-done | bytes 262176 | tf_op jit(solution)/shard_map/ppermute | solution.py:24
  103.5 2.9 %collective-permute-start.23 = (bf16[512,256]{1,0:T(8,128)(2,1)S(1)}, bf16[512,256]{1,0:T(8,128)(2,1)S(1)}, u32[]{:S(2)}, u32[]{:S(2)}) collective-permute-start(bf16[512,256]{1,0:T(8,128)(2,1)S(1)} %get-tuple-element.171), channel_id=1, source_target_pairs={{0,3},{1,0},{2,1},{3,2},{4,7},{5,4},{6,5},{7,6},{8,11},{9,8},{10,9... | collective-permute-start | bytes 786440 | tf_op jit(solution)/shard_map/ppermute | solution.py:24
  107.2 7.7 %shard_map.135.rest_0_ = bf16[512,8192]{1,0:T(8,128)(2,1)} custom-call(s32[4]{0:T(128)S(1)} %get-tuple-element.192.places_ref, bf16[512,8192]{1,0:T(8,128)(2,1)} %resid_ref.4, bf16[4,1024,512]{2,1,0:T(8,128)(2,1)} %get-tuple-element.142.weight_ref, bf16[512,512]{1,0:T(8,128)(2,1)S(1)} %get-tuple-element.144.cot_ref, f32[512,1]{1,0:T(8,128)S(1)} %get-tuple-element.160.coef_ref), custom_call_target="tpu_custom_call" | custom-call | flops 1024 | bytes 1024 | tf_op jit(solution)/shard_map/pallas_call | solution.py:275
  115.0 1.6 %collective-permute-start.21 = (bf16[512,256]{1,0:T(8,128)(2,1)S(1)}, bf16[512,256]{1,0:T(8,128)(2,1)S(1)}, u32[]{:S(2)}, u32[]{:S(2)}) collective-permute-start(bf16[512,256]{1,0:T(8,128)(2,1)S(1)} %get-tuple-element.167), channel_id=1, source_target_pairs={{0,16},{16,0},{1,17},{17,1},{2,18},{18,2},{3,19},{19,3},{4,20},{20... | collective-permute-start | bytes 786440 | tf_op jit(solution)/shard_map/ppermute | solution.py:24
  116.6 1.5 %collective-permute-start.22 = (bf16[512,256]{1,0:T(8,128)(2,1)S(1)}, bf16[512,256]{1,0:T(8,128)(2,1)S(1)}, u32[]{:S(2)}, u32[]{:S(2)}) collective-permute-start(bf16[512,256]{1,0:T(8,128)(2,1)S(1)} %get-tuple-element.168), channel_id=1, source_target_pairs={{0,8},{8,0},{1,9},{9,1},{2,10},{10,2},{3,11},{11,3},{4,12},{12,4},... | collective-permute-start | bytes 786440 | tf_op jit(solution)/shard_map/ppermute | solution.py:24
  118.2 4.6 %shard_map.138.rest_0_ = bf16[512,8192]{1,0:T(8,128)(2,1)} custom-call(s32[2]{0:T(128)S(1)} %pad_add_fusion.5.places_ref, bf16[512,8192]{1,0:T(8,128)(2,1)} %resid_ref.4, bf16[4,1024,512]{2,1,0:T(8,128)(2,1)} %collective-permute-done.16.weight_ref, bf16[512,512]{1,0:T(8,128)(2,1)S(1)} %get-tuple-element.144.cot_ref, ...), custom_call_target="tpu_custom_call", output_to_operand_aliasing={{}: (5, {})} | custom-call | flops 1024 | bytes 1024 | tf_op jit(solution)/shard_map/pallas_call | solution.py:275
  124.6 4.6 %shard_map.139 = bf16[512,8192]{1,0:T(8,128)(2,1)} custom-call(s32[2]{0:T(128)S(1)} %pad_add_fusion.4.places_ref, bf16[512,8192]{1,0:T(8,128)(2,1)} %resid_ref.4, bf16[4,1024,512]{2,1,0:T(8,128)(2,1)} %collective-permute-done.16.weight_ref, bf16[512,512]{1,0:T(8,128)(2,1)S(1)} %get-tuple-element.144.cot_ref, ...), custom_call_target="tpu_custom_call", output_to_operand_aliasing={{}: (5, {})} | custom-call | flops 1024 | bytes 1024 | tf_op jit(solution)/shard_map/pallas_call | solution.py:275
  129.2 4.6 %collective-permute-done.25 = bf16[512,256]{1,0:T(8,128)(2,1)S(1)} collective-permute-done((bf16[512,256]{1,0:T(8,128)(2,1)S(1)}, bf16[512,256]{1,0:T(8,128)(2,1)S(1)}, u32[]{:S(2)}, u32[]{:S(2)}) %collective-permute-start.25) | collective-permute-done | bytes 262176 | tf_op jit(solution)/shard_map/ppermute | solution.py:24
  (83 shorter events, 24.8 us)
Async XLA Ops:
  2.1 6.7 %collective-permute-start = (f32[1,52,128]{2,1,0:T(8,128)S(1)}, f32[1,52,128]{2,1,0:T(8,128)S(1)}, u32[]{:S(2)}, u32[]{:S(2)}) collective-permute-start(f32[1,52,128]{2,1,0:T(8,128)S(1)} %maximum_bitcast_fusion), channel_id=1, source_target_pairs={{0,1},{1,0},{2,3},{3,2},{4,5},{5,4},{6,7},{7,6},{8,9},{9,8},{10,11... | collective-permute-start | bytes 79880 | tf_op jit(solution)/shard_map/ppermute | solution.py:29
  8.8 9.8 %collective-permute-start.2 = (bf16[256,512]{1,0:T(8,128)(2,1)}, bf16[256,512]{1,0:T(8,128)(2,1)S(1)}, u32[]{:S(2)}, u32[]{:S(2)}) collective-permute-start(bf16[256,512]{1,0:T(8,128)(2,1)} %multiply_convert_fusion), channel_id=1, source_target_pairs={{0,8},{8,0},{1,9},{9,1},{2,10},{10,2},{3,11},{11,3},{4,12},{12,4},... | collective-permute-start | bytes 786440 | tf_op jit(solution)/shard_map/ppermute | solution.py:24
  10.4 9.6 %collective-permute-start.1 = (bf16[256,512]{1,0:T(8,128)(2,1)}, bf16[256,512]{1,0:T(8,128)(2,1)S(1)}, u32[]{:S(2)}, u32[]{:S(2)}) collective-permute-start(bf16[256,512]{1,0:T(8,128)(2,1)} %multiply_convert_fusion), channel_id=1, source_target_pairs={{0,1},{1,2},{2,3},{3,0},{4,5},{5,6},{6,7},{7,4},{8,9},{9,10},{10,1... | collective-permute-start | bytes 786440 | tf_op jit(solution)/shard_map/ppermute | solution.py:24
  15.9 7.4 %collective-permute-start.5 = (f32[2,52,128]{2,1,0:T(8,128)S(1)}, f32[2,52,128]{2,1,0:T(8,128)S(1)}, u32[]{:S(2)}, u32[]{:S(2)}) collective-permute-start(f32[2,52,128]{2,1,0:T(8,128)S(1)} %pad_maximum_fusion.5), channel_id=1, source_target_pairs={{0,2},{1,3},{2,0},{3,1},{4,6},{5,7},{6,4},{7,5},{8,10},{9,11},{10,... | collective-permute-start | bytes 159752 | tf_op jit(solution)/shard_map/ppermute | solution.py:29
  19.9 7.2 %collective-permute-start.4 = (bf16[256,512]{1,0:T(8,128)(2,1)}, bf16[256,512]{1,0:T(8,128)(2,1)}, u32[]{:S(2)}, u32[]{:S(2)}) collective-permute-start(bf16[256,512]{1,0:T(8,128)(2,1)} %multiply_convert_fusion), channel_id=1, source_target_pairs={{0,3},{1,0},{2,1},{3,2},{4,7},{5,4},{6,5},{7,6},{8,11},{9,8},{10,9... | collective-permute-start | bytes 786440 | tf_op jit(solution)/shard_map/ppermute | solution.py:24
  21.0 9.2 %collective-permute-start.3 = (bf16[256,512]{1,0:T(8,128)(2,1)S(1)}, bf16[256,512]{1,0:T(8,128)(2,1)S(1)}, u32[]{:S(2)}, u32[]{:S(2)}) collective-permute-start(bf16[256,512]{1,0:T(8,128)(2,1)S(1)} %collective-permute-done.1), channel_id=1, source_target_pairs={{0,16},{16,0},{1,17},{17,1},{2,18},{18,2},{3,19},{19,3},{4,20},{20... | collective-permute-start | bytes 786440 | tf_op jit(solution)/shard_map/ppermute | solution.py:24
  24.3 19.1 %collective-permute-start.7 = (bf16[2,256,512]{2,1,0:T(8,128)(2,1)S(1)}, bf16[2,256,512]{2,1,0:T(8,128)(2,1)S(1)}, u32[]{:S(2)}, u32[]{:S(2)}) collective-permute-start(bf16[2,256,512]{2,1,0:T(8,128)(2,1)S(1)} %pad_maximum_fusion.rest_0_), channel_id=1, source_target_pairs={{0,16},{16,0},{1,17},{17,1},{2,18},{18,2},{3,19},{19,3},{4,20},{20... | collective-permute-start | bytes 1572872 | tf_op jit(solution)/shard_map/ppermute | solution.py:24
  30.2 11.6 %collective-permute-start.6 = (bf16[256,512]{1,0:T(8,128)(2,1)}, bf16[256,512]{1,0:T(8,128)(2,1)}, u32[]{:S(2)}, u32[]{:S(2)}) collective-permute-start(bf16[256,512]{1,0:T(8,128)(2,1)} %multiply_convert_fusion), channel_id=1, source_target_pairs={{0,2},{1,3},{2,0},{3,1},{4,6},{5,7},{6,4},{7,5},{8,10},{9,11},{10,... | collective-permute-start | bytes 786440 | tf_op jit(solution)/shard_map/ppermute | solution.py:24
  30.6 14.0 %collective-permute-start.8 = (bf16[2,256,512]{2,1,0:T(8,128)(2,1)S(1)}, bf16[2,256,512]{2,1,0:T(8,128)(2,1)S(1)}, u32[]{:S(2)}, u32[]{:S(2)}) collective-permute-start(bf16[2,256,512]{2,1,0:T(8,128)(2,1)S(1)} %pad_maximum_fusion.1.rest_2_), channel_id=1, source_target_pairs={{0,8},{8,0},{1,9},{9,1},{2,10},{10,2},{3,11},{11,3},{4,12},{12,4},... | collective-permute-start | bytes 1572872 | tf_op jit(solution)/shard_map/ppermute | solution.py:24
  31.5 13.2 %collective-permute-start.9 = (bf16[256,512]{1,0:T(8,128)(2,1)}, bf16[256,512]{1,0:T(8,128)(2,1)}, u32[]{:S(2)}, u32[]{:S(2)}) collective-permute-start(bf16[256,512]{1,0:T(8,128)(2,1)} %collective-permute-done.4), channel_id=1, source_target_pairs={{0,16},{16,0},{1,17},{17,1},{2,18},{18,2},{3,19},{19,3},{4,20},{20... | collective-permute-start | bytes 786440 | tf_op jit(solution)/shard_map/ppermute | solution.py:24
  41.8 6.8 %collective-permute-start.10 = (bf16[256,512]{1,0:T(8,128)(2,1)}, bf16[256,512]{1,0:T(8,128)(2,1)}, u32[]{:S(2)}, u32[]{:S(2)}) collective-permute-start(bf16[256,512]{1,0:T(8,128)(2,1)} %collective-permute-done.6), channel_id=1, source_target_pairs={{0,8},{8,0},{1,9},{9,1},{2,10},{10,2},{3,11},{11,3},{4,12},{12,4},... | collective-permute-start | bytes 786440 | tf_op jit(solution)/shard_map/ppermute | solution.py:24
  48.6 7.5 %collective-permute-start.11 = (bf16[4,4,512,256]{3,2,1,0:T(8,128)(2,1)}, bf16[4,4,512,256]{3,2,1,0:T(8,128)(2,1)}, u32[]{:S(2)}, u32[]{:S(2)}) collective-permute-start(bf16[4,4,512,256]{3,2,1,0:T(8,128)(2,1)} %shard_map.130), channel_id=1, source_target_pairs={{0,4},{4,0},{1,5},{5,1},{2,6},{6,2},{3,7},{7,3},{8,12},{12,8},{9,1... | collective-permute-start | bytes 12582920 | tf_op jit(solution)/shard_map/ppermute | solution.py:24
  49.7 16.8 %collective-permute-start.15 = (bf16[2,256,512]{2,1,0:T(8,128)(2,1)S(1)}, bf16[2,256,512]{2,1,0:T(8,128)(2,1)}, u32[]{:S(2)}, u32[]{:S(2)}) collective-permute-start(bf16[2,256,512]{2,1,0:T(8,128)(2,1)S(1)} %pad_maximum_fusion.3.rest_6_), channel_id=1, source_target_pairs={{0,16},{16,0},{1,17},{17,1},{2,18},{18,2},{3,19},{19,3},{4,20},{20... | collective-permute-start | bytes 1572872 | tf_op jit(solution)/shard_map/ppermute | solution.py:24
  51.3 15.2 %collective-permute-start.14 = (bf16[2,256,512]{2,1,0:T(8,128)(2,1)S(1)}, bf16[2,256,512]{2,1,0:T(8,128)(2,1)}, u32[]{:S(2)}, u32[]{:S(2)}) collective-permute-start(bf16[2,256,512]{2,1,0:T(8,128)(2,1)S(1)} %pad_maximum_fusion.2.rest_4_), channel_id=1, source_target_pairs={{0,8},{8,0},{1,9},{9,1},{2,10},{10,2},{3,11},{11,3},{4,12},{12,4},... | collective-permute-start | bytes 1572872 | tf_op jit(solution)/shard_map/ppermute | solution.py:24
  56.1 31.3 %copy-start.10 = (f32[512,1]{1,0:T(8,128)S(1)}, f32[512,1]{1,0:T(8,128)}, u32[]{:S(2)}) copy-start(f32[512,1]{1,0:T(8,128)} %copy-done.9) | copy-start | bytes 6148
  64.4 15.6 %copy-start = (bf16[2,512,256]{2,1,0:T(8,128)(2,1)S(1)}, bf16[2,512,256]{2,1,0:T(8,128)(2,1)}, u32[]{:S(2)}) copy-start(bf16[2,512,256]{2,1,0:T(8,128)(2,1)} %get-tuple-element.147.refs_0_) | copy-start | bytes 1572868
  64.4 14.3 %collective-permute-start.12 = (bf16[2,512,256]{2,1,0:T(8,128)(2,1)}, bf16[2,512,256]{2,1,0:T(8,128)(2,1)}, u32[]{:S(2)}, u32[]{:S(2)}) collective-permute-start(bf16[2,512,256]{2,1,0:T(8,128)(2,1)} %get-tuple-element.109), channel_id=1, source_target_pairs={{0,8},{8,0},{1,9},{9,1},{2,10},{10,2},{3,11},{11,3},{4,12},{12,4},... | collective-permute-start | bytes 1572872 | tf_op jit(solution)/shard_map/ppermute | solution.py:24
  65.9 14.0 %collective-permute-start.13 = (bf16[2,512,256]{2,1,0:T(8,128)(2,1)}, bf16[2,512,256]{2,1,0:T(8,128)(2,1)}, u32[]{:S(2)}, u32[]{:S(2)}) collective-permute-start(bf16[2,512,256]{2,1,0:T(8,128)(2,1)} %get-tuple-element.110), channel_id=1, source_target_pairs={{0,16},{16,0},{1,17},{17,1},{2,18},{18,2},{3,19},{19,3},{4,20},{20... | collective-permute-start | bytes 1572872 | tf_op jit(solution)/shard_map/ppermute | solution.py:24
  66.4 13.5 %copy-start.1 = (bf16[2,512,256]{2,1,0:T(8,128)(2,1)S(1)}, bf16[2,512,256]{2,1,0:T(8,128)(2,1)}, u32[]{:S(2)}) copy-start(bf16[2,512,256]{2,1,0:T(8,128)(2,1)} %get-tuple-element.149.refs_2_.refs_3_) | copy-start | bytes 1572868
  76.5 25.8 %copy-start.2 = (bf16[2,512,256]{2,1,0:T(8,128)(2,1)S(1)}, bf16[2,512,256]{2,1,0:T(8,128)(2,1)}, u32[]{:S(2)}) copy-start(bf16[2,512,256]{2,1,0:T(8,128)(2,1)} %get-tuple-element.149.refs_2_.refs_3_) | copy-start | bytes 1572868
  79.9 7.5 %collective-permute-start.16 = (bf16[4,1024,512]{2,1,0:T(8,128)(2,1)}, bf16[4,1024,512]{2,1,0:T(8,128)(2,1)}, u32[]{:S(2)}, u32[]{:S(2)}) collective-permute-start(bf16[4,1024,512]{2,1,0:T(8,128)(2,1)} %get-tuple-element.142.weight_ref), channel_id=1, source_target_pairs={{0,4},{4,0},{1,5},{5,1},{2,6},{6,2},{3,7},{7,3},{8,12},{12,8},{9,1... | collective-permute-start | bytes 12582920 | tf_op jit(solution)/shard_map/ppermute | solution.py:24
  81.8 33.0 %collective-permute-start.19 = (bf16[2,512,256]{2,1,0:T(8,128)(2,1)}, bf16[2,512,256]{2,1,0:T(8,128)(2,1)S(1)}, u32[]{:S(2)}, u32[]{:S(2)}) collective-permute-start(bf16[2,512,256]{2,1,0:T(8,128)(2,1)} %get-tuple-element.162), channel_id=1, source_target_pairs={{0,8},{8,0},{1,9},{9,1},{2,10},{10,2},{3,11},{11,3},{4,12},{12,4},... | collective-permute-start | bytes 1572872 | tf_op jit(solution)/shard_map/ppermute | solution.py:24
  82.4 32.5 %collective-permute-start.20 = (bf16[2,512,256]{2,1,0:T(8,128)(2,1)}, bf16[2,512,256]{2,1,0:T(8,128)(2,1)S(1)}, u32[]{:S(2)}, u32[]{:S(2)}) collective-permute-start(bf16[2,512,256]{2,1,0:T(8,128)(2,1)} %get-tuple-element.163), channel_id=1, source_target_pairs={{0,16},{16,0},{1,17},{17,1},{2,18},{18,2},{3,19},{19,3},{4,20},{20... | collective-permute-start | bytes 1572872 | tf_op jit(solution)/shard_map/ppermute | solution.py:24
  82.8 19.4 %collective-permute-start.17 = (bf16[512,256]{1,0:T(8,128)(2,1)}, bf16[512,256]{1,0:T(8,128)(2,1)S(1)}, u32[]{:S(2)}, u32[]{:S(2)}) collective-permute-start(bf16[512,256]{1,0:T(8,128)(2,1)} %get-tuple-element.157), channel_id=1, source_target_pairs={{0,16},{16,0},{1,17},{17,1},{2,18},{18,2},{3,19},{19,3},{4,20},{20... | collective-permute-start | bytes 786440 | tf_op jit(solution)/shard_map/ppermute | solution.py:24
  84.4 17.9 %collective-permute-start.18 = (bf16[512,256]{1,0:T(8,128)(2,1)}, bf16[512,256]{1,0:T(8,128)(2,1)S(1)}, u32[]{:S(2)}, u32[]{:S(2)}) collective-permute-start(bf16[512,256]{1,0:T(8,128)(2,1)} %get-tuple-element.158), channel_id=1, source_target_pairs={{0,8},{8,0},{1,9},{9,1},{2,10},{10,2},{3,11},{11,3},{4,12},{12,4},... | collective-permute-start | bytes 786440 | tf_op jit(solution)/shard_map/ppermute | solution.py:24
  103.5 19.3 %collective-permute-start.23 = (bf16[512,256]{1,0:T(8,128)(2,1)S(1)}, bf16[512,256]{1,0:T(8,128)(2,1)S(1)}, u32[]{:S(2)}, u32[]{:S(2)}) collective-permute-start(bf16[512,256]{1,0:T(8,128)(2,1)S(1)} %get-tuple-element.171), channel_id=1, source_target_pairs={{0,3},{1,0},{2,1},{3,2},{4,7},{5,4},{6,5},{7,6},{8,11},{9,8},{10,9... | collective-permute-start | bytes 786440 | tf_op jit(solution)/shard_map/ppermute | solution.py:24
  106.4 17.6 %collective-permute-start.24 = (bf16[512,256]{1,0:T(8,128)(2,1)S(1)}, bf16[512,256]{1,0:T(8,128)(2,1)S(1)}, u32[]{:S(2)}, u32[]{:S(2)}) collective-permute-start(bf16[512,256]{1,0:T(8,128)(2,1)S(1)} %get-tuple-element.172), channel_id=1, source_target_pairs={{0,2},{1,3},{2,0},{3,1},{4,6},{5,7},{6,4},{7,5},{8,10},{9,11},{10,... | collective-permute-start | bytes 786440 | tf_op jit(solution)/shard_map/ppermute | solution.py:24
  115.0 9.0 %collective-permute-start.21 = (bf16[512,256]{1,0:T(8,128)(2,1)S(1)}, bf16[512,256]{1,0:T(8,128)(2,1)S(1)}, u32[]{:S(2)}, u32[]{:S(2)}) collective-permute-start(bf16[512,256]{1,0:T(8,128)(2,1)S(1)} %get-tuple-element.167), channel_id=1, source_target_pairs={{0,16},{16,0},{1,17},{17,1},{2,18},{18,2},{3,19},{19,3},{4,20},{20... | collective-permute-start | bytes 786440 | tf_op jit(solution)/shard_map/ppermute | solution.py:24
  116.6 7.4 %collective-permute-start.22 = (bf16[512,256]{1,0:T(8,128)(2,1)S(1)}, bf16[512,256]{1,0:T(8,128)(2,1)S(1)}, u32[]{:S(2)}, u32[]{:S(2)}) collective-permute-start(bf16[512,256]{1,0:T(8,128)(2,1)S(1)} %get-tuple-element.168), channel_id=1, source_target_pairs={{0,8},{8,0},{1,9},{9,1},{2,10},{10,2},{3,11},{11,3},{4,12},{12,4},... | collective-permute-start | bytes 786440 | tf_op jit(solution)/shard_map/ppermute | solution.py:24
  124.2 9.6 %collective-permute-start.25 = (bf16[512,256]{1,0:T(8,128)(2,1)S(1)}, bf16[512,256]{1,0:T(8,128)(2,1)S(1)}, u32[]{:S(2)}, u32[]{:S(2)}) collective-permute-start(bf16[512,256]{1,0:T(8,128)(2,1)S(1)} %fusion.1), channel_id=1, source_target_pairs={{0,1},{1,2},{2,3},{3,0},{4,5},{5,6},{6,7},{7,4},{8,9},{9,10},{10,1... | collective-permute-start | bytes 786440 | tf_op jit(solution)/shard_map/ppermute | solution.py:24
  124.5 9.4 %copy-start.12 = (bf16[256]{0:T(256)(128)(2,1)S(1)}, bf16[256]{0:T(256)(128)(2,1)}, u32[]{:S(2)}) copy-start(bf16[256]{0:T(256)(128)(2,1)} %param.11) | copy-start | bytes 1540
  124.6 9.4 %copy-start.11 = (bf16[256,512]{1,0:T(8,128)(2,1)S(1)}, bf16[256,512]{1,0:T(8,128)(2,1)}, u32[]{:S(2)}) copy-start(bf16[256,512]{1,0:T(8,128)(2,1)} %param.12) | copy-start | bytes 786436
  (7 other events, 32.1 us)

commit v12 on v11

--- a/solution.py
+++ b/solution.py
@@ -414,13 +414,7 @@
     own_pieces[0] = far_of(0, gained, near[0])
     seq_length = lax.dynamic_index_in_dim(lengths, rep_place, keepdims=False)
     info = jnp.stack([tp_place, seq_length]).astype(jnp.int32)
-    near[1], arrived[2], packed, late_gained, info = lax.optimization_barrier(
-        (near[1], arrived[2], packed, late_gained, info)
-    )
-    near[2] = near_of(2, arrived[2])
-    for k in order[3:]:
-        arrived[k] = swap(late_gained, "tp", shifts[k])
-    own_pieces[1] = far_of(1, arrived[1], near[1])
+    packed, squares, info = lax.optimization_barrier((packed, squares, info))
     cot, cot_t, inv_rms = scaled_cot(width, rep_count, info, packed, squares, value_cot)
 
     def place_of(o, i, c, k):
@@ -486,16 +480,28 @@
         ]
 
     theirs = for_others(cot_t)
-    theirs, arrived = lax.optimization_barrier((theirs, arrived))
-    near.update({k: near_of(k, arrived[k]) for k in order[3:]})
-    theirs, own_pieces, near = lax.optimization_barrier((theirs, own_pieces, near))
+    theirs, near[1], arrived[2], late_gained = lax.optimization_barrier(
+        (theirs, near[1], arrived[2], late_gained)
+    )
     other = swap(theirs, "core", 1)
-    near, own_pieces = lax.optimization_barrier((near, own_pieces))
+    for k in order[3:]:
+        arrived[k] = swap(late_gained, "tp", shifts[k])
+    own_pieces[1] = far_of(1, arrived[1], near[1])
+    near[2] = near_of(2, arrived[2])
+    sides = for_us(other)
+    sides, arrived, own_pieces, near[2] = lax.optimization_barrier(
+        (sides, arrived, own_pieces, near[2])
+    )
+    for k in order[3:]:
+        near[k] = near_of(k, arrived[k])
+    got = [first_round(sides[0])]
+    near, sides[1:] = lax.optimization_barrier((near, sides[1:]))
     for k in order[2:]:
         own_pieces[k] = far_of(k, arrived[k], near[k])
-    sides = for_us(other)
-    got = [first_round(sides[0])]
+    first_later, _ = second_round(sides[0], got[0])
+    later = [first_later]
     sides[1:], own_pieces = lax.optimization_barrier((sides[1:], own_pieces))
+    got += [first_round(side) for side in sides[1:]]
 
     if in_place:
         pieces = [piece for k in order for piece in own_pieces[k]]
@@ -518,13 +524,15 @@
         weight = weight[:, :, (at_inner - jnp.arange(inner)) % inner]
         own_weight = weight.transpose(1, 2, 0, 3, 4).reshape(outer * inner, depth, features)
         total = jnp.zeros((), F32)
-    got[0], sides[1:], total, own_weight = lax.optimization_barrier(
-        (got[0], sides[1:], total, own_weight)
-    )
+    total, own_weight, later[0] = lax.optimization_barrier((total, own_weight, later[0]))
     other_weight = swap(own_weight, "core", 1)
-    first_later, sides[1:] = second_round(sides[0], got[0], sides[1:])
-    later = [first_later]
-    got += [first_round(side) for side in sides[1:]]
+    if in_place:
+        groups = [[keep] + parts + then for (_, keep), parts, then in zip(sides[0], got[0], later[0])]
+        sums = dict(zip(pairs[0], sums_of(groups, 0)))
+    else:
+        sums = dict(zip(pairs[0], summed(sides[0], got[0], later[0])))
+    last = [swap(sums[k].astype(BF16), "tp", k) for k in pairs[0]]
+    total = after(total, sums)
     if in_place:
         value_proj, coefficient = weight_call(
             functools.partial(value_end_kernel, width),
@@ -544,36 +552,25 @@
         value_proj = (inv_rms * value_acc).astype(BF16)
         share = jnp.sum(cot.astype(F32) * value_acc, axis=1, keepdims=True)
         coefficient = inv_rms * inv_rms * share * (1.0 / width)
-    later[0], coefficient = lax.optimization_barrier((later[0], coefficient))
-    if in_place:
-        groups = [[keep] + parts + then for (_, keep), parts, then in zip(sides[0], got[0], later[0])]
-        sums = dict(zip(pairs[0], sums_of(groups, 0)))
-    else:
-        sums = dict(zip(pairs[0], summed(sides[0], got[0], later[0])))
-    last = [swap(sums[k].astype(BF16), "tp", k) for k in pairs[0]]
+    got[1:], coefficient = lax.optimization_barrier((got[1:], coefficient))
+    later += [second_round(side, parts)[0] for side, parts in zip(sides[1:], got[1:])]
     if in_place:
         grad_shape = jax.ShapeDtypeStruct((rows_here, width), BF16)
         resid_grad = weight_call(
             grad_kernel, places[0], residual, in_hbm(own_weight), [cot, coefficient], grad_shape
         )
-        got[1:], resid_grad = lax.optimization_barrier((got[1:], resid_grad))
+        later[1], last, resid_grad = lax.optimization_barrier((later[1], last, resid_grad))
     else:
         normed_grad = lax.dot_general(
             cot, weight, (((1,), (1,)), ((), ())), preferred_element_type=F32
         )
         resid_grad = (normed_grad - residual.astype(F32) * coefficient).astype(BF16)
-    later += [second_round(side, parts)[0] for side, parts in zip(sides[1:], got[1:])]
-    if in_place:
-        resid_grad = weight_call(
-            grad_kernel, places[1][:2], residual, other_weight, [cot, coefficient], grad_shape, resid_grad
-        )
-        later[1], last, resid_grad = lax.optimization_barrier((later[1], last, resid_grad))
     for pair, *rounds in zip(pairs[1:], sides[1:], got[1:], later[1:]):
         sums.update(zip(pair, summed(*rounds)))
     last += [swap(sums[k].astype(BF16), "tp", k) for k in backward[2:-1]]
     if in_place:
         resid_grad = weight_call(
-            grad_kernel, places[1][2:], residual, other_weight, [cot, coefficient], grad_shape, resid_grad
+            grad_kernel, places[1], residual, other_weight, [cot, coefficient], grad_shape, resid_grad
         )
     grad_rows = widen([sums[0]] + last)
     late_gain, late_weight, grad_rows = lax.optimization_barrier((norm_gain, value_weight, grad_rows))

time: 137 us -> 139 us (1.015)
  local copies, waits for them, and re-layouts: 5.65 us -> 11.1 us
  Pallas kernels: 52.7 us -> 50.2 us
    unnamed x27 -> x45, local copies, waits for them, and re-layouts: 3.95 us -> 10.1 us
    ppermute x2, waiting for transfers between devices: 0.01 us -> 5.26 us  [trade(): lax.ppermute(value, axis, [(place, place ^ mask) for place in range(size)])]
    ppermute x24, waiting for transfers between devices: 32.2 us -> 27.8 us  [swap(): lax.ppermute(value, axis, [(place, (place + step) % size) for place in ra...]
    ppermute x2, starting transfers between devices: 5.67 us -> 3.81 us  [trade(): lax.ppermute(value, axis, [(place, place ^ mask) for place in range(size)])]
    pallas_call x4 -> x3, Pallas kernels: 24.6 us -> 23 us  [weight_call(): pl.pallas_call(kernel, out_shape=out_shape, grid_spec=pltpu.PrefetchScala...]
  transfers between devices with their start and end apart: 26 -> 26, of which waited for: 12 -> 10; matrix products, arithmetic and copies ran while one was open for 10% -> 9% of each run, Pallas kernels for 39% -> 36%
where the time goes in v12:
time: 139 us; the launch traced here: 138 us
  Pallas kernels  50.2 us (36%)
  waiting for transfers between devices  33 us (24%)
  starting transfers between devices  29.2 us (21%)
  other arithmetic  13.4 us (10%)
  local copies, waits for them, and re-layouts  11.1 us (8%)
    ppermute x24, waiting for transfers between devices, swap(): lax.ppermute(value, axis, [(place, (place + step) % size) for place in ra...  27.8 us
    ppermute x24, starting transfers between devices, swap(): lax.ppermute(value, axis, [(place, (place + step) % size) for place in ra...  25.4 us
    pallas_call x3, Pallas kernels, weight_call(): pl.pallas_call(kernel, out_shape=out_shape, grid_spec=pltpu.PrefetchScala...  23 us
    pallas_call x2, Pallas kernels, grad_product(): pl.pallas_call(kernel, out_shape=out_shape, grid_spec=pltpu.PrefetchScala...  14.9 us
    unnamed x45, local copies, waits for them, and re-layouts  10.1 us
    pallas_call x1, Pallas kernels, first_value(): pl.pallas_call(functools.partial(value_kernel, inner_flags), out_shape=[t...  7.77 us
    ppermute x2, waiting for transfers between devices, trade(): lax.ppermute(value, axis, [(place, place ^ mask) for place in range(size)])  5.26 us
    reduce_sum x1, other arithmetic, per_device(): squares = jnp.sum(resid_wide * resid_wide, axis=1, keepdims=True)  5.1 us
  transfers between devices with their start and end apart: 26, of which 10 were waited for; matrix products, arithmetic and copies ran while one was open for 9% of the time, Pallas kernels for 36%

profile of v12, /device:TPU:0, one launch (start us, length us, event | category | flops | bytes accessed | tf_op | source)
XLA Modules:
  0.0 138.0 jit_solution(16254472911715266335)
XLA Ops:
  2.1 3.0 %collective-permute-start = (f32[1,52,128]{2,1,0:T(8,128)S(1)}, f32[1,52,128]{2,1,0:T(8,128)S(1)}, u32[]{:S(2)}, u32[]{:S(2)}) collective-permute-start(f32[1,52,128]{2,1,0:T(8,128)S(1)} %maximum_bitcast_fusion), channel_id=1, source_target_pairs={{0,1},{1,0},{2,3},{3,2},{4,5},{5,4},{6,7},{7,6},{8,9},{9,8},{10,11... | collective-permute-start | bytes 79880 | tf_op jit(solution)/shard_map/ppermute | solution.py:29
  7.0 2.0 %collective-permute-start.1 = (bf16[256,512]{1,0:T(8,128)(2,1)S(1)}, bf16[256,512]{1,0:T(8,128)(2,1)S(1)}, u32[]{:S(2)}, u32[]{:S(2)}) collective-permute-start(bf16[256,512]{1,0:T(8,128)(2,1)S(1)} %multiply_convert_fusion), channel_id=1, source_target_pairs={{0,1},{1,2},{2,3},{3,0},{4,5},{5,6},{6,7},{7,4},{8,9},{9,10},{10,1... | collective-permute-start | bytes 786440 | tf_op jit(solution)/shard_map/ppermute | solution.py:24
  9.0 1.5 %collective-permute-start.2 = (bf16[256,512]{1,0:T(8,128)(2,1)S(1)}, bf16[256,512]{1,0:T(8,128)(2,1)S(1)}, u32[]{:S(2)}, u32[]{:S(2)}) collective-permute-start(bf16[256,512]{1,0:T(8,128)(2,1)S(1)} %multiply_convert_fusion), channel_id=1, source_target_pairs={{0,8},{8,0},{1,9},{9,1},{2,10},{10,2},{3,11},{11,3},{4,12},{12,4},... | collective-permute-start | bytes 786440 | tf_op jit(solution)/shard_map/ppermute | solution.py:24
  10.5 5.1 %multiply_reduce_fusion = f32[512]{0:T(512)S(1)} fusion(bf16[512,8192]{1,0:T(8,128)(2,1)} %resid_ref.3), kind=kLoop, calls=%fused_computation | loop fusion | flops 12582400 | bytes 8390656 | tf_op jit(solution)/shard_map/reduce_sum | solution.py:391
  16.5 1.5 %collective-permute-start.4 = (bf16[256,512]{1,0:T(8,128)(2,1)S(1)}, bf16[256,512]{1,0:T(8,128)(2,1)S(1)}, u32[]{:S(2)}, u32[]{:S(2)}) collective-permute-start(bf16[256,512]{1,0:T(8,128)(2,1)S(1)} %collective-permute-done.1), channel_id=1, source_target_pairs={{0,16},{16,0},{1,17},{17,1},{2,18},{18,2},{3,19},{19,3},{4,20},{20... | collective-permute-start | bytes 786440 | tf_op jit(solution)/shard_map/ppermute | solution.py:24
  18.0 1.7 %collective-permute-start.5 = (bf16[256,512]{1,0:T(8,128)(2,1)S(1)}, bf16[256,512]{1,0:T(8,128)(2,1)S(1)}, u32[]{:S(2)}, u32[]{:S(2)}) collective-permute-start(bf16[256,512]{1,0:T(8,128)(2,1)S(1)} %multiply_convert_fusion), channel_id=1, source_target_pairs={{0,3},{1,0},{2,1},{3,2},{4,7},{5,4},{6,5},{7,6},{8,11},{9,8},{10,9... | collective-permute-start | bytes 786440 | tf_op jit(solution)/shard_map/ppermute | solution.py:24
  22.0 5.1 %collective-permute-done.3 = f32[2,52,128]{2,1,0:T(8,128)S(1)} collective-permute-done((f32[2,52,128]{2,1,0:T(8,128)S(1)}, f32[2,52,128]{2,1,0:T(8,128)S(1)}, u32[]{:S(2)}, u32[]{:S(2)}) %collective-permute-start.3) | collective-permute-done | bytes 53280 | tf_op jit(solution)/shard_map/ppermute | solution.py:29
  27.3 2.1 %shard_map.129 = (bf16[512,512]{1,0:T(8,128)(2,1)S(1)}, bf16[512,512]{1,0:T(8,128)(2,1)S(1)}, f32[512,1]{1,0:T(8,128)S(1)}) custom-call(s32[2]{0:T(128)S(1)} %pad_add_fusion.3.info_ref, f32[4,52,128]{2,1,0:T(8,128)S(1)} %pad_maximum_fusion.4.shares_ref, f32[512,1]{1,0:T(8,128)S(1)} %copy.17.squares_ref, bf16[512,512]{1,0:T(8,128)(2,1)} %value_cot_ref.1), custom_call_target="tpu_custom_call" | custom-call | flops 1024 | bytes 1024 | tf_op jit(solution)/shard_map/pallas_call | solution.py:337
  29.4 6.6 %shard_map.130 = bf16[4,4,512,256]{3,2,1,0:T(8,128)(2,1)} custom-call(s32[16]{0:T(128)S(1)} %stack.221.places_ref, bf16[512,512]{1,0:T(8,128)(2,1)S(1)} %get-tuple-element.96.cot_ref, bf16[512,8192]{1,0:T(8,128)(2,1)} %resid_ref.3, bf16[512,8192]{1,0:T(8,128)(2,1)} %resid_ref.3, bf16[512,8192]{1,0:T(8,128)(2,1)} %resid_ref.3, bf16[512,8192]{1,0:T(8,128)(2,1)} %resid_ref.3), custom_call_target="tpu_custom_call" | custom-call | flops 1024 | bytes 1024 | tf_op jit(solution)/shard_map/pallas_call | solution.py:115
  37.5 1.1 pad_maximum_fusion.1.rest_2_
  38.5 1.2 collective-permute-start.9
  39.8 1.5 %collective-permute-start.10 = (bf16[256,512]{1,0:T(8,128)(2,1)}, bf16[256,512]{1,0:T(8,128)(2,1)}, u32[]{:S(2)}, u32[]{:S(2)}) collective-permute-start(bf16[256,512]{1,0:T(8,128)(2,1)} %copy-done.16), channel_id=1, source_target_pairs={{0,16},{16,0},{1,17},{17,1},{2,18},{18,2},{3,19},{19,3},{4,20},{20... | collective-permute-start | bytes 786440 | tf_op jit(solution)/shard_map/ppermute | solution.py:24
  42.4 1.2 collective-permute-done.6.rest_4_
  43.6 8.3 %shard_map.131 = (bf16[2,512,256]{2,1,0:T(8,128)(2,1)}, bf16[2,512,256]{2,1,0:T(8,128)(2,1)}, bf16[2,512,256]{2,1,0:T(8,128)(2,1)}, bf16[2,512,256]{2,1,0:T(8,12...) custom-call(s32[16]{0:T(128)S(1)} %stack.240.places_ref, ...), custom_call_target="tpu_custom_call" | custom-call | flops 1024 | bytes 1024 | tf_op jit(solution)/shard_map/pallas_call | solution.py:115
  51.9 4.4 %collective-permute-done.10 = bf16[256,512]{1,0:T(8,128)(2,1)} collective-permute-done((bf16[256,512]{1,0:T(8,128)(2,1)}, bf16[256,512]{1,0:T(8,128)(2,1)}, u32[]{:S(2)}, u32[]{:S(2)}) %collective-permute-start.10) | collective-permute-done | bytes 262176 | tf_op jit(solution)/shard_map/ppermute | solution.py:24
  57.1 1.2 collective-permute-start.11
  59.6 6.9 %collective-permute-done.11 = bf16[256,512]{1,0:T(8,128)(2,1)S(1)} collective-permute-done((bf16[256,512]{1,0:T(8,128)(2,1)}, bf16[256,512]{1,0:T(8,128)(2,1)S(1)}, u32[]{:S(2)}, u32[]{:S(2)}) %collective-permute-start.11) | collective-permute-done | bytes 262176 | tf_op jit(solution)/shard_map/ppermute | solution.py:24
  66.6 1.1 pad_maximum_fusion.3.rest_6_
  69.2 1.2 collective-permute-start.12
  70.4 7.4 %collective-permute-done.14.refs_1_ = bf16[2,512,256]{2,1,0:T(8,128)(2,1)S(1)} collective-permute-done((bf16[2,512,256]{2,1,0:T(8,128)(2,1)}, bf16[2,512,256]{2,1,0:T(8,128)(2,1)S(1)}, u32[]{:S(2)}, u32[]{:S(2)}) %collective-permute-start.14) | collective-permute-done | bytes 524320 | tf_op jit(solution)/shard_map/ppermute | solution.py:24
  77.8 1.2 copy-done
  81.6 1.2 collective-permute-start.17
  82.9 2.6 %collective-permute-done.13.rest_7_ = bf16[2,256,512]{2,1,0:T(8,128)(2,1)} collective-permute-done((bf16[2,256,512]{2,1,0:T(8,128)(2,1)S(1)}, bf16[2,256,512]{2,1,0:T(8,128)(2,1)}, u32[]{:S(2)}, u32[]{:S(2)}) %collective-permute-start.13) | collective-permute-done | bytes 524320 | tf_op jit(solution)/shard_map/ppermute | solution.py:24
  85.5 3.6 %collective-permute-done.12.rest_5_ = bf16[2,256,512]{2,1,0:T(8,128)(2,1)} collective-permute-done((bf16[2,256,512]{2,1,0:T(8,128)(2,1)S(1)}, bf16[2,256,512]{2,1,0:T(8,128)(2,1)}, u32[]{:S(2)}, u32[]{:S(2)}) %collective-permute-start.12) | collective-permute-done | bytes 524320 | tf_op jit(solution)/shard_map/ppermute | solution.py:24
  91.2 7.8 %shard_map.132 = (f32[512,512]{1,0:T(8,128)}, bf16[4,1024,512]{2,1,0:T(8,128)(2,1)}) custom-call(s32[4]{0:T(128)S(1)} %pad_add_fusion.1.places_ref, s32[4]{0:T(128)S(1)} %pad_add_fusion.2.offsets_ref, bf16[512,8192]{1,0:T(8,128)(2,1)} %resid_ref.3, bf16[2,256,512]{2,1,0:T(8,128)(2,1)S(1)} %pad_maximum_fusion.rest_0_, bf16[2,256,512]{2,1,0:T(8,128)(2,1)S(1)} %copy-done.11, ...), custom_call_target="tpu_custom_call" | custom-call | flops 1024 | bytes 1024 | tf_op jit(solution)/shard_map/pallas_call | solution.py:237
  99.1 1.2 collective-permute-start.19
  104.0 1.3 shard_map.134
  105.3 3.3 %collective-permute-start.23 = (bf16[512,256]{1,0:T(8,128)(2,1)S(1)}, bf16[512,256]{1,0:T(8,128)(2,1)S(1)}, u32[]{:S(2)}, u32[]{:S(2)}) collective-permute-start(bf16[512,256]{1,0:T(8,128)(2,1)S(1)} %get-tuple-element.149), channel_id=1, source_target_pairs={{0,3},{1,0},{2,1},{3,2},{4,7},{5,4},{6,5},{7,6},{8,11},{9,8},{10,9... | collective-permute-start | bytes 786440 | tf_op jit(solution)/shard_map/ppermute | solution.py:24
  108.7 7.7 %shard_map.135 = (bf16[512,512]{1,0:T(8,128)(2,1)}, f32[512,1]{1,0:T(8,128)S(1)}) custom-call(s32[4]{0:T(128)S(1)} %pad_add_fusion.places_ref, bf16[512,8192]{1,0:T(8,128)(2,1)} %resid_ref.3, bf16[4,1024,512]{2,1,0:T(8,128)(2,1)} %collective-permute-done.18.weight_ref, f32[512,512]{1,0:T(8,128)} %get-tuple-element.150.first_ref, ...), custom_call_target="tpu_custom_call" | custom-call | flops 1024 | bytes 1024 | tf_op jit(solution)/shard_map/pallas_call | solution.py:275
  116.5 1.6 %collective-permute-start.21 = (bf16[512,256]{1,0:T(8,128)(2,1)S(1)}, bf16[512,256]{1,0:T(8,128)(2,1)S(1)}, u32[]{:S(2)}, u32[]{:S(2)}) collective-permute-start(bf16[512,256]{1,0:T(8,128)(2,1)S(1)} %get-tuple-element.162), channel_id=1, source_target_pairs={{0,16},{16,0},{1,17},{17,1},{2,18},{18,2},{3,19},{19,3},{4,20},{20... | collective-permute-start | bytes 786440 | tf_op jit(solution)/shard_map/ppermute | solution.py:24
  118.9 7.7 %shard_map.137.rest_0_ = bf16[512,8192]{1,0:T(8,128)(2,1)} custom-call(s32[4]{0:T(128)S(1)} %pad_add_fusion.1.places_ref, bf16[512,8192]{1,0:T(8,128)(2,1)} %resid_ref.3, bf16[4,1024,512]{2,1,0:T(8,128)(2,1)} %get-tuple-element.144.weight_ref, bf16[512,512]{1,0:T(8,128)(2,1)S(1)} %get-tuple-element.151.cot_ref, f32[512,1]{1,0:T(8,128)S(1)} %get-tuple-element.157.coef_ref), custom_call_target="tpu_custom_call" | custom-call | flops 1024 | bytes 1024 | tf_op jit(solution)/shard_map/pallas_call | solution.py:275
  127.5 7.7 %shard_map.138 = bf16[512,8192]{1,0:T(8,128)(2,1)} custom-call(s32[4]{0:T(128)S(1)} %pad_add_fusion.places_ref, bf16[512,8192]{1,0:T(8,128)(2,1)} %resid_ref.3, bf16[4,1024,512]{2,1,0:T(8,128)(2,1)} %collective-permute-done.18.weight_ref, bf16[512,512]{1,0:T(8,128)(2,1)S(1)} %get-tuple-element.151.cot_ref, ...), custom_call_target="tpu_custom_call", output_to_operand_aliasing={{}: (5, {})} | custom-call | flops 1024 | bytes 1024 | tf_op jit(solution)/shard_map/pallas_call | solution.py:275
  (99 shorter events, 26.1 us)
Async XLA Ops:
  0.6 19.1 %copy-start.20 = (s32[8]{0:T(128)S(1)}, s32[8]{0:T(128)}, u32[]{:S(2)}) copy-start(s32[8]{0:T(128)} %param.19) | copy-start | bytes 100
  2.1 4.9 %collective-permute-start = (f32[1,52,128]{2,1,0:T(8,128)S(1)}, f32[1,52,128]{2,1,0:T(8,128)S(1)}, u32[]{:S(2)}, u32[]{:S(2)}) collective-permute-start(f32[1,52,128]{2,1,0:T(8,128)S(1)} %maximum_bitcast_fusion), channel_id=1, source_target_pairs={{0,1},{1,0},{2,3},{3,2},{4,5},{5,4},{6,7},{7,6},{8,9},{9,8},{10,11... | collective-permute-start | bytes 79880 | tf_op jit(solution)/shard_map/ppermute | solution.py:29
  6.9 30.0 %copy-start.15 = (bf16[256,512]{1,0:T(8,128)(2,1)}, bf16[256,512]{1,0:T(8,128)(2,1)S(1)}, u32[]{:S(2)}) copy-start(bf16[256,512]{1,0:T(8,128)(2,1)S(1)} %multiply_convert_fusion) | copy-start | bytes 786436
  7.0 9.5 %collective-permute-start.1 = (bf16[256,512]{1,0:T(8,128)(2,1)S(1)}, bf16[256,512]{1,0:T(8,128)(2,1)S(1)}, u32[]{:S(2)}, u32[]{:S(2)}) collective-permute-start(bf16[256,512]{1,0:T(8,128)(2,1)S(1)} %multiply_convert_fusion), channel_id=1, source_target_pairs={{0,1},{1,2},{2,3},{3,0},{4,5},{5,6},{6,7},{7,4},{8,9},{9,10},{10,1... | collective-permute-start | bytes 786440 | tf_op jit(solution)/shard_map/ppermute | solution.py:24
  9.0 7.5 %collective-permute-start.2 = (bf16[256,512]{1,0:T(8,128)(2,1)S(1)}, bf16[256,512]{1,0:T(8,128)(2,1)S(1)}, u32[]{:S(2)}, u32[]{:S(2)}) collective-permute-start(bf16[256,512]{1,0:T(8,128)(2,1)S(1)} %multiply_convert_fusion), channel_id=1, source_target_pairs={{0,8},{8,0},{1,9},{9,1},{2,10},{10,2},{3,11},{11,3},{4,12},{12,4},... | collective-permute-start | bytes 786440 | tf_op jit(solution)/shard_map/ppermute | solution.py:24
  16.5 19.5 %copy-start.18 = (bf16[256,512]{1,0:T(8,128)(2,1)}, bf16[256,512]{1,0:T(8,128)(2,1)S(1)}, u32[]{:S(2)}) copy-start(bf16[256,512]{1,0:T(8,128)(2,1)S(1)} %collective-permute-done.1) | copy-start | bytes 786436
  16.5 19.5 %collective-permute-start.4 = (bf16[256,512]{1,0:T(8,128)(2,1)S(1)}, bf16[256,512]{1,0:T(8,128)(2,1)S(1)}, u32[]{:S(2)}, u32[]{:S(2)}) collective-permute-start(bf16[256,512]{1,0:T(8,128)(2,1)S(1)} %collective-permute-done.1), channel_id=1, source_target_pairs={{0,16},{16,0},{1,17},{17,1},{2,18},{18,2},{3,19},{19,3},{4,20},{20... | collective-permute-start | bytes 786440 | tf_op jit(solution)/shard_map/ppermute | solution.py:24
  18.0 18.0 %collective-permute-start.5 = (bf16[256,512]{1,0:T(8,128)(2,1)S(1)}, bf16[256,512]{1,0:T(8,128)(2,1)S(1)}, u32[]{:S(2)}, u32[]{:S(2)}) collective-permute-start(bf16[256,512]{1,0:T(8,128)(2,1)S(1)} %multiply_convert_fusion), channel_id=1, source_target_pairs={{0,3},{1,0},{2,1},{3,2},{4,7},{5,4},{6,5},{7,6},{8,11},{9,8},{10,9... | collective-permute-start | bytes 786440 | tf_op jit(solution)/shard_map/ppermute | solution.py:24
  20.4 6.8 %collective-permute-start.3 = (f32[2,52,128]{2,1,0:T(8,128)S(1)}, f32[2,52,128]{2,1,0:T(8,128)S(1)}, u32[]{:S(2)}, u32[]{:S(2)}) collective-permute-start(f32[2,52,128]{2,1,0:T(8,128)S(1)} %pad_maximum_fusion.5), channel_id=1, source_target_pairs={{0,2},{1,3},{2,0},{3,1},{4,6},{5,7},{6,4},{7,5},{8,10},{9,11},{10,... | collective-permute-start | bytes 159752 | tf_op jit(solution)/shard_map/ppermute | solution.py:29
  36.0 7.6 %collective-permute-start.6 = (bf16[4,4,512,256]{3,2,1,0:T(8,128)(2,1)}, bf16[4,4,512,256]{3,2,1,0:T(8,128)(2,1)}, u32[]{:S(2)}, u32[]{:S(2)}) collective-permute-start(bf16[4,4,512,256]{3,2,1,0:T(8,128)(2,1)} %shard_map.130), channel_id=1, source_target_pairs={{0,4},{4,0},{1,5},{5,1},{2,6},{6,2},{3,7},{7,3},{8,12},{12,8},{9,1... | collective-permute-start | bytes 12582920 | tf_op jit(solution)/shard_map/ppermute | solution.py:24
  36.9 15.0 %collective-permute-start.8 = (bf16[2,256,512]{2,1,0:T(8,128)(2,1)S(1)}, bf16[2,256,512]{2,1,0:T(8,128)(2,1)S(1)}, u32[]{:S(2)}, u32[]{:S(2)}) collective-permute-start(bf16[2,256,512]{2,1,0:T(8,128)(2,1)S(1)} %pad_maximum_fusion.rest_0_), channel_id=1, source_target_pairs={{0,16},{16,0},{1,17},{17,1},{2,18},{18,2},{3,19},{19,3},{4,20},{20... | collective-permute-start | bytes 1572872 | tf_op jit(solution)/shard_map/ppermute | solution.py:24
  38.5 17.8 %collective-permute-start.9 = (bf16[2,256,512]{2,1,0:T(8,128)(2,1)S(1)}, bf16[2,256,512]{2,1,0:T(8,128)(2,1)S(1)}, u32[]{:S(2)}, u32[]{:S(2)}) collective-permute-start(bf16[2,256,512]{2,1,0:T(8,128)(2,1)S(1)} %pad_maximum_fusion.1.rest_2_), channel_id=1, source_target_pairs={{0,8},{8,0},{1,9},{9,1},{2,10},{10,2},{3,11},{11,3},{4,12},{12,4},... | collective-permute-start | bytes 1572872 | tf_op jit(solution)/shard_map/ppermute | solution.py:24
  39.8 16.5 %collective-permute-start.10 = (bf16[256,512]{1,0:T(8,128)(2,1)}, bf16[256,512]{1,0:T(8,128)(2,1)}, u32[]{:S(2)}, u32[]{:S(2)}) collective-permute-start(bf16[256,512]{1,0:T(8,128)(2,1)} %copy-done.16), channel_id=1, source_target_pairs={{0,16},{16,0},{1,17},{17,1},{2,18},{18,2},{3,19},{19,3},{4,20},{20... | collective-permute-start | bytes 786440 | tf_op jit(solution)/shard_map/ppermute | solution.py:24
  41.3 15.0 %collective-permute-start.7 = (bf16[256,512]{1,0:T(8,128)(2,1)}, bf16[256,512]{1,0:T(8,128)(2,1)}, u32[]{:S(2)}, u32[]{:S(2)}) collective-permute-start(bf16[256,512]{1,0:T(8,128)(2,1)} %copy-done.15), channel_id=1, source_target_pairs={{0,2},{1,3},{2,0},{3,1},{4,6},{5,7},{6,4},{7,5},{8,10},{9,11},{10,... | collective-permute-start | bytes 786440 | tf_op jit(solution)/shard_map/ppermute | solution.py:24
  42.4 25.8 %copy-start.17 = (bf16[256,512]{1,0:T(8,128)(2,1)S(1)}, bf16[256,512]{1,0:T(8,128)(2,1)}, u32[]{:S(2)}) copy-start(bf16[256,512]{1,0:T(8,128)(2,1)} %copy-done.16) | copy-start | bytes 786436
  51.9 16.3 %copy-start.10 = (bf16[2,256,512]{2,1,0:T(8,128)(2,1)}, bf16[2,256,512]{2,1,0:T(8,128)(2,1)S(1)}, u32[]{:S(2)}) copy-start(bf16[2,256,512]{2,1,0:T(8,128)(2,1)S(1)} %collective-permute-done.8.rest_1_) | copy-start | bytes 1572868
  57.1 9.5 %collective-permute-start.11 = (bf16[256,512]{1,0:T(8,128)(2,1)}, bf16[256,512]{1,0:T(8,128)(2,1)S(1)}, u32[]{:S(2)}, u32[]{:S(2)}) collective-permute-start(bf16[256,512]{1,0:T(8,128)(2,1)} %collective-permute-done.7), channel_id=1, source_target_pairs={{0,8},{8,0},{1,9},{9,1},{2,10},{10,2},{3,11},{11,3},{4,12},{12,4},... | collective-permute-start | bytes 786440 | tf_op jit(solution)/shard_map/ppermute | solution.py:24
  58.3 19.5 %collective-permute-start.14 = (bf16[2,512,256]{2,1,0:T(8,128)(2,1)}, bf16[2,512,256]{2,1,0:T(8,128)(2,1)S(1)}, u32[]{:S(2)}, u32[]{:S(2)}) collective-permute-start(bf16[2,512,256]{2,1,0:T(8,128)(2,1)} %get-tuple-element.139), channel_id=1, source_target_pairs={{0,8},{8,0},{1,9},{9,1},{2,10},{10,2},{3,11},{11,3},{4,12},{12,4},... | collective-permute-start | bytes 1572872 | tf_op jit(solution)/shard_map/ppermute | solution.py:24
  59.1 18.7 %collective-permute-start.15 = (bf16[2,512,256]{2,1,0:T(8,128)(2,1)}, bf16[2,512,256]{2,1,0:T(8,128)(2,1)S(1)}, u32[]{:S(2)}, u32[]{:S(2)}) collective-permute-start(bf16[2,512,256]{2,1,0:T(8,128)(2,1)} %get-tuple-element.141), channel_id=1, source_target_pairs={{0,16},{16,0},{1,17},{17,1},{2,18},{18,2},{3,19},{19,3},{4,20},{20... | collective-permute-start | bytes 1572872 | tf_op jit(solution)/shard_map/ppermute | solution.py:24
  66.6 34.3 %copy-start.1 = (bf16[2,512,256]{2,1,0:T(8,128)(2,1)S(1)}, bf16[2,512,256]{2,1,0:T(8,128)(2,1)}, u32[]{:S(2)}) copy-start(bf16[2,512,256]{2,1,0:T(8,128)(2,1)} %get-tuple-element.138.refs_0_) | copy-start | bytes 1572868
  67.6 17.9 %collective-permute-start.13 = (bf16[2,256,512]{2,1,0:T(8,128)(2,1)S(1)}, bf16[2,256,512]{2,1,0:T(8,128)(2,1)}, u32[]{:S(2)}, u32[]{:S(2)}) collective-permute-start(bf16[2,256,512]{2,1,0:T(8,128)(2,1)S(1)} %pad_maximum_fusion.3.rest_6_), channel_id=1, source_target_pairs={{0,16},{16,0},{1,17},{17,1},{2,18},{18,2},{3,19},{19,3},{4,20},{20... | collective-permute-start | bytes 1572872 | tf_op jit(solution)/shard_map/ppermute | solution.py:24
  69.2 19.9 %collective-permute-start.12 = (bf16[2,256,512]{2,1,0:T(8,128)(2,1)S(1)}, bf16[2,256,512]{2,1,0:T(8,128)(2,1)}, u32[]{:S(2)}, u32[]{:S(2)}) collective-permute-start(bf16[2,256,512]{2,1,0:T(8,128)(2,1)S(1)} %pad_maximum_fusion.2.rest_4_), channel_id=1, source_target_pairs={{0,8},{8,0},{1,9},{9,1},{2,10},{10,2},{3,11},{11,3},{4,12},{12,4},... | collective-permute-start | bytes 1572872 | tf_op jit(solution)/shard_map/ppermute | solution.py:24
  81.1 17.9 %collective-permute-start.16 = (bf16[512,256]{1,0:T(8,128)(2,1)}, bf16[512,256]{1,0:T(8,128)(2,1)}, u32[]{:S(2)}, u32[]{:S(2)}) collective-permute-start(bf16[512,256]{1,0:T(8,128)(2,1)} %get-tuple-element.142), channel_id=1, source_target_pairs={{0,16},{16,0},{1,17},{17,1},{2,18},{18,2},{3,19},{19,3},{4,20},{20... | collective-permute-start | bytes 786440 | tf_op jit(solution)/shard_map/ppermute | solution.py:24
  81.6 17.4 %collective-permute-start.17 = (bf16[512,256]{1,0:T(8,128)(2,1)}, bf16[512,256]{1,0:T(8,128)(2,1)}, u32[]{:S(2)}, u32[]{:S(2)}) collective-permute-start(bf16[512,256]{1,0:T(8,128)(2,1)} %get-tuple-element.143), channel_id=1, source_target_pairs={{0,8},{8,0},{1,9},{9,1},{2,10},{10,2},{3,11},{11,3},{4,12},{12,4},... | collective-permute-start | bytes 786440 | tf_op jit(solution)/shard_map/ppermute | solution.py:24
  99.0 9.7 %collective-permute-start.18 = (bf16[4,1024,512]{2,1,0:T(8,128)(2,1)}, bf16[4,1024,512]{2,1,0:T(8,128)(2,1)}, u32[]{:S(2)}, u32[]{:S(2)}) collective-permute-start(bf16[4,1024,512]{2,1,0:T(8,128)(2,1)} %get-tuple-element.144.weight_ref), channel_id=1, source_target_pairs={{0,4},{4,0},{1,5},{5,1},{2,6},{6,2},{3,7},{7,3},{8,12},{12,8},{9,1... | collective-permute-start | bytes 12582920 | tf_op jit(solution)/shard_map/ppermute | solution.py:24
  99.1 17.3 %collective-permute-start.19 = (bf16[2,512,256]{2,1,0:T(8,128)(2,1)}, bf16[2,512,256]{2,1,0:T(8,128)(2,1)S(1)}, u32[]{:S(2)}, u32[]{:S(2)}) collective-permute-start(bf16[2,512,256]{2,1,0:T(8,128)(2,1)} %get-tuple-element.154), channel_id=1, source_target_pairs={{0,8},{8,0},{1,9},{9,1},{2,10},{10,2},{3,11},{11,3},{4,12},{12,4},... | collective-permute-start | bytes 1572872 | tf_op jit(solution)/shard_map/ppermute | solution.py:24
  100.3 16.1 %collective-permute-start.20 = (bf16[2,512,256]{2,1,0:T(8,128)(2,1)}, bf16[2,512,256]{2,1,0:T(8,128)(2,1)S(1)}, u32[]{:S(2)}, u32[]{:S(2)}) collective-permute-start(bf16[2,512,256]{2,1,0:T(8,128)(2,1)} %get-tuple-element.155), channel_id=1, source_target_pairs={{0,16},{16,0},{1,17},{17,1},{2,18},{18,2},{3,19},{19,3},{4,20},{20... | collective-permute-start | bytes 1572872 | tf_op jit(solution)/shard_map/ppermute | solution.py:24
  105.3 21.3 %collective-permute-start.23 = (bf16[512,256]{1,0:T(8,128)(2,1)S(1)}, bf16[512,256]{1,0:T(8,128)(2,1)S(1)}, u32[]{:S(2)}, u32[]{:S(2)}) collective-permute-start(bf16[512,256]{1,0:T(8,128)(2,1)S(1)} %get-tuple-element.149), channel_id=1, source_target_pairs={{0,3},{1,0},{2,1},{3,2},{4,7},{5,4},{6,5},{7,6},{8,11},{9,8},{10,9... | collective-permute-start | bytes 786440 | tf_op jit(solution)/shard_map/ppermute | solution.py:24
  108.6 18.0 %collective-permute-start.24 = (bf16[512,256]{1,0:T(8,128)(2,1)S(1)}, bf16[512,256]{1,0:T(8,128)(2,1)S(1)}, u32[]{:S(2)}, u32[]{:S(2)}) collective-permute-start(bf16[512,256]{1,0:T(8,128)(2,1)S(1)} %get-tuple-element.148), channel_id=1, source_target_pairs={{0,2},{1,3},{2,0},{3,1},{4,6},{5,7},{6,4},{7,5},{8,10},{9,11},{10,... | collective-permute-start | bytes 786440 | tf_op jit(solution)/shard_map/ppermute | solution.py:24
  116.5 10.1 %collective-permute-start.21 = (bf16[512,256]{1,0:T(8,128)(2,1)S(1)}, bf16[512,256]{1,0:T(8,128)(2,1)S(1)}, u32[]{:S(2)}, u32[]{:S(2)}) collective-permute-start(bf16[512,256]{1,0:T(8,128)(2,1)S(1)} %get-tuple-element.162), channel_id=1, source_target_pairs={{0,16},{16,0},{1,17},{17,1},{2,18},{18,2},{3,19},{19,3},{4,20},{20... | collective-permute-start | bytes 786440 | tf_op jit(solution)/shard_map/ppermute | solution.py:24
  118.0 8.6 %collective-permute-start.22 = (bf16[512,256]{1,0:T(8,128)(2,1)S(1)}, bf16[512,256]{1,0:T(8,128)(2,1)S(1)}, u32[]{:S(2)}, u32[]{:S(2)}) collective-permute-start(bf16[512,256]{1,0:T(8,128)(2,1)S(1)} %get-tuple-element.163), channel_id=1, source_target_pairs={{0,8},{8,0},{1,9},{9,1},{2,10},{10,2},{3,11},{11,3},{4,12},{12,4},... | collective-permute-start | bytes 786440 | tf_op jit(solution)/shard_map/ppermute | solution.py:24
  126.8 9.1 %collective-permute-start.25 = (bf16[512,256]{1,0:T(8,128)(2,1)S(1)}, bf16[512,256]{1,0:T(8,128)(2,1)S(1)}, u32[]{:S(2)}, u32[]{:S(2)}) collective-permute-start(bf16[512,256]{1,0:T(8,128)(2,1)S(1)} %fusion.1), channel_id=1, source_target_pairs={{0,1},{1,2},{2,3},{3,0},{4,5},{5,6},{6,7},{7,4},{8,9},{9,10},{10,1... | collective-permute-start | bytes 786440 | tf_op jit(solution)/shard_map/ppermute | solution.py:24
  (16 other events, 57.7 us)

commit v13 on v12

--- a/solution.py
+++ b/solution.py
@@ -383,21 +383,23 @@
     )
     packed = jnp.concatenate([ref_shard_max[0], ref_shard_sum[0], owned, trainee_logp])
     packed = packed.reshape(1, -1, 128)
-    packed = jnp.concatenate([packed, trade(packed, "tp", 1)])
-
-    gained = (value_weight.astype(F32) * norm_gain.astype(F32)[:, None]).astype(BF16)
-    residual, gained, packed = lax.optimization_barrier((residual, gained, packed))
     resid_wide = residual.astype(F32)
     squares = jnp.sum(resid_wide * resid_wide, axis=1, keepdims=True)
+    squares, packed, late_gain, late_weight = lax.optimization_barrier(
+        (squares, packed, norm_gain, value_weight)
+    )
+    packed = jnp.concatenate([packed, trade(packed, "tp", 1)])
+
+    gained = (late_weight.astype(F32) * late_gain.astype(F32)[:, None]).astype(BF16)
+    gained, packed = lax.optimization_barrier((gained, packed))
 
     def near_of(k, block):
         first = "inner" if inner_first(k) else "outer"
         return [swap(block, first, s) for s in range(1, lax.axis_size(first))]
 
-    def far_of(k, block, nears):
+    def far_of(k, stacked):
         second = "outer" if inner_first(k) else "inner"
-        near = jnp.stack([block] + nears)
-        return [near] + [swap(near, second, s) for s in range(1, lax.axis_size(second))]
+        return [stacked] + [swap(stacked, second, s) for s in range(1, lax.axis_size(second))]
 
     mask = 2
     while mask < tp_count:
@@ -406,15 +408,14 @@
     own_pieces, near = {}, {}
     arrived = {0: gained, 1: swap(gained, "tp", shifts[1])}
     near[0] = near_of(0, gained)
-    arrived[1], near[0], squares, late_gained = lax.optimization_barrier(
-        (arrived[1], near[0], squares, gained)
+    arrived[1], near[0], packed, late_gained = lax.optimization_barrier(
+        (arrived[1], near[0], packed, gained)
     )
     near[1] = near_of(1, arrived[1])
-    arrived[2] = swap(late_gained, "tp", shifts[2])
-    own_pieces[0] = far_of(0, gained, near[0])
+    for k in order[2:]:
+        arrived[k] = swap(late_gained, "tp", shifts[k])
     seq_length = lax.dynamic_index_in_dim(lengths, rep_place, keepdims=False)
     info = jnp.stack([tp_place, seq_length]).astype(jnp.int32)
-    packed, squares, info = lax.optimization_barrier((packed, squares, info))
     cot, cot_t, inv_rms = scaled_cot(width, rep_count, info, packed, squares, value_cot)
 
     def place_of(o, i, c, k):
@@ -480,24 +481,19 @@
         ]
 
     theirs = for_others(cot_t)
-    theirs, near[1], arrived[2], late_gained = lax.optimization_barrier(
-        (theirs, near[1], arrived[2], late_gained)
-    )
+    theirs, near[1], arrived = lax.optimization_barrier((theirs, near[1], arrived))
     other = swap(theirs, "core", 1)
-    for k in order[3:]:
-        arrived[k] = swap(late_gained, "tp", shifts[k])
-    own_pieces[1] = far_of(1, arrived[1], near[1])
-    near[2] = near_of(2, arrived[2])
+    for k in order[2:]:
+        near[k] = near_of(k, arrived[k])
+    for k in order[:2]:
+        own_pieces[k] = far_of(k, jnp.stack([arrived[k]] + near[k]))
     sides = for_us(other)
-    sides, arrived, own_pieces, near[2] = lax.optimization_barrier(
-        (sides, arrived, own_pieces, near[2])
-    )
-    for k in order[3:]:
-        near[k] = near_of(k, arrived[k])
+    near, own_pieces, late_sides = lax.optimization_barrier((near, own_pieces, sides))
+    stacked = {k: jnp.stack([arrived[k]] + near[k]) for k in order[2:]}
+    sides, stacked = lax.optimization_barrier((late_sides, stacked))
+    for k in order[2:]:
+        own_pieces[k] = far_of(k, stacked[k])
     got = [first_round(sides[0])]
-    near, sides[1:] = lax.optimization_barrier((near, sides[1:]))
-    for k in order[2:]:
-        own_pieces[k] = far_of(k, arrived[k], near[k])
     first_later, _ = second_round(sides[0], got[0])
     later = [first_later]
     sides[1:], own_pieces = lax.optimization_barrier((sides[1:], own_pieces))

time: 139 us -> 145 us (1.043)
  waiting for transfers between devices: 33 us -> 39.7 us
  local copies, waits for them, and re-layouts: 11.1 us -> 8.14 us
  starting transfers between devices: 29.2 us -> 31.9 us
  other arithmetic: 13.4 us -> 11.7 us
    ppermute x24, waiting for transfers between devices: 27.8 us -> 32.4 us  [swap(): lax.ppermute(value, axis, [(place, (place + step) % size) for place in ra...]
    unnamed x45 -> x43, local copies, waits for them, and re-layouts: 10.1 us -> 7.09 us
    ppermute x2, waiting for transfers between devices: 5.26 us -> 7.28 us  [trade(): lax.ppermute(value, axis, [(place, place ^ mask) for place in range(size)])]
    ppermute x2, starting transfers between devices: 3.81 us -> 5.68 us  [trade(): lax.ppermute(value, axis, [(place, place ^ mask) for place in range(size)])]
    convert_element_type x2, other arithmetic: 1.71 us -> 0.11 us  [the longest x1 0.11 us: per_device(): (late_weight.astype(F32) * late_gain.astype(F32)[:, None]).astype(BF16)]
    another operation x4 -> x3, other arithmetic: 3.18 us -> 2.6 us  [the longest x1 2.5 us: per_device(): stacked = {k: jnp.stack([arrived[k]] + near[k]) for k in order[2:]}]
  transfers between devices with their start and end apart: 26 -> 26, of which waited for: 10 -> 10; matrix products, arithmetic and copies ran while one was open for 9% -> 1% of each run, Pallas kernels for 36% -> 36%
where the time goes in v13:
time: 145 us; the launch traced here: 144 us
  Pallas kernels  51.5 us (36%)
  waiting for transfers between devices  39.7 us (27%)
  starting transfers between devices  31.9 us (22%)
  other arithmetic  11.7 us (8%)
  local copies, waits for them, and re-layouts  8.14 us (6%)
    ppermute x24, waiting for transfers between devices, swap(): lax.ppermute(value, axis, [(place, (place + step) % size) for place in ra...  32.4 us
    ppermute x24, starting transfers between devices, swap(): lax.ppermute(value, axis, [(place, (place + step) % size) for place in ra...  26.2 us
    pallas_call x3, Pallas kernels, weight_call(): pl.pallas_call(kernel, out_shape=out_shape, grid_spec=pltpu.PrefetchScala...  23.1 us
    pallas_call x2, Pallas kernels, grad_product(): pl.pallas_call(kernel, out_shape=out_shape, grid_spec=pltpu.PrefetchScala...  14.9 us
    pallas_call x1, Pallas kernels, first_value(): pl.pallas_call(functools.partial(value_kernel, inner_flags), out_shape=[t...  7.96 us
    ppermute x2, waiting for transfers between devices, trade(): lax.ppermute(value, axis, [(place, place ^ mask) for place in range(size)])  7.28 us
    unnamed x43, local copies, waits for them, and re-layouts  7.09 us
    ppermute x2, starting transfers between devices, trade(): lax.ppermute(value, axis, [(place, place ^ mask) for place in range(size)])  5.68 us
  transfers between devices with their start and end apart: 26, of which 10 were waited for; matrix products, arithmetic and copies ran while one was open for 1% of the time, Pallas kernels for 36%

profile of v13, /device:TPU:0, one launch (start us, length us, event | category | flops | bytes accessed | tf_op | source)
XLA Modules:
  0.0 143.9 jit_solution(409104930681080413)
XLA Ops:
  0.7 5.1 %multiply_reduce_fusion = f32[512]{0:T(512)S(1)} fusion(bf16[512,8192]{1,0:T(8,128)(2,1)} %resid_ref.7), kind=kLoop, calls=%fused_computation | loop fusion | flops 12582400 | bytes 8390656 | tf_op jit(solution)/shard_map/reduce_sum | solution.py:387
  5.9 3.1 %collective-permute-start = (f32[1,52,128]{2,1,0:T(8,128)S(1)}, f32[1,52,128]{2,1,0:T(8,128)S(1)}, u32[]{:S(2)}, u32[]{:S(2)}) collective-permute-start(f32[1,52,128]{2,1,0:T(8,128)S(1)} %maximum_bitcast_fusion), channel_id=1, source_target_pairs={{0,1},{1,0},{2,3},{3,2},{4,5},{5,4},{6,7},{7,6},{8,9},{9,8},{10,11... | collective-permute-start | bytes 79880 | tf_op jit(solution)/shard_map/ppermute | solution.py:29
  9.2 1.7 %collective-permute-done = f32[1,52,128]{2,1,0:T(8,128)S(1)} collective-permute-done((f32[1,52,128]{2,1,0:T(8,128)S(1)}, f32[1,52,128]{2,1,0:T(8,128)S(1)}, u32[]{:S(2)}, u32[]{:S(2)}) %collective-permute-start) | collective-permute-done | bytes 26656 | tf_op jit(solution)/shard_map/ppermute | solution.py:29
  10.9 2.0 %collective-permute-start.1 = (bf16[256,512]{1,0:T(8,128)(2,1)S(1)}, bf16[256,512]{1,0:T(8,128)(2,1)S(1)}, u32[]{:S(2)}, u32[]{:S(2)}) collective-permute-start(bf16[256,512]{1,0:T(8,128)(2,1)S(1)} %multiply_convert_fusion), channel_id=1, source_target_pairs={{0,1},{1,2},{2,3},{3,0},{4,5},{5,6},{6,7},{7,4},{8,9},{9,10},{10,1... | collective-permute-start | bytes 786440 | tf_op jit(solution)/shard_map/ppermute | solution.py:24
  12.9 1.5 %collective-permute-start.2 = (bf16[256,512]{1,0:T(8,128)(2,1)S(1)}, bf16[256,512]{1,0:T(8,128)(2,1)S(1)}, u32[]{:S(2)}, u32[]{:S(2)}) collective-permute-start(bf16[256,512]{1,0:T(8,128)(2,1)S(1)} %multiply_convert_fusion), channel_id=1, source_target_pairs={{0,8},{8,0},{1,9},{9,1},{2,10},{10,2},{3,11},{11,3},{4,12},{12,4},... | collective-permute-start | bytes 786440 | tf_op jit(solution)/shard_map/ppermute | solution.py:24
  14.4 2.6 %collective-permute-start.3 = (f32[2,52,128]{2,1,0:T(8,128)S(1)}, f32[2,52,128]{2,1,0:T(8,128)S(1)}, u32[]{:S(2)}, u32[]{:S(2)}) collective-permute-start(f32[2,52,128]{2,1,0:T(8,128)S(1)} %pad_maximum_fusion.5), channel_id=1, source_target_pairs={{0,2},{1,3},{2,0},{3,1},{4,6},{5,7},{6,4},{7,5},{8,10},{9,11},{10,... | collective-permute-start | bytes 159752 | tf_op jit(solution)/shard_map/ppermute | solution.py:29
  17.0 5.6 %collective-permute-done.3 = f32[2,52,128]{2,1,0:T(8,128)S(1)} collective-permute-done((f32[2,52,128]{2,1,0:T(8,128)S(1)}, f32[2,52,128]{2,1,0:T(8,128)S(1)}, u32[]{:S(2)}, u32[]{:S(2)}) %collective-permute-start.3) | collective-permute-done | bytes 53280 | tf_op jit(solution)/shard_map/ppermute | solution.py:29
  22.6 1.6 %collective-permute-start.4 = (bf16[256,512]{1,0:T(8,128)(2,1)S(1)}, bf16[256,512]{1,0:T(8,128)(2,1)S(1)}, u32[]{:S(2)}, u32[]{:S(2)}) collective-permute-start(bf16[256,512]{1,0:T(8,128)(2,1)S(1)} %collective-permute-done.1), channel_id=1, source_target_pairs={{0,16},{16,0},{1,17},{17,1},{2,18},{18,2},{3,19},{19,3},{4,20},{20... | collective-permute-start | bytes 786440 | tf_op jit(solution)/shard_map/ppermute | solution.py:24
  24.2 1.6 %collective-permute-start.5 = (bf16[256,512]{1,0:T(8,128)(2,1)S(1)}, bf16[256,512]{1,0:T(8,128)(2,1)}, u32[]{:S(2)}, u32[]{:S(2)}) collective-permute-start(bf16[256,512]{1,0:T(8,128)(2,1)S(1)} %multiply_convert_fusion), channel_id=1, source_target_pairs={{0,3},{1,0},{2,1},{3,2},{4,7},{5,4},{6,5},{7,6},{8,11},{9,8},{10,9... | collective-permute-start | bytes 786440 | tf_op jit(solution)/shard_map/ppermute | solution.py:24
  27.4 2.1 %shard_map.129 = (bf16[512,512]{1,0:T(8,128)(2,1)S(1)}, bf16[512,512]{1,0:T(8,128)(2,1)S(1)}, f32[512,1]{1,0:T(8,128)S(1)}) custom-call(s32[2]{0:T(128)S(1)} %pad_add_fusion.3.info_ref, f32[4,52,128]{2,1,0:T(8,128)S(1)} %pad_maximum_fusion.4.shares_ref, f32[512,1]{1,0:T(8,128)S(1)} %copy.17.squares_ref, bf16[512,512]{1,0:T(8,128)(2,1)} %value_cot_ref.1), custom_call_target="tpu_custom_call" | custom-call | flops 1024 | bytes 1024 | tf_op jit(solution)/shard_map/pallas_call | solution.py:337
  29.5 6.6 %shard_map.130 = bf16[4,4,512,256]{3,2,1,0:T(8,128)(2,1)} custom-call(s32[16]{0:T(128)S(1)} %stack.221.places_ref, bf16[512,512]{1,0:T(8,128)(2,1)S(1)} %get-tuple-element.101.cot_ref, bf16[512,8192]{1,0:T(8,128)(2,1)} %resid_ref.7, bf16[512,8192]{1,0:T(8,128)(2,1)} %resid_ref.7, bf16[512,8192]{1,0:T(8,128)(2,1)} %resid_ref.7, bf16[512,8192]{1,0:T(8,128)(2,1)} %resid_ref.7), custom_call_target="tpu_custom_call" | custom-call | flops 1024 | bytes 1024 | tf_op jit(solution)/shard_map/pallas_call | solution.py:115
  36.1 5.2 %collective-permute-done.6 = bf16[256,512]{1,0:T(8,128)(2,1)} collective-permute-done((bf16[256,512]{1,0:T(8,128)(2,1)S(1)}, bf16[256,512]{1,0:T(8,128)(2,1)}, u32[]{:S(2)}, u32[]{:S(2)}) %collective-permute-start.6) | collective-permute-done | bytes 262176 | tf_op jit(solution)/shard_map/ppermute | solution.py:24
  41.3 1.6 %collective-permute-start.10 = (bf16[2,256,512]{2,1,0:T(8,128)(2,1)S(1)}, bf16[2,256,512]{2,1,0:T(8,128)(2,1)S(1)}, u32[]{:S(2)}, u32[]{:S(2)}) collective-permute-start(bf16[2,256,512]{2,1,0:T(8,128)(2,1)S(1)} %pad_maximum_fusion.1.rest_2_), channel_id=1, source_target_pairs={{0,8},{8,0},{1,9},{9,1},{2,10},{10,2},{3,11},{11,3},{4,12},{12,4},... | collective-permute-start | bytes 1572872 | tf_op jit(solution)/shard_map/ppermute | solution.py:24
  43.5 1.5 %collective-permute-start.7 = (bf16[256,512]{1,0:T(8,128)(2,1)}, bf16[256,512]{1,0:T(8,128)(2,1)}, u32[]{:S(2)}, u32[]{:S(2)}) collective-permute-start(bf16[256,512]{1,0:T(8,128)(2,1)} %collective-permute-done.5), channel_id=1, source_target_pairs={{0,16},{16,0},{1,17},{17,1},{2,18},{18,2},{3,19},{19,3},{4,20},{20... | collective-permute-start | bytes 786440 | tf_op jit(solution)/shard_map/ppermute | solution.py:24
  45.6 3.1 %collective-permute-done.11.rest_4_ = bf16[4,4,512,256]{3,2,1,0:T(8,128)(2,1)} collective-permute-done((bf16[4,4,512,256]{3,2,1,0:T(8,128)(2,1)}, bf16[4,4,512,256]{3,2,1,0:T(8,128)(2,1)}, u32[]{:S(2)}, u32[]{:S(2)}) %collective-permute-start.11) | collective-permute-done | bytes 4194336 | tf_op jit(solution)/shard_map/ppermute | solution.py:24
  48.8 8.3 %shard_map.131 = (bf16[2,512,256]{2,1,0:T(8,128)(2,1)}, bf16[2,512,256]{2,1,0:T(8,128)(2,1)}, bf16[2,512,256]{2,1,0:T(8,128)(2,1)}, bf16[2,512,256]{2,1,0:T(8,12...) custom-call(s32[16]{0:T(128)S(1)} %stack.246.places_ref, ...), custom_call_target="tpu_custom_call" | custom-call | flops 1024 | bytes 1024 | tf_op jit(solution)/shard_map/pallas_call | solution.py:115
  57.1 5.7 %collective-permute-done.7 = bf16[256,512]{1,0:T(8,128)(2,1)} collective-permute-done((bf16[256,512]{1,0:T(8,128)(2,1)}, bf16[256,512]{1,0:T(8,128)(2,1)}, u32[]{:S(2)}, u32[]{:S(2)}) %collective-permute-start.7) | collective-permute-done | bytes 262176 | tf_op jit(solution)/shard_map/ppermute | solution.py:24
  63.6 2.5 %pad_maximum_fusion.2 = (bf16[2,256,512]{2,1,0:T(8,128)(2,1)}, bf16[2,256,512]{2,1,0:T(8,128)(2,1)}) fusion(bf16[1,256,512]{2,1,0:T(8,128)(2,1)} %bitcast.55, bf16[1,256,512]{2,1,0:T(8,128)(2,1)} %bitcast.54, bf16[1,256,512]{2,1,0:T(8,128)(2,1)} %bitcast.57, bf16[1,256,512]{2,1,0:T(8,128)(2,1)} %bitcast.56), kind=kLoop, calls=%fused_computation.3 | loop fusion | flops 524288 | bytes 2097152 | tf_op jit(solution)/shard_map/stack | solution.py:492
  67.1 1.5 %collective-permute-start.12 = (bf16[2,256,512]{2,1,0:T(8,128)(2,1)}, bf16[2,256,512]{2,1,0:T(8,128)(2,1)}, u32[]{:S(2)}, u32[]{:S(2)}) collective-permute-start(bf16[2,256,512]{2,1,0:T(8,128)(2,1)} %get-tuple-element.142.rest_4_), channel_id=1, source_target_pairs={{0,8},{8,0},{1,9},{9,1},{2,10},{10,2},{3,11},{11,3},{4,12},{12,4},... | collective-permute-start | bytes 1572872 | tf_op jit(solution)/shard_map/ppermute | solution.py:24
  68.6 1.5 %collective-permute-start.13 = (bf16[2,256,512]{2,1,0:T(8,128)(2,1)}, bf16[2,256,512]{2,1,0:T(8,128)(2,1)}, u32[]{:S(2)}, u32[]{:S(2)}) collective-permute-start(bf16[2,256,512]{2,1,0:T(8,128)(2,1)} %get-tuple-element.144.rest_6_), channel_id=1, source_target_pairs={{0,16},{16,0},{1,17},{17,1},{2,18},{18,2},{3,19},{19,3},{4,20},{20... | collective-permute-start | bytes 1572872 | tf_op jit(solution)/shard_map/ppermute | solution.py:24
  70.1 11.0 %collective-permute-done.14.refs_1_ = bf16[2,512,256]{2,1,0:T(8,128)(2,1)S(1)} collective-permute-done((bf16[2,512,256]{2,1,0:T(8,128)(2,1)}, bf16[2,512,256]{2,1,0:T(8,128)(2,1)S(1)}, u32[]{:S(2)}, u32[]{:S(2)}) %collective-permute-start.14) | collective-permute-done | bytes 524320 | tf_op jit(solution)/shard_map/ppermute | solution.py:24
  85.3 1.5 %collective-permute-start.17 = (bf16[512,256]{1,0:T(8,128)(2,1)}, bf16[512,256]{1,0:T(8,128)(2,1)}, u32[]{:S(2)}, u32[]{:S(2)}) collective-permute-start(bf16[512,256]{1,0:T(8,128)(2,1)} %get-tuple-element.153), channel_id=1, source_target_pairs={{0,8},{8,0},{1,9},{9,1},{2,10},{10,2},{3,11},{11,3},{4,12},{12,4},... | collective-permute-start | bytes 786440 | tf_op jit(solution)/shard_map/ppermute | solution.py:24
  87.0 5.5 %collective-permute-done.12.rest_5_ = bf16[2,256,512]{2,1,0:T(8,128)(2,1)} collective-permute-done((bf16[2,256,512]{2,1,0:T(8,128)(2,1)}, bf16[2,256,512]{2,1,0:T(8,128)(2,1)}, u32[]{:S(2)}, u32[]{:S(2)}) %collective-permute-start.12) | collective-permute-done | bytes 524320 | tf_op jit(solution)/shard_map/ppermute | solution.py:24
  95.1 8.0 %shard_map.132 = (f32[512,512]{1,0:T(8,128)}, bf16[4,1024,512]{2,1,0:T(8,128)(2,1)}) custom-call(s32[4]{0:T(128)S(1)} %pad_add_fusion.1.places_ref, s32[4]{0:T(128)S(1)} %pad_add_fusion.2.offsets_ref, bf16[512,8192]{1,0:T(8,128)(2,1)} %resid_ref.7, bf16[2,256,512]{2,1,0:T(8,128)(2,1)S(1)} %pad_maximum_fusion.rest_0_, bf16[2,256,512]{2,1,0:T(8,128)(2,1)S(1)} %copy-done.11, ...), custom_call_target="tpu_custom_call" | custom-call | flops 1024 | bytes 1024 | tf_op jit(solution)/shard_map/pallas_call | solution.py:237
  103.2 1.5 %collective-permute-start.19 = (bf16[2,512,256]{2,1,0:T(8,128)(2,1)}, bf16[2,512,256]{2,1,0:T(8,128)(2,1)}, u32[]{:S(2)}, u32[]{:S(2)}) collective-permute-start(bf16[2,512,256]{2,1,0:T(8,128)(2,1)} %get-tuple-element.164), channel_id=1, source_target_pairs={{0,8},{8,0},{1,9},{9,1},{2,10},{10,2},{3,11},{11,3},{4,12},{12,4},... | collective-permute-start | bytes 1572872 | tf_op jit(solution)/shard_map/ppermute | solution.py:24
  106.4 1.3 shard_map.134
  107.7 4.3 %collective-permute-start.23 = (bf16[512,256]{1,0:T(8,128)(2,1)S(1)}, bf16[512,256]{1,0:T(8,128)(2,1)S(1)}, u32[]{:S(2)}, u32[]{:S(2)}) collective-permute-start(bf16[512,256]{1,0:T(8,128)(2,1)S(1)} %get-tuple-element.159), channel_id=1, source_target_pairs={{0,3},{1,0},{2,1},{3,2},{4,7},{5,4},{6,5},{7,6},{8,11},{9,8},{10,9... | collective-permute-start | bytes 786440 | tf_op jit(solution)/shard_map/ppermute | solution.py:24
  112.0 7.7 %shard_map.135 = (bf16[512,512]{1,0:T(8,128)(2,1)}, f32[512,1]{1,0:T(8,128)S(1)}) custom-call(s32[4]{0:T(128)S(1)} %pad_add_fusion.places_ref, bf16[512,8192]{1,0:T(8,128)(2,1)} %resid_ref.7, bf16[4,1024,512]{2,1,0:T(8,128)(2,1)} %collective-permute-done.18.weight_ref, f32[512,512]{1,0:T(8,128)} %get-tuple-element.160.first_ref, ...), custom_call_target="tpu_custom_call" | custom-call | flops 1024 | bytes 1024 | tf_op jit(solution)/shard_map/pallas_call | solution.py:275
  119.7 1.2 shard_map.136
  120.9 1.6 %collective-permute-start.21 = (bf16[512,256]{1,0:T(8,128)(2,1)S(1)}, bf16[512,256]{1,0:T(8,128)(2,1)S(1)}, u32[]{:S(2)}, u32[]{:S(2)}) collective-permute-start(bf16[512,256]{1,0:T(8,128)(2,1)S(1)} %get-tuple-element.172), channel_id=1, source_target_pairs={{0,16},{16,0},{1,17},{17,1},{2,18},{18,2},{3,19},{19,3},{4,20},{20... | collective-permute-start | bytes 786440 | tf_op jit(solution)/shard_map/ppermute | solution.py:24
  123.0 7.7 %shard_map.137.rest_0_ = bf16[512,8192]{1,0:T(8,128)(2,1)} custom-call(s32[4]{0:T(128)S(1)} %pad_add_fusion.1.places_ref, bf16[512,8192]{1,0:T(8,128)(2,1)} %resid_ref.7, bf16[4,1024,512]{2,1,0:T(8,128)(2,1)} %get-tuple-element.154.weight_ref, bf16[512,512]{1,0:T(8,128)(2,1)S(1)} %get-tuple-element.161.cot_ref, f32[512,1]{1,0:T(8,128)S(1)} %get-tuple-element.167.coef_ref), custom_call_target="tpu_custom_call" | custom-call | flops 1024 | bytes 1024 | tf_op jit(solution)/shard_map/pallas_call | solution.py:275
  132.5 7.7 %shard_map.138 = bf16[512,8192]{1,0:T(8,128)(2,1)} custom-call(s32[4]{0:T(128)S(1)} %pad_add_fusion.places_ref, bf16[512,8192]{1,0:T(8,128)(2,1)} %resid_ref.7, bf16[4,1024,512]{2,1,0:T(8,128)(2,1)} %collective-permute-done.18.weight_ref, bf16[512,512]{1,0:T(8,128)(2,1)S(1)} %get-tuple-element.161.cot_ref, ...), custom_call_target="tpu_custom_call", output_to_operand_aliasing={{}: (5, {})} | custom-call | flops 1024 | bytes 1024 | tf_op jit(solution)/shard_map/pallas_call | solution.py:275
  (96 shorter events, 19.6 us)
Async XLA Ops:
  0.7 25.3 %copy-start.19 = (s32[8]{0:T(128)S(1)}, s32[8]{0:T(128)}, u32[]{:S(2)}) copy-start(s32[8]{0:T(128)} %param.19) | copy-start | bytes 100
  5.9 4.9 %collective-permute-start = (f32[1,52,128]{2,1,0:T(8,128)S(1)}, f32[1,52,128]{2,1,0:T(8,128)S(1)}, u32[]{:S(2)}, u32[]{:S(2)}) collective-permute-start(f32[1,52,128]{2,1,0:T(8,128)S(1)} %maximum_bitcast_fusion), channel_id=1, source_target_pairs={{0,1},{1,0},{2,3},{3,2},{4,5},{5,4},{6,7},{7,6},{8,9},{9,8},{10,11... | collective-permute-start | bytes 79880 | tf_op jit(solution)/shard_map/ppermute | solution.py:29
  10.9 11.7 %collective-permute-start.1 = (bf16[256,512]{1,0:T(8,128)(2,1)S(1)}, bf16[256,512]{1,0:T(8,128)(2,1)S(1)}, u32[]{:S(2)}, u32[]{:S(2)}) collective-permute-start(bf16[256,512]{1,0:T(8,128)(2,1)S(1)} %multiply_convert_fusion), channel_id=1, source_target_pairs={{0,1},{1,2},{2,3},{3,0},{4,5},{5,6},{6,7},{7,4},{8,9},{9,10},{10,1... | collective-permute-start | bytes 786440 | tf_op jit(solution)/shard_map/ppermute | solution.py:24
  12.9 9.7 %collective-permute-start.2 = (bf16[256,512]{1,0:T(8,128)(2,1)S(1)}, bf16[256,512]{1,0:T(8,128)(2,1)S(1)}, u32[]{:S(2)}, u32[]{:S(2)}) collective-permute-start(bf16[256,512]{1,0:T(8,128)(2,1)S(1)} %multiply_convert_fusion), channel_id=1, source_target_pairs={{0,8},{8,0},{1,9},{9,1},{2,10},{10,2},{3,11},{11,3},{4,12},{12,4},... | collective-permute-start | bytes 786440 | tf_op jit(solution)/shard_map/ppermute | solution.py:24
  14.4 8.1 %collective-permute-start.3 = (f32[2,52,128]{2,1,0:T(8,128)S(1)}, f32[2,52,128]{2,1,0:T(8,128)S(1)}, u32[]{:S(2)}, u32[]{:S(2)}) collective-permute-start(f32[2,52,128]{2,1,0:T(8,128)S(1)} %pad_maximum_fusion.5), channel_id=1, source_target_pairs={{0,2},{1,3},{2,0},{3,1},{4,6},{5,7},{6,4},{7,5},{8,10},{9,11},{10,... | collective-permute-start | bytes 159752 | tf_op jit(solution)/shard_map/ppermute | solution.py:29
  22.6 13.5 %collective-permute-start.4 = (bf16[256,512]{1,0:T(8,128)(2,1)S(1)}, bf16[256,512]{1,0:T(8,128)(2,1)S(1)}, u32[]{:S(2)}, u32[]{:S(2)}) collective-permute-start(bf16[256,512]{1,0:T(8,128)(2,1)S(1)} %collective-permute-done.1), channel_id=1, source_target_pairs={{0,16},{16,0},{1,17},{17,1},{2,18},{18,2},{3,19},{19,3},{4,20},{20... | collective-permute-start | bytes 786440 | tf_op jit(solution)/shard_map/ppermute | solution.py:24
  24.2 11.9 %collective-permute-start.5 = (bf16[256,512]{1,0:T(8,128)(2,1)S(1)}, bf16[256,512]{1,0:T(8,128)(2,1)}, u32[]{:S(2)}, u32[]{:S(2)}) collective-permute-start(bf16[256,512]{1,0:T(8,128)(2,1)S(1)} %multiply_convert_fusion), channel_id=1, source_target_pairs={{0,3},{1,0},{2,1},{3,2},{4,7},{5,4},{6,5},{7,6},{8,11},{9,8},{10,9... | collective-permute-start | bytes 786440 | tf_op jit(solution)/shard_map/ppermute | solution.py:24
  25.8 15.5 %collective-permute-start.6 = (bf16[256,512]{1,0:T(8,128)(2,1)S(1)}, bf16[256,512]{1,0:T(8,128)(2,1)}, u32[]{:S(2)}, u32[]{:S(2)}) collective-permute-start(bf16[256,512]{1,0:T(8,128)(2,1)S(1)} %multiply_convert_fusion), channel_id=1, source_target_pairs={{0,2},{1,3},{2,0},{3,1},{4,6},{5,7},{6,4},{7,5},{8,10},{9,11},{10,... | collective-permute-start | bytes 786440 | tf_op jit(solution)/shard_map/ppermute | solution.py:24
  41.3 7.5 %collective-permute-start.11 = (bf16[4,4,512,256]{3,2,1,0:T(8,128)(2,1)}, bf16[4,4,512,256]{3,2,1,0:T(8,128)(2,1)}, u32[]{:S(2)}, u32[]{:S(2)}) collective-permute-start(bf16[4,4,512,256]{3,2,1,0:T(8,128)(2,1)} %shard_map.130), channel_id=1, source_target_pairs={{0,4},{4,0},{1,5},{5,1},{2,6},{6,2},{3,7},{7,3},{8,12},{12,8},{9,1... | collective-permute-start | bytes 12582920 | tf_op jit(solution)/shard_map/ppermute | solution.py:24
  41.3 21.5 %collective-permute-start.10 = (bf16[2,256,512]{2,1,0:T(8,128)(2,1)S(1)}, bf16[2,256,512]{2,1,0:T(8,128)(2,1)S(1)}, u32[]{:S(2)}, u32[]{:S(2)}) collective-permute-start(bf16[2,256,512]{2,1,0:T(8,128)(2,1)S(1)} %pad_maximum_fusion.1.rest_2_), channel_id=1, source_target_pairs={{0,8},{8,0},{1,9},{9,1},{2,10},{10,2},{3,11},{11,3},{4,12},{12,4},... | collective-permute-start | bytes 1572872 | tf_op jit(solution)/shard_map/ppermute | solution.py:24
  42.9 20.6 %collective-permute-start.9 = (bf16[2,256,512]{2,1,0:T(8,128)(2,1)S(1)}, bf16[2,256,512]{2,1,0:T(8,128)(2,1)S(1)}, u32[]{:S(2)}, u32[]{:S(2)}) collective-permute-start(bf16[2,256,512]{2,1,0:T(8,128)(2,1)S(1)} %pad_maximum_fusion.rest_0_), channel_id=1, source_target_pairs={{0,16},{16,0},{1,17},{17,1},{2,18},{18,2},{3,19},{19,3},{4,20},{20... | collective-permute-start | bytes 1572872 | tf_op jit(solution)/shard_map/ppermute | solution.py:24
  43.5 19.3 %collective-permute-start.7 = (bf16[256,512]{1,0:T(8,128)(2,1)}, bf16[256,512]{1,0:T(8,128)(2,1)}, u32[]{:S(2)}, u32[]{:S(2)}) collective-permute-start(bf16[256,512]{1,0:T(8,128)(2,1)} %collective-permute-done.5), channel_id=1, source_target_pairs={{0,16},{16,0},{1,17},{17,1},{2,18},{18,2},{3,19},{19,3},{4,20},{20... | collective-permute-start | bytes 786440 | tf_op jit(solution)/shard_map/ppermute | solution.py:24
  45.0 17.8 %collective-permute-start.8 = (bf16[256,512]{1,0:T(8,128)(2,1)}, bf16[256,512]{1,0:T(8,128)(2,1)}, u32[]{:S(2)}, u32[]{:S(2)}) collective-permute-start(bf16[256,512]{1,0:T(8,128)(2,1)} %collective-permute-done.6), channel_id=1, source_target_pairs={{0,8},{8,0},{1,9},{9,1},{2,10},{10,2},{3,11},{11,3},{4,12},{12,4},... | collective-permute-start | bytes 786440 | tf_op jit(solution)/shard_map/ppermute | solution.py:24
  63.6 41.7 %copy-start.1 = (bf16[2,512,256]{2,1,0:T(8,128)(2,1)S(1)}, bf16[2,512,256]{2,1,0:T(8,128)(2,1)}, u32[]{:S(2)}) copy-start(bf16[2,512,256]{2,1,0:T(8,128)(2,1)} %get-tuple-element.148.refs_0_) | copy-start | bytes 1572868
  63.6 41.7 %copy-start.3 = (bf16[2,512,256]{2,1,0:T(8,128)(2,1)S(1)}, bf16[2,512,256]{2,1,0:T(8,128)(2,1)}, u32[]{:S(2)}) copy-start(bf16[2,512,256]{2,1,0:T(8,128)(2,1)} %get-tuple-element.150.refs_2_.refs_3_) | copy-start | bytes 1572868
  66.1 15.1 %collective-permute-start.14 = (bf16[2,512,256]{2,1,0:T(8,128)(2,1)}, bf16[2,512,256]{2,1,0:T(8,128)(2,1)S(1)}, u32[]{:S(2)}, u32[]{:S(2)}) collective-permute-start(bf16[2,512,256]{2,1,0:T(8,128)(2,1)} %get-tuple-element.149), channel_id=1, source_target_pairs={{0,8},{8,0},{1,9},{9,1},{2,10},{10,2},{3,11},{11,3},{4,12},{12,4},... | collective-permute-start | bytes 1572872 | tf_op jit(solution)/shard_map/ppermute | solution.py:24
  66.6 15.1 %collective-permute-start.15 = (bf16[2,512,256]{2,1,0:T(8,128)(2,1)}, bf16[2,512,256]{2,1,0:T(8,128)(2,1)S(1)}, u32[]{:S(2)}, u32[]{:S(2)}) collective-permute-start(bf16[2,512,256]{2,1,0:T(8,128)(2,1)} %get-tuple-element.151), channel_id=1, source_target_pairs={{0,16},{16,0},{1,17},{17,1},{2,18},{18,2},{3,19},{19,3},{4,20},{20... | collective-permute-start | bytes 1572872 | tf_op jit(solution)/shard_map/ppermute | solution.py:24
  67.1 25.4 %collective-permute-start.12 = (bf16[2,256,512]{2,1,0:T(8,128)(2,1)}, bf16[2,256,512]{2,1,0:T(8,128)(2,1)}, u32[]{:S(2)}, u32[]{:S(2)}) collective-permute-start(bf16[2,256,512]{2,1,0:T(8,128)(2,1)} %get-tuple-element.142.rest_4_), channel_id=1, source_target_pairs={{0,8},{8,0},{1,9},{9,1},{2,10},{10,2},{3,11},{11,3},{4,12},{12,4},... | collective-permute-start | bytes 1572872 | tf_op jit(solution)/shard_map/ppermute | solution.py:24
  68.6 24.4 %collective-permute-start.13 = (bf16[2,256,512]{2,1,0:T(8,128)(2,1)}, bf16[2,256,512]{2,1,0:T(8,128)(2,1)}, u32[]{:S(2)}, u32[]{:S(2)}) collective-permute-start(bf16[2,256,512]{2,1,0:T(8,128)(2,1)} %get-tuple-element.144.rest_6_), channel_id=1, source_target_pairs={{0,16},{16,0},{1,17},{17,1},{2,18},{18,2},{3,19},{19,3},{4,20},{20... | collective-permute-start | bytes 1572872 | tf_op jit(solution)/shard_map/ppermute | solution.py:24
  84.8 18.3 %collective-permute-start.16 = (bf16[512,256]{1,0:T(8,128)(2,1)}, bf16[512,256]{1,0:T(8,128)(2,1)}, u32[]{:S(2)}, u32[]{:S(2)}) collective-permute-start(bf16[512,256]{1,0:T(8,128)(2,1)} %get-tuple-element.152), channel_id=1, source_target_pairs={{0,16},{16,0},{1,17},{17,1},{2,18},{18,2},{3,19},{19,3},{4,20},{20... | collective-permute-start | bytes 786440 | tf_op jit(solution)/shard_map/ppermute | solution.py:24
  85.3 17.8 %collective-permute-start.17 = (bf16[512,256]{1,0:T(8,128)(2,1)}, bf16[512,256]{1,0:T(8,128)(2,1)}, u32[]{:S(2)}, u32[]{:S(2)}) collective-permute-start(bf16[512,256]{1,0:T(8,128)(2,1)} %get-tuple-element.153), channel_id=1, source_target_pairs={{0,8},{8,0},{1,9},{9,1},{2,10},{10,2},{3,11},{11,3},{4,12},{12,4},... | collective-permute-start | bytes 786440 | tf_op jit(solution)/shard_map/ppermute | solution.py:24
  103.1 8.9 %collective-permute-start.18 = (bf16[4,1024,512]{2,1,0:T(8,128)(2,1)}, bf16[4,1024,512]{2,1,0:T(8,128)(2,1)}, u32[]{:S(2)}, u32[]{:S(2)}) collective-permute-start(bf16[4,1024,512]{2,1,0:T(8,128)(2,1)} %get-tuple-element.154.weight_ref), channel_id=1, source_target_pairs={{0,4},{4,0},{1,5},{5,1},{2,6},{6,2},{3,7},{7,3},{8,12},{12,8},{9,1... | collective-permute-start | bytes 12582920 | tf_op jit(solution)/shard_map/ppermute | solution.py:24
  103.2 16.5 %collective-permute-start.19 = (bf16[2,512,256]{2,1,0:T(8,128)(2,1)}, bf16[2,512,256]{2,1,0:T(8,128)(2,1)}, u32[]{:S(2)}, u32[]{:S(2)}) collective-permute-start(bf16[2,512,256]{2,1,0:T(8,128)(2,1)} %get-tuple-element.164), channel_id=1, source_target_pairs={{0,8},{8,0},{1,9},{9,1},{2,10},{10,2},{3,11},{11,3},{4,12},{12,4},... | collective-permute-start | bytes 1572872 | tf_op jit(solution)/shard_map/ppermute | solution.py:24
  104.7 15.0 %collective-permute-start.20 = (bf16[2,512,256]{2,1,0:T(8,128)(2,1)}, bf16[2,512,256]{2,1,0:T(8,128)(2,1)}, u32[]{:S(2)}, u32[]{:S(2)}) collective-permute-start(bf16[2,512,256]{2,1,0:T(8,128)(2,1)} %get-tuple-element.165), channel_id=1, source_target_pairs={{0,16},{16,0},{1,17},{17,1},{2,18},{18,2},{3,19},{19,3},{4,20},{20... | collective-permute-start | bytes 1572872 | tf_op jit(solution)/shard_map/ppermute | solution.py:24
  106.4 13.3 %copy-start.6 = (bf16[2,512,256]{2,1,0:T(8,128)(2,1)S(1)}, bf16[2,512,256]{2,1,0:T(8,128)(2,1)}, u32[]{:S(2)}) copy-start(bf16[2,512,256]{2,1,0:T(8,128)(2,1)} %get-tuple-element.168.refs_0_) | copy-start | bytes 1572868
  106.4 13.3 %copy-start.7 = (bf16[2,512,256]{2,1,0:T(8,128)(2,1)S(1)}, bf16[2,512,256]{2,1,0:T(8,128)(2,1)}, u32[]{:S(2)}) copy-start(bf16[2,512,256]{2,1,0:T(8,128)(2,1)} %get-tuple-element.170.refs_2_) | copy-start | bytes 1572868
  107.7 23.0 %collective-permute-start.23 = (bf16[512,256]{1,0:T(8,128)(2,1)S(1)}, bf16[512,256]{1,0:T(8,128)(2,1)S(1)}, u32[]{:S(2)}, u32[]{:S(2)}) collective-permute-start(bf16[512,256]{1,0:T(8,128)(2,1)S(1)} %get-tuple-element.159), channel_id=1, source_target_pairs={{0,3},{1,0},{2,1},{3,2},{4,7},{5,4},{6,5},{7,6},{8,11},{9,8},{10,9... | collective-permute-start | bytes 786440 | tf_op jit(solution)/shard_map/ppermute | solution.py:24
  112.0 18.7 %collective-permute-start.24 = (bf16[512,256]{1,0:T(8,128)(2,1)S(1)}, bf16[512,256]{1,0:T(8,128)(2,1)S(1)}, u32[]{:S(2)}, u32[]{:S(2)}) collective-permute-start(bf16[512,256]{1,0:T(8,128)(2,1)S(1)} %get-tuple-element.158), channel_id=1, source_target_pairs={{0,2},{1,3},{2,0},{3,1},{4,6},{5,7},{6,4},{7,5},{8,10},{9,11},{10,... | collective-permute-start | bytes 786440 | tf_op jit(solution)/shard_map/ppermute | solution.py:24
  120.9 9.8 %collective-permute-start.21 = (bf16[512,256]{1,0:T(8,128)(2,1)S(1)}, bf16[512,256]{1,0:T(8,128)(2,1)S(1)}, u32[]{:S(2)}, u32[]{:S(2)}) collective-permute-start(bf16[512,256]{1,0:T(8,128)(2,1)S(1)} %get-tuple-element.172), channel_id=1, source_target_pairs={{0,16},{16,0},{1,17},{17,1},{2,18},{18,2},{3,19},{19,3},{4,20},{20... | collective-permute-start | bytes 786440 | tf_op jit(solution)/shard_map/ppermute | solution.py:24
  122.4 8.3 %collective-permute-start.22 = (bf16[512,256]{1,0:T(8,128)(2,1)S(1)}, bf16[512,256]{1,0:T(8,128)(2,1)S(1)}, u32[]{:S(2)}, u32[]{:S(2)}) collective-permute-start(bf16[512,256]{1,0:T(8,128)(2,1)S(1)} %get-tuple-element.173), channel_id=1, source_target_pairs={{0,8},{8,0},{1,9},{9,1},{2,10},{10,2},{3,11},{11,3},{4,12},{12,4},... | collective-permute-start | bytes 786440 | tf_op jit(solution)/shard_map/ppermute | solution.py:24
  131.8 10.3 %copy-start.13 = (bf16[256,512]{1,0:T(8,128)(2,1)S(1)}, bf16[256,512]{1,0:T(8,128)(2,1)}, u32[]{:S(2)}) copy-start(bf16[256,512]{1,0:T(8,128)(2,1)} %param.12) | copy-start | bytes 786436
  131.8 9.1 %collective-permute-start.25 = (bf16[512,256]{1,0:T(8,128)(2,1)S(1)}, bf16[512,256]{1,0:T(8,128)(2,1)S(1)}, u32[]{:S(2)}, u32[]{:S(2)}) collective-permute-start(bf16[512,256]{1,0:T(8,128)(2,1)S(1)} %fusion.1), channel_id=1, source_target_pairs={{0,1},{1,2},{2,3},{3,0},{4,5},{5,6},{6,7},{7,4},{8,9},{9,10},{10,1... | collective-permute-start | bytes 786440 | tf_op jit(solution)/shard_map/ppermute | solution.py:24
  (15 other events, 52.5 us)

commit v14 on v11

--- a/solution.py
+++ b/solution.py
@@ -60,7 +60,7 @@
 
 
 def ours_kernel(places_ref, cot_ref, *rest):
-    slots = len(rest) // 3
+    slots = 4
     blocks, other_ref, outs = rest[:slots], rest[slots], rest[slots + 1 :]
     step = pl.program_id(0)
     ways = (lax.rem(step, 2), step // 2)
@@ -71,17 +71,19 @@
         ).astype(BF16)
         for slot, resid_ref in enumerate(blocks)
     ]
-    for which, way in enumerate(ways):
+    for slot, way in enumerate(ways):
+        send_ref, keep_ref = outs[2 * slot : 2 * slot + 2]
 
         @pl.when(way == 1)
         def _():
-            for slot in range(which, slots, 2):
-                outs[2 * slot][0] = totals[slot]
+            send_ref[0] = totals[slot]
 
         @pl.when(way == 0)
         def _():
-            for slot in range(which, slots, 2):
-                outs[2 * slot + 1][0] = totals[slot]
+            keep_ref[0] = totals[slot]
+
+    for slot in (2, 3):
+        outs[slot + 2][0] = totals[slot]
 
 
 def grad_product(residual, cot_t, places, rows, other):
@@ -106,12 +108,14 @@
             lambda i: i // 2,
             lambda i: jnp.maximum(i - 2, 0),
             lambda i: jnp.minimum(i, 1),
+            lambda i: i,
+            lambda i: i,
         ]
         out_specs = [
             pl.BlockSpec((1, features, rows), lambda i, p, index=index: (index(i), 0, 0))
             for index in indices
-        ] * (slots // 2)
-        out_shape = [pltpu.HBM((2, features, rows), BF16)] * (2 * slots)
+        ]
+        out_shape = [pltpu.HBM((n, features, rows), BF16) for n in (2, 2, 2, 2, steps, steps)]
     return pl.pallas_call(
         kernel,
         out_shape=out_shape,
@@ -374,7 +378,7 @@
     rows = depth // tp_count
     order = list(range(tp_count))
     shifts = chunk_shifts(tp_count)
-    in_place = rows % 128 == 0 and outer == 2 and inner == 2
+    in_place = rows % 128 == 0 and outer == 2 and inner == 2 and tp_count == 4
 
     owned = jnp.where(
         target_ids // (VOCAB // tp_count) == tp_place,
@@ -448,7 +452,7 @@
         places = places_of(backward, core)
         if in_place:
             outs = grad_product(residual, cot_t, places, rows, other)
-            sides = [([outs[2 * n]], outs[2 * n + 1]) for n in range(tp_count)]
+            return [[([outs[0]], outs[1]), ([outs[2]], outs[3])], outs[4], outs[5]]
         else:
             both = product[places].reshape(len(chips), tp_count, features, rows).swapaxes(0, 1)
             total = widen([both, other]).astype(BF16)
@@ -465,19 +469,16 @@
             for axis, (sends, _) in zip(("inner", "outer"), sides)
         ]
 
-    def second_round(sides, got, following=()):
+    def second_round(sides, got):
         axes = ("outer", "inner")
         groups = [[keep] + parts for (_, keep), parts in zip(sides, got)]
-        if in_place:
-            sent, following = lax.optimization_barrier((sums_of(groups, 1), following))
-            return [[swap(x, axis, 1)] for x, axis in zip(sent, axes)], following
         return [
             [
                 swap(widen([part[s] for part in parts]).astype(BF16), axis, s)
                 for s in range(1, lax.axis_size(axis))
             ]
             for parts, axis in zip(groups, axes)
-        ], following
+        ]
 
     def summed(sides, got, later):
         return [
@@ -494,6 +495,10 @@
     for k in order[2:]:
         own_pieces[k] = far_of(k, arrived[k], near[k])
     sides = for_us(other)
+    if in_place:
+        sides, passed, kept = sides[:1], sides[1], sides[2]
+        kept, own_pieces = lax.optimization_barrier((kept, own_pieces))
+        passed = swap(passed, "tp", 1)
     got = [first_round(sides[0])]
     sides[1:], own_pieces = lax.optimization_barrier((sides[1:], own_pieces))
 
@@ -522,8 +527,7 @@
         (got[0], sides[1:], total, own_weight)
     )
     other_weight = swap(own_weight, "core", 1)
-    first_later, sides[1:] = second_round(sides[0], got[0], sides[1:])
-    later = [first_later]
+    later = [second_round(sides[0], got[0])]
     got += [first_round(side) for side in sides[1:]]
     if in_place:
         value_proj, coefficient = weight_call(
@@ -546,36 +550,35 @@
         coefficient = inv_rms * inv_rms * share * (1.0 / width)
     later[0], coefficient = lax.optimization_barrier((later[0], coefficient))
     if in_place:
+        passed, coefficient = lax.optimization_barrier((passed, coefficient))
+        crossed = swap(widen([kept[2:], passed[2:]]).astype(BF16), "outer", 1)
         groups = [[keep] + parts + then for (_, keep), parts, then in zip(sides[0], got[0], later[0])]
-        sums = dict(zip(pairs[0], sums_of(groups, 0)))
-    else:
-        sums = dict(zip(pairs[0], summed(sides[0], got[0], later[0])))
-    last = [swap(sums[k].astype(BF16), "tp", k) for k in pairs[0]]
-    if in_place:
+        last = [swap(x, "tp", k) for x, k in zip(sums_of(groups, 0), pairs[0])]
         grad_shape = jax.ShapeDtypeStruct((rows_here, width), BF16)
         resid_grad = weight_call(
             grad_kernel, places[0], residual, in_hbm(own_weight), [cot, coefficient], grad_shape
         )
-        got[1:], resid_grad = lax.optimization_barrier((got[1:], resid_grad))
+        crossed, resid_grad = lax.optimization_barrier((crossed, resid_grad))
+        beside = swap(widen([kept[1], passed[1], crossed[1]]).astype(BF16), "inner", 1)
+        resid_grad = weight_call(
+            grad_kernel, places[1][:3], residual, other_weight, [cot, coefficient], grad_shape, resid_grad
+        )
+        beside, last, resid_grad = lax.optimization_barrier((beside, last, resid_grad))
+        resid_grad = weight_call(
+            grad_kernel, places[1][3:], residual, other_weight, [cot, coefficient], grad_shape, resid_grad
+        )
+        grad_rows = widen([kept[0], passed[0], crossed[0], beside] + last)
     else:
         normed_grad = lax.dot_general(
             cot, weight, (((1,), (1,)), ((), ())), preferred_element_type=F32
         )
         resid_grad = (normed_grad - residual.astype(F32) * coefficient).astype(BF16)
-    later += [second_round(side, parts)[0] for side, parts in zip(sides[1:], got[1:])]
-    if in_place:
-        resid_grad = weight_call(
-            grad_kernel, places[1][:2], residual, other_weight, [cot, coefficient], grad_shape, resid_grad
-        )
-        later[1], last, resid_grad = lax.optimization_barrier((later[1], last, resid_grad))
-    for pair, *rounds in zip(pairs[1:], sides[1:], got[1:], later[1:]):
-        sums.update(zip(pair, summed(*rounds)))
-    last += [swap(sums[k].astype(BF16), "tp", k) for k in backward[2:-1]]
-    if in_place:
-        resid_grad = weight_call(
-            grad_kernel, places[1][2:], residual, other_weight, [cot, coefficient], grad_shape, resid_grad
-        )
-    grad_rows = widen([sums[0]] + last)
+        later += [second_round(side, parts) for side, parts in zip(sides[1:], got[1:])]
+        sums = {}
+        for pair, *rounds in zip(pairs, sides, got, later):
+            sums.update(zip(pair, summed(*rounds)))
+        last = [swap(sums[k].astype(BF16), "tp", k) for k in backward[:-1]]
+        grad_rows = widen([sums[0]] + last)
     late_gain, late_weight, grad_rows = lax.optimization_barrier((norm_gain, value_weight, grad_rows))
     weight_grad = (late_gain.astype(F32)[None, :] * grad_rows).T
     gain_grad = jnp.sum(late_weight.astype(F32).T * grad_rows, axis=0)

time: 137 us -> 138 us (level)
  other arithmetic: 14.2 us -> 19.5 us
  starting transfers between devices: 30.2 us -> 27.6 us
  Pallas kernels: 52.7 us -> 51.2 us
    convert_element_type x1 -> x4, other arithmetic: 0.11 us -> 4.5 us  [the longest x2 2.12 us: second_round(): widen([part[s] for part in parts]).astype(BF16)]
    ppermute x24 -> x22, starting transfers between devices: 24.5 us -> 21.9 us  [swap(): lax.ppermute(value, axis, [(place, (place + step) % size) for place in ra...]
    pallas_call x3 -> x1, Pallas kernels: 3.25 us -> 1.22 us  [sums_of(): pl.pallas_call(functools.partial(sum_kernel, [len(parts) for parts in gro...]
    ppermute x24 -> x22, waiting for transfers between devices: 32.2 us -> 32.4 us  [swap(): lax.ppermute(value, axis, [(place, (place + step) % size) for place in ra...]
  transfers between devices with their start and end apart: 26 -> 24, of which waited for: 12 -> 11; matrix products, arithmetic and copies ran while one was open for 10% -> 12% of each run, Pallas kernels for 39% -> 35%
where the time goes in v14:
time: 138 us; the launch traced here: 137 us
  Pallas kernels  51.2 us (37%)
  waiting for transfers between devices  32.5 us (24%)
  starting transfers between devices  27.6 us (20%)
  other arithmetic  19.5 us (14%)
  local copies, waits for them, and re-layouts  5.69 us (4%)
    ppermute x22, waiting for transfers between devices, swap(): lax.ppermute(value, axis, [(place, (place + step) % size) for place in ra...  32.4 us
    pallas_call x4, Pallas kernels, weight_call(): pl.pallas_call(kernel, out_shape=out_shape, grid_spec=pltpu.PrefetchScala...  25.5 us
    ppermute x22, starting transfers between devices, swap(): lax.ppermute(value, axis, [(place, (place + step) % size) for place in ra...  21.9 us
    pallas_call x2, Pallas kernels, grad_product(): pl.pallas_call(kernel, out_shape=out_shape, grid_spec=pltpu.PrefetchScala...  14.7 us
    pallas_call x1, Pallas kernels, first_value(): pl.pallas_call(functools.partial(value_kernel, inner_flags), out_shape=[t...  7.77 us
    ppermute x2, starting transfers between devices, trade(): lax.ppermute(value, axis, [(place, place ^ mask) for place in range(size)])  5.67 us
    reduce_sum x1, other arithmetic, per_device(): squares = jnp.sum(resid_wide * resid_wide, axis=1, keepdims=True)  5.1 us
    unnamed x27, local copies, waits for them, and re-layouts  3.99 us
  transfers between devices with their start and end apart: 24, of which 11 were waited for; matrix products, arithmetic and copies ran while one was open for 12% of the time, Pallas kernels for 35%

profile of v14, /device:TPU:0, one launch (start us, length us, event | category | flops | bytes accessed | tf_op | source)
XLA Modules:
  0.0 137.2 jit_solution(2023573155468769487)
XLA Ops:
  2.1 3.0 %collective-permute-start = (f32[1,52,128]{2,1,0:T(8,128)S(1)}, f32[1,52,128]{2,1,0:T(8,128)S(1)}, u32[]{:S(2)}, u32[]{:S(2)}) collective-permute-start(f32[1,52,128]{2,1,0:T(8,128)S(1)} %maximum_bitcast_fusion), channel_id=1, source_target_pairs={{0,1},{1,0},{2,3},{3,2},{4,5},{5,4},{6,7},{7,6},{8,9},{9,8},{10,11... | collective-permute-start | bytes 79880 | tf_op jit(solution)/shard_map/ppermute | solution.py:29
  5.8 1.8 %multiply_convert_fusion = bf16[256,512]{1,0:T(8,128)(2,1)} fusion(bf16[256,512]{1,0:T(8,128)(2,1)} %param.12, f32[256]{0:T(256)S(1)} %convert_element_type.93), kind=kLoop, calls=%fused_computation.15 | loop fusion | flops 393216 | bytes 525312 | tf_op jit(solution)/shard_map/convert_element_type | solution.py:392
  7.5 1.2 dynamic_slice.4
  8.8 1.6 %collective-permute-start.2 = (bf16[256,512]{1,0:T(8,128)(2,1)}, bf16[256,512]{1,0:T(8,128)(2,1)S(1)}, u32[]{:S(2)}, u32[]{:S(2)}) collective-permute-start(bf16[256,512]{1,0:T(8,128)(2,1)} %multiply_convert_fusion), channel_id=1, source_target_pairs={{0,8},{8,0},{1,9},{9,1},{2,10},{10,2},{3,11},{11,3},{4,12},{12,4},... | collective-permute-start | bytes 786440 | tf_op jit(solution)/shard_map/ppermute | solution.py:24
  10.8 5.1 %multiply_reduce_fusion = f32[512]{0:T(512)S(1)} fusion(bf16[512,8192]{1,0:T(8,128)(2,1)} %resid_ref.4), kind=kLoop, calls=%fused_computation | loop fusion | flops 12582400 | bytes 8390656 | tf_op jit(solution)/shard_map/reduce_sum | solution.py:395
  15.9 2.6 %collective-permute-start.5 = (f32[2,52,128]{2,1,0:T(8,128)S(1)}, f32[2,52,128]{2,1,0:T(8,128)S(1)}, u32[]{:S(2)}, u32[]{:S(2)}) collective-permute-start(f32[2,52,128]{2,1,0:T(8,128)S(1)} %pad_maximum_fusion.5), channel_id=1, source_target_pairs={{0,2},{1,3},{2,0},{3,1},{4,6},{5,7},{6,4},{7,5},{8,10},{9,11},{10,... | collective-permute-start | bytes 159752 | tf_op jit(solution)/shard_map/ppermute | solution.py:29
  18.6 1.4 %collective-permute-done.1 = bf16[256,512]{1,0:T(8,128)(2,1)S(1)} collective-permute-done((bf16[256,512]{1,0:T(8,128)(2,1)}, bf16[256,512]{1,0:T(8,128)(2,1)S(1)}, u32[]{:S(2)}, u32[]{:S(2)}) %collective-permute-start.1) | collective-permute-done | bytes 262176 | tf_op jit(solution)/shard_map/ppermute | solution.py:24
  21.0 1.5 %collective-permute-start.3 = (bf16[256,512]{1,0:T(8,128)(2,1)S(1)}, bf16[256,512]{1,0:T(8,128)(2,1)S(1)}, u32[]{:S(2)}, u32[]{:S(2)}) collective-permute-start(bf16[256,512]{1,0:T(8,128)(2,1)S(1)} %collective-permute-done.1), channel_id=1, source_target_pairs={{0,16},{16,0},{1,17},{17,1},{2,18},{18,2},{3,19},{19,3},{4,20},{20... | collective-permute-start | bytes 786440 | tf_op jit(solution)/shard_map/ppermute | solution.py:24
  24.9 2.2 %collective-permute-done.4 = bf16[256,512]{1,0:T(8,128)(2,1)} collective-permute-done((bf16[256,512]{1,0:T(8,128)(2,1)}, bf16[256,512]{1,0:T(8,128)(2,1)}, u32[]{:S(2)}, u32[]{:S(2)}) %collective-permute-start.4) | collective-permute-done | bytes 262176 | tf_op jit(solution)/shard_map/ppermute | solution.py:24
  27.1 3.1 %collective-permute-done.3 = bf16[256,512]{1,0:T(8,128)(2,1)S(1)} collective-permute-done((bf16[256,512]{1,0:T(8,128)(2,1)S(1)}, bf16[256,512]{1,0:T(8,128)(2,1)S(1)}, u32[]{:S(2)}, u32[]{:S(2)}) %collective-permute-start.3) | collective-permute-done | bytes 262176 | tf_op jit(solution)/shard_map/ppermute | solution.py:24
  31.5 1.6 %collective-permute-start.9 = (bf16[256,512]{1,0:T(8,128)(2,1)}, bf16[256,512]{1,0:T(8,128)(2,1)}, u32[]{:S(2)}, u32[]{:S(2)}) collective-permute-start(bf16[256,512]{1,0:T(8,128)(2,1)} %collective-permute-done.4), channel_id=1, source_target_pairs={{0,16},{16,0},{1,17},{17,1},{2,18},{18,2},{3,19},{19,3},{4,20},{20... | collective-permute-start | bytes 786440 | tf_op jit(solution)/shard_map/ppermute | solution.py:24
  33.1 2.1 %shard_map.129 = (bf16[512,512]{1,0:T(8,128)(2,1)S(1)}, bf16[512,512]{1,0:T(8,128)(2,1)S(1)}, f32[512,1]{1,0:T(8,128)S(1)}) custom-call(s32[2]{0:T(128)S(1)} %pad_add_fusion.1.info_ref, f32[4,52,128]{2,1,0:T(8,128)S(1)} %pad_maximum_fusion.4.shares_ref, f32[512,1]{1,0:T(8,128)S(1)} %copy.18.squares_ref, bf16[512,512]{1,0:T(8,128)(2,1)} %value_cot_ref.1), custom_call_target="tpu_custom_call" | custom-call | flops 1024 | bytes 1024 | tf_op jit(solution)/shard_map/pallas_call | solution.py:341
  35.2 6.6 %shard_map.130 = bf16[4,4,512,256]{3,2,1,0:T(8,128)(2,1)} custom-call(s32[16]{0:T(128)S(1)} %stack.232.places_ref, bf16[512,512]{1,0:T(8,128)(2,1)S(1)} %get-tuple-element.90.cot_ref, bf16[512,8192]{1,0:T(8,128)(2,1)} %resid_ref.4, bf16[512,8192]{1,0:T(8,128)(2,1)} %resid_ref.4, bf16[512,8192]{1,0:T(8,128)(2,1)} %resid_ref.4, bf16[512,8192]{1,0:T(8,128)(2,1)} %resid_ref.4), custom_call_target="tpu_custom_call" | custom-call | flops 1024 | bytes 1024 | tf_op jit(solution)/shard_map/pallas_call | solution.py:119
  41.8 1.6 %collective-permute-start.10 = (bf16[256,512]{1,0:T(8,128)(2,1)}, bf16[256,512]{1,0:T(8,128)(2,1)}, u32[]{:S(2)}, u32[]{:S(2)}) collective-permute-start(bf16[256,512]{1,0:T(8,128)(2,1)} %collective-permute-done.6), channel_id=1, source_target_pairs={{0,8},{8,0},{1,9},{9,1},{2,10},{10,2},{3,11},{11,3},{4,12},{12,4},... | collective-permute-start | bytes 786440 | tf_op jit(solution)/shard_map/ppermute | solution.py:24
  44.6 3.9 %collective-permute-done.10 = bf16[256,512]{1,0:T(8,128)(2,1)} collective-permute-done((bf16[256,512]{1,0:T(8,128)(2,1)}, bf16[256,512]{1,0:T(8,128)(2,1)}, u32[]{:S(2)}, u32[]{:S(2)}) %collective-permute-start.10) | collective-permute-done | bytes 262176 | tf_op jit(solution)/shard_map/ppermute | solution.py:24
  51.3 1.6 %collective-permute-start.14 = (bf16[2,256,512]{2,1,0:T(8,128)(2,1)S(1)}, bf16[2,256,512]{2,1,0:T(8,128)(2,1)}, u32[]{:S(2)}, u32[]{:S(2)}) collective-permute-start(bf16[2,256,512]{2,1,0:T(8,128)(2,1)S(1)} %pad_maximum_fusion.2.rest_4_), channel_id=1, source_target_pairs={{0,8},{8,0},{1,9},{9,1},{2,10},{10,2},{3,11},{11,3},{4,12},{12,4},... | collective-permute-start | bytes 1572872 | tf_op jit(solution)/shard_map/ppermute | solution.py:24
  52.9 3.1 %collective-permute-done.11.rest_4_ = bf16[4,4,512,256]{3,2,1,0:T(8,128)(2,1)} collective-permute-done((bf16[4,4,512,256]{3,2,1,0:T(8,128)(2,1)}, bf16[4,4,512,256]{3,2,1,0:T(8,128)(2,1)}, u32[]{:S(2)}, u32[]{:S(2)}) %collective-permute-start.11) | collective-permute-done | bytes 4194336 | tf_op jit(solution)/shard_map/ppermute | solution.py:24
  56.1 8.0 %shard_map.131 = (bf16[2,512,256]{2,1,0:T(8,128)(2,1)}, bf16[2,512,256]{2,1,0:T(8,128)(2,1)}, bf16[2,512,256]{2,1,0:T(8,128)(2,1)}, bf16[2,512,256]{2,1,0:T(8,12...) custom-call(s32[16]{0:T(128)S(1)} %stack.213.places_ref, ...), custom_call_target="tpu_custom_call" | custom-call | flops 1024 | bytes 1024 | tf_op jit(solution)/shard_map/pallas_call | solution.py:119
  64.1 1.6 %collective-permute-start.12 = (bf16[2,512,256]{2,1,0:T(8,128)(2,1)}, bf16[2,512,256]{2,1,0:T(8,128)(2,1)}, u32[]{:S(2)}, u32[]{:S(2)}) collective-permute-start(bf16[2,512,256]{2,1,0:T(8,128)(2,1)} %get-tuple-element.98), channel_id=1, source_target_pairs={{0,8},{8,0},{1,9},{9,1},{2,10},{10,2},{3,11},{11,3},{4,12},{12,4},... | collective-permute-start | bytes 1572872 | tf_op jit(solution)/shard_map/ppermute | solution.py:24
  68.4 7.8 %shard_map.132 = (f32[512,512]{1,0:T(8,128)}, bf16[4,1024,512]{2,1,0:T(8,128)(2,1)}) custom-call(s32[4]{0:T(128)S(1)} %get-tuple-element.170.places_ref, s32[4]{0:T(128)S(1)} %get-tuple-element.171.offsets_ref, bf16[512,8192]{1,0:T(8,128)(2,1)} %resid_ref.4, bf16[2,256,512]{2,1,0:T(8,128)(2,1)S(1)} %pad_maximum_fusion.rest_0_, ...), custom_call_target="tpu_custom_call" | custom-call | flops 1024 | bytes 1024 | tf_op jit(solution)/shard_map/pallas_call | solution.py:241
  76.2 2.3 %collective-permute-done.12.refs_1_ = bf16[2,512,256]{2,1,0:T(8,128)(2,1)} collective-permute-done((bf16[2,512,256]{2,1,0:T(8,128)(2,1)}, bf16[2,512,256]{2,1,0:T(8,128)(2,1)}, u32[]{:S(2)}, u32[]{:S(2)}) %collective-permute-start.12) | collective-permute-done | bytes 524320 | tf_op jit(solution)/shard_map/ppermute | solution.py:24
  78.5 1.2 collective-permute-done.13.refs_4_
  79.7 2.2 %collective-permute-start.17 = (bf16[4,512,256]{2,1,0:T(8,128)(2,1)}, bf16[4,512,256]{2,1,0:T(8,128)(2,1)}, u32[]{:S(2)}, u32[]{:S(2)}) collective-permute-start(bf16[4,512,256]{2,1,0:T(8,128)(2,1)} %get-tuple-element.137), channel_id=1, source_target_pairs={{0,1},{1,2},{2,3},{3,0},{4,5},{5,6},{6,7},{7,4},{8,9},{9,10},{10,1... | collective-permute-start | bytes 3145736 | tf_op jit(solution)/shard_map/ppermute | solution.py:24
  84.6 1.6 %collective-permute-start.18 = (bf16[512,256]{1,0:T(8,128)(2,1)S(1)}, bf16[512,256]{1,0:T(8,128)(2,1)S(1)}, u32[]{:S(2)}, u32[]{:S(2)}) collective-permute-start(bf16[512,256]{1,0:T(8,128)(2,1)S(1)} %fusion.3), channel_id=1, source_target_pairs={{0,16},{16,0},{1,17},{17,1},{2,18},{18,2},{3,19},{19,3},{4,20},{20... | collective-permute-start | bytes 786440 | tf_op jit(solution)/shard_map/ppermute | solution.py:24
  87.2 7.7 %shard_map.133 = (bf16[512,512]{1,0:T(8,128)(2,1)}, f32[512,1]{1,0:T(8,128)S(1)}) custom-call(s32[4]{0:T(128)S(1)} %pad_add_fusion.places_ref, bf16[512,8192]{1,0:T(8,128)(2,1)} %resid_ref.4, bf16[4,1024,512]{2,1,0:T(8,128)(2,1)} %collective-permute-done.16.weight_ref, f32[512,512]{1,0:T(8,128)} %get-tuple-element.133.first_ref, ...), custom_call_target="tpu_custom_call" | custom-call | flops 1024 | bytes 1024 | tf_op jit(solution)/shard_map/pallas_call | solution.py:279
  94.9 12.5 %collective-permute-done.17 = bf16[4,512,256]{2,1,0:T(8,128)(2,1)} collective-permute-done((bf16[4,512,256]{2,1,0:T(8,128)(2,1)}, bf16[4,512,256]{2,1,0:T(8,128)(2,1)}, u32[]{:S(2)}, u32[]{:S(2)}) %collective-permute-start.17) | collective-permute-done | bytes 1048608 | tf_op jit(solution)/shard_map/ppermute | solution.py:24
  107.4 1.3 add_convert_fusion
  109.3 1.2 shard_map.135
  111.6 1.8 %collective-permute-start.23 = (bf16[512,256]{1,0:T(8,128)(2,1)S(1)}, bf16[512,256]{1,0:T(8,128)(2,1)S(1)}, u32[]{:S(2)}, u32[]{:S(2)}) collective-permute-start(bf16[512,256]{1,0:T(8,128)(2,1)S(1)} %get-tuple-element.151), channel_id=1, source_target_pairs={{0,2},{1,3},{2,0},{3,1},{4,6},{5,7},{6,4},{7,5},{8,10},{9,11},{10,... | collective-permute-start | bytes 786440 | tf_op jit(solution)/shard_map/ppermute | solution.py:24
  113.4 7.7 %shard_map.134.rest_0_ = bf16[512,8192]{1,0:T(8,128)(2,1)} custom-call(s32[4]{0:T(128)S(1)} %get-tuple-element.170.places_ref, bf16[512,8192]{1,0:T(8,128)(2,1)} %resid_ref.4, bf16[4,1024,512]{2,1,0:T(8,128)(2,1)} %get-tuple-element.132.weight_ref, bf16[512,512]{1,0:T(8,128)(2,1)S(1)} %get-tuple-element.134.cot_ref, f32[512,1]{1,0:T(8,128)S(1)} %get-tuple-element.144.coef_ref), custom_call_target="tpu_custom_call" | custom-call | flops 1024 | bytes 1024 | tf_op jit(solution)/shard_map/pallas_call | solution.py:279
  124.1 6.9 %shard_map.136.rest_0_ = bf16[512,8192]{1,0:T(8,128)(2,1)} custom-call(s32[3]{0:T(128)S(1)} %pad_add_fusion.4.places_ref, bf16[512,8192]{1,0:T(8,128)(2,1)} %resid_ref.4, bf16[4,1024,512]{2,1,0:T(8,128)(2,1)} %collective-permute-done.16.weight_ref, bf16[512,512]{1,0:T(8,128)(2,1)S(1)} %get-tuple-element.134.cot_ref, ...), custom_call_target="tpu_custom_call", output_to_operand_aliasing={{}: (5, {})} | custom-call | flops 1024 | bytes 1024 | tf_op jit(solution)/shard_map/pallas_call | solution.py:279
  134.0 3.3 %shard_map.137 = bf16[512,8192]{1,0:T(8,128)(2,1)} custom-call(s32[1]{0:T(128)} %bitcast.3.places_ref, bf16[512,8192]{1,0:T(8,128)(2,1)} %resid_ref.4, bf16[4,1024,512]{2,1,0:T(8,128)(2,1)} %collective-permute-done.16.weight_ref, bf16[512,512]{1,0:T(8,128)(2,1)S(1)} %get-tuple-element.134.cot_ref, ...), custom_call_target="tpu_custom_call", output_to_operand_aliasing={{}: (5, {})} | custom-call | flops 1024 | bytes 1024 | tf_op jit(solution)/shard_map/pallas_call | solution.py:279
  (79 shorter events, 25.3 us)
Async XLA Ops:
  2.1 6.7 %collective-permute-start = (f32[1,52,128]{2,1,0:T(8,128)S(1)}, f32[1,52,128]{2,1,0:T(8,128)S(1)}, u32[]{:S(2)}, u32[]{:S(2)}) collective-permute-start(f32[1,52,128]{2,1,0:T(8,128)S(1)} %maximum_bitcast_fusion), channel_id=1, source_target_pairs={{0,1},{1,0},{2,3},{3,2},{4,5},{5,4},{6,7},{7,6},{8,9},{9,8},{10,11... | collective-permute-start | bytes 79880 | tf_op jit(solution)/shard_map/ppermute | solution.py:29
  8.8 9.8 %collective-permute-start.2 = (bf16[256,512]{1,0:T(8,128)(2,1)}, bf16[256,512]{1,0:T(8,128)(2,1)S(1)}, u32[]{:S(2)}, u32[]{:S(2)}) collective-permute-start(bf16[256,512]{1,0:T(8,128)(2,1)} %multiply_convert_fusion), channel_id=1, source_target_pairs={{0,8},{8,0},{1,9},{9,1},{2,10},{10,2},{3,11},{11,3},{4,12},{12,4},... | collective-permute-start | bytes 786440 | tf_op jit(solution)/shard_map/ppermute | solution.py:24
  10.4 9.6 %collective-permute-start.1 = (bf16[256,512]{1,0:T(8,128)(2,1)}, bf16[256,512]{1,0:T(8,128)(2,1)S(1)}, u32[]{:S(2)}, u32[]{:S(2)}) collective-permute-start(bf16[256,512]{1,0:T(8,128)(2,1)} %multiply_convert_fusion), channel_id=1, source_target_pairs={{0,1},{1,2},{2,3},{3,0},{4,5},{5,6},{6,7},{7,4},{8,9},{9,10},{10,1... | collective-permute-start | bytes 786440 | tf_op jit(solution)/shard_map/ppermute | solution.py:24
  15.9 7.4 %collective-permute-start.5 = (f32[2,52,128]{2,1,0:T(8,128)S(1)}, f32[2,52,128]{2,1,0:T(8,128)S(1)}, u32[]{:S(2)}, u32[]{:S(2)}) collective-permute-start(f32[2,52,128]{2,1,0:T(8,128)S(1)} %pad_maximum_fusion.5), channel_id=1, source_target_pairs={{0,2},{1,3},{2,0},{3,1},{4,6},{5,7},{6,4},{7,5},{8,10},{9,11},{10,... | collective-permute-start | bytes 159752 | tf_op jit(solution)/shard_map/ppermute | solution.py:29
  19.9 7.2 %collective-permute-start.4 = (bf16[256,512]{1,0:T(8,128)(2,1)}, bf16[256,512]{1,0:T(8,128)(2,1)}, u32[]{:S(2)}, u32[]{:S(2)}) collective-permute-start(bf16[256,512]{1,0:T(8,128)(2,1)} %multiply_convert_fusion), channel_id=1, source_target_pairs={{0,3},{1,0},{2,1},{3,2},{4,7},{5,4},{6,5},{7,6},{8,11},{9,8},{10,9... | collective-permute-start | bytes 786440 | tf_op jit(solution)/shard_map/ppermute | solution.py:24
  21.0 9.2 %collective-permute-start.3 = (bf16[256,512]{1,0:T(8,128)(2,1)S(1)}, bf16[256,512]{1,0:T(8,128)(2,1)S(1)}, u32[]{:S(2)}, u32[]{:S(2)}) collective-permute-start(bf16[256,512]{1,0:T(8,128)(2,1)S(1)} %collective-permute-done.1), channel_id=1, source_target_pairs={{0,16},{16,0},{1,17},{17,1},{2,18},{18,2},{3,19},{19,3},{4,20},{20... | collective-permute-start | bytes 786440 | tf_op jit(solution)/shard_map/ppermute | solution.py:24
  24.3 19.1 %collective-permute-start.7 = (bf16[2,256,512]{2,1,0:T(8,128)(2,1)S(1)}, bf16[2,256,512]{2,1,0:T(8,128)(2,1)S(1)}, u32[]{:S(2)}, u32[]{:S(2)}) collective-permute-start(bf16[2,256,512]{2,1,0:T(8,128)(2,1)S(1)} %pad_maximum_fusion.rest_0_), channel_id=1, source_target_pairs={{0,16},{16,0},{1,17},{17,1},{2,18},{18,2},{3,19},{19,3},{4,20},{20... | collective-permute-start | bytes 1572872 | tf_op jit(solution)/shard_map/ppermute | solution.py:24
  30.2 11.6 %collective-permute-start.6 = (bf16[256,512]{1,0:T(8,128)(2,1)}, bf16[256,512]{1,0:T(8,128)(2,1)}, u32[]{:S(2)}, u32[]{:S(2)}) collective-permute-start(bf16[256,512]{1,0:T(8,128)(2,1)} %multiply_convert_fusion), channel_id=1, source_target_pairs={{0,2},{1,3},{2,0},{3,1},{4,6},{5,7},{6,4},{7,5},{8,10},{9,11},{10,... | collective-permute-start | bytes 786440 | tf_op jit(solution)/shard_map/ppermute | solution.py:24
  30.6 14.0 %collective-permute-start.8 = (bf16[2,256,512]{2,1,0:T(8,128)(2,1)S(1)}, bf16[2,256,512]{2,1,0:T(8,128)(2,1)S(1)}, u32[]{:S(2)}, u32[]{:S(2)}) collective-permute-start(bf16[2,256,512]{2,1,0:T(8,128)(2,1)S(1)} %pad_maximum_fusion.1.rest_2_), channel_id=1, source_target_pairs={{0,8},{8,0},{1,9},{9,1},{2,10},{10,2},{3,11},{11,3},{4,12},{12,4},... | collective-permute-start | bytes 1572872 | tf_op jit(solution)/shard_map/ppermute | solution.py:24
  31.5 13.2 %collective-permute-start.9 = (bf16[256,512]{1,0:T(8,128)(2,1)}, bf16[256,512]{1,0:T(8,128)(2,1)}, u32[]{:S(2)}, u32[]{:S(2)}) collective-permute-start(bf16[256,512]{1,0:T(8,128)(2,1)} %collective-permute-done.4), channel_id=1, source_target_pairs={{0,16},{16,0},{1,17},{17,1},{2,18},{18,2},{3,19},{19,3},{4,20},{20... | collective-permute-start | bytes 786440 | tf_op jit(solution)/shard_map/ppermute | solution.py:24
  41.8 6.8 %collective-permute-start.10 = (bf16[256,512]{1,0:T(8,128)(2,1)}, bf16[256,512]{1,0:T(8,128)(2,1)}, u32[]{:S(2)}, u32[]{:S(2)}) collective-permute-start(bf16[256,512]{1,0:T(8,128)(2,1)} %collective-permute-done.6), channel_id=1, source_target_pairs={{0,8},{8,0},{1,9},{9,1},{2,10},{10,2},{3,11},{11,3},{4,12},{12,4},... | collective-permute-start | bytes 786440 | tf_op jit(solution)/shard_map/ppermute | solution.py:24
  48.6 7.5 %collective-permute-start.11 = (bf16[4,4,512,256]{3,2,1,0:T(8,128)(2,1)}, bf16[4,4,512,256]{3,2,1,0:T(8,128)(2,1)}, u32[]{:S(2)}, u32[]{:S(2)}) collective-permute-start(bf16[4,4,512,256]{3,2,1,0:T(8,128)(2,1)} %shard_map.130), channel_id=1, source_target_pairs={{0,4},{4,0},{1,5},{5,1},{2,6},{6,2},{3,7},{7,3},{8,12},{12,8},{9,1... | collective-permute-start | bytes 12582920 | tf_op jit(solution)/shard_map/ppermute | solution.py:24
  49.7 16.6 %collective-permute-start.15 = (bf16[2,256,512]{2,1,0:T(8,128)(2,1)S(1)}, bf16[2,256,512]{2,1,0:T(8,128)(2,1)}, u32[]{:S(2)}, u32[]{:S(2)}) collective-permute-start(bf16[2,256,512]{2,1,0:T(8,128)(2,1)S(1)} %pad_maximum_fusion.3.rest_6_), channel_id=1, source_target_pairs={{0,16},{16,0},{1,17},{17,1},{2,18},{18,2},{3,19},{19,3},{4,20},{20... | collective-permute-start | bytes 1572872 | tf_op jit(solution)/shard_map/ppermute | solution.py:24
  51.3 15.0 %collective-permute-start.14 = (bf16[2,256,512]{2,1,0:T(8,128)(2,1)S(1)}, bf16[2,256,512]{2,1,0:T(8,128)(2,1)}, u32[]{:S(2)}, u32[]{:S(2)}) collective-permute-start(bf16[2,256,512]{2,1,0:T(8,128)(2,1)S(1)} %pad_maximum_fusion.2.rest_4_), channel_id=1, source_target_pairs={{0,8},{8,0},{1,9},{9,1},{2,10},{10,2},{3,11},{11,3},{4,12},{12,4},... | collective-permute-start | bytes 1572872 | tf_op jit(solution)/shard_map/ppermute | solution.py:24
  56.1 31.1 %copy-start.9 = (f32[512,1]{1,0:T(8,128)S(1)}, f32[512,1]{1,0:T(8,128)}, u32[]{:S(2)}) copy-start(f32[512,1]{1,0:T(8,128)} %copy-done.8) | copy-start | bytes 6148
  64.1 19.4 %copy-start = (bf16[2,512,256]{2,1,0:T(8,128)(2,1)S(1)}, bf16[2,512,256]{2,1,0:T(8,128)(2,1)}, u32[]{:S(2)}) copy-start(bf16[2,512,256]{2,1,0:T(8,128)(2,1)} %get-tuple-element.138.refs_0_) | copy-start | bytes 1572868
  64.1 14.3 %collective-permute-start.12 = (bf16[2,512,256]{2,1,0:T(8,128)(2,1)}, bf16[2,512,256]{2,1,0:T(8,128)(2,1)}, u32[]{:S(2)}, u32[]{:S(2)}) collective-permute-start(bf16[2,512,256]{2,1,0:T(8,128)(2,1)} %get-tuple-element.98), channel_id=1, source_target_pairs={{0,8},{8,0},{1,9},{9,1},{2,10},{10,2},{3,11},{11,3},{4,12},{12,4},... | collective-permute-start | bytes 1572872 | tf_op jit(solution)/shard_map/ppermute | solution.py:24
  65.7 14.0 %collective-permute-start.13 = (bf16[2,512,256]{2,1,0:T(8,128)(2,1)}, bf16[2,512,256]{2,1,0:T(8,128)(2,1)}, u32[]{:S(2)}, u32[]{:S(2)}) collective-permute-start(bf16[2,512,256]{2,1,0:T(8,128)(2,1)} %get-tuple-element.99), channel_id=1, source_target_pairs={{0,16},{16,0},{1,17},{17,1},{2,18},{18,2},{3,19},{19,3},{4,20},{20... | collective-permute-start | bytes 1572872 | tf_op jit(solution)/shard_map/ppermute | solution.py:24
  66.2 15.7 %copy-start.2 = (bf16[2,512,256]{2,1,0:T(8,128)(2,1)S(1)}, bf16[2,512,256]{2,1,0:T(8,128)(2,1)}, u32[]{:S(2)}) copy-start(bf16[2,512,256]{2,1,0:T(8,128)(2,1)} %get-tuple-element.140.refs_3_) | copy-start | bytes 1572868
  79.7 7.5 %collective-permute-start.16 = (bf16[4,1024,512]{2,1,0:T(8,128)(2,1)}, bf16[4,1024,512]{2,1,0:T(8,128)(2,1)}, u32[]{:S(2)}, u32[]{:S(2)}) collective-permute-start(bf16[4,1024,512]{2,1,0:T(8,128)(2,1)} %get-tuple-element.132.weight_ref), channel_id=1, source_target_pairs={{0,4},{4,0},{1,5},{5,1},{2,6},{6,2},{3,7},{7,3},{8,12},{12,8},{9,1... | collective-permute-start | bytes 12582920 | tf_op jit(solution)/shard_map/ppermute | solution.py:24
  79.7 27.7 %collective-permute-start.17 = (bf16[4,512,256]{2,1,0:T(8,128)(2,1)}, bf16[4,512,256]{2,1,0:T(8,128)(2,1)}, u32[]{:S(2)}, u32[]{:S(2)}) collective-permute-start(bf16[4,512,256]{2,1,0:T(8,128)(2,1)} %get-tuple-element.137), channel_id=1, source_target_pairs={{0,1},{1,2},{2,3},{3,0},{4,5},{5,6},{6,7},{7,4},{8,9},{9,10},{10,1... | collective-permute-start | bytes 3145736 | tf_op jit(solution)/shard_map/ppermute | solution.py:24
  82.9 12.0 %collective-permute-start.19 = (bf16[512,256]{1,0:T(8,128)(2,1)S(1)}, bf16[512,256]{1,0:T(8,128)(2,1)S(1)}, u32[]{:S(2)}, u32[]{:S(2)}) collective-permute-start(bf16[512,256]{1,0:T(8,128)(2,1)S(1)} %fusion.4), channel_id=1, source_target_pairs={{0,8},{8,0},{1,9},{9,1},{2,10},{10,2},{3,11},{11,3},{4,12},{12,4},... | collective-permute-start | bytes 786440 | tf_op jit(solution)/shard_map/ppermute | solution.py:24
  83.5 25.7 %copy-start.1 = (bf16[2,512,256]{2,1,0:T(8,128)(2,1)S(1)}, bf16[2,512,256]{2,1,0:T(8,128)(2,1)}, u32[]{:S(2)}) copy-start(bf16[2,512,256]{2,1,0:T(8,128)(2,1)} %get-tuple-element.138.refs_0_) | copy-start | bytes 1572868
  83.5 25.7 %copy-start.3 = (bf16[2,512,256]{2,1,0:T(8,128)(2,1)S(1)}, bf16[2,512,256]{2,1,0:T(8,128)(2,1)}, u32[]{:S(2)}) copy-start(bf16[2,512,256]{2,1,0:T(8,128)(2,1)} %get-tuple-element.140.refs_3_) | copy-start | bytes 1572868
  84.6 10.3 %collective-permute-start.18 = (bf16[512,256]{1,0:T(8,128)(2,1)S(1)}, bf16[512,256]{1,0:T(8,128)(2,1)S(1)}, u32[]{:S(2)}, u32[]{:S(2)}) collective-permute-start(bf16[512,256]{1,0:T(8,128)(2,1)S(1)} %fusion.3), channel_id=1, source_target_pairs={{0,16},{16,0},{1,17},{17,1},{2,18},{18,2},{3,19},{19,3},{4,20},{20... | collective-permute-start | bytes 786440 | tf_op jit(solution)/shard_map/ppermute | solution.py:24
  108.7 13.6 %collective-permute-start.20 = (bf16[2,512,256]{2,1,0:T(8,128)(2,1)S(1)}, bf16[2,512,256]{2,1,0:T(8,128)(2,1)S(1)}, u32[]{:S(2)}, u32[]{:S(2)}) collective-permute-start(bf16[2,512,256]{2,1,0:T(8,128)(2,1)S(1)} %add_convert_fusion), channel_id=1, source_target_pairs={{0,16},{16,0},{1,17},{17,1},{2,18},{18,2},{3,19},{19,3},{4,20},{20... | collective-permute-start | bytes 1572872 | tf_op jit(solution)/shard_map/ppermute | solution.py:24
  110.5 20.5 %collective-permute-start.22 = (bf16[512,256]{1,0:T(8,128)(2,1)S(1)}, bf16[512,256]{1,0:T(8,128)(2,1)S(1)}, u32[]{:S(2)}, u32[]{:S(2)}) collective-permute-start(bf16[512,256]{1,0:T(8,128)(2,1)S(1)} %get-tuple-element.150), channel_id=1, source_target_pairs={{0,3},{1,0},{2,1},{3,2},{4,7},{5,4},{6,5},{7,6},{8,11},{9,8},{10,9... | collective-permute-start | bytes 786440 | tf_op jit(solution)/shard_map/ppermute | solution.py:24
  111.6 10.7 %copy-start.11 = (bf16[4,512,256]{2,1,0:T(8,128)(2,1)S(1)}, bf16[4,512,256]{2,1,0:T(8,128)(2,1)}, u32[]{:S(2)}) copy-start(bf16[4,512,256]{2,1,0:T(8,128)(2,1)} %get-tuple-element.145) | copy-start | bytes 3145732
  111.6 19.3 %collective-permute-start.23 = (bf16[512,256]{1,0:T(8,128)(2,1)S(1)}, bf16[512,256]{1,0:T(8,128)(2,1)S(1)}, u32[]{:S(2)}, u32[]{:S(2)}) collective-permute-start(bf16[512,256]{1,0:T(8,128)(2,1)S(1)} %get-tuple-element.151), channel_id=1, source_target_pairs={{0,2},{1,3},{2,0},{3,1},{4,6},{5,7},{6,4},{7,5},{8,10},{9,11},{10,... | collective-permute-start | bytes 786440 | tf_op jit(solution)/shard_map/ppermute | solution.py:24
  123.4 7.6 %collective-permute-start.21 = (bf16[512,256]{1,0:T(8,128)(2,1)S(1)}, bf16[512,256]{1,0:T(8,128)(2,1)S(1)}, u32[]{:S(2)}, u32[]{:S(2)}) collective-permute-start(bf16[512,256]{1,0:T(8,128)(2,1)S(1)} %fusion.5), channel_id=1, source_target_pairs={{0,8},{8,0},{1,9},{9,1},{2,10},{10,2},{3,11},{11,3},{4,12},{12,4},... | collective-permute-start | bytes 786440 | tf_op jit(solution)/shard_map/ppermute | solution.py:24
  124.1 8.1 %copy-start.12 = (bf16[256]{0:T(256)(128)(2,1)S(1)}, bf16[256]{0:T(256)(128)(2,1)}, u32[]{:S(2)}) copy-start(bf16[256]{0:T(256)(128)(2,1)} %param.11) | copy-start | bytes 1540
  124.1 8.1 %copy-start.10 = (bf16[256,512]{1,0:T(8,128)(2,1)S(1)}, bf16[256,512]{1,0:T(8,128)(2,1)}, u32[]{:S(2)}) copy-start(bf16[256,512]{1,0:T(8,128)(2,1)} %param.12) | copy-start | bytes 786436
  (5 other events, 15.2 us)

commit v15 on v14

--- a/solution.py
+++ b/solution.py
@@ -82,8 +82,16 @@
         def _():
             keep_ref[0] = totals[slot]
 
-    for slot in (2, 3):
-        outs[slot + 2][0] = totals[slot]
+    near_ref, far_ref, kept_ref = outs[4:]
+    kept_ref[0] = totals[3]
+
+    @pl.when(ways[1] == 1)
+    def _():
+        far_ref[0] = totals[2]
+
+    @pl.when(ways[1] == 0)
+    def _():
+        near_ref[0] = totals[2]
 
 
 def grad_product(residual, cot_t, places, rows, other):
@@ -108,14 +116,15 @@
             lambda i: i // 2,
             lambda i: jnp.maximum(i - 2, 0),
             lambda i: jnp.minimum(i, 1),
-            lambda i: i,
+            lambda i: jnp.minimum(i, 1),
+            lambda i: jnp.maximum(i - 2, 0),
             lambda i: i,
         ]
         out_specs = [
             pl.BlockSpec((1, features, rows), lambda i, p, index=index: (index(i), 0, 0))
             for index in indices
         ]
-        out_shape = [pltpu.HBM((n, features, rows), BF16) for n in (2, 2, 2, 2, steps, steps)]
+        out_shape = [pltpu.HBM((n, features, rows), BF16) for n in (2, 2, 2, 2, 2, 2, steps)]
     return pl.pallas_call(
         kernel,
         out_shape=out_shape,
@@ -452,7 +461,7 @@
         places = places_of(backward, core)
         if in_place:
             outs = grad_product(residual, cot_t, places, rows, other)
-            return [[([outs[0]], outs[1]), ([outs[2]], outs[3])], outs[4], outs[5]]
+            return [[([outs[0]], outs[1]), ([outs[2]], outs[3])], outs[4], outs[5], outs[6]]
         else:
             both = product[places].reshape(len(chips), tp_count, features, rows).swapaxes(0, 1)
             total = widen([both, other]).astype(BF16)
@@ -496,9 +505,11 @@
         own_pieces[k] = far_of(k, arrived[k], near[k])
     sides = for_us(other)
     if in_place:
-        sides, passed, kept = sides[:1], sides[1], sides[2]
+        sides, passed_near, passed_far, kept = sides[:1], sides[1], sides[2], sides[3]
         kept, own_pieces = lax.optimization_barrier((kept, own_pieces))
-        passed = swap(passed, "tp", 1)
+        beyond = swap(passed_far, "tp", 1)
+    else:
+        beyond = ()
     got = [first_round(sides[0])]
     sides[1:], own_pieces = lax.optimization_barrier((sides[1:], own_pieces))
 
@@ -523,9 +534,13 @@
         weight = weight[:, :, (at_inner - jnp.arange(inner)) % inner]
         own_weight = weight.transpose(1, 2, 0, 3, 4).reshape(outer * inner, depth, features)
         total = jnp.zeros((), F32)
-    got[0], sides[1:], total, own_weight = lax.optimization_barrier(
-        (got[0], sides[1:], total, own_weight)
-    )
+    got[0], sides[1:], total, own_weight, beyond = lax.optimization_barrier(
+        (got[0], sides[1:], total, own_weight, beyond)
+    )
+    if in_place:
+        beyond, passed_near = lax.optimization_barrier((beyond, passed_near))
+        passed_near = swap(passed_near, "tp", 1)
+        crossed = swap(widen([kept[2:], beyond]).astype(BF16), "outer", 1)
     other_weight = swap(own_weight, "core", 1)
     later = [second_round(sides[0], got[0])]
     got += [first_round(side) for side in sides[1:]]
@@ -550,24 +565,25 @@
         coefficient = inv_rms * inv_rms * share * (1.0 / width)
     later[0], coefficient = lax.optimization_barrier((later[0], coefficient))
     if in_place:
-        passed, coefficient = lax.optimization_barrier((passed, coefficient))
-        crossed = swap(widen([kept[2:], passed[2:]]).astype(BF16), "outer", 1)
+        crossed, passed_near, coefficient = lax.optimization_barrier(
+            (crossed, passed_near, coefficient)
+        )
+        beside = swap(widen([kept[1], passed_near[1], crossed[1]]).astype(BF16), "inner", 1)
         groups = [[keep] + parts + then for (_, keep), parts, then in zip(sides[0], got[0], later[0])]
         last = [swap(x, "tp", k) for x, k in zip(sums_of(groups, 0), pairs[0])]
         grad_shape = jax.ShapeDtypeStruct((rows_here, width), BF16)
         resid_grad = weight_call(
             grad_kernel, places[0], residual, in_hbm(own_weight), [cot, coefficient], grad_shape
         )
-        crossed, resid_grad = lax.optimization_barrier((crossed, resid_grad))
-        beside = swap(widen([kept[1], passed[1], crossed[1]]).astype(BF16), "inner", 1)
+        beside, resid_grad = lax.optimization_barrier((beside, resid_grad))
         resid_grad = weight_call(
             grad_kernel, places[1][:3], residual, other_weight, [cot, coefficient], grad_shape, resid_grad
         )
-        beside, last, resid_grad = lax.optimization_barrier((beside, last, resid_grad))
+        last, resid_grad = lax.optimization_barrier((last, resid_grad))
         resid_grad = weight_call(
             grad_kernel, places[1][3:], residual, other_weight, [cot, coefficient], grad_shape, resid_grad
         )
-        grad_rows = widen([kept[0], passed[0], crossed[0], beside] + last)
+        grad_rows = widen([kept[0], passed_near[0], crossed[0], beside] + last)
     else:
         normed_grad = lax.dot_general(
             cot, weight, (((1,), (1,)), ((), ())), preferred_element_type=F32

time: 138 us -> 133 us (0.964)
  waiting for transfers between devices: 32.5 us -> 23.5 us
  starting transfers between devices: 27.6 us -> 29.9 us
  other arithmetic: 19.5 us -> 21 us
    ppermute x22 -> x23, waiting for transfers between devices: 32.4 us -> 23.5 us  [swap(): lax.ppermute(value, axis, [(place, (place + step) % size) for place in ra...]
    ppermute x22 -> x23, starting transfers between devices: 21.9 us -> 24.3 us  [swap(): lax.ppermute(value, axis, [(place, (place + step) % size) for place in ra...]
  transfers between devices with their start and end apart: 24 -> 25, of which waited for: 11 -> 10; matrix products, arithmetic and copies ran while one was open for 12% -> 14% of each run, Pallas kernels for 35% -> 36%
where the time goes in v15:
time: 133 us; the launch traced here: 132 us
  Pallas kernels  51.4 us (39%)
  starting transfers between devices  29.9 us (22%)
  waiting for transfers between devices  23.5 us (18%)
  other arithmetic  21 us (16%)
  local copies, waits for them, and re-layouts  5.69 us (4%)
    pallas_call x4, Pallas kernels, weight_call(): pl.pallas_call(kernel, out_shape=out_shape, grid_spec=pltpu.PrefetchScala...  25.5 us
    ppermute x23, starting transfers between devices, swap(): lax.ppermute(value, axis, [(place, (place + step) % size) for place in ra...  24.3 us
    ppermute x23, waiting for transfers between devices, swap(): lax.ppermute(value, axis, [(place, (place + step) % size) for place in ra...  23.5 us
    pallas_call x2, Pallas kernels, grad_product(): pl.pallas_call(kernel, out_shape=out_shape, grid_spec=pltpu.PrefetchScala...  14.8 us
    pallas_call x1, Pallas kernels, first_value(): pl.pallas_call(functools.partial(value_kernel, inner_flags), out_shape=[t...  7.78 us
    ppermute x2, starting transfers between devices, trade(): lax.ppermute(value, axis, [(place, place ^ mask) for place in range(size)])  5.67 us
    reduce_sum x1, other arithmetic, per_device(): squares = jnp.sum(resid_wide * resid_wide, axis=1, keepdims=True)  5.1 us
    unnamed x27, local copies, waits for them, and re-layouts  3.99 us
  transfers between devices with their start and end apart: 25, of which 10 were waited for; matrix products, arithmetic and copies ran while one was open for 14% of the time, Pallas kernels for 36%

profile of v15, /device:TPU:0, one launch (start us, length us, event | category | flops | bytes accessed | tf_op | source)
XLA Modules:
  0.0 132.3 jit_solution(8092526584691857800)
XLA Ops:
  2.1 3.0 %collective-permute-start = (f32[1,52,128]{2,1,0:T(8,128)S(1)}, f32[1,52,128]{2,1,0:T(8,128)S(1)}, u32[]{:S(2)}, u32[]{:S(2)}) collective-permute-start(f32[1,52,128]{2,1,0:T(8,128)S(1)} %maximum_bitcast_fusion), channel_id=1, source_target_pairs={{0,1},{1,0},{2,3},{3,2},{4,5},{5,4},{6,7},{7,6},{8,9},{9,8},{10,11... | collective-permute-start | bytes 79880 | tf_op jit(solution)/shard_map/ppermute | solution.py:29
  5.8 1.8 %multiply_convert_fusion = bf16[256,512]{1,0:T(8,128)(2,1)} fusion(bf16[256,512]{1,0:T(8,128)(2,1)} %param.12, f32[256]{0:T(256)S(1)} %convert_element_type.93), kind=kLoop, calls=%fused_computation.15 | loop fusion | flops 393216 | bytes 525312 | tf_op jit(solution)/shard_map/convert_element_type | solution.py:401
  8.8 1.6 %collective-permute-start.2 = (bf16[256,512]{1,0:T(8,128)(2,1)}, bf16[256,512]{1,0:T(8,128)(2,1)S(1)}, u32[]{:S(2)}, u32[]{:S(2)}) collective-permute-start(bf16[256,512]{1,0:T(8,128)(2,1)} %multiply_convert_fusion), channel_id=1, source_target_pairs={{0,8},{8,0},{1,9},{9,1},{2,10},{10,2},{3,11},{11,3},{4,12},{12,4},... | collective-permute-start | bytes 786440 | tf_op jit(solution)/shard_map/ppermute | solution.py:24
  10.8 5.1 %multiply_reduce_fusion = f32[512]{0:T(512)S(1)} fusion(bf16[512,8192]{1,0:T(8,128)(2,1)} %resid_ref.4), kind=kLoop, calls=%fused_computation | loop fusion | flops 12582400 | bytes 8390656 | tf_op jit(solution)/shard_map/reduce_sum | solution.py:404
  15.9 2.6 %collective-permute-start.5 = (f32[2,52,128]{2,1,0:T(8,128)S(1)}, f32[2,52,128]{2,1,0:T(8,128)S(1)}, u32[]{:S(2)}, u32[]{:S(2)}) collective-permute-start(f32[2,52,128]{2,1,0:T(8,128)S(1)} %pad_maximum_fusion.5), channel_id=1, source_target_pairs={{0,2},{1,3},{2,0},{3,1},{4,6},{5,7},{6,4},{7,5},{8,10},{9,11},{10,... | collective-permute-start | bytes 159752 | tf_op jit(solution)/shard_map/ppermute | solution.py:29
  18.6 1.4 %collective-permute-done.1 = bf16[256,512]{1,0:T(8,128)(2,1)S(1)} collective-permute-done((bf16[256,512]{1,0:T(8,128)(2,1)}, bf16[256,512]{1,0:T(8,128)(2,1)S(1)}, u32[]{:S(2)}, u32[]{:S(2)}) %collective-permute-start.1) | collective-permute-done | bytes 262176 | tf_op jit(solution)/shard_map/ppermute | solution.py:24
  21.0 1.5 %collective-permute-start.3 = (bf16[256,512]{1,0:T(8,128)(2,1)S(1)}, bf16[256,512]{1,0:T(8,128)(2,1)S(1)}, u32[]{:S(2)}, u32[]{:S(2)}) collective-permute-start(bf16[256,512]{1,0:T(8,128)(2,1)S(1)} %collective-permute-done.1), channel_id=1, source_target_pairs={{0,16},{16,0},{1,17},{17,1},{2,18},{18,2},{3,19},{19,3},{4,20},{20... | collective-permute-start | bytes 786440 | tf_op jit(solution)/shard_map/ppermute | solution.py:24
  24.9 2.2 %collective-permute-done.4 = bf16[256,512]{1,0:T(8,128)(2,1)} collective-permute-done((bf16[256,512]{1,0:T(8,128)(2,1)}, bf16[256,512]{1,0:T(8,128)(2,1)}, u32[]{:S(2)}, u32[]{:S(2)}) %collective-permute-start.4) | collective-permute-done | bytes 262176 | tf_op jit(solution)/shard_map/ppermute | solution.py:24
  27.1 3.1 %collective-permute-done.3 = bf16[256,512]{1,0:T(8,128)(2,1)S(1)} collective-permute-done((bf16[256,512]{1,0:T(8,128)(2,1)S(1)}, bf16[256,512]{1,0:T(8,128)(2,1)S(1)}, u32[]{:S(2)}, u32[]{:S(2)}) %collective-permute-start.3) | collective-permute-done | bytes 262176 | tf_op jit(solution)/shard_map/ppermute | solution.py:24
  31.5 1.6 %collective-permute-start.9 = (bf16[256,512]{1,0:T(8,128)(2,1)}, bf16[256,512]{1,0:T(8,128)(2,1)}, u32[]{:S(2)}, u32[]{:S(2)}) collective-permute-start(bf16[256,512]{1,0:T(8,128)(2,1)} %collective-permute-done.4), channel_id=1, source_target_pairs={{0,16},{16,0},{1,17},{17,1},{2,18},{18,2},{3,19},{19,3},{4,20},{20... | collective-permute-start | bytes 786440 | tf_op jit(solution)/shard_map/ppermute | solution.py:24
  33.1 2.1 %shard_map.129 = (bf16[512,512]{1,0:T(8,128)(2,1)S(1)}, bf16[512,512]{1,0:T(8,128)(2,1)S(1)}, f32[512,1]{1,0:T(8,128)S(1)}) custom-call(s32[2]{0:T(128)S(1)} %pad_add_fusion.1.info_ref, f32[4,52,128]{2,1,0:T(8,128)S(1)} %pad_maximum_fusion.4.shares_ref, f32[512,1]{1,0:T(8,128)S(1)} %copy.18.squares_ref, bf16[512,512]{1,0:T(8,128)(2,1)} %value_cot_ref.1), custom_call_target="tpu_custom_call" | custom-call | flops 1024 | bytes 1024 | tf_op jit(solution)/shard_map/pallas_call | solution.py:350
  35.2 6.6 %shard_map.130 = bf16[4,4,512,256]{3,2,1,0:T(8,128)(2,1)} custom-call(s32[16]{0:T(128)S(1)} %stack.232.places_ref, bf16[512,512]{1,0:T(8,128)(2,1)S(1)} %get-tuple-element.94.cot_ref, bf16[512,8192]{1,0:T(8,128)(2,1)} %resid_ref.4, bf16[512,8192]{1,0:T(8,128)(2,1)} %resid_ref.4, bf16[512,8192]{1,0:T(8,128)(2,1)} %resid_ref.4, bf16[512,8192]{1,0:T(8,128)(2,1)} %resid_ref.4), custom_call_target="tpu_custom_call" | custom-call | flops 1024 | bytes 1024 | tf_op jit(solution)/shard_map/pallas_call | solution.py:128
  41.8 1.6 %collective-permute-start.10 = (bf16[256,512]{1,0:T(8,128)(2,1)}, bf16[256,512]{1,0:T(8,128)(2,1)}, u32[]{:S(2)}, u32[]{:S(2)}) collective-permute-start(bf16[256,512]{1,0:T(8,128)(2,1)} %collective-permute-done.6), channel_id=1, source_target_pairs={{0,8},{8,0},{1,9},{9,1},{2,10},{10,2},{3,11},{11,3},{4,12},{12,4},... | collective-permute-start | bytes 786440 | tf_op jit(solution)/shard_map/ppermute | solution.py:24
  44.6 3.9 %collective-permute-done.10 = bf16[256,512]{1,0:T(8,128)(2,1)} collective-permute-done((bf16[256,512]{1,0:T(8,128)(2,1)}, bf16[256,512]{1,0:T(8,128)(2,1)}, u32[]{:S(2)}, u32[]{:S(2)}) %collective-permute-start.10) | collective-permute-done | bytes 262176 | tf_op jit(solution)/shard_map/ppermute | solution.py:24
  51.3 1.6 %collective-permute-start.14 = (bf16[2,256,512]{2,1,0:T(8,128)(2,1)S(1)}, bf16[2,256,512]{2,1,0:T(8,128)(2,1)}, u32[]{:S(2)}, u32[]{:S(2)}) collective-permute-start(bf16[2,256,512]{2,1,0:T(8,128)(2,1)S(1)} %pad_maximum_fusion.2.rest_4_), channel_id=1, source_target_pairs={{0,8},{8,0},{1,9},{9,1},{2,10},{10,2},{3,11},{11,3},{4,12},{12,4},... | collective-permute-start | bytes 1572872 | tf_op jit(solution)/shard_map/ppermute | solution.py:24
  52.9 3.1 %collective-permute-done.11.rest_4_ = bf16[4,4,512,256]{3,2,1,0:T(8,128)(2,1)} collective-permute-done((bf16[4,4,512,256]{3,2,1,0:T(8,128)(2,1)}, bf16[4,4,512,256]{3,2,1,0:T(8,128)(2,1)}, u32[]{:S(2)}, u32[]{:S(2)}) %collective-permute-start.11) | collective-permute-done | bytes 4194336 | tf_op jit(solution)/shard_map/ppermute | solution.py:24
  56.1 8.2 %shard_map.131 = (bf16[2,512,256]{2,1,0:T(8,128)(2,1)}, bf16[2,512,256]{2,1,0:T(8,128)(2,1)}, bf16[2,512,256]{2,1,0:T(8,128)(2,1)}, bf16[2,512,256]{2,1,0:T(8,12...) custom-call(s32[16]{0:T(128)S(1)} %stack.213.places_ref, ...), custom_call_target="tpu_custom_call" | custom-call | flops 1024 | bytes 1024 | tf_op jit(solution)/shard_map/pallas_call | solution.py:128
  64.3 1.6 %collective-permute-start.12 = (bf16[2,512,256]{2,1,0:T(8,128)(2,1)}, bf16[2,512,256]{2,1,0:T(8,128)(2,1)}, u32[]{:S(2)}, u32[]{:S(2)}) collective-permute-start(bf16[2,512,256]{2,1,0:T(8,128)(2,1)} %get-tuple-element.102), channel_id=1, source_target_pairs={{0,8},{8,0},{1,9},{9,1},{2,10},{10,2},{3,11},{11,3},{4,12},{12,4},... | collective-permute-start | bytes 1572872 | tf_op jit(solution)/shard_map/ppermute | solution.py:24
  66.3 3.2 %collective-permute-start.16 = (bf16[2,512,256]{2,1,0:T(8,128)(2,1)}, bf16[2,512,256]{2,1,0:T(8,128)(2,1)}, u32[]{:S(2)}, u32[]{:S(2)}) collective-permute-start(bf16[2,512,256]{2,1,0:T(8,128)(2,1)} %get-tuple-element.136), channel_id=1, source_target_pairs={{0,1},{1,2},{2,3},{3,0},{4,5},{5,6},{6,7},{7,4},{8,9},{9,10},{10,1... | collective-permute-start | bytes 1572872 | tf_op jit(solution)/shard_map/ppermute | solution.py:24
  71.8 7.8 %shard_map.132 = (f32[512,512]{1,0:T(8,128)}, bf16[4,1024,512]{2,1,0:T(8,128)(2,1)}) custom-call(s32[4]{0:T(128)S(1)} %get-tuple-element.178.places_ref, s32[4]{0:T(128)S(1)} %get-tuple-element.179.offsets_ref, bf16[512,8192]{1,0:T(8,128)(2,1)} %resid_ref.4, bf16[2,256,512]{2,1,0:T(8,128)(2,1)S(1)} %pad_maximum_fusion.rest_0_, ...), custom_call_target="tpu_custom_call" | custom-call | flops 1024 | bytes 1024 | tf_op jit(solution)/shard_map/pallas_call | solution.py:250
  79.8 2.0 %collective-permute-done.16 = bf16[2,512,256]{2,1,0:T(8,128)(2,1)} collective-permute-done((bf16[2,512,256]{2,1,0:T(8,128)(2,1)}, bf16[2,512,256]{2,1,0:T(8,128)(2,1)}, u32[]{:S(2)}, u32[]{:S(2)}) %collective-permute-start.16) | collective-permute-done | bytes 524320 | tf_op jit(solution)/shard_map/ppermute | solution.py:24
  83.0 1.6 %collective-permute-start.18 = (bf16[2,512,256]{2,1,0:T(8,128)(2,1)S(1)}, bf16[2,512,256]{2,1,0:T(8,128)(2,1)}, u32[]{:S(2)}, u32[]{:S(2)}) collective-permute-start(bf16[2,512,256]{2,1,0:T(8,128)(2,1)S(1)} %add_convert_fusion), channel_id=1, source_target_pairs={{0,16},{16,0},{1,17},{17,1},{2,18},{18,2},{3,19},{19,3},{4,20},{20... | collective-permute-start | bytes 1572872 | tf_op jit(solution)/shard_map/ppermute | solution.py:24
  85.0 1.7 %fusion.4 = bf16[512,256]{1,0:T(8,128)(2,1)} fusion(bf16[2,512,256]{2,1,0:T(8,128)(2,1)} %collective-permute-done.13.refs_4_, bf16[2,512,256]{2,1,0:T(8,128)(2,1)S(1)} %copy-done.2), kind=kLoop, calls=%fused_computation.17 | loop fusion | flops 524288 | bytes 786432 | tf_op jit(solution)/shard_map/convert_element_type | solution.py:486
  87.3 1.7 %fusion.3 = bf16[512,256]{1,0:T(8,128)(2,1)} fusion(bf16[2,512,256]{2,1,0:T(8,128)(2,1)} %collective-permute-done.12.refs_1_, bf16[2,512,256]{2,1,0:T(8,128)(2,1)S(1)} %copy-done), kind=kLoop, calls=%fused_computation.16 | loop fusion | flops 524288 | bytes 786432 | tf_op jit(solution)/shard_map/convert_element_type | solution.py:486
  89.0 1.5 %collective-permute-start.20 = (bf16[512,256]{1,0:T(8,128)(2,1)}, bf16[512,256]{1,0:T(8,128)(2,1)S(1)}, u32[]{:S(2)}, u32[]{:S(2)}) collective-permute-start(bf16[512,256]{1,0:T(8,128)(2,1)} %fusion.3), channel_id=1, source_target_pairs={{0,16},{16,0},{1,17},{17,1},{2,18},{18,2},{3,19},{19,3},{4,20},{20... | collective-permute-start | bytes 786440 | tf_op jit(solution)/shard_map/ppermute | solution.py:24
  90.6 7.7 %shard_map.133 = (bf16[512,512]{1,0:T(8,128)(2,1)}, f32[512,1]{1,0:T(8,128)S(1)}) custom-call(s32[4]{0:T(128)S(1)} %pad_add_fusion.places_ref, bf16[512,8192]{1,0:T(8,128)(2,1)} %resid_ref.4, bf16[4,1024,512]{2,1,0:T(8,128)(2,1)} %collective-permute-done.17.weight_ref, f32[512,512]{1,0:T(8,128)} %get-tuple-element.138.first_ref, ...), custom_call_target="tpu_custom_call" | custom-call | flops 1024 | bytes 1024 | tf_op jit(solution)/shard_map/pallas_call | solution.py:288
  98.3 4.7 %collective-permute-done.20.refs_2_ = bf16[512,256]{1,0:T(8,128)(2,1)S(1)} collective-permute-done((bf16[512,256]{1,0:T(8,128)(2,1)}, bf16[512,256]{1,0:T(8,128)(2,1)S(1)}, u32[]{:S(2)}, u32[]{:S(2)}) %collective-permute-start.20) | collective-permute-done | bytes 262176 | tf_op jit(solution)/shard_map/ppermute | solution.py:24
  107.2 1.8 %collective-permute-start.23 = (bf16[512,256]{1,0:T(8,128)(2,1)S(1)}, bf16[512,256]{1,0:T(8,128)(2,1)S(1)}, u32[]{:S(2)}, u32[]{:S(2)}) collective-permute-start(bf16[512,256]{1,0:T(8,128)(2,1)S(1)} %get-tuple-element.157), channel_id=1, source_target_pairs={{0,2},{1,3},{2,0},{3,1},{4,6},{5,7},{6,4},{7,5},{8,10},{9,11},{10,... | collective-permute-start | bytes 786440 | tf_op jit(solution)/shard_map/ppermute | solution.py:24
  109.1 7.7 %shard_map.135.rest_0_ = bf16[512,8192]{1,0:T(8,128)(2,1)} custom-call(s32[4]{0:T(128)S(1)} %get-tuple-element.178.places_ref, bf16[512,8192]{1,0:T(8,128)(2,1)} %resid_ref.4, bf16[4,1024,512]{2,1,0:T(8,128)(2,1)} %get-tuple-element.137.weight_ref, bf16[512,512]{1,0:T(8,128)(2,1)S(1)} %get-tuple-element.139.cot_ref, f32[512,1]{1,0:T(8,128)S(1)} %get-tuple-element.153.coef_ref), custom_call_target="tpu_custom_call" | custom-call | flops 1024 | bytes 1024 | tf_op jit(solution)/shard_map/pallas_call | solution.py:288
  116.8 6.9 %shard_map.136.rest_0_ = bf16[512,8192]{1,0:T(8,128)(2,1)} custom-call(s32[3]{0:T(128)S(1)} %pad_add_fusion.4.places_ref, bf16[512,8192]{1,0:T(8,128)(2,1)} %resid_ref.4, bf16[4,1024,512]{2,1,0:T(8,128)(2,1)} %collective-permute-done.17.weight_ref, bf16[512,512]{1,0:T(8,128)(2,1)S(1)} %get-tuple-element.139.cot_ref, ...), custom_call_target="tpu_custom_call", output_to_operand_aliasing={{}: (5, {})} | custom-call | flops 1024 | bytes 1024 | tf_op jit(solution)/shard_map/pallas_call | solution.py:288
  123.7 2.2 %collective-permute-done.23 = bf16[512,256]{1,0:T(8,128)(2,1)S(1)} collective-permute-done((bf16[512,256]{1,0:T(8,128)(2,1)S(1)}, bf16[512,256]{1,0:T(8,128)(2,1)S(1)}, u32[]{:S(2)}, u32[]{:S(2)}) %collective-permute-start.23) | collective-permute-done | bytes 262176 | tf_op jit(solution)/shard_map/ppermute | solution.py:24
  129.0 3.3 %shard_map.137 = bf16[512,8192]{1,0:T(8,128)(2,1)} custom-call(s32[1]{0:T(128)} %bitcast.3.places_ref, bf16[512,8192]{1,0:T(8,128)(2,1)} %resid_ref.4, bf16[4,1024,512]{2,1,0:T(8,128)(2,1)} %collective-permute-done.17.weight_ref, bf16[512,512]{1,0:T(8,128)(2,1)S(1)} %get-tuple-element.139.cot_ref, ...), custom_call_target="tpu_custom_call", output_to_operand_aliasing={{}: (5, {})} | custom-call | flops 1024 | bytes 1024 | tf_op jit(solution)/shard_map/pallas_call | solution.py:288
  (81 shorter events, 25.0 us)
Async XLA Ops:
  2.1 6.7 %collective-permute-start = (f32[1,52,128]{2,1,0:T(8,128)S(1)}, f32[1,52,128]{2,1,0:T(8,128)S(1)}, u32[]{:S(2)}, u32[]{:S(2)}) collective-permute-start(f32[1,52,128]{2,1,0:T(8,128)S(1)} %maximum_bitcast_fusion), channel_id=1, source_target_pairs={{0,1},{1,0},{2,3},{3,2},{4,5},{5,4},{6,7},{7,6},{8,9},{9,8},{10,11... | collective-permute-start | bytes 79880 | tf_op jit(solution)/shard_map/ppermute | solution.py:29
  8.8 9.8 %collective-permute-start.2 = (bf16[256,512]{1,0:T(8,128)(2,1)}, bf16[256,512]{1,0:T(8,128)(2,1)S(1)}, u32[]{:S(2)}, u32[]{:S(2)}) collective-permute-start(bf16[256,512]{1,0:T(8,128)(2,1)} %multiply_convert_fusion), channel_id=1, source_target_pairs={{0,8},{8,0},{1,9},{9,1},{2,10},{10,2},{3,11},{11,3},{4,12},{12,4},... | collective-permute-start | bytes 786440 | tf_op jit(solution)/shard_map/ppermute | solution.py:24
  10.4 9.6 %collective-permute-start.1 = (bf16[256,512]{1,0:T(8,128)(2,1)}, bf16[256,512]{1,0:T(8,128)(2,1)S(1)}, u32[]{:S(2)}, u32[]{:S(2)}) collective-permute-start(bf16[256,512]{1,0:T(8,128)(2,1)} %multiply_convert_fusion), channel_id=1, source_target_pairs={{0,1},{1,2},{2,3},{3,0},{4,5},{5,6},{6,7},{7,4},{8,9},{9,10},{10,1... | collective-permute-start | bytes 786440 | tf_op jit(solution)/shard_map/ppermute | solution.py:24
  15.9 7.4 %collective-permute-start.5 = (f32[2,52,128]{2,1,0:T(8,128)S(1)}, f32[2,52,128]{2,1,0:T(8,128)S(1)}, u32[]{:S(2)}, u32[]{:S(2)}) collective-permute-start(f32[2,52,128]{2,1,0:T(8,128)S(1)} %pad_maximum_fusion.5), channel_id=1, source_target_pairs={{0,2},{1,3},{2,0},{3,1},{4,6},{5,7},{6,4},{7,5},{8,10},{9,11},{10,... | collective-permute-start | bytes 159752 | tf_op jit(solution)/shard_map/ppermute | solution.py:29
  19.9 7.2 %collective-permute-start.4 = (bf16[256,512]{1,0:T(8,128)(2,1)}, bf16[256,512]{1,0:T(8,128)(2,1)}, u32[]{:S(2)}, u32[]{:S(2)}) collective-permute-start(bf16[256,512]{1,0:T(8,128)(2,1)} %multiply_convert_fusion), channel_id=1, source_target_pairs={{0,3},{1,0},{2,1},{3,2},{4,7},{5,4},{6,5},{7,6},{8,11},{9,8},{10,9... | collective-permute-start | bytes 786440 | tf_op jit(solution)/shard_map/ppermute | solution.py:24
  21.0 9.2 %collective-permute-start.3 = (bf16[256,512]{1,0:T(8,128)(2,1)S(1)}, bf16[256,512]{1,0:T(8,128)(2,1)S(1)}, u32[]{:S(2)}, u32[]{:S(2)}) collective-permute-start(bf16[256,512]{1,0:T(8,128)(2,1)S(1)} %collective-permute-done.1), channel_id=1, source_target_pairs={{0,16},{16,0},{1,17},{17,1},{2,18},{18,2},{3,19},{19,3},{4,20},{20... | collective-permute-start | bytes 786440 | tf_op jit(solution)/shard_map/ppermute | solution.py:24
  24.3 19.1 %collective-permute-start.7 = (bf16[2,256,512]{2,1,0:T(8,128)(2,1)S(1)}, bf16[2,256,512]{2,1,0:T(8,128)(2,1)S(1)}, u32[]{:S(2)}, u32[]{:S(2)}) collective-permute-start(bf16[2,256,512]{2,1,0:T(8,128)(2,1)S(1)} %pad_maximum_fusion.rest_0_), channel_id=1, source_target_pairs={{0,16},{16,0},{1,17},{17,1},{2,18},{18,2},{3,19},{19,3},{4,20},{20... | collective-permute-start | bytes 1572872 | tf_op jit(solution)/shard_map/ppermute | solution.py:24
  30.2 11.6 %collective-permute-start.6 = (bf16[256,512]{1,0:T(8,128)(2,1)}, bf16[256,512]{1,0:T(8,128)(2,1)}, u32[]{:S(2)}, u32[]{:S(2)}) collective-permute-start(bf16[256,512]{1,0:T(8,128)(2,1)} %multiply_convert_fusion), channel_id=1, source_target_pairs={{0,2},{1,3},{2,0},{3,1},{4,6},{5,7},{6,4},{7,5},{8,10},{9,11},{10,... | collective-permute-start | bytes 786440 | tf_op jit(solution)/shard_map/ppermute | solution.py:24
  30.6 14.0 %collective-permute-start.8 = (bf16[2,256,512]{2,1,0:T(8,128)(2,1)S(1)}, bf16[2,256,512]{2,1,0:T(8,128)(2,1)S(1)}, u32[]{:S(2)}, u32[]{:S(2)}) collective-permute-start(bf16[2,256,512]{2,1,0:T(8,128)(2,1)S(1)} %pad_maximum_fusion.1.rest_2_), channel_id=1, source_target_pairs={{0,8},{8,0},{1,9},{9,1},{2,10},{10,2},{3,11},{11,3},{4,12},{12,4},... | collective-permute-start | bytes 1572872 | tf_op jit(solution)/shard_map/ppermute | solution.py:24
  31.5 13.2 %collective-permute-start.9 = (bf16[256,512]{1,0:T(8,128)(2,1)}, bf16[256,512]{1,0:T(8,128)(2,1)}, u32[]{:S(2)}, u32[]{:S(2)}) collective-permute-start(bf16[256,512]{1,0:T(8,128)(2,1)} %collective-permute-done.4), channel_id=1, source_target_pairs={{0,16},{16,0},{1,17},{17,1},{2,18},{18,2},{3,19},{19,3},{4,20},{20... | collective-permute-start | bytes 786440 | tf_op jit(solution)/shard_map/ppermute | solution.py:24
  41.8 6.8 %collective-permute-start.10 = (bf16[256,512]{1,0:T(8,128)(2,1)}, bf16[256,512]{1,0:T(8,128)(2,1)}, u32[]{:S(2)}, u32[]{:S(2)}) collective-permute-start(bf16[256,512]{1,0:T(8,128)(2,1)} %collective-permute-done.6), channel_id=1, source_target_pairs={{0,8},{8,0},{1,9},{9,1},{2,10},{10,2},{3,11},{11,3},{4,12},{12,4},... | collective-permute-start | bytes 786440 | tf_op jit(solution)/shard_map/ppermute | solution.py:24
  48.6 7.5 %collective-permute-start.11 = (bf16[4,4,512,256]{3,2,1,0:T(8,128)(2,1)}, bf16[4,4,512,256]{3,2,1,0:T(8,128)(2,1)}, u32[]{:S(2)}, u32[]{:S(2)}) collective-permute-start(bf16[4,4,512,256]{3,2,1,0:T(8,128)(2,1)} %shard_map.130), channel_id=1, source_target_pairs={{0,4},{4,0},{1,5},{5,1},{2,6},{6,2},{3,7},{7,3},{8,12},{12,8},{9,1... | collective-permute-start | bytes 12582920 | tf_op jit(solution)/shard_map/ppermute | solution.py:24
  49.7 19.9 %collective-permute-start.15 = (bf16[2,256,512]{2,1,0:T(8,128)(2,1)S(1)}, bf16[2,256,512]{2,1,0:T(8,128)(2,1)}, u32[]{:S(2)}, u32[]{:S(2)}) collective-permute-start(bf16[2,256,512]{2,1,0:T(8,128)(2,1)S(1)} %pad_maximum_fusion.3.rest_6_), channel_id=1, source_target_pairs={{0,16},{16,0},{1,17},{17,1},{2,18},{18,2},{3,19},{19,3},{4,20},{20... | collective-permute-start | bytes 1572872 | tf_op jit(solution)/shard_map/ppermute | solution.py:24
  51.3 18.3 %collective-permute-start.14 = (bf16[2,256,512]{2,1,0:T(8,128)(2,1)S(1)}, bf16[2,256,512]{2,1,0:T(8,128)(2,1)}, u32[]{:S(2)}, u32[]{:S(2)}) collective-permute-start(bf16[2,256,512]{2,1,0:T(8,128)(2,1)S(1)} %pad_maximum_fusion.2.rest_4_), channel_id=1, source_target_pairs={{0,8},{8,0},{1,9},{9,1},{2,10},{10,2},{3,11},{11,3},{4,12},{12,4},... | collective-permute-start | bytes 1572872 | tf_op jit(solution)/shard_map/ppermute | solution.py:24
  56.1 34.5 %copy-start.9 = (f32[512,1]{1,0:T(8,128)S(1)}, f32[512,1]{1,0:T(8,128)}, u32[]{:S(2)}) copy-start(f32[512,1]{1,0:T(8,128)} %copy-done.8) | copy-start | bytes 6148
  64.2 23.0 %copy-start = (bf16[2,512,256]{2,1,0:T(8,128)(2,1)S(1)}, bf16[2,512,256]{2,1,0:T(8,128)(2,1)}, u32[]{:S(2)}) copy-start(bf16[2,512,256]{2,1,0:T(8,128)(2,1)} %get-tuple-element.147.refs_0_) | copy-start | bytes 1572868
  64.3 15.3 %collective-permute-start.12 = (bf16[2,512,256]{2,1,0:T(8,128)(2,1)}, bf16[2,512,256]{2,1,0:T(8,128)(2,1)}, u32[]{:S(2)}, u32[]{:S(2)}) collective-permute-start(bf16[2,512,256]{2,1,0:T(8,128)(2,1)} %get-tuple-element.102), channel_id=1, source_target_pairs={{0,8},{8,0},{1,9},{9,1},{2,10},{10,2},{3,11},{11,3},{4,12},{12,4},... | collective-permute-start | bytes 1572872 | tf_op jit(solution)/shard_map/ppermute | solution.py:24
  65.8 14.0 %collective-permute-start.13 = (bf16[2,512,256]{2,1,0:T(8,128)(2,1)}, bf16[2,512,256]{2,1,0:T(8,128)(2,1)}, u32[]{:S(2)}, u32[]{:S(2)}) collective-permute-start(bf16[2,512,256]{2,1,0:T(8,128)(2,1)} %get-tuple-element.103), channel_id=1, source_target_pairs={{0,16},{16,0},{1,17},{17,1},{2,18},{18,2},{3,19},{19,3},{4,20},{20... | collective-permute-start | bytes 1572872 | tf_op jit(solution)/shard_map/ppermute | solution.py:24
  66.3 15.5 %collective-permute-start.16 = (bf16[2,512,256]{2,1,0:T(8,128)(2,1)}, bf16[2,512,256]{2,1,0:T(8,128)(2,1)}, u32[]{:S(2)}, u32[]{:S(2)}) collective-permute-start(bf16[2,512,256]{2,1,0:T(8,128)(2,1)} %get-tuple-element.136), channel_id=1, source_target_pairs={{0,1},{1,2},{2,3},{3,0},{4,5},{5,6},{6,7},{7,4},{8,9},{9,10},{10,1... | collective-permute-start | bytes 1572872 | tf_op jit(solution)/shard_map/ppermute | solution.py:24
  69.5 15.5 %copy-start.2 = (bf16[2,512,256]{2,1,0:T(8,128)(2,1)S(1)}, bf16[2,512,256]{2,1,0:T(8,128)(2,1)}, u32[]{:S(2)}) copy-start(bf16[2,512,256]{2,1,0:T(8,128)(2,1)} %get-tuple-element.149.refs_3_) | copy-start | bytes 1572868
  81.8 8.8 %collective-permute-start.17 = (bf16[4,1024,512]{2,1,0:T(8,128)(2,1)}, bf16[4,1024,512]{2,1,0:T(8,128)(2,1)}, u32[]{:S(2)}, u32[]{:S(2)}) collective-permute-start(bf16[4,1024,512]{2,1,0:T(8,128)(2,1)} %get-tuple-element.137.weight_ref), channel_id=1, source_target_pairs={{0,4},{4,0},{1,5},{5,1},{2,6},{6,2},{3,7},{7,3},{8,12},{12,8},{9,1... | collective-permute-start | bytes 12582920 | tf_op jit(solution)/shard_map/ppermute | solution.py:24
  83.0 20.0 %collective-permute-start.18 = (bf16[2,512,256]{2,1,0:T(8,128)(2,1)S(1)}, bf16[2,512,256]{2,1,0:T(8,128)(2,1)}, u32[]{:S(2)}, u32[]{:S(2)}) collective-permute-start(bf16[2,512,256]{2,1,0:T(8,128)(2,1)S(1)} %add_convert_fusion), channel_id=1, source_target_pairs={{0,16},{16,0},{1,17},{17,1},{2,18},{18,2},{3,19},{19,3},{4,20},{20... | collective-permute-start | bytes 1572872 | tf_op jit(solution)/shard_map/ppermute | solution.py:24
  84.6 18.4 %collective-permute-start.19 = (bf16[2,512,256]{2,1,0:T(8,128)(2,1)}, bf16[2,512,256]{2,1,0:T(8,128)(2,1)}, u32[]{:S(2)}, u32[]{:S(2)}) collective-permute-start(bf16[2,512,256]{2,1,0:T(8,128)(2,1)} %get-tuple-element.146), channel_id=1, source_target_pairs={{0,1},{1,2},{2,3},{3,0},{4,5},{5,6},{6,7},{7,4},{8,9},{9,10},{10,1... | collective-permute-start | bytes 1572872 | tf_op jit(solution)/shard_map/ppermute | solution.py:24
  86.7 18.1 %copy-start.1 = (bf16[2,512,256]{2,1,0:T(8,128)(2,1)S(1)}, bf16[2,512,256]{2,1,0:T(8,128)(2,1)}, u32[]{:S(2)}) copy-start(bf16[2,512,256]{2,1,0:T(8,128)(2,1)} %get-tuple-element.147.refs_0_) | copy-start | bytes 1572868
  86.7 18.1 %copy-start.3 = (bf16[2,512,256]{2,1,0:T(8,128)(2,1)S(1)}, bf16[2,512,256]{2,1,0:T(8,128)(2,1)}, u32[]{:S(2)}) copy-start(bf16[2,512,256]{2,1,0:T(8,128)(2,1)} %get-tuple-element.149.refs_3_) | copy-start | bytes 1572868
  86.7 11.5 %collective-permute-start.21 = (bf16[512,256]{1,0:T(8,128)(2,1)}, bf16[512,256]{1,0:T(8,128)(2,1)S(1)}, u32[]{:S(2)}, u32[]{:S(2)}) collective-permute-start(bf16[512,256]{1,0:T(8,128)(2,1)} %fusion.4), channel_id=1, source_target_pairs={{0,8},{8,0},{1,9},{9,1},{2,10},{10,2},{3,11},{11,3},{4,12},{12,4},... | collective-permute-start | bytes 786440 | tf_op jit(solution)/shard_map/ppermute | solution.py:24
  89.0 14.0 %collective-permute-start.20 = (bf16[512,256]{1,0:T(8,128)(2,1)}, bf16[512,256]{1,0:T(8,128)(2,1)S(1)}, u32[]{:S(2)}, u32[]{:S(2)}) collective-permute-start(bf16[512,256]{1,0:T(8,128)(2,1)} %fusion.3), channel_id=1, source_target_pairs={{0,16},{16,0},{1,17},{17,1},{2,18},{18,2},{3,19},{19,3},{4,20},{20... | collective-permute-start | bytes 786440 | tf_op jit(solution)/shard_map/ppermute | solution.py:24
  104.2 12.5 %collective-permute-start.24 = (bf16[512,256]{1,0:T(8,128)(2,1)S(1)}, bf16[512,256]{1,0:T(8,128)(2,1)S(1)}, u32[]{:S(2)}, u32[]{:S(2)}) collective-permute-start(bf16[512,256]{1,0:T(8,128)(2,1)S(1)} %fusion.5), channel_id=1, source_target_pairs={{0,8},{8,0},{1,9},{9,1},{2,10},{10,2},{3,11},{11,3},{4,12},{12,4},... | collective-permute-start | bytes 786440 | tf_op jit(solution)/shard_map/ppermute | solution.py:24
  106.1 17.6 %collective-permute-start.22 = (bf16[512,256]{1,0:T(8,128)(2,1)S(1)}, bf16[512,256]{1,0:T(8,128)(2,1)S(1)}, u32[]{:S(2)}, u32[]{:S(2)}) collective-permute-start(bf16[512,256]{1,0:T(8,128)(2,1)S(1)} %get-tuple-element.156), channel_id=1, source_target_pairs={{0,3},{1,0},{2,1},{3,2},{4,7},{5,4},{6,5},{7,6},{8,11},{9,8},{10,9... | collective-permute-start | bytes 786440 | tf_op jit(solution)/shard_map/ppermute | solution.py:24
  107.2 18.7 %collective-permute-start.23 = (bf16[512,256]{1,0:T(8,128)(2,1)S(1)}, bf16[512,256]{1,0:T(8,128)(2,1)S(1)}, u32[]{:S(2)}, u32[]{:S(2)}) collective-permute-start(bf16[512,256]{1,0:T(8,128)(2,1)S(1)} %get-tuple-element.157), channel_id=1, source_target_pairs={{0,2},{1,3},{2,0},{3,1},{4,6},{5,7},{6,4},{7,5},{8,10},{9,11},{10,... | collective-permute-start | bytes 786440 | tf_op jit(solution)/shard_map/ppermute | solution.py:24
  116.8 10.4 %copy-start.12 = (bf16[256]{0:T(256)(128)(2,1)S(1)}, bf16[256]{0:T(256)(128)(2,1)}, u32[]{:S(2)}) copy-start(bf16[256]{0:T(256)(128)(2,1)} %param.11) | copy-start | bytes 1540
  116.8 10.4 %copy-start.10 = (bf16[256,512]{1,0:T(8,128)(2,1)S(1)}, bf16[256,512]{1,0:T(8,128)(2,1)}, u32[]{:S(2)}) copy-start(bf16[256,512]{1,0:T(8,128)(2,1)} %param.12) | copy-start | bytes 786436
  (6 other events, 25.2 us)

commit v16 on v15

--- a/solution.py
+++ b/solution.py
@@ -538,11 +538,15 @@
         (got[0], sides[1:], total, own_weight, beyond)
     )
     if in_place:
-        beyond, passed_near = lax.optimization_barrier((beyond, passed_near))
+        sent = [
+            widen([keep[1], parts[0][1]]).astype(BF16) for (_, keep), parts in zip(sides[0], got[0])
+        ]
+        sent, beyond, passed_near = lax.optimization_barrier((sent, beyond, passed_near))
+        later = [[[swap(x, axis, 1)] for x, axis in zip(sent, ("outer", "inner"))]]
         passed_near = swap(passed_near, "tp", 1)
-        crossed = swap(widen([kept[2:], beyond]).astype(BF16), "outer", 1)
+    else:
+        later = [second_round(sides[0], got[0])]
     other_weight = swap(own_weight, "core", 1)
-    later = [second_round(sides[0], got[0])]
     got += [first_round(side) for side in sides[1:]]
     if in_place:
         value_proj, coefficient = weight_call(
@@ -565,24 +569,23 @@
         coefficient = inv_rms * inv_rms * share * (1.0 / width)
     later[0], coefficient = lax.optimization_barrier((later[0], coefficient))
     if in_place:
-        crossed, passed_near, coefficient = lax.optimization_barrier(
-            (crossed, passed_near, coefficient)
-        )
-        beside = swap(widen([kept[1], passed_near[1], crossed[1]]).astype(BF16), "inner", 1)
         groups = [[keep] + parts + then for (_, keep), parts, then in zip(sides[0], got[0], later[0])]
-        last = [swap(x, "tp", k) for x, k in zip(sums_of(groups, 0), pairs[0])]
+        sent = sums_of(groups, 0)
+        last = [swap(x, "tp", k) for x, k in zip(sent, pairs[0])]
+        coefficient, beyond, _ = lax.optimization_barrier((coefficient, beyond, sent))
+        crossed = swap(widen([kept[2:], beyond]).astype(BF16), "outer", 1)
         grad_shape = jax.ShapeDtypeStruct((rows_here, width), BF16)
         resid_grad = weight_call(
             grad_kernel, places[0], residual, in_hbm(own_weight), [cot, coefficient], grad_shape
         )
-        beside, resid_grad = lax.optimization_barrier((beside, resid_grad))
+        crossed, passed_near, resid_grad = lax.optimization_barrier(
+            (crossed, passed_near, resid_grad)
+        )
+        beside = swap(widen([kept[1], passed_near[1], crossed[1]]).astype(BF16), "inner", 1)
         resid_grad = weight_call(
-            grad_kernel, places[1][:3], residual, other_weight, [cot, coefficient], grad_shape, resid_grad
+            grad_kernel, places[1], residual, other_weight, [cot, coefficient], grad_shape, resid_grad
         )
-        last, resid_grad = lax.optimization_barrier((last, resid_grad))
-        resid_grad = weight_call(
-            grad_kernel, places[1][3:], residual, other_weight, [cot, coefficient], grad_shape, resid_grad
-        )
+        last, beside, resid_grad = lax.optimization_barrier((last, beside, resid_grad))
         grad_rows = widen([kept[0], passed_near[0], crossed[0], beside] + last)
     else:
         normed_grad = lax.dot_general(

time: 133 us -> 125 us (0.940)
  other arithmetic: 21 us -> 16.5 us
  Pallas kernels: 51.4 us -> 49 us
    pallas_call x4 -> x3, Pallas kernels: 25.5 us -> 23.1 us  [weight_call(): pl.pallas_call(kernel, out_shape=out_shape, grid_spec=pltpu.PrefetchScala...]
    convert_element_type x2 -> x1, other arithmetic: 3.43 us -> 1.18 us  [per_device(): widen([keep[1], parts[0][1]]).astype(BF16)]
    unnamed x27 -> x25, local copies, waits for them, and re-layouts: 3.99 us -> 3.91 us
  transfers between devices with their start and end apart: 25 -> 25, of which waited for: 10 -> 10; matrix products, arithmetic and copies ran while one was open for 14% -> 13% of each run, Pallas kernels for 36% -> 39%
where the time goes in v16:
time: 125 us; the launch traced here: 124 us
  Pallas kernels  49 us (39%)
  starting transfers between devices  28.9 us (23%)
  waiting for transfers between devices  23.2 us (19%)
  other arithmetic  16.5 us (13%)
  local copies, waits for them, and re-layouts  5.6 us (4%)
    ppermute x23, starting transfers between devices, swap(): lax.ppermute(value, axis, [(place, (place + step) % size) for place in ra...  23.3 us
    ppermute x23, waiting for transfers between devices, swap(): lax.ppermute(value, axis, [(place, (place + step) % size) for place in ra...  23.1 us
    pallas_call x3, Pallas kernels, weight_call(): pl.pallas_call(kernel, out_shape=out_shape, grid_spec=pltpu.PrefetchScala...  23.1 us
    pallas_call x2, Pallas kernels, grad_product(): pl.pallas_call(kernel, out_shape=out_shape, grid_spec=pltpu.PrefetchScala...  14.8 us
    pallas_call x1, Pallas kernels, first_value(): pl.pallas_call(functools.partial(value_kernel, inner_flags), out_shape=[t...  7.77 us
    ppermute x2, starting transfers between devices, trade(): lax.ppermute(value, axis, [(place, place ^ mask) for place in range(size)])  5.67 us
    reduce_sum x1, other arithmetic, per_device(): squares = jnp.sum(resid_wide * resid_wide, axis=1, keepdims=True)  5.1 us
    unnamed x25, local copies, waits for them, and re-layouts  3.91 us
  transfers between devices with their start and end apart: 25, of which 10 were waited for; matrix products, arithmetic and copies ran while one was open for 13% of the time, Pallas kernels for 39%

profile of v16, /device:TPU:0, one launch (start us, length us, event | category | flops | bytes accessed | tf_op | source)
XLA Modules:
  0.0 124.0 jit_solution(7296041435601890419)
XLA Ops:
  2.1 3.0 %collective-permute-start = (f32[1,52,128]{2,1,0:T(8,128)S(1)}, f32[1,52,128]{2,1,0:T(8,128)S(1)}, u32[]{:S(2)}, u32[]{:S(2)}) collective-permute-start(f32[1,52,128]{2,1,0:T(8,128)S(1)} %maximum_bitcast_fusion), channel_id=1, source_target_pairs={{0,1},{1,0},{2,3},{3,2},{4,5},{5,4},{6,7},{7,6},{8,9},{9,8},{10,11... | collective-permute-start | bytes 79880 | tf_op jit(solution)/shard_map/ppermute | solution.py:29
  5.8 1.8 %multiply_convert_fusion = bf16[256,512]{1,0:T(8,128)(2,1)} fusion(bf16[256,512]{1,0:T(8,128)(2,1)} %param.12, f32[256]{0:T(256)S(1)} %convert_element_type.93), kind=kLoop, calls=%fused_computation.15 | loop fusion | flops 393216 | bytes 525312 | tf_op jit(solution)/shard_map/convert_element_type | solution.py:401
  7.5 1.2 dynamic_slice.4
  8.8 1.6 %collective-permute-start.2 = (bf16[256,512]{1,0:T(8,128)(2,1)}, bf16[256,512]{1,0:T(8,128)(2,1)S(1)}, u32[]{:S(2)}, u32[]{:S(2)}) collective-permute-start(bf16[256,512]{1,0:T(8,128)(2,1)} %multiply_convert_fusion), channel_id=1, source_target_pairs={{0,8},{8,0},{1,9},{9,1},{2,10},{10,2},{3,11},{11,3},{4,12},{12,4},... | collective-permute-start | bytes 786440 | tf_op jit(solution)/shard_map/ppermute | solution.py:24
  10.8 5.1 %multiply_reduce_fusion = f32[512]{0:T(512)S(1)} fusion(bf16[512,8192]{1,0:T(8,128)(2,1)} %resid_ref.3), kind=kLoop, calls=%fused_computation | loop fusion | flops 12582400 | bytes 8390656 | tf_op jit(solution)/shard_map/reduce_sum | solution.py:404
  15.9 2.6 %collective-permute-start.5 = (f32[2,52,128]{2,1,0:T(8,128)S(1)}, f32[2,52,128]{2,1,0:T(8,128)S(1)}, u32[]{:S(2)}, u32[]{:S(2)}) collective-permute-start(f32[2,52,128]{2,1,0:T(8,128)S(1)} %pad_maximum_fusion.5), channel_id=1, source_target_pairs={{0,2},{1,3},{2,0},{3,1},{4,6},{5,7},{6,4},{7,5},{8,10},{9,11},{10,... | collective-permute-start | bytes 159752 | tf_op jit(solution)/shard_map/ppermute | solution.py:29
  18.6 1.4 %collective-permute-done.1 = bf16[256,512]{1,0:T(8,128)(2,1)S(1)} collective-permute-done((bf16[256,512]{1,0:T(8,128)(2,1)}, bf16[256,512]{1,0:T(8,128)(2,1)S(1)}, u32[]{:S(2)}, u32[]{:S(2)}) %collective-permute-start.1) | collective-permute-done | bytes 262176 | tf_op jit(solution)/shard_map/ppermute | solution.py:24
  21.0 1.5 %collective-permute-start.3 = (bf16[256,512]{1,0:T(8,128)(2,1)S(1)}, bf16[256,512]{1,0:T(8,128)(2,1)S(1)}, u32[]{:S(2)}, u32[]{:S(2)}) collective-permute-start(bf16[256,512]{1,0:T(8,128)(2,1)S(1)} %collective-permute-done.1), channel_id=1, source_target_pairs={{0,16},{16,0},{1,17},{17,1},{2,18},{18,2},{3,19},{19,3},{4,20},{20... | collective-permute-start | bytes 786440 | tf_op jit(solution)/shard_map/ppermute | solution.py:24
  24.9 2.2 %collective-permute-done.4 = bf16[256,512]{1,0:T(8,128)(2,1)} collective-permute-done((bf16[256,512]{1,0:T(8,128)(2,1)}, bf16[256,512]{1,0:T(8,128)(2,1)}, u32[]{:S(2)}, u32[]{:S(2)}) %collective-permute-start.4) | collective-permute-done | bytes 262176 | tf_op jit(solution)/shard_map/ppermute | solution.py:24
  27.1 3.1 %collective-permute-done.3 = bf16[256,512]{1,0:T(8,128)(2,1)S(1)} collective-permute-done((bf16[256,512]{1,0:T(8,128)(2,1)S(1)}, bf16[256,512]{1,0:T(8,128)(2,1)S(1)}, u32[]{:S(2)}, u32[]{:S(2)}) %collective-permute-start.3) | collective-permute-done | bytes 262176 | tf_op jit(solution)/shard_map/ppermute | solution.py:24
  31.5 1.6 %collective-permute-start.9 = (bf16[256,512]{1,0:T(8,128)(2,1)}, bf16[256,512]{1,0:T(8,128)(2,1)}, u32[]{:S(2)}, u32[]{:S(2)}) collective-permute-start(bf16[256,512]{1,0:T(8,128)(2,1)} %collective-permute-done.4), channel_id=1, source_target_pairs={{0,16},{16,0},{1,17},{17,1},{2,18},{18,2},{3,19},{19,3},{4,20},{20... | collective-permute-start | bytes 786440 | tf_op jit(solution)/shard_map/ppermute | solution.py:24
  33.1 2.1 %shard_map.129 = (bf16[512,512]{1,0:T(8,128)(2,1)S(1)}, bf16[512,512]{1,0:T(8,128)(2,1)S(1)}, f32[512,1]{1,0:T(8,128)S(1)}) custom-call(s32[2]{0:T(128)S(1)} %pad_add_fusion.1.info_ref, f32[4,52,128]{2,1,0:T(8,128)S(1)} %pad_maximum_fusion.4.shares_ref, f32[512,1]{1,0:T(8,128)S(1)} %copy.17.squares_ref, bf16[512,512]{1,0:T(8,128)(2,1)} %value_cot_ref.1), custom_call_target="tpu_custom_call" | custom-call | flops 1024 | bytes 1024 | tf_op jit(solution)/shard_map/pallas_call | solution.py:350
  35.2 6.6 %shard_map.130 = bf16[4,4,512,256]{3,2,1,0:T(8,128)(2,1)} custom-call(s32[16]{0:T(128)S(1)} %stack.230.places_ref, bf16[512,512]{1,0:T(8,128)(2,1)S(1)} %get-tuple-element.97.cot_ref, bf16[512,8192]{1,0:T(8,128)(2,1)} %resid_ref.3, bf16[512,8192]{1,0:T(8,128)(2,1)} %resid_ref.3, bf16[512,8192]{1,0:T(8,128)(2,1)} %resid_ref.3, bf16[512,8192]{1,0:T(8,128)(2,1)} %resid_ref.3), custom_call_target="tpu_custom_call" | custom-call | flops 1024 | bytes 1024 | tf_op jit(solution)/shard_map/pallas_call | solution.py:128
  41.8 1.6 %collective-permute-start.10 = (bf16[256,512]{1,0:T(8,128)(2,1)}, bf16[256,512]{1,0:T(8,128)(2,1)}, u32[]{:S(2)}, u32[]{:S(2)}) collective-permute-start(bf16[256,512]{1,0:T(8,128)(2,1)} %collective-permute-done.6), channel_id=1, source_target_pairs={{0,8},{8,0},{1,9},{9,1},{2,10},{10,2},{3,11},{11,3},{4,12},{12,4},... | collective-permute-start | bytes 786440 | tf_op jit(solution)/shard_map/ppermute | solution.py:24
  44.6 3.9 %collective-permute-done.10 = bf16[256,512]{1,0:T(8,128)(2,1)} collective-permute-done((bf16[256,512]{1,0:T(8,128)(2,1)}, bf16[256,512]{1,0:T(8,128)(2,1)}, u32[]{:S(2)}, u32[]{:S(2)}) %collective-permute-start.10) | collective-permute-done | bytes 262176 | tf_op jit(solution)/shard_map/ppermute | solution.py:24
  51.3 1.6 %collective-permute-start.14 = (bf16[2,256,512]{2,1,0:T(8,128)(2,1)S(1)}, bf16[2,256,512]{2,1,0:T(8,128)(2,1)}, u32[]{:S(2)}, u32[]{:S(2)}) collective-permute-start(bf16[2,256,512]{2,1,0:T(8,128)(2,1)S(1)} %pad_maximum_fusion.2.rest_4_), channel_id=1, source_target_pairs={{0,8},{8,0},{1,9},{9,1},{2,10},{10,2},{3,11},{11,3},{4,12},{12,4},... | collective-permute-start | bytes 1572872 | tf_op jit(solution)/shard_map/ppermute | solution.py:24
  52.9 3.1 %collective-permute-done.11.rest_4_ = bf16[4,4,512,256]{3,2,1,0:T(8,128)(2,1)} collective-permute-done((bf16[4,4,512,256]{3,2,1,0:T(8,128)(2,1)}, bf16[4,4,512,256]{3,2,1,0:T(8,128)(2,1)}, u32[]{:S(2)}, u32[]{:S(2)}) %collective-permute-start.11) | collective-permute-done | bytes 4194336 | tf_op jit(solution)/shard_map/ppermute | solution.py:24
  56.1 8.2 %shard_map.131 = (bf16[2,512,256]{2,1,0:T(8,128)(2,1)}, bf16[2,512,256]{2,1,0:T(8,128)(2,1)}, bf16[2,512,256]{2,1,0:T(8,128)(2,1)}, bf16[2,512,256]{2,1,0:T(8,12...) custom-call(s32[16]{0:T(128)S(1)} %stack.211.places_ref, ...), custom_call_target="tpu_custom_call" | custom-call | flops 1024 | bytes 1024 | tf_op jit(solution)/shard_map/pallas_call | solution.py:128
  64.3 1.6 %collective-permute-start.12 = (bf16[2,512,256]{2,1,0:T(8,128)(2,1)}, bf16[2,512,256]{2,1,0:T(8,128)(2,1)}, u32[]{:S(2)}, u32[]{:S(2)}) collective-permute-start(bf16[2,512,256]{2,1,0:T(8,128)(2,1)} %get-tuple-element.105), channel_id=1, source_target_pairs={{0,8},{8,0},{1,9},{9,1},{2,10},{10,2},{3,11},{11,3},{4,12},{12,4},... | collective-permute-start | bytes 1572872 | tf_op jit(solution)/shard_map/ppermute | solution.py:24
  66.3 3.2 %collective-permute-start.16 = (bf16[2,512,256]{2,1,0:T(8,128)(2,1)}, bf16[2,512,256]{2,1,0:T(8,128)(2,1)}, u32[]{:S(2)}, u32[]{:S(2)}) collective-permute-start(bf16[2,512,256]{2,1,0:T(8,128)(2,1)} %get-tuple-element.139), channel_id=1, source_target_pairs={{0,1},{1,2},{2,3},{3,0},{4,5},{5,6},{6,7},{7,4},{8,9},{9,10},{10,1... | collective-permute-start | bytes 1572872 | tf_op jit(solution)/shard_map/ppermute | solution.py:24
  71.8 7.8 %shard_map.132 = (f32[512,512]{1,0:T(8,128)}, bf16[4,1024,512]{2,1,0:T(8,128)(2,1)}) custom-call(s32[4]{0:T(128)S(1)} %pad_add_fusion.2.places_ref, s32[4]{0:T(128)S(1)} %pad_add_fusion.3.offsets_ref, bf16[512,8192]{1,0:T(8,128)(2,1)} %resid_ref.3, bf16[2,256,512]{2,1,0:T(8,128)(2,1)S(1)} %pad_maximum_fusion.rest_0_, bf16[2,256,512]{2,1,0:T(8,128)(2,1)S(1)} %copy-done.4, ...), custom_call_target="tpu_custom_call" | custom-call | flops 1024 | bytes 1024 | tf_op jit(solution)/shard_map/pallas_call | solution.py:250
  79.9 2.0 %collective-permute-done.16 = bf16[2,512,256]{2,1,0:T(8,128)(2,1)} collective-permute-done((bf16[2,512,256]{2,1,0:T(8,128)(2,1)}, bf16[2,512,256]{2,1,0:T(8,128)(2,1)}, u32[]{:S(2)}, u32[]{:S(2)}) %collective-permute-start.16) | collective-permute-done | bytes 524320 | tf_op jit(solution)/shard_map/ppermute | solution.py:24
  81.9 1.2 fusion.3
  83.0 1.6 %collective-permute-start.18 = (bf16[512,256]{1,0:T(8,128)(2,1)S(1)}, bf16[512,256]{1,0:T(8,128)(2,1)S(1)}, u32[]{:S(2)}, u32[]{:S(2)}) collective-permute-start(bf16[512,256]{1,0:T(8,128)(2,1)S(1)} %get-tuple-element.151), channel_id=1, source_target_pairs={{0,16},{16,0},{1,17},{17,1},{2,18},{18,2},{3,19},{19,3},{4,20},{20... | collective-permute-start | bytes 786440 | tf_op jit(solution)/shard_map/ppermute | solution.py:24
  85.7 3.7 %collective-permute-done.17.weight_ref = bf16[4,1024,512]{2,1,0:T(8,128)(2,1)} collective-permute-done((bf16[4,1024,512]{2,1,0:T(8,128)(2,1)}, bf16[4,1024,512]{2,1,0:T(8,128)(2,1)}, u32[]{:S(2)}, u32[]{:S(2)}) %collective-permute-start.17) | collective-permute-done | bytes 4194336 | tf_op jit(solution)/shard_map/ppermute | solution.py:24
  89.4 7.7 %shard_map.133 = (bf16[512,512]{1,0:T(8,128)(2,1)}, f32[512,1]{1,0:T(8,128)S(1)}) custom-call(s32[4]{0:T(128)S(1)} %pad_add_fusion.places_ref, bf16[512,8192]{1,0:T(8,128)(2,1)} %resid_ref.3, bf16[4,1024,512]{2,1,0:T(8,128)(2,1)} %collective-permute-done.17.weight_ref, f32[512,512]{1,0:T(8,128)} %get-tuple-element.141.first_ref, ...), custom_call_target="tpu_custom_call" | custom-call | flops 1024 | bytes 1024 | tf_op jit(solution)/shard_map/pallas_call | solution.py:288
  97.1 1.2 shard_map.134
  98.3 1.2 add_convert_fusion
  99.5 1.6 %collective-permute-start.22 = (bf16[2,512,256]{2,1,0:T(8,128)(2,1)S(1)}, bf16[2,512,256]{2,1,0:T(8,128)(2,1)S(1)}, u32[]{:S(2)}, u32[]{:S(2)}) collective-permute-start(bf16[2,512,256]{2,1,0:T(8,128)(2,1)S(1)} %add_convert_fusion), channel_id=1, source_target_pairs={{0,16},{16,0},{1,17},{17,1},{2,18},{18,2},{3,19},{19,3},{4,20},{20... | collective-permute-start | bytes 1572872 | tf_op jit(solution)/shard_map/ppermute | solution.py:24
  103.0 7.7 %shard_map.135.rest_0_ = bf16[512,8192]{1,0:T(8,128)(2,1)} custom-call(s32[4]{0:T(128)S(1)} %pad_add_fusion.2.places_ref, bf16[512,8192]{1,0:T(8,128)(2,1)} %resid_ref.3, bf16[4,1024,512]{2,1,0:T(8,128)(2,1)} %get-tuple-element.140.weight_ref, bf16[512,512]{1,0:T(8,128)(2,1)S(1)} %get-tuple-element.142.cot_ref, f32[512,1]{1,0:T(8,128)S(1)} %get-tuple-element.163.coef_ref), custom_call_target="tpu_custom_call" | custom-call | flops 1024 | bytes 1024 | tf_op jit(solution)/shard_map/pallas_call | solution.py:288
  110.6 2.9 %collective-permute-done.22 = bf16[2,512,256]{2,1,0:T(8,128)(2,1)S(1)} collective-permute-done((bf16[2,512,256]{2,1,0:T(8,128)(2,1)S(1)}, bf16[2,512,256]{2,1,0:T(8,128)(2,1)S(1)}, u32[]{:S(2)}, u32[]{:S(2)}) %collective-permute-start.22) | collective-permute-done | bytes 524320 | tf_op jit(solution)/shard_map/ppermute | solution.py:24
  114.2 7.7 %shard_map.136 = bf16[512,8192]{1,0:T(8,128)(2,1)} custom-call(s32[4]{0:T(128)S(1)} %pad_add_fusion.places_ref, bf16[512,8192]{1,0:T(8,128)(2,1)} %resid_ref.3, bf16[4,1024,512]{2,1,0:T(8,128)(2,1)} %collective-permute-done.17.weight_ref, bf16[512,512]{1,0:T(8,128)(2,1)S(1)} %get-tuple-element.142.cot_ref, ...), custom_call_target="tpu_custom_call", output_to_operand_aliasing={{}: (5, {})} | custom-call | flops 1024 | bytes 1024 | tf_op jit(solution)/shard_map/pallas_call | solution.py:288
  (77 shorter events, 19.9 us)
Async XLA Ops:
  2.1 6.7 %collective-permute-start = (f32[1,52,128]{2,1,0:T(8,128)S(1)}, f32[1,52,128]{2,1,0:T(8,128)S(1)}, u32[]{:S(2)}, u32[]{:S(2)}) collective-permute-start(f32[1,52,128]{2,1,0:T(8,128)S(1)} %maximum_bitcast_fusion), channel_id=1, source_target_pairs={{0,1},{1,0},{2,3},{3,2},{4,5},{5,4},{6,7},{7,6},{8,9},{9,8},{10,11... | collective-permute-start | bytes 79880 | tf_op jit(solution)/shard_map/ppermute | solution.py:29
  8.8 9.8 %collective-permute-start.2 = (bf16[256,512]{1,0:T(8,128)(2,1)}, bf16[256,512]{1,0:T(8,128)(2,1)S(1)}, u32[]{:S(2)}, u32[]{:S(2)}) collective-permute-start(bf16[256,512]{1,0:T(8,128)(2,1)} %multiply_convert_fusion), channel_id=1, source_target_pairs={{0,8},{8,0},{1,9},{9,1},{2,10},{10,2},{3,11},{11,3},{4,12},{12,4},... | collective-permute-start | bytes 786440 | tf_op jit(solution)/shard_map/ppermute | solution.py:24
  10.4 9.6 %collective-permute-start.1 = (bf16[256,512]{1,0:T(8,128)(2,1)}, bf16[256,512]{1,0:T(8,128)(2,1)S(1)}, u32[]{:S(2)}, u32[]{:S(2)}) collective-permute-start(bf16[256,512]{1,0:T(8,128)(2,1)} %multiply_convert_fusion), channel_id=1, source_target_pairs={{0,1},{1,2},{2,3},{3,0},{4,5},{5,6},{6,7},{7,4},{8,9},{9,10},{10,1... | collective-permute-start | bytes 786440 | tf_op jit(solution)/shard_map/ppermute | solution.py:24
  15.9 7.4 %collective-permute-start.5 = (f32[2,52,128]{2,1,0:T(8,128)S(1)}, f32[2,52,128]{2,1,0:T(8,128)S(1)}, u32[]{:S(2)}, u32[]{:S(2)}) collective-permute-start(f32[2,52,128]{2,1,0:T(8,128)S(1)} %pad_maximum_fusion.5), channel_id=1, source_target_pairs={{0,2},{1,3},{2,0},{3,1},{4,6},{5,7},{6,4},{7,5},{8,10},{9,11},{10,... | collective-permute-start | bytes 159752 | tf_op jit(solution)/shard_map/ppermute | solution.py:29
  19.9 7.2 %collective-permute-start.4 = (bf16[256,512]{1,0:T(8,128)(2,1)}, bf16[256,512]{1,0:T(8,128)(2,1)}, u32[]{:S(2)}, u32[]{:S(2)}) collective-permute-start(bf16[256,512]{1,0:T(8,128)(2,1)} %multiply_convert_fusion), channel_id=1, source_target_pairs={{0,3},{1,0},{2,1},{3,2},{4,7},{5,4},{6,5},{7,6},{8,11},{9,8},{10,9... | collective-permute-start | bytes 786440 | tf_op jit(solution)/shard_map/ppermute | solution.py:24
  21.0 9.2 %collective-permute-start.3 = (bf16[256,512]{1,0:T(8,128)(2,1)S(1)}, bf16[256,512]{1,0:T(8,128)(2,1)S(1)}, u32[]{:S(2)}, u32[]{:S(2)}) collective-permute-start(bf16[256,512]{1,0:T(8,128)(2,1)S(1)} %collective-permute-done.1), channel_id=1, source_target_pairs={{0,16},{16,0},{1,17},{17,1},{2,18},{18,2},{3,19},{19,3},{4,20},{20... | collective-permute-start | bytes 786440 | tf_op jit(solution)/shard_map/ppermute | solution.py:24
  24.3 19.1 %collective-permute-start.7 = (bf16[2,256,512]{2,1,0:T(8,128)(2,1)S(1)}, bf16[2,256,512]{2,1,0:T(8,128)(2,1)S(1)}, u32[]{:S(2)}, u32[]{:S(2)}) collective-permute-start(bf16[2,256,512]{2,1,0:T(8,128)(2,1)S(1)} %pad_maximum_fusion.rest_0_), channel_id=1, source_target_pairs={{0,16},{16,0},{1,17},{17,1},{2,18},{18,2},{3,19},{19,3},{4,20},{20... | collective-permute-start | bytes 1572872 | tf_op jit(solution)/shard_map/ppermute | solution.py:24
  30.2 11.6 %collective-permute-start.6 = (bf16[256,512]{1,0:T(8,128)(2,1)}, bf16[256,512]{1,0:T(8,128)(2,1)}, u32[]{:S(2)}, u32[]{:S(2)}) collective-permute-start(bf16[256,512]{1,0:T(8,128)(2,1)} %multiply_convert_fusion), channel_id=1, source_target_pairs={{0,2},{1,3},{2,0},{3,1},{4,6},{5,7},{6,4},{7,5},{8,10},{9,11},{10,... | collective-permute-start | bytes 786440 | tf_op jit(solution)/shard_map/ppermute | solution.py:24
  30.6 14.0 %collective-permute-start.8 = (bf16[2,256,512]{2,1,0:T(8,128)(2,1)S(1)}, bf16[2,256,512]{2,1,0:T(8,128)(2,1)S(1)}, u32[]{:S(2)}, u32[]{:S(2)}) collective-permute-start(bf16[2,256,512]{2,1,0:T(8,128)(2,1)S(1)} %pad_maximum_fusion.1.rest_2_), channel_id=1, source_target_pairs={{0,8},{8,0},{1,9},{9,1},{2,10},{10,2},{3,11},{11,3},{4,12},{12,4},... | collective-permute-start | bytes 1572872 | tf_op jit(solution)/shard_map/ppermute | solution.py:24
  31.5 13.2 %collective-permute-start.9 = (bf16[256,512]{1,0:T(8,128)(2,1)}, bf16[256,512]{1,0:T(8,128)(2,1)}, u32[]{:S(2)}, u32[]{:S(2)}) collective-permute-start(bf16[256,512]{1,0:T(8,128)(2,1)} %collective-permute-done.4), channel_id=1, source_target_pairs={{0,16},{16,0},{1,17},{17,1},{2,18},{18,2},{3,19},{19,3},{4,20},{20... | collective-permute-start | bytes 786440 | tf_op jit(solution)/shard_map/ppermute | solution.py:24
  41.8 6.8 %collective-permute-start.10 = (bf16[256,512]{1,0:T(8,128)(2,1)}, bf16[256,512]{1,0:T(8,128)(2,1)}, u32[]{:S(2)}, u32[]{:S(2)}) collective-permute-start(bf16[256,512]{1,0:T(8,128)(2,1)} %collective-permute-done.6), channel_id=1, source_target_pairs={{0,8},{8,0},{1,9},{9,1},{2,10},{10,2},{3,11},{11,3},{4,12},{12,4},... | collective-permute-start | bytes 786440 | tf_op jit(solution)/shard_map/ppermute | solution.py:24
  48.6 7.5 %collective-permute-start.11 = (bf16[4,4,512,256]{3,2,1,0:T(8,128)(2,1)}, bf16[4,4,512,256]{3,2,1,0:T(8,128)(2,1)}, u32[]{:S(2)}, u32[]{:S(2)}) collective-permute-start(bf16[4,4,512,256]{3,2,1,0:T(8,128)(2,1)} %shard_map.130), channel_id=1, source_target_pairs={{0,4},{4,0},{1,5},{5,1},{2,6},{6,2},{3,7},{7,3},{8,12},{12,8},{9,1... | collective-permute-start | bytes 12582920 | tf_op jit(solution)/shard_map/ppermute | solution.py:24
  49.7 20.1 %collective-permute-start.15 = (bf16[2,256,512]{2,1,0:T(8,128)(2,1)S(1)}, bf16[2,256,512]{2,1,0:T(8,128)(2,1)}, u32[]{:S(2)}, u32[]{:S(2)}) collective-permute-start(bf16[2,256,512]{2,1,0:T(8,128)(2,1)S(1)} %pad_maximum_fusion.3.rest_6_), channel_id=1, source_target_pairs={{0,16},{16,0},{1,17},{17,1},{2,18},{18,2},{3,19},{19,3},{4,20},{20... | collective-permute-start | bytes 1572872 | tf_op jit(solution)/shard_map/ppermute | solution.py:24
  51.3 18.4 %collective-permute-start.14 = (bf16[2,256,512]{2,1,0:T(8,128)(2,1)S(1)}, bf16[2,256,512]{2,1,0:T(8,128)(2,1)}, u32[]{:S(2)}, u32[]{:S(2)}) collective-permute-start(bf16[2,256,512]{2,1,0:T(8,128)(2,1)S(1)} %pad_maximum_fusion.2.rest_4_), channel_id=1, source_target_pairs={{0,8},{8,0},{1,9},{9,1},{2,10},{10,2},{3,11},{11,3},{4,12},{12,4},... | collective-permute-start | bytes 1572872 | tf_op jit(solution)/shard_map/ppermute | solution.py:24
  56.1 33.3 %copy-start.8 = (f32[512,1]{1,0:T(8,128)S(1)}, f32[512,1]{1,0:T(8,128)}, u32[]{:S(2)}) copy-start(f32[512,1]{1,0:T(8,128)} %copy-done.7) | copy-start | bytes 6148
  64.3 17.6 %copy-start = (bf16[2,512,256]{2,1,0:T(8,128)(2,1)S(1)}, bf16[2,512,256]{2,1,0:T(8,128)(2,1)}, u32[]{:S(2)}) copy-start(bf16[2,512,256]{2,1,0:T(8,128)(2,1)} %get-tuple-element.145.refs_0_) | copy-start | bytes 1572868
  64.3 15.3 %collective-permute-start.12 = (bf16[2,512,256]{2,1,0:T(8,128)(2,1)}, bf16[2,512,256]{2,1,0:T(8,128)(2,1)}, u32[]{:S(2)}, u32[]{:S(2)}) collective-permute-start(bf16[2,512,256]{2,1,0:T(8,128)(2,1)} %get-tuple-element.105), channel_id=1, source_target_pairs={{0,8},{8,0},{1,9},{9,1},{2,10},{10,2},{3,11},{11,3},{4,12},{12,4},... | collective-permute-start | bytes 1572872 | tf_op jit(solution)/shard_map/ppermute | solution.py:24
  65.9 14.0 %collective-permute-start.13 = (bf16[2,512,256]{2,1,0:T(8,128)(2,1)}, bf16[2,512,256]{2,1,0:T(8,128)(2,1)}, u32[]{:S(2)}, u32[]{:S(2)}) collective-permute-start(bf16[2,512,256]{2,1,0:T(8,128)(2,1)} %get-tuple-element.106), channel_id=1, source_target_pairs={{0,16},{16,0},{1,17},{17,1},{2,18},{18,2},{3,19},{19,3},{4,20},{20... | collective-permute-start | bytes 1572872 | tf_op jit(solution)/shard_map/ppermute | solution.py:24
  66.3 15.5 %collective-permute-start.16 = (bf16[2,512,256]{2,1,0:T(8,128)(2,1)}, bf16[2,512,256]{2,1,0:T(8,128)(2,1)}, u32[]{:S(2)}, u32[]{:S(2)}) collective-permute-start(bf16[2,512,256]{2,1,0:T(8,128)(2,1)} %get-tuple-element.139), channel_id=1, source_target_pairs={{0,1},{1,2},{2,3},{3,0},{4,5},{5,6},{6,7},{7,4},{8,9},{9,10},{10,1... | collective-permute-start | bytes 1572872 | tf_op jit(solution)/shard_map/ppermute | solution.py:24
  69.6 12.3 %copy-start.1 = (bf16[2,512,256]{2,1,0:T(8,128)(2,1)S(1)}, bf16[2,512,256]{2,1,0:T(8,128)(2,1)}, u32[]{:S(2)}) copy-start(bf16[2,512,256]{2,1,0:T(8,128)(2,1)} %get-tuple-element.147.refs_3_) | copy-start | bytes 1572868
  79.6 17.5 %copy-start.2 = (bf16[2,512,256]{2,1,0:T(8,128)(2,1)S(1)}, bf16[2,512,256]{2,1,0:T(8,128)(2,1)}, u32[]{:S(2)}) copy-start(bf16[2,512,256]{2,1,0:T(8,128)(2,1)} %get-tuple-element.147.refs_3_) | copy-start | bytes 1572868
  81.9 7.5 %collective-permute-start.17 = (bf16[4,1024,512]{2,1,0:T(8,128)(2,1)}, bf16[4,1024,512]{2,1,0:T(8,128)(2,1)}, u32[]{:S(2)}, u32[]{:S(2)}) collective-permute-start(bf16[4,1024,512]{2,1,0:T(8,128)(2,1)} %get-tuple-element.140.weight_ref), channel_id=1, source_target_pairs={{0,4},{4,0},{1,5},{5,1},{2,6},{6,2},{3,7},{7,3},{8,12},{12,8},{9,1... | collective-permute-start | bytes 12582920 | tf_op jit(solution)/shard_map/ppermute | solution.py:24
  83.0 14.0 %collective-permute-start.18 = (bf16[512,256]{1,0:T(8,128)(2,1)S(1)}, bf16[512,256]{1,0:T(8,128)(2,1)S(1)}, u32[]{:S(2)}, u32[]{:S(2)}) collective-permute-start(bf16[512,256]{1,0:T(8,128)(2,1)S(1)} %get-tuple-element.151), channel_id=1, source_target_pairs={{0,16},{16,0},{1,17},{17,1},{2,18},{18,2},{3,19},{19,3},{4,20},{20... | collective-permute-start | bytes 786440 | tf_op jit(solution)/shard_map/ppermute | solution.py:24
  84.7 12.4 %collective-permute-start.19 = (bf16[512,256]{1,0:T(8,128)(2,1)S(1)}, bf16[512,256]{1,0:T(8,128)(2,1)S(1)}, u32[]{:S(2)}, u32[]{:S(2)}) collective-permute-start(bf16[512,256]{1,0:T(8,128)(2,1)S(1)} %get-tuple-element.152), channel_id=1, source_target_pairs={{0,8},{8,0},{1,9},{9,1},{2,10},{10,2},{3,11},{11,3},{4,12},{12,4},... | collective-permute-start | bytes 786440 | tf_op jit(solution)/shard_map/ppermute | solution.py:24
  85.3 25.4 %collective-permute-start.23 = (bf16[2,512,256]{2,1,0:T(8,128)(2,1)}, bf16[2,512,256]{2,1,0:T(8,128)(2,1)S(1)}, u32[]{:S(2)}, u32[]{:S(2)}) collective-permute-start(bf16[2,512,256]{2,1,0:T(8,128)(2,1)} %get-tuple-element.162), channel_id=1, source_target_pairs={{0,1},{1,2},{2,3},{3,0},{4,5},{5,6},{6,7},{7,4},{8,9},{9,10},{10,1... | collective-permute-start | bytes 1572872 | tf_op jit(solution)/shard_map/ppermute | solution.py:24
  89.4 8.9 %copy-start.10 = (bf16[4,512,256]{2,1,0:T(8,128)(2,1)S(1)}, bf16[4,512,256]{2,1,0:T(8,128)(2,1)}, u32[]{:S(2)}) copy-start(bf16[4,512,256]{2,1,0:T(8,128)(2,1)} %get-tuple-element.158) | copy-start | bytes 3145732
  99.5 14.0 %collective-permute-start.22 = (bf16[2,512,256]{2,1,0:T(8,128)(2,1)S(1)}, bf16[2,512,256]{2,1,0:T(8,128)(2,1)S(1)}, u32[]{:S(2)}, u32[]{:S(2)}) collective-permute-start(bf16[2,512,256]{2,1,0:T(8,128)(2,1)S(1)} %add_convert_fusion), channel_id=1, source_target_pairs={{0,16},{16,0},{1,17},{17,1},{2,18},{18,2},{3,19},{19,3},{4,20},{20... | collective-permute-start | bytes 1572872 | tf_op jit(solution)/shard_map/ppermute | solution.py:24
  101.1 20.8 %collective-permute-start.20 = (bf16[512,256]{1,0:T(8,128)(2,1)S(1)}, bf16[512,256]{1,0:T(8,128)(2,1)S(1)}, u32[]{:S(2)}, u32[]{:S(2)}) collective-permute-start(bf16[512,256]{1,0:T(8,128)(2,1)S(1)} %get-tuple-element.156), channel_id=1, source_target_pairs={{0,3},{1,0},{2,1},{3,2},{4,7},{5,4},{6,5},{7,6},{8,11},{9,8},{10,9... | collective-permute-start | bytes 786440 | tf_op jit(solution)/shard_map/ppermute | solution.py:24
  102.2 19.7 %collective-permute-start.21 = (bf16[512,256]{1,0:T(8,128)(2,1)S(1)}, bf16[512,256]{1,0:T(8,128)(2,1)S(1)}, u32[]{:S(2)}, u32[]{:S(2)}) collective-permute-start(bf16[512,256]{1,0:T(8,128)(2,1)S(1)} %get-tuple-element.157), channel_id=1, source_target_pairs={{0,2},{1,3},{2,0},{3,1},{4,6},{5,7},{6,4},{7,5},{8,10},{9,11},{10,... | collective-permute-start | bytes 786440 | tf_op jit(solution)/shard_map/ppermute | solution.py:24
  113.6 8.6 %copy-start.11 = (bf16[256]{0:T(256)(128)(2,1)S(1)}, bf16[256]{0:T(256)(128)(2,1)}, u32[]{:S(2)}) copy-start(bf16[256]{0:T(256)(128)(2,1)} %param.11) | copy-start | bytes 1540
  113.6 8.6 %copy-start.9 = (bf16[256,512]{1,0:T(8,128)(2,1)S(1)}, bf16[256,512]{1,0:T(8,128)(2,1)}, u32[]{:S(2)}) copy-start(bf16[256,512]{1,0:T(8,128)(2,1)} %param.12) | copy-start | bytes 786436
  113.6 8.3 %collective-permute-start.24 = (bf16[512,256]{1,0:T(8,128)(2,1)S(1)}, bf16[512,256]{1,0:T(8,128)(2,1)S(1)}, u32[]{:S(2)}, u32[]{:S(2)}) collective-permute-start(bf16[512,256]{1,0:T(8,128)(2,1)S(1)} %fusion.5), channel_id=1, source_target_pairs={{0,8},{8,0},{1,9},{9,1},{2,10},{10,2},{3,11},{11,3},{4,12},{12,4},... | collective-permute-start | bytes 786440 | tf_op jit(solution)/shard_map/ppermute | solution.py:24
  (5 other events, 15.1 us)

commit v17 on v16

--- a/solution.py
+++ b/solution.py
@@ -12,8 +12,8 @@
 BETA = 0.5
 CORES = 2
 OUTER = 2
-PAIR_VMEM = 18 * 1024 * 1024
-WEIGHT_VMEM = 22 * 1024 * 1024
+PAIR_VMEM = 12 * 1024 * 1024
+WEIGHT_VMEM = 15 * 1024 * 1024
 NOMINAL = pl.CostEstimate(flops=1024, bytes_accessed=1024, transcendentals=0)
 BF16 = jnp.bfloat16
 F32 = jnp.float32
@@ -572,7 +572,7 @@
         groups = [[keep] + parts + then for (_, keep), parts, then in zip(sides[0], got[0], later[0])]
         sent = sums_of(groups, 0)
         last = [swap(x, "tp", k) for x, k in zip(sent, pairs[0])]
-        coefficient, beyond, _ = lax.optimization_barrier((coefficient, beyond, sent))
+        coefficient, beyond = lax.optimization_barrier((coefficient, beyond))
         crossed = swap(widen([kept[2:], beyond]).astype(BF16), "outer", 1)
         grad_shape = jax.ShapeDtypeStruct((rows_here, width), BF16)
         resid_grad = weight_call(

time: 125 us -> 124 us (level)
  waiting for transfers between devices: 23.2 us -> 21.1 us
    ppermute x23, waiting for transfers between devices: 23.1 us -> 21.1 us  [swap(): lax.ppermute(value, axis, [(place, (place + step) % size) for place in ra...]
    unnamed x25 -> x27, local copies, waits for them, and re-layouts: 3.91 us -> 3.91 us
  transfers between devices with their start and end apart: 25 -> 25, of which waited for: 10 -> 10; matrix products, arithmetic and copies ran while one was open for 13% -> 13% of each run, Pallas kernels for 39% -> 40%
where the time goes in v17:
time: 124 us; the launch traced here: 123 us
  Pallas kernels  48.9 us (39%)
  starting transfers between devices  28.9 us (23%)
  waiting for transfers between devices  21.1 us (17%)
  other arithmetic  17.3 us (14%)
  local copies, waits for them, and re-layouts  5.61 us (5%)
    ppermute x23, starting transfers between devices, swap(): lax.ppermute(value, axis, [(place, (place + step) % size) for place in ra...  23.3 us
    pallas_call x3, Pallas kernels, weight_call(): pl.pallas_call(kernel, out_shape=out_shape, grid_spec=pltpu.PrefetchScala...  23.1 us
    ppermute x23, waiting for transfers between devices, swap(): lax.ppermute(value, axis, [(place, (place + step) % size) for place in ra...  21.1 us
    pallas_call x2, Pallas kernels, grad_product(): pl.pallas_call(kernel, out_shape=out_shape, grid_spec=pltpu.PrefetchScala...  14.8 us
    pallas_call x1, Pallas kernels, first_value(): pl.pallas_call(functools.partial(value_kernel, inner_flags), out_shape=[t...  7.78 us
    ppermute x2, starting transfers between devices, trade(): lax.ppermute(value, axis, [(place, place ^ mask) for place in range(size)])  5.67 us
    reduce_sum x1, other arithmetic, per_device(): squares = jnp.sum(resid_wide * resid_wide, axis=1, keepdims=True)  5.1 us
    unnamed x27, local copies, waits for them, and re-layouts  3.91 us
  transfers between devices with their start and end apart: 25, of which 10 were waited for; matrix products, arithmetic and copies ran while one was open for 13% of the time, Pallas kernels for 40%

profile of v17, /device:TPU:0, one launch (start us, length us, event | category | flops | bytes accessed | tf_op | source)
XLA Modules:
  0.0 122.7 jit_solution(8537007163116672599)
XLA Ops:
  2.1 3.0 %collective-permute-start = (f32[1,52,128]{2,1,0:T(8,128)S(1)}, f32[1,52,128]{2,1,0:T(8,128)S(1)}, u32[]{:S(2)}, u32[]{:S(2)}) collective-permute-start(f32[1,52,128]{2,1,0:T(8,128)S(1)} %maximum_bitcast_fusion), channel_id=1, source_target_pairs={{0,1},{1,0},{2,3},{3,2},{4,5},{5,4},{6,7},{7,6},{8,9},{9,8},{10,11... | collective-permute-start | bytes 79880 | tf_op jit(solution)/shard_map/ppermute | solution.py:29
  5.8 1.8 %multiply_convert_fusion = bf16[256,512]{1,0:T(8,128)(2,1)} fusion(bf16[256,512]{1,0:T(8,128)(2,1)} %param.12, f32[256]{0:T(256)S(1)} %convert_element_type.93), kind=kLoop, calls=%fused_computation.15 | loop fusion | flops 393216 | bytes 525312 | tf_op jit(solution)/shard_map/convert_element_type | solution.py:401
  7.5 1.2 %dynamic_slice.4 = s32[1]{0:T(128)} dynamic-slice(s32[8]{0:T(128)} %param.19, s32[]{:T(128)S(6)} %select_n.45), dynamic_slice_sizes={1} | dynamic-slice | bytes 12 | tf_op jit(solution)/shard_map/jit(dynamic_index_in_dim)/dynamic_slice | solution.py:428
  8.8 1.6 %collective-permute-start.2 = (bf16[256,512]{1,0:T(8,128)(2,1)}, bf16[256,512]{1,0:T(8,128)(2,1)S(1)}, u32[]{:S(2)}, u32[]{:S(2)}) collective-permute-start(bf16[256,512]{1,0:T(8,128)(2,1)} %multiply_convert_fusion), channel_id=1, source_target_pairs={{0,8},{8,0},{1,9},{9,1},{2,10},{10,2},{3,11},{11,3},{4,12},{12,4},... | collective-permute-start | bytes 786440 | tf_op jit(solution)/shard_map/ppermute | solution.py:24
  10.8 5.1 %multiply_reduce_fusion = f32[512]{0:T(512)S(1)} fusion(bf16[512,8192]{1,0:T(8,128)(2,1)} %resid_ref.3), kind=kLoop, calls=%fused_computation | loop fusion | flops 12582400 | bytes 8390656 | tf_op jit(solution)/shard_map/reduce_sum | solution.py:404
  15.9 2.6 %collective-permute-start.5 = (f32[2,52,128]{2,1,0:T(8,128)S(1)}, f32[2,52,128]{2,1,0:T(8,128)S(1)}, u32[]{:S(2)}, u32[]{:S(2)}) collective-permute-start(f32[2,52,128]{2,1,0:T(8,128)S(1)} %pad_maximum_fusion.5), channel_id=1, source_target_pairs={{0,2},{1,3},{2,0},{3,1},{4,6},{5,7},{6,4},{7,5},{8,10},{9,11},{10,... | collective-permute-start | bytes 159752 | tf_op jit(solution)/shard_map/ppermute | solution.py:29
  18.6 1.4 %collective-permute-done.1 = bf16[256,512]{1,0:T(8,128)(2,1)S(1)} collective-permute-done((bf16[256,512]{1,0:T(8,128)(2,1)}, bf16[256,512]{1,0:T(8,128)(2,1)S(1)}, u32[]{:S(2)}, u32[]{:S(2)}) %collective-permute-start.1) | collective-permute-done | bytes 262176 | tf_op jit(solution)/shard_map/ppermute | solution.py:24
  21.0 1.5 %collective-permute-start.3 = (bf16[256,512]{1,0:T(8,128)(2,1)S(1)}, bf16[256,512]{1,0:T(8,128)(2,1)S(1)}, u32[]{:S(2)}, u32[]{:S(2)}) collective-permute-start(bf16[256,512]{1,0:T(8,128)(2,1)S(1)} %collective-permute-done.1), channel_id=1, source_target_pairs={{0,16},{16,0},{1,17},{17,1},{2,18},{18,2},{3,19},{19,3},{4,20},{20... | collective-permute-start | bytes 786440 | tf_op jit(solution)/shard_map/ppermute | solution.py:24
  24.9 2.2 %collective-permute-done.4 = bf16[256,512]{1,0:T(8,128)(2,1)} collective-permute-done((bf16[256,512]{1,0:T(8,128)(2,1)}, bf16[256,512]{1,0:T(8,128)(2,1)}, u32[]{:S(2)}, u32[]{:S(2)}) %collective-permute-start.4) | collective-permute-done | bytes 262176 | tf_op jit(solution)/shard_map/ppermute | solution.py:24
  27.1 3.1 %collective-permute-done.3 = bf16[256,512]{1,0:T(8,128)(2,1)S(1)} collective-permute-done((bf16[256,512]{1,0:T(8,128)(2,1)S(1)}, bf16[256,512]{1,0:T(8,128)(2,1)S(1)}, u32[]{:S(2)}, u32[]{:S(2)}) %collective-permute-start.3) | collective-permute-done | bytes 262176 | tf_op jit(solution)/shard_map/ppermute | solution.py:24
  31.5 1.6 %collective-permute-start.9 = (bf16[256,512]{1,0:T(8,128)(2,1)}, bf16[256,512]{1,0:T(8,128)(2,1)}, u32[]{:S(2)}, u32[]{:S(2)}) collective-permute-start(bf16[256,512]{1,0:T(8,128)(2,1)} %collective-permute-done.4), channel_id=1, source_target_pairs={{0,16},{16,0},{1,17},{17,1},{2,18},{18,2},{3,19},{19,3},{4,20},{20... | collective-permute-start | bytes 786440 | tf_op jit(solution)/shard_map/ppermute | solution.py:24
  33.1 2.1 %shard_map.129 = (bf16[512,512]{1,0:T(8,128)(2,1)S(1)}, bf16[512,512]{1,0:T(8,128)(2,1)S(1)}, f32[512,1]{1,0:T(8,128)S(1)}) custom-call(s32[2]{0:T(128)S(1)} %pad_add_fusion.1.info_ref, f32[4,52,128]{2,1,0:T(8,128)S(1)} %pad_maximum_fusion.4.shares_ref, f32[512,1]{1,0:T(8,128)S(1)} %copy.17.squares_ref, bf16[512,512]{1,0:T(8,128)(2,1)} %value_cot_ref.1), custom_call_target="tpu_custom_call" | custom-call | flops 1024 | bytes 1024 | tf_op jit(solution)/shard_map/pallas_call | solution.py:350
  35.2 6.6 %shard_map.130 = bf16[4,4,512,256]{3,2,1,0:T(8,128)(2,1)} custom-call(s32[16]{0:T(128)S(1)} %stack.230.places_ref, bf16[512,512]{1,0:T(8,128)(2,1)S(1)} %get-tuple-element.97.cot_ref, bf16[512,8192]{1,0:T(8,128)(2,1)} %resid_ref.3, bf16[512,8192]{1,0:T(8,128)(2,1)} %resid_ref.3, bf16[512,8192]{1,0:T(8,128)(2,1)} %resid_ref.3, bf16[512,8192]{1,0:T(8,128)(2,1)} %resid_ref.3), custom_call_target="tpu_custom_call" | custom-call | flops 1024 | bytes 1024 | tf_op jit(solution)/shard_map/pallas_call | solution.py:128
  41.8 1.6 %collective-permute-start.10 = (bf16[256,512]{1,0:T(8,128)(2,1)}, bf16[256,512]{1,0:T(8,128)(2,1)}, u32[]{:S(2)}, u32[]{:S(2)}) collective-permute-start(bf16[256,512]{1,0:T(8,128)(2,1)} %collective-permute-done.6), channel_id=1, source_target_pairs={{0,8},{8,0},{1,9},{9,1},{2,10},{10,2},{3,11},{11,3},{4,12},{12,4},... | collective-permute-start | bytes 786440 | tf_op jit(solution)/shard_map/ppermute | solution.py:24
  44.6 3.9 %collective-permute-done.10 = bf16[256,512]{1,0:T(8,128)(2,1)} collective-permute-done((bf16[256,512]{1,0:T(8,128)(2,1)}, bf16[256,512]{1,0:T(8,128)(2,1)}, u32[]{:S(2)}, u32[]{:S(2)}) %collective-permute-start.10) | collective-permute-done | bytes 262176 | tf_op jit(solution)/shard_map/ppermute | solution.py:24
  51.3 1.6 %collective-permute-start.14 = (bf16[2,256,512]{2,1,0:T(8,128)(2,1)S(1)}, bf16[2,256,512]{2,1,0:T(8,128)(2,1)}, u32[]{:S(2)}, u32[]{:S(2)}) collective-permute-start(bf16[2,256,512]{2,1,0:T(8,128)(2,1)S(1)} %pad_maximum_fusion.2.rest_4_), channel_id=1, source_target_pairs={{0,8},{8,0},{1,9},{9,1},{2,10},{10,2},{3,11},{11,3},{4,12},{12,4},... | collective-permute-start | bytes 1572872 | tf_op jit(solution)/shard_map/ppermute | solution.py:24
  52.9 3.1 %collective-permute-done.11.rest_4_ = bf16[4,4,512,256]{3,2,1,0:T(8,128)(2,1)} collective-permute-done((bf16[4,4,512,256]{3,2,1,0:T(8,128)(2,1)}, bf16[4,4,512,256]{3,2,1,0:T(8,128)(2,1)}, u32[]{:S(2)}, u32[]{:S(2)}) %collective-permute-start.11) | collective-permute-done | bytes 4194336 | tf_op jit(solution)/shard_map/ppermute | solution.py:24
  56.1 8.2 %shard_map.131 = (bf16[2,512,256]{2,1,0:T(8,128)(2,1)}, bf16[2,512,256]{2,1,0:T(8,128)(2,1)}, bf16[2,512,256]{2,1,0:T(8,128)(2,1)}, bf16[2,512,256]{2,1,0:T(8,12...) custom-call(s32[16]{0:T(128)S(1)} %stack.211.places_ref, ...), custom_call_target="tpu_custom_call" | custom-call | flops 1024 | bytes 1024 | tf_op jit(solution)/shard_map/pallas_call | solution.py:128
  64.3 1.6 %collective-permute-start.12 = (bf16[2,512,256]{2,1,0:T(8,128)(2,1)}, bf16[2,512,256]{2,1,0:T(8,128)(2,1)}, u32[]{:S(2)}, u32[]{:S(2)}) collective-permute-start(bf16[2,512,256]{2,1,0:T(8,128)(2,1)} %get-tuple-element.105), channel_id=1, source_target_pairs={{0,8},{8,0},{1,9},{9,1},{2,10},{10,2},{3,11},{11,3},{4,12},{12,4},... | collective-permute-start | bytes 1572872 | tf_op jit(solution)/shard_map/ppermute | solution.py:24
  66.3 3.2 %collective-permute-start.16 = (bf16[2,512,256]{2,1,0:T(8,128)(2,1)}, bf16[2,512,256]{2,1,0:T(8,128)(2,1)}, u32[]{:S(2)}, u32[]{:S(2)}) collective-permute-start(bf16[2,512,256]{2,1,0:T(8,128)(2,1)} %get-tuple-element.139), channel_id=1, source_target_pairs={{0,1},{1,2},{2,3},{3,0},{4,5},{5,6},{6,7},{7,4},{8,9},{9,10},{10,1... | collective-permute-start | bytes 1572872 | tf_op jit(solution)/shard_map/ppermute | solution.py:24
  71.8 7.8 %shard_map.132 = (f32[512,512]{1,0:T(8,128)}, bf16[4,1024,512]{2,1,0:T(8,128)(2,1)}) custom-call(s32[4]{0:T(128)S(1)} %pad_add_fusion.2.places_ref, s32[4]{0:T(128)S(1)} %pad_add_fusion.3.offsets_ref, bf16[512,8192]{1,0:T(8,128)(2,1)} %resid_ref.3, bf16[2,256,512]{2,1,0:T(8,128)(2,1)S(1)} %pad_maximum_fusion.rest_0_, bf16[2,256,512]{2,1,0:T(8,128)(2,1)S(1)} %copy-done.4, ...), custom_call_target="tpu_custom_call" | custom-call | flops 1024 | bytes 1024 | tf_op jit(solution)/shard_map/pallas_call | solution.py:250
  79.8 2.0 %collective-permute-done.16 = bf16[2,512,256]{2,1,0:T(8,128)(2,1)} collective-permute-done((bf16[2,512,256]{2,1,0:T(8,128)(2,1)}, bf16[2,512,256]{2,1,0:T(8,128)(2,1)}, u32[]{:S(2)}, u32[]{:S(2)}) %collective-permute-start.16) | collective-permute-done | bytes 524320 | tf_op jit(solution)/shard_map/ppermute | solution.py:24
  81.8 2.0 %fusion.3 = (bf16[512,256]{1,0:T(8,128)(2,1)}, bf16[512,256]{1,0:T(8,128)(2,1)}) fusion(bf16[2,512,256]{2,1,0:T(8,128)(2,1)} %collective-permute-done.12.refs_1_, bf16[2,512,256]{2,1,0:T(8,128)(2,1)S(1)} %copy-done, bf16[2,512,256]{2,1,0:T(8,128)(2,1)} %collective-permute-done.13.refs_4_, bf16[2,512,256]{2,1,0:T(8,128)(2,1)S(1)} %copy-done.1), kind=kLoop, calls=%fused_computation.16 | loop fusion | flops 1048576 | bytes 1572864 | tf_op jit(solution)/shard_map/convert_element_type | solution.py:542
  83.8 1.6 %collective-permute-start.18 = (bf16[512,256]{1,0:T(8,128)(2,1)}, bf16[512,256]{1,0:T(8,128)(2,1)S(1)}, u32[]{:S(2)}, u32[]{:S(2)}) collective-permute-start(bf16[512,256]{1,0:T(8,128)(2,1)} %get-tuple-element.151), channel_id=1, source_target_pairs={{0,16},{16,0},{1,17},{17,1},{2,18},{18,2},{3,19},{19,3},{4,20},{20... | collective-permute-start | bytes 786440 | tf_op jit(solution)/shard_map/ppermute | solution.py:24
  86.4 3.0 %collective-permute-done.17.weight_ref = bf16[4,1024,512]{2,1,0:T(8,128)(2,1)} collective-permute-done((bf16[4,1024,512]{2,1,0:T(8,128)(2,1)}, bf16[4,1024,512]{2,1,0:T(8,128)(2,1)}, u32[]{:S(2)}, u32[]{:S(2)}) %collective-permute-start.17) | collective-permute-done | bytes 4194336 | tf_op jit(solution)/shard_map/ppermute | solution.py:24
  89.3 7.7 %shard_map.133 = (bf16[512,512]{1,0:T(8,128)(2,1)}, f32[512,1]{1,0:T(8,128)S(1)}) custom-call(s32[4]{0:T(128)S(1)} %pad_add_fusion.places_ref, bf16[512,8192]{1,0:T(8,128)(2,1)} %resid_ref.3, bf16[4,1024,512]{2,1,0:T(8,128)(2,1)} %collective-permute-done.17.weight_ref, f32[512,512]{1,0:T(8,128)} %get-tuple-element.141.first_ref, ...), custom_call_target="tpu_custom_call" | custom-call | flops 1024 | bytes 1024 | tf_op jit(solution)/shard_map/pallas_call | solution.py:288
  97.0 1.2 add_convert_fusion
  98.2 1.6 %collective-permute-start.22 = (bf16[2,512,256]{2,1,0:T(8,128)(2,1)S(1)}, bf16[2,512,256]{2,1,0:T(8,128)(2,1)S(1)}, u32[]{:S(2)}, u32[]{:S(2)}) collective-permute-start(bf16[2,512,256]{2,1,0:T(8,128)(2,1)S(1)} %add_convert_fusion), channel_id=1, source_target_pairs={{0,16},{16,0},{1,17},{17,1},{2,18},{18,2},{3,19},{19,3},{4,20},{20... | collective-permute-start | bytes 1572872 | tf_op jit(solution)/shard_map/ppermute | solution.py:24
  99.8 1.2 shard_map.134
  102.9 7.7 %shard_map.135.rest_0_ = bf16[512,8192]{1,0:T(8,128)(2,1)} custom-call(s32[4]{0:T(128)S(1)} %pad_add_fusion.2.places_ref, bf16[512,8192]{1,0:T(8,128)(2,1)} %resid_ref.3, bf16[4,1024,512]{2,1,0:T(8,128)(2,1)} %get-tuple-element.140.weight_ref, bf16[512,512]{1,0:T(8,128)(2,1)S(1)} %get-tuple-element.142.cot_ref, f32[512,1]{1,0:T(8,128)S(1)} %get-tuple-element.163.coef_ref), custom_call_target="tpu_custom_call" | custom-call | flops 1024 | bytes 1024 | tf_op jit(solution)/shard_map/pallas_call | solution.py:288
  110.6 1.6 %collective-permute-done.22 = bf16[2,512,256]{2,1,0:T(8,128)(2,1)S(1)} collective-permute-done((bf16[2,512,256]{2,1,0:T(8,128)(2,1)S(1)}, bf16[2,512,256]{2,1,0:T(8,128)(2,1)S(1)}, u32[]{:S(2)}, u32[]{:S(2)}) %collective-permute-start.22) | collective-permute-done | bytes 524320 | tf_op jit(solution)/shard_map/ppermute | solution.py:24
  113.0 7.7 %shard_map.136 = bf16[512,8192]{1,0:T(8,128)(2,1)} custom-call(s32[4]{0:T(128)S(1)} %pad_add_fusion.places_ref, bf16[512,8192]{1,0:T(8,128)(2,1)} %resid_ref.3, bf16[4,1024,512]{2,1,0:T(8,128)(2,1)} %collective-permute-done.17.weight_ref, bf16[512,512]{1,0:T(8,128)(2,1)S(1)} %get-tuple-element.142.cot_ref, ...), custom_call_target="tpu_custom_call", output_to_operand_aliasing={{}: (5, {})} | custom-call | flops 1024 | bytes 1024 | tf_op jit(solution)/shard_map/pallas_call | solution.py:288
  (79 shorter events, 19.9 us)
Async XLA Ops:
  2.1 6.7 %collective-permute-start = (f32[1,52,128]{2,1,0:T(8,128)S(1)}, f32[1,52,128]{2,1,0:T(8,128)S(1)}, u32[]{:S(2)}, u32[]{:S(2)}) collective-permute-start(f32[1,52,128]{2,1,0:T(8,128)S(1)} %maximum_bitcast_fusion), channel_id=1, source_target_pairs={{0,1},{1,0},{2,3},{3,2},{4,5},{5,4},{6,7},{7,6},{8,9},{9,8},{10,11... | collective-permute-start | bytes 79880 | tf_op jit(solution)/shard_map/ppermute | solution.py:29
  8.8 9.8 %collective-permute-start.2 = (bf16[256,512]{1,0:T(8,128)(2,1)}, bf16[256,512]{1,0:T(8,128)(2,1)S(1)}, u32[]{:S(2)}, u32[]{:S(2)}) collective-permute-start(bf16[256,512]{1,0:T(8,128)(2,1)} %multiply_convert_fusion), channel_id=1, source_target_pairs={{0,8},{8,0},{1,9},{9,1},{2,10},{10,2},{3,11},{11,3},{4,12},{12,4},... | collective-permute-start | bytes 786440 | tf_op jit(solution)/shard_map/ppermute | solution.py:24
  10.4 9.6 %collective-permute-start.1 = (bf16[256,512]{1,0:T(8,128)(2,1)}, bf16[256,512]{1,0:T(8,128)(2,1)S(1)}, u32[]{:S(2)}, u32[]{:S(2)}) collective-permute-start(bf16[256,512]{1,0:T(8,128)(2,1)} %multiply_convert_fusion), channel_id=1, source_target_pairs={{0,1},{1,2},{2,3},{3,0},{4,5},{5,6},{6,7},{7,4},{8,9},{9,10},{10,1... | collective-permute-start | bytes 786440 | tf_op jit(solution)/shard_map/ppermute | solution.py:24
  15.9 7.4 %collective-permute-start.5 = (f32[2,52,128]{2,1,0:T(8,128)S(1)}, f32[2,52,128]{2,1,0:T(8,128)S(1)}, u32[]{:S(2)}, u32[]{:S(2)}) collective-permute-start(f32[2,52,128]{2,1,0:T(8,128)S(1)} %pad_maximum_fusion.5), channel_id=1, source_target_pairs={{0,2},{1,3},{2,0},{3,1},{4,6},{5,7},{6,4},{7,5},{8,10},{9,11},{10,... | collective-permute-start | bytes 159752 | tf_op jit(solution)/shard_map/ppermute | solution.py:29
  19.9 7.2 %collective-permute-start.4 = (bf16[256,512]{1,0:T(8,128)(2,1)}, bf16[256,512]{1,0:T(8,128)(2,1)}, u32[]{:S(2)}, u32[]{:S(2)}) collective-permute-start(bf16[256,512]{1,0:T(8,128)(2,1)} %multiply_convert_fusion), channel_id=1, source_target_pairs={{0,3},{1,0},{2,1},{3,2},{4,7},{5,4},{6,5},{7,6},{8,11},{9,8},{10,9... | collective-permute-start | bytes 786440 | tf_op jit(solution)/shard_map/ppermute | solution.py:24
  21.0 9.2 %collective-permute-start.3 = (bf16[256,512]{1,0:T(8,128)(2,1)S(1)}, bf16[256,512]{1,0:T(8,128)(2,1)S(1)}, u32[]{:S(2)}, u32[]{:S(2)}) collective-permute-start(bf16[256,512]{1,0:T(8,128)(2,1)S(1)} %collective-permute-done.1), channel_id=1, source_target_pairs={{0,16},{16,0},{1,17},{17,1},{2,18},{18,2},{3,19},{19,3},{4,20},{20... | collective-permute-start | bytes 786440 | tf_op jit(solution)/shard_map/ppermute | solution.py:24
  24.3 19.1 %collective-permute-start.7 = (bf16[2,256,512]{2,1,0:T(8,128)(2,1)S(1)}, bf16[2,256,512]{2,1,0:T(8,128)(2,1)S(1)}, u32[]{:S(2)}, u32[]{:S(2)}) collective-permute-start(bf16[2,256,512]{2,1,0:T(8,128)(2,1)S(1)} %pad_maximum_fusion.rest_0_), channel_id=1, source_target_pairs={{0,16},{16,0},{1,17},{17,1},{2,18},{18,2},{3,19},{19,3},{4,20},{20... | collective-permute-start | bytes 1572872 | tf_op jit(solution)/shard_map/ppermute | solution.py:24
  30.2 11.6 %collective-permute-start.6 = (bf16[256,512]{1,0:T(8,128)(2,1)}, bf16[256,512]{1,0:T(8,128)(2,1)}, u32[]{:S(2)}, u32[]{:S(2)}) collective-permute-start(bf16[256,512]{1,0:T(8,128)(2,1)} %multiply_convert_fusion), channel_id=1, source_target_pairs={{0,2},{1,3},{2,0},{3,1},{4,6},{5,7},{6,4},{7,5},{8,10},{9,11},{10,... | collective-permute-start | bytes 786440 | tf_op jit(solution)/shard_map/ppermute | solution.py:24
  30.6 14.0 %collective-permute-start.8 = (bf16[2,256,512]{2,1,0:T(8,128)(2,1)S(1)}, bf16[2,256,512]{2,1,0:T(8,128)(2,1)S(1)}, u32[]{:S(2)}, u32[]{:S(2)}) collective-permute-start(bf16[2,256,512]{2,1,0:T(8,128)(2,1)S(1)} %pad_maximum_fusion.1.rest_2_), channel_id=1, source_target_pairs={{0,8},{8,0},{1,9},{9,1},{2,10},{10,2},{3,11},{11,3},{4,12},{12,4},... | collective-permute-start | bytes 1572872 | tf_op jit(solution)/shard_map/ppermute | solution.py:24
  31.5 13.2 %collective-permute-start.9 = (bf16[256,512]{1,0:T(8,128)(2,1)}, bf16[256,512]{1,0:T(8,128)(2,1)}, u32[]{:S(2)}, u32[]{:S(2)}) collective-permute-start(bf16[256,512]{1,0:T(8,128)(2,1)} %collective-permute-done.4), channel_id=1, source_target_pairs={{0,16},{16,0},{1,17},{17,1},{2,18},{18,2},{3,19},{19,3},{4,20},{20... | collective-permute-start | bytes 786440 | tf_op jit(solution)/shard_map/ppermute | solution.py:24
  41.8 6.8 %collective-permute-start.10 = (bf16[256,512]{1,0:T(8,128)(2,1)}, bf16[256,512]{1,0:T(8,128)(2,1)}, u32[]{:S(2)}, u32[]{:S(2)}) collective-permute-start(bf16[256,512]{1,0:T(8,128)(2,1)} %collective-permute-done.6), channel_id=1, source_target_pairs={{0,8},{8,0},{1,9},{9,1},{2,10},{10,2},{3,11},{11,3},{4,12},{12,4},... | collective-permute-start | bytes 786440 | tf_op jit(solution)/shard_map/ppermute | solution.py:24
  48.6 7.5 %collective-permute-start.11 = (bf16[4,4,512,256]{3,2,1,0:T(8,128)(2,1)}, bf16[4,4,512,256]{3,2,1,0:T(8,128)(2,1)}, u32[]{:S(2)}, u32[]{:S(2)}) collective-permute-start(bf16[4,4,512,256]{3,2,1,0:T(8,128)(2,1)} %shard_map.130), channel_id=1, source_target_pairs={{0,4},{4,0},{1,5},{5,1},{2,6},{6,2},{3,7},{7,3},{8,12},{12,8},{9,1... | collective-permute-start | bytes 12582920 | tf_op jit(solution)/shard_map/ppermute | solution.py:24
  49.7 20.0 %collective-permute-start.15 = (bf16[2,256,512]{2,1,0:T(8,128)(2,1)S(1)}, bf16[2,256,512]{2,1,0:T(8,128)(2,1)}, u32[]{:S(2)}, u32[]{:S(2)}) collective-permute-start(bf16[2,256,512]{2,1,0:T(8,128)(2,1)S(1)} %pad_maximum_fusion.3.rest_6_), channel_id=1, source_target_pairs={{0,16},{16,0},{1,17},{17,1},{2,18},{18,2},{3,19},{19,3},{4,20},{20... | collective-permute-start | bytes 1572872 | tf_op jit(solution)/shard_map/ppermute | solution.py:24
  51.3 18.4 %collective-permute-start.14 = (bf16[2,256,512]{2,1,0:T(8,128)(2,1)S(1)}, bf16[2,256,512]{2,1,0:T(8,128)(2,1)}, u32[]{:S(2)}, u32[]{:S(2)}) collective-permute-start(bf16[2,256,512]{2,1,0:T(8,128)(2,1)S(1)} %pad_maximum_fusion.2.rest_4_), channel_id=1, source_target_pairs={{0,8},{8,0},{1,9},{9,1},{2,10},{10,2},{3,11},{11,3},{4,12},{12,4},... | collective-permute-start | bytes 1572872 | tf_op jit(solution)/shard_map/ppermute | solution.py:24
  56.1 33.2 %copy-start.8 = (f32[512,1]{1,0:T(8,128)S(1)}, f32[512,1]{1,0:T(8,128)}, u32[]{:S(2)}) copy-start(f32[512,1]{1,0:T(8,128)} %copy-done.7) | copy-start | bytes 6148
  64.3 17.6 %copy-start = (bf16[2,512,256]{2,1,0:T(8,128)(2,1)S(1)}, bf16[2,512,256]{2,1,0:T(8,128)(2,1)}, u32[]{:S(2)}) copy-start(bf16[2,512,256]{2,1,0:T(8,128)(2,1)} %get-tuple-element.145.refs_0_) | copy-start | bytes 1572868
  64.3 15.3 %collective-permute-start.12 = (bf16[2,512,256]{2,1,0:T(8,128)(2,1)}, bf16[2,512,256]{2,1,0:T(8,128)(2,1)}, u32[]{:S(2)}, u32[]{:S(2)}) collective-permute-start(bf16[2,512,256]{2,1,0:T(8,128)(2,1)} %get-tuple-element.105), channel_id=1, source_target_pairs={{0,8},{8,0},{1,9},{9,1},{2,10},{10,2},{3,11},{11,3},{4,12},{12,4},... | collective-permute-start | bytes 1572872 | tf_op jit(solution)/shard_map/ppermute | solution.py:24
  65.8 14.0 %collective-permute-start.13 = (bf16[2,512,256]{2,1,0:T(8,128)(2,1)}, bf16[2,512,256]{2,1,0:T(8,128)(2,1)}, u32[]{:S(2)}, u32[]{:S(2)}) collective-permute-start(bf16[2,512,256]{2,1,0:T(8,128)(2,1)} %get-tuple-element.106), channel_id=1, source_target_pairs={{0,16},{16,0},{1,17},{17,1},{2,18},{18,2},{3,19},{19,3},{4,20},{20... | collective-permute-start | bytes 1572872 | tf_op jit(solution)/shard_map/ppermute | solution.py:24
  66.3 15.5 %collective-permute-start.16 = (bf16[2,512,256]{2,1,0:T(8,128)(2,1)}, bf16[2,512,256]{2,1,0:T(8,128)(2,1)}, u32[]{:S(2)}, u32[]{:S(2)}) collective-permute-start(bf16[2,512,256]{2,1,0:T(8,128)(2,1)} %get-tuple-element.139), channel_id=1, source_target_pairs={{0,1},{1,2},{2,3},{3,0},{4,5},{5,6},{6,7},{7,4},{8,9},{9,10},{10,1... | collective-permute-start | bytes 1572872 | tf_op jit(solution)/shard_map/ppermute | solution.py:24
  69.5 12.3 %copy-start.1 = (bf16[2,512,256]{2,1,0:T(8,128)(2,1)S(1)}, bf16[2,512,256]{2,1,0:T(8,128)(2,1)}, u32[]{:S(2)}) copy-start(bf16[2,512,256]{2,1,0:T(8,128)(2,1)} %get-tuple-element.147.refs_3_) | copy-start | bytes 1572868
  79.6 17.4 %copy-start.10 = (bf16[4,512,256]{2,1,0:T(8,128)(2,1)S(1)}, bf16[4,512,256]{2,1,0:T(8,128)(2,1)}, u32[]{:S(2)}) copy-start(bf16[4,512,256]{2,1,0:T(8,128)(2,1)} %get-tuple-element.158) | copy-start | bytes 3145732
  81.8 7.5 %collective-permute-start.17 = (bf16[4,1024,512]{2,1,0:T(8,128)(2,1)}, bf16[4,1024,512]{2,1,0:T(8,128)(2,1)}, u32[]{:S(2)}, u32[]{:S(2)}) collective-permute-start(bf16[4,1024,512]{2,1,0:T(8,128)(2,1)} %get-tuple-element.140.weight_ref), channel_id=1, source_target_pairs={{0,4},{4,0},{1,5},{5,1},{2,6},{6,2},{3,7},{7,3},{8,12},{12,8},{9,1... | collective-permute-start | bytes 12582920 | tf_op jit(solution)/shard_map/ppermute | solution.py:24
  83.8 16.0 %copy-start.2 = (bf16[2,512,256]{2,1,0:T(8,128)(2,1)S(1)}, bf16[2,512,256]{2,1,0:T(8,128)(2,1)}, u32[]{:S(2)}) copy-start(bf16[2,512,256]{2,1,0:T(8,128)(2,1)} %get-tuple-element.147.refs_3_) | copy-start | bytes 1572868
  83.8 13.2 %collective-permute-start.18 = (bf16[512,256]{1,0:T(8,128)(2,1)}, bf16[512,256]{1,0:T(8,128)(2,1)S(1)}, u32[]{:S(2)}, u32[]{:S(2)}) collective-permute-start(bf16[512,256]{1,0:T(8,128)(2,1)} %get-tuple-element.151), channel_id=1, source_target_pairs={{0,16},{16,0},{1,17},{17,1},{2,18},{18,2},{3,19},{19,3},{4,20},{20... | collective-permute-start | bytes 786440 | tf_op jit(solution)/shard_map/ppermute | solution.py:24
  85.3 11.7 %collective-permute-start.19 = (bf16[512,256]{1,0:T(8,128)(2,1)}, bf16[512,256]{1,0:T(8,128)(2,1)S(1)}, u32[]{:S(2)}, u32[]{:S(2)}) collective-permute-start(bf16[512,256]{1,0:T(8,128)(2,1)} %get-tuple-element.152), channel_id=1, source_target_pairs={{0,8},{8,0},{1,9},{9,1},{2,10},{10,2},{3,11},{11,3},{4,12},{12,4},... | collective-permute-start | bytes 786440 | tf_op jit(solution)/shard_map/ppermute | solution.py:24
  86.0 24.7 %collective-permute-start.23 = (bf16[2,512,256]{2,1,0:T(8,128)(2,1)}, bf16[2,512,256]{2,1,0:T(8,128)(2,1)S(1)}, u32[]{:S(2)}, u32[]{:S(2)}) collective-permute-start(bf16[2,512,256]{2,1,0:T(8,128)(2,1)} %get-tuple-element.162), channel_id=1, source_target_pairs={{0,1},{1,2},{2,3},{3,0},{4,5},{5,6},{6,7},{7,4},{8,9},{9,10},{10,1... | collective-permute-start | bytes 1572872 | tf_op jit(solution)/shard_map/ppermute | solution.py:24
  98.2 14.0 %collective-permute-start.22 = (bf16[2,512,256]{2,1,0:T(8,128)(2,1)S(1)}, bf16[2,512,256]{2,1,0:T(8,128)(2,1)S(1)}, u32[]{:S(2)}, u32[]{:S(2)}) collective-permute-start(bf16[2,512,256]{2,1,0:T(8,128)(2,1)S(1)} %add_convert_fusion), channel_id=1, source_target_pairs={{0,16},{16,0},{1,17},{17,1},{2,18},{18,2},{3,19},{19,3},{4,20},{20... | collective-permute-start | bytes 1572872 | tf_op jit(solution)/shard_map/ppermute | solution.py:24
  101.0 19.6 %collective-permute-start.20 = (bf16[512,256]{1,0:T(8,128)(2,1)S(1)}, bf16[512,256]{1,0:T(8,128)(2,1)S(1)}, u32[]{:S(2)}, u32[]{:S(2)}) collective-permute-start(bf16[512,256]{1,0:T(8,128)(2,1)S(1)} %get-tuple-element.156), channel_id=1, source_target_pairs={{0,3},{1,0},{2,1},{3,2},{4,7},{5,4},{6,5},{7,6},{8,11},{9,8},{10,9... | collective-permute-start | bytes 786440 | tf_op jit(solution)/shard_map/ppermute | solution.py:24
  102.2 10.0 %copy-start.11 = (bf16[4,512,256]{2,1,0:T(8,128)(2,1)S(1)}, bf16[4,512,256]{2,1,0:T(8,128)(2,1)}, u32[]{:S(2)}) copy-start(bf16[4,512,256]{2,1,0:T(8,128)(2,1)} %get-tuple-element.158) | copy-start | bytes 3145732
  102.2 18.5 %collective-permute-start.21 = (bf16[512,256]{1,0:T(8,128)(2,1)S(1)}, bf16[512,256]{1,0:T(8,128)(2,1)S(1)}, u32[]{:S(2)}, u32[]{:S(2)}) collective-permute-start(bf16[512,256]{1,0:T(8,128)(2,1)S(1)} %get-tuple-element.157), channel_id=1, source_target_pairs={{0,2},{1,3},{2,0},{3,1},{4,6},{5,7},{6,4},{7,5},{8,10},{9,11},{10,... | collective-permute-start | bytes 786440 | tf_op jit(solution)/shard_map/ppermute | solution.py:24
  112.3 8.6 %copy-start.9 = (bf16[256,512]{1,0:T(8,128)(2,1)S(1)}, bf16[256,512]{1,0:T(8,128)(2,1)}, u32[]{:S(2)}) copy-start(bf16[256,512]{1,0:T(8,128)(2,1)} %param.12) | copy-start | bytes 786436
  112.4 8.3 %collective-permute-start.24 = (bf16[512,256]{1,0:T(8,128)(2,1)S(1)}, bf16[512,256]{1,0:T(8,128)(2,1)S(1)}, u32[]{:S(2)}, u32[]{:S(2)}) collective-permute-start(bf16[512,256]{1,0:T(8,128)(2,1)S(1)} %fusion.5), channel_id=1, source_target_pairs={{0,8},{8,0},{1,9},{9,1},{2,10},{10,2},{3,11},{11,3},{4,12},{12,4},... | collective-permute-start | bytes 786440 | tf_op jit(solution)/shard_map/ppermute | solution.py:24
  (6 other events, 23.6 us)

commit v18 on v17

--- a/solution.py
+++ b/solution.py
@@ -424,16 +424,16 @@
     )
     near[1] = near_of(1, arrived[1])
     arrived[2] = swap(late_gained, "tp", shifts[2])
-    own_pieces[0] = far_of(0, gained, near[0])
     seq_length = lax.dynamic_index_in_dim(lengths, rep_place, keepdims=False)
     info = jnp.stack([tp_place, seq_length]).astype(jnp.int32)
-    near[1], arrived[2], packed, late_gained, info = lax.optimization_barrier(
-        (near[1], arrived[2], packed, late_gained, info)
+    near[0], near[1], arrived[2], packed, late_gained, info = lax.optimization_barrier(
+        (near[0], near[1], arrived[2], packed, late_gained, info)
     )
     near[2] = near_of(2, arrived[2])
     for k in order[3:]:
         arrived[k] = swap(late_gained, "tp", shifts[k])
     own_pieces[1] = far_of(1, arrived[1], near[1])
+    own_pieces[0] = far_of(0, gained, near[0])
     cot, cot_t, inv_rms = scaled_cot(width, rep_count, info, packed, squares, value_cot)
 
     def place_of(o, i, c, k):

time: 124 us -> 127 us (1.024)
  starting transfers between devices: 28.9 us -> 36.9 us
  waiting for transfers between devices: 21.1 us -> 17 us
    ppermute x23, starting transfers between devices: 23.3 us -> 33.9 us  [swap(): lax.ppermute(value, axis, [(place, (place + step) % size) for place in ra...]
    ppermute x23, waiting for transfers between devices: 21.1 us -> 12.6 us  [swap(): lax.ppermute(value, axis, [(place, (place + step) % size) for place in ra...]
    ppermute x2, waiting for transfers between devices: 0.01 us -> 4.38 us  [trade(): lax.ppermute(value, axis, [(place, place ^ mask) for place in range(size)])]
    ppermute x2, starting transfers between devices: 5.67 us -> 3.08 us  [trade(): lax.ppermute(value, axis, [(place, place ^ mask) for place in range(size)])]
    unnamed x27 -> x29, local copies, waits for them, and re-layouts: 3.91 us -> 3.92 us
  transfers between devices with their start and end apart: 25 -> 25, of which waited for: 10 -> 8; matrix products, arithmetic and copies ran while one was open for 13% -> 13% of each run, Pallas kernels for 40% -> 39%
where the time goes in v18:
time: 127 us; the launch traced here: 126 us
  Pallas kernels  48.9 us (39%)
  starting transfers between devices  36.9 us (29%)
  other arithmetic  17.3 us (14%)
  waiting for transfers between devices  17 us (13%)
  local copies, waits for them, and re-layouts  4.96 us (4%)
    ppermute x23, starting transfers between devices, swap(): lax.ppermute(value, axis, [(place, (place + step) % size) for place in ra...  33.9 us
    pallas_call x3, Pallas kernels, weight_call(): pl.pallas_call(kernel, out_shape=out_shape, grid_spec=pltpu.PrefetchScala...  23.1 us
    pallas_call x2, Pallas kernels, grad_product(): pl.pallas_call(kernel, out_shape=out_shape, grid_spec=pltpu.PrefetchScala...  14.8 us
    ppermute x23, waiting for transfers between devices, swap(): lax.ppermute(value, axis, [(place, (place + step) % size) for place in ra...  12.6 us
    pallas_call x1, Pallas kernels, first_value(): pl.pallas_call(functools.partial(value_kernel, inner_flags), out_shape=[t...  7.8 us
    reduce_sum x1, other arithmetic, per_device(): squares = jnp.sum(resid_wide * resid_wide, axis=1, keepdims=True)  5.1 us
    ppermute x2, waiting for transfers between devices, trade(): lax.ppermute(value, axis, [(place, place ^ mask) for place in range(size)])  4.38 us
    unnamed x29, local copies, waits for them, and re-layouts  3.92 us
  transfers between devices with their start and end apart: 25, of which 8 were waited for; matrix products, arithmetic and copies ran while one was open for 13% of the time, Pallas kernels for 39%

profile of v18, /device:TPU:0, one launch (start us, length us, event | category | flops | bytes accessed | tf_op | source)
XLA Modules:
  0.0 126.0 jit_solution(6090626292153042534)
XLA Ops:
  2.1 3.0 %collective-permute-start = (f32[1,52,128]{2,1,0:T(8,128)S(1)}, f32[1,52,128]{2,1,0:T(8,128)S(1)}, u32[]{:S(2)}, u32[]{:S(2)}) collective-permute-start(f32[1,52,128]{2,1,0:T(8,128)S(1)} %maximum_bitcast_fusion), channel_id=1, source_target_pairs={{0,1},{1,0},{2,3},{3,2},{4,5},{5,4},{6,7},{7,6},{8,9},{9,8},{10,11... | collective-permute-start | bytes 79880 | tf_op jit(solution)/shard_map/ppermute | solution.py:29
  5.8 1.8 %multiply_convert_fusion = bf16[256,512]{1,0:T(8,128)(2,1)} fusion(bf16[256,512]{1,0:T(8,128)(2,1)} %param.12, f32[256]{0:T(256)S(1)} %convert_element_type.93), kind=kLoop, calls=%fused_computation.15 | loop fusion | flops 393216 | bytes 525312 | tf_op jit(solution)/shard_map/convert_element_type | solution.py:401
  7.6 1.6 %collective-permute-start.2 = (bf16[256,512]{1,0:T(8,128)(2,1)}, bf16[256,512]{1,0:T(8,128)(2,1)S(1)}, u32[]{:S(2)}, u32[]{:S(2)}) collective-permute-start(bf16[256,512]{1,0:T(8,128)(2,1)} %multiply_convert_fusion), channel_id=1, source_target_pairs={{0,8},{8,0},{1,9},{9,1},{2,10},{10,2},{3,11},{11,3},{4,12},{12,4},... | collective-permute-start | bytes 786440 | tf_op jit(solution)/shard_map/ppermute | solution.py:24
  9.1 1.4 %collective-permute-start.1 = (bf16[256,512]{1,0:T(8,128)(2,1)}, bf16[256,512]{1,0:T(8,128)(2,1)S(1)}, u32[]{:S(2)}, u32[]{:S(2)}) collective-permute-start(bf16[256,512]{1,0:T(8,128)(2,1)} %multiply_convert_fusion), channel_id=1, source_target_pairs={{0,1},{1,2},{2,3},{3,0},{4,5},{5,6},{6,7},{7,4},{8,9},{9,10},{10,1... | collective-permute-start | bytes 786440 | tf_op jit(solution)/shard_map/ppermute | solution.py:24
  10.5 5.1 %multiply_reduce_fusion = f32[512]{0:T(512)S(1)} fusion(bf16[512,8192]{1,0:T(8,128)(2,1)} %resid_ref.3), kind=kLoop, calls=%fused_computation | loop fusion | flops 12582400 | bytes 8390656 | tf_op jit(solution)/shard_map/reduce_sum | solution.py:404
  15.6 3.0 %collective-permute-done.1 = bf16[256,512]{1,0:T(8,128)(2,1)S(1)} collective-permute-done((bf16[256,512]{1,0:T(8,128)(2,1)}, bf16[256,512]{1,0:T(8,128)(2,1)S(1)}, u32[]{:S(2)}, u32[]{:S(2)}) %collective-permute-start.1) | collective-permute-done | bytes 262176 | tf_op jit(solution)/shard_map/ppermute | solution.py:24
  19.4 1.5 %collective-permute-start.3 = (bf16[256,512]{1,0:T(8,128)(2,1)S(1)}, bf16[256,512]{1,0:T(8,128)(2,1)S(1)}, u32[]{:S(2)}, u32[]{:S(2)}) collective-permute-start(bf16[256,512]{1,0:T(8,128)(2,1)S(1)} %collective-permute-done.1), channel_id=1, source_target_pairs={{0,16},{16,0},{1,17},{17,1},{2,18},{18,2},{3,19},{19,3},{4,20},{20... | collective-permute-start | bytes 786440 | tf_op jit(solution)/shard_map/ppermute | solution.py:24
  22.2 4.4 %collective-permute-done.5 = f32[2,52,128]{2,1,0:T(8,128)S(1)} collective-permute-done((f32[2,52,128]{2,1,0:T(8,128)S(1)}, f32[2,52,128]{2,1,0:T(8,128)S(1)}, u32[]{:S(2)}, u32[]{:S(2)}) %collective-permute-start.5) | collective-permute-done | bytes 53280 | tf_op jit(solution)/shard_map/ppermute | solution.py:29
  29.0 1.6 %collective-permute-start.7 = (bf16[2,256,512]{2,1,0:T(8,128)(2,1)S(1)}, bf16[2,256,512]{2,1,0:T(8,128)(2,1)S(1)}, u32[]{:S(2)}, u32[]{:S(2)}) collective-permute-start(bf16[2,256,512]{2,1,0:T(8,128)(2,1)S(1)} %pad_maximum_fusion.rest_0_), channel_id=1, source_target_pairs={{0,16},{16,0},{1,17},{17,1},{2,18},{18,2},{3,19},{19,3},{4,20},{20... | collective-permute-start | bytes 1572872 | tf_op jit(solution)/shard_map/ppermute | solution.py:24
  32.1 2.1 %shard_map.129 = (bf16[512,512]{1,0:T(8,128)(2,1)S(1)}, bf16[512,512]{1,0:T(8,128)(2,1)S(1)}, f32[512,1]{1,0:T(8,128)S(1)}) custom-call(s32[2]{0:T(128)S(1)} %pad_add_fusion.1.info_ref, f32[4,52,128]{2,1,0:T(8,128)S(1)} %pad_maximum_fusion.4.shares_ref, f32[512,1]{1,0:T(8,128)S(1)} %copy.17.squares_ref, bf16[512,512]{1,0:T(8,128)(2,1)} %value_cot_ref.1), custom_call_target="tpu_custom_call" | custom-call | flops 1024 | bytes 1024 | tf_op jit(solution)/shard_map/pallas_call | solution.py:350
  34.2 6.6 %shard_map.130 = bf16[4,4,512,256]{3,2,1,0:T(8,128)(2,1)} custom-call(s32[16]{0:T(128)S(1)} %stack.230.places_ref, bf16[512,512]{1,0:T(8,128)(2,1)S(1)} %get-tuple-element.99.cot_ref, bf16[512,8192]{1,0:T(8,128)(2,1)} %resid_ref.3, bf16[512,8192]{1,0:T(8,128)(2,1)} %resid_ref.3, bf16[512,8192]{1,0:T(8,128)(2,1)} %resid_ref.3, bf16[512,8192]{1,0:T(8,128)(2,1)} %resid_ref.3), custom_call_target="tpu_custom_call" | custom-call | flops 1024 | bytes 1024 | tf_op jit(solution)/shard_map/pallas_call | solution.py:128
  40.8 1.6 %collective-permute-start.10 = (bf16[256,512]{1,0:T(8,128)(2,1)}, bf16[256,512]{1,0:T(8,128)(2,1)}, u32[]{:S(2)}, u32[]{:S(2)}) collective-permute-start(bf16[256,512]{1,0:T(8,128)(2,1)} %collective-permute-done.6), channel_id=1, source_target_pairs={{0,8},{8,0},{1,9},{9,1},{2,10},{10,2},{3,11},{11,3},{4,12},{12,4},... | collective-permute-start | bytes 786440 | tf_op jit(solution)/shard_map/ppermute | solution.py:24
  42.4 2.7 %collective-permute-done.9 = bf16[256,512]{1,0:T(8,128)(2,1)} collective-permute-done((bf16[256,512]{1,0:T(8,128)(2,1)}, bf16[256,512]{1,0:T(8,128)(2,1)}, u32[]{:S(2)}, u32[]{:S(2)}) %collective-permute-start.9) | collective-permute-done | bytes 262176 | tf_op jit(solution)/shard_map/ppermute | solution.py:24
  45.9 1.7 %collective-permute-done.10 = bf16[256,512]{1,0:T(8,128)(2,1)} collective-permute-done((bf16[256,512]{1,0:T(8,128)(2,1)}, bf16[256,512]{1,0:T(8,128)(2,1)}, u32[]{:S(2)}, u32[]{:S(2)}) %collective-permute-start.10) | collective-permute-done | bytes 262176 | tf_op jit(solution)/shard_map/ppermute | solution.py:24
  48.7 1.6 %collective-permute-start.15 = (bf16[2,256,512]{2,1,0:T(8,128)(2,1)S(1)}, bf16[2,256,512]{2,1,0:T(8,128)(2,1)}, u32[]{:S(2)}, u32[]{:S(2)}) collective-permute-start(bf16[2,256,512]{2,1,0:T(8,128)(2,1)S(1)} %pad_maximum_fusion.3.rest_6_), channel_id=1, source_target_pairs={{0,16},{16,0},{1,17},{17,1},{2,18},{18,2},{3,19},{19,3},{4,20},{20... | collective-permute-start | bytes 1572872 | tf_op jit(solution)/shard_map/ppermute | solution.py:24
  51.3 1.6 %collective-permute-start.14 = (bf16[2,256,512]{2,1,0:T(8,128)(2,1)S(1)}, bf16[2,256,512]{2,1,0:T(8,128)(2,1)}, u32[]{:S(2)}, u32[]{:S(2)}) collective-permute-start(bf16[2,256,512]{2,1,0:T(8,128)(2,1)S(1)} %pad_maximum_fusion.2.rest_4_), channel_id=1, source_target_pairs={{0,8},{8,0},{1,9},{9,1},{2,10},{10,2},{3,11},{11,3},{4,12},{12,4},... | collective-permute-start | bytes 1572872 | tf_op jit(solution)/shard_map/ppermute | solution.py:24
  53.0 2.1 %collective-permute-done.11.rest_4_ = bf16[4,4,512,256]{3,2,1,0:T(8,128)(2,1)} collective-permute-done((bf16[4,4,512,256]{3,2,1,0:T(8,128)(2,1)}, bf16[4,4,512,256]{3,2,1,0:T(8,128)(2,1)}, u32[]{:S(2)}, u32[]{:S(2)}) %collective-permute-start.11) | collective-permute-done | bytes 4194336 | tf_op jit(solution)/shard_map/ppermute | solution.py:24
  55.1 8.1 %shard_map.131 = (bf16[2,512,256]{2,1,0:T(8,128)(2,1)}, bf16[2,512,256]{2,1,0:T(8,128)(2,1)}, bf16[2,512,256]{2,1,0:T(8,128)(2,1)}, bf16[2,512,256]{2,1,0:T(8,12...) custom-call(s32[16]{0:T(128)S(1)} %stack.211.places_ref, ...), custom_call_target="tpu_custom_call" | custom-call | flops 1024 | bytes 1024 | tf_op jit(solution)/shard_map/pallas_call | solution.py:128
  63.2 1.6 %collective-permute-start.12 = (bf16[2,512,256]{2,1,0:T(8,128)(2,1)}, bf16[2,512,256]{2,1,0:T(8,128)(2,1)}, u32[]{:S(2)}, u32[]{:S(2)}) collective-permute-start(bf16[2,512,256]{2,1,0:T(8,128)(2,1)} %get-tuple-element.107), channel_id=1, source_target_pairs={{0,8},{8,0},{1,9},{9,1},{2,10},{10,2},{3,11},{11,3},{4,12},{12,4},... | collective-permute-start | bytes 1572872 | tf_op jit(solution)/shard_map/ppermute | solution.py:24
  64.8 1.5 %collective-permute-start.13 = (bf16[2,512,256]{2,1,0:T(8,128)(2,1)}, bf16[2,512,256]{2,1,0:T(8,128)(2,1)}, u32[]{:S(2)}, u32[]{:S(2)}) collective-permute-start(bf16[2,512,256]{2,1,0:T(8,128)(2,1)} %get-tuple-element.108), channel_id=1, source_target_pairs={{0,16},{16,0},{1,17},{17,1},{2,18},{18,2},{3,19},{19,3},{4,20},{20... | collective-permute-start | bytes 1572872 | tf_op jit(solution)/shard_map/ppermute | solution.py:24
  66.3 6.1 %collective-permute-start.16 = (bf16[2,512,256]{2,1,0:T(8,128)(2,1)}, bf16[2,512,256]{2,1,0:T(8,128)(2,1)}, u32[]{:S(2)}, u32[]{:S(2)}) collective-permute-start(bf16[2,512,256]{2,1,0:T(8,128)(2,1)} %get-tuple-element.141), channel_id=1, source_target_pairs={{0,1},{1,2},{2,3},{3,0},{4,5},{5,6},{6,7},{7,4},{8,9},{9,10},{10,1... | collective-permute-start | bytes 1572872 | tf_op jit(solution)/shard_map/ppermute | solution.py:24
  74.7 7.8 %shard_map.132 = (f32[512,512]{1,0:T(8,128)}, bf16[4,1024,512]{2,1,0:T(8,128)(2,1)}) custom-call(s32[4]{0:T(128)S(1)} %pad_add_fusion.2.places_ref, s32[4]{0:T(128)S(1)} %pad_add_fusion.3.offsets_ref, bf16[512,8192]{1,0:T(8,128)(2,1)} %resid_ref.3, bf16[2,256,512]{2,1,0:T(8,128)(2,1)S(1)} %pad_maximum_fusion.rest_0_, bf16[2,256,512]{2,1,0:T(8,128)(2,1)S(1)} %copy-done.4, ...), custom_call_target="tpu_custom_call" | custom-call | flops 1024 | bytes 1024 | tf_op jit(solution)/shard_map/pallas_call | solution.py:250
  82.5 1.6 %collective-permute-done.16 = bf16[2,512,256]{2,1,0:T(8,128)(2,1)} collective-permute-done((bf16[2,512,256]{2,1,0:T(8,128)(2,1)}, bf16[2,512,256]{2,1,0:T(8,128)(2,1)}, u32[]{:S(2)}, u32[]{:S(2)}) %collective-permute-start.16) | collective-permute-done | bytes 524320 | tf_op jit(solution)/shard_map/ppermute | solution.py:24
  84.2 2.0 %fusion.3 = (bf16[512,256]{1,0:T(8,128)(2,1)}, bf16[512,256]{1,0:T(8,128)(2,1)}) fusion(bf16[2,512,256]{2,1,0:T(8,128)(2,1)} %collective-permute-done.12.refs_1_, bf16[2,512,256]{2,1,0:T(8,128)(2,1)S(1)} %copy-done, bf16[2,512,256]{2,1,0:T(8,128)(2,1)} %collective-permute-done.13.refs_4_, bf16[2,512,256]{2,1,0:T(8,128)(2,1)S(1)} %copy-done.1), kind=kLoop, calls=%fused_computation.16 | loop fusion | flops 1048576 | bytes 1572864 | tf_op jit(solution)/shard_map/convert_element_type | solution.py:542
  87.1 1.5 %collective-permute-start.19 = (bf16[512,256]{1,0:T(8,128)(2,1)}, bf16[512,256]{1,0:T(8,128)(2,1)S(1)}, u32[]{:S(2)}, u32[]{:S(2)}) collective-permute-start(bf16[512,256]{1,0:T(8,128)(2,1)} %get-tuple-element.154), channel_id=1, source_target_pairs={{0,8},{8,0},{1,9},{9,1},{2,10},{10,2},{3,11},{11,3},{4,12},{12,4},... | collective-permute-start | bytes 786440 | tf_op jit(solution)/shard_map/ppermute | solution.py:24
  88.7 2.0 %collective-permute-start.23 = (bf16[2,512,256]{2,1,0:T(8,128)(2,1)}, bf16[2,512,256]{2,1,0:T(8,128)(2,1)S(1)}, u32[]{:S(2)}, u32[]{:S(2)}) collective-permute-start(bf16[2,512,256]{2,1,0:T(8,128)(2,1)} %get-tuple-element.164), channel_id=1, source_target_pairs={{0,1},{1,2},{2,3},{3,0},{4,5},{5,6},{6,7},{7,4},{8,9},{9,10},{10,1... | collective-permute-start | bytes 1572872 | tf_op jit(solution)/shard_map/ppermute | solution.py:24
  91.7 7.7 %shard_map.133 = (bf16[512,512]{1,0:T(8,128)(2,1)}, f32[512,1]{1,0:T(8,128)S(1)}) custom-call(s32[4]{0:T(128)S(1)} %pad_add_fusion.places_ref, bf16[512,8192]{1,0:T(8,128)(2,1)} %resid_ref.3, bf16[4,1024,512]{2,1,0:T(8,128)(2,1)} %collective-permute-done.17.weight_ref, f32[512,512]{1,0:T(8,128)} %get-tuple-element.143.first_ref, ...), custom_call_target="tpu_custom_call" | custom-call | flops 1024 | bytes 1024 | tf_op jit(solution)/shard_map/pallas_call | solution.py:288
  102.8 1.8 %collective-permute-start.20 = (bf16[512,256]{1,0:T(8,128)(2,1)S(1)}, bf16[512,256]{1,0:T(8,128)(2,1)S(1)}, u32[]{:S(2)}, u32[]{:S(2)}) collective-permute-start(bf16[512,256]{1,0:T(8,128)(2,1)S(1)} %get-tuple-element.158), channel_id=1, source_target_pairs={{0,3},{1,0},{2,1},{3,2},{4,7},{5,4},{6,5},{7,6},{8,11},{9,8},{10,9... | collective-permute-start | bytes 786440 | tf_op jit(solution)/shard_map/ppermute | solution.py:24
  104.6 1.7 %collective-permute-start.21 = (bf16[512,256]{1,0:T(8,128)(2,1)S(1)}, bf16[512,256]{1,0:T(8,128)(2,1)S(1)}, u32[]{:S(2)}, u32[]{:S(2)}) collective-permute-start(bf16[512,256]{1,0:T(8,128)(2,1)S(1)} %get-tuple-element.159), channel_id=1, source_target_pairs={{0,2},{1,3},{2,0},{3,1},{4,6},{5,7},{6,4},{7,5},{8,10},{9,11},{10,... | collective-permute-start | bytes 786440 | tf_op jit(solution)/shard_map/ppermute | solution.py:24
  106.3 7.7 %shard_map.135.rest_0_ = bf16[512,8192]{1,0:T(8,128)(2,1)} custom-call(s32[4]{0:T(128)S(1)} %pad_add_fusion.2.places_ref, bf16[512,8192]{1,0:T(8,128)(2,1)} %resid_ref.3, bf16[4,1024,512]{2,1,0:T(8,128)(2,1)} %get-tuple-element.142.weight_ref, bf16[512,512]{1,0:T(8,128)(2,1)S(1)} %get-tuple-element.144.cot_ref, f32[512,1]{1,0:T(8,128)S(1)} %get-tuple-element.165.coef_ref), custom_call_target="tpu_custom_call" | custom-call | flops 1024 | bytes 1024 | tf_op jit(solution)/shard_map/pallas_call | solution.py:288
  114.7 1.6 %collective-permute-start.24 = (bf16[512,256]{1,0:T(8,128)(2,1)S(1)}, bf16[512,256]{1,0:T(8,128)(2,1)S(1)}, u32[]{:S(2)}, u32[]{:S(2)}) collective-permute-start(bf16[512,256]{1,0:T(8,128)(2,1)S(1)} %fusion.5), channel_id=1, source_target_pairs={{0,8},{8,0},{1,9},{9,1},{2,10},{10,2},{3,11},{11,3},{4,12},{12,4},... | collective-permute-start | bytes 786440 | tf_op jit(solution)/shard_map/ppermute | solution.py:24
  116.2 7.7 %shard_map.136 = bf16[512,8192]{1,0:T(8,128)(2,1)} custom-call(s32[4]{0:T(128)S(1)} %pad_add_fusion.places_ref, bf16[512,8192]{1,0:T(8,128)(2,1)} %resid_ref.3, bf16[4,1024,512]{2,1,0:T(8,128)(2,1)} %collective-permute-done.17.weight_ref, bf16[512,512]{1,0:T(8,128)(2,1)S(1)} %get-tuple-element.144.cot_ref, ...), custom_call_target="tpu_custom_call", output_to_operand_aliasing={{}: (5, {})} | custom-call | flops 1024 | bytes 1024 | tf_op jit(solution)/shard_map/pallas_call | solution.py:288
  (81 shorter events, 21.6 us)
Async XLA Ops:
  0.6 20.2 %copy-start.12 = (s32[8]{0:T(128)S(1)}, s32[8]{0:T(128)}, u32[]{:S(2)}) copy-start(s32[8]{0:T(128)} %param.19) | copy-start | bytes 100
  2.1 5.4 %collective-permute-start = (f32[1,52,128]{2,1,0:T(8,128)S(1)}, f32[1,52,128]{2,1,0:T(8,128)S(1)}, u32[]{:S(2)}, u32[]{:S(2)}) collective-permute-start(f32[1,52,128]{2,1,0:T(8,128)S(1)} %maximum_bitcast_fusion), channel_id=1, source_target_pairs={{0,1},{1,0},{2,3},{3,2},{4,5},{5,4},{6,7},{7,6},{8,9},{9,8},{10,11... | collective-permute-start | bytes 79880 | tf_op jit(solution)/shard_map/ppermute | solution.py:29
  7.6 8.0 %collective-permute-start.2 = (bf16[256,512]{1,0:T(8,128)(2,1)}, bf16[256,512]{1,0:T(8,128)(2,1)S(1)}, u32[]{:S(2)}, u32[]{:S(2)}) collective-permute-start(bf16[256,512]{1,0:T(8,128)(2,1)} %multiply_convert_fusion), channel_id=1, source_target_pairs={{0,8},{8,0},{1,9},{9,1},{2,10},{10,2},{3,11},{11,3},{4,12},{12,4},... | collective-permute-start | bytes 786440 | tf_op jit(solution)/shard_map/ppermute | solution.py:24
  9.1 9.5 %collective-permute-start.1 = (bf16[256,512]{1,0:T(8,128)(2,1)}, bf16[256,512]{1,0:T(8,128)(2,1)S(1)}, u32[]{:S(2)}, u32[]{:S(2)}) collective-permute-start(bf16[256,512]{1,0:T(8,128)(2,1)} %multiply_convert_fusion), channel_id=1, source_target_pairs={{0,1},{1,2},{2,3},{3,0},{4,5},{5,6},{6,7},{7,4},{8,9},{9,10},{10,1... | collective-permute-start | bytes 786440 | tf_op jit(solution)/shard_map/ppermute | solution.py:24
  18.6 8.0 %collective-permute-start.4 = (bf16[256,512]{1,0:T(8,128)(2,1)}, bf16[256,512]{1,0:T(8,128)(2,1)}, u32[]{:S(2)}, u32[]{:S(2)}) collective-permute-start(bf16[256,512]{1,0:T(8,128)(2,1)} %multiply_convert_fusion), channel_id=1, source_target_pairs={{0,3},{1,0},{2,1},{3,2},{4,7},{5,4},{6,5},{7,6},{8,11},{9,8},{10,9... | collective-permute-start | bytes 786440 | tf_op jit(solution)/shard_map/ppermute | solution.py:24
  19.4 7.3 %collective-permute-start.3 = (bf16[256,512]{1,0:T(8,128)(2,1)S(1)}, bf16[256,512]{1,0:T(8,128)(2,1)S(1)}, u32[]{:S(2)}, u32[]{:S(2)}) collective-permute-start(bf16[256,512]{1,0:T(8,128)(2,1)S(1)} %collective-permute-done.1), channel_id=1, source_target_pairs={{0,16},{16,0},{1,17},{17,1},{2,18},{18,2},{3,19},{19,3},{4,20},{20... | collective-permute-start | bytes 786440 | tf_op jit(solution)/shard_map/ppermute | solution.py:24
  21.5 5.2 %collective-permute-start.5 = (f32[2,52,128]{2,1,0:T(8,128)S(1)}, f32[2,52,128]{2,1,0:T(8,128)S(1)}, u32[]{:S(2)}, u32[]{:S(2)}) collective-permute-start(f32[2,52,128]{2,1,0:T(8,128)S(1)} %pad_maximum_fusion.5), channel_id=1, source_target_pairs={{0,2},{1,3},{2,0},{3,1},{4,6},{5,7},{6,4},{7,5},{8,10},{9,11},{10,... | collective-permute-start | bytes 159752 | tf_op jit(solution)/shard_map/ppermute | solution.py:29
  26.7 14.2 %collective-permute-start.6 = (bf16[256,512]{1,0:T(8,128)(2,1)}, bf16[256,512]{1,0:T(8,128)(2,1)}, u32[]{:S(2)}, u32[]{:S(2)}) collective-permute-start(bf16[256,512]{1,0:T(8,128)(2,1)} %multiply_convert_fusion), channel_id=1, source_target_pairs={{0,2},{1,3},{2,0},{3,1},{4,6},{5,7},{6,4},{7,5},{8,10},{9,11},{10,... | collective-permute-start | bytes 786440 | tf_op jit(solution)/shard_map/ppermute | solution.py:24
  29.0 16.0 %collective-permute-start.7 = (bf16[2,256,512]{2,1,0:T(8,128)(2,1)S(1)}, bf16[2,256,512]{2,1,0:T(8,128)(2,1)S(1)}, u32[]{:S(2)}, u32[]{:S(2)}) collective-permute-start(bf16[2,256,512]{2,1,0:T(8,128)(2,1)S(1)} %pad_maximum_fusion.rest_0_), channel_id=1, source_target_pairs={{0,16},{16,0},{1,17},{17,1},{2,18},{18,2},{3,19},{19,3},{4,20},{20... | collective-permute-start | bytes 1572872 | tf_op jit(solution)/shard_map/ppermute | solution.py:24
  30.7 15.2 %collective-permute-start.8 = (bf16[2,256,512]{2,1,0:T(8,128)(2,1)S(1)}, bf16[2,256,512]{2,1,0:T(8,128)(2,1)S(1)}, u32[]{:S(2)}, u32[]{:S(2)}) collective-permute-start(bf16[2,256,512]{2,1,0:T(8,128)(2,1)S(1)} %pad_maximum_fusion.1.rest_2_), channel_id=1, source_target_pairs={{0,8},{8,0},{1,9},{9,1},{2,10},{10,2},{3,11},{11,3},{4,12},{12,4},... | collective-permute-start | bytes 1572872 | tf_op jit(solution)/shard_map/ppermute | solution.py:24
  31.5 13.5 %collective-permute-start.9 = (bf16[256,512]{1,0:T(8,128)(2,1)}, bf16[256,512]{1,0:T(8,128)(2,1)}, u32[]{:S(2)}, u32[]{:S(2)}) collective-permute-start(bf16[256,512]{1,0:T(8,128)(2,1)} %collective-permute-done.4), channel_id=1, source_target_pairs={{0,16},{16,0},{1,17},{17,1},{2,18},{18,2},{3,19},{19,3},{4,20},{20... | collective-permute-start | bytes 786440 | tf_op jit(solution)/shard_map/ppermute | solution.py:24
  40.8 6.8 %collective-permute-start.10 = (bf16[256,512]{1,0:T(8,128)(2,1)}, bf16[256,512]{1,0:T(8,128)(2,1)}, u32[]{:S(2)}, u32[]{:S(2)}) collective-permute-start(bf16[256,512]{1,0:T(8,128)(2,1)} %collective-permute-done.6), channel_id=1, source_target_pairs={{0,8},{8,0},{1,9},{9,1},{2,10},{10,2},{3,11},{11,3},{4,12},{12,4},... | collective-permute-start | bytes 786440 | tf_op jit(solution)/shard_map/ppermute | solution.py:24
  47.6 7.5 %collective-permute-start.11 = (bf16[4,4,512,256]{3,2,1,0:T(8,128)(2,1)}, bf16[4,4,512,256]{3,2,1,0:T(8,128)(2,1)}, u32[]{:S(2)}, u32[]{:S(2)}) collective-permute-start(bf16[4,4,512,256]{3,2,1,0:T(8,128)(2,1)} %shard_map.130), channel_id=1, source_target_pairs={{0,4},{4,0},{1,5},{5,1},{2,6},{6,2},{3,7},{7,3},{8,12},{12,8},{9,1... | collective-permute-start | bytes 12582920 | tf_op jit(solution)/shard_map/ppermute | solution.py:24
  48.7 23.9 %collective-permute-start.15 = (bf16[2,256,512]{2,1,0:T(8,128)(2,1)S(1)}, bf16[2,256,512]{2,1,0:T(8,128)(2,1)}, u32[]{:S(2)}, u32[]{:S(2)}) collective-permute-start(bf16[2,256,512]{2,1,0:T(8,128)(2,1)S(1)} %pad_maximum_fusion.3.rest_6_), channel_id=1, source_target_pairs={{0,16},{16,0},{1,17},{17,1},{2,18},{18,2},{3,19},{19,3},{4,20},{20... | collective-permute-start | bytes 1572872 | tf_op jit(solution)/shard_map/ppermute | solution.py:24
  51.3 21.3 %collective-permute-start.14 = (bf16[2,256,512]{2,1,0:T(8,128)(2,1)S(1)}, bf16[2,256,512]{2,1,0:T(8,128)(2,1)}, u32[]{:S(2)}, u32[]{:S(2)}) collective-permute-start(bf16[2,256,512]{2,1,0:T(8,128)(2,1)S(1)} %pad_maximum_fusion.2.rest_4_), channel_id=1, source_target_pairs={{0,8},{8,0},{1,9},{9,1},{2,10},{10,2},{3,11},{11,3},{4,12},{12,4},... | collective-permute-start | bytes 1572872 | tf_op jit(solution)/shard_map/ppermute | solution.py:24
  55.1 36.6 %copy-start.8 = (f32[512,1]{1,0:T(8,128)S(1)}, f32[512,1]{1,0:T(8,128)}, u32[]{:S(2)}) copy-start(f32[512,1]{1,0:T(8,128)} %copy-done.7) | copy-start | bytes 6148
  63.2 20.9 %copy-start = (bf16[2,512,256]{2,1,0:T(8,128)(2,1)S(1)}, bf16[2,512,256]{2,1,0:T(8,128)(2,1)}, u32[]{:S(2)}) copy-start(bf16[2,512,256]{2,1,0:T(8,128)(2,1)} %get-tuple-element.147.refs_0_) | copy-start | bytes 1572868
  63.2 19.3 %collective-permute-start.12 = (bf16[2,512,256]{2,1,0:T(8,128)(2,1)}, bf16[2,512,256]{2,1,0:T(8,128)(2,1)}, u32[]{:S(2)}, u32[]{:S(2)}) collective-permute-start(bf16[2,512,256]{2,1,0:T(8,128)(2,1)} %get-tuple-element.107), channel_id=1, source_target_pairs={{0,8},{8,0},{1,9},{9,1},{2,10},{10,2},{3,11},{11,3},{4,12},{12,4},... | collective-permute-start | bytes 1572872 | tf_op jit(solution)/shard_map/ppermute | solution.py:24
  64.8 17.7 %collective-permute-start.13 = (bf16[2,512,256]{2,1,0:T(8,128)(2,1)}, bf16[2,512,256]{2,1,0:T(8,128)(2,1)}, u32[]{:S(2)}, u32[]{:S(2)}) collective-permute-start(bf16[2,512,256]{2,1,0:T(8,128)(2,1)} %get-tuple-element.108), channel_id=1, source_target_pairs={{0,16},{16,0},{1,17},{17,1},{2,18},{18,2},{3,19},{19,3},{4,20},{20... | collective-permute-start | bytes 1572872 | tf_op jit(solution)/shard_map/ppermute | solution.py:24
  66.3 17.8 %collective-permute-start.16 = (bf16[2,512,256]{2,1,0:T(8,128)(2,1)}, bf16[2,512,256]{2,1,0:T(8,128)(2,1)}, u32[]{:S(2)}, u32[]{:S(2)}) collective-permute-start(bf16[2,512,256]{2,1,0:T(8,128)(2,1)} %get-tuple-element.141), channel_id=1, source_target_pairs={{0,1},{1,2},{2,3},{3,0},{4,5},{5,6},{6,7},{7,4},{8,9},{9,10},{10,1... | collective-permute-start | bytes 1572872 | tf_op jit(solution)/shard_map/ppermute | solution.py:24
  72.4 11.7 %copy-start.1 = (bf16[2,512,256]{2,1,0:T(8,128)(2,1)S(1)}, bf16[2,512,256]{2,1,0:T(8,128)(2,1)}, u32[]{:S(2)}) copy-start(bf16[2,512,256]{2,1,0:T(8,128)(2,1)} %get-tuple-element.149.refs_3_) | copy-start | bytes 1572868
  82.5 16.8 %copy-start.10 = (bf16[4,512,256]{2,1,0:T(8,128)(2,1)S(1)}, bf16[4,512,256]{2,1,0:T(8,128)(2,1)}, u32[]{:S(2)}) copy-start(bf16[4,512,256]{2,1,0:T(8,128)(2,1)} %get-tuple-element.160) | copy-start | bytes 3145732
  84.1 7.5 %collective-permute-start.17 = (bf16[4,1024,512]{2,1,0:T(8,128)(2,1)}, bf16[4,1024,512]{2,1,0:T(8,128)(2,1)}, u32[]{:S(2)}, u32[]{:S(2)}) collective-permute-start(bf16[4,1024,512]{2,1,0:T(8,128)(2,1)} %get-tuple-element.142.weight_ref), channel_id=1, source_target_pairs={{0,4},{4,0},{1,5},{5,1},{2,6},{6,2},{3,7},{7,3},{8,12},{12,8},{9,1... | collective-permute-start | bytes 12582920 | tf_op jit(solution)/shard_map/ppermute | solution.py:24
  86.1 15.4 %copy-start.2 = (bf16[2,512,256]{2,1,0:T(8,128)(2,1)S(1)}, bf16[2,512,256]{2,1,0:T(8,128)(2,1)}, u32[]{:S(2)}) copy-start(bf16[2,512,256]{2,1,0:T(8,128)(2,1)} %get-tuple-element.149.refs_3_) | copy-start | bytes 1572868
  86.1 13.2 %collective-permute-start.18 = (bf16[512,256]{1,0:T(8,128)(2,1)}, bf16[512,256]{1,0:T(8,128)(2,1)S(1)}, u32[]{:S(2)}, u32[]{:S(2)}) collective-permute-start(bf16[512,256]{1,0:T(8,128)(2,1)} %get-tuple-element.153), channel_id=1, source_target_pairs={{0,16},{16,0},{1,17},{17,1},{2,18},{18,2},{3,19},{19,3},{4,20},{20... | collective-permute-start | bytes 786440 | tf_op jit(solution)/shard_map/ppermute | solution.py:24
  87.1 12.2 %collective-permute-start.19 = (bf16[512,256]{1,0:T(8,128)(2,1)}, bf16[512,256]{1,0:T(8,128)(2,1)S(1)}, u32[]{:S(2)}, u32[]{:S(2)}) collective-permute-start(bf16[512,256]{1,0:T(8,128)(2,1)} %get-tuple-element.154), channel_id=1, source_target_pairs={{0,8},{8,0},{1,9},{9,1},{2,10},{10,2},{3,11},{11,3},{4,12},{12,4},... | collective-permute-start | bytes 786440 | tf_op jit(solution)/shard_map/ppermute | solution.py:24
  88.7 25.3 %collective-permute-start.23 = (bf16[2,512,256]{2,1,0:T(8,128)(2,1)}, bf16[2,512,256]{2,1,0:T(8,128)(2,1)S(1)}, u32[]{:S(2)}, u32[]{:S(2)}) collective-permute-start(bf16[2,512,256]{2,1,0:T(8,128)(2,1)} %get-tuple-element.164), channel_id=1, source_target_pairs={{0,1},{1,2},{2,3},{3,0},{4,5},{5,6},{6,7},{7,4},{8,9},{9,10},{10,1... | collective-permute-start | bytes 1572872 | tf_op jit(solution)/shard_map/ppermute | solution.py:24
  100.5 14.0 %collective-permute-start.22 = (bf16[2,512,256]{2,1,0:T(8,128)(2,1)S(1)}, bf16[2,512,256]{2,1,0:T(8,128)(2,1)S(1)}, u32[]{:S(2)}, u32[]{:S(2)}) collective-permute-start(bf16[2,512,256]{2,1,0:T(8,128)(2,1)S(1)} %add_convert_fusion), channel_id=1, source_target_pairs={{0,16},{16,0},{1,17},{17,1},{2,18},{18,2},{3,19},{19,3},{4,20},{20... | collective-permute-start | bytes 1572872 | tf_op jit(solution)/shard_map/ppermute | solution.py:24
  102.8 21.1 %collective-permute-start.20 = (bf16[512,256]{1,0:T(8,128)(2,1)S(1)}, bf16[512,256]{1,0:T(8,128)(2,1)S(1)}, u32[]{:S(2)}, u32[]{:S(2)}) collective-permute-start(bf16[512,256]{1,0:T(8,128)(2,1)S(1)} %get-tuple-element.158), channel_id=1, source_target_pairs={{0,3},{1,0},{2,1},{3,2},{4,7},{5,4},{6,5},{7,6},{8,11},{9,8},{10,9... | collective-permute-start | bytes 786440 | tf_op jit(solution)/shard_map/ppermute | solution.py:24
  104.6 10.0 %copy-start.11 = (bf16[4,512,256]{2,1,0:T(8,128)(2,1)S(1)}, bf16[4,512,256]{2,1,0:T(8,128)(2,1)}, u32[]{:S(2)}) copy-start(bf16[4,512,256]{2,1,0:T(8,128)(2,1)} %get-tuple-element.160) | copy-start | bytes 3145732
  104.6 19.3 %collective-permute-start.21 = (bf16[512,256]{1,0:T(8,128)(2,1)S(1)}, bf16[512,256]{1,0:T(8,128)(2,1)S(1)}, u32[]{:S(2)}, u32[]{:S(2)}) collective-permute-start(bf16[512,256]{1,0:T(8,128)(2,1)S(1)} %get-tuple-element.159), channel_id=1, source_target_pairs={{0,2},{1,3},{2,0},{3,1},{4,6},{5,7},{6,4},{7,5},{8,10},{9,11},{10,... | collective-permute-start | bytes 786440 | tf_op jit(solution)/shard_map/ppermute | solution.py:24
  114.7 9.3 %collective-permute-start.24 = (bf16[512,256]{1,0:T(8,128)(2,1)S(1)}, bf16[512,256]{1,0:T(8,128)(2,1)S(1)}, u32[]{:S(2)}, u32[]{:S(2)}) collective-permute-start(bf16[512,256]{1,0:T(8,128)(2,1)S(1)} %fusion.5), channel_id=1, source_target_pairs={{0,8},{8,0},{1,9},{9,1},{2,10},{10,2},{3,11},{11,3},{4,12},{12,4},... | collective-permute-start | bytes 786440 | tf_op jit(solution)/shard_map/ppermute | solution.py:24
  (7 other events, 33.0 us)
